TPU v7x, 32 devices: a whole 2x2x4 slice. The times are simulated.
32 devices in a mesh: lev: 4 (over z), gx: 2 (over x), gy: 4 (over y, core).
Axes of the slice: x: 2, y: 2, z: 4, core: 2. Of those that a mesh axis runs over, the one named last changes fastest.
Arguments:
- increment: float32 [2, 64, 128, 512], P(None, 'lev', 'gx', 'gy'), may hold values from -6 to 6
- norm_gain: float32 [2, 64, 128, 512], P(None, 'lev', 'gx', 'gy'), may hold values from 0.5 to 2
- diffusion_i: float32 [64, 128, 512], P('lev', 'gx', 'gy'), may hold values from 0.1 to 0.24
- diffusion_j: float32 [64, 128, 512], P('lev', 'gx', 'gy'), may hold values from 0.1 to 0.24
- sea_mask: int32 [64, 128, 512], P('lev', 'gx', 'gy'), may hold values from 0 to 1, as said below
- coupling: float32 [128, 128], replicated, may hold values from -0.5 to 0.5
Outputs:
- correlated: float32 [2, 64, 128, 512], P(None, 'lev', 'gx', 'gy')
Inputs may be any that keep to these rules, and one draw needn't show every extreme that they name: `sea_mask`: in every column the sea cells are the levels from the top down to some depth, which may be zero.
All inputs are finite; a program needn't handle non-finite values.
Results may differ from a plain program's by a relative error of at most 0.00009.
Values sent between devices are 32-bit elements; how exact they have to be, the bound alone decides.
No kernel may reach another device: no remote copies, remote signals or barrier semaphores. Data moves between devices by JAX's collectives and lax.ppermute only.
A program may use at most 64 MiB of HBM per device.

v0:
```python
import jax
import jax.numpy as jnp
from jax import lax
from jax.sharding import PartitionSpec as P

ITERS = 2


def with_halo(x, sides, width, wrap):
    for axis, dim in sides:
        devices, length = (lax.axis_size(axis), x.shape[dim])
        up = [(i, (i + 1) % devices) for i in range(devices if wrap else devices - 1)]
        down = [(j, i) for i, j in up]
        last = lax.slice_in_dim(x, length - width, length, axis=dim)
        first = lax.slice_in_dim(x, 0, width, axis=dim)
        before = lax.ppermute(last, axis, up)
        after = lax.ppermute(first, axis, down)
        x = jnp.concatenate([before, x, after], axis=dim)
    return x


def diffuse(values, coefficients):
    along_i = coefficients[0]
    along_j = coefficients[1]
    ocean = coefficients[2]
    weight_i = along_i[:, :-1, :] * ocean[:, :-1, :] * ocean[:, 1:, :]
    flux_i = weight_i[None] * (values[:, :, 1:, :] - values[:, :, :-1, :])
    weight_j = along_j[:, :, :-1] * ocean[:, :, :-1] * ocean[:, :, 1:]
    flux_j = weight_j[None] * (values[:, :, :, 1:] - values[:, :, :, :-1])
    return (
        values[:, :, 1:-1, 1:-1]
        + flux_i[:, :, 1:, 1:-1]
        - flux_i[:, :, :-1, 1:-1]
        + flux_j[:, :, 1:-1, 1:]
        - flux_j[:, :, 1:-1, :-1]
    )


def level_mix(fields, matrix):
    levels = fields.shape[1]
    first_level = lax.axis_index("lev") * levels
    own_rows = lax.dynamic_slice_in_dim(matrix, first_level, levels, 1)
    return jnp.einsum(
        "abcd,cdij->abij",
        own_rows,
        lax.all_gather(fields, "lev", axis=1, tiled=True),
        precision=lax.Precision.HIGHEST,
    )


def level_coef(coefficients, margin):
    coefficients = with_halo(coefficients, (("gx", 2),), margin, True)
    return with_halo(coefficients, (("gy", 3),), margin, False)


def level_field(values, margin):
    values = with_halo(values, (("gx", 2),), margin, True)
    return with_halo(values, (("gy", 3),), margin, False)


def diffusion(values, coefficients, extend_coef, extend_field, total_steps):
    coefs = extend_coef(coefficients, 1)
    spread = values
    for repeat in range(total_steps):
        spread = diffuse(extend_field(spread, 1), coefs)
    return spread


def shards(increment, norm_gain, diffusion_i, diffusion_j, sea_mask, coupling):
    total_steps = 2 * ITERS
    ocean = sea_mask.astype(jnp.float32)
    scaled = ocean[None] * norm_gain * increment
    order_count = coupling.shape[0]
    level_count = order_count // 2
    balance = jnp.eye(order_count, dtype=jnp.float32) + coupling
    forward = balance.reshape(2, level_count, 2, level_count)
    adjoint = jnp.transpose(forward, (2, 3, 0, 1))
    coefficients = jnp.stack([diffusion_i, diffusion_j, ocean])
    adjoint_mixed = level_mix(scaled, adjoint) * ocean[None]
    spread = diffusion(adjoint_mixed, coefficients, level_coef, level_field, total_steps)
    forward_mixed = level_mix(spread, forward)
    return ocean[None] * norm_gain * forward_mixed


def solution(mesh):
    return jax.shard_map(
        shards,
        mesh=mesh,
        in_specs=(
            P(None, "lev", "gx", "gy"),
            P(None, "lev", "gx", "gy"),
            P("lev", "gx", "gy"),
            P("lev", "gx", "gy"),
            P("lev", "gx", "gy"),
            P(),
        ),
        out_specs=P(None, "lev", "gx", "gy"),
        check_vma=False,
    )
```

profile of v0, /device:TPU:0, one launch (start us, length us, event | category | flops | bytes accessed | tf_op | source)
XLA Modules:
  0.0 297.4 jit_solution(16750456459297167882)
XLA Ops:
  6.5 1.4 fusion.25
  8.0 3.6 %copy_multiply_fusion = f32[2,16,64,128]{3,1,0,2:T(8,128)} fusion(f32[2,16,64,128]{3,2,1,0:T(8,128)} %param.6, f32[2,16,64,128]{3,2,1,0:T(8,128)S(1)} %copy-done.18, f32[16,64,128]{2,0,1:T(8,128)S(1)} %get-tuple-element.29), kind=kLoop, calls=%fused_computation.57 | loop fusion | flops 524288 | bytes 3670016 | tf_op jit(solution)/shard_map/mul | solution.py:72
  11.6 1.8 copy_bitcast_fusion
  13.5 3.0 %collective-permute-start = (f32[3,16,1,128]{3,1,2,0:T(8,128)S(1)}, f32[3,16,1,128]{3,1,2,0:T(8,128)S(1)}, u32[]{:S(2)}, u32[]{:S(2)}) collective-permute-start(f32[3,16,1,128]{3,1,2,0:T(8,128)S(1)} %get-tuple-element.10), channel_id=1, source_target_pairs={{0,4},{4,0},{1,5},{5,1},{2,6},{6,2},{3,7},{7,3},{8,12},{12,8},{9,1... | collective-permute-start | bytes 73736 | tf_op jit(solution)/shard_map/ppermute | solution.py:16
  16.7 1.6 collective-permute-done
  18.3 2.0 collective-permute-done.1
  20.4 2.2 fusion.26
  22.6 2.2 copy.71
  24.8 1.3 collective-permute-start.2
  26.1 2.1 copy.72
  28.2 1.3 collective-permute-start.3
  29.8 1.9 copy.73
  31.6 1.4 collective-permute-done.3
  33.0 1.9 copy.74
  35.0 3.3 %pad_maximum_fusion = f32[3,16,66,130]{3,1,2,0:T(8,128)S(1)} fusion(f32[3,16,66,1]{3,1,2,0:T(8,128)} %copy.74, f32[3,16,1,128]{3,1,2,0:T(8,128)S(1)} %collective-permute-done.1, f32[1,16,64,128]{3,1,2,0:T(8,128)S(1)} %get-tuple-element.28, f32[1,16,64,128]{3,1,2,0:T(8,128)S(1)} %get-tuple-element.30, f32[1,16,64,128]{3,1,2,0:T(8,128)S(1)} %get-tuple-element.31, ...), kind=kLoop, calls=%fused_computation.4 | loop fusion | flops 2471040 | bytes 3294720 | tf_op jit(solution)/shard_map/concatenate | solution.py:18
  38.2 1.7 slice_bitcast_fusion.2
  39.9 55.3 %all-gather.3.cloned.1.call-done = f32[2,64,64,128]{3,1,0,2:T(8,128)} async-done(((f32[2,16,64,128]{3,1,0,2:T(8,128)}), f32[2,64,64,128]{3,1,0,2:T(8,128)}) %all-gather.3.cloned.1.call-update) | async-done | bytes 4194320 | tf_op jit(solution)/shard_map/all_gather | solution.py:46
  95.2 4.0 %fusion.21 = f32[2,16,64,128]{3,1,0,2:T(8,128)S(1)} fusion(f32[2,64,64,128]{3,1,0,2:T(8,128)} %all-gather.3.cloned.1.call-done, f32[16,64,128]{2,0,1:T(8,128)S(1)} %get-tuple-element.29, f32[2,64,2,16]{1,3,0,2:T(8,128)S(1)} %copy.108), kind=kOutput, calls=%fused_computation.29 | convolution fusion | flops 402915328 | bytes 5783552 | tf_op jit(solution)/shard_map/abcd,cdij->abij/dot_general | solution.py:43
  99.3 1.5 collective-permute-start.4
  101.8 1.4 collective-permute-done.4
  103.2 1.3 collective-permute-done.5
  104.6 1.8 fusion.30
  106.4 1.9 copy.75
  109.5 1.9 copy.76
  111.4 1.5 collective-permute-start.7
  112.9 1.5 slice_multiply_fusion.2
  114.3 1.9 copy.77
  116.3 1.9 copy.78
  118.2 2.5 pad_maximum_fusion.1
  124.4 1.5 collective-permute-start.9
  125.9 1.7 collective-permute-done.8
  128.2 1.8 fusion.29
  130.0 1.9 copy.81
  131.9 3.3 %collective-permute-start.10 = (f32[2,16,66,1]{2,1,3,0:T(8,128)S(1)}, f32[2,16,66,1]{2,1,3,0:T(8,128)S(1)}, u32[]{:S(2)}, u32[]{:S(2)}) collective-permute-start(f32[2,16,66,1]{2,1,3,0:T(8,128)S(1)} %copy.81), channel_id=1, source_target_pairs={{0,1},{1,2},{2,3},{4,5},{5,6},{6,7},{8,9},{9,10},{10,11},{12,13},{... | collective-permute-start | bytes 25352 | tf_op jit(solution)/shard_map/ppermute | solution.py:16
  135.2 1.9 copy.82
  138.4 1.9 copy.83
  140.3 2.5 collective-permute-done.11
  142.8 1.9 copy.84
  144.8 2.5 pad_maximum_fusion.2
  150.4 1.5 collective-permute-start.12
  152.4 1.7 collective-permute-done.12
  154.2 1.6 collective-permute-done.13
  155.8 1.8 fusion.28
  157.6 1.9 copy.87
  159.6 2.8 collective-permute-start.14
  162.4 1.9 copy.88
  164.2 1.5 collective-permute-start.15
  165.7 1.9 copy.89
  168.7 1.9 copy.90
  170.7 2.5 pad_maximum_fusion.3
  177.5 1.5 collective-permute-start.17
  178.9 1.7 collective-permute-done.16
  181.3 1.8 fusion.27
  183.0 1.9 copy.93
  184.9 2.9 collective-permute-start.18
  187.8 1.9 copy.94
  189.7 1.5 collective-permute-start.19
  191.3 1.9 copy.95
  194.5 1.9 copy.96
  196.4 2.5 pad_maximum_fusion.4
  201.1 1.9 slice_subtract_fusion.4
  203.0 81.1 %all-gather.5.cloned.1.call-done = f32[2,64,64,128]{3,1,0,2:T(8,128)} async-done(((f32[2,16,64,128]{3,1,0,2:T(8,128)}), f32[2,64,64,128]{3,1,0,2:T(8,128)}) %all-gather.5.cloned.1.call-update) | async-done | bytes 4194320 | tf_op jit(solution)/shard_map/all_gather | solution.py:46
  284.1 4.9 %fusion.18 = f32[2,16,64,128]{3,1,0,2:T(8,128)S(1)} fusion(f32[2,64,64,128]{3,1,0,2:T(8,128)} %all-gather.5.cloned.1.call-done, f32[2,16,64,128]{3,2,1,0:T(8,128)S(1)} %copy-done.19, f32[16,64,128]{2,0,1:T(8,128)S(1)} %copy-done.16, f32[2,16,2,64]{3,2,1,0:T(2,128)S(1)} %constant_dynamic-slice_fusion.1), kind=kOutput, calls=%fused_computation.28 | convolution fusion | flops 403177472 | bytes 6832128 | tf_op jit(solution)/shard_map/abcd,cdij->abij/dot_general | solution.py:43
  288.9 1.6 copy.100
  (90 shorter events, 21.9 us)
Async XLA Ops:
  6.5 1.5 copy-start.18
  6.5 88.7 %all-gather.3.cloned.1.call-start = ((), (), s32[]{:S(2)}) async-start(), calls=%async_computation | async-start | bytes 5242880 | tf_op jit(solution)/shard_map/all_gather | solution.py:46
  8.0 87.2 %copy-start.15 = (f32[16,64,128]{2,0,1:T(8,128)}, f32[16,64,128]{2,0,1:T(8,128)S(1)}, u32[]{:S(2)}) copy-start(f32[16,64,128]{2,0,1:T(8,128)S(1)} %get-tuple-element.29) | copy-start | bytes 1572868
  11.6 5.0 %copy-start.20 = (f32[128,128]{1,0:T(8,128)S(1)}, f32[128,128]{1,0:T(8,128)}, u32[]{:S(2)}) copy-start(f32[128,128]{1,0:T(8,128)} %param.11) | copy-start | bytes 196612
  11.6 272.5 %all-gather.5.cloned.1.call-start = ((), (), s32[]{:S(2)}) async-start(), calls=%async_computation.1 | async-start | bytes 5242880 | tf_op jit(solution)/shard_map/all_gather | solution.py:46
  13.5 4.8 %collective-permute-start = (f32[3,16,1,128]{3,1,2,0:T(8,128)S(1)}, f32[3,16,1,128]{3,1,2,0:T(8,128)S(1)}, u32[]{:S(2)}, u32[]{:S(2)}) collective-permute-start(f32[3,16,1,128]{3,1,2,0:T(8,128)S(1)} %get-tuple-element.10), channel_id=1, source_target_pairs={{0,4},{4,0},{1,5},{5,1},{2,6},{6,2},{3,7},{7,3},{8,12},{12,8},{9,1... | collective-permute-start | bytes 73736 | tf_op jit(solution)/shard_map/ppermute | solution.py:16
  16.5 3.8 %collective-permute-start.1 = (f32[3,16,1,128]{3,1,2,0:T(8,128)S(1)}, f32[3,16,1,128]{3,1,2,0:T(8,128)S(1)}, u32[]{:S(2)}, u32[]{:S(2)}) collective-permute-start(f32[3,16,1,128]{3,1,2,0:T(8,128)S(1)} %get-tuple-element.11), channel_id=1, source_target_pairs={{4,0},{0,4},{5,1},{1,5},{6,2},{2,6},{7,3},{3,7},{12,8},{8,12},{13,... | collective-permute-start | bytes 73736 | tf_op jit(solution)/shard_map/ppermute | solution.py:17
  24.8 5.0 %collective-permute-start.2 = (f32[3,16,66,1]{2,1,3,0:T(8,128)S(1)}, f32[3,16,66,1]{2,1,3,0:T(8,128)S(1)}, u32[]{:S(2)}, u32[]{:S(2)}) collective-permute-start(f32[3,16,66,1]{2,1,3,0:T(8,128)S(1)} %copy.71), channel_id=1, source_target_pairs={{0,1},{1,2},{2,3},{4,5},{5,6},{6,7},{8,9},{9,10},{10,11},{12,13},{... | collective-permute-start | bytes 38024 | tf_op jit(solution)/shard_map/ppermute | solution.py:16
  28.2 4.9 %collective-permute-start.3 = (f32[3,16,66,1]{2,1,3,0:T(8,128)S(1)}, f32[3,16,66,1]{2,1,3,0:T(8,128)S(1)}, u32[]{:S(2)}, u32[]{:S(2)}) collective-permute-start(f32[3,16,66,1]{2,1,3,0:T(8,128)S(1)} %copy.72), channel_id=1, source_target_pairs={{1,0},{2,1},{3,2},{5,4},{6,5},{7,6},{9,8},{10,9},{11,10},{13,12},{... | collective-permute-start | bytes 38024 | tf_op jit(solution)/shard_map/ppermute | solution.py:17
  95.2 6.2 %copy-start.17 = (f32[16,66,130]{2,0,1:T(8,128)S(1)}, f32[16,66,130]{2,0,1:T(8,128)}, u32[]{:S(2)}) copy-start(f32[16,66,130]{2,0,1:T(8,128)} %get-tuple-element.6) | copy-start | bytes 1647364
  99.3 5.3 %copy-start = (f32[2,16,64,128]{3,1,0,2:T(8,128)}, f32[2,16,64,128]{3,1,0,2:T(8,128)S(1)}, u32[]{:S(2)}) copy-start(f32[2,16,64,128]{3,1,0,2:T(8,128)S(1)} %fusion.21) | copy-start | bytes 3145732
  99.3 3.9 %collective-permute-start.4 = (f32[2,16,1,128]{3,1,0,2:T(8,128)S(1)}, f32[2,16,1,128]{3,1,0,2:T(8,128)S(1)}, u32[]{:S(2)}, u32[]{:S(2)}) collective-permute-start(f32[2,16,1,128]{3,1,0,2:T(8,128)S(1)} %get-tuple-element.26), channel_id=1, source_target_pairs={{0,4},{4,0},{1,5},{5,1},{2,6},{6,2},{3,7},{7,3},{8,12},{12,8},{9,1... | collective-permute-start | bytes 49160 | tf_op jit(solution)/shard_map/ppermute | solution.py:16
  100.8 3.7 %collective-permute-start.5 = (f32[2,16,1,128]{3,1,0,2:T(8,128)S(1)}, f32[2,16,1,128]{3,1,0,2:T(8,128)S(1)}, u32[]{:S(2)}, u32[]{:S(2)}) collective-permute-start(f32[2,16,1,128]{3,1,0,2:T(8,128)S(1)} %get-tuple-element.27), channel_id=1, source_target_pairs={{4,0},{0,4},{5,1},{1,5},{6,2},{2,6},{7,3},{3,7},{12,8},{8,12},{13,... | collective-permute-start | bytes 49160 | tf_op jit(solution)/shard_map/ppermute | solution.py:17
  108.2 6.1 %collective-permute-start.6 = (f32[2,16,66,1]{2,1,3,0:T(8,128)S(1)}, f32[2,16,66,1]{2,1,3,0:T(8,128)S(1)}, u32[]{:S(2)}, u32[]{:S(2)}) collective-permute-start(f32[2,16,66,1]{2,1,3,0:T(8,128)S(1)} %copy.75), channel_id=1, source_target_pairs={{0,1},{1,2},{2,3},{4,5},{5,6},{6,7},{8,9},{9,10},{10,11},{12,13},{... | collective-permute-start | bytes 25352 | tf_op jit(solution)/shard_map/ppermute | solution.py:16
  111.4 4.9 %collective-permute-start.7 = (f32[2,16,66,1]{2,1,3,0:T(8,128)S(1)}, f32[2,16,66,1]{2,1,3,0:T(8,128)S(1)}, u32[]{:S(2)}, u32[]{:S(2)}) collective-permute-start(f32[2,16,66,1]{2,1,3,0:T(8,128)S(1)} %copy.76), channel_id=1, source_target_pairs={{1,0},{2,1},{3,2},{5,4},{6,5},{7,6},{9,8},{10,9},{11,10},{13,12},{... | collective-permute-start | bytes 25352 | tf_op jit(solution)/shard_map/ppermute | solution.py:17
  114.3 3.9 %copy-start.1 = (f32[2,16,64,128]{3,1,0,2:T(8,128)S(1)}, f32[2,16,64,128]{3,1,0,2:T(8,128)}, u32[]{:S(2)}) copy-start(f32[2,16,64,128]{3,1,0,2:T(8,128)} %copy-done) | copy-start | bytes 3145732
  120.7 1.2 copy-start.8
  120.7 1.6 copy-start.12
  123.8 6.2 %copy-start.2 = (f32[2,16,64,128]{3,1,0,2:T(8,128)}, f32[2,16,64,128]{3,1,0,2:T(8,128)S(1)}, u32[]{:S(2)}) copy-start(f32[2,16,64,128]{3,1,0,2:T(8,128)S(1)} %slice_subtract_fusion.10) | copy-start | bytes 3145732
  123.8 3.8 %collective-permute-start.8 = (f32[2,16,1,128]{3,1,0,2:T(8,128)S(1)}, f32[2,16,1,128]{3,1,0,2:T(8,128)S(1)}, u32[]{:S(2)}, u32[]{:S(2)}) collective-permute-start(f32[2,16,1,128]{3,1,0,2:T(8,128)S(1)} %get-tuple-element.24), channel_id=1, source_target_pairs={{0,4},{4,0},{1,5},{5,1},{2,6},{6,2},{3,7},{7,3},{8,12},{12,8},{9,1... | collective-permute-start | bytes 49160 | tf_op jit(solution)/shard_map/ppermute | solution.py:16
  124.4 3.7 %collective-permute-start.9 = (f32[2,16,1,128]{3,1,0,2:T(8,128)S(1)}, f32[2,16,1,128]{3,1,0,2:T(8,128)S(1)}, u32[]{:S(2)}, u32[]{:S(2)}) collective-permute-start(f32[2,16,1,128]{3,1,0,2:T(8,128)S(1)} %get-tuple-element.25), channel_id=1, source_target_pairs={{4,0},{0,4},{5,1},{1,5},{6,2},{2,6},{7,3},{3,7},{12,8},{8,12},{13,... | collective-permute-start | bytes 49160 | tf_op jit(solution)/shard_map/ppermute | solution.py:17
  130.0 14.8 %copy-start.3 = (f32[2,16,64,128]{3,1,0,2:T(8,128)S(1)}, f32[2,16,64,128]{3,1,0,2:T(8,128)}, u32[]{:S(2)}) copy-start(f32[2,16,64,128]{3,1,0,2:T(8,128)} %copy-done.2) | copy-start | bytes 3145732
  131.9 6.5 %collective-permute-start.10 = (f32[2,16,66,1]{2,1,3,0:T(8,128)S(1)}, f32[2,16,66,1]{2,1,3,0:T(8,128)S(1)}, u32[]{:S(2)}, u32[]{:S(2)}) collective-permute-start(f32[2,16,66,1]{2,1,3,0:T(8,128)S(1)} %copy.81), channel_id=1, source_target_pairs={{0,1},{1,2},{2,3},{4,5},{5,6},{6,7},{8,9},{9,10},{10,11},{12,13},{... | collective-permute-start | bytes 25352 | tf_op jit(solution)/shard_map/ppermute | solution.py:16
  137.1 5.7 %collective-permute-start.11 = (f32[2,16,66,1]{2,1,3,0:T(8,128)S(1)}, f32[2,16,66,1]{2,1,3,0:T(8,128)S(1)}, u32[]{:S(2)}, u32[]{:S(2)}) collective-permute-start(f32[2,16,66,1]{2,1,3,0:T(8,128)S(1)} %copy.82), channel_id=1, source_target_pairs={{1,0},{2,1},{3,2},{5,4},{6,5},{7,6},{9,8},{10,9},{11,10},{13,12},{... | collective-permute-start | bytes 25352 | tf_op jit(solution)/shard_map/ppermute | solution.py:17
  147.2 1.2 copy-start.9
  147.3 1.6 copy-start.13
  150.3 7.3 %copy-start.4 = (f32[2,16,64,128]{3,1,0,2:T(8,128)}, f32[2,16,64,128]{3,1,0,2:T(8,128)S(1)}, u32[]{:S(2)}) copy-start(f32[2,16,64,128]{3,1,0,2:T(8,128)S(1)} %slice_subtract_fusion.8) | copy-start | bytes 3145732
  150.4 3.8 %collective-permute-start.12 = (f32[2,16,1,128]{3,1,0,2:T(8,128)S(1)}, f32[2,16,1,128]{3,1,0,2:T(8,128)S(1)}, u32[]{:S(2)}, u32[]{:S(2)}) collective-permute-start(f32[2,16,1,128]{3,1,0,2:T(8,128)S(1)} %get-tuple-element.22), channel_id=1, source_target_pairs={{0,4},{4,0},{1,5},{5,1},{2,6},{6,2},{3,7},{7,3},{8,12},{12,8},{9,1... | collective-permute-start | bytes 49160 | tf_op jit(solution)/shard_map/ppermute | solution.py:16
  151.9 3.9 %collective-permute-start.13 = (f32[2,16,1,128]{3,1,0,2:T(8,128)S(1)}, f32[2,16,1,128]{3,1,0,2:T(8,128)S(1)}, u32[]{:S(2)}, u32[]{:S(2)}) collective-permute-start(f32[2,16,1,128]{3,1,0,2:T(8,128)S(1)} %get-tuple-element.23), channel_id=1, source_target_pairs={{4,0},{0,4},{5,1},{1,5},{6,2},{2,6},{7,3},{3,7},{12,8},{8,12},{13,... | collective-permute-start | bytes 49160 | tf_op jit(solution)/shard_map/ppermute | solution.py:17
  157.6 13.1 %copy-start.5 = (f32[2,16,64,128]{3,1,0,2:T(8,128)S(1)}, f32[2,16,64,128]{3,1,0,2:T(8,128)}, u32[]{:S(2)}) copy-start(f32[2,16,64,128]{3,1,0,2:T(8,128)} %copy-done.4) | copy-start | bytes 3145732
  159.6 6.2 %collective-permute-start.14 = (f32[2,16,66,1]{2,1,3,0:T(8,128)S(1)}, f32[2,16,66,1]{2,1,3,0:T(8,128)S(1)}, u32[]{:S(2)}, u32[]{:S(2)}) collective-permute-start(f32[2,16,66,1]{2,1,3,0:T(8,128)S(1)} %copy.87), channel_id=1, source_target_pairs={{0,1},{1,2},{2,3},{4,5},{5,6},{6,7},{8,9},{9,10},{10,11},{12,13},{... | collective-permute-start | bytes 25352 | tf_op jit(solution)/shard_map/ppermute | solution.py:16
  164.2 4.5 %collective-permute-start.15 = (f32[2,16,66,1]{2,1,3,0:T(8,128)S(1)}, f32[2,16,66,1]{2,1,3,0:T(8,128)S(1)}, u32[]{:S(2)}, u32[]{:S(2)}) collective-permute-start(f32[2,16,66,1]{2,1,3,0:T(8,128)S(1)} %copy.88), channel_id=1, source_target_pairs={{1,0},{2,1},{3,2},{5,4},{6,5},{7,6},{9,8},{10,9},{11,10},{13,12},{... | collective-permute-start | bytes 25352 | tf_op jit(solution)/shard_map/ppermute | solution.py:17
  173.2 1.2 copy-start.10
  173.2 1.6 copy-start.14
  174.7 1.2 copy-start.6
  176.8 3.8 %collective-permute-start.16 = (f32[2,16,1,128]{3,1,0,2:T(8,128)S(1)}, f32[2,16,1,128]{3,1,0,2:T(8,128)S(1)}, u32[]{:S(2)}, u32[]{:S(2)}) collective-permute-start(f32[2,16,1,128]{3,1,0,2:T(8,128)S(1)} %get-tuple-element.20), channel_id=1, source_target_pairs={{0,4},{4,0},{1,5},{5,1},{2,6},{6,2},{3,7},{7,3},{8,12},{12,8},{9,1... | collective-permute-start | bytes 49160 | tf_op jit(solution)/shard_map/ppermute | solution.py:16
  177.5 3.7 %collective-permute-start.17 = (f32[2,16,1,128]{3,1,0,2:T(8,128)S(1)}, f32[2,16,1,128]{3,1,0,2:T(8,128)S(1)}, u32[]{:S(2)}, u32[]{:S(2)}) collective-permute-start(f32[2,16,1,128]{3,1,0,2:T(8,128)S(1)} %get-tuple-element.21), channel_id=1, source_target_pairs={{4,0},{0,4},{5,1},{1,5},{6,2},{2,6},{7,3},{3,7},{12,8},{8,12},{13,... | collective-permute-start | bytes 49160 | tf_op jit(solution)/shard_map/ppermute | solution.py:17
  184.9 6.4 %collective-permute-start.18 = (f32[2,16,66,1]{2,1,3,0:T(8,128)S(1)}, f32[2,16,66,1]{2,1,3,0:T(8,128)S(1)}, u32[]{:S(2)}, u32[]{:S(2)}) collective-permute-start(f32[2,16,66,1]{2,1,3,0:T(8,128)S(1)} %copy.93), channel_id=1, source_target_pairs={{0,1},{1,2},{2,3},{4,5},{5,6},{6,7},{8,9},{9,10},{10,11},{12,13},{... | collective-permute-start | bytes 25352 | tf_op jit(solution)/shard_map/ppermute | solution.py:16
  189.7 4.7 %collective-permute-start.19 = (f32[2,16,66,1]{2,1,3,0:T(8,128)S(1)}, f32[2,16,66,1]{2,1,3,0:T(8,128)S(1)}, u32[]{:S(2)}, u32[]{:S(2)}) collective-permute-start(f32[2,16,66,1]{2,1,3,0:T(8,128)S(1)} %copy.94), channel_id=1, source_target_pairs={{1,0},{2,1},{3,2},{5,4},{6,5},{7,6},{9,8},{10,9},{11,10},{13,12},{... | collective-permute-start | bytes 25352 | tf_op jit(solution)/shard_map/ppermute | solution.py:17
  198.9 1.2 copy-start.7
  198.9 1.6 copy-start.11
  201.1 83.0 %copy-start.16 = (f32[16,64,128]{2,0,1:T(8,128)S(1)}, f32[16,64,128]{2,0,1:T(8,128)}, u32[]{:S(2)}) copy-start(f32[16,64,128]{2,0,1:T(8,128)} %copy-done.15) | copy-start | bytes 1572868
  201.1 83.0 %copy-start.19 = (f32[2,16,64,128]{3,2,1,0:T(8,128)S(1)}, f32[2,16,64,128]{3,2,1,0:T(8,128)}, u32[]{:S(2)}) copy-start(f32[2,16,64,128]{3,2,1,0:T(8,128)} %param.7) | copy-start | bytes 3145732
Sparse Core Ops, SparseCore 0:
  11.7 83.4 all-gather.2
  203.1 80.9 all-gather.4
where the time goes:
time: 298 us; the launch traced here: 297 us
  waiting for transfers between devices  157 us (53%)
  local copies, waits for them, and re-layouts  58.1 us (19%)
  starting transfers between devices  30.2 us (10%)
  other arithmetic  29.5 us (10%)
  between operations  13.9 us (5%)
  matrix products  8.9 us (3%)
    all_gather x2, waiting for transfers between devices, level_mix(): lax.all_gather(fields, 'lev', axis=1, tiled=True)  136 us
    slice x14, local copies, waits for them, and re-layouts, with_halo(): last = lax.slice_in_dim(x, length - width, length, axis=dim)  19 us
    ppermute x10, starting transfers between devices, with_halo(): before = lax.ppermute(last, axis, up)  18.9 us
    concatenate x10, other arithmetic, with_halo(): x = jnp.concatenate([before, x, after], axis=dim)  13.5 us
    ppermute x10, waiting for transfers between devices, with_halo(): after = lax.ppermute(first, axis, down)  12.4 us
    ppermute x10, starting transfers between devices, with_halo(): after = lax.ppermute(first, axis, down)  11.2 us
    ppermute x5, local copies, waits for them, and re-layouts, with_halo(): after = lax.ppermute(first, axis, down)  9.72 us
    slice x5, local copies, waits for them, and re-layouts, with_halo(): first = lax.slice_in_dim(x, 0, width, axis=dim)  9.54 us
  transfers between devices with their start and end apart: 22, of which 16 were waited for; matrix products, arithmetic and copies ran while one was open for 12% of the time, Pallas kernels for 0%

commit v1 on v0

v1 whole, which is shorter than its diff:
```python
import functools

import jax
import jax.numpy as jnp
from jax import lax
from jax.experimental import pallas as pl
from jax.experimental.pallas import tpu as pltpu
from jax.sharding import PartitionSpec as P

ITERS = 2
STEPS = 2 * ITERS
PAD = 8
VMEM_LIMIT = 40 * 1024 * 1024
HIGHEST = lax.Precision.HIGHEST


def params(**more):
    return pltpu.CompilerParams(vmem_limit_bytes=VMEM_LIMIT, **more)


def smem():
    return pl.BlockSpec(memory_space=pltpu.SMEM)


def vmem():
    return pl.BlockSpec(memory_space=pltpu.VMEM)


def scaled_kernel(slab, increment, gain, mask, out):
    fields, levels, rows, _ = increment.shape
    depth = jnp.zeros((rows, increment.shape[3]), jnp.float32)
    for level in range(levels):
        ocean = mask[level].astype(jnp.float32)
        depth = depth + ocean
        for field in range(fields):
            at = (field * levels + level) * rows
            out[pl.ds(at, rows), :] = ocean * gain[field, level] * increment[field, level]
    out[pl.ds(fields * levels * rows, rows), :] = depth


def scaled_message(slab, increment, gain, mask, rows):
    fields, levels, _, cols = increment.shape
    block = pl.BlockSpec((fields, levels, rows, cols), lambda step, slab: (0, 0, slab[0], 0))
    mask_block = pl.BlockSpec((levels, rows, cols), lambda step, slab: (0, slab[0], 0))
    shape = ((fields * levels + 1) * rows, cols)
    return pl.pallas_call(
        scaled_kernel,
        grid_spec=pltpu.PrefetchScalarGridSpec(
            num_scalar_prefetch=1,
            grid=(1,),
            in_specs=[block, block, mask_block],
            out_specs=pl.BlockSpec(shape, lambda step, slab: (0, 0)),
        ),
        out_shape=jax.ShapeDtypeStruct(shape, jnp.float32),
        compiler_params=params(),
        name="scaled_message",
    )(slab.reshape(1), increment, gain, mask)


def weight_kernel(slabs, along_i, along_j, mask, row_depth, col_depth, *refs):
    outs, (wi, wj) = refs[:-2], refs[-2:]
    levels, length, cols = along_i.shape
    lane = lax.broadcasted_iota(jnp.int32, (length, cols), 1)
    row = lax.broadcasted_iota(jnp.int32, (length, cols), 0)

    def one(level, carry):
        ocean = mask[level]
        next_row = jnp.broadcast_to((level < row_depth[...]).astype(jnp.int32), (length, cols))
        next_col = jnp.broadcast_to((level < col_depth[...]).astype(jnp.int32), (length, cols))
        below = jnp.where(row == length - 1, next_row, pltpu.roll(ocean, length - 1, 0))
        right = jnp.where(lane == cols - 1, next_col, pltpu.roll(ocean, cols - 1, 1))
        wi[level] = along_i[level] * (ocean * below).astype(jnp.float32)
        wj[level] = along_j[level] * (ocean * right).astype(jnp.float32)
        return carry

    lax.fori_loop(0, levels, one, 0)
    rows = outs[0].shape[0] // (2 * levels)
    for d, out in enumerate(outs):
        at = pl.multiple_of(slabs[d] * rows, rows)
        for level in range(levels):
            out[pl.ds(level * rows, rows), :] = wi[level, pl.ds(at, rows), :]
            out[pl.ds((levels + level) * rows, rows), :] = wj[level, pl.ds(at, rows), :]


def weight_messages(slabs, along_i, along_j, mask, row_depth, col_depth, rows):
    levels, _, cols = along_i.shape
    shape = jax.ShapeDtypeStruct((2 * levels * rows, cols), jnp.float32)
    return pl.pallas_call(
        weight_kernel,
        in_specs=[smem()] + [vmem()] * 5,
        out_specs=[vmem()] * slabs.shape[0],
        out_shape=[shape] * slabs.shape[0],
        scratch_shapes=[pltpu.VMEM(along_i.shape, jnp.float32)] * 2,
        compiler_params=params(),
        name="weight_messages",
    )(slabs, along_i, along_j, mask, row_depth, col_depth)


def adjoint_kernel(matrix, *refs):
    parts, out = refs[:-1], refs[-1]
    rows, cols, order = out.shape
    count = order // len(parts)
    level = lax.rem(lax.broadcasted_iota(jnp.int32, (order, cols), 0), order // 2).astype(jnp.float32)

    def one(i, carry):
        x = jnp.concatenate([part[pl.ds(i, count, rows), :] for part in parts], axis=0)
        depth = parts[0][pl.ds(count * rows + i, 1), :]
        for part in parts[1:]:
            depth = depth + part[pl.ds(count * rows + i, 1), :]
        y = jnp.dot(matrix[...], x, precision=HIGHEST, preferred_element_type=jnp.float32)
        out[i] = jnp.where(level < depth, y, 0.0).T
        return carry

    lax.fori_loop(0, rows, one, 0, unroll=4)


def adjoint_mix(matrix, parts, rows):
    order = matrix.shape[0]
    cols = parts[0].shape[1]
    return pl.pallas_call(
        adjoint_kernel,
        in_specs=[vmem()] * (1 + len(parts)),
        out_specs=vmem(),
        out_shape=jax.ShapeDtypeStruct((rows, cols, order), jnp.float32),
        compiler_params=params(),
        name="adjoint_mix",
    )(matrix, *parts)


def turn_kernel(sources, *refs):
    parts, out, held = refs[:-2], refs[-2], refs[-1]
    rows, cols, order = out.shape
    count = order // (2 * len(parts))

    def one(i, carry):
        for d, part in enumerate(parts):
            for side in range(2):
                at = pl.multiple_of(side * (order // 2) + sources[d] * count, 8)
                held[pl.ds(at, count), :] = part[pl.ds(side * count * rows + i, count, rows), :]
        out[i] = held[...].T
        return carry

    lax.fori_loop(0, rows, one, 0)


def turn_weights(sources, parts, rows):
    cols = parts[0].shape[1]
    order = parts[0].shape[0] // rows * len(parts)
    return pl.pallas_call(
        turn_kernel,
        in_specs=[smem()] + [vmem()] * len(parts),
        out_specs=vmem(),
        out_shape=jax.ShapeDtypeStruct((rows, cols, order), jnp.float32),
        scratch_shapes=[pltpu.VMEM((order, cols), jnp.float32)],
        compiler_params=params(),
        name="turn_weights",
    )(sources, *parts)


def spread_kernel(matrix, *refs):
    field, weight = refs[0:5], refs[5:10]
    outs, (a, b, wi, wj) = refs[10:-4], refs[-4:]
    rows, cols, order = field[0].shape
    half = order // 2
    ext = rows + 2 * STEPS
    wide = cols + 2 * PAD
    lane = lax.broadcasted_iota(jnp.int32, (wide, order), 1)

    def row_of(five, r):
        main, above, below, left, right = five
        if r < STEPS:
            mid = above[r]
        elif r < STEPS + rows:
            mid = main[r - STEPS]
        else:
            mid = below[r - STEPS - rows]
        return jnp.concatenate([left[r], mid, right[r]], axis=0)

    for r in range(ext):
        a[r] = row_of(field, r)
        w = row_of(weight, r)
        other = pltpu.roll(w, half, 1)
        wi[r] = jnp.where(lane < half, w, other)
        wj[r] = jnp.where(lane < half, other, w)

    src, dst = a, b
    for step in range(STEPS):
        first, last = step + 1, ext - 2 - step

        def one(r, carry, src=src, dst=dst):
            v, before = carry
            after = src[r + 1]
            flux = wi[r] * (after - v)
            across = wj[r] * (pltpu.roll(v, wide - 1, 0) - v)
            dst[r] = v + (flux - before) + (across - pltpu.roll(across, 1, 0))
            return after, flux

        v = src[first]
        lax.fori_loop(first, last + 1, one, (v, wi[first - 1] * (v - src[first - 1])))
        src, dst = dst, src

    count = order // len(outs)

    def mix(i, carry):
        x = src[STEPS + i, pl.ds(PAD, cols), :]
        y = lax.dot_general(
            matrix[...], x, (((1,), (1,)), ((), ())), precision=HIGHEST, preferred_element_type=jnp.float32
        )
        for d, out in enumerate(outs):
            out[pl.ds(i, count, rows), :] = y[d * count:(d + 1) * count]
        return carry

    lax.fori_loop(0, rows, mix, 0, unroll=4)


def spread_mix(matrix, field, weight, devices):
    rows, cols, order = field[0].shape
    shape = jax.ShapeDtypeStruct((order // devices * rows, cols), jnp.float32)
    ext = pltpu.VMEM((rows + 2 * STEPS, cols + 2 * PAD, order), jnp.float32)
    return pl.pallas_call(
        spread_kernel,
        in_specs=[vmem()] * 11,
        out_specs=[vmem()] * devices,
        out_shape=[shape] * devices,
        scratch_shapes=[ext] * 4,
        compiler_params=params(),
        name="spread_mix",
    )(matrix, *field, *weight)


def result_kernel(slabs, gain, mask, *refs):
    parts, out = refs[:-1], refs[-1]
    fields, levels, _, cols = gain.shape
    rows = parts[0].shape[0] // (fields * levels)
    for d, part in enumerate(parts):
        at = pl.multiple_of(slabs[d] * rows, rows)
        for level in range(levels):
            ocean = mask[level, pl.ds(at, rows), :].astype(jnp.float32)
            for field in range(fields):
                value = part[pl.ds((field * levels + level) * rows, rows), :]
                out[field, level, pl.ds(at, rows), :] = ocean * gain[field, level, pl.ds(at, rows), :] * value


def result(slabs, gain, mask, parts):
    return pl.pallas_call(
        result_kernel,
        in_specs=[smem()] + [vmem()] * (2 + len(parts)),
        out_specs=vmem(),
        out_shape=jax.ShapeDtypeStruct(gain.shape, jnp.float32),
        compiler_params=params(),
        name="result",
    )(slabs, gain, mask, *parts)


def shards(increment, norm_gain, diffusion_i, diffusion_j, sea_mask, coupling):
    devices = lax.axis_size("lev")
    gx_size = lax.axis_size("gx")
    gy_size = lax.axis_size("gy")
    me = lax.axis_index("lev")
    gx = lax.axis_index("gx")
    _, levels, length, cols = increment.shape
    rows = length // devices
    order = coupling.shape[0]

    snake = gx_size % 2 == 0

    def place(x, lev):
        return devices - 1 - lev if snake and x % 2 else lev

    def slab_of(lev):
        return jnp.where(gx % 2 == 1, devices - 1 - lev, lev) if snake else lev

    to = [lax.rem(me + d, devices) for d in range(devices)]
    source = [lax.rem(me + devices - d, devices) for d in range(devices)]
    to_slabs = jnp.stack([slab_of(t) for t in to]).astype(jnp.int32)
    source_slabs = jnp.stack([slab_of(s) for s in source]).astype(jnp.int32)
    sources = jnp.stack(source).astype(jnp.int32)

    def exchange(parts):
        moved = [parts[0]]
        for d in range(1, devices):
            moved.append(lax.ppermute(parts[d], "lev", [(k, (k + d) % devices) for k in range(devices)]))
        return moved

    chain = [place(x, s) * gx_size + x for x in range(gx_size) for s in range(devices)]
    ahead = [(chain[p], chain[(p + 1) % len(chain)]) for p in range(len(chain))]
    back = [(b, a) for a, b in ahead]
    right = [(k, k + 1) for k in range(gy_size - 1)]
    left = [(b, a) for a, b in right]

    def halo(x):
        above = lax.ppermute(x[-STEPS:], ("lev", "gx"), ahead)
        below = lax.ppermute(x[:STEPS], ("lev", "gx"), back)
        first = jnp.concatenate([above[:, :PAD], x[:, :PAD], below[:, :PAD]], axis=0)
        last = jnp.concatenate([above[:, -PAD:], x[:, -PAD:], below[:, -PAD:]], axis=0)
        from_left = lax.ppermute(last, "gy", right)
        from_right = lax.ppermute(first, "gy", left)
        return x, above, below, from_left, from_right

    scaled = [scaled_message(to_slabs[d], increment, norm_gain, sea_mask, rows) for d in range(devices)]
    scaled = exchange(scaled)

    depth = jnp.sum(sea_mask, axis=0)
    row_depth = lax.ppermute(depth[:1], "gx", [((k + 1) % gx_size, k) for k in range(gx_size)])
    col_depth = lax.ppermute(depth[:, :1], "gy", left)
    weights = weight_messages(to_slabs, diffusion_i, diffusion_j, sea_mask, row_depth, col_depth, rows)
    weights = exchange(weights)

    balance = jnp.eye(order, dtype=jnp.float32) + coupling
    by_device = balance.reshape(2, devices, levels, order)
    adjoint = jnp.concatenate(
        [by_device[:, s].reshape(2 * levels, order) for s in source], axis=0
    ).T
    forward = jnp.concatenate([by_device[:, t].reshape(2 * levels, order) for t in to], axis=0)

    field = halo(adjoint_mix(adjoint, scaled, rows))
    weight = halo(turn_weights(sources, weights, rows))
    mixed = exchange(spread_mix(forward, field, weight, devices))
    return result(source_slabs, norm_gain, sea_mask, mixed)


def solution(mesh):
    return jax.shard_map(
        shards,
        mesh=mesh,
        in_specs=(
            P(None, "lev", "gx", "gy"),
            P(None, "lev", "gx", "gy"),
            P("lev", "gx", "gy"),
            P("lev", "gx", "gy"),
            P("lev", "gx", "gy"),
            P(),
        ),
        out_specs=P(None, "lev", "gx", "gy"),
        check_vma=False,
    )
```

time: 298 us -> 114 us (0.38)
  the two profiles are of different devices: /device:TPU:0 before, /device:TPU:11 now
where the time goes in v1:
time: 114 us; the launch traced here: 113 us
  waiting for transfers between devices  54.6 us (48%)
  starting transfers between devices  30.8 us (27%)
  Pallas kernels  18.7 us (16%)
  local copies, waits for them, and re-layouts  6.78 us (6%)
  other arithmetic  2.28 us (2%)
    ppermute x9, waiting for transfers between devices, exchange(): lax.ppermute(parts[d], 'lev', [(k, (k + d) % devices) for k in range(devi...  47.5 us
    ppermute x9, starting transfers between devices, exchange(): lax.ppermute(parts[d], 'lev', [(k, (k + d) % devices) for k in range(devi...  12.1 us
    ppermute x2, starting transfers between devices, halo(): from_left = lax.ppermute(last, 'gy', right)  8.47 us
    pallas_call x1, Pallas kernels, spread_mix(): pl.pallas_call(spread_kernel, in_specs=[vmem()] * 11, out_specs=[vmem()]...  6.22 us
    unnamed x22, local copies, waits for them, and re-layouts  6.04 us
    ppermute x2, waiting for transfers between devices, halo(): from_right = lax.ppermute(first, 'gy', left)  3.98 us
    ppermute x2, starting transfers between devices, halo(): from_right = lax.ppermute(first, 'gy', left)  3.84 us
    pallas_call x1, Pallas kernels, turn_weights(): pl.pallas_call(turn_kernel, in_specs=[smem()] + [vmem()] * len(parts), ou...  3.33 us
  transfers between devices with their start and end apart: 19, of which 9 were waited for; matrix products, arithmetic and copies ran while one was open for 1% of the time, Pallas kernels for 10%

profile of v1, /device:TPU:11, one launch (start us, length us, event | category | flops | bytes accessed | tf_op | source)
XLA Modules:
  0.0 113.5 jit_solution(17050789389739348355)
XLA Ops:
  0.0 1.1 %reduce_sum.9 = s32[64,128]{1,0:T(8,128)S(1)} reduce(s32[16,64,128]{2,1,0:T(8,128)} %mask.11, s32[]{:T(128)} %constant.59.clone.1), dimensions={0}, to_apply=%region_0.1 | reduce | flops 122880 | bytes 557060 | tf_op jit(solution)/shard_map/reduce_sum | solution.py:303
  1.2 0.5 slice.80
  1.7 0.3 collective-permute-start.7
  1.9 2.9 %collective-permute-start.8 = (s32[64,1]{1,0:T(8,128)S(1)}, s32[64,1]{1,0:T(8,128)S(1)}, u32[]{:S(2)}, u32[]{:S(2)}) collective-permute-start(s32[64,1]{1,0:T(8,128)S(1)} %bitcast.34), channel_id=1, source_target_pairs={{1,0},{2,1},{3,2},{5,4},{6,5},{7,6},{9,8},{10,9},{11,10},{13,12},{... | collective-permute-start | bytes 776 | tf_op jit(solution)/shard_map/ppermute | solution.py:305
  4.8 0.0 copy-start
  4.8 1.2 %copy-done = f32[2,16,64,128]{3,2,1,0:T(8,128)S(1)} copy-done((f32[2,16,64,128]{3,2,1,0:T(8,128)S(1)}, f32[2,16,64,128]{3,2,1,0:T(8,128)}, u32[]{:S(2)}) %copy-start) | copy-done | bytes 1048600
  6.1 1.2 %copy-done.3 = f32[2,16,64,128]{3,2,1,0:T(8,128)S(1)} copy-done((f32[2,16,64,128]{3,2,1,0:T(8,128)S(1)}, f32[2,16,64,128]{3,2,1,0:T(8,128)}, u32[]{:S(2)}) %copy-start.3) | copy-done | bytes 1048600
  7.3 0.7 scaled_message.7
  8.0 0.0 collective-permute-start.2
  8.0 0.6 copy-done.1
  8.6 0.3 copy-done.4
  8.9 0.8 scaled_message.5
  9.7 1.3 %collective-permute-start = (f32[528,128]{1,0:T(8,128)}, f32[528,128]{1,0:T(8,128)}, u32[]{:S(2)}, u32[]{:S(2)}) collective-permute-start(f32[528,128]{1,0:T(8,128)} %scaled_message.5), channel_id=1, source_target_pairs={{0,8},{8,16},{16,24},{24,0},{1,9},{9,17},{17,25},{25,1},{2,10},{10... | collective-permute-start | bytes 811016 | tf_op jit(solution)/shard_map/ppermute | solution.py:282
  11.0 0.9 convert_add_fusion
  11.8 0.1 pad_add_fusion.2.slabs
  11.9 0.0 collective-permute-done.8.col_depth
  11.9 0.0 collective-permute-done.7.row_depth
  11.9 0.0 copy-start.6
  11.9 1.0 copy-done.6
  13.0 2.9 %weight_messages.1 = (f32[512,128]{1,0:T(8,128)S(1)}, f32[512,128]{1,0:T(8,128)}, f32[512,128]{1,0:T(8,128)}, f32[512,128]{1,0:T(8,128)}) custom-call(s32[4]{0:T(128)S(1)} %pad_add_fusion.2.slabs, f32[16,64,128]{2,1,0:T(8,128)S(1)} %copy-done.5, f32[16,64,128]{2,1,0:T(8,128)S(1)} %copy-done.6, s32[16,64,128]{2,1,0:T(8,128)S(1)} %copy-done.2, ...), custom_call_target="tpu_custom_call" | custom-call | tf_op jit(solution)/shard_map/weight_messages/pallas_call | solution.py:88
  15.9 1.3 %collective-permute-start.9 = (f32[512,128]{1,0:T(8,128)}, f32[512,128]{1,0:T(8,128)}, u32[]{:S(2)}, u32[]{:S(2)}) collective-permute-start(f32[512,128]{1,0:T(8,128)} %get-tuple-element.14), channel_id=1, source_target_pairs={{0,8},{8,16},{16,24},{24,0},{1,9},{9,17},{17,25},{25,1},{2,10},{10... | collective-permute-start | bytes 786440 | tf_op jit(solution)/shard_map/ppermute | solution.py:282
  17.2 2.1 %collective-permute-start.10 = (f32[512,128]{1,0:T(8,128)}, f32[512,128]{1,0:T(8,128)}, u32[]{:S(2)}, u32[]{:S(2)}) collective-permute-start(f32[512,128]{1,0:T(8,128)} %get-tuple-element.15), channel_id=1, source_target_pairs={{0,16},{8,24},{16,0},{24,8},{1,17},{9,25},{17,1},{25,9},{2,18},{10... | collective-permute-start | bytes 786440 | tf_op jit(solution)/shard_map/ppermute | solution.py:282
  19.3 1.5 %collective-permute-start.11 = (f32[512,128]{1,0:T(8,128)}, f32[512,128]{1,0:T(8,128)}, u32[]{:S(2)}, u32[]{:S(2)}) collective-permute-start(f32[512,128]{1,0:T(8,128)} %get-tuple-element.16), channel_id=1, source_target_pairs={{0,24},{8,0},{16,8},{24,16},{1,25},{9,1},{17,9},{25,17},{2,26},{10... | collective-permute-start | bytes 786440 | tf_op jit(solution)/shard_map/ppermute | solution.py:282
  20.8 0.1 scaled_message.6
  20.8 0.7 copy-done.7
  21.5 0.1 scaled_message.4.refs_0_
  21.6 0.0 copy-start.8
  21.6 0.1 copy.12.matrix
  21.7 0.1 pad_add_fusion.1.sources
  21.8 8.5 %collective-permute-done.9.refs_1_ = f32[512,128]{1,0:T(8,128)} collective-permute-done((f32[512,128]{1,0:T(8,128)}, f32[512,128]{1,0:T(8,128)}, u32[]{:S(2)}, u32[]{:S(2)}) %collective-permute-start.9) | collective-permute-done | bytes 262176 | tf_op jit(solution)/shard_map/ppermute | solution.py:282
  30.3 2.0 %collective-permute-start.1 = (f32[528,128]{1,0:T(8,128)S(1)}, f32[528,128]{1,0:T(8,128)S(1)}, u32[]{:S(2)}, u32[]{:S(2)}) collective-permute-start(f32[528,128]{1,0:T(8,128)S(1)} %copy-done.8), channel_id=1, source_target_pairs={{0,16},{8,24},{16,0},{24,8},{1,17},{9,25},{17,1},{25,9},{2,18},{10... | collective-permute-start | bytes 811016 | tf_op jit(solution)/shard_map/ppermute | solution.py:282
  32.3 19.3 %collective-permute-done.10.refs_2_ = f32[512,128]{1,0:T(8,128)} collective-permute-done((f32[512,128]{1,0:T(8,128)}, f32[512,128]{1,0:T(8,128)}, u32[]{:S(2)}, u32[]{:S(2)}) %collective-permute-start.10) | collective-permute-done | bytes 262176 | tf_op jit(solution)/shard_map/ppermute | solution.py:282
  51.7 0.1 collective-permute-done.11.refs_3_
  51.8 0.9 copy-done.10
  52.7 3.3 %turn_weights.1.refs_5_ = f32[16,128,128]{2,1,0:T(8,128)S(1)} custom-call(s32[4]{0:T(128)S(1)} %pad_add_fusion.1.sources, f32[512,128]{1,0:T(8,128)S(1)} %copy-done.10, f32[512,128]{1,0:T(8,128)} %collective-permute-done.9.refs_1_, f32[512,128]{1,0:T(8,128)} %collective-permute-done.10.refs_2_, f32[512,128]{1,0:T(8,128)} %collective-permute-done.11.refs_3_), custom_call_target="tpu_custom_call" | custom-call | tf_op jit(solution)/shard_map/turn_weights/pallas_call | solution.py:149
  56.1 0.1 collective-permute-start.13
  56.2 1.5 %collective-permute-start.12 = (f32[4,128,128]{2,1,0:T(8,128)S(1)}, f32[4,128,128]{2,1,0:T(8,128)S(1)}, u32[]{:S(2)}, u32[]{:S(2)}) collective-permute-start(f32[4,128,128]{2,1,0:T(8,128)S(1)} %get-tuple-element.24), channel_id=1, source_target_pairs={{0,8},{8,16},{16,24},{24,28},{28,20},{20,12},{12,4},{4,0},{1,9},{9... | collective-permute-start | bytes 786440 | tf_op jit(solution)/shard_map/ppermute | solution.py:292
  57.6 0.0 collective-permute-done.2.refs_3_
  57.7 0.0 collective-permute-done.refs_1_
  57.7 0.0 collective-permute-done.1.refs_2_
  57.7 2.9 %adjoint_mix.1.refs_0_ = f32[16,128,128]{2,1,0:T(8,128)S(1)} custom-call(f32[128,128]{1,0:T(8,128)S(1)} %copy.12.matrix, f32[528,128]{1,0:T(8,128)S(1)} %scaled_message.4.refs_0_, f32[528,128]{1,0:T(8,128)} %collective-permute-done.refs_1_, f32[528,128]{1,0:T(8,128)S(1)} %collective-permute-done.1.refs_2_, f32[528,128]{1,0:T(8,128)S(1)} %collective-permute-done.2.refs_3_), custom_call_target="tpu_custom_call" | custom-call | tf_op jit(solution)/shard_map/adjoint_mix/pallas_call | solution.py:120
  60.7 1.8 %collective-permute-start.4 = (f32[4,128,128]{2,1,0:T(8,128)S(1)}, f32[4,128,128]{2,1,0:T(8,128)S(1)}, u32[]{:S(2)}, u32[]{:S(2)}) collective-permute-start(f32[4,128,128]{2,1,0:T(8,128)S(1)} %get-tuple-element.27), channel_id=1, source_target_pairs={{8,0},{16,8},{24,16},{28,24},{20,28},{12,20},{4,12},{0,4},{9,1},{1... | collective-permute-start | bytes 786440 | tf_op jit(solution)/shard_map/ppermute | solution.py:293
  62.4 0.0 collective-permute-start.3
  62.5 1.1 collective-permute-done.13.refs_7_
  63.6 2.0 %collective-permute-done.12.refs_6_ = f32[4,128,128]{2,1,0:T(8,128)S(1)} collective-permute-done((f32[4,128,128]{2,1,0:T(8,128)S(1)}, f32[4,128,128]{2,1,0:T(8,128)S(1)}, u32[]{:S(2)}, u32[]{:S(2)}) %collective-permute-start.12) | collective-permute-done | bytes 262176 | tf_op jit(solution)/shard_map/ppermute | solution.py:292
  65.6 4.8 %collective-permute-start.14 = (f32[24,8,128]{2,1,0:T(8,128)S(1)}, f32[24,8,128]{2,1,0:T(8,128)S(1)}, u32[]{:S(2)}, u32[]{:S(2)}) collective-permute-start(f32[24,8,128]{2,1,0:T(8,128)S(1)} %pad_maximum_fusion.2), channel_id=1, source_target_pairs={{0,1},{1,2},{2,3},{4,5},{5,6},{6,7},{8,9},{9,10},{10,11},{12,13},{... | collective-permute-start | bytes 294920 | tf_op jit(solution)/shard_map/ppermute | solution.py:296
  70.5 1.9 %collective-permute-start.15 = (f32[24,8,128]{2,1,0:T(8,128)S(1)}, f32[24,8,128]{2,1,0:T(8,128)S(1)}, u32[]{:S(2)}, u32[]{:S(2)}) collective-permute-start(f32[24,8,128]{2,1,0:T(8,128)S(1)} %pad_maximum_fusion.3), channel_id=1, source_target_pairs={{1,0},{2,1},{3,2},{5,4},{6,5},{7,6},{9,8},{10,9},{11,10},{13,12},{... | collective-permute-start | bytes 294920 | tf_op jit(solution)/shard_map/ppermute | solution.py:297
  72.4 0.0 collective-permute-done.4.refs_2_
  72.4 0.0 collective-permute-done.3.refs_1_
  72.5 3.6 %collective-permute-start.5 = (f32[24,8,128]{2,1,0:T(8,128)S(1)}, f32[24,8,128]{2,1,0:T(8,128)S(1)}, u32[]{:S(2)}, u32[]{:S(2)}) collective-permute-start(f32[24,8,128]{2,1,0:T(8,128)S(1)} %pad_maximum_fusion), channel_id=1, source_target_pairs={{0,1},{1,2},{2,3},{4,5},{5,6},{6,7},{8,9},{9,10},{10,11},{12,13},{... | collective-permute-start | bytes 294920 | tf_op jit(solution)/shard_map/ppermute | solution.py:296
  76.1 1.9 %collective-permute-start.6 = (f32[24,8,128]{2,1,0:T(8,128)S(1)}, f32[24,8,128]{2,1,0:T(8,128)S(1)}, u32[]{:S(2)}, u32[]{:S(2)}) collective-permute-start(f32[24,8,128]{2,1,0:T(8,128)S(1)} %pad_maximum_fusion.1), channel_id=1, source_target_pairs={{1,0},{2,1},{3,2},{5,4},{6,5},{7,6},{9,8},{10,9},{11,10},{13,12},{... | collective-permute-start | bytes 294920 | tf_op jit(solution)/shard_map/ppermute | solution.py:297
  78.0 0.0 collective-permute-done.14.refs_8_
  78.1 0.0 collective-permute-done.15.refs_9_
  78.1 0.0 collective-permute-done.5.refs_3_
  78.1 4.0 %collective-permute-done.6.refs_4_ = f32[24,8,128]{2,1,0:T(8,128)S(1)} collective-permute-done((f32[24,8,128]{2,1,0:T(8,128)S(1)}, f32[24,8,128]{2,1,0:T(8,128)S(1)}, u32[]{:S(2)}, u32[]{:S(2)}) %collective-permute-start.6) | collective-permute-done | bytes 98336 | tf_op jit(solution)/shard_map/ppermute | solution.py:297
  82.1 6.2 %spread_mix.1 = (f32[512,128]{1,0:T(8,128)S(1)}, f32[512,128]{1,0:T(8,128)S(1)}, f32[512,128]{1,0:T(8,128)S(1)}, f32[512,128]{1,0:T(8,128)S(1)}) custom-call(f32[128,128]{1,0:T(8,128)S(1)} %get-tuple-element.43.matrix, f32[16,128,128]{2,1,0:T(8,128)S(1)} %adjoint_mix.1.refs_0_, f32[4,128,128]{2,1,0:T(8,128)S(1)} %collective-permute-done.3.refs_1_, ...), custom_call_target="tpu_custom_call" | custom-call | tf_op jit(solution)/shard_map/spread_mix/pallas_call | solution.py:220
  88.3 1.5 %collective-permute-start.16 = (f32[512,128]{1,0:T(8,128)S(1)}, f32[512,128]{1,0:T(8,128)S(1)}, u32[]{:S(2)}, u32[]{:S(2)}) collective-permute-start(f32[512,128]{1,0:T(8,128)S(1)} %get-tuple-element.18), channel_id=1, source_target_pairs={{0,8},{8,16},{16,24},{24,0},{1,9},{9,17},{17,25},{25,1},{2,10},{10... | collective-permute-start | bytes 786440 | tf_op jit(solution)/shard_map/ppermute | solution.py:282
  89.8 1.0 collective-permute-start.17
  90.8 1.4 %collective-permute-start.18 = (f32[512,128]{1,0:T(8,128)S(1)}, f32[512,128]{1,0:T(8,128)S(1)}, u32[]{:S(2)}, u32[]{:S(2)}) collective-permute-start(f32[512,128]{1,0:T(8,128)S(1)} %get-tuple-element.20), channel_id=1, source_target_pairs={{0,24},{8,0},{16,8},{24,16},{1,25},{9,1},{17,9},{25,17},{2,26},{10... | collective-permute-start | bytes 786440 | tf_op jit(solution)/shard_map/ppermute | solution.py:282
  92.2 0.1 pad_add_fusion.slabs
  92.3 15.0 %collective-permute-done.16.refs_1_ = f32[512,128]{1,0:T(8,128)S(1)} collective-permute-done((f32[512,128]{1,0:T(8,128)S(1)}, f32[512,128]{1,0:T(8,128)S(1)}, u32[]{:S(2)}, u32[]{:S(2)}) %collective-permute-start.16) | collective-permute-done | bytes 262176 | tf_op jit(solution)/shard_map/ppermute | solution.py:282
  107.2 3.3 %collective-permute-done.17.refs_2_ = f32[512,128]{1,0:T(8,128)S(1)} collective-permute-done((f32[512,128]{1,0:T(8,128)S(1)}, f32[512,128]{1,0:T(8,128)S(1)}, u32[]{:S(2)}, u32[]{:S(2)}) %collective-permute-start.17) | collective-permute-done | bytes 262176 | tf_op jit(solution)/shard_map/ppermute | solution.py:282
  110.5 1.3 %collective-permute-done.18.refs_3_ = f32[512,128]{1,0:T(8,128)S(1)} collective-permute-done((f32[512,128]{1,0:T(8,128)S(1)}, f32[512,128]{1,0:T(8,128)S(1)}, u32[]{:S(2)}, u32[]{:S(2)}) %collective-permute-start.18) | collective-permute-done | bytes 262176 | tf_op jit(solution)/shard_map/ppermute | solution.py:282
  111.8 1.7 %result.1 = f32[2,16,64,128]{3,2,1,0:T(8,128)} custom-call(s32[4]{0:T(128)S(1)} %pad_add_fusion.slabs, f32[2,16,64,128]{3,2,1,0:T(8,128)S(1)} %copy-done.1, s32[16,64,128]{2,1,0:T(8,128)S(1)} %copy-done.2, f32[512,128]{1,0:T(8,128)S(1)} %get-tuple-element.17.refs_0_, f32[512,128]{1,0:T(8,128)S(1)} %collective-permute-done.16.refs_1_, ...), custom_call_target="tpu_custom_call" | custom-call | tf_op jit(solution)/shard_map/result/pallas_call | solution.py:245
  (26 shorter events, 0.2 us)
Async XLA Ops:
  0.0 4.8 %copy-start.2 = (s32[16,64,128]{2,1,0:T(8,128)S(1)}, s32[16,64,128]{2,1,0:T(8,128)}, u32[]{:S(2)}) copy-start(s32[16,64,128]{2,1,0:T(8,128)} %mask.11) | copy-start | bytes 1572868
  1.7 10.2 %collective-permute-start.7 = (s32[1,128]{1,0:T(1,128)}, s32[1,128]{1,0:T(1,128)S(1)}, u32[]{:S(2)}, u32[]{:S(2)}) collective-permute-start(s32[1,128]{1,0:T(1,128)} %slice.80), channel_id=1, source_target_pairs={{4,0},{0,4},{5,1},{1,5},{6,2},{2,6},{7,3},{3,7},{12,8},{8,12},{13,... | collective-permute-start | bytes 1544 | tf_op jit(solution)/shard_map/ppermute | solution.py:304
  1.9 10.0 %collective-permute-start.8 = (s32[64,1]{1,0:T(8,128)S(1)}, s32[64,1]{1,0:T(8,128)S(1)}, u32[]{:S(2)}, u32[]{:S(2)}) collective-permute-start(s32[64,1]{1,0:T(8,128)S(1)} %bitcast.34), channel_id=1, source_target_pairs={{1,0},{2,1},{3,2},{5,4},{6,5},{7,6},{9,8},{10,9},{11,10},{13,12},{... | collective-permute-start | bytes 776 | tf_op jit(solution)/shard_map/ppermute | solution.py:305
  4.8 1.2 %copy-start = (f32[2,16,64,128]{3,2,1,0:T(8,128)S(1)}, f32[2,16,64,128]{3,2,1,0:T(8,128)}, u32[]{:S(2)}) copy-start(f32[2,16,64,128]{3,2,1,0:T(8,128)} %gain.9) | copy-start | bytes 3145732
  6.1 1.2 %copy-start.3 = (f32[2,16,64,128]{3,2,1,0:T(8,128)S(1)}, f32[2,16,64,128]{3,2,1,0:T(8,128)}, u32[]{:S(2)}) copy-start(f32[2,16,64,128]{3,2,1,0:T(8,128)} %increment.7) | copy-start | bytes 3145732
  7.3 1.3 %copy-start.1 = (f32[2,16,64,128]{3,2,1,0:T(8,128)S(1)}, f32[2,16,64,128]{3,2,1,0:T(8,128)}, u32[]{:S(2)}) copy-start(f32[2,16,64,128]{3,2,1,0:T(8,128)} %gain.9) | copy-start | bytes 3145732
  7.3 1.6 %copy-start.4 = (f32[2,16,64,128]{3,2,1,0:T(8,128)S(1)}, f32[2,16,64,128]{3,2,1,0:T(8,128)}, u32[]{:S(2)}) copy-start(f32[2,16,64,128]{3,2,1,0:T(8,128)} %increment.7) | copy-start | bytes 3145732
  8.0 49.6 %collective-permute-start.2 = (f32[528,128]{1,0:T(8,128)}, f32[528,128]{1,0:T(8,128)S(1)}, u32[]{:S(2)}, u32[]{:S(2)}) collective-permute-start(f32[528,128]{1,0:T(8,128)} %scaled_message.7), channel_id=1, source_target_pairs={{0,24},{8,0},{16,8},{24,16},{1,25},{9,1},{17,9},{25,17},{2,26},{10... | collective-permute-start | bytes 811016 | tf_op jit(solution)/shard_map/ppermute | solution.py:282
  8.9 3.0 %copy-start.5 = (f32[16,64,128]{2,1,0:T(8,128)S(1)}, f32[16,64,128]{2,1,0:T(8,128)}, u32[]{:S(2)}) copy-start(f32[16,64,128]{2,1,0:T(8,128)} %along_i.1) | copy-start | bytes 1572868
  9.7 48.0 %collective-permute-start = (f32[528,128]{1,0:T(8,128)}, f32[528,128]{1,0:T(8,128)}, u32[]{:S(2)}, u32[]{:S(2)}) collective-permute-start(f32[528,128]{1,0:T(8,128)} %scaled_message.5), channel_id=1, source_target_pairs={{0,8},{8,16},{16,24},{24,0},{1,9},{9,17},{17,25},{25,1},{2,10},{10... | collective-permute-start | bytes 811016 | tf_op jit(solution)/shard_map/ppermute | solution.py:282
  11.9 1.0 copy-start.6
  15.9 4.9 %copy-start.9 = (f32[512,128]{1,0:T(8,128)}, f32[512,128]{1,0:T(8,128)S(1)}, u32[]{:S(2)}) copy-start(f32[512,128]{1,0:T(8,128)S(1)} %get-tuple-element.13.refs_0_) | copy-start | bytes 786436
  15.9 14.4 %collective-permute-start.9 = (f32[512,128]{1,0:T(8,128)}, f32[512,128]{1,0:T(8,128)}, u32[]{:S(2)}, u32[]{:S(2)}) collective-permute-start(f32[512,128]{1,0:T(8,128)} %get-tuple-element.14), channel_id=1, source_target_pairs={{0,8},{8,16},{16,24},{24,0},{1,9},{9,17},{17,25},{25,1},{2,10},{10... | collective-permute-start | bytes 786440 | tf_op jit(solution)/shard_map/ppermute | solution.py:282
  17.2 34.5 %collective-permute-start.10 = (f32[512,128]{1,0:T(8,128)}, f32[512,128]{1,0:T(8,128)}, u32[]{:S(2)}, u32[]{:S(2)}) collective-permute-start(f32[512,128]{1,0:T(8,128)} %get-tuple-element.15), channel_id=1, source_target_pairs={{0,16},{8,24},{16,0},{24,8},{1,17},{9,25},{17,1},{25,9},{2,18},{10... | collective-permute-start | bytes 786440 | tf_op jit(solution)/shard_map/ppermute | solution.py:282
  19.3 32.5 %collective-permute-start.11 = (f32[512,128]{1,0:T(8,128)}, f32[512,128]{1,0:T(8,128)}, u32[]{:S(2)}, u32[]{:S(2)}) collective-permute-start(f32[512,128]{1,0:T(8,128)} %get-tuple-element.16), channel_id=1, source_target_pairs={{0,24},{8,0},{16,8},{24,16},{1,25},{9,1},{17,9},{25,17},{2,26},{10... | collective-permute-start | bytes 786440 | tf_op jit(solution)/shard_map/ppermute | solution.py:282
  20.8 0.7 copy-start.7
  21.6 8.7 %copy-start.8 = (f32[528,128]{1,0:T(8,128)S(1)}, f32[528,128]{1,0:T(8,128)}, u32[]{:S(2)}) copy-start(f32[528,128]{1,0:T(8,128)} %copy-done.7) | copy-start | bytes 811012
  30.3 27.3 %collective-permute-start.1 = (f32[528,128]{1,0:T(8,128)S(1)}, f32[528,128]{1,0:T(8,128)S(1)}, u32[]{:S(2)}, u32[]{:S(2)}) collective-permute-start(f32[528,128]{1,0:T(8,128)S(1)} %copy-done.8), channel_id=1, source_target_pairs={{0,16},{8,24},{16,0},{24,8},{1,17},{9,25},{17,1},{25,9},{2,18},{10... | collective-permute-start | bytes 811016 | tf_op jit(solution)/shard_map/ppermute | solution.py:282
  51.8 1.0 copy-start.10
  56.1 7.5 %collective-permute-start.13 = (f32[4,128,128]{2,1,0:T(8,128)S(1)}, f32[4,128,128]{2,1,0:T(8,128)S(1)}, u32[]{:S(2)}, u32[]{:S(2)}) collective-permute-start(f32[4,128,128]{2,1,0:T(8,128)S(1)} %get-tuple-element.23), channel_id=1, source_target_pairs={{8,0},{16,8},{24,16},{28,24},{20,28},{12,20},{4,12},{0,4},{9,1},{1... | collective-permute-start | bytes 786440 | tf_op jit(solution)/shard_map/ppermute | solution.py:293
  56.2 9.4 %collective-permute-start.12 = (f32[4,128,128]{2,1,0:T(8,128)S(1)}, f32[4,128,128]{2,1,0:T(8,128)S(1)}, u32[]{:S(2)}, u32[]{:S(2)}) collective-permute-start(f32[4,128,128]{2,1,0:T(8,128)S(1)} %get-tuple-element.24), channel_id=1, source_target_pairs={{0,8},{8,16},{16,24},{24,28},{28,20},{20,12},{12,4},{4,0},{1,9},{9... | collective-permute-start | bytes 786440 | tf_op jit(solution)/shard_map/ppermute | solution.py:292
  60.7 11.7 %collective-permute-start.4 = (f32[4,128,128]{2,1,0:T(8,128)S(1)}, f32[4,128,128]{2,1,0:T(8,128)S(1)}, u32[]{:S(2)}, u32[]{:S(2)}) collective-permute-start(f32[4,128,128]{2,1,0:T(8,128)S(1)} %get-tuple-element.27), channel_id=1, source_target_pairs={{8,0},{16,8},{24,16},{28,24},{20,28},{12,20},{4,12},{0,4},{9,1},{1... | collective-permute-start | bytes 786440 | tf_op jit(solution)/shard_map/ppermute | solution.py:293
  62.4 10.0 %collective-permute-start.3 = (f32[4,128,128]{2,1,0:T(8,128)S(1)}, f32[4,128,128]{2,1,0:T(8,128)S(1)}, u32[]{:S(2)}, u32[]{:S(2)}) collective-permute-start(f32[4,128,128]{2,1,0:T(8,128)S(1)} %get-tuple-element.28), channel_id=1, source_target_pairs={{0,8},{8,16},{16,24},{24,28},{28,20},{20,12},{12,4},{4,0},{1,9},{9... | collective-permute-start | bytes 786440 | tf_op jit(solution)/shard_map/ppermute | solution.py:292
  65.6 12.4 %collective-permute-start.14 = (f32[24,8,128]{2,1,0:T(8,128)S(1)}, f32[24,8,128]{2,1,0:T(8,128)S(1)}, u32[]{:S(2)}, u32[]{:S(2)}) collective-permute-start(f32[24,8,128]{2,1,0:T(8,128)S(1)} %pad_maximum_fusion.2), channel_id=1, source_target_pairs={{0,1},{1,2},{2,3},{4,5},{5,6},{6,7},{8,9},{9,10},{10,11},{12,13},{... | collective-permute-start | bytes 294920 | tf_op jit(solution)/shard_map/ppermute | solution.py:296
  70.5 7.6 %collective-permute-start.15 = (f32[24,8,128]{2,1,0:T(8,128)S(1)}, f32[24,8,128]{2,1,0:T(8,128)S(1)}, u32[]{:S(2)}, u32[]{:S(2)}) collective-permute-start(f32[24,8,128]{2,1,0:T(8,128)S(1)} %pad_maximum_fusion.3), channel_id=1, source_target_pairs={{1,0},{2,1},{3,2},{5,4},{6,5},{7,6},{9,8},{10,9},{11,10},{13,12},{... | collective-permute-start | bytes 294920 | tf_op jit(solution)/shard_map/ppermute | solution.py:297
  72.5 5.6 %collective-permute-start.5 = (f32[24,8,128]{2,1,0:T(8,128)S(1)}, f32[24,8,128]{2,1,0:T(8,128)S(1)}, u32[]{:S(2)}, u32[]{:S(2)}) collective-permute-start(f32[24,8,128]{2,1,0:T(8,128)S(1)} %pad_maximum_fusion), channel_id=1, source_target_pairs={{0,1},{1,2},{2,3},{4,5},{5,6},{6,7},{8,9},{9,10},{10,11},{12,13},{... | collective-permute-start | bytes 294920 | tf_op jit(solution)/shard_map/ppermute | solution.py:296
  76.1 5.9 %collective-permute-start.6 = (f32[24,8,128]{2,1,0:T(8,128)S(1)}, f32[24,8,128]{2,1,0:T(8,128)S(1)}, u32[]{:S(2)}, u32[]{:S(2)}) collective-permute-start(f32[24,8,128]{2,1,0:T(8,128)S(1)} %pad_maximum_fusion.1), channel_id=1, source_target_pairs={{1,0},{2,1},{3,2},{5,4},{6,5},{7,6},{9,8},{10,9},{11,10},{13,12},{... | collective-permute-start | bytes 294920 | tf_op jit(solution)/shard_map/ppermute | solution.py:297
  88.3 18.9 %collective-permute-start.16 = (f32[512,128]{1,0:T(8,128)S(1)}, f32[512,128]{1,0:T(8,128)S(1)}, u32[]{:S(2)}, u32[]{:S(2)}) collective-permute-start(f32[512,128]{1,0:T(8,128)S(1)} %get-tuple-element.18), channel_id=1, source_target_pairs={{0,8},{8,16},{16,24},{24,0},{1,9},{9,17},{17,25},{25,1},{2,10},{10... | collective-permute-start | bytes 786440 | tf_op jit(solution)/shard_map/ppermute | solution.py:282
  89.8 20.7 %collective-permute-start.17 = (f32[512,128]{1,0:T(8,128)S(1)}, f32[512,128]{1,0:T(8,128)S(1)}, u32[]{:S(2)}, u32[]{:S(2)}) collective-permute-start(f32[512,128]{1,0:T(8,128)S(1)} %get-tuple-element.19), channel_id=1, source_target_pairs={{0,16},{8,24},{16,0},{24,8},{1,17},{9,25},{17,1},{25,9},{2,18},{10... | collective-permute-start | bytes 786440 | tf_op jit(solution)/shard_map/ppermute | solution.py:282
  90.8 21.0 %collective-permute-start.18 = (f32[512,128]{1,0:T(8,128)S(1)}, f32[512,128]{1,0:T(8,128)S(1)}, u32[]{:S(2)}, u32[]{:S(2)}) collective-permute-start(f32[512,128]{1,0:T(8,128)S(1)} %get-tuple-element.20), channel_id=1, source_target_pairs={{0,24},{8,0},{16,8},{24,16},{1,25},{9,1},{17,9},{25,17},{2,26},{10... | collective-permute-start | bytes 786440 | tf_op jit(solution)/shard_map/ppermute | solution.py:282

commit v2 on v1

v2 whole, which is shorter than its diff:
```python
import functools

import jax
import jax.numpy as jnp
from jax import lax
from jax.experimental import pallas as pl
from jax.experimental.pallas import tpu as pltpu
from jax.sharding import PartitionSpec as P

ITERS = 2
STEPS = 2 * ITERS
PAD = 8
PARTS = 2
VMEM_LIMIT = 40 * 1024 * 1024
VMEM_WHOLE = 60 * 1024 * 1024
HIGHEST = lax.Precision.HIGHEST


def params(limit=VMEM_LIMIT):
    return pltpu.CompilerParams(vmem_limit_bytes=limit)


def smem():
    return pl.BlockSpec(memory_space=pltpu.SMEM)


def vmem():
    return pl.BlockSpec(memory_space=pltpu.VMEM)


def groups_of(slots, d, groups, cols):
    width = cols // groups
    return [lax.rem((group - slots[d]) * width + cols, cols) for group in range(groups)]


def pack(blocks, shifts, group):
    out = pltpu.roll(blocks[0], shifts[0], 1)
    for a in range(1, len(blocks)):
        out = jnp.where(group == a, pltpu.roll(blocks[a], shifts[a], 1), out)
    return out


def scaled_kernel(slots, increment, gain, mask, *refs):
    outs, total = refs[:-1], refs[-1]
    fields, some, length, cols = increment.shape
    groups = len(outs)
    rows = length // groups
    count = outs[0].shape[0] // rows - 1
    levels = count // fields
    group = lax.broadcasted_iota(jnp.int32, (rows, cols), 1) // (cols // groups)
    step = pl.program_id(0)
    shifts = [groups_of(slots, d, groups, cols) for d in range(groups)]

    @pl.when(step == 0)
    def _():
        total[...] = jnp.zeros_like(total)

    for level in range(some):
        ocean = mask[level].astype(jnp.float32)
        total[...] += ocean
        for field in range(fields):
            x = ocean * gain[field, level] * increment[field, level]
            blocks = [x[a * rows:(a + 1) * rows] for a in range(groups)]
            at = pl.multiple_of((field * levels + step * some + level) * rows, rows)
            for d, out in enumerate(outs):
                out[pl.ds(at, rows), :] = pack(blocks, shifts[d], group)

    @pl.when(step == pl.num_programs(0) - 1)
    def _():
        blocks = [total[pl.ds(a * rows, rows), :] for a in range(groups)]
        for d, out in enumerate(outs):
            out[pl.ds(count * rows, rows), :] = pack(blocks, shifts[d], group)


def scaled_messages(slots, increment, gain, mask):
    fields, levels, length, cols = increment.shape
    groups = slots.shape[0]
    rows = length // groups
    some = 4
    block = pl.BlockSpec((fields, some, length, cols), lambda step, slots: (0, step, 0, 0))
    mask_block = pl.BlockSpec((some, length, cols), lambda step, slots: (step, 0, 0))
    shape = ((fields * levels + 1) * rows, cols)
    whole = lambda step, slots: (0, 0)
    *messages, depth = pl.pallas_call(
        scaled_kernel,
        grid_spec=pltpu.PrefetchScalarGridSpec(
            num_scalar_prefetch=1,
            grid=(levels // some,),
            in_specs=[block, block, mask_block],
            out_specs=[pl.BlockSpec(shape, whole)] * groups + [pl.BlockSpec((length, cols), whole)],
        ),
        out_shape=[jax.ShapeDtypeStruct(shape, jnp.float32)] * groups
        + [jax.ShapeDtypeStruct((length, cols), jnp.float32)],
        compiler_params=params(VMEM_WHOLE),
        name="scaled_messages",
    )(slots, increment, gain, mask)
    return messages, depth


def weight_kernel(along_i, along_j, mask, next_tile, right_tile, out, edge):
    levels, length, cols = along_i.shape
    lane = lax.broadcasted_iota(jnp.int32, (length, cols), 1)
    row = lax.broadcasted_iota(jnp.int32, (length, cols), 0)
    next_row = jnp.broadcast_to(next_tile[pl.ds(0, 1), :], (length, cols))
    next_col = pltpu.roll(right_tile[...], cols - 1, 1)

    def one(level, carry):
        at = level.astype(jnp.float32)
        ocean = mask[level].astype(jnp.float32)
        below = jnp.where(row == length - 1, (at < next_row).astype(jnp.float32), pltpu.roll(ocean, length - 1, 0))
        right = jnp.where(lane == cols - 1, (at < next_col).astype(jnp.float32), pltpu.roll(ocean, cols - 1, 1))
        for side, weight in ((0, along_i[level] * ocean * below), (1, along_j[level] * ocean * right)):
            index = side * levels + level
            out[index] = weight
            edge[index, pl.ds(0, STEPS), :] = weight[:STEPS]
            edge[index, pl.ds(STEPS, STEPS), :] = weight[length - STEPS:]
        return carry

    lax.fori_loop(0, levels, one, 0, unroll=2)


def tile_weights(along_i, along_j, mask, next_tile, right_tile):
    levels, length, cols = along_i.shape
    return pl.pallas_call(
        weight_kernel,
        in_specs=[vmem()] * 5,
        out_specs=[vmem()] * 2,
        out_shape=[
            jax.ShapeDtypeStruct((2 * levels, length, cols), jnp.float32),
            jax.ShapeDtypeStruct((2 * levels, 2 * STEPS, cols), jnp.float32),
        ],
        compiler_params=params(),
        name="tile_weights",
    )(along_i, along_j, mask, next_tile, right_tile)


def pack_kernel(first, slots, weight, above, below, *refs):
    outs, held = refs[:-1], refs[-1]
    count, length, cols = weight.shape
    groups = len(outs)
    rows = outs[0].shape[0] // count
    group = lax.broadcasted_iota(jnp.int32, (rows, cols), 1) // (cols // groups)
    shifts = [groups_of(slots, d, groups, cols) for d in range(groups)]
    unroll = held.shape[0]

    def some(outer, carry):
        for k in range(unroll):
            index = outer * unroll + k
            held[k, pl.ds(0, STEPS), :] = above[index]
            held[k, pl.ds(STEPS, length), :] = weight[index]
            held[k, pl.ds(STEPS + length, STEPS), :] = below[index]
        blocks = [[held[k, pl.ds(first + a * rows, rows), :] for a in range(groups)] for k in range(unroll)]
        at = pl.multiple_of(outer * unroll * rows, 8)
        for d, out in enumerate(outs):
            packed = [pack(blocks[k], shifts[d], group) for k in range(unroll)]
            out[pl.ds(at, unroll * rows), :] = jnp.concatenate(packed, axis=0)
        return carry

    lax.fori_loop(0, count // unroll, some, 0)


def weight_messages(first, rows, slots, weight, above, below):
    count, length, cols = weight.shape
    groups = slots.shape[0]
    shape = jax.ShapeDtypeStruct((count * rows // groups, cols), jnp.float32)

    def kernel(slots, weight, above, below, *refs):
        pack_kernel(first, slots, weight, above, below, *refs)

    return pl.pallas_call(
        kernel,
        in_specs=[smem()] + [vmem()] * 3,
        out_specs=[vmem()] * groups,
        out_shape=[shape] * groups,
        scratch_shapes=[pltpu.VMEM((4, length + 2 * STEPS, cols), jnp.float32)],
        compiler_params=params(),
        name="weight_messages",
    )(slots, weight, above, below)


def adjoint_kernel(matrix, *refs):
    parts, out = refs[:-1], refs[-1]
    length, width, order = out.shape
    groups = len(parts)
    rows = length // groups
    cols = groups * width
    count = order // groups
    level = lax.rem(lax.broadcasted_iota(jnp.int32, (order, cols), 0), order // 2).astype(jnp.float32)

    def one(i, carry):
        x = jnp.concatenate([part[pl.ds(i, count, rows), :] for part in parts], axis=0)
        depth = sum(part[pl.ds(count * rows + i, 1), :] for part in parts)
        y = jnp.dot(matrix[...], x, precision=HIGHEST, preferred_element_type=jnp.float32)
        y = jnp.where(level < depth, y, 0.0).T
        for a in range(groups):
            out[a * rows + i] = y[a * width:(a + 1) * width]
        return carry

    lax.fori_loop(0, rows, one, 0, unroll=4)


def adjoint_mix(matrix, parts, length, width):
    return pl.pallas_call(
        adjoint_kernel,
        in_specs=[vmem()] * (1 + len(parts)),
        out_specs=vmem(),
        out_shape=jax.ShapeDtypeStruct((length, width, matrix.shape[0]), jnp.float32),
        compiler_params=params(),
        name="adjoint_mix",
    )(matrix, *parts)


def turn_kernel(sources, *refs):
    parts, out, held = refs[:-2], refs[-2], refs[-1]
    length, width, order = out.shape
    groups = len(parts)
    rows = length // groups
    half = order // 2
    count = half // groups
    for i in range(rows):
        for d, part in enumerate(parts):
            for side in range(2):
                at = pl.multiple_of(side * half + sources[d] * count, 8)
                held[i, pl.ds(at, count), :] = part[pl.ds(side * count * rows + i, count, rows), :]
    for i in range(rows):
        turned = held[i].T
        for a in range(groups):
            out[a * rows + i] = turned[a * width:(a + 1) * width]


def turn_weights(sources, parts, order):
    groups = len(parts)
    cols = parts[0].shape[1]
    rows = parts[0].shape[0] * groups // order
    return pl.pallas_call(
        turn_kernel,
        in_specs=[smem()] + [vmem()] * groups,
        out_specs=vmem(),
        out_shape=jax.ShapeDtypeStruct((rows * groups, cols // groups, order), jnp.float32),
        scratch_shapes=[pltpu.VMEM((rows, order, cols), jnp.float32)],
        compiler_params=params(),
        name="turn_weights",
    )(sources, *parts)


def spread_kernel(first, pieces, matrix, *refs):
    field, weights = refs[:5], refs[5:5 + 3 * len(pieces)]
    outs, (a, b, wi, wj) = refs[5 + 3 * len(pieces):-4], refs[-4:]
    length, width, order = field[0].shape
    half = order // 2
    ext, wide, _ = a.shape
    lane = lax.broadcasted_iota(jnp.int32, (wide, order), 1)
    nothing = jnp.zeros((PAD - STEPS, order), jnp.float32)

    def widen(left, mid, right):
        return jnp.concatenate([nothing, left, mid, right, nothing], axis=0)

    for e in range(ext):
        r = first + e
        main, above, below, left, right = field
        if r < STEPS:
            mid = above[r]
        elif r < STEPS + length:
            mid = main[r - STEPS]
        else:
            mid = below[r - STEPS - length]
        a[e] = widen(left[r], mid, right[r])
        piece = [k for k, (at, rows) in enumerate(pieces) if at <= r < at + rows][0]
        main, left, right = weights[3 * piece:3 * piece + 3]
        k = r - pieces[piece][0]
        w = widen(left[k], main[k], right[k])
        other = pltpu.roll(w, half, 1)
        wi[e] = jnp.where(lane < half, w, other)
        wj[e] = jnp.where(lane < half, other, w)

    src, dst = a, b
    for step in range(STEPS):
        begin, last = step + 1, ext - 2 - step

        def one(r, carry, src=src, dst=dst):
            v, before = carry
            after = src[r + 1]
            flux = wi[r] * (after - v)
            across = wj[r] * (pltpu.roll(v, wide - 1, 0) - v)
            dst[r] = v + (flux - before) + (across - pltpu.roll(across, 1, 0))
            return after, flux

        v = src[begin]
        lax.fori_loop(begin, last + 1, one, (v, wi[begin - 1] * (v - src[begin - 1])), unroll=2)
        src, dst = dst, src

    groups = len(outs)
    count = order // groups
    rows = (ext - 2 * STEPS) // groups

    def mix(i, carry):
        x = jnp.concatenate([src[STEPS + g * rows + i, pl.ds(PAD, width), :] for g in range(groups)], axis=0)
        y = lax.dot_general(
            matrix[...], x, (((1,), (1,)), ((), ())), precision=HIGHEST, preferred_element_type=jnp.float32
        )
        for d, out in enumerate(outs):
            out[pl.ds(i, count, rows), :] = y[d * count:(d + 1) * count]
        return carry

    lax.fori_loop(0, rows, mix, 0, unroll=4)


def spread_mix(first, last, pieces, matrix, field, weights, groups):
    length, width, order = field[0].shape
    cols = width * groups
    rows = (last - first - 2 * STEPS) // groups
    shape = jax.ShapeDtypeStruct((order // groups * rows, cols), jnp.float32)
    ext = pltpu.VMEM((last - first, width + 2 * PAD, order), jnp.float32)

    def kernel(matrix, *refs):
        spread_kernel(first, pieces, matrix, *refs)

    return pl.pallas_call(
        kernel,
        in_specs=[vmem()] * (1 + len(field) + len(weights)),
        out_specs=[vmem()] * groups,
        out_shape=[shape] * groups,
        scratch_shapes=[ext] * 4,
        compiler_params=params(),
        name="spread_mix",
    )(matrix, *field, *weights)


def result_kernel(slots, gain, mask, *refs):
    parts, out = refs[:-1], refs[-1]
    fields, levels, length, cols = gain.shape
    groups = len(parts) // PARTS
    rows = parts[0].shape[0] // (fields * levels)
    group = lax.broadcasted_iota(jnp.int32, (rows, cols), 1) // (cols // groups)
    shifts = [[lax.rem((slots[d] - a) * (cols // groups) + cols, cols) for a in range(groups)] for d in range(groups)]

    def one(level, carry):
        for field in range(fields):
            at = pl.multiple_of((field * levels + level) * rows, rows)
            for part in range(PARTS):
                values = [parts[part * groups + d][pl.ds(at, rows), :] for d in range(groups)]
                for a in range(groups):
                    x = pltpu.roll(values[0], shifts[0][a], 1)
                    for d in range(1, groups):
                        x = jnp.where(group == slots[d], pltpu.roll(values[d], shifts[d][a], 1), x)
                    here = pl.ds((part * groups + a) * rows, rows)
                    ocean = mask[level, here, :].astype(jnp.float32)
                    out[field, level, here, :] = ocean * gain[field, level, here, :] * x
        return carry

    lax.fori_loop(0, levels, one, 0, unroll=2)


def result(slots, gain, mask, parts):
    return pl.pallas_call(
        result_kernel,
        in_specs=[smem()] + [vmem()] * (2 + len(parts)),
        out_specs=vmem(),
        out_shape=jax.ShapeDtypeStruct(gain.shape, jnp.float32),
        compiler_params=params(),
        name="result",
    )(slots, gain, mask, *parts)


def shards(increment, norm_gain, diffusion_i, diffusion_j, sea_mask, coupling):
    devices = lax.axis_size("lev")
    gx_size = lax.axis_size("gx")
    gy_size = lax.axis_size("gy")
    me = lax.axis_index("lev")
    gy = lax.axis_index("gy")
    _, levels, length, cols = increment.shape
    width = cols // devices
    order = coupling.shape[0]

    def place(y, slot):
        return devices - 1 - slot if y % 2 else slot

    def slot_of(lev):
        return jnp.where(gy % 2 == 1, devices - 1 - lev, lev)

    to = [lax.rem(me + d, devices) for d in range(devices)]
    source = [lax.rem(me + devices - d, devices) for d in range(devices)]
    to_slots = jnp.stack([slot_of(t) for t in to]).astype(jnp.int32)
    source_slots = jnp.stack([slot_of(s) for s in source]).astype(jnp.int32)
    sources = jnp.stack(source).astype(jnp.int32)

    def exchange(parts):
        return [parts[0]] + [
            lax.ppermute(parts[d], "lev", [(k, (k + d) % devices) for k in range(devices)]) for d in range(1, devices)
        ]

    up = [((k + 1) % gx_size, k) for k in range(gx_size)]
    down = [(b, a) for a, b in up]
    right = [(k, k + 1) for k in range(gy_size - 1)]
    left = [(b, a) for a, b in right]
    chain = [place(y, slot) * gy_size + y for y in range(gy_size) for slot in range(devices)]
    ahead = list(zip(chain[:-1], chain[1:]))
    back = [(b, a) for a, b in ahead]

    def halo_i(edge, axis):
        first, last = lax.split(edge, (STEPS, STEPS), axis)
        if gx_size == 2:
            below, above = lax.split(lax.ppermute(edge, "gx", up), (STEPS, STEPS), axis)
            return above, below
        return lax.ppermute(last, "gx", down), lax.ppermute(first, "gx", up)

    def halo_j(first, last):
        return lax.ppermute(last, ("lev", "gy"), ahead), lax.ppermute(first, ("lev", "gy"), back)

    messages, depth = scaled_messages(to_slots, increment, norm_gain, sea_mask)
    scaled = exchange(messages)
    next_tile = lax.ppermute(depth, "gx", up)
    right_tile = lax.ppermute(depth, "gy", left)
    weight, edge = tile_weights(diffusion_i, diffusion_j, sea_mask, next_tile, right_tile)
    weight_above, weight_below = halo_i(edge, 1)

    part = length // PARTS
    pieces = [(0, part + 2 * STEPS)] + [(k * part + 2 * STEPS, part) for k in range(1, PARTS)]

    def send(piece, weight):
        return exchange(weight_messages(*piece, to_slots, weight, weight_above, weight_below))

    arrived = [send(pieces[0], weight)]

    balance = jnp.eye(order, dtype=jnp.float32) + coupling
    by_device = balance.reshape(2, devices, levels, order)
    adjoint = jnp.concatenate([by_device[:, s].reshape(2 * levels, order) for s in source], axis=0).T
    forward = jnp.concatenate([by_device[:, t].reshape(2 * levels, order) for t in to], axis=0)

    mixed = adjoint_mix(adjoint, scaled, length, width)
    above, below = halo_i(jnp.concatenate([mixed[:STEPS], mixed[-STEPS:]], axis=0), 0)
    above, weight = lax.optimization_barrier((above, weight))
    tall = [above, mixed, below]
    field = [mixed, above, below] + list(
        halo_j(
            jnp.concatenate([x[:, :STEPS] for x in tall], axis=0),
            jnp.concatenate([x[:, -STEPS:] for x in tall], axis=0),
        )
    )

    field, arrived = lax.optimization_barrier((field, arrived))

    turned, out = [], []
    for k in range(PARTS):
        if k > 0:
            arrived.append(send(pieces[k], weight))
        here = turn_weights(sources, arrived[k], order)
        turned += [here, *halo_j(here[:, :STEPS], here[:, -STEPS:])]
        first, last = k * part, (k + 1) * part + 2 * STEPS
        out += exchange(spread_mix(first, last, pieces[:k + 1], forward, field, turned, devices))
    return result(source_slots, norm_gain, sea_mask, out)


def solution(mesh):
    return jax.shard_map(
        shards,
        mesh=mesh,
        in_specs=(
            P(None, "lev", "gx", "gy"),
            P(None, "lev", "gx", "gy"),
            P("lev", "gx", "gy"),
            P("lev", "gx", "gy"),
            P("lev", "gx", "gy"),
            P(),
        ),
        out_specs=P(None, "lev", "gx", "gy"),
        check_vma=False,
    )
```

time: 114 us -> 124 us (1.088)
  the two profiles are of different devices: /device:TPU:11 before, /device:TPU:0 now
where the time goes in v2:
time: 124 us; the launch traced here: 123 us
  starting transfers between devices  57 us (46%)
  waiting for transfers between devices  39.6 us (32%)
  Pallas kernels  24 us (19%)
  other arithmetic  1.53 us (1%)
    ppermute x15, starting transfers between devices, exchange(): lax.ppermute(parts[d], 'lev', [(k, (k + d) % devices) for k in range(devi...  32.5 us
    ppermute x15, waiting for transfers between devices, exchange(): lax.ppermute(parts[d], 'lev', [(k, (k + d) % devices) for k in range(devi...  22.9 us
    ppermute x3, starting transfers between devices, halo_j(): lax.ppermute(last, ('lev', 'gy'), ahead)  15.3 us
    ppermute x2, waiting for transfers between devices, halo_i(): below, above = lax.split(lax.ppermute(edge, 'gx', up), (STEPS, STEPS), axis)  10.2 us
    pallas_call x2, Pallas kernels, spread_mix(): pl.pallas_call(kernel, in_specs=[vmem()] * (1 + len(field) + len(weights)...  6.49 us
    pallas_call x1, Pallas kernels, scaled_messages(): pl.pallas_call(scaled_kernel, grid_spec=pltpu.PrefetchScalarGridSpec(num_...  5.2 us
    ppermute x3, waiting for transfers between devices, halo_j(): lax.ppermute(first, ('lev', 'gy'), back)  4.14 us
    pallas_call x2, Pallas kernels, weight_messages(): pl.pallas_call(kernel, in_specs=[smem()] + [vmem()] * 3, out_specs=[vmem(...  4 us
  transfers between devices with their start and end apart: 25, of which 11 were waited for; matrix products, arithmetic and copies ran while one was open for 1% of the time, Pallas kernels for 9%

profile of v2, /device:TPU:0, one launch (start us, length us, event | category | flops | bytes accessed | tf_op | source)
XLA Modules:
  0.0 123.4 jit_solution(17377768080102017215)
XLA Ops:
  0.0 0.7 pad_add_fusion.1.slots
  0.7 5.2 %scaled_messages.1 = (f32[528,128]{1,0:T(8,128)}, f32[528,128]{1,0:T(8,128)}, f32[528,128]{1,0:T(8,128)}, f32[528,128]{1,0:T(8,128)}, f32[64,128]{1,0:T(8,128)}) custom-call(s32[4]{0:T(128)} %pad_add_fusion.1.slots, f32[2,16,64,128]{3,2,1,0:T(8,128)} %increment.1, f32[2,16,64,128]{3,2,1,0:T(8,128)} %gain.3, s32[16,64,128]{2,1,0:T(8,128)} %mask.5), custom_call_target="tpu_custom_call" | custom-call | tf_op jit(solution)/shard_map/scaled_messages/pallas_call | solution.py:84
  5.9 2.9 %collective-permute-start.4 = (f32[64,128]{1,0:T(8,128)}, f32[64,128]{1,0:T(8,128)S(1)}, u32[]{:S(2)}, u32[]{:S(2)}) collective-permute-start(f32[64,128]{1,0:T(8,128)} %get-tuple-element.43), channel_id=1, source_target_pairs={{4,0},{0,4},{5,1},{1,5},{6,2},{2,6},{7,3},{3,7},{12,8},{8,12},{13,... | collective-permute-start | bytes 98312 | tf_op jit(solution)/shard_map/ppermute | solution.py:412
  8.8 1.3 %collective-permute-start.5 = (f32[64,128]{1,0:T(8,128)}, f32[64,128]{1,0:T(8,128)S(1)}, u32[]{:S(2)}, u32[]{:S(2)}) collective-permute-start(f32[64,128]{1,0:T(8,128)} %get-tuple-element.43), channel_id=1, source_target_pairs={{1,0},{2,1},{3,2},{5,4},{6,5},{7,6},{9,8},{10,9},{11,10},{13,12},{... | collective-permute-start | bytes 98312 | tf_op jit(solution)/shard_map/ppermute | solution.py:413
  10.1 1.6 %collective-permute-start = (f32[528,128]{1,0:T(8,128)}, f32[528,128]{1,0:T(8,128)S(1)}, u32[]{:S(2)}, u32[]{:S(2)}) collective-permute-start(f32[528,128]{1,0:T(8,128)} %get-tuple-element.40), channel_id=1, source_target_pairs={{0,8},{8,16},{16,24},{24,0},{1,9},{9,17},{17,25},{25,1},{2,10},{10... | collective-permute-start | bytes 811016 | tf_op jit(solution)/shard_map/ppermute | solution.py:389
  11.7 2.6 %collective-permute-start.1 = (f32[528,128]{1,0:T(8,128)}, f32[528,128]{1,0:T(8,128)S(1)}, u32[]{:S(2)}, u32[]{:S(2)}) collective-permute-start(f32[528,128]{1,0:T(8,128)} %get-tuple-element.41), channel_id=1, source_target_pairs={{0,16},{8,24},{16,0},{24,8},{1,17},{9,25},{17,1},{25,9},{2,18},{10... | collective-permute-start | bytes 811016 | tf_op jit(solution)/shard_map/ppermute | solution.py:389
  14.3 1.3 %collective-permute-start.2 = (f32[528,128]{1,0:T(8,128)}, f32[528,128]{1,0:T(8,128)S(1)}, u32[]{:S(2)}, u32[]{:S(2)}) collective-permute-start(f32[528,128]{1,0:T(8,128)} %get-tuple-element.42), channel_id=1, source_target_pairs={{0,24},{8,0},{16,8},{24,16},{1,25},{9,1},{17,9},{25,17},{2,26},{10... | collective-permute-start | bytes 811016 | tf_op jit(solution)/shard_map/ppermute | solution.py:389
  15.7 0.6 convert_add_fusion
  16.3 0.0 collective-permute-done.4.next_tile
  16.3 0.0 collective-permute-done.5.right_tile
  16.3 1.4 %tile_weights.1 = (f32[32,64,128]{2,1,0:T(8,128)S(1)}, f32[32,8,128]{2,1,0:T(8,128)}) custom-call(f32[16,64,128]{2,1,0:T(8,128)S(1)} %copy-done.2, f32[16,64,128]{2,1,0:T(8,128)S(1)} %copy-done.3, s32[16,64,128]{2,1,0:T(8,128)S(1)} %copy-done, f32[64,128]{1,0:T(8,128)S(1)} %collective-permute-done.4.next_tile, f32[64,128]{1,0:T(8,128)S(1)} %collective-permute-done.5.right_tile), custom_call_target="tpu_custom_call" | custom-call | tf_op jit(solution)/shard_map/tile_weights/pallas_call | solution.py:124
  17.8 0.5 collective-permute-start.8
  18.3 0.1 copy.12.matrix
  18.4 5.2 %collective-permute-done.8 = f32[32,8,128]{2,1,0:T(8,128)S(1)} collective-permute-done((f32[32,8,128]{2,1,0:T(8,128)}, f32[32,8,128]{2,1,0:T(8,128)S(1)}, u32[]{:S(2)}, u32[]{:S(2)}) %collective-permute-start.8) | collective-permute-done | bytes 131104 | tf_op jit(solution)/shard_map/ppermute | solution.py:403
  23.7 0.7 copy-done.5
  24.4 2.3 %weight_messages.2 = (f32[320,128]{1,0:T(8,128)S(1)}, f32[320,128]{1,0:T(8,128)S(1)}, f32[320,128]{1,0:T(8,128)S(1)}, f32[320,128]{1,0:T(8,128)S(1)}) custom-call(s32[4]{0:T(128)S(1)} %copy-done.5, f32[32,64,128]{2,1,0:T(8,128)S(1)} %get-tuple-element.64.weight, f32[32,4,128]{2,1,0:T(4,128)S(1)} %get-tuple-element.82.above, ...), custom_call_target="tpu_custom_call" | custom-call | tf_op jit(solution)/shard_map/weight_messages/pallas_call | solution.py:170
  26.6 0.6 collective-permute-start.10
  27.2 2.6 %collective-permute-start.11 = (f32[320,128]{1,0:T(8,128)S(1)}, f32[320,128]{1,0:T(8,128)S(1)}, u32[]{:S(2)}, u32[]{:S(2)}) collective-permute-start(f32[320,128]{1,0:T(8,128)S(1)} %get-tuple-element.50), channel_id=1, source_target_pairs={{0,24},{8,0},{16,8},{24,16},{1,25},{9,1},{17,9},{25,17},{2,26},{10... | collective-permute-start | bytes 491528 | tf_op jit(solution)/shard_map/ppermute | solution.py:389
  29.7 0.0 collective-permute-done.refs_1_
  29.7 3.7 %collective-permute-done.1.refs_2_ = f32[528,128]{1,0:T(8,128)S(1)} collective-permute-done((f32[528,128]{1,0:T(8,128)}, f32[528,128]{1,0:T(8,128)S(1)}, u32[]{:S(2)}, u32[]{:S(2)}) %collective-permute-start.1) | collective-permute-done | bytes 270368 | tf_op jit(solution)/shard_map/ppermute | solution.py:389
  33.4 0.0 collective-permute-done.2.refs_3_
  33.4 2.0 %adjoint_mix.1.refs_0_ = f32[64,32,128]{2,1,0:T(8,128)S(1)} custom-call(f32[128,128]{1,0:T(8,128)S(1)} %copy.12.matrix, f32[528,128]{1,0:T(8,128)S(1)} %copy-done.4, f32[528,128]{1,0:T(8,128)S(1)} %collective-permute-done.refs_1_, f32[528,128]{1,0:T(8,128)S(1)} %collective-permute-done.1.refs_2_, f32[528,128]{1,0:T(8,128)S(1)} %collective-permute-done.2.refs_3_), custom_call_target="tpu_custom_call" | custom-call | tf_op jit(solution)/shard_map/adjoint_mix/pallas_call | solution.py:203
  35.5 0.5 collective-permute-start.3
  36.0 5.0 %collective-permute-done.3 = f32[8,32,128]{2,1,0:T(8,128)S(1)} collective-permute-done((f32[8,32,128]{2,1,0:T(8,128)S(1)}, f32[8,32,128]{2,1,0:T(8,128)S(1)}, u32[]{:S(2)}, u32[]{:S(2)}) %collective-permute-start.3) | collective-permute-done | bytes 131104 | tf_op jit(solution)/shard_map/ppermute | solution.py:403
  41.0 1.7 %weight_messages.3 = (f32[256,128]{1,0:T(8,128)S(1)}, f32[256,128]{1,0:T(8,128)S(1)}, f32[256,128]{1,0:T(8,128)S(1)}, f32[256,128]{1,0:T(8,128)S(1)}) custom-call(s32[4]{0:T(128)S(1)} %copy-done.5, f32[32,64,128]{2,1,0:T(8,128)S(1)} %get-tuple-element.64.weight, f32[32,4,128]{2,1,0:T(4,128)S(1)} %get-tuple-element.82.above, ...), custom_call_target="tpu_custom_call" | custom-call | tf_op jit(solution)/shard_map/weight_messages/pallas_call | solution.py:170
  42.8 11.7 %collective-permute-start.17 = (f32[256,128]{1,0:T(8,128)S(1)}, f32[256,128]{1,0:T(8,128)S(1)}, u32[]{:S(2)}, u32[]{:S(2)}) collective-permute-start(f32[256,128]{1,0:T(8,128)S(1)} %get-tuple-element.66), channel_id=1, source_target_pairs={{0,8},{8,16},{16,24},{24,0},{1,9},{9,17},{17,25},{25,1},{2,10},{10... | collective-permute-start | bytes 393224 | tf_op jit(solution)/shard_map/ppermute | solution.py:389
  54.5 3.3 %collective-permute-start.18 = (f32[256,128]{1,0:T(8,128)S(1)}, f32[256,128]{1,0:T(8,128)S(1)}, u32[]{:S(2)}, u32[]{:S(2)}) collective-permute-start(f32[256,128]{1,0:T(8,128)S(1)} %get-tuple-element.67), channel_id=1, source_target_pairs={{0,16},{8,24},{16,0},{24,8},{1,17},{9,25},{17,1},{25,9},{2,18},{10... | collective-permute-start | bytes 393224 | tf_op jit(solution)/shard_map/ppermute | solution.py:389
  57.8 0.0 collective-permute-start.19
  57.8 3.8 %collective-permute-done.17.refs_1_ = f32[256,128]{1,0:T(8,128)S(1)} collective-permute-done((f32[256,128]{1,0:T(8,128)S(1)}, f32[256,128]{1,0:T(8,128)S(1)}, u32[]{:S(2)}, u32[]{:S(2)}) %collective-permute-start.17) | collective-permute-done | bytes 131104 | tf_op jit(solution)/shard_map/ppermute | solution.py:389
  61.7 0.0 collective-permute-start.9
  61.7 5.6 %collective-permute-done.18.refs_2_ = f32[256,128]{1,0:T(8,128)S(1)} collective-permute-done((f32[256,128]{1,0:T(8,128)S(1)}, f32[256,128]{1,0:T(8,128)S(1)}, u32[]{:S(2)}, u32[]{:S(2)}) %collective-permute-start.18) | collective-permute-done | bytes 131104 | tf_op jit(solution)/shard_map/ppermute | solution.py:389
  67.3 1.3 %collective-permute-start.7 = (f32[72,4,128]{2,1,0:T(4,128)S(1)}, f32[72,4,128]{2,1,0:T(4,128)S(1)}, u32[]{:S(2)}, u32[]{:S(2)}) collective-permute-start(f32[72,4,128]{2,1,0:T(4,128)S(1)} %pad_maximum_fusion.1), channel_id=1, source_target_pairs={{8,0},{16,8},{24,16},{25,24},{17,25},{9,17},{1,9},{2,1},{10,2},{18... | collective-permute-start | bytes 442376 | tf_op jit(solution)/shard_map/ppermute | solution.py:408
  68.6 6.3 %collective-permute-start.6 = (f32[72,4,128]{2,1,0:T(4,128)S(1)}, f32[72,4,128]{2,1,0:T(4,128)S(1)}, u32[]{:S(2)}, u32[]{:S(2)}) collective-permute-start(f32[72,4,128]{2,1,0:T(4,128)S(1)} %pad_maximum_fusion), channel_id=1, source_target_pairs={{0,8},{8,16},{16,24},{24,25},{25,17},{17,9},{9,1},{1,2},{2,10},{10... | collective-permute-start | bytes 442376 | tf_op jit(solution)/shard_map/ppermute | solution.py:408
  74.9 0.1 pad_add_fusion.2.sources
  75.0 0.8 turn_weights.3.refs_8_
  75.9 0.0 collective-permute-done.10.refs_2_
  75.9 0.0 collective-permute-done.11.refs_3_
  75.9 0.0 collective-permute-done.7.refs_4_
  75.9 1.7 %collective-permute-done.6.refs_3_ = f32[72,4,128]{2,1,0:T(4,128)S(1)} collective-permute-done((f32[72,4,128]{2,1,0:T(4,128)S(1)}, f32[72,4,128]{2,1,0:T(4,128)S(1)}, u32[]{:S(2)}, u32[]{:S(2)}) %collective-permute-start.6) | collective-permute-done | bytes 147488 | tf_op jit(solution)/shard_map/ppermute | solution.py:408
  77.6 0.8 turn_weights.2.refs_5_
  78.4 4.4 %collective-permute-start.12 = (f32[40,4,128]{2,1,0:T(4,128)S(1)}, f32[40,4,128]{2,1,0:T(4,128)S(1)}, u32[]{:S(2)}, u32[]{:S(2)}) collective-permute-start(f32[40,4,128]{2,1,0:T(4,128)S(1)} %get-tuple-element.78), channel_id=1, source_target_pairs={{0,8},{8,16},{16,24},{24,25},{25,17},{17,9},{9,1},{1,2},{2,10},{10... | collective-permute-start | bytes 245768 | tf_op jit(solution)/shard_map/ppermute | solution.py:408
  82.8 1.3 %collective-permute-start.13 = (f32[40,4,128]{2,1,0:T(4,128)S(1)}, f32[40,4,128]{2,1,0:T(4,128)S(1)}, u32[]{:S(2)}, u32[]{:S(2)}) collective-permute-start(f32[40,4,128]{2,1,0:T(4,128)S(1)} %get-tuple-element.77), channel_id=1, source_target_pairs={{8,0},{16,8},{24,16},{25,24},{17,25},{9,17},{1,9},{2,1},{10,2},{18... | collective-permute-start | bytes 245768 | tf_op jit(solution)/shard_map/ppermute | solution.py:408
  84.2 4.5 %collective-permute-start.20 = (f32[32,4,128]{2,1,0:T(4,128)S(1)}, f32[32,4,128]{2,1,0:T(4,128)S(1)}, u32[]{:S(2)}, u32[]{:S(2)}) collective-permute-start(f32[32,4,128]{2,1,0:T(4,128)S(1)} %get-tuple-element.80), channel_id=1, source_target_pairs={{0,8},{8,16},{16,24},{24,25},{25,17},{17,9},{9,1},{1,2},{2,10},{10... | collective-permute-start | bytes 196616 | tf_op jit(solution)/shard_map/ppermute | solution.py:408
  88.7 1.3 %collective-permute-start.21 = (f32[32,4,128]{2,1,0:T(4,128)S(1)}, f32[32,4,128]{2,1,0:T(4,128)S(1)}, u32[]{:S(2)}, u32[]{:S(2)}) collective-permute-start(f32[32,4,128]{2,1,0:T(4,128)S(1)} %get-tuple-element.79), channel_id=1, source_target_pairs={{8,0},{16,8},{24,16},{25,24},{17,25},{9,17},{1,9},{2,1},{10,2},{18... | collective-permute-start | bytes 196616 | tf_op jit(solution)/shard_map/ppermute | solution.py:408
  90.0 0.7 collective-permute-done.20.refs_9_
  90.7 4.1 %collective-permute-done.21.refs_10_ = f32[32,4,128]{2,1,0:T(4,128)S(1)} collective-permute-done((f32[32,4,128]{2,1,0:T(4,128)S(1)}, f32[32,4,128]{2,1,0:T(4,128)S(1)}, u32[]{:S(2)}, u32[]{:S(2)}) %collective-permute-start.21) | collective-permute-done | bytes 65568 | tf_op jit(solution)/shard_map/ppermute | solution.py:408
  94.9 0.0 collective-permute-done.12.refs_6_
  94.9 0.0 collective-permute-done.13.refs_7_
  94.9 3.2 %spread_mix.3 = (f32[256,128]{1,0:T(8,128)S(1)}, f32[256,128]{1,0:T(8,128)S(1)}, f32[256,128]{1,0:T(8,128)S(1)}, f32[256,128]{1,0:T(8,128)S(1)}) custom-call(f32[128,128]{1,0:T(8,128)S(1)} %get-tuple-element.95.matrix, f32[64,32,128]{2,1,0:T(8,128)S(1)} %adjoint_mix.1.refs_0_, f32[4,32,128]{2,1,0:T(8,128)S(1)} %get-tuple-element.52.refs_1_, ...), custom_call_target="tpu_custom_call" | custom-call | tf_op jit(solution)/shard_map/spread_mix/pallas_call | solution.py:318
  98.1 0.1 collective-permute-start.22
  98.2 0.1 collective-permute-start.23
  98.3 0.0 copy-start.1
  98.3 3.7 %collective-permute-start.24 = (f32[256,128]{1,0:T(8,128)S(1)}, f32[256,128]{1,0:T(8,128)S(1)}, u32[]{:S(2)}, u32[]{:S(2)}) collective-permute-start(f32[256,128]{1,0:T(8,128)S(1)} %get-tuple-element.72), channel_id=1, source_target_pairs={{0,24},{8,0},{16,8},{24,16},{1,25},{9,1},{17,9},{25,17},{2,26},{10... | collective-permute-start | bytes 393224 | tf_op jit(solution)/shard_map/ppermute | solution.py:389
  102.0 3.2 %spread_mix.2 = (f32[256,128]{1,0:T(8,128)S(1)}, f32[256,128]{1,0:T(8,128)S(1)}, f32[256,128]{1,0:T(8,128)S(1)}, f32[256,128]{1,0:T(8,128)S(1)}) custom-call(f32[128,128]{1,0:T(8,128)S(1)} %get-tuple-element.95.matrix, f32[64,32,128]{2,1,0:T(8,128)S(1)} %adjoint_mix.1.refs_0_, f32[4,32,128]{2,1,0:T(8,128)S(1)} %get-tuple-element.52.refs_1_, ...), custom_call_target="tpu_custom_call" | custom-call | tf_op jit(solution)/shard_map/spread_mix/pallas_call | solution.py:318
  105.3 0.6 collective-permute-start.14
  105.9 1.5 %collective-permute-start.15 = (f32[256,128]{1,0:T(8,128)S(1)}, f32[256,128]{1,0:T(8,128)S(1)}, u32[]{:S(2)}, u32[]{:S(2)}) collective-permute-start(f32[256,128]{1,0:T(8,128)S(1)} %get-tuple-element.62), channel_id=1, source_target_pairs={{0,16},{8,24},{16,0},{24,8},{1,17},{9,25},{17,1},{25,9},{2,18},{10... | collective-permute-start | bytes 393224 | tf_op jit(solution)/shard_map/ppermute | solution.py:389
  107.4 0.0 collective-permute-done.22.refs_5_
  107.4 2.8 %collective-permute-start.16 = (f32[256,128]{1,0:T(8,128)S(1)}, f32[256,128]{1,0:T(8,128)S(1)}, u32[]{:S(2)}, u32[]{:S(2)}) collective-permute-start(f32[256,128]{1,0:T(8,128)S(1)} %get-tuple-element.63), channel_id=1, source_target_pairs={{0,24},{8,0},{16,8},{24,16},{1,25},{9,1},{17,9},{25,17},{2,26},{10... | collective-permute-start | bytes 393224 | tf_op jit(solution)/shard_map/ppermute | solution.py:389
  110.3 0.1 pad_add_fusion.slots
  110.4 2.3 %collective-permute-done.23.refs_6_ = f32[256,128]{1,0:T(8,128)S(1)} collective-permute-done((f32[256,128]{1,0:T(8,128)S(1)}, f32[256,128]{1,0:T(8,128)S(1)}, u32[]{:S(2)}, u32[]{:S(2)}) %collective-permute-start.23) | collective-permute-done | bytes 131104 | tf_op jit(solution)/shard_map/ppermute | solution.py:389
  112.7 0.0 collective-permute-done.24.refs_7_
  112.7 0.9 collective-permute-done.14.refs_1_
  113.6 6.6 %collective-permute-done.15.refs_2_ = f32[256,128]{1,0:T(8,128)S(1)} collective-permute-done((f32[256,128]{1,0:T(8,128)S(1)}, f32[256,128]{1,0:T(8,128)S(1)}, u32[]{:S(2)}, u32[]{:S(2)}) %collective-permute-start.15) | collective-permute-done | bytes 131104 | tf_op jit(solution)/shard_map/ppermute | solution.py:389
  120.1 3.2 %result.1 = f32[2,16,64,128]{3,2,1,0:T(8,128)} custom-call(s32[4]{0:T(128)S(1)} %pad_add_fusion.slots, f32[2,16,64,128]{3,2,1,0:T(8,128)S(1)} %copy-done.1, s32[16,64,128]{2,1,0:T(8,128)S(1)} %copy-done, f32[256,128]{1,0:T(8,128)S(1)} %get-tuple-element.60.refs_0_, f32[256,128]{1,0:T(8,128)S(1)} %collective-permute-done.14.refs_1_, ...), custom_call_target="tpu_custom_call" | custom-call | tf_op jit(solution)/shard_map/result/pallas_call | solution.py:355
  (30 shorter events, 0.3 us)
Async XLA Ops:
  0.7 15.0 %copy-start.7 = (f32[128,128]{1,0:T(8,128)S(1)}, f32[128,128]{1,0:T(8,128)}, u32[]{:S(2)}) copy-start(f32[128,128]{1,0:T(8,128)} %param.11) | copy-start | bytes 196612
  0.7 15.7 %copy-start = (s32[16,64,128]{2,1,0:T(8,128)S(1)}, s32[16,64,128]{2,1,0:T(8,128)}, u32[]{:S(2)}) copy-start(s32[16,64,128]{2,1,0:T(8,128)} %mask.5) | copy-start | bytes 1572868
  0.7 15.7 %copy-start.2 = (f32[16,64,128]{2,1,0:T(8,128)S(1)}, f32[16,64,128]{2,1,0:T(8,128)}, u32[]{:S(2)}) copy-start(f32[16,64,128]{2,1,0:T(8,128)} %along_i.1) | copy-start | bytes 1572868
  0.7 15.7 %copy-start.3 = (f32[16,64,128]{2,1,0:T(8,128)S(1)}, f32[16,64,128]{2,1,0:T(8,128)}, u32[]{:S(2)}) copy-start(f32[16,64,128]{2,1,0:T(8,128)} %along_j.1) | copy-start | bytes 1572868
  5.9 10.4 %collective-permute-start.4 = (f32[64,128]{1,0:T(8,128)}, f32[64,128]{1,0:T(8,128)S(1)}, u32[]{:S(2)}, u32[]{:S(2)}) collective-permute-start(f32[64,128]{1,0:T(8,128)} %get-tuple-element.43), channel_id=1, source_target_pairs={{4,0},{0,4},{5,1},{1,5},{6,2},{2,6},{7,3},{3,7},{12,8},{8,12},{13,... | collective-permute-start | bytes 98312 | tf_op jit(solution)/shard_map/ppermute | solution.py:412
  8.8 7.5 %collective-permute-start.5 = (f32[64,128]{1,0:T(8,128)}, f32[64,128]{1,0:T(8,128)S(1)}, u32[]{:S(2)}, u32[]{:S(2)}) collective-permute-start(f32[64,128]{1,0:T(8,128)} %get-tuple-element.43), channel_id=1, source_target_pairs={{1,0},{2,1},{3,2},{5,4},{6,5},{7,6},{9,8},{10,9},{11,10},{13,12},{... | collective-permute-start | bytes 98312 | tf_op jit(solution)/shard_map/ppermute | solution.py:413
  10.1 19.6 %collective-permute-start = (f32[528,128]{1,0:T(8,128)}, f32[528,128]{1,0:T(8,128)S(1)}, u32[]{:S(2)}, u32[]{:S(2)}) collective-permute-start(f32[528,128]{1,0:T(8,128)} %get-tuple-element.40), channel_id=1, source_target_pairs={{0,8},{8,16},{16,24},{24,0},{1,9},{9,17},{17,25},{25,1},{2,10},{10... | collective-permute-start | bytes 811016 | tf_op jit(solution)/shard_map/ppermute | solution.py:389
  11.7 21.7 %collective-permute-start.1 = (f32[528,128]{1,0:T(8,128)}, f32[528,128]{1,0:T(8,128)S(1)}, u32[]{:S(2)}, u32[]{:S(2)}) collective-permute-start(f32[528,128]{1,0:T(8,128)} %get-tuple-element.41), channel_id=1, source_target_pairs={{0,16},{8,24},{16,0},{24,8},{1,17},{9,25},{17,1},{25,9},{2,18},{10... | collective-permute-start | bytes 811016 | tf_op jit(solution)/shard_map/ppermute | solution.py:389
  14.3 19.1 %collective-permute-start.2 = (f32[528,128]{1,0:T(8,128)}, f32[528,128]{1,0:T(8,128)S(1)}, u32[]{:S(2)}, u32[]{:S(2)}) collective-permute-start(f32[528,128]{1,0:T(8,128)} %get-tuple-element.42), channel_id=1, source_target_pairs={{0,24},{8,0},{16,8},{24,16},{1,25},{9,1},{17,9},{25,17},{2,26},{10... | collective-permute-start | bytes 811016 | tf_op jit(solution)/shard_map/ppermute | solution.py:389
  16.3 2.0 %copy-start.6 = (f32[128,128]{1,0:T(8,128)S(1)}, f32[128,128]{1,0:T(8,128)}, u32[]{:S(2)}) copy-start(f32[128,128]{1,0:T(8,128)} %convert_add_fusion) | copy-start | bytes 196612
  17.8 5.9 %collective-permute-start.8 = (f32[32,8,128]{2,1,0:T(8,128)}, f32[32,8,128]{2,1,0:T(8,128)S(1)}, u32[]{:S(2)}, u32[]{:S(2)}) collective-permute-start(f32[32,8,128]{2,1,0:T(8,128)} %get-tuple-element.46), channel_id=1, source_target_pairs={{4,0},{0,4},{5,1},{1,5},{6,2},{2,6},{7,3},{3,7},{12,8},{8,12},{13,... | collective-permute-start | bytes 393224 | tf_op jit(solution)/shard_map/ppermute | solution.py:403
  23.7 0.7 copy-start.5
  24.4 9.1 %copy-start.4 = (f32[528,128]{1,0:T(8,128)S(1)}, f32[528,128]{1,0:T(8,128)}, u32[]{:S(2)}) copy-start(f32[528,128]{1,0:T(8,128)} %get-tuple-element.39.refs_0_) | copy-start | bytes 811012
  26.6 49.2 %collective-permute-start.10 = (f32[320,128]{1,0:T(8,128)S(1)}, f32[320,128]{1,0:T(8,128)S(1)}, u32[]{:S(2)}, u32[]{:S(2)}) collective-permute-start(f32[320,128]{1,0:T(8,128)S(1)} %get-tuple-element.49), channel_id=1, source_target_pairs={{0,16},{8,24},{16,0},{24,8},{1,17},{9,25},{17,1},{25,9},{2,18},{10... | collective-permute-start | bytes 491528 | tf_op jit(solution)/shard_map/ppermute | solution.py:389
  27.2 48.7 %collective-permute-start.11 = (f32[320,128]{1,0:T(8,128)S(1)}, f32[320,128]{1,0:T(8,128)S(1)}, u32[]{:S(2)}, u32[]{:S(2)}) collective-permute-start(f32[320,128]{1,0:T(8,128)S(1)} %get-tuple-element.50), channel_id=1, source_target_pairs={{0,24},{8,0},{16,8},{24,16},{1,25},{9,1},{17,9},{25,17},{2,26},{10... | collective-permute-start | bytes 491528 | tf_op jit(solution)/shard_map/ppermute | solution.py:389
  35.5 5.5 %collective-permute-start.3 = (f32[8,32,128]{2,1,0:T(8,128)S(1)}, f32[8,32,128]{2,1,0:T(8,128)S(1)}, u32[]{:S(2)}, u32[]{:S(2)}) collective-permute-start(f32[8,32,128]{2,1,0:T(8,128)S(1)} %pad_maximum_fusion.2), channel_id=1, source_target_pairs={{4,0},{0,4},{5,1},{1,5},{6,2},{2,6},{7,3},{3,7},{12,8},{8,12},{13,... | collective-permute-start | bytes 393224 | tf_op jit(solution)/shard_map/ppermute | solution.py:403
  42.8 18.9 %collective-permute-start.17 = (f32[256,128]{1,0:T(8,128)S(1)}, f32[256,128]{1,0:T(8,128)S(1)}, u32[]{:S(2)}, u32[]{:S(2)}) collective-permute-start(f32[256,128]{1,0:T(8,128)S(1)} %get-tuple-element.66), channel_id=1, source_target_pairs={{0,8},{8,16},{16,24},{24,0},{1,9},{9,17},{17,25},{25,1},{2,10},{10... | collective-permute-start | bytes 393224 | tf_op jit(solution)/shard_map/ppermute | solution.py:389
  54.5 12.8 %collective-permute-start.18 = (f32[256,128]{1,0:T(8,128)S(1)}, f32[256,128]{1,0:T(8,128)S(1)}, u32[]{:S(2)}, u32[]{:S(2)}) collective-permute-start(f32[256,128]{1,0:T(8,128)S(1)} %get-tuple-element.67), channel_id=1, source_target_pairs={{0,16},{8,24},{16,0},{24,8},{1,17},{9,25},{17,1},{25,9},{2,18},{10... | collective-permute-start | bytes 393224 | tf_op jit(solution)/shard_map/ppermute | solution.py:389
  57.8 10.8 %collective-permute-start.19 = (f32[256,128]{1,0:T(8,128)S(1)}, f32[256,128]{1,0:T(8,128)S(1)}, u32[]{:S(2)}, u32[]{:S(2)}) collective-permute-start(f32[256,128]{1,0:T(8,128)S(1)} %get-tuple-element.68), channel_id=1, source_target_pairs={{0,24},{8,0},{16,8},{24,16},{1,25},{9,1},{17,9},{25,17},{2,26},{10... | collective-permute-start | bytes 393224 | tf_op jit(solution)/shard_map/ppermute | solution.py:389
  61.7 14.2 %collective-permute-start.9 = (f32[320,128]{1,0:T(8,128)S(1)}, f32[320,128]{1,0:T(8,128)S(1)}, u32[]{:S(2)}, u32[]{:S(2)}) collective-permute-start(f32[320,128]{1,0:T(8,128)S(1)} %get-tuple-element.48), channel_id=1, source_target_pairs={{0,8},{8,16},{16,24},{24,0},{1,9},{9,17},{17,25},{25,1},{2,10},{10... | collective-permute-start | bytes 491528 | tf_op jit(solution)/shard_map/ppermute | solution.py:389
  67.3 8.6 %collective-permute-start.7 = (f32[72,4,128]{2,1,0:T(4,128)S(1)}, f32[72,4,128]{2,1,0:T(4,128)S(1)}, u32[]{:S(2)}, u32[]{:S(2)}) collective-permute-start(f32[72,4,128]{2,1,0:T(4,128)S(1)} %pad_maximum_fusion.1), channel_id=1, source_target_pairs={{8,0},{16,8},{24,16},{25,24},{17,25},{9,17},{1,9},{2,1},{10,2},{18... | collective-permute-start | bytes 442376 | tf_op jit(solution)/shard_map/ppermute | solution.py:408
  68.6 9.0 %collective-permute-start.6 = (f32[72,4,128]{2,1,0:T(4,128)S(1)}, f32[72,4,128]{2,1,0:T(4,128)S(1)}, u32[]{:S(2)}, u32[]{:S(2)}) collective-permute-start(f32[72,4,128]{2,1,0:T(4,128)S(1)} %pad_maximum_fusion), channel_id=1, source_target_pairs={{0,8},{8,16},{16,24},{24,25},{25,17},{17,9},{9,1},{1,2},{2,10},{10... | collective-permute-start | bytes 442376 | tf_op jit(solution)/shard_map/ppermute | solution.py:408
  78.4 16.4 %collective-permute-start.12 = (f32[40,4,128]{2,1,0:T(4,128)S(1)}, f32[40,4,128]{2,1,0:T(4,128)S(1)}, u32[]{:S(2)}, u32[]{:S(2)}) collective-permute-start(f32[40,4,128]{2,1,0:T(4,128)S(1)} %get-tuple-element.78), channel_id=1, source_target_pairs={{0,8},{8,16},{16,24},{24,25},{25,17},{17,9},{9,1},{1,2},{2,10},{10... | collective-permute-start | bytes 245768 | tf_op jit(solution)/shard_map/ppermute | solution.py:408
  82.8 12.1 %collective-permute-start.13 = (f32[40,4,128]{2,1,0:T(4,128)S(1)}, f32[40,4,128]{2,1,0:T(4,128)S(1)}, u32[]{:S(2)}, u32[]{:S(2)}) collective-permute-start(f32[40,4,128]{2,1,0:T(4,128)S(1)} %get-tuple-element.77), channel_id=1, source_target_pairs={{8,0},{16,8},{24,16},{25,24},{17,25},{9,17},{1,9},{2,1},{10,2},{18... | collective-permute-start | bytes 245768 | tf_op jit(solution)/shard_map/ppermute | solution.py:408
  84.2 6.6 %collective-permute-start.20 = (f32[32,4,128]{2,1,0:T(4,128)S(1)}, f32[32,4,128]{2,1,0:T(4,128)S(1)}, u32[]{:S(2)}, u32[]{:S(2)}) collective-permute-start(f32[32,4,128]{2,1,0:T(4,128)S(1)} %get-tuple-element.80), channel_id=1, source_target_pairs={{0,8},{8,16},{16,24},{24,25},{25,17},{17,9},{9,1},{1,2},{2,10},{10... | collective-permute-start | bytes 196616 | tf_op jit(solution)/shard_map/ppermute | solution.py:408
  88.7 6.2 %collective-permute-start.21 = (f32[32,4,128]{2,1,0:T(4,128)S(1)}, f32[32,4,128]{2,1,0:T(4,128)S(1)}, u32[]{:S(2)}, u32[]{:S(2)}) collective-permute-start(f32[32,4,128]{2,1,0:T(4,128)S(1)} %get-tuple-element.79), channel_id=1, source_target_pairs={{8,0},{16,8},{24,16},{25,24},{17,25},{9,17},{1,9},{2,1},{10,2},{18... | collective-permute-start | bytes 196616 | tf_op jit(solution)/shard_map/ppermute | solution.py:408
  98.1 9.3 %collective-permute-start.22 = (f32[256,128]{1,0:T(8,128)S(1)}, f32[256,128]{1,0:T(8,128)S(1)}, u32[]{:S(2)}, u32[]{:S(2)}) collective-permute-start(f32[256,128]{1,0:T(8,128)S(1)} %get-tuple-element.70), channel_id=1, source_target_pairs={{0,8},{8,16},{16,24},{24,0},{1,9},{9,17},{17,25},{25,1},{2,10},{10... | collective-permute-start | bytes 393224 | tf_op jit(solution)/shard_map/ppermute | solution.py:389
  98.2 14.5 %collective-permute-start.23 = (f32[256,128]{1,0:T(8,128)S(1)}, f32[256,128]{1,0:T(8,128)S(1)}, u32[]{:S(2)}, u32[]{:S(2)}) collective-permute-start(f32[256,128]{1,0:T(8,128)S(1)} %get-tuple-element.71), channel_id=1, source_target_pairs={{0,16},{8,24},{16,0},{24,8},{1,17},{9,25},{17,1},{25,9},{2,18},{10... | collective-permute-start | bytes 393224 | tf_op jit(solution)/shard_map/ppermute | solution.py:389
  98.3 21.9 %copy-start.1 = (f32[2,16,64,128]{3,2,1,0:T(8,128)S(1)}, f32[2,16,64,128]{3,2,1,0:T(8,128)}, u32[]{:S(2)}) copy-start(f32[2,16,64,128]{3,2,1,0:T(8,128)} %gain.3) | copy-start | bytes 3145732
  98.3 14.4 %collective-permute-start.24 = (f32[256,128]{1,0:T(8,128)S(1)}, f32[256,128]{1,0:T(8,128)S(1)}, u32[]{:S(2)}, u32[]{:S(2)}) collective-permute-start(f32[256,128]{1,0:T(8,128)S(1)} %get-tuple-element.72), channel_id=1, source_target_pairs={{0,24},{8,0},{16,8},{24,16},{1,25},{9,1},{17,9},{25,17},{2,26},{10... | collective-permute-start | bytes 393224 | tf_op jit(solution)/shard_map/ppermute | solution.py:389
  105.3 8.3 %collective-permute-start.14 = (f32[256,128]{1,0:T(8,128)S(1)}, f32[256,128]{1,0:T(8,128)S(1)}, u32[]{:S(2)}, u32[]{:S(2)}) collective-permute-start(f32[256,128]{1,0:T(8,128)S(1)} %get-tuple-element.61), channel_id=1, source_target_pairs={{0,8},{8,16},{16,24},{24,0},{1,9},{9,17},{17,25},{25,1},{2,10},{10... | collective-permute-start | bytes 393224 | tf_op jit(solution)/shard_map/ppermute | solution.py:389
  105.9 14.2 %collective-permute-start.15 = (f32[256,128]{1,0:T(8,128)S(1)}, f32[256,128]{1,0:T(8,128)S(1)}, u32[]{:S(2)}, u32[]{:S(2)}) collective-permute-start(f32[256,128]{1,0:T(8,128)S(1)} %get-tuple-element.62), channel_id=1, source_target_pairs={{0,16},{8,24},{16,0},{24,8},{1,17},{9,25},{17,1},{25,9},{2,18},{10... | collective-permute-start | bytes 393224 | tf_op jit(solution)/shard_map/ppermute | solution.py:389
  107.4 12.7 %collective-permute-start.16 = (f32[256,128]{1,0:T(8,128)S(1)}, f32[256,128]{1,0:T(8,128)S(1)}, u32[]{:S(2)}, u32[]{:S(2)}) collective-permute-start(f32[256,128]{1,0:T(8,128)S(1)} %get-tuple-element.63), channel_id=1, source_target_pairs={{0,24},{8,0},{16,8},{24,16},{1,25},{9,1},{17,9},{25,17},{2,26},{10... | collective-permute-start | bytes 393224 | tf_op jit(solution)/shard_map/ppermute | solution.py:389

commit v3 on v2

v3 whole, which is shorter than its diff:
```python
import functools

import jax
import jax.numpy as jnp
from jax import lax
from jax.experimental import pallas as pl
from jax.experimental.pallas import tpu as pltpu
from jax.sharding import PartitionSpec as P

ITERS = 2
STEPS = 2 * ITERS
PAD = 8
PARTS = 2
VMEM_LIMIT = 40 * 1024 * 1024
VMEM_WHOLE = 60 * 1024 * 1024
HIGHEST = lax.Precision.HIGHEST


def params(limit=VMEM_LIMIT):
    return pltpu.CompilerParams(vmem_limit_bytes=limit)


def smem():
    return pl.BlockSpec(memory_space=pltpu.SMEM)


def vmem():
    return pl.BlockSpec(memory_space=pltpu.VMEM)


def position():
    devices = lax.axis_size("lev")
    me = lax.axis_index("lev")
    flipped = lax.rem(lax.axis_index("gy"), 2) == 1

    def slot(lev):
        return jnp.where(flipped, devices - 1 - lev, lev)

    to = [lax.rem(me + d, devices) for d in range(devices)]
    source = [lax.rem(me + devices - d, devices) for d in range(devices)]
    return [slot(lev) for lev in to], [slot(lev) for lev in source], source


def swap(blocks, group, width):
    blocks = list(blocks)
    cols = blocks[0].shape[1]
    bit = len(blocks) // 2
    while bit:
        shift = bit * width
        low = (group & bit) == 0
        for a in range(len(blocks)):
            if not a & bit:
                x, y = blocks[a], blocks[a + bit]
                blocks[a] = jnp.where(low, x, pltpu.roll(y, shift, 1))
                blocks[a + bit] = jnp.where(low, pltpu.roll(x, cols - shift, 1), y)
        bit //= 2
    return blocks


def lane_groups(rows, cols, groups):
    return lax.broadcasted_iota(jnp.int32, (rows, cols), 1) // (cols // groups)


def copies(pairs, sems):
    made = [pltpu.make_async_copy(src, dst, sems.at[k]) for k, (src, dst) in enumerate(pairs)]
    for copy in made:
        copy.start()
    return made


SCALED_STEPS = 4


def scaled_kernel(increment, gain, mask, *refs):
    outs, (inc, gn, sea, held, sems, out_sems) = refs[:-6], refs[-6:]
    fields, levels, length, cols = increment.shape
    groups = len(outs)
    rows = length // groups
    some = levels // SCALED_STEPS
    group = lane_groups(rows, cols, groups)
    fetched = []
    for step in range(SCALED_STEPS):
        part = pl.ds(step * some, some)
        fetched.append(
            copies(
                [
                    (increment.at[:, part], inc.at[:, part]),
                    (gain.at[:, part], gn.at[:, part]),
                    (mask.at[part], sea.at[part]),
                ],
                sems.at[step],
            )
        )
    depth = jnp.zeros((length, cols), jnp.float32)

    def put(at, x):
        for slot, block in enumerate(swap([x[a * rows:(a + 1) * rows] for a in range(groups)], group, cols // groups)):
            held[slot, pl.ds(at, rows), :] = block

    for step in range(SCALED_STEPS):
        for copy in fetched[step]:
            copy.wait()

        def one(level, depth):
            ocean = sea[level].astype(jnp.float32)
            for field in range(fields):
                at = pl.multiple_of((field * levels + level) * rows, rows)
                put(at, ocean * gn[field, level] * inc[field, level])
            return depth + ocean

        depth = lax.fori_loop(step * some, (step + 1) * some, one, depth, unroll=True)
    put(fields * levels * rows, depth)
    slots = position()[0]
    for copy in copies([(held.at[slots[d]], out) for d, out in enumerate(outs)], out_sems):
        copy.wait()


def scaled_messages(increment, gain, mask, groups):
    fields, levels, length, cols = increment.shape
    shape = ((fields * levels + 1) * length // groups, cols)
    return pl.pallas_call(
        scaled_kernel,
        in_specs=[pl.BlockSpec(memory_space=pl.ANY)] * 3,
        out_specs=[pl.BlockSpec(memory_space=pl.ANY)] * groups,
        out_shape=[jax.ShapeDtypeStruct(shape, jnp.float32)] * groups,
        scratch_shapes=[
            pltpu.VMEM(increment.shape, jnp.float32),
            pltpu.VMEM(gain.shape, jnp.float32),
            pltpu.VMEM(mask.shape, mask.dtype),
            pltpu.VMEM((groups, *shape), jnp.float32),
            pltpu.SemaphoreType.DMA((SCALED_STEPS, 3)),
            pltpu.SemaphoreType.DMA((groups,)),
        ],
        compiler_params=params(VMEM_WHOLE),
        name="scaled_messages",
    )(increment, gain, mask)


def pack_kernel(first, along_i, along_j, above, below, *refs):
    outs, (held, slots_held, sems) = refs[:-3], refs[-3:]
    levels, length, cols = along_i.shape
    groups = len(outs)
    rows = outs[0].shape[0] // (2 * levels)
    group = lane_groups(rows, cols, groups)
    unroll = held.shape[0]

    for side, weight in enumerate((along_i, along_j)):

        def some(outer, carry, side=side, weight=weight):
            for k in range(unroll):
                level = outer * unroll + k
                held[k, pl.ds(0, STEPS), :] = above[side * levels + level]
                held[k, pl.ds(STEPS, length), :] = weight[level]
                held[k, pl.ds(STEPS + length, STEPS), :] = below[side * levels + level]
            packed = [
                swap([held[k, pl.ds(first + a * rows, rows), :] for a in range(groups)], group, cols // groups)
                for k in range(unroll)
            ]
            at = pl.multiple_of((side * levels + outer * unroll) * rows, 8)
            for slot in range(groups):
                block = jnp.concatenate([packed[k][slot] for k in range(unroll)], axis=0)
                slots_held[slot, pl.ds(at, unroll * rows), :] = block
            return carry

        lax.fori_loop(0, levels // unroll, some, 0)
    slots = position()[0]
    for copy in copies([(slots_held.at[slots[d]], out) for d, out in enumerate(outs)], sems):
        copy.wait()


def weight_messages(first, rows, along_i, along_j, above, below, groups):
    levels, length, cols = along_i.shape
    shape = (2 * levels * rows // groups, cols)
    unroll = 4
    return pl.pallas_call(
        functools.partial(pack_kernel, first),
        in_specs=[vmem()] * 4,
        out_specs=[pl.BlockSpec(memory_space=pl.ANY)] * groups,
        out_shape=[jax.ShapeDtypeStruct(shape, jnp.float32)] * groups,
        scratch_shapes=[
            pltpu.VMEM((unroll, length + 2 * STEPS, cols), jnp.float32),
            pltpu.VMEM((groups, *shape), jnp.float32),
            pltpu.SemaphoreType.DMA((groups,)),
        ],
        compiler_params=params(),
        name="weight_messages",
    )(along_i, along_j, above, below)


def adjoint_kernel(matrix, *refs):
    parts, out, depths = refs[:-2], refs[-2], refs[-1]
    length, width, order = out.shape
    groups = len(parts)
    rows = length // groups
    cols = groups * width
    count = order // groups
    depths[...] = sum(part[pl.ds(count * rows, rows), :] for part in parts)
    level = lax.rem(lax.broadcasted_iota(jnp.int32, (order, cols), 0), order // 2).astype(jnp.float32)

    def one(i, carry):
        x = jnp.concatenate([part[pl.ds(i, count, rows), :] for part in parts], axis=0)
        depth = depths[pl.ds(i, 1), :]
        y = jnp.dot(matrix[...], x, precision=HIGHEST, preferred_element_type=jnp.float32)
        y = jnp.where(level < depth, y, 0.0).T
        for a in range(groups):
            out[a * rows + i] = y[a * width:(a + 1) * width]
        return carry

    lax.fori_loop(0, rows, one, 0, unroll=4)


def adjoint_mix(matrix, parts, length, width):
    return pl.pallas_call(
        adjoint_kernel,
        in_specs=[vmem()] * (1 + len(parts)),
        out_specs=[vmem()] * 2,
        out_shape=[
            jax.ShapeDtypeStruct((length, width, matrix.shape[0]), jnp.float32),
            jax.ShapeDtypeStruct((length // len(parts), width * len(parts)), jnp.float32),
        ],
        compiler_params=params(),
        name="adjoint_mix",
    )(matrix, *parts)


def unfold(main, halo, groups):
    cols = main.shape[1]
    width = cols // groups
    below = halo[:STEPS]
    above = pltpu.roll(halo[STEPS:], width, 1)
    return jnp.concatenate(
        [above] + [main] + [pltpu.roll(main, cols - a * width, 1) for a in range(1, groups)] + [below], axis=0
    )


def turn_kernel(first, main, halo, right_main, right_halo, *refs):
    parts, (out, held, depth_i, depth_j) = refs[:-4], refs[-4:]
    length, width, order = out.shape
    groups = len(parts)
    rows = length // groups
    half = order // 2
    count = half // groups
    cols = width * groups
    source = position()[2]
    for i in range(rows):
        for d, part in enumerate(parts):
            for side in range(2):
                at = pl.multiple_of(side * half + source[d] * count, 8)
                held[i, pl.ds(at, count), :] = part[pl.ds(side * count * rows + i, count, rows), :]

    gy = lax.axis_index("gy")
    ends = (position()[0][0] == groups - 1) & (gy == lax.axis_size("gy") - 1)
    depth = unfold(main[...], halo[...], groups)
    right = jnp.where(ends, 0.0, unfold(right_main[...], right_halo[...], groups))
    tall = depth.shape[0]
    lane = lax.broadcasted_iota(jnp.int32, depth.shape, 1)
    right = jnp.where(lane == width - 1, pltpu.roll(right, width - 1, 1), pltpu.roll(depth, cols - 1, 1))
    depth_j[...] = jnp.minimum(depth, right)
    depth_i[pl.ds(0, tall - 1), :] = jnp.minimum(depth[:-1], depth[1:])
    depth_i[pl.ds(tall - 1, 1), :] = depth[tall - 1:]
    group = lane_groups(rows, cols, groups)

    def fold(ref):
        x = ref[pl.ds(first, rows), :]
        for a in range(1, groups):
            x = jnp.where(group == a, pltpu.roll(ref[pl.ds(first + a * rows, rows), :], a * width, 1), x)
        return x

    folded_i, folded_j = fold(depth_i), fold(depth_j)
    level = lax.broadcasted_iota(jnp.int32, (half, cols), 0).astype(jnp.float32)
    for i in range(rows):
        along_i = jnp.where(level < folded_i[i:i + 1], held[i, pl.ds(0, half), :], 0.0)
        along_j = jnp.where(level < folded_j[i:i + 1], held[i, pl.ds(half, half), :], 0.0)
        turned = jnp.concatenate([along_i, along_j], axis=0).T
        for a in range(groups):
            out[a * rows + i] = turned[a * width:(a + 1) * width]


def turn_weights(first, depths, parts, order):
    groups = len(parts)
    cols = parts[0].shape[1]
    rows = parts[0].shape[0] * groups // order
    tall = depths[0].shape[0] * groups + 2 * STEPS
    return pl.pallas_call(
        functools.partial(turn_kernel, first),
        in_specs=[vmem()] * (4 + groups),
        out_specs=vmem(),
        out_shape=jax.ShapeDtypeStruct((rows * groups, cols // groups, order), jnp.float32),
        scratch_shapes=[pltpu.VMEM((rows, order, cols), jnp.float32)] + [pltpu.VMEM((tall, cols), jnp.float32)] * 2,
        compiler_params=params(),
        name="turn_weights",
    )(*depths, *parts)


def spread_kernel(first, pieces, matrix, *refs):
    field, weights = refs[:5], refs[5:5 + 3 * len(pieces)]
    outs, (a, b, wi, wj) = refs[5 + 3 * len(pieces):-4], refs[-4:]
    length, width, order = field[0].shape
    half = order // 2
    ext, wide, _ = a.shape
    lane = lax.broadcasted_iota(jnp.int32, (wide, order), 1)
    nothing = jnp.zeros((PAD - STEPS, order), jnp.float32)

    def widen(left, mid, right):
        return jnp.concatenate([nothing, left, mid, right, nothing], axis=0)

    for e in range(ext):
        r = first + e
        main, above, below, left, right = field
        if r < STEPS:
            mid = above[r]
        elif r < STEPS + length:
            mid = main[r - STEPS]
        else:
            mid = below[r - STEPS - length]
        a[e] = widen(left[pl.ds(r * STEPS, STEPS), :], mid, right[pl.ds(r * STEPS, STEPS), :])
        piece = [k for k, (at, rows) in enumerate(pieces) if at <= r < at + rows][0]
        main, left, right = weights[3 * piece:3 * piece + 3]
        k = r - pieces[piece][0]
        w = widen(left[pl.ds(k * STEPS, STEPS), :], main[k], right[pl.ds(k * STEPS, STEPS), :])
        other = pltpu.roll(w, half, 1)
        wi[e] = jnp.where(lane < half, w, other)
        wj[e] = jnp.where(lane < half, other, w)

    src, dst = a, b
    for step in range(STEPS):
        begin, last = step + 1, ext - 2 - step

        def one(r, carry, src=src, dst=dst):
            v, before = carry
            after = src[r + 1]
            flux = wi[r] * (after - v)
            across = wj[r] * (pltpu.roll(v, wide - 1, 0) - v)
            dst[r] = v + (flux - before) + (across - pltpu.roll(across, 1, 0))
            return after, flux

        v = src[begin]
        lax.fori_loop(begin, last + 1, one, (v, wi[begin - 1] * (v - src[begin - 1])), unroll=2)
        src, dst = dst, src

    groups = len(outs)
    count = order // groups
    rows = (ext - 2 * STEPS) // groups

    def mix(i, carry):
        x = jnp.concatenate([src[STEPS + g * rows + i, pl.ds(PAD, width), :] for g in range(groups)], axis=0)
        y = lax.dot_general(
            matrix[...], x, (((1,), (1,)), ((), ())), precision=HIGHEST, preferred_element_type=jnp.float32
        )
        for d, out in enumerate(outs):
            out[pl.ds(i, count, rows), :] = y[d * count:(d + 1) * count]
        return carry

    lax.fori_loop(0, rows, mix, 0, unroll=4)


def spread_mix(first, last, pieces, matrix, field, weights, groups):
    length, width, order = field[0].shape
    cols = width * groups
    rows = (last - first - 2 * STEPS) // groups
    shape = jax.ShapeDtypeStruct((order // groups * rows, cols), jnp.float32)
    ext = pltpu.VMEM((last - first, width + 2 * PAD, order), jnp.float32)

    def kernel(matrix, *refs):
        spread_kernel(first, pieces, matrix, *refs)

    return pl.pallas_call(
        kernel,
        in_specs=[vmem()] * (1 + len(field) + len(weights)),
        out_specs=[vmem()] * groups,
        out_shape=[shape] * groups,
        scratch_shapes=[ext] * 4,
        compiler_params=params(),
        name="spread_mix",
    )(matrix, *field, *weights)


def result_kernel(gain, mask, *refs):
    parts, (out, held, sems) = refs[:-3], refs[-3:]
    fields, levels, length, cols = gain.shape
    groups = held.shape[0]
    rows = length // groups
    slots = position()[1]
    fetched = copies([(parts[d], held.at[slots[d]]) for d in range(groups)], sems)
    group = lane_groups(rows, cols, groups)
    for copy in fetched:
        copy.wait()

    def one(level, carry):
        ocean = mask[level].astype(jnp.float32)
        for field in range(fields):
            at = pl.multiple_of((field * levels + level) * rows, rows)
            blocks = swap([held[slot, pl.ds(at, rows), :] for slot in range(groups)], group, cols // groups)
            out[field, level] = ocean * gain[field, level] * jnp.concatenate(blocks, axis=0)
        return carry

    lax.fori_loop(0, levels, one, 0, unroll=4)


def result(part, gain, mask, parts, before):
    fields, levels, length, cols = gain.shape
    groups = len(parts)
    rows = length // PARTS
    block = pl.BlockSpec((fields, levels, rows, cols), lambda step: (0, 0, part, 0))
    mask_block = pl.BlockSpec((levels, rows, cols), lambda step: (0, part, 0))
    anywhere = pl.BlockSpec(memory_space=pl.ANY)
    more = [] if before is None else [before]
    return pl.pallas_call(
        result_kernel if before is None else lambda gain, mask, *refs: result_kernel(
            gain, mask, *refs[:groups], *refs[groups + 1:]
        ),
        grid=(1,),
        in_specs=[block, mask_block] + [anywhere] * (groups + len(more)),
        out_specs=block,
        out_shape=jax.ShapeDtypeStruct(gain.shape, jnp.float32),
        scratch_shapes=[
            pltpu.VMEM((groups, *parts[0].shape), jnp.float32),
            pltpu.SemaphoreType.DMA((groups,)),
        ],
        input_output_aliases={2 + groups: 0} if more else {},
        compiler_params=params(),
        name="result",
    )(gain, mask, *parts, *more)


def shards(increment, norm_gain, diffusion_i, diffusion_j, sea_mask, coupling):
    devices = lax.axis_size("lev")
    gx_size = lax.axis_size("gx")
    gy_size = lax.axis_size("gy")
    _, levels, length, cols = increment.shape
    width = cols // devices
    rows = length // devices
    order = coupling.shape[0]
    to = [lax.rem(lax.axis_index("lev") + d, devices) for d in range(devices)]
    source = [lax.rem(lax.axis_index("lev") + devices - d, devices) for d in range(devices)]

    def exchange(parts):
        return [parts[0]] + [
            lax.ppermute(parts[d], "lev", [(k, (k + d) % devices) for k in range(devices)]) for d in range(1, devices)
        ]

    up = [((k + 1) % gx_size, k) for k in range(gx_size)]
    down = [(b, a) for a, b in up]
    ring = [(devices - 1 - slot if y % 2 else slot) * gy_size + y for y in range(gy_size) for slot in range(devices)]
    ahead = list(zip(ring, ring[1:] + ring[:1]))
    back = [(b, a) for a, b in ahead]

    def halo_i(first, last, axis):
        if gx_size == 2:
            size = first.shape[axis]
            both = lax.ppermute(jnp.concatenate([first, last], axis=axis), "gx", up)
            below, above = lax.split(both, (size, size), axis)
            return above, below
        return lax.ppermute(last, "gx", down), lax.ppermute(first, "gx", up)

    def halo_j(first, last):
        return lax.ppermute(last, ("lev", "gy"), ahead), lax.ppermute(first, ("lev", "gy"), back)

    def flat(x):
        return x.reshape(-1, x.shape[-1])

    scaled = exchange(scaled_messages(increment, norm_gain, sea_mask, devices))

    above, below = halo_i(
        jnp.concatenate([diffusion_i[:, :STEPS], diffusion_j[:, :STEPS]], axis=0),
        jnp.concatenate([diffusion_i[:, -STEPS:], diffusion_j[:, -STEPS:]], axis=0),
        1,
    )
    part = length // PARTS
    pieces = [(0, part + 2 * STEPS)] + [(k * part + 2 * STEPS, part) for k in range(1, PARTS)]
    messages = [weight_messages(*piece, diffusion_i, diffusion_j, above, below, devices) for piece in pieces]
    arrived = exchange(messages[0])

    balance = jnp.eye(order, dtype=jnp.float32) + coupling
    by_device = balance.reshape(2, devices, levels, order)
    adjoint = jnp.concatenate([by_device[:, s].reshape(2 * levels, order) for s in source], axis=0).T
    forward = jnp.concatenate([by_device[:, t].reshape(2 * levels, order) for t in to], axis=0)

    mixed, depth = adjoint_mix(adjoint, scaled, length, width)
    above, below = halo_i(
        jnp.concatenate([flat(mixed[:STEPS]), depth[:STEPS]], axis=0),
        jnp.concatenate([flat(mixed[-STEPS:]), depth[-STEPS:]], axis=0),
        0,
    )
    size = STEPS * width
    halo_depth = jnp.concatenate([below[size:], above[size:]], axis=0)
    above, below = [x[:size].reshape(STEPS, width, order) for x in (above, below)]
    tall = [above, mixed, below]
    left, right = halo_j(
        jnp.concatenate([flat(jnp.concatenate([x[:, :STEPS] for x in tall], axis=0)), depth, halo_depth], axis=0),
        flat(jnp.concatenate([x[:, -STEPS:] for x in tall], axis=0)),
    )
    size = left.shape[0]
    depths = [depth, halo_depth, right[size:size + rows], right[size + rows:]]
    field = [mixed, above, below, left, right[:size]]

    turned, out = [], None
    for k, piece in enumerate(pieces):
        if k + 1 < PARTS:
            field, depths, arrived, messages = lax.optimization_barrier((field, depths, arrived, messages))
            coming = exchange(messages[k + 1])
        here = turn_weights(piece[0], depths, arrived, order)
        turned += [here, *halo_j(flat(here[:, :STEPS]), flat(here[:, -STEPS:]))]
        first, last = k * part, (k + 1) * part + 2 * STEPS
        mixed = exchange(spread_mix(first, last, pieces[:k + 1], forward, field, turned, devices))
        out = result(k, norm_gain, sea_mask, mixed, out)
        arrived = coming
    return out


def solution(mesh):
    return jax.shard_map(
        shards,
        mesh=mesh,
        in_specs=(
            P(None, "lev", "gx", "gy"),
            P(None, "lev", "gx", "gy"),
            P("lev", "gx", "gy"),
            P("lev", "gx", "gy"),
            P("lev", "gx", "gy"),
            P(),
        ),
        out_specs=P(None, "lev", "gx", "gy"),
        check_vma=False,
    )
```

time: 124 us -> 99.3 us (0.80)
  waiting for transfers between devices: 39.6 us -> 23.2 us
  starting transfers between devices: 57 us -> 53.5 us
  Pallas kernels: 24 us -> 21.6 us
  other arithmetic: 1.53 us -> 0.16 us
    ppermute x15, waiting for transfers between devices: 22.9 us -> 7.06 us  [exchange(): lax.ppermute(parts[d], 'lev', [(k, (k + d) % devices) for k in range(devi...]
    ppermute x4 -> x2, waiting for transfers between devices: 10.2 us -> 6.8 us  [halo_i(): both = lax.ppermute(jnp.concatenate([first, last], axis=axis), 'gx', up)]
    pallas_call x7, Pallas kernels: 15.5 us -> 13.1 us  [the longest x2 4.51 us: result(): pl.pallas_call(result_kernel if before is None else lambda gain, mask, *r...]
    ppermute x3, waiting for transfers between devices: 4.14 us -> 6.39 us  [halo_j(): lax.ppermute(first, ('lev', 'gy'), back)]
    ppermute x4 -> x2, starting transfers between devices: 5.28 us -> 3.36 us  [halo_i(): both = lax.ppermute(jnp.concatenate([first, last], axis=axis), 'gx', up)]
    ppermute x3, starting transfers between devices: 15.3 us -> 13.9 us  [halo_j(): lax.ppermute(last, ('lev', 'gy'), ahead)]
    ppermute x3, starting transfers between devices: 3.86 us -> 2.49 us  [halo_j(): lax.ppermute(first, ('lev', 'gy'), back)]
  transfers between devices with their start and end apart: 25 -> 23, of which waited for: 11 -> 8; matrix products, arithmetic and copies ran while one was open for 1% -> 0% of each run, Pallas kernels for 9% -> 16%
where the time goes in v3:
time: 99.3 us; the launch traced here: 99.1 us
  starting transfers between devices  53.5 us (54%)
  waiting for transfers between devices  23.2 us (23%)
  Pallas kernels  21.6 us (22%)
    ppermute x15, starting transfers between devices, exchange(): lax.ppermute(parts[d], 'lev', [(k, (k + d) % devices) for k in range(devi...  33.7 us
    ppermute x3, starting transfers between devices, halo_j(): lax.ppermute(last, ('lev', 'gy'), ahead)  13.9 us
    ppermute x15, waiting for transfers between devices, exchange(): lax.ppermute(parts[d], 'lev', [(k, (k + d) % devices) for k in range(devi...  7.06 us
    ppermute x2, waiting for transfers between devices, halo_i(): both = lax.ppermute(jnp.concatenate([first, last], axis=axis), 'gx', up)  6.8 us
    pallas_call x2, Pallas kernels, spread_mix(): pl.pallas_call(kernel, in_specs=[vmem()] * (1 + len(field) + len(weights)...  6.49 us
    ppermute x3, waiting for transfers between devices, halo_j(): lax.ppermute(first, ('lev', 'gy'), back)  6.39 us
    pallas_call x2, Pallas kernels, result(): pl.pallas_call(result_kernel if before is None else lambda gain, mask, *r...  4.51 us
    pallas_call x2, Pallas kernels, weight_messages(): pl.pallas_call(functools.partial(pack_kernel, first), in_specs=[vmem()] *...  4.38 us
  transfers between devices with their start and end apart: 23, of which 8 were waited for; matrix products, arithmetic and copies ran while one was open for 0% of the time, Pallas kernels for 16%

profile of v3, /device:TPU:0, one launch (start us, length us, event | category | flops | bytes accessed | tf_op | source)
XLA Modules:
  0.0 99.1 jit_solution(4498587840010440915)
XLA Ops:
  0.0 3.4 %scaled_messages.1 = (f32[528,128]{1,0:T(8,128)}, f32[528,128]{1,0:T(8,128)}, f32[528,128]{1,0:T(8,128)}, f32[528,128]{1,0:T(8,128)}) custom-call(f32[2,16,64,128]{3,2,1,0:T(8,128)} %increment.1, f32[2,16,64,128]{3,2,1,0:T(8,128)} %gain.5, s32[16,64,128]{2,1,0:T(8,128)} %mask.5), custom_call_target="tpu_custom_call" | custom-call | tf_op jit(solution)/shard_map/scaled_messages/pallas_call | solution.py:121
  3.4 3.1 %collective-permute-start = (f32[528,128]{1,0:T(8,128)}, f32[528,128]{1,0:T(8,128)S(1)}, u32[]{:S(2)}, u32[]{:S(2)}) collective-permute-start(f32[528,128]{1,0:T(8,128)} %get-tuple-element.45), channel_id=1, source_target_pairs={{0,8},{8,16},{16,24},{24,0},{1,9},{9,17},{17,25},{25,1},{2,10},{10... | collective-permute-start | bytes 811016 | tf_op jit(solution)/shard_map/ppermute | solution.py:439
  6.5 2.6 %collective-permute-start.1 = (f32[528,128]{1,0:T(8,128)}, f32[528,128]{1,0:T(8,128)S(1)}, u32[]{:S(2)}, u32[]{:S(2)}) collective-permute-start(f32[528,128]{1,0:T(8,128)} %get-tuple-element.46), channel_id=1, source_target_pairs={{0,16},{8,24},{16,0},{24,8},{1,17},{9,25},{17,1},{25,9},{2,18},{10... | collective-permute-start | bytes 811016 | tf_op jit(solution)/shard_map/ppermute | solution.py:439
  9.1 1.3 %collective-permute-start.2 = (f32[528,128]{1,0:T(8,128)}, f32[528,128]{1,0:T(8,128)S(1)}, u32[]{:S(2)}, u32[]{:S(2)}) collective-permute-start(f32[528,128]{1,0:T(8,128)} %get-tuple-element.47), channel_id=1, source_target_pairs={{0,24},{8,0},{16,8},{24,16},{1,25},{9,1},{17,9},{25,17},{2,26},{10... | collective-permute-start | bytes 811016 | tf_op jit(solution)/shard_map/ppermute | solution.py:439
  10.4 0.0 copy-done.2
  10.4 0.0 copy-done.3
  10.5 0.0 copy-start.5
  10.5 1.6 %collective-permute-start.6 = (f32[32,8,128]{2,1,0:T(8,128)S(1)}, f32[32,8,128]{2,1,0:T(8,128)S(1)}, u32[]{:S(2)}, u32[]{:S(2)}) collective-permute-start(f32[32,8,128]{2,1,0:T(8,128)S(1)} %maximum_maximum_fusion), channel_id=1, source_target_pairs={{4,0},{0,4},{5,1},{1,5},{6,2},{2,6},{7,3},{3,7},{12,8},{8,12},{13,... | collective-permute-start | bytes 393224 | tf_op jit(solution)/shard_map/ppermute | solution.py:451
  12.1 0.0 copy-done.5
  12.2 0.1 copy.13.matrix
  12.2 3.3 %collective-permute-done.6 = f32[32,8,128]{2,1,0:T(8,128)S(1)} collective-permute-done((f32[32,8,128]{2,1,0:T(8,128)S(1)}, f32[32,8,128]{2,1,0:T(8,128)S(1)}, u32[]{:S(2)}, u32[]{:S(2)}) %collective-permute-start.6) | collective-permute-done | bytes 131104 | tf_op jit(solution)/shard_map/ppermute | solution.py:451
  15.6 0.0 copy-start.4
  15.6 2.3 %weight_messages.2 = (f32[320,128]{1,0:T(8,128)S(1)}, f32[320,128]{1,0:T(8,128)S(1)}, f32[320,128]{1,0:T(8,128)S(1)}, f32[320,128]{1,0:T(8,128)S(1)}) custom-call(f32[16,64,128]{2,1,0:T(8,128)S(1)} %copy-done.2, f32[16,64,128]{2,1,0:T(8,128)S(1)} %copy-done.3, f32[32,4,128]{2,1,0:T(4,128)S(1)} %get-tuple-element.100.above, ...), custom_call_target="tpu_custom_call" | custom-call | tf_op jit(solution)/shard_map/weight_messages/pallas_call | solution.py:175
  17.9 0.7 collective-permute-start.7
  18.7 0.3 collective-permute-start.8
  19.0 0.0 collective-permute-done.refs_1_
  19.0 2.8 %collective-permute-start.9 = (f32[320,128]{1,0:T(8,128)S(1)}, f32[320,128]{1,0:T(8,128)S(1)}, u32[]{:S(2)}, u32[]{:S(2)}) collective-permute-start(f32[320,128]{1,0:T(8,128)S(1)} %get-tuple-element.53), channel_id=1, source_target_pairs={{0,24},{8,0},{16,8},{24,16},{1,25},{9,1},{17,9},{25,17},{2,26},{10... | collective-permute-start | bytes 491528 | tf_op jit(solution)/shard_map/ppermute | solution.py:439
  21.8 6.0 %collective-permute-done.1.refs_2_ = f32[528,128]{1,0:T(8,128)S(1)} collective-permute-done((f32[528,128]{1,0:T(8,128)}, f32[528,128]{1,0:T(8,128)S(1)}, u32[]{:S(2)}, u32[]{:S(2)}) %collective-permute-start.1) | collective-permute-done | bytes 270368 | tf_op jit(solution)/shard_map/ppermute | solution.py:439
  27.8 0.0 collective-permute-done.2.refs_3_
  27.8 0.0 copy-done.4
  27.8 2.0 %adjoint_mix.1 = (f32[64,32,128]{2,1,0:T(8,128)S(1)}, f32[16,128]{1,0:T(8,128)S(1)}) custom-call(f32[128,128]{1,0:T(8,128)S(1)} %copy.13.matrix, f32[528,128]{1,0:T(8,128)S(1)} %copy-done.4, f32[528,128]{1,0:T(8,128)S(1)} %collective-permute-done.refs_1_, f32[528,128]{1,0:T(8,128)S(1)} %collective-permute-done.1.refs_2_, ...), custom_call_target="tpu_custom_call" | custom-call | tf_op jit(solution)/shard_map/adjoint_mix/pallas_call | solution.py:213
  29.9 1.8 %collective-permute-start.3 = (f32[264,128]{1,0:T(8,128)S(1)}, f32[264,128]{1,0:T(8,128)S(1)}, u32[]{:S(2)}, u32[]{:S(2)}) collective-permute-start(f32[264,128]{1,0:T(8,128)S(1)} %pad_maximum_fusion.3), channel_id=1, source_target_pairs={{4,0},{0,4},{5,1},{1,5},{6,2},{2,6},{7,3},{3,7},{12,8},{8,12},{13,... | collective-permute-start | bytes 405512 | tf_op jit(solution)/shard_map/ppermute | solution.py:451
  31.7 3.5 %collective-permute-done.3 = f32[264,128]{1,0:T(8,128)S(1)} collective-permute-done((f32[264,128]{1,0:T(8,128)S(1)}, f32[264,128]{1,0:T(8,128)S(1)}, u32[]{:S(2)}, u32[]{:S(2)}) %collective-permute-start.3) | collective-permute-done | bytes 135200 | tf_op jit(solution)/shard_map/ppermute | solution.py:451
  35.3 0.4 collective-permute-start.5
  35.8 12.4 %collective-permute-start.4 = (f32[288,128]{1,0:T(8,128)S(1)}, f32[288,128]{1,0:T(8,128)S(1)}, u32[]{:S(2)}, u32[]{:S(2)}) collective-permute-start(f32[288,128]{1,0:T(8,128)S(1)} %bitcast.38), channel_id=1, source_target_pairs={{0,8},{8,16},{16,24},{24,25},{25,17},{17,9},{9,1},{1,2},{2,10},{10... | collective-permute-start | bytes 442376 | tf_op jit(solution)/shard_map/ppermute | solution.py:457
  48.2 2.0 %weight_messages.3 = (f32[256,128]{1,0:T(8,128)S(1)}, f32[256,128]{1,0:T(8,128)S(1)}, f32[256,128]{1,0:T(8,128)S(1)}, f32[256,128]{1,0:T(8,128)S(1)}) custom-call(f32[16,64,128]{2,1,0:T(8,128)S(1)} %copy-done.2, f32[16,64,128]{2,1,0:T(8,128)S(1)} %copy-done.3, f32[32,4,128]{2,1,0:T(4,128)S(1)} %get-tuple-element.100.above, ...), custom_call_target="tpu_custom_call" | custom-call | tf_op jit(solution)/shard_map/weight_messages/pallas_call | solution.py:175
  50.2 2.6 %collective-permute-done.5 = f32[312,128]{1,0:T(8,128)S(1)} collective-permute-done((f32[312,128]{1,0:T(8,128)S(1)}, f32[312,128]{1,0:T(8,128)S(1)}, u32[]{:S(2)}, u32[]{:S(2)}) %collective-permute-start.5) | collective-permute-done | bytes 159776 | tf_op jit(solution)/shard_map/ppermute | solution.py:457
  52.8 0.0 collective-permute-done.7.refs_1_
  52.8 0.0 collective-permute-done.8.refs_2_
  52.9 0.0 collective-permute-done.9.refs_3_
  52.9 0.0 collective-permute-done.4.refs_3_
  52.9 0.6 collective-permute-start.12
  53.4 2.1 %collective-permute-start.13 = (f32[256,128]{1,0:T(8,128)S(1)}, f32[256,128]{1,0:T(8,128)S(1)}, u32[]{:S(2)}, u32[]{:S(2)}) collective-permute-start(f32[256,128]{1,0:T(8,128)S(1)} %get-tuple-element.73), channel_id=1, source_target_pairs={{0,16},{8,24},{16,0},{24,8},{1,17},{9,25},{17,1},{25,9},{2,18},{10... | collective-permute-start | bytes 393224 | tf_op jit(solution)/shard_map/ppermute | solution.py:439
  55.5 2.5 %collective-permute-start.14 = (f32[256,128]{1,0:T(8,128)S(1)}, f32[256,128]{1,0:T(8,128)S(1)}, u32[]{:S(2)}, u32[]{:S(2)}) collective-permute-start(f32[256,128]{1,0:T(8,128)S(1)} %get-tuple-element.74), channel_id=1, source_target_pairs={{0,24},{8,0},{16,8},{24,16},{1,25},{9,1},{17,9},{25,17},{2,26},{10... | collective-permute-start | bytes 393224 | tf_op jit(solution)/shard_map/ppermute | solution.py:439
  58.1 0.4 turn_weights.2.refs_5_
  58.6 0.1 collective-permute-start.10
  58.6 1.7 %collective-permute-start.11 = (f32[160,128]{1,0:T(8,128)S(1)}, f32[160,128]{1,0:T(8,128)S(1)}, u32[]{:S(2)}, u32[]{:S(2)}) collective-permute-start(f32[160,128]{1,0:T(8,128)S(1)} %bitcast.39), channel_id=1, source_target_pairs={{8,0},{16,8},{24,16},{25,24},{17,25},{9,17},{1,9},{2,1},{10,2},{18... | collective-permute-start | bytes 245768 | tf_op jit(solution)/shard_map/ppermute | solution.py:457
  60.4 2.9 %collective-permute-done.10.refs_6_ = f32[160,128]{1,0:T(8,128)S(1)} collective-permute-done((f32[160,128]{1,0:T(8,128)S(1)}, f32[160,128]{1,0:T(8,128)S(1)}, u32[]{:S(2)}, u32[]{:S(2)}) %collective-permute-start.10) | collective-permute-done | bytes 81952 | tf_op jit(solution)/shard_map/ppermute | solution.py:457
  63.3 3.1 %collective-permute-done.11.refs_7_ = f32[160,128]{1,0:T(8,128)S(1)} collective-permute-done((f32[160,128]{1,0:T(8,128)S(1)}, f32[160,128]{1,0:T(8,128)S(1)}, u32[]{:S(2)}, u32[]{:S(2)}) %collective-permute-start.11) | collective-permute-done | bytes 81952 | tf_op jit(solution)/shard_map/ppermute | solution.py:457
  66.4 3.2 %spread_mix.3 = (f32[256,128]{1,0:T(8,128)S(1)}, f32[256,128]{1,0:T(8,128)S(1)}, f32[256,128]{1,0:T(8,128)S(1)}, f32[256,128]{1,0:T(8,128)S(1)}) custom-call(f32[128,128]{1,0:T(8,128)S(1)} %get-tuple-element.111.matrix, f32[64,32,128]{2,1,0:T(8,128)S(1)} %get-tuple-element.58.refs_0_, f32[4,32,128]{2,1,0:T(8,128)S(1)} %bitcast.32, ...), custom_call_target="tpu_custom_call" | custom-call | tf_op jit(solution)/shard_map/spread_mix/pallas_call | solution.py:367
  69.6 3.4 %collective-permute-start.20 = (f32[256,128]{1,0:T(8,128)S(1)}, f32[256,128]{1,0:T(8,128)S(1)}, u32[]{:S(2)}, u32[]{:S(2)}) collective-permute-start(f32[256,128]{1,0:T(8,128)S(1)} %get-tuple-element.80), channel_id=1, source_target_pairs={{0,8},{8,16},{16,24},{24,0},{1,9},{9,17},{17,25},{25,1},{2,10},{10... | collective-permute-start | bytes 393224 | tf_op jit(solution)/shard_map/ppermute | solution.py:439
  73.1 0.0 collective-permute-done.12.refs_1_
  73.1 0.0 collective-permute-done.13.refs_2_
  73.1 0.0 collective-permute-done.14.refs_3_
  73.1 0.4 turn_weights.3.refs_8_
  73.5 1.4 %collective-permute-start.15 = (f32[128,128]{1,0:T(8,128)S(1)}, f32[128,128]{1,0:T(8,128)S(1)}, u32[]{:S(2)}, u32[]{:S(2)}) collective-permute-start(f32[128,128]{1,0:T(8,128)S(1)} %bitcast.42), channel_id=1, source_target_pairs={{0,8},{8,16},{16,24},{24,25},{25,17},{17,9},{9,1},{1,2},{2,10},{10... | collective-permute-start | bytes 196616 | tf_op jit(solution)/shard_map/ppermute | solution.py:457
  74.9 0.4 collective-permute-start.16
  75.3 1.2 %collective-permute-start.21 = (f32[256,128]{1,0:T(8,128)S(1)}, f32[256,128]{1,0:T(8,128)S(1)}, u32[]{:S(2)}, u32[]{:S(2)}) collective-permute-start(f32[256,128]{1,0:T(8,128)S(1)} %get-tuple-element.81), channel_id=1, source_target_pairs={{0,16},{8,24},{16,0},{24,8},{1,17},{9,25},{17,1},{25,9},{2,18},{10... | collective-permute-start | bytes 393224 | tf_op jit(solution)/shard_map/ppermute | solution.py:439
  76.5 2.9 %collective-permute-start.22 = (f32[256,128]{1,0:T(8,128)S(1)}, f32[256,128]{1,0:T(8,128)S(1)}, u32[]{:S(2)}, u32[]{:S(2)}) collective-permute-start(f32[256,128]{1,0:T(8,128)S(1)} %get-tuple-element.82), channel_id=1, source_target_pairs={{0,24},{8,0},{16,8},{24,16},{1,25},{9,1},{17,9},{25,17},{2,26},{10... | collective-permute-start | bytes 393224 | tf_op jit(solution)/shard_map/ppermute | solution.py:439
  79.3 0.0 collective-permute-done.15.refs_9_
  79.3 0.7 collective-permute-done.16.refs_10_
  80.1 3.2 %spread_mix.2 = (f32[256,128]{1,0:T(8,128)S(1)}, f32[256,128]{1,0:T(8,128)S(1)}, f32[256,128]{1,0:T(8,128)S(1)}, f32[256,128]{1,0:T(8,128)S(1)}) custom-call(f32[128,128]{1,0:T(8,128)S(1)} %get-tuple-element.111.matrix, f32[64,32,128]{2,1,0:T(8,128)S(1)} %get-tuple-element.58.refs_0_, f32[4,32,128]{2,1,0:T(8,128)S(1)} %bitcast.33, ...), custom_call_target="tpu_custom_call" | custom-call | tf_op jit(solution)/shard_map/spread_mix/pallas_call | solution.py:367
  83.3 5.4 %collective-permute-start.17 = (f32[256,128]{1,0:T(8,128)S(1)}, f32[256,128]{1,0:T(8,128)S(1)}, u32[]{:S(2)}, u32[]{:S(2)}) collective-permute-start(f32[256,128]{1,0:T(8,128)S(1)} %get-tuple-element.76), channel_id=1, source_target_pairs={{0,8},{8,16},{16,24},{24,0},{1,9},{9,17},{17,25},{25,1},{2,10},{10... | collective-permute-start | bytes 393224 | tf_op jit(solution)/shard_map/ppermute | solution.py:439
  88.7 2.0 %collective-permute-start.18 = (f32[256,128]{1,0:T(8,128)S(1)}, f32[256,128]{1,0:T(8,128)S(1)}, u32[]{:S(2)}, u32[]{:S(2)}) collective-permute-start(f32[256,128]{1,0:T(8,128)S(1)} %get-tuple-element.77), channel_id=1, source_target_pairs={{0,16},{8,24},{16,0},{24,8},{1,17},{9,25},{17,1},{25,9},{2,18},{10... | collective-permute-start | bytes 393224 | tf_op jit(solution)/shard_map/ppermute | solution.py:439
  90.7 0.0 collective-permute-done.20.refs_1_
  90.7 2.8 %collective-permute-start.19 = (f32[256,128]{1,0:T(8,128)S(1)}, f32[256,128]{1,0:T(8,128)S(1)}, u32[]{:S(2)}, u32[]{:S(2)}) collective-permute-start(f32[256,128]{1,0:T(8,128)S(1)} %get-tuple-element.78), channel_id=1, source_target_pairs={{0,24},{8,0},{16,8},{24,16},{1,25},{9,1},{17,9},{25,17},{2,26},{10... | collective-permute-start | bytes 393224 | tf_op jit(solution)/shard_map/ppermute | solution.py:439
  93.5 0.0 collective-permute-done.21.refs_2_
  93.5 0.0 collective-permute-done.22.refs_3_
  93.5 0.0 copy-done
  93.5 2.3 %result.2.refs_4_ = f32[2,16,64,128]{3,2,1,0:T(8,128)} custom-call(f32[2,16,64,128]{3,2,1,0:T(8,128)S(1)} %copy-done, s32[16,64,128]{2,1,0:T(8,128)S(1)} %copy-done.1, f32[256,128]{1,0:T(8,128)S(1)} %get-tuple-element.79.refs_0_, f32[256,128]{1,0:T(8,128)S(1)} %collective-permute-done.20.refs_1_, f32[256,128]{1,0:T(8,128)S(1)} %collective-permute-done.21.refs_2_, ...), custom_call_target="tpu_custom_call" | custom-call | tf_op jit(solution)/shard_map/result/pallas_call | solution.py:408
  95.8 0.0 collective-permute-done.17.refs_1_
  95.8 1.0 %collective-permute-done.18.refs_2_ = f32[256,128]{1,0:T(8,128)S(1)} collective-permute-done((f32[256,128]{1,0:T(8,128)S(1)}, f32[256,128]{1,0:T(8,128)S(1)}, u32[]{:S(2)}, u32[]{:S(2)}) %collective-permute-start.18) | collective-permute-done | bytes 131104 | tf_op jit(solution)/shard_map/ppermute | solution.py:439
  96.9 0.0 collective-permute-done.19.refs_3_
  96.9 2.3 %result.3 = f32[2,16,64,128]{3,2,1,0:T(8,128)} custom-call(f32[2,16,64,128]{3,2,1,0:T(8,128)S(1)} %copy-done, s32[16,64,128]{2,1,0:T(8,128)S(1)} %copy-done.1, f32[256,128]{1,0:T(8,128)S(1)} %get-tuple-element.75.refs_0_, f32[256,128]{1,0:T(8,128)S(1)} %collective-permute-done.17.refs_1_, ...), custom_call_target="tpu_custom_call", output_to_operand_aliasing={{}: (6, {})} | custom-call | tf_op jit(solution)/shard_map/result/pallas_call | solution.py:408
  (27 shorter events, 0.4 us)
Async XLA Ops:
  0.0 10.4 %copy-start.2 = (f32[16,64,128]{2,1,0:T(8,128)S(1)}, f32[16,64,128]{2,1,0:T(8,128)}, u32[]{:S(2)}) copy-start(f32[16,64,128]{2,1,0:T(8,128)} %along_i.3) | copy-start | bytes 1572868
  0.0 10.4 %copy-start.3 = (f32[16,64,128]{2,1,0:T(8,128)S(1)}, f32[16,64,128]{2,1,0:T(8,128)}, u32[]{:S(2)}) copy-start(f32[16,64,128]{2,1,0:T(8,128)} %along_j.3) | copy-start | bytes 1572868
  3.4 15.6 %collective-permute-start = (f32[528,128]{1,0:T(8,128)}, f32[528,128]{1,0:T(8,128)S(1)}, u32[]{:S(2)}, u32[]{:S(2)}) collective-permute-start(f32[528,128]{1,0:T(8,128)} %get-tuple-element.45), channel_id=1, source_target_pairs={{0,8},{8,16},{16,24},{24,0},{1,9},{9,17},{17,25},{25,1},{2,10},{10... | collective-permute-start | bytes 811016 | tf_op jit(solution)/shard_map/ppermute | solution.py:439
  6.5 21.3 %collective-permute-start.1 = (f32[528,128]{1,0:T(8,128)}, f32[528,128]{1,0:T(8,128)S(1)}, u32[]{:S(2)}, u32[]{:S(2)}) collective-permute-start(f32[528,128]{1,0:T(8,128)} %get-tuple-element.46), channel_id=1, source_target_pairs={{0,16},{8,24},{16,0},{24,8},{1,17},{9,25},{17,1},{25,9},{2,18},{10... | collective-permute-start | bytes 811016 | tf_op jit(solution)/shard_map/ppermute | solution.py:439
  9.1 18.7 %collective-permute-start.2 = (f32[528,128]{1,0:T(8,128)}, f32[528,128]{1,0:T(8,128)S(1)}, u32[]{:S(2)}, u32[]{:S(2)}) collective-permute-start(f32[528,128]{1,0:T(8,128)} %get-tuple-element.47), channel_id=1, source_target_pairs={{0,24},{8,0},{16,8},{24,16},{1,25},{9,1},{17,9},{25,17},{2,26},{10... | collective-permute-start | bytes 811016 | tf_op jit(solution)/shard_map/ppermute | solution.py:439
  10.5 1.6 %copy-start.5 = (f32[128,128]{1,0:T(8,128)S(1)}, f32[128,128]{1,0:T(8,128)}, u32[]{:S(2)}) copy-start(f32[128,128]{1,0:T(8,128)} %param.11) | copy-start | bytes 196612
  10.5 5.0 %collective-permute-start.6 = (f32[32,8,128]{2,1,0:T(8,128)S(1)}, f32[32,8,128]{2,1,0:T(8,128)S(1)}, u32[]{:S(2)}, u32[]{:S(2)}) collective-permute-start(f32[32,8,128]{2,1,0:T(8,128)S(1)} %maximum_maximum_fusion), channel_id=1, source_target_pairs={{4,0},{0,4},{5,1},{1,5},{6,2},{2,6},{7,3},{3,7},{12,8},{8,12},{13,... | collective-permute-start | bytes 393224 | tf_op jit(solution)/shard_map/ppermute | solution.py:451
  15.6 12.2 %copy-start.4 = (f32[528,128]{1,0:T(8,128)S(1)}, f32[528,128]{1,0:T(8,128)}, u32[]{:S(2)}) copy-start(f32[528,128]{1,0:T(8,128)} %get-tuple-element.44.refs_0_) | copy-start | bytes 811012
  17.9 34.9 %collective-permute-start.7 = (f32[320,128]{1,0:T(8,128)S(1)}, f32[320,128]{1,0:T(8,128)S(1)}, u32[]{:S(2)}, u32[]{:S(2)}) collective-permute-start(f32[320,128]{1,0:T(8,128)S(1)} %get-tuple-element.51), channel_id=1, source_target_pairs={{0,8},{8,16},{16,24},{24,0},{1,9},{9,17},{17,25},{25,1},{2,10},{10... | collective-permute-start | bytes 491528 | tf_op jit(solution)/shard_map/ppermute | solution.py:439
  18.7 34.2 %collective-permute-start.8 = (f32[320,128]{1,0:T(8,128)S(1)}, f32[320,128]{1,0:T(8,128)S(1)}, u32[]{:S(2)}, u32[]{:S(2)}) collective-permute-start(f32[320,128]{1,0:T(8,128)S(1)} %get-tuple-element.52), channel_id=1, source_target_pairs={{0,16},{8,24},{16,0},{24,8},{1,17},{9,25},{17,1},{25,9},{2,18},{10... | collective-permute-start | bytes 491528 | tf_op jit(solution)/shard_map/ppermute | solution.py:439
  19.0 33.9 %collective-permute-start.9 = (f32[320,128]{1,0:T(8,128)S(1)}, f32[320,128]{1,0:T(8,128)S(1)}, u32[]{:S(2)}, u32[]{:S(2)}) collective-permute-start(f32[320,128]{1,0:T(8,128)S(1)} %get-tuple-element.53), channel_id=1, source_target_pairs={{0,24},{8,0},{16,8},{24,16},{1,25},{9,1},{17,9},{25,17},{2,26},{10... | collective-permute-start | bytes 491528 | tf_op jit(solution)/shard_map/ppermute | solution.py:439
  29.9 5.4 %collective-permute-start.3 = (f32[264,128]{1,0:T(8,128)S(1)}, f32[264,128]{1,0:T(8,128)S(1)}, u32[]{:S(2)}, u32[]{:S(2)}) collective-permute-start(f32[264,128]{1,0:T(8,128)S(1)} %pad_maximum_fusion.3), channel_id=1, source_target_pairs={{4,0},{0,4},{5,1},{1,5},{6,2},{2,6},{7,3},{3,7},{12,8},{8,12},{13,... | collective-permute-start | bytes 405512 | tf_op jit(solution)/shard_map/ppermute | solution.py:451
  35.3 17.5 %collective-permute-start.5 = (f32[312,128]{1,0:T(8,128)S(1)}, f32[312,128]{1,0:T(8,128)S(1)}, u32[]{:S(2)}, u32[]{:S(2)}) collective-permute-start(f32[312,128]{1,0:T(8,128)S(1)} %pad_maximum_fusion), channel_id=1, source_target_pairs={{8,0},{16,8},{24,16},{25,24},{17,25},{9,17},{1,9},{2,1},{10,2},{18... | collective-permute-start | bytes 479240 | tf_op jit(solution)/shard_map/ppermute | solution.py:457
  35.8 17.1 %collective-permute-start.4 = (f32[288,128]{1,0:T(8,128)S(1)}, f32[288,128]{1,0:T(8,128)S(1)}, u32[]{:S(2)}, u32[]{:S(2)}) collective-permute-start(f32[288,128]{1,0:T(8,128)S(1)} %bitcast.38), channel_id=1, source_target_pairs={{0,8},{8,16},{16,24},{24,25},{25,17},{17,9},{9,1},{1,2},{2,10},{10... | collective-permute-start | bytes 442376 | tf_op jit(solution)/shard_map/ppermute | solution.py:457
  52.9 20.2 %collective-permute-start.12 = (f32[256,128]{1,0:T(8,128)S(1)}, f32[256,128]{1,0:T(8,128)S(1)}, u32[]{:S(2)}, u32[]{:S(2)}) collective-permute-start(f32[256,128]{1,0:T(8,128)S(1)} %get-tuple-element.72), channel_id=1, source_target_pairs={{0,8},{8,16},{16,24},{24,0},{1,9},{9,17},{17,25},{25,1},{2,10},{10... | collective-permute-start | bytes 393224 | tf_op jit(solution)/shard_map/ppermute | solution.py:439
  53.4 19.6 %collective-permute-start.13 = (f32[256,128]{1,0:T(8,128)S(1)}, f32[256,128]{1,0:T(8,128)S(1)}, u32[]{:S(2)}, u32[]{:S(2)}) collective-permute-start(f32[256,128]{1,0:T(8,128)S(1)} %get-tuple-element.73), channel_id=1, source_target_pairs={{0,16},{8,24},{16,0},{24,8},{1,17},{9,25},{17,1},{25,9},{2,18},{10... | collective-permute-start | bytes 393224 | tf_op jit(solution)/shard_map/ppermute | solution.py:439
  55.5 17.5 %collective-permute-start.14 = (f32[256,128]{1,0:T(8,128)S(1)}, f32[256,128]{1,0:T(8,128)S(1)}, u32[]{:S(2)}, u32[]{:S(2)}) collective-permute-start(f32[256,128]{1,0:T(8,128)S(1)} %get-tuple-element.74), channel_id=1, source_target_pairs={{0,24},{8,0},{16,8},{24,16},{1,25},{9,1},{17,9},{25,17},{2,26},{10... | collective-permute-start | bytes 393224 | tf_op jit(solution)/shard_map/ppermute | solution.py:439
  58.6 4.7 %collective-permute-start.10 = (f32[160,128]{1,0:T(8,128)S(1)}, f32[160,128]{1,0:T(8,128)S(1)}, u32[]{:S(2)}, u32[]{:S(2)}) collective-permute-start(f32[160,128]{1,0:T(8,128)S(1)} %bitcast.40), channel_id=1, source_target_pairs={{0,8},{8,16},{16,24},{24,25},{25,17},{17,9},{9,1},{1,2},{2,10},{10... | collective-permute-start | bytes 245768 | tf_op jit(solution)/shard_map/ppermute | solution.py:457
  58.6 7.7 %collective-permute-start.11 = (f32[160,128]{1,0:T(8,128)S(1)}, f32[160,128]{1,0:T(8,128)S(1)}, u32[]{:S(2)}, u32[]{:S(2)}) collective-permute-start(f32[160,128]{1,0:T(8,128)S(1)} %bitcast.39), channel_id=1, source_target_pairs={{8,0},{16,8},{24,16},{25,24},{17,25},{9,17},{1,9},{2,1},{10,2},{18... | collective-permute-start | bytes 245768 | tf_op jit(solution)/shard_map/ppermute | solution.py:457
  69.6 21.1 %collective-permute-start.20 = (f32[256,128]{1,0:T(8,128)S(1)}, f32[256,128]{1,0:T(8,128)S(1)}, u32[]{:S(2)}, u32[]{:S(2)}) collective-permute-start(f32[256,128]{1,0:T(8,128)S(1)} %get-tuple-element.80), channel_id=1, source_target_pairs={{0,8},{8,16},{16,24},{24,0},{1,9},{9,17},{17,25},{25,1},{2,10},{10... | collective-permute-start | bytes 393224 | tf_op jit(solution)/shard_map/ppermute | solution.py:439
  73.5 5.8 %collective-permute-start.15 = (f32[128,128]{1,0:T(8,128)S(1)}, f32[128,128]{1,0:T(8,128)S(1)}, u32[]{:S(2)}, u32[]{:S(2)}) collective-permute-start(f32[128,128]{1,0:T(8,128)S(1)} %bitcast.42), channel_id=1, source_target_pairs={{0,8},{8,16},{16,24},{24,25},{25,17},{17,9},{9,1},{1,2},{2,10},{10... | collective-permute-start | bytes 196616 | tf_op jit(solution)/shard_map/ppermute | solution.py:457
  74.9 5.1 %collective-permute-start.16 = (f32[128,128]{1,0:T(8,128)S(1)}, f32[128,128]{1,0:T(8,128)S(1)}, u32[]{:S(2)}, u32[]{:S(2)}) collective-permute-start(f32[128,128]{1,0:T(8,128)S(1)} %bitcast.41), channel_id=1, source_target_pairs={{8,0},{16,8},{24,16},{25,24},{17,25},{9,17},{1,9},{2,1},{10,2},{18... | collective-permute-start | bytes 196616 | tf_op jit(solution)/shard_map/ppermute | solution.py:457
  75.3 18.2 %collective-permute-start.21 = (f32[256,128]{1,0:T(8,128)S(1)}, f32[256,128]{1,0:T(8,128)S(1)}, u32[]{:S(2)}, u32[]{:S(2)}) collective-permute-start(f32[256,128]{1,0:T(8,128)S(1)} %get-tuple-element.81), channel_id=1, source_target_pairs={{0,16},{8,24},{16,0},{24,8},{1,17},{9,25},{17,1},{25,9},{2,18},{10... | collective-permute-start | bytes 393224 | tf_op jit(solution)/shard_map/ppermute | solution.py:439
  76.5 17.1 %copy-start = (f32[2,16,64,128]{3,2,1,0:T(8,128)S(1)}, f32[2,16,64,128]{3,2,1,0:T(8,128)}, u32[]{:S(2)}) copy-start(f32[2,16,64,128]{3,2,1,0:T(8,128)} %gain.5) | copy-start | bytes 3145732
  76.5 17.1 %copy-start.1 = (s32[16,64,128]{2,1,0:T(8,128)S(1)}, s32[16,64,128]{2,1,0:T(8,128)}, u32[]{:S(2)}) copy-start(s32[16,64,128]{2,1,0:T(8,128)} %mask.5) | copy-start | bytes 1572868
  76.5 17.1 %collective-permute-start.22 = (f32[256,128]{1,0:T(8,128)S(1)}, f32[256,128]{1,0:T(8,128)S(1)}, u32[]{:S(2)}, u32[]{:S(2)}) collective-permute-start(f32[256,128]{1,0:T(8,128)S(1)} %get-tuple-element.82), channel_id=1, source_target_pairs={{0,24},{8,0},{16,8},{24,16},{1,25},{9,1},{17,9},{25,17},{2,26},{10... | collective-permute-start | bytes 393224 | tf_op jit(solution)/shard_map/ppermute | solution.py:439
  83.3 12.5 %collective-permute-start.17 = (f32[256,128]{1,0:T(8,128)S(1)}, f32[256,128]{1,0:T(8,128)S(1)}, u32[]{:S(2)}, u32[]{:S(2)}) collective-permute-start(f32[256,128]{1,0:T(8,128)S(1)} %get-tuple-element.76), channel_id=1, source_target_pairs={{0,8},{8,16},{16,24},{24,0},{1,9},{9,17},{17,25},{25,1},{2,10},{10... | collective-permute-start | bytes 393224 | tf_op jit(solution)/shard_map/ppermute | solution.py:439
  88.7 8.2 %collective-permute-start.18 = (f32[256,128]{1,0:T(8,128)S(1)}, f32[256,128]{1,0:T(8,128)S(1)}, u32[]{:S(2)}, u32[]{:S(2)}) collective-permute-start(f32[256,128]{1,0:T(8,128)S(1)} %get-tuple-element.77), channel_id=1, source_target_pairs={{0,16},{8,24},{16,0},{24,8},{1,17},{9,25},{17,1},{25,9},{2,18},{10... | collective-permute-start | bytes 393224 | tf_op jit(solution)/shard_map/ppermute | solution.py:439
  90.7 6.2 %collective-permute-start.19 = (f32[256,128]{1,0:T(8,128)S(1)}, f32[256,128]{1,0:T(8,128)S(1)}, u32[]{:S(2)}, u32[]{:S(2)}) collective-permute-start(f32[256,128]{1,0:T(8,128)S(1)} %get-tuple-element.78), channel_id=1, source_target_pairs={{0,24},{8,0},{16,8},{24,16},{1,25},{9,1},{17,9},{25,17},{2,26},{10... | collective-permute-start | bytes 393224 | tf_op jit(solution)/shard_map/ppermute | solution.py:439

commit v4 on v3

v4 whole, which is shorter than its diff:
```python
import functools

import jax
import jax.numpy as jnp
from jax import lax
from jax.experimental import pallas as pl
from jax.experimental.pallas import tpu as pltpu
from jax.sharding import PartitionSpec as P

ITERS = 2
STEPS = 2 * ITERS
PAD = 8
VMEM_LIMIT = 40 * 1024 * 1024
VMEM_WHOLE = 60 * 1024 * 1024
HIGHEST = lax.Precision.HIGHEST


def params(limit=VMEM_LIMIT):
    return pltpu.CompilerParams(vmem_limit_bytes=limit)


def smem():
    return pl.BlockSpec(memory_space=pltpu.SMEM)


def vmem():
    return pl.BlockSpec(memory_space=pltpu.VMEM)


def position():
    devices = lax.axis_size("lev")
    me = lax.axis_index("lev")
    flipped = lax.rem(lax.axis_index("gy"), 2) == 1

    def slot(lev):
        return jnp.where(flipped, devices - 1 - lev, lev)

    to = [lax.rem(me + d, devices) for d in range(devices)]
    source = [lax.rem(me + devices - d, devices) for d in range(devices)]
    return [slot(lev) for lev in to], [slot(lev) for lev in source], source


def swap(blocks, group, width):
    blocks = list(blocks)
    cols = blocks[0].shape[1]
    bit = len(blocks) // 2
    while bit:
        shift = bit * width
        low = (group & bit) == 0
        for a in range(len(blocks)):
            if not a & bit:
                x, y = blocks[a], blocks[a + bit]
                blocks[a] = jnp.where(low, x, pltpu.roll(y, shift, 1))
                blocks[a + bit] = jnp.where(low, pltpu.roll(x, cols - shift, 1), y)
        bit //= 2
    return blocks


def lane_groups(rows, cols, groups):
    return lax.broadcasted_iota(jnp.int32, (rows, cols), 1) // (cols // groups)


def copies(pairs, sems):
    made = [pltpu.make_async_copy(src, dst, sems.at[k]) for k, (src, dst) in enumerate(pairs)]
    for copy in made:
        copy.start()
    return made


SCALED_STEPS = 4


def scaled_kernel(increment, gain, mask, *refs):
    outs, (inc, gn, sea, held, sems, out_sems) = refs[:-6], refs[-6:]
    fields, levels, length, cols = increment.shape
    groups = len(outs)
    rows = length // groups
    some = levels // SCALED_STEPS
    group = lane_groups(rows, cols, groups)
    fetched = []
    for step in range(SCALED_STEPS):
        part = pl.ds(step * some, some)
        fetched.append(
            copies(
                [
                    (increment.at[:, part], inc.at[:, part]),
                    (gain.at[:, part], gn.at[:, part]),
                    (mask.at[part], sea.at[part]),
                ],
                sems.at[step],
            )
        )

    for step in range(SCALED_STEPS):
        for copy in fetched[step]:
            copy.wait()

        def one(level, carry):
            ocean = sea[level].astype(jnp.float32)
            for field in range(fields):
                at = pl.multiple_of((field * levels + level) * rows, rows)
                x = ocean * gn[field, level] * inc[field, level]
                blocks = swap([x[a * rows:(a + 1) * rows] for a in range(groups)], group, cols // groups)
                for slot, block in enumerate(blocks):
                    held[slot, pl.ds(at, rows), :] = block
            return carry

        lax.fori_loop(step * some, (step + 1) * some, one, 0, unroll=True)
    slots = position()[0]
    for copy in copies([(held.at[slots[d]], out) for d, out in enumerate(outs)], out_sems):
        copy.wait()


def scaled_messages(increment, gain, mask, groups):
    fields, levels, length, cols = increment.shape
    shape = (fields * levels * length // groups, cols)
    return pl.pallas_call(
        scaled_kernel,
        in_specs=[pl.BlockSpec(memory_space=pl.ANY)] * 3,
        out_specs=[pl.BlockSpec(memory_space=pl.ANY)] * groups,
        out_shape=[jax.ShapeDtypeStruct(shape, jnp.float32)] * groups,
        scratch_shapes=[
            pltpu.VMEM(increment.shape, jnp.float32),
            pltpu.VMEM(gain.shape, jnp.float32),
            pltpu.VMEM(mask.shape, mask.dtype),
            pltpu.VMEM((groups, *shape), jnp.float32),
            pltpu.SemaphoreType.DMA((SCALED_STEPS, 3)),
            pltpu.SemaphoreType.DMA((groups,)),
        ],
        compiler_params=params(VMEM_WHOLE),
        name="scaled_messages",
    )(increment, gain, mask)


def pack_kernel(starts, rows, masked, along_i, along_j, *refs):
    levels, length, cols = along_i.shape
    groups = len(starts)
    halos, outs = refs[masked:-4 - groups - 3 * masked], refs[-4 - groups - 3 * masked:-4 - 3 * masked]
    held, slots_held, sems, fetch_sems = refs[-4:]
    if masked:
        pairs = list(zip((along_i, along_j, refs[0]), refs[-7:-4]))
        fetched = copies(pairs, fetch_sems)
        along_i, along_j, sea = refs[-7:-4]
        for copy in fetched[:2]:
            copy.wait()
    group = lane_groups(rows, cols, groups)
    unroll = held.shape[0]

    for side, weight in enumerate((along_i, along_j)):

        def some(outer, carry, side=side, weight=weight):
            for halo, at in zip(halos, (0, STEPS + length)):
                size = unroll * STEPS
                block = halo[pl.ds(pl.multiple_of(side * levels * STEPS + outer * size, 8), size), :]
                for k in range(unroll):
                    held[k, pl.ds(at, STEPS), :] = block[k * STEPS:(k + 1) * STEPS]
            for k in range(unroll):
                held[k, pl.ds(STEPS, length), :] = weight[outer * unroll + k]
            packed = [
                swap([held[k, pl.ds(start, rows), :] for start in starts], group, cols // groups)
                for k in range(unroll)
            ]
            at = pl.multiple_of((side * levels + outer * unroll) * rows, 8)
            for slot in range(groups):
                block = jnp.concatenate([packed[k][slot] for k in range(unroll)], axis=0)
                slots_held[slot, pl.ds(at, unroll * rows), :] = block
            return carry

        lax.fori_loop(0, levels // unroll, some, 0)
    if masked:
        fetched[2].wait()
        depth = sea[0]
        for level in range(1, levels):
            depth = depth + sea[level]
        depth = depth.astype(jnp.float32)
        size = length // groups
        blocks = [depth[a * size:(a + 1) * size] for a in range(groups)]
        for slot, block in enumerate(swap(blocks, lane_groups(size, cols, groups), cols // groups)):
            slots_held[slot, pl.ds(2 * levels * rows, size), :] = block
    slots = position()[0]
    for copy in copies([(slots_held.at[slots[d]], out) for d, out in enumerate(outs)], sems):
        copy.wait()


def weight_messages(starts, rows, along_i, along_j, mask=(), halos=()):
    levels, length, cols = along_i.shape
    groups = len(starts)
    shape = (2 * levels * rows + len(mask) * length // groups, cols)
    unroll = 4
    return list(
        pl.pallas_call(
            functools.partial(pack_kernel, starts, rows, len(mask)),
            in_specs=[pl.BlockSpec(memory_space=pl.ANY) if mask else vmem()] * (2 + len(mask) + len(halos)),
            out_specs=[pl.BlockSpec(memory_space=pl.ANY)] * groups,
            out_shape=[jax.ShapeDtypeStruct(shape, jnp.float32)] * groups,
            scratch_shapes=[pltpu.VMEM(x.shape, x.dtype) for x in ([along_i, along_j, *mask] if mask else [])]
            + [
                pltpu.VMEM((unroll, length + 2 * STEPS, cols), jnp.float32),
                pltpu.VMEM((groups, *shape), jnp.float32),
                pltpu.SemaphoreType.DMA((groups,)),
                pltpu.SemaphoreType.DMA((3,)),
            ],
            compiler_params=params(VMEM_WHOLE if mask else VMEM_LIMIT),
            name="weight_messages",
        )(along_i, along_j, *mask, *halos)
    )


def adjoint_kernel(matrix, depths, *refs):
    parts, out = refs[:-1], refs[-1]
    length, width, order = out.shape
    groups = len(parts)
    rows = length // groups
    cols = groups * width
    count = order // groups
    level = lax.rem(lax.broadcasted_iota(jnp.int32, (order, cols), 0), order // 2).astype(jnp.float32)

    def one(i, carry):
        x = jnp.concatenate([part[pl.ds(i, count, rows), :] for part in parts], axis=0)
        depth = depths[pl.ds(i, 1), :]
        y = jnp.dot(matrix[...], x, precision=HIGHEST, preferred_element_type=jnp.float32)
        y = jnp.where(level < depth, y, 0.0).T
        for a in range(groups):
            out[a * rows + i] = y[a * width:(a + 1) * width]
        return carry

    lax.fori_loop(0, rows, one, 0, unroll=4)


def adjoint_mix(matrix, depths, parts, length, width):
    return pl.pallas_call(
        adjoint_kernel,
        in_specs=[vmem()] * (2 + len(parts)),
        out_specs=vmem(),
        out_shape=jax.ShapeDtypeStruct((length, width, matrix.shape[0]), jnp.float32),
        compiler_params=params(),
        name="adjoint_mix",
    )(matrix, depths, *parts)


def unfold(main, halo, groups):
    cols = main.shape[1]
    width = cols // groups
    below = halo[:STEPS]
    above = pltpu.roll(halo[STEPS:], width, 1)
    return jnp.concatenate(
        [above] + [main] + [pltpu.roll(main, cols - a * width, 1) for a in range(1, groups)] + [below], axis=0
    )


def turn_kernel(starts, *refs):
    depths, parts, (out, held, depth_i, depth_j) = refs[:-4 - len(starts)], refs[-4 - len(starts):-4], refs[-4:]
    length, width, order = out.shape
    groups = len(parts)
    rows = length // groups
    half = order // 2
    count = half // groups
    cols = width * groups
    source = position()[2]
    for i in range(rows):
        for d, part in enumerate(parts):
            for side in range(2):
                at = pl.multiple_of(side * half + source[d] * count, 8)
                held[i, pl.ds(at, count), :] = part[pl.ds(side * count * rows + i, count, rows), :]

    ends = (position()[0][0] == groups - 1) & (lax.axis_index("gy") == lax.axis_size("gy") - 1)
    no_halo = jnp.zeros((2 * STEPS, cols), jnp.float32)
    main, right_main = depths[0][...], depths[1][...]
    halo, right_halo = [ref[...] for ref in depths[2:]] or (no_halo, no_halo)
    depth = unfold(main, halo, groups)
    right = jnp.where(ends, 0.0, unfold(right_main, right_halo, groups))
    tall = depth.shape[0]
    lane = lax.broadcasted_iota(jnp.int32, depth.shape, 1)
    right = jnp.where(lane == width - 1, pltpu.roll(right, width - 1, 1), pltpu.roll(depth, cols - 1, 1))
    depth_j[...] = jnp.minimum(depth, right)
    depth_i[pl.ds(0, tall - 1), :] = jnp.minimum(depth[:-1], depth[1:])
    depth_i[pl.ds(tall - 1, 1), :] = depth[tall - 1:]
    group = lane_groups(rows, cols, groups)

    def fold(ref):
        x = ref[pl.ds(starts[0], rows), :]
        for a in range(1, groups):
            x = jnp.where(group == a, pltpu.roll(ref[pl.ds(starts[a], rows), :], a * width, 1), x)
        return x

    folded_i, folded_j = fold(depth_i), fold(depth_j)
    level = lax.broadcasted_iota(jnp.int32, (half, cols), 0).astype(jnp.float32)
    for i in range(rows):
        along_i = jnp.where(level < folded_i[i:i + 1], held[i, pl.ds(0, half), :], 0.0)
        along_j = jnp.where(level < folded_j[i:i + 1], held[i, pl.ds(half, half), :], 0.0)
        turned = jnp.concatenate([along_i, along_j], axis=0).T
        for a in range(groups):
            out[a * rows + i] = turned[a * width:(a + 1) * width]


def turn_weights(starts, rows, depths, parts, order):
    groups = len(parts)
    cols = parts[0].shape[1]
    tall = depths[0].shape[0] * groups + 2 * STEPS
    return pl.pallas_call(
        functools.partial(turn_kernel, starts),
        in_specs=[vmem()] * (len(depths) + groups),
        out_specs=vmem(),
        out_shape=jax.ShapeDtypeStruct((rows * groups, cols // groups, order), jnp.float32),
        scratch_shapes=[pltpu.VMEM((rows, order, cols), jnp.float32)] + [pltpu.VMEM((tall, cols), jnp.float32)] * 2,
        compiler_params=params(),
        name="turn_weights",
    )(*depths, *parts)


def spread_kernel(windows, field_rows, weight_rows, matrix, *refs):
    pieces = [refs[3 * k:3 * k + 3] for k in range(len(field_rows) + len(weight_rows))]
    outs, (a, b, wi, wj) = refs[3 * len(pieces):-4], refs[-4:]
    width, order = pieces[0][0].shape[1:]
    half = order // 2
    _, ext, wide, _ = a.shape
    lane = lax.broadcasted_iota(jnp.int32, (wide, order), 1)
    nothing = jnp.zeros((PAD - STEPS, order), jnp.float32)

    def row_of(some, rows, r):
        piece = [k for k in range(len(rows)) if r in rows[k]][0]
        main, left, right = some[piece]
        k = rows[piece].index(r)
        side = pl.ds(k * STEPS, STEPS)
        return jnp.concatenate([nothing, left[side, :], main[k], right[side, :], nothing], axis=0)

    for n, window in enumerate(windows):
        for e, r in enumerate(window):
            a[n, e] = row_of(pieces[:len(field_rows)], field_rows, r)
            w = row_of(pieces[len(field_rows):], weight_rows, r)
            other = pltpu.roll(w, half, 1)
            wi[n, e] = jnp.where(lane < half, w, other)
            wj[n, e] = jnp.where(lane < half, other, w)

    src, dst = a, b
    for step in range(STEPS):
        begin, last = step + 1, ext - 2 - step
        for n in range(len(windows)):

            def one(r, carry, n=n, src=src, dst=dst):
                v, before = carry
                after = src[n, r + 1]
                flux = wi[n, r] * (after - v)
                across = wj[n, r] * (pltpu.roll(v, wide - 1, 0) - v)
                dst[n, r] = v + (flux - before) + (across - pltpu.roll(across, 1, 0))
                return after, flux

            v = src[n, begin]
            lax.fori_loop(begin, last + 1, one, (v, wi[n, begin - 1] * (v - src[n, begin - 1])), unroll=2)
        src, dst = dst, src

    groups = len(outs)
    count = order // groups
    rows = len(windows) * (ext - 2 * STEPS) // groups
    each = groups // len(windows)

    def mix(i, carry):
        x = jnp.concatenate(
            [src[g // each, STEPS + g % each * rows + i, pl.ds(PAD, width), :] for g in range(groups)], axis=0
        )
        y = lax.dot_general(
            matrix[...], x, (((1,), (1,)), ((), ())), precision=HIGHEST, preferred_element_type=jnp.float32
        )
        for d, out in enumerate(outs):
            out[pl.ds(i, count, rows), :] = y[d * count:(d + 1) * count]
        return carry

    lax.fori_loop(0, rows, mix, 0, unroll=4)


def spread_mix(windows, matrix, field, weights, groups):
    width, order = field[0][1].shape[1:]
    cols = width * groups
    ext = len(windows[0])
    rows = len(windows) * (ext - 2 * STEPS) // groups
    shape = jax.ShapeDtypeStruct((order // groups * rows, cols), jnp.float32)
    arrays = [x for piece in field + weights for x in piece[1:]]
    return pl.pallas_call(
        functools.partial(spread_kernel, windows, [piece[0] for piece in field], [piece[0] for piece in weights]),
        in_specs=[vmem()] * (1 + len(arrays)),
        out_specs=[vmem()] * groups,
        out_shape=[shape] * groups,
        scratch_shapes=[pltpu.VMEM((len(windows), ext, width + 2 * PAD, order), jnp.float32)] * 4,
        compiler_params=params(),
        name="spread_mix",
    )(matrix, *arrays)


RESULT_STEPS = 4


def result_kernel(runs, gain, mask, *refs):
    parts, (out, held, done, sems, out_sems) = refs[:-5], refs[-5:]
    fields, levels, _, cols = gain.shape
    groups = held.shape[0]
    rows = done.shape[2] // groups
    some = levels // RESULT_STEPS
    slots = position()[1]
    fetched = copies([(parts[d], held.at[slots[d]]) for d in range(groups)], sems)
    group = lane_groups(rows, cols, groups)
    for copy in fetched:
        copy.wait()
    stored = []
    for step in range(RESULT_STEPS):

        def one(level, carry):
            ocean = jnp.concatenate([mask[level, pl.ds(*run), :] for run in runs], axis=0).astype(jnp.float32)
            for field in range(fields):
                at = pl.multiple_of((field * levels + level) * rows, rows)
                blocks = swap([held[slot, pl.ds(at, rows), :] for slot in range(groups)], group, cols // groups)
                gains = jnp.concatenate([gain[field, level, pl.ds(*run), :] for run in runs], axis=0)
                done[field, level] = ocean * gains * jnp.concatenate(blocks, axis=0)
            return carry

        lax.fori_loop(step * some, (step + 1) * some, one, 0, unroll=True)
        these = pl.ds(step * some, some)
        pairs, at = [], 0
        for first, number in runs:
            pairs.append((done.at[:, these, pl.ds(at, number)], out.at[:, these, pl.ds(first, number)]))
            at += number
        stored += copies(pairs, out_sems.at[step])
    for copy in stored:
        copy.wait()


def result(runs, gain, mask, parts, before):
    fields, levels, _, cols = gain.shape
    groups = len(parts)
    rows = sum(number for _, number in runs)
    anywhere = pl.BlockSpec(memory_space=pl.ANY)
    more = [] if before is None else [before]

    def kernel(gain, mask, *refs):
        result_kernel(runs, gain, mask, *refs[:groups], *refs[groups + len(more):])

    return pl.pallas_call(
        kernel,
        in_specs=[vmem()] * 2 + [anywhere] * (groups + len(more)),
        out_specs=anywhere,
        out_shape=jax.ShapeDtypeStruct(gain.shape, jnp.float32),
        scratch_shapes=[
            pltpu.VMEM((groups, *parts[0].shape), jnp.float32),
            pltpu.VMEM((fields, levels, rows, cols), jnp.float32),
            pltpu.SemaphoreType.DMA((groups,)),
            pltpu.SemaphoreType.DMA((RESULT_STEPS, len(runs))),
        ],
        input_output_aliases={2 + groups: 0} if more else {},
        compiler_params=params(),
        name="result",
    )(gain, mask, *parts, *more)


def shards(increment, norm_gain, diffusion_i, diffusion_j, sea_mask, coupling):
    devices = lax.axis_size("lev")
    gx_size = lax.axis_size("gx")
    gy_size = lax.axis_size("gy")
    _, levels, length, cols = increment.shape
    width = cols // devices
    rows = length // devices
    order = coupling.shape[0]
    to = [lax.rem(lax.axis_index("lev") + d, devices) for d in range(devices)]
    source = [lax.rem(lax.axis_index("lev") + devices - d, devices) for d in range(devices)]

    def shift(x, d):
        return lax.ppermute(x, "lev", [(k, (k + d) % devices) for k in range(devices)])

    def exchange(parts):
        return [parts[0]] + [shift(parts[d], d) for d in range(1, devices)]

    up = [((k + 1) % gx_size, k) for k in range(gx_size)]
    down = [(b, a) for a, b in up]
    ring = [(devices - 1 - slot if y % 2 else slot) * gy_size + y for y in range(gy_size) for slot in range(devices)]
    ahead = list(zip(ring, ring[1:] + ring[:1]))
    back = [(b, a) for a, b in ahead]

    def halo_i(first, last):
        if gx_size == 2:
            size = first.shape[0]
            both = lax.ppermute(jnp.concatenate([first, last], axis=0), "gx", up)
            return both[size:], both[:size]
        return lax.ppermute(last, "gx", down), lax.ppermute(first, "gx", up)

    def halo_j(first, last):
        return lax.ppermute(last, ("lev", "gy"), ahead), lax.ppermute(first, ("lev", "gy"), back)

    def flat(x):
        return x.reshape(-1, x.shape[-1])

    def cut(x, *sizes):
        return lax.split(x, sizes, 0)

    quarter = length // 4
    some = 2 * quarter // devices
    half = devices // 2
    inner = (quarter, 2 * quarter)
    outer = ((0, quarter), (3 * quarter, quarter))
    inner_rows = list(range(quarter - STEPS, 3 * quarter + STEPS))
    outer_rows = list(range(-STEPS, quarter - STEPS)) + list(range(3 * quarter + STEPS, length + STEPS))
    inner_starts = [quarter + a * len(inner_rows) // devices for a in range(devices)]
    outer_starts = [a * some for a in range(half)] + [3 * quarter + 2 * STEPS + a * some for a in range(half)]
    windows = [list(range(-STEPS, quarter + STEPS)), list(range(3 * quarter - STEPS, length + STEPS))]

    inner_size = len(inner_rows) // devices
    inner_messages = weight_messages(inner_starts, inner_size, diffusion_i, diffusion_j, [sea_mask])
    inner_parts = exchange(inner_messages)
    inner_messages, increment, norm_gain = lax.optimization_barrier((inner_messages, increment, norm_gain))
    scaled = exchange(scaled_messages(increment, norm_gain, sea_mask, devices))

    depth = sum(part[2 * levels * inner_size:] for part in inner_parts)
    right_depth = lax.ppermute(depth, ("lev", "gy"), back)
    depth, edge_i, edge_j = lax.optimization_barrier((depth, diffusion_i, diffusion_j))
    above, below = halo_i(
        *[
            jnp.concatenate([depth[at], flat(edge_i[:, at]), flat(edge_j[:, at])], axis=0)
            for at in (slice(0, STEPS), slice(-STEPS, None))
        ]
    )
    sizes = STEPS, 2 * levels * STEPS
    above_depth, above_weight = cut(above, *sizes)
    below_depth, below_weight = cut(below, *sizes)
    halo_depth = jnp.concatenate([below_depth, above_depth], axis=0)
    here = turn_weights(inner_starts, inner_size, [depth, right_depth], inner_parts, order)
    left, right = halo_j(
        jnp.concatenate([flat(here[:, :STEPS]), halo_depth], axis=0),
        flat(here[:, -STEPS:]),
    )
    right, right_halo_depth = cut(right, len(inner_rows) * STEPS, 2 * STEPS)
    outer_messages = weight_messages(
        outer_starts, some, diffusion_i, diffusion_j, halos=[above_weight, below_weight]
    )

    balance = jnp.eye(order, dtype=jnp.float32) + coupling
    by_device = balance.reshape(2, devices, levels, order)
    adjoint = jnp.concatenate([by_device[:, s].reshape(2 * levels, order) for s in source], axis=0).T
    forward = jnp.concatenate([by_device[:, t].reshape(2 * levels, order) for t in to], axis=0)

    scaled[1], left, right = lax.optimization_barrier((scaled[1], left, right))
    weights = [(inner_rows, here, left, right)]
    mixed = adjoint_mix(adjoint, depth, scaled, length, width)
    left, right = halo_j(flat(mixed[:, :STEPS]), flat(mixed[:, -STEPS:]))
    scaled[1], outer_messages[1] = lax.optimization_barrier((scaled[1], outer_messages[1]))
    early = shift(outer_messages[1], 1)
    left, right, outer_messages, early = lax.optimization_barrier((left, right, outer_messages, early))
    outer_parts = [outer_messages[0], early] + [shift(outer_messages[d], d) for d in range(2, devices)]
    field = [(list(range(length)), mixed, left, right)]
    inner_mixed = spread_mix([inner_rows], forward, field, weights, devices)
    _, outer_parts = lax.optimization_barrier((inner_mixed[0], outer_parts))
    inner_mixed = exchange(inner_mixed)
    out = result((inner,), norm_gain, sea_mask, inner_mixed, None)

    above, below = halo_i(flat(mixed[:STEPS]), flat(mixed[-STEPS:]))
    halo = jnp.concatenate([above, below], axis=0).reshape(2 * STEPS, width, order)
    here = turn_weights(outer_starts, some, [depth, right_depth, halo_depth, right_halo_depth], outer_parts, order)
    left, right = halo_j(
        jnp.concatenate([flat(here[:, :STEPS]), flat(halo[:, :STEPS])], axis=0),
        jnp.concatenate([flat(here[:, -STEPS:]), flat(halo[:, -STEPS:])], axis=0),
    )
    sizes = len(outer_rows) * STEPS, 2 * STEPS * STEPS
    left, halo_left = cut(left, *sizes)
    right, halo_right = cut(right, *sizes)
    weights.append((outer_rows, here, left, right))
    field.append((list(range(-STEPS, 0)) + list(range(length, length + STEPS)), halo, halo_left, halo_right))
    outer_mixed = exchange(spread_mix(windows, forward, field, weights, devices))
    return result(outer, norm_gain, sea_mask, outer_mixed, out)


def solution(mesh):
    return jax.shard_map(
        shards,
        mesh=mesh,
        in_specs=(
            P(None, "lev", "gx", "gy"),
            P(None, "lev", "gx", "gy"),
            P("lev", "gx", "gy"),
            P("lev", "gx", "gy"),
            P("lev", "gx", "gy"),
            P(),
        ),
        out_specs=P(None, "lev", "gx", "gy"),
        check_vma=False,
    )
```

time: 99.3 us -> 98.3 us (0.990)
  starting transfers between devices: 53.5 us -> 41.3 us
  waiting for transfers between devices: 23.2 us -> 32.6 us
  Pallas kernels: 21.6 us -> 22.9 us
    ppermute x17 -> x18, waiting for transfers between devices: 13.9 us -> 29.4 us  [the longest x15 23.7 us: shift(): lax.ppermute(x, 'lev', [(k, (k + d) % devices) for k in range(devices)])]
    ppermute x17 -> x18, starting transfers between devices: 37.1 us -> 27.2 us  [the longest x15 24.2 us: shift(): lax.ppermute(x, 'lev', [(k, (k + d) % devices) for k in range(devices)])]
    ppermute x3, waiting for transfers between devices: 6.39 us -> 3.22 us  [halo_j(): lax.ppermute(first, ('lev', 'gy'), back)]
    ppermute x3, waiting for transfers between devices: 2.93 us -> 0.01 us  [halo_j(): lax.ppermute(last, ('lev', 'gy'), ahead)]
    ppermute x3, starting transfers between devices: 13.9 us -> 12.3 us  [halo_j(): lax.ppermute(last, ('lev', 'gy'), ahead)]
    pallas_call x9, Pallas kernels: 18.2 us -> 19.5 us  [the longest x2 6.69 us: spread_mix(): pl.pallas_call(functools.partial(spread_kernel, windows, [piece[0] for pi...]
  transfers between devices with their start and end apart: 23 -> 24, of which waited for: 8 -> 8; matrix products, arithmetic and copies ran while one was open for 0% -> 1% of each run, Pallas kernels for 16% -> 15%
where the time goes in v4:
time: 98.3 us; the launch traced here: 97.9 us
  starting transfers between devices  41.3 us (42%)
  waiting for transfers between devices  32.6 us (33%)
  Pallas kernels  22.9 us (23%)
    ppermute x15, starting transfers between devices, shift(): lax.ppermute(x, 'lev', [(k, (k + d) % devices) for k in range(devices)])  24.2 us
    ppermute x15, waiting for transfers between devices, shift(): lax.ppermute(x, 'lev', [(k, (k + d) % devices) for k in range(devices)])  23.7 us
    ppermute x3, starting transfers between devices, halo_j(): lax.ppermute(last, ('lev', 'gy'), ahead)  12.3 us
    pallas_call x2, Pallas kernels, spread_mix(): pl.pallas_call(functools.partial(spread_kernel, windows, [piece[0] for pi...  6.69 us
    pallas_call x2, Pallas kernels, weight_messages(): pl.pallas_call(functools.partial(pack_kernel, starts, rows, len(mask)), i...  5.8 us
    ppermute x1, waiting for transfers between devices, shards(): right_depth = lax.ppermute(depth, ('lev', 'gy'), back)  5.68 us
    pallas_call x2, Pallas kernels, result(): pl.pallas_call(kernel, in_specs=[vmem()] * 2 + [anywhere] * (groups + len...  4.23 us
    pallas_call x1, Pallas kernels, scaled_messages(): pl.pallas_call(scaled_kernel, in_specs=[pl.BlockSpec(memory_space=pl.ANY)...  3.33 us
  transfers between devices with their start and end apart: 24, of which 8 were waited for; matrix products, arithmetic and copies ran while one was open for 1% of the time, Pallas kernels for 15%

profile of v4, /device:TPU:0, one launch (start us, length us, event | category | flops | bytes accessed | tf_op | source)
XLA Modules:
  0.0 97.9 jit_solution(41277456407822402)
XLA Ops:
  0.0 3.7 %weight_messages.2 = (f32[336,128]{1,0:T(8,128)}, f32[336,128]{1,0:T(8,128)}, f32[336,128]{1,0:T(8,128)}, f32[336,128]{1,0:T(8,128)}) custom-call(f32[16,64,128]{2,1,0:T(8,128)} %along_i.3, f32[16,64,128]{2,1,0:T(8,128)} %along_j.3, s32[16,64,128]{2,1,0:T(8,128)} %mask.5), custom_call_target="tpu_custom_call" | custom-call | tf_op jit(solution)/shard_map/weight_messages/pallas_call | solution.py:191
  3.7 3.1 %collective-permute-start = (f32[336,128]{1,0:T(8,128)}, f32[336,128]{1,0:T(8,128)S(1)}, u32[]{:S(2)}, u32[]{:S(2)}) collective-permute-start(f32[336,128]{1,0:T(8,128)} %get-tuple-element.45), channel_id=1, source_target_pairs={{0,8},{8,16},{16,24},{24,0},{1,9},{9,17},{17,25},{25,1},{2,10},{10... | collective-permute-start | bytes 516104 | tf_op jit(solution)/shard_map/ppermute | solution.py:465
  6.8 2.6 %collective-permute-start.1 = (f32[336,128]{1,0:T(8,128)}, f32[336,128]{1,0:T(8,128)S(1)}, u32[]{:S(2)}, u32[]{:S(2)}) collective-permute-start(f32[336,128]{1,0:T(8,128)} %get-tuple-element.46), channel_id=1, source_target_pairs={{0,16},{8,24},{16,0},{24,8},{1,17},{9,25},{17,1},{25,9},{2,18},{10... | collective-permute-start | bytes 516104 | tf_op jit(solution)/shard_map/ppermute | solution.py:465
  9.4 1.3 %collective-permute-start.2 = (f32[336,128]{1,0:T(8,128)}, f32[336,128]{1,0:T(8,128)S(1)}, u32[]{:S(2)}, u32[]{:S(2)}) collective-permute-start(f32[336,128]{1,0:T(8,128)} %get-tuple-element.47), channel_id=1, source_target_pairs={{0,24},{8,0},{16,8},{24,16},{1,25},{9,1},{17,9},{25,17},{2,26},{10... | collective-permute-start | bytes 516104 | tf_op jit(solution)/shard_map/ppermute | solution.py:465
  10.8 3.3 %scaled_messages.1 = (f32[512,128]{1,0:T(8,128)}, f32[512,128]{1,0:T(8,128)}, f32[512,128]{1,0:T(8,128)}, f32[512,128]{1,0:T(8,128)}) custom-call(f32[2,16,64,128]{3,2,1,0:T(8,128)} %increment, f32[2,16,64,128]{3,2,1,0:T(8,128)} %gain.2, s32[16,64,128]{2,1,0:T(8,128)} %mask.5), custom_call_target="tpu_custom_call" | custom-call | tf_op jit(solution)/shard_map/scaled_messages/pallas_call | solution.py:117
  14.1 0.0 copy-start.2
  14.1 0.7 collective-permute-start.3
  14.8 0.3 collective-permute-start.8
  15.3 0.1 copy.13.matrix
  15.4 0.0 collective-permute-done.refs_3_
  15.4 2.9 %collective-permute-start.9 = (f32[512,128]{1,0:T(8,128)}, f32[512,128]{1,0:T(8,128)S(1)}, u32[]{:S(2)}, u32[]{:S(2)}) collective-permute-start(f32[512,128]{1,0:T(8,128)} %get-tuple-element.57), channel_id=1, source_target_pairs={{0,24},{8,0},{16,8},{24,16},{1,25},{9,1},{17,9},{25,17},{2,26},{10... | collective-permute-start | bytes 786440 | tf_op jit(solution)/shard_map/ppermute | solution.py:465
  18.3 13.2 %collective-permute-done.1.refs_4_ = f32[336,128]{1,0:T(8,128)S(1)} collective-permute-done((f32[336,128]{1,0:T(8,128)}, f32[336,128]{1,0:T(8,128)S(1)}, u32[]{:S(2)}, u32[]{:S(2)}) %collective-permute-start.1) | collective-permute-done | bytes 172064 | tf_op jit(solution)/shard_map/ppermute | solution.py:465
  31.4 0.0 collective-permute-done.2.refs_5_
  31.5 0.1 collective-permute-start.4
  31.6 0.3 concatenate.30
  31.9 1.3 %collective-permute-start.6 = (f32[264,128]{1,0:T(8,128)S(1)}, f32[264,128]{1,0:T(8,128)S(1)}, u32[]{:S(2)}, u32[]{:S(2)}) collective-permute-start(f32[264,128]{1,0:T(8,128)S(1)} %concatenate.30), channel_id=1, source_target_pairs={{4,0},{0,4},{5,1},{1,5},{6,2},{2,6},{7,3},{3,7},{12,8},{8,12},{13,... | collective-permute-start | bytes 405512 | tf_op jit(solution)/shard_map/ppermute | solution.py:479
  33.2 5.7 %collective-permute-done.4.refs_1_ = f32[16,128]{1,0:T(8,128)S(1)} collective-permute-done((f32[16,128]{1,0:T(8,128)S(1)}, f32[16,128]{1,0:T(8,128)S(1)}, u32[]{:S(2)}, u32[]{:S(2)}) %collective-permute-start.4) | collective-permute-done | bytes 8224 | tf_op jit(solution)/shard_map/ppermute | solution.py:510
  38.9 0.4 turn_weights.2.refs_3_.refs_6_
  39.4 8.8 %collective-permute-start.5 = (f32[160,128]{1,0:T(8,128)S(1)}, f32[160,128]{1,0:T(8,128)S(1)}, u32[]{:S(2)}, u32[]{:S(2)}) collective-permute-start(f32[160,128]{1,0:T(8,128)S(1)} %bitcast.47), channel_id=1, source_target_pairs={{0,8},{8,16},{16,24},{24,25},{25,17},{17,9},{9,1},{1,2},{2,10},{10... | collective-permute-start | bytes 245768 | tf_op jit(solution)/shard_map/ppermute | solution.py:484
  48.2 0.0 collective-permute-done.6
  48.3 0.1 collective-permute-start.7
  48.3 0.0 copy-start.4
  48.4 2.1 %weight_messages.3 = (f32[256,128]{1,0:T(8,128)S(1)}, f32[256,128]{1,0:T(8,128)S(1)}, f32[256,128]{1,0:T(8,128)S(1)}, f32[256,128]{1,0:T(8,128)S(1)}) custom-call(f32[16,64,128]{2,1,0:T(8,128)S(1)} %copy-done.2, f32[16,64,128]{2,1,0:T(8,128)S(1)} %copy-done.3, f32[128,128]{1,0:T(8,128)S(1)} %get-tuple-element.96.refs_0_, ...), custom_call_target="tpu_custom_call" | custom-call | tf_op jit(solution)/shard_map/weight_messages/pallas_call | solution.py:191
  50.4 2.4 %collective-permute-done.7 = f32[168,128]{1,0:T(8,128)S(1)} collective-permute-done((f32[168,128]{1,0:T(8,128)S(1)}, f32[168,128]{1,0:T(8,128)S(1)}, u32[]{:S(2)}, u32[]{:S(2)}) %collective-permute-start.7) | collective-permute-done | bytes 86048 | tf_op jit(solution)/shard_map/ppermute | solution.py:484
  52.8 0.0 collective-permute-done.3.refs_1_
  52.8 0.0 collective-permute-done.5.refs_4_.refs_7_
  52.8 0.0 collective-permute-done.8.refs_2_
  52.8 0.0 collective-permute-done.9.refs_3_
  52.9 2.0 %adjoint_mix.1.refs_0_ = f32[64,32,128]{2,1,0:T(8,128)S(1)} custom-call(f32[128,128]{1,0:T(8,128)S(1)} %copy.13.matrix, f32[16,128]{1,0:T(8,128)S(1)} %slice_add_fusion.refs_0_.depths, f32[512,128]{1,0:T(8,128)S(1)} %copy-done.4, f32[512,128]{1,0:T(8,128)S(1)} %collective-permute-done.3.refs_1_, f32[512,128]{1,0:T(8,128)S(1)} %collective-permute-done.8.refs_2_, ...), custom_call_target="tpu_custom_call" | custom-call | tf_op jit(solution)/shard_map/adjoint_mix/pallas_call | solution.py:231
  54.9 0.1 collective-permute-start.12
  55.0 0.1 collective-permute-start.10
  55.1 1.7 %collective-permute-start.11 = (f32[256,128]{1,0:T(8,128)S(1)}, f32[256,128]{1,0:T(8,128)S(1)}, u32[]{:S(2)}, u32[]{:S(2)}) collective-permute-start(f32[256,128]{1,0:T(8,128)S(1)} %bitcast.41), channel_id=1, source_target_pairs={{8,0},{16,8},{24,16},{25,24},{17,25},{9,17},{1,9},{2,1},{10,2},{18... | collective-permute-start | bytes 393224 | tf_op jit(solution)/shard_map/ppermute | solution.py:484
  56.8 1.6 %collective-permute-start.13 = (f32[256,128]{1,0:T(8,128)S(1)}, f32[256,128]{1,0:T(8,128)S(1)}, u32[]{:S(2)}, u32[]{:S(2)}) collective-permute-start(f32[256,128]{1,0:T(8,128)S(1)} %pad_maximum_fusion), channel_id=1, source_target_pairs={{4,0},{0,4},{5,1},{1,5},{6,2},{2,6},{7,3},{3,7},{12,8},{8,12},{13,... | collective-permute-start | bytes 393224 | tf_op jit(solution)/shard_map/ppermute | solution.py:479
  58.4 4.8 %collective-permute-done.12.refs_5_ = f32[256,128]{1,0:T(8,128)S(1)} collective-permute-done((f32[256,128]{1,0:T(8,128)S(1)}, f32[256,128]{1,0:T(8,128)S(1)}, u32[]{:S(2)}, u32[]{:S(2)}) %collective-permute-start.12) | collective-permute-done | bytes 131104 | tf_op jit(solution)/shard_map/ppermute | solution.py:465
  63.2 0.0 collective-permute-done.10.refs_1_
  63.2 0.0 collective-permute-done.11.refs_2_
  63.2 2.0 %collective-permute-start.14 = (f32[256,128]{1,0:T(8,128)S(1)}, f32[256,128]{1,0:T(8,128)S(1)}, u32[]{:S(2)}, u32[]{:S(2)}) collective-permute-start(f32[256,128]{1,0:T(8,128)S(1)} %get-tuple-element.70), channel_id=1, source_target_pairs={{0,16},{8,24},{16,0},{24,8},{1,17},{9,25},{17,1},{25,9},{2,18},{10... | collective-permute-start | bytes 393224 | tf_op jit(solution)/shard_map/ppermute | solution.py:465
  65.2 1.2 %collective-permute-start.15 = (f32[256,128]{1,0:T(8,128)S(1)}, f32[256,128]{1,0:T(8,128)S(1)}, u32[]{:S(2)}, u32[]{:S(2)}) collective-permute-start(f32[256,128]{1,0:T(8,128)S(1)} %get-tuple-element.71), channel_id=1, source_target_pairs={{0,24},{8,0},{16,8},{24,16},{1,25},{9,1},{17,9},{25,17},{2,26},{10... | collective-permute-start | bytes 393224 | tf_op jit(solution)/shard_map/ppermute | solution.py:465
  66.4 3.2 %spread_mix.2 = (f32[256,128]{1,0:T(8,128)S(1)}, f32[256,128]{1,0:T(8,128)S(1)}, f32[256,128]{1,0:T(8,128)S(1)}, f32[256,128]{1,0:T(8,128)S(1)}) custom-call(f32[128,128]{1,0:T(8,128)S(1)} %get-tuple-element.109.matrix, f32[64,32,128]{2,1,0:T(8,128)S(1)} %adjoint_mix.1.refs_0_, f32[256,128]{1,0:T(8,128)S(1)} %collective-permute-done.10.refs_1_, ...), custom_call_target="tpu_custom_call" | custom-call | tf_op jit(solution)/shard_map/spread_mix/pallas_call | solution.py:378
  69.6 0.9 collective-permute-start.21
  70.5 0.0 collective-permute-done.13
  70.6 1.3 %collective-permute-done.14.refs_6_ = f32[256,128]{1,0:T(8,128)S(1)} collective-permute-done((f32[256,128]{1,0:T(8,128)S(1)}, f32[256,128]{1,0:T(8,128)S(1)}, u32[]{:S(2)}, u32[]{:S(2)}) %collective-permute-start.14) | collective-permute-done | bytes 131104 | tf_op jit(solution)/shard_map/ppermute | solution.py:465
  71.9 0.0 collective-permute-done.15.refs_7_
  71.9 0.4 turn_weights.3.refs_9_
  72.3 3.4 %collective-permute-start.16 = (f32[160,128]{1,0:T(8,128)S(1)}, f32[160,128]{1,0:T(8,128)S(1)}, u32[]{:S(2)}, u32[]{:S(2)}) collective-permute-start(f32[160,128]{1,0:T(8,128)S(1)} %pad_maximum_fusion.5), channel_id=1, source_target_pairs={{0,8},{8,16},{16,24},{24,25},{25,17},{17,9},{9,1},{1,2},{2,10},{10... | collective-permute-start | bytes 245768 | tf_op jit(solution)/shard_map/ppermute | solution.py:484
  75.8 0.0 collective-permute-start.17
  75.8 2.0 %collective-permute-start.22 = (f32[256,128]{1,0:T(8,128)S(1)}, f32[256,128]{1,0:T(8,128)S(1)}, u32[]{:S(2)}, u32[]{:S(2)}) collective-permute-start(f32[256,128]{1,0:T(8,128)S(1)} %get-tuple-element.81), channel_id=1, source_target_pairs={{0,16},{8,24},{16,0},{24,8},{1,17},{9,25},{17,1},{25,9},{2,18},{10... | collective-permute-start | bytes 393224 | tf_op jit(solution)/shard_map/ppermute | solution.py:465
  77.8 2.4 %collective-permute-start.23 = (f32[256,128]{1,0:T(8,128)S(1)}, f32[256,128]{1,0:T(8,128)S(1)}, u32[]{:S(2)}, u32[]{:S(2)}) collective-permute-start(f32[256,128]{1,0:T(8,128)S(1)} %get-tuple-element.82), channel_id=1, source_target_pairs={{0,24},{8,0},{16,8},{24,16},{1,25},{9,1},{17,9},{25,17},{2,26},{10... | collective-permute-start | bytes 393224 | tf_op jit(solution)/shard_map/ppermute | solution.py:465
  80.2 0.0 collective-permute-done.16
  80.2 0.8 collective-permute-done.17
  81.0 0.0 copy-start
  81.0 0.0 copy-start.1
  81.1 3.5 %spread_mix.3 = (f32[256,128]{1,0:T(8,128)S(1)}, f32[256,128]{1,0:T(8,128)S(1)}, f32[256,128]{1,0:T(8,128)S(1)}, f32[256,128]{1,0:T(8,128)S(1)}) custom-call(f32[128,128]{1,0:T(8,128)S(1)} %get-tuple-element.109.matrix, f32[64,32,128]{2,1,0:T(8,128)S(1)} %adjoint_mix.1.refs_0_, f32[256,128]{1,0:T(8,128)S(1)} %collective-permute-done.10.refs_1_, ...), custom_call_target="tpu_custom_call" | custom-call | tf_op jit(solution)/shard_map/spread_mix/pallas_call | solution.py:378
  84.5 1.2 %collective-permute-start.18 = (f32[256,128]{1,0:T(8,128)S(1)}, f32[256,128]{1,0:T(8,128)S(1)}, u32[]{:S(2)}, u32[]{:S(2)}) collective-permute-start(f32[256,128]{1,0:T(8,128)S(1)} %get-tuple-element.77), channel_id=1, source_target_pairs={{0,8},{8,16},{16,24},{24,0},{1,9},{9,17},{17,25},{25,1},{2,10},{10... | collective-permute-start | bytes 393224 | tf_op jit(solution)/shard_map/ppermute | solution.py:465
  85.8 2.1 %collective-permute-start.19 = (f32[256,128]{1,0:T(8,128)S(1)}, f32[256,128]{1,0:T(8,128)S(1)}, u32[]{:S(2)}, u32[]{:S(2)}) collective-permute-start(f32[256,128]{1,0:T(8,128)S(1)} %get-tuple-element.78), channel_id=1, source_target_pairs={{0,16},{8,24},{16,0},{24,8},{1,17},{9,25},{17,1},{25,9},{2,18},{10... | collective-permute-start | bytes 393224 | tf_op jit(solution)/shard_map/ppermute | solution.py:465
  87.9 0.0 collective-permute-done.21.refs_1_
  87.9 1.4 %collective-permute-start.20 = (f32[256,128]{1,0:T(8,128)S(1)}, f32[256,128]{1,0:T(8,128)S(1)}, u32[]{:S(2)}, u32[]{:S(2)}) collective-permute-start(f32[256,128]{1,0:T(8,128)S(1)} %get-tuple-element.79), channel_id=1, source_target_pairs={{0,24},{8,0},{16,8},{24,16},{1,25},{9,1},{17,9},{25,17},{2,26},{10... | collective-permute-start | bytes 393224 | tf_op jit(solution)/shard_map/ppermute | solution.py:465
  89.3 0.0 collective-permute-done.22.refs_2_
  89.3 0.0 collective-permute-done.23.refs_3_
  89.3 2.1 %result.2.refs_4_ = f32[2,16,64,128]{3,2,1,0:T(8,128)} custom-call(f32[2,16,64,128]{3,2,1,0:T(8,128)S(1)} %copy-done, s32[16,64,128]{2,1,0:T(8,128)S(1)} %copy-done.1, f32[256,128]{1,0:T(8,128)S(1)} %get-tuple-element.67.refs_0_, f32[256,128]{1,0:T(8,128)S(1)} %collective-permute-done.21.refs_1_, f32[256,128]{1,0:T(8,128)S(1)} %collective-permute-done.22.refs_2_, ...), custom_call_target="tpu_custom_call" | custom-call | tf_op jit(solution)/shard_map/result/pallas_call | solution.py:436
  91.4 1.3 %collective-permute-done.18.refs_1_ = f32[256,128]{1,0:T(8,128)S(1)} collective-permute-done((f32[256,128]{1,0:T(8,128)S(1)}, f32[256,128]{1,0:T(8,128)S(1)}, u32[]{:S(2)}, u32[]{:S(2)}) %collective-permute-start.18) | collective-permute-done | bytes 131104 | tf_op jit(solution)/shard_map/ppermute | solution.py:465
  92.7 3.1 %collective-permute-done.19.refs_2_ = f32[256,128]{1,0:T(8,128)S(1)} collective-permute-done((f32[256,128]{1,0:T(8,128)S(1)}, f32[256,128]{1,0:T(8,128)S(1)}, u32[]{:S(2)}, u32[]{:S(2)}) %collective-permute-start.19) | collective-permute-done | bytes 131104 | tf_op jit(solution)/shard_map/ppermute | solution.py:465
  95.8 0.0 collective-permute-done.20.refs_3_
  95.8 2.1 %result.3 = f32[2,16,64,128]{3,2,1,0:T(8,128)} custom-call(f32[2,16,64,128]{3,2,1,0:T(8,128)S(1)} %copy-done, s32[16,64,128]{2,1,0:T(8,128)S(1)} %copy-done.1, f32[256,128]{1,0:T(8,128)S(1)} %get-tuple-element.76.refs_0_, f32[256,128]{1,0:T(8,128)S(1)} %collective-permute-done.18.refs_1_, ...), custom_call_target="tpu_custom_call", output_to_operand_aliasing={{}: (6, {})} | custom-call | tf_op jit(solution)/shard_map/result/pallas_call | solution.py:436
  (36 shorter events, 0.3 us)
Async XLA Ops:
  3.7 11.6 %collective-permute-start = (f32[336,128]{1,0:T(8,128)}, f32[336,128]{1,0:T(8,128)S(1)}, u32[]{:S(2)}, u32[]{:S(2)}) collective-permute-start(f32[336,128]{1,0:T(8,128)} %get-tuple-element.45), channel_id=1, source_target_pairs={{0,8},{8,16},{16,24},{24,0},{1,9},{9,17},{17,25},{25,1},{2,10},{10... | collective-permute-start | bytes 516104 | tf_op jit(solution)/shard_map/ppermute | solution.py:465
  6.8 24.6 %collective-permute-start.1 = (f32[336,128]{1,0:T(8,128)}, f32[336,128]{1,0:T(8,128)S(1)}, u32[]{:S(2)}, u32[]{:S(2)}) collective-permute-start(f32[336,128]{1,0:T(8,128)} %get-tuple-element.46), channel_id=1, source_target_pairs={{0,16},{8,24},{16,0},{24,8},{1,17},{9,25},{17,1},{25,9},{2,18},{10... | collective-permute-start | bytes 516104 | tf_op jit(solution)/shard_map/ppermute | solution.py:465
  9.4 22.0 %collective-permute-start.2 = (f32[336,128]{1,0:T(8,128)}, f32[336,128]{1,0:T(8,128)S(1)}, u32[]{:S(2)}, u32[]{:S(2)}) collective-permute-start(f32[336,128]{1,0:T(8,128)} %get-tuple-element.47), channel_id=1, source_target_pairs={{0,24},{8,0},{16,8},{24,16},{1,25},{9,1},{17,9},{25,17},{2,26},{10... | collective-permute-start | bytes 516104 | tf_op jit(solution)/shard_map/ppermute | solution.py:465
  10.8 4.4 %copy-start.6 = (f32[128,128]{1,0:T(8,128)S(1)}, f32[128,128]{1,0:T(8,128)}, u32[]{:S(2)}) copy-start(f32[128,128]{1,0:T(8,128)} %param.11) | copy-start | bytes 196612
  10.8 20.8 %copy-start.3 = (f32[16,64,128]{2,1,0:T(8,128)S(1)}, f32[16,64,128]{2,1,0:T(8,128)}, u32[]{:S(2)}) copy-start(f32[16,64,128]{2,1,0:T(8,128)} %along_j.3) | copy-start | bytes 1572868
  14.1 17.4 %copy-start.2 = (f32[16,64,128]{2,1,0:T(8,128)S(1)}, f32[16,64,128]{2,1,0:T(8,128)}, u32[]{:S(2)}) copy-start(f32[16,64,128]{2,1,0:T(8,128)} %along_i.3) | copy-start | bytes 1572868
  14.1 38.7 %collective-permute-start.3 = (f32[512,128]{1,0:T(8,128)}, f32[512,128]{1,0:T(8,128)S(1)}, u32[]{:S(2)}, u32[]{:S(2)}) collective-permute-start(f32[512,128]{1,0:T(8,128)} %get-tuple-element.52), channel_id=1, source_target_pairs={{0,8},{8,16},{16,24},{24,0},{1,9},{9,17},{17,25},{25,1},{2,10},{10... | collective-permute-start | bytes 786440 | tf_op jit(solution)/shard_map/ppermute | solution.py:465
  14.8 38.0 %collective-permute-start.8 = (f32[512,128]{1,0:T(8,128)}, f32[512,128]{1,0:T(8,128)S(1)}, u32[]{:S(2)}, u32[]{:S(2)}) collective-permute-start(f32[512,128]{1,0:T(8,128)} %get-tuple-element.56), channel_id=1, source_target_pairs={{0,16},{8,24},{16,0},{24,8},{1,17},{9,25},{17,1},{25,9},{2,18},{10... | collective-permute-start | bytes 786440 | tf_op jit(solution)/shard_map/ppermute | solution.py:465
  15.3 16.2 %copy-start.5 = (f32[336,128]{1,0:T(8,128)S(1)}, f32[336,128]{1,0:T(8,128)}, u32[]{:S(2)}) copy-start(f32[336,128]{1,0:T(8,128)} %get-tuple-element.44.refs_2_) | copy-start | bytes 516100
  15.4 37.4 %collective-permute-start.9 = (f32[512,128]{1,0:T(8,128)}, f32[512,128]{1,0:T(8,128)S(1)}, u32[]{:S(2)}, u32[]{:S(2)}) collective-permute-start(f32[512,128]{1,0:T(8,128)} %get-tuple-element.57), channel_id=1, source_target_pairs={{0,24},{8,0},{16,8},{24,16},{1,25},{9,1},{17,9},{25,17},{2,26},{10... | collective-permute-start | bytes 786440 | tf_op jit(solution)/shard_map/ppermute | solution.py:465
  31.5 7.5 %collective-permute-start.4 = (f32[16,128]{1,0:T(8,128)S(1)}, f32[16,128]{1,0:T(8,128)S(1)}, u32[]{:S(2)}, u32[]{:S(2)}) collective-permute-start(f32[16,128]{1,0:T(8,128)S(1)} %slice_add_fusion.refs_0_.depths), channel_id=1, source_target_pairs={{8,0},{16,8},{24,16},{25,24},{17,25},{9,17},{1,9},{2,1},{10,2},{18... | collective-permute-start | bytes 24584 | tf_op jit(solution)/shard_map/ppermute | solution.py:510
  31.9 16.3 %collective-permute-start.6 = (f32[264,128]{1,0:T(8,128)S(1)}, f32[264,128]{1,0:T(8,128)S(1)}, u32[]{:S(2)}, u32[]{:S(2)}) collective-permute-start(f32[264,128]{1,0:T(8,128)S(1)} %concatenate.30), channel_id=1, source_target_pairs={{4,0},{0,4},{5,1},{1,5},{6,2},{2,6},{7,3},{3,7},{12,8},{8,12},{13,... | collective-permute-start | bytes 405512 | tf_op jit(solution)/shard_map/ppermute | solution.py:479
  39.4 13.4 %collective-permute-start.5 = (f32[160,128]{1,0:T(8,128)S(1)}, f32[160,128]{1,0:T(8,128)S(1)}, u32[]{:S(2)}, u32[]{:S(2)}) collective-permute-start(f32[160,128]{1,0:T(8,128)S(1)} %bitcast.47), channel_id=1, source_target_pairs={{0,8},{8,16},{16,24},{24,25},{25,17},{17,9},{9,1},{1,2},{2,10},{10... | collective-permute-start | bytes 245768 | tf_op jit(solution)/shard_map/ppermute | solution.py:484
  48.3 4.5 %collective-permute-start.7 = (f32[168,128]{1,0:T(8,128)S(1)}, f32[168,128]{1,0:T(8,128)S(1)}, u32[]{:S(2)}, u32[]{:S(2)}) collective-permute-start(f32[168,128]{1,0:T(8,128)S(1)} %pad_maximum_fusion.4), channel_id=1, source_target_pairs={{8,0},{16,8},{24,16},{25,24},{17,25},{9,17},{1,9},{2,1},{10,2},{18... | collective-permute-start | bytes 258056 | tf_op jit(solution)/shard_map/ppermute | solution.py:484
  48.3 4.5 %copy-start.4 = (f32[512,128]{1,0:T(8,128)S(1)}, f32[512,128]{1,0:T(8,128)}, u32[]{:S(2)}) copy-start(f32[512,128]{1,0:T(8,128)} %get-tuple-element.51.refs_0_) | copy-start | bytes 786436
  54.9 8.3 %collective-permute-start.12 = (f32[256,128]{1,0:T(8,128)S(1)}, f32[256,128]{1,0:T(8,128)S(1)}, u32[]{:S(2)}, u32[]{:S(2)}) collective-permute-start(f32[256,128]{1,0:T(8,128)S(1)} %get-tuple-element.60), channel_id=1, source_target_pairs={{0,8},{8,16},{16,24},{24,0},{1,9},{9,17},{17,25},{25,1},{2,10},{10... | collective-permute-start | bytes 393224 | tf_op jit(solution)/shard_map/ppermute | solution.py:465
  55.0 8.2 %collective-permute-start.10 = (f32[256,128]{1,0:T(8,128)S(1)}, f32[256,128]{1,0:T(8,128)S(1)}, u32[]{:S(2)}, u32[]{:S(2)}) collective-permute-start(f32[256,128]{1,0:T(8,128)S(1)} %bitcast.42), channel_id=1, source_target_pairs={{0,8},{8,16},{16,24},{24,25},{25,17},{17,9},{9,1},{1,2},{2,10},{10... | collective-permute-start | bytes 393224 | tf_op jit(solution)/shard_map/ppermute | solution.py:484
  55.1 8.1 %collective-permute-start.11 = (f32[256,128]{1,0:T(8,128)S(1)}, f32[256,128]{1,0:T(8,128)S(1)}, u32[]{:S(2)}, u32[]{:S(2)}) collective-permute-start(f32[256,128]{1,0:T(8,128)S(1)} %bitcast.41), channel_id=1, source_target_pairs={{8,0},{16,8},{24,16},{25,24},{17,25},{9,17},{1,9},{2,1},{10,2},{18... | collective-permute-start | bytes 393224 | tf_op jit(solution)/shard_map/ppermute | solution.py:484
  56.8 13.7 %collective-permute-start.13 = (f32[256,128]{1,0:T(8,128)S(1)}, f32[256,128]{1,0:T(8,128)S(1)}, u32[]{:S(2)}, u32[]{:S(2)}) collective-permute-start(f32[256,128]{1,0:T(8,128)S(1)} %pad_maximum_fusion), channel_id=1, source_target_pairs={{4,0},{0,4},{5,1},{1,5},{6,2},{2,6},{7,3},{3,7},{12,8},{8,12},{13,... | collective-permute-start | bytes 393224 | tf_op jit(solution)/shard_map/ppermute | solution.py:479
  63.2 8.7 %collective-permute-start.14 = (f32[256,128]{1,0:T(8,128)S(1)}, f32[256,128]{1,0:T(8,128)S(1)}, u32[]{:S(2)}, u32[]{:S(2)}) collective-permute-start(f32[256,128]{1,0:T(8,128)S(1)} %get-tuple-element.70), channel_id=1, source_target_pairs={{0,16},{8,24},{16,0},{24,8},{1,17},{9,25},{17,1},{25,9},{2,18},{10... | collective-permute-start | bytes 393224 | tf_op jit(solution)/shard_map/ppermute | solution.py:465
  65.2 6.7 %collective-permute-start.15 = (f32[256,128]{1,0:T(8,128)S(1)}, f32[256,128]{1,0:T(8,128)S(1)}, u32[]{:S(2)}, u32[]{:S(2)}) collective-permute-start(f32[256,128]{1,0:T(8,128)S(1)} %get-tuple-element.71), channel_id=1, source_target_pairs={{0,24},{8,0},{16,8},{24,16},{1,25},{9,1},{17,9},{25,17},{2,26},{10... | collective-permute-start | bytes 393224 | tf_op jit(solution)/shard_map/ppermute | solution.py:465
  69.6 18.2 %collective-permute-start.21 = (f32[256,128]{1,0:T(8,128)S(1)}, f32[256,128]{1,0:T(8,128)S(1)}, u32[]{:S(2)}, u32[]{:S(2)}) collective-permute-start(f32[256,128]{1,0:T(8,128)S(1)} %get-tuple-element.80), channel_id=1, source_target_pairs={{0,8},{8,16},{16,24},{24,0},{1,9},{9,17},{17,25},{25,1},{2,10},{10... | collective-permute-start | bytes 393224 | tf_op jit(solution)/shard_map/ppermute | solution.py:465
  72.3 7.8 %collective-permute-start.16 = (f32[160,128]{1,0:T(8,128)S(1)}, f32[160,128]{1,0:T(8,128)S(1)}, u32[]{:S(2)}, u32[]{:S(2)}) collective-permute-start(f32[160,128]{1,0:T(8,128)S(1)} %pad_maximum_fusion.5), channel_id=1, source_target_pairs={{0,8},{8,16},{16,24},{24,25},{25,17},{17,9},{9,1},{1,2},{2,10},{10... | collective-permute-start | bytes 245768 | tf_op jit(solution)/shard_map/ppermute | solution.py:484
  75.8 5.2 %collective-permute-start.17 = (f32[160,128]{1,0:T(8,128)S(1)}, f32[160,128]{1,0:T(8,128)S(1)}, u32[]{:S(2)}, u32[]{:S(2)}) collective-permute-start(f32[160,128]{1,0:T(8,128)S(1)} %pad_maximum_fusion.6), channel_id=1, source_target_pairs={{8,0},{16,8},{24,16},{25,24},{17,25},{9,17},{1,9},{2,1},{10,2},{18... | collective-permute-start | bytes 245768 | tf_op jit(solution)/shard_map/ppermute | solution.py:484
  75.8 13.5 %collective-permute-start.22 = (f32[256,128]{1,0:T(8,128)S(1)}, f32[256,128]{1,0:T(8,128)S(1)}, u32[]{:S(2)}, u32[]{:S(2)}) collective-permute-start(f32[256,128]{1,0:T(8,128)S(1)} %get-tuple-element.81), channel_id=1, source_target_pairs={{0,16},{8,24},{16,0},{24,8},{1,17},{9,25},{17,1},{25,9},{2,18},{10... | collective-permute-start | bytes 393224 | tf_op jit(solution)/shard_map/ppermute | solution.py:465
  77.8 11.5 %collective-permute-start.23 = (f32[256,128]{1,0:T(8,128)S(1)}, f32[256,128]{1,0:T(8,128)S(1)}, u32[]{:S(2)}, u32[]{:S(2)}) collective-permute-start(f32[256,128]{1,0:T(8,128)S(1)} %get-tuple-element.82), channel_id=1, source_target_pairs={{0,24},{8,0},{16,8},{24,16},{1,25},{9,1},{17,9},{25,17},{2,26},{10... | collective-permute-start | bytes 393224 | tf_op jit(solution)/shard_map/ppermute | solution.py:465
  81.0 8.3 %copy-start = (f32[2,16,64,128]{3,2,1,0:T(8,128)S(1)}, f32[2,16,64,128]{3,2,1,0:T(8,128)}, u32[]{:S(2)}) copy-start(f32[2,16,64,128]{3,2,1,0:T(8,128)} %gain.2) | copy-start | bytes 3145732
  81.0 8.3 %copy-start.1 = (s32[16,64,128]{2,1,0:T(8,128)S(1)}, s32[16,64,128]{2,1,0:T(8,128)}, u32[]{:S(2)}) copy-start(s32[16,64,128]{2,1,0:T(8,128)} %mask.5) | copy-start | bytes 1572868
  84.5 8.2 %collective-permute-start.18 = (f32[256,128]{1,0:T(8,128)S(1)}, f32[256,128]{1,0:T(8,128)S(1)}, u32[]{:S(2)}, u32[]{:S(2)}) collective-permute-start(f32[256,128]{1,0:T(8,128)S(1)} %get-tuple-element.77), channel_id=1, source_target_pairs={{0,8},{8,16},{16,24},{24,0},{1,9},{9,17},{17,25},{25,1},{2,10},{10... | collective-permute-start | bytes 393224 | tf_op jit(solution)/shard_map/ppermute | solution.py:465
  85.8 10.0 %collective-permute-start.19 = (f32[256,128]{1,0:T(8,128)S(1)}, f32[256,128]{1,0:T(8,128)S(1)}, u32[]{:S(2)}, u32[]{:S(2)}) collective-permute-start(f32[256,128]{1,0:T(8,128)S(1)} %get-tuple-element.78), channel_id=1, source_target_pairs={{0,16},{8,24},{16,0},{24,8},{1,17},{9,25},{17,1},{25,9},{2,18},{10... | collective-permute-start | bytes 393224 | tf_op jit(solution)/shard_map/ppermute | solution.py:465
  87.9 7.9 %collective-permute-start.20 = (f32[256,128]{1,0:T(8,128)S(1)}, f32[256,128]{1,0:T(8,128)S(1)}, u32[]{:S(2)}, u32[]{:S(2)}) collective-permute-start(f32[256,128]{1,0:T(8,128)S(1)} %get-tuple-element.79), channel_id=1, source_target_pairs={{0,24},{8,0},{16,8},{24,16},{1,25},{9,1},{17,9},{25,17},{2,26},{10... | collective-permute-start | bytes 393224 | tf_op jit(solution)/shard_map/ppermute | solution.py:465

commit v5 on v4

--- a/solution.py
+++ b/solution.py
@@ -263,15 +263,11 @@
                 at = pl.multiple_of(side * half + source[d] * count, 8)
                 held[i, pl.ds(at, count), :] = part[pl.ds(side * count * rows + i, count, rows), :]
 
-    ends = (position()[0][0] == groups - 1) & (lax.axis_index("gy") == lax.axis_size("gy") - 1)
     no_halo = jnp.zeros((2 * STEPS, cols), jnp.float32)
-    main, right_main = depths[0][...], depths[1][...]
-    halo, right_halo = [ref[...] for ref in depths[2:]] or (no_halo, no_halo)
-    depth = unfold(main, halo, groups)
-    right = jnp.where(ends, 0.0, unfold(right_main, right_halo, groups))
+    depth = unfold(depths[0][...], depths[1][...] if len(depths) > 1 else no_halo, groups)
     tall = depth.shape[0]
     lane = lax.broadcasted_iota(jnp.int32, depth.shape, 1)
-    right = jnp.where(lane == width - 1, pltpu.roll(right, width - 1, 1), pltpu.roll(depth, cols - 1, 1))
+    right = jnp.where(lane == width - 1, depth, pltpu.roll(depth, cols - 1, 1))
     depth_j[...] = jnp.minimum(depth, right)
     depth_i[pl.ds(0, tall - 1), :] = jnp.minimum(depth[:-1], depth[1:])
     depth_i[pl.ds(tall - 1, 1), :] = depth[tall - 1:]
@@ -308,14 +304,35 @@
     )(*depths, *parts)
 
 
-def spread_kernel(windows, field_rows, weight_rows, matrix, *refs):
+def edge_masks(depths, order):
+    groups = lax.axis_size("lev")
+    slot = position()[0][0]
+    gy = lax.axis_index("gy")
+    start = (slot == 0) & (gy == 0)
+    end = (slot == groups - 1) & (gy == lax.axis_size("gy") - 1)
+    no_halo = jnp.zeros((2 * STEPS, depths[0].shape[1]), jnp.float32)
+    masks = []
+    for k, out in enumerate((start, end)):
+        x = unfold(depths[k][...], depths[2 + k][...] if len(depths) > 2 else no_halo, groups)
+        x = jnp.where(out, 0.0, x)
+        x = jnp.broadcast_to(x[:, :1], (x.shape[0], order))
+        lane = lax.broadcasted_iota(jnp.int32, x.shape, 1)
+        level = lax.rem(lane, order // 2).astype(jnp.float32)
+        masks.append(jnp.where((lane < order // 2) | (level < x), 1.0, 0.0))
+    return masks
+
+
+def spread_kernel(windows, field_rows, weight_rows, count, matrix, *refs):
+    depths, refs = refs[:count], refs[count:]
     pieces = [refs[3 * k:3 * k + 3] for k in range(len(field_rows) + len(weight_rows))]
-    outs, (a, b, wi, wj) = refs[3 * len(pieces):-4], refs[-4:]
+    outs, (a, b, wi, wj, masks) = refs[3 * len(pieces):-5], refs[-5:]
     width, order = pieces[0][0].shape[1:]
     half = order // 2
     _, ext, wide, _ = a.shape
     lane = lax.broadcasted_iota(jnp.int32, (wide, order), 1)
+    row = lax.broadcasted_iota(jnp.int32, (wide, order), 0)
     nothing = jnp.zeros((PAD - STEPS, order), jnp.float32)
+    masks[0], masks[1] = edge_masks(depths, order)
 
     def row_of(some, rows, r):
         piece = [k for k in range(len(rows)) if r in rows[k]][0]
@@ -328,6 +345,9 @@
         for e, r in enumerate(window):
             a[n, e] = row_of(pieces[:len(field_rows)], field_rows, r)
             w = row_of(pieces[len(field_rows):], weight_rows, r)
+            at = pl.ds(STEPS + r, 1)
+            w = w * jnp.where(row == PAD - 1, masks[0, at, :], 1.0)
+            w = w * jnp.where(row == PAD + width - 1, masks[1, at, :], 1.0)
             other = pltpu.roll(w, half, 1)
             wi[n, e] = jnp.where(lane < half, w, other)
             wj[n, e] = jnp.where(lane < half, other, w)
@@ -368,19 +388,24 @@
     lax.fori_loop(0, rows, mix, 0, unroll=4)
 
 
-def spread_mix(windows, matrix, field, weights, groups):
+def spread_mix(windows, matrix, depths, field, weights, groups):
     width, order = field[0][1].shape[1:]
     cols = width * groups
     ext = len(windows[0])
     rows = len(windows) * (ext - 2 * STEPS) // groups
     shape = jax.ShapeDtypeStruct((order // groups * rows, cols), jnp.float32)
-    arrays = [x for piece in field + weights for x in piece[1:]]
+    arrays = list(depths) + [x for piece in field + weights for x in piece[1:]]
+    kernel = functools.partial(
+        spread_kernel, windows, [piece[0] for piece in field], [piece[0] for piece in weights], len(depths)
+    )
+    tall = field[0][1].shape[0] + 2 * STEPS
     return pl.pallas_call(
-        functools.partial(spread_kernel, windows, [piece[0] for piece in field], [piece[0] for piece in weights]),
+        kernel,
         in_specs=[vmem()] * (1 + len(arrays)),
         out_specs=[vmem()] * groups,
         out_shape=[shape] * groups,
-        scratch_shapes=[pltpu.VMEM((len(windows), ext, width + 2 * PAD, order), jnp.float32)] * 4,
+        scratch_shapes=[pltpu.VMEM((len(windows), ext, width + 2 * PAD, order), jnp.float32)] * 4
+        + [pltpu.VMEM((2, tall, order), jnp.float32)],
         compiler_params=params(),
         name="spread_mix",
     )(matrix, *arrays)
@@ -503,64 +528,70 @@
     inner_size = len(inner_rows) // devices
     inner_messages = weight_messages(inner_starts, inner_size, diffusion_i, diffusion_j, [sea_mask])
     inner_parts = exchange(inner_messages)
-    inner_messages, increment, norm_gain = lax.optimization_barrier((inner_messages, increment, norm_gain))
-    scaled = exchange(scaled_messages(increment, norm_gain, sea_mask, devices))
-
-    depth = sum(part[2 * levels * inner_size:] for part in inner_parts)
-    right_depth = lax.ppermute(depth, ("lev", "gy"), back)
-    depth, edge_i, edge_j = lax.optimization_barrier((depth, diffusion_i, diffusion_j))
-    above, below = halo_i(
+    inner_messages, edge_i, edge_j, increment, norm_gain = lax.optimization_barrier(
+        (inner_messages, diffusion_i, diffusion_j, increment, norm_gain)
+    )
+    halos = halo_i(
         *[
-            jnp.concatenate([depth[at], flat(edge_i[:, at]), flat(edge_j[:, at])], axis=0)
+            jnp.concatenate([flat(edge_i[:, at]), flat(edge_j[:, at])], axis=0)
             for at in (slice(0, STEPS), slice(-STEPS, None))
         ]
     )
-    sizes = STEPS, 2 * levels * STEPS
-    above_depth, above_weight = cut(above, *sizes)
-    below_depth, below_weight = cut(below, *sizes)
-    halo_depth = jnp.concatenate([below_depth, above_depth], axis=0)
-    here = turn_weights(inner_starts, inner_size, [depth, right_depth], inner_parts, order)
+    messages = scaled_messages(increment, norm_gain, sea_mask, devices)
+    scaled = exchange(messages)
+    messages, halos = lax.optimization_barrier((messages, halos))
+    outer_messages = weight_messages(outer_starts, some, diffusion_i, diffusion_j, halos=halos)
+
+    depth = sum(part[2 * levels * inner_size:] for part in inner_parts)
+    here = turn_weights(inner_starts, inner_size, [depth], inner_parts, order)
     left, right = halo_j(
-        jnp.concatenate([flat(here[:, :STEPS]), halo_depth], axis=0),
+        jnp.concatenate([flat(here[:, :STEPS]), depth], axis=0),
         flat(here[:, -STEPS:]),
     )
-    right, right_halo_depth = cut(right, len(inner_rows) * STEPS, 2 * STEPS)
-    outer_messages = weight_messages(
-        outer_starts, some, diffusion_i, diffusion_j, halos=[above_weight, below_weight]
-    )
+    right, right_depth = cut(right, len(inner_rows) * STEPS, rows)
 
     balance = jnp.eye(order, dtype=jnp.float32) + coupling
     by_device = balance.reshape(2, devices, levels, order)
     adjoint = jnp.concatenate([by_device[:, s].reshape(2 * levels, order) for s in source], axis=0).T
     forward = jnp.concatenate([by_device[:, t].reshape(2 * levels, order) for t in to], axis=0)
 
-    scaled[1], left, right = lax.optimization_barrier((scaled[1], left, right))
-    weights = [(inner_rows, here, left, right)]
+    scaled[1], outer_messages = lax.optimization_barrier((scaled[1], outer_messages))
+    early = shift(outer_messages[1], 1)
     mixed = adjoint_mix(adjoint, depth, scaled, length, width)
-    left, right = halo_j(flat(mixed[:, :STEPS]), flat(mixed[:, -STEPS:]))
-    scaled[1], outer_messages[1] = lax.optimization_barrier((scaled[1], outer_messages[1]))
-    early = shift(outer_messages[1], 1)
+    edges = flat(mixed[:, :STEPS]), flat(mixed[:, -STEPS:])
+    edges, inner_weights = lax.optimization_barrier((edges, (here, left, right)))
+    left, right = halo_j(*edges)
     left, right, outer_messages, early = lax.optimization_barrier((left, right, outer_messages, early))
     outer_parts = [outer_messages[0], early] + [shift(outer_messages[d], d) for d in range(2, devices)]
     field = [(list(range(length)), mixed, left, right)]
-    inner_mixed = spread_mix([inner_rows], forward, field, weights, devices)
+    weights = [(inner_rows, *inner_weights)]
+    depths = [depth, right_depth]
+    inner_mixed = spread_mix([inner_rows], forward, depths, field, weights, devices)
+    _, upper, lower = lax.optimization_barrier((left, mixed[:STEPS], mixed[-STEPS:]))
     _, outer_parts = lax.optimization_barrier((inner_mixed[0], outer_parts))
     inner_mixed = exchange(inner_mixed)
     out = result((inner,), norm_gain, sea_mask, inner_mixed, None)
 
-    above, below = halo_i(flat(mixed[:STEPS]), flat(mixed[-STEPS:]))
+    above, below = halo_i(
+        jnp.concatenate([flat(upper), depth[:STEPS]], axis=0),
+        jnp.concatenate([flat(lower), depth[-STEPS:]], axis=0),
+    )
+    above, above_depth = cut(above, STEPS * width, STEPS)
+    below, below_depth = cut(below, STEPS * width, STEPS)
+    halo_depth = jnp.concatenate([below_depth, above_depth], axis=0)
     halo = jnp.concatenate([above, below], axis=0).reshape(2 * STEPS, width, order)
-    here = turn_weights(outer_starts, some, [depth, right_depth, halo_depth, right_halo_depth], outer_parts, order)
+    here = turn_weights(outer_starts, some, [depth, halo_depth], outer_parts, order)
     left, right = halo_j(
-        jnp.concatenate([flat(here[:, :STEPS]), flat(halo[:, :STEPS])], axis=0),
+        jnp.concatenate([flat(here[:, :STEPS]), flat(halo[:, :STEPS]), halo_depth], axis=0),
         jnp.concatenate([flat(here[:, -STEPS:]), flat(halo[:, -STEPS:])], axis=0),
     )
     sizes = len(outer_rows) * STEPS, 2 * STEPS * STEPS
     left, halo_left = cut(left, *sizes)
-    right, halo_right = cut(right, *sizes)
+    right, halo_right, right_halo_depth = cut(right, *sizes, 2 * STEPS)
     weights.append((outer_rows, here, left, right))
     field.append((list(range(-STEPS, 0)) + list(range(length, length + STEPS)), halo, halo_left, halo_right))
-    outer_mixed = exchange(spread_mix(windows, forward, field, weights, devices))
+    depths += [halo_depth, right_halo_depth]
+    outer_mixed = exchange(spread_mix(windows, forward, depths, field, weights, devices))
     return result(outer, norm_gain, sea_mask, outer_mixed, out)
 
 

time: 98.3 us -> 96.6 us (0.983)
  waiting for transfers between devices: 32.6 us -> 11.4 us
  starting transfers between devices: 41.3 us -> 60 us
    ppermute x15, waiting for transfers between devices: 23.7 us -> 6.45 us  [shift(): lax.ppermute(x, 'lev', [(k, (k + d) % devices) for k in range(devices)])]
    ppermute x3, starting transfers between devices: 12.3 us -> 25.4 us  [halo_j(): lax.ppermute(last, ('lev', 'gy'), ahead)]
    ppermute x15, starting transfers between devices: 24.2 us -> 31.5 us  [shift(): lax.ppermute(x, 'lev', [(k, (k + d) % devices) for k in range(devices)])]
    ppermute x1 -> x0, waiting for transfers between devices: 5.68 us -> none  [shards(): right_depth = lax.ppermute(depth, ('lev', 'gy'), back)]
    ppermute x3, waiting for transfers between devices: 0.01 us -> 2.9 us  [halo_j(): lax.ppermute(last, ('lev', 'gy'), ahead)]
    ppermute x3, starting transfers between devices: 1.78 us -> 0.07 us  [halo_j(): lax.ppermute(first, ('lev', 'gy'), back)]
    ppermute x3, waiting for transfers between devices: 3.22 us -> 2.05 us  [halo_j(): lax.ppermute(first, ('lev', 'gy'), back)]
  transfers between devices with their start and end apart: 24 -> 23, of which waited for: 8 -> 5; matrix products, arithmetic and copies ran while one was open for 1% -> 0% of each run, Pallas kernels for 15% -> 18%
where the time goes in v5:
time: 96.6 us; the launch traced here: 96.3 us
  starting transfers between devices  60 us (62%)
  Pallas kernels  23.1 us (24%)
  waiting for transfers between devices  11.4 us (12%)
  local copies, waits for them, and re-layouts  1.24 us (1%)
    ppermute x15, starting transfers between devices, shift(): lax.ppermute(x, 'lev', [(k, (k + d) % devices) for k in range(devices)])  31.5 us
    ppermute x3, starting transfers between devices, halo_j(): lax.ppermute(last, ('lev', 'gy'), ahead)  25.4 us
    pallas_call x2, Pallas kernels, spread_mix(): pl.pallas_call(kernel, in_specs=[vmem()] * (1 + len(arrays)), out_specs=[...  6.91 us
    ppermute x15, waiting for transfers between devices, shift(): lax.ppermute(x, 'lev', [(k, (k + d) % devices) for k in range(devices)])  6.45 us
    pallas_call x2, Pallas kernels, weight_messages(): pl.pallas_call(functools.partial(pack_kernel, starts, rows, len(mask)), i...  5.9 us
    pallas_call x2, Pallas kernels, result(): pl.pallas_call(kernel, in_specs=[vmem()] * 2 + [anywhere] * (groups + len...  4.23 us
    pallas_call x1, Pallas kernels, scaled_messages(): pl.pallas_call(scaled_kernel, in_specs=[pl.BlockSpec(memory_space=pl.ANY)...  3.25 us
    ppermute x2, starting transfers between devices, halo_i(): both = lax.ppermute(jnp.concatenate([first, last], axis=0), 'gx', up)  3.11 us
  transfers between devices with their start and end apart: 23, of which 5 were waited for; matrix products, arithmetic and copies ran while one was open for 0% of the time, Pallas kernels for 18%

profile of v5, /device:TPU:0, one launch (start us, length us, event | category | flops | bytes accessed | tf_op | source)
XLA Modules:
  0.0 96.3 jit_solution(10427195218167428301)
XLA Ops:
  0.0 3.8 %weight_messages.2 = (f32[336,128]{1,0:T(8,128)}, f32[336,128]{1,0:T(8,128)}, f32[336,128]{1,0:T(8,128)}, f32[336,128]{1,0:T(8,128)}) custom-call(f32[16,64,128]{2,1,0:T(8,128)} %along_i.3, f32[16,64,128]{2,1,0:T(8,128)} %along_j.3, s32[16,64,128]{2,1,0:T(8,128)} %mask.5), custom_call_target="tpu_custom_call" | custom-call | tf_op jit(solution)/shard_map/weight_messages/pallas_call | solution.py:191
  3.9 3.1 %collective-permute-start = (f32[336,128]{1,0:T(8,128)}, f32[336,128]{1,0:T(8,128)S(1)}, u32[]{:S(2)}, u32[]{:S(2)}) collective-permute-start(f32[336,128]{1,0:T(8,128)} %get-tuple-element.54), channel_id=1, source_target_pairs={{0,8},{8,16},{16,24},{24,0},{1,9},{9,17},{17,25},{25,1},{2,10},{10... | collective-permute-start | bytes 516104 | tf_op jit(solution)/shard_map/ppermute | solution.py:490
  6.9 2.6 %collective-permute-start.1 = (f32[336,128]{1,0:T(8,128)}, f32[336,128]{1,0:T(8,128)S(1)}, u32[]{:S(2)}, u32[]{:S(2)}) collective-permute-start(f32[336,128]{1,0:T(8,128)} %get-tuple-element.55), channel_id=1, source_target_pairs={{0,16},{8,24},{16,0},{24,8},{1,17},{9,25},{17,1},{25,9},{2,18},{10... | collective-permute-start | bytes 516104 | tf_op jit(solution)/shard_map/ppermute | solution.py:490
  9.5 1.3 %collective-permute-start.2 = (f32[336,128]{1,0:T(8,128)}, f32[336,128]{1,0:T(8,128)S(1)}, u32[]{:S(2)}, u32[]{:S(2)}) collective-permute-start(f32[336,128]{1,0:T(8,128)} %get-tuple-element.56), channel_id=1, source_target_pairs={{0,24},{8,0},{16,8},{24,16},{1,25},{9,1},{17,9},{25,17},{2,26},{10... | collective-permute-start | bytes 516104 | tf_op jit(solution)/shard_map/ppermute | solution.py:490
  10.9 0.0 copy-done.2
  10.9 1.6 %collective-permute-start.5 = (f32[256,128]{1,0:T(8,128)S(1)}, f32[256,128]{1,0:T(8,128)S(1)}, u32[]{:S(2)}, u32[]{:S(2)}) collective-permute-start(f32[256,128]{1,0:T(8,128)S(1)} %pad_maximum_fusion.1), channel_id=1, source_target_pairs={{4,0},{0,4},{5,1},{1,5},{6,2},{2,6},{7,3},{3,7},{12,8},{8,12},{13,... | collective-permute-start | bytes 393224 | tf_op jit(solution)/shard_map/ppermute | solution.py:504
  12.5 3.3 %scaled_messages.1 = (f32[512,128]{1,0:T(8,128)}, f32[512,128]{1,0:T(8,128)}, f32[512,128]{1,0:T(8,128)}, f32[512,128]{1,0:T(8,128)}) custom-call(f32[2,16,64,128]{3,2,1,0:T(8,128)} %increment, f32[2,16,64,128]{3,2,1,0:T(8,128)} %gain.2, s32[16,64,128]{2,1,0:T(8,128)} %mask.5), custom_call_target="tpu_custom_call" | custom-call | tf_op jit(solution)/shard_map/scaled_messages/pallas_call | solution.py:117
  15.7 0.0 copy-start.6
  15.8 0.7 collective-permute-start.4
  16.5 0.1 copy-done.6
  16.7 0.1 copy.13.matrix
  16.8 0.0 collective-permute-done.5
  16.8 0.8 copy-done.8
  17.6 0.3 collective-permute-start.6
  18.0 2.1 %weight_messages.3 = (f32[256,128]{1,0:T(8,128)S(1)}, f32[256,128]{1,0:T(8,128)S(1)}, f32[256,128]{1,0:T(8,128)S(1)}, f32[256,128]{1,0:T(8,128)S(1)}) custom-call(f32[16,64,128]{2,1,0:T(8,128)S(1)} %copy-done.2, f32[16,64,128]{2,1,0:T(8,128)S(1)} %copy-done.3, f32[128,128]{1,0:T(8,128)S(1)} %get-tuple-element.65.refs_0_, ...), custom_call_target="tpu_custom_call" | custom-call | tf_op jit(solution)/shard_map/weight_messages/pallas_call | solution.py:191
  20.0 0.0 collective-permute-done.refs_2_
  20.0 2.8 %collective-permute-start.7 = (f32[512,128]{1,0:T(8,128)S(1)}, f32[512,128]{1,0:T(8,128)S(1)}, u32[]{:S(2)}, u32[]{:S(2)}) collective-permute-start(f32[512,128]{1,0:T(8,128)S(1)} %copy-done.7), channel_id=1, source_target_pairs={{0,24},{8,0},{16,8},{24,16},{1,25},{9,1},{17,9},{25,17},{2,26},{10... | collective-permute-start | bytes 786440 | tf_op jit(solution)/shard_map/ppermute | solution.py:490
  22.8 0.0 collective-permute-done.1.refs_3_
  22.8 0.0 collective-permute-done.2.refs_4_
  22.8 0.4 turn_weights.2.refs_5_.refs_10_
  23.3 0.0 copy-start.4
  23.3 13.7 %collective-permute-start.8 = (f32[160,128]{1,0:T(8,128)S(1)}, f32[160,128]{1,0:T(8,128)S(1)}, u32[]{:S(2)}, u32[]{:S(2)}) collective-permute-start(f32[160,128]{1,0:T(8,128)S(1)} %bitcast.47), channel_id=1, source_target_pairs={{0,8},{8,16},{16,24},{24,25},{25,17},{17,9},{9,1},{1,2},{2,10},{10... | collective-permute-start | bytes 245768 | tf_op jit(solution)/shard_map/ppermute | solution.py:509
  37.1 0.0 collective-permute-start.3
  37.1 0.0 collective-permute-done.4.refs_1_
  37.1 4.5 %collective-permute-start.11 = (f32[256,128]{1,0:T(8,128)S(1)}, f32[256,128]{1,0:T(8,128)S(1)}, u32[]{:S(2)}, u32[]{:S(2)}) collective-permute-start(f32[256,128]{1,0:T(8,128)S(1)} %get-tuple-element.75), channel_id=1, source_target_pairs={{0,8},{8,16},{16,24},{24,0},{1,9},{9,17},{17,25},{25,1},{2,10},{10... | collective-permute-start | bytes 393224 | tf_op jit(solution)/shard_map/ppermute | solution.py:490
  41.6 2.8 %collective-permute-done.6.refs_2_ = f32[512,128]{1,0:T(8,128)S(1)} collective-permute-done((f32[512,128]{1,0:T(8,128)S(1)}, f32[512,128]{1,0:T(8,128)S(1)}, u32[]{:S(2)}, u32[]{:S(2)}) %collective-permute-start.6) | collective-permute-done | bytes 262176 | tf_op jit(solution)/shard_map/ppermute | solution.py:490
  44.4 0.0 collective-permute-done.7.refs_3_
  44.4 2.0 %adjoint_mix.1.refs_2_.refs_4_ = f32[64,32,128]{2,1,0:T(8,128)S(1)} custom-call(f32[128,128]{1,0:T(8,128)S(1)} %copy.13.matrix, f32[16,128]{1,0:T(8,128)S(1)} %slice_add_fusion.refs_0_.depths, f32[512,128]{1,0:T(8,128)S(1)} %copy-done.4, f32[512,128]{1,0:T(8,128)S(1)} %collective-permute-done.4.refs_1_, f32[512,128]{1,0:T(8,128)S(1)} %collective-permute-done.6.refs_2_, ...), custom_call_target="tpu_custom_call" | custom-call | tf_op jit(solution)/shard_map/adjoint_mix/pallas_call | solution.py:231
  46.5 0.0 collective-permute-done.3
  46.5 0.0 collective-permute-done.8.refs_6_.refs_11_
  46.5 6.2 %collective-permute-start.9 = (f32[256,128]{1,0:T(8,128)S(1)}, f32[256,128]{1,0:T(8,128)S(1)}, u32[]{:S(2)}, u32[]{:S(2)}) collective-permute-start(f32[256,128]{1,0:T(8,128)S(1)} %bitcast.42), channel_id=1, source_target_pairs={{0,8},{8,16},{16,24},{24,25},{25,17},{17,9},{9,1},{1,2},{2,10},{10... | collective-permute-start | bytes 393224 | tf_op jit(solution)/shard_map/ppermute | solution.py:509
  52.7 0.0 collective-permute-start.10
  52.7 0.0 collective-permute-done.11.refs_3_
  52.8 2.9 %collective-permute-done.9.refs_3_.refs_5_ = f32[256,128]{1,0:T(8,128)S(1)} collective-permute-done((f32[256,128]{1,0:T(8,128)S(1)}, f32[256,128]{1,0:T(8,128)S(1)}, u32[]{:S(2)}, u32[]{:S(2)}) %collective-permute-start.9) | collective-permute-done | bytes 131104 | tf_op jit(solution)/shard_map/ppermute | solution.py:509
  55.7 2.0 %collective-permute-done.10.refs_4_.refs_6_ = f32[256,128]{1,0:T(8,128)S(1)} collective-permute-done((f32[256,128]{1,0:T(8,128)S(1)}, f32[256,128]{1,0:T(8,128)S(1)}, u32[]{:S(2)}, u32[]{:S(2)}) %collective-permute-start.10) | collective-permute-done | bytes 131104 | tf_op jit(solution)/shard_map/ppermute | solution.py:509
  57.7 1.6 %collective-permute-start.12 = (f32[264,128]{1,0:T(8,128)S(1)}, f32[264,128]{1,0:T(8,128)S(1)}, u32[]{:S(2)}, u32[]{:S(2)}) collective-permute-start(f32[264,128]{1,0:T(8,128)S(1)} %pad_maximum_fusion), channel_id=1, source_target_pairs={{4,0},{0,4},{5,1},{1,5},{6,2},{2,6},{7,3},{3,7},{12,8},{8,12},{13,... | collective-permute-start | bytes 405512 | tf_op jit(solution)/shard_map/ppermute | solution.py:504
  59.3 0.2 collective-permute-start.13
  59.5 2.6 %collective-permute-start.14 = (f32[256,128]{1,0:T(8,128)S(1)}, f32[256,128]{1,0:T(8,128)S(1)}, u32[]{:S(2)}, u32[]{:S(2)}) collective-permute-start(f32[256,128]{1,0:T(8,128)S(1)} %get-tuple-element.89), channel_id=1, source_target_pairs={{0,24},{8,0},{16,8},{24,16},{1,25},{9,1},{17,9},{25,17},{2,26},{10... | collective-permute-start | bytes 393224 | tf_op jit(solution)/shard_map/ppermute | solution.py:490
  62.1 3.4 %spread_mix.2 = (f32[256,128]{1,0:T(8,128)S(1)}, f32[256,128]{1,0:T(8,128)S(1)}, f32[256,128]{1,0:T(8,128)S(1)}, f32[256,128]{1,0:T(8,128)S(1)}) custom-call(f32[128,128]{1,0:T(8,128)S(1)} %get-tuple-element.127.matrix, f32[16,128]{1,0:T(8,128)S(1)} %slice_add_fusion.refs_0_.depths, f32[16,128]{1,0:T(8,128)S(1)} %split.44.refs_1_, ...), custom_call_target="tpu_custom_call" | custom-call | tf_op jit(solution)/shard_map/spread_mix/pallas_call | solution.py:402
  65.4 0.1 collective-permute-start.20
  65.5 2.4 %collective-permute-done.13.refs_4_ = f32[256,128]{1,0:T(8,128)S(1)} collective-permute-done((f32[256,128]{1,0:T(8,128)S(1)}, f32[256,128]{1,0:T(8,128)S(1)}, u32[]{:S(2)}, u32[]{:S(2)}) %collective-permute-start.13) | collective-permute-done | bytes 131104 | tf_op jit(solution)/shard_map/ppermute | solution.py:490
  67.9 0.0 collective-permute-done.14.refs_5_
  68.0 0.0 collective-permute-done.12
  68.0 0.4 turn_weights.3.refs_13_
  68.5 0.1 collective-permute-start.15
  68.6 5.4 %collective-permute-start.16 = (f32[160,128]{1,0:T(8,128)S(1)}, f32[160,128]{1,0:T(8,128)S(1)}, u32[]{:S(2)}, u32[]{:S(2)}) collective-permute-start(f32[160,128]{1,0:T(8,128)S(1)} %pad_maximum_fusion.7), channel_id=1, source_target_pairs={{0,8},{8,16},{16,24},{24,25},{25,17},{17,9},{9,1},{1,2},{2,10},{10... | collective-permute-start | bytes 245768 | tf_op jit(solution)/shard_map/ppermute | solution.py:509
  74.0 1.5 %collective-permute-start.21 = (f32[256,128]{1,0:T(8,128)S(1)}, f32[256,128]{1,0:T(8,128)S(1)}, u32[]{:S(2)}, u32[]{:S(2)}) collective-permute-start(f32[256,128]{1,0:T(8,128)S(1)} %get-tuple-element.99), channel_id=1, source_target_pairs={{0,16},{8,24},{16,0},{24,8},{1,17},{9,25},{17,1},{25,9},{2,18},{10... | collective-permute-start | bytes 393224 | tf_op jit(solution)/shard_map/ppermute | solution.py:490
  75.4 2.9 %collective-permute-start.22 = (f32[256,128]{1,0:T(8,128)S(1)}, f32[256,128]{1,0:T(8,128)S(1)}, u32[]{:S(2)}, u32[]{:S(2)}) collective-permute-start(f32[256,128]{1,0:T(8,128)S(1)} %get-tuple-element.100), channel_id=1, source_target_pairs={{0,24},{8,0},{16,8},{24,16},{1,25},{9,1},{17,9},{25,17},{2,26},{10... | collective-permute-start | bytes 393224 | tf_op jit(solution)/shard_map/ppermute | solution.py:490
  78.3 0.0 collective-permute-done.16
  78.3 0.0 collective-permute-done.15
  78.3 0.0 copy-start
  78.4 0.0 copy-start.1
  78.4 3.5 %spread_mix.3 = (f32[256,128]{1,0:T(8,128)S(1)}, f32[256,128]{1,0:T(8,128)S(1)}, f32[256,128]{1,0:T(8,128)S(1)}, f32[256,128]{1,0:T(8,128)S(1)}) custom-call(f32[128,128]{1,0:T(8,128)S(1)} %get-tuple-element.127.matrix, f32[16,128]{1,0:T(8,128)S(1)} %slice_add_fusion.refs_0_.depths, f32[16,128]{1,0:T(8,128)S(1)} %split.44.refs_1_, ...), custom_call_target="tpu_custom_call" | custom-call | tf_op jit(solution)/shard_map/spread_mix/pallas_call | solution.py:402
  81.9 3.7 %collective-permute-start.17 = (f32[256,128]{1,0:T(8,128)S(1)}, f32[256,128]{1,0:T(8,128)S(1)}, u32[]{:S(2)}, u32[]{:S(2)}) collective-permute-start(f32[256,128]{1,0:T(8,128)S(1)} %get-tuple-element.95), channel_id=1, source_target_pairs={{0,8},{8,16},{16,24},{24,0},{1,9},{9,17},{17,25},{25,1},{2,10},{10... | collective-permute-start | bytes 393224 | tf_op jit(solution)/shard_map/ppermute | solution.py:490
  85.6 2.5 %collective-permute-start.18 = (f32[256,128]{1,0:T(8,128)S(1)}, f32[256,128]{1,0:T(8,128)S(1)}, u32[]{:S(2)}, u32[]{:S(2)}) collective-permute-start(f32[256,128]{1,0:T(8,128)S(1)} %get-tuple-element.96), channel_id=1, source_target_pairs={{0,16},{8,24},{16,0},{24,8},{1,17},{9,25},{17,1},{25,9},{2,18},{10... | collective-permute-start | bytes 393224 | tf_op jit(solution)/shard_map/ppermute | solution.py:490
  88.1 0.0 collective-permute-done.20.refs_1_
  88.1 2.8 %collective-permute-start.19 = (f32[256,128]{1,0:T(8,128)S(1)}, f32[256,128]{1,0:T(8,128)S(1)}, u32[]{:S(2)}, u32[]{:S(2)}) collective-permute-start(f32[256,128]{1,0:T(8,128)S(1)} %get-tuple-element.97), channel_id=1, source_target_pairs={{0,24},{8,0},{16,8},{24,16},{1,25},{9,1},{17,9},{25,17},{2,26},{10... | collective-permute-start | bytes 393224 | tf_op jit(solution)/shard_map/ppermute | solution.py:490
  90.9 0.0 collective-permute-done.21.refs_2_
  90.9 0.0 collective-permute-done.22.refs_3_
  91.0 2.1 %result.2.refs_4_ = f32[2,16,64,128]{3,2,1,0:T(8,128)} custom-call(f32[2,16,64,128]{3,2,1,0:T(8,128)S(1)} %copy-done, s32[16,64,128]{2,1,0:T(8,128)S(1)} %copy-done.1, f32[256,128]{1,0:T(8,128)S(1)} %get-tuple-element.85.refs_0_, f32[256,128]{1,0:T(8,128)S(1)} %collective-permute-done.20.refs_1_, f32[256,128]{1,0:T(8,128)S(1)} %collective-permute-done.21.refs_2_, ...), custom_call_target="tpu_custom_call" | custom-call | tf_op jit(solution)/shard_map/result/pallas_call | solution.py:461
  93.1 0.0 collective-permute-done.17.refs_1_
  93.1 1.1 %collective-permute-done.18.refs_2_ = f32[256,128]{1,0:T(8,128)S(1)} collective-permute-done((f32[256,128]{1,0:T(8,128)S(1)}, f32[256,128]{1,0:T(8,128)S(1)}, u32[]{:S(2)}, u32[]{:S(2)}) %collective-permute-start.18) | collective-permute-done | bytes 131104 | tf_op jit(solution)/shard_map/ppermute | solution.py:490
  94.2 0.0 collective-permute-done.19.refs_3_
  94.2 2.1 %result.3 = f32[2,16,64,128]{3,2,1,0:T(8,128)} custom-call(f32[2,16,64,128]{3,2,1,0:T(8,128)S(1)} %copy-done, s32[16,64,128]{2,1,0:T(8,128)S(1)} %copy-done.1, f32[256,128]{1,0:T(8,128)S(1)} %get-tuple-element.94.refs_0_, f32[256,128]{1,0:T(8,128)S(1)} %collective-permute-done.17.refs_1_, ...), custom_call_target="tpu_custom_call", output_to_operand_aliasing={{}: (6, {})} | custom-call | tf_op jit(solution)/shard_map/result/pallas_call | solution.py:461
  (39 shorter events, 0.4 us)
Async XLA Ops:
  0.0 10.9 %copy-start.3 = (f32[16,64,128]{2,1,0:T(8,128)S(1)}, f32[16,64,128]{2,1,0:T(8,128)}, u32[]{:S(2)}) copy-start(f32[16,64,128]{2,1,0:T(8,128)} %along_j.3) | copy-start | bytes 1572868
  0.0 10.9 %copy-start.2 = (f32[16,64,128]{2,1,0:T(8,128)S(1)}, f32[16,64,128]{2,1,0:T(8,128)}, u32[]{:S(2)}) copy-start(f32[16,64,128]{2,1,0:T(8,128)} %along_i.3) | copy-start | bytes 1572868
  3.9 16.2 %collective-permute-start = (f32[336,128]{1,0:T(8,128)}, f32[336,128]{1,0:T(8,128)S(1)}, u32[]{:S(2)}, u32[]{:S(2)}) collective-permute-start(f32[336,128]{1,0:T(8,128)} %get-tuple-element.54), channel_id=1, source_target_pairs={{0,8},{8,16},{16,24},{24,0},{1,9},{9,17},{17,25},{25,1},{2,10},{10... | collective-permute-start | bytes 516104 | tf_op jit(solution)/shard_map/ppermute | solution.py:490
  6.9 15.9 %collective-permute-start.1 = (f32[336,128]{1,0:T(8,128)}, f32[336,128]{1,0:T(8,128)S(1)}, u32[]{:S(2)}, u32[]{:S(2)}) collective-permute-start(f32[336,128]{1,0:T(8,128)} %get-tuple-element.55), channel_id=1, source_target_pairs={{0,16},{8,24},{16,0},{24,8},{1,17},{9,25},{17,1},{25,9},{2,18},{10... | collective-permute-start | bytes 516104 | tf_op jit(solution)/shard_map/ppermute | solution.py:490
  9.5 13.3 %collective-permute-start.2 = (f32[336,128]{1,0:T(8,128)}, f32[336,128]{1,0:T(8,128)S(1)}, u32[]{:S(2)}, u32[]{:S(2)}) collective-permute-start(f32[336,128]{1,0:T(8,128)} %get-tuple-element.56), channel_id=1, source_target_pairs={{0,24},{8,0},{16,8},{24,16},{1,25},{9,1},{17,9},{25,17},{2,26},{10... | collective-permute-start | bytes 516104 | tf_op jit(solution)/shard_map/ppermute | solution.py:490
  10.9 5.9 %collective-permute-start.5 = (f32[256,128]{1,0:T(8,128)S(1)}, f32[256,128]{1,0:T(8,128)S(1)}, u32[]{:S(2)}, u32[]{:S(2)}) collective-permute-start(f32[256,128]{1,0:T(8,128)S(1)} %pad_maximum_fusion.1), channel_id=1, source_target_pairs={{4,0},{0,4},{5,1},{1,5},{6,2},{2,6},{7,3},{3,7},{12,8},{8,12},{13,... | collective-permute-start | bytes 393224 | tf_op jit(solution)/shard_map/ppermute | solution.py:504
  15.7 0.8 copy-start.6
  15.8 21.3 %collective-permute-start.4 = (f32[512,128]{1,0:T(8,128)}, f32[512,128]{1,0:T(8,128)S(1)}, u32[]{:S(2)}, u32[]{:S(2)}) collective-permute-start(f32[512,128]{1,0:T(8,128)} %get-tuple-element.60), channel_id=1, source_target_pairs={{0,8},{8,16},{16,24},{24,0},{1,9},{9,17},{17,25},{25,1},{2,10},{10... | collective-permute-start | bytes 786440 | tf_op jit(solution)/shard_map/ppermute | solution.py:490
  16.6 1.0 copy-start.8
  17.6 26.8 %collective-permute-start.6 = (f32[512,128]{1,0:T(8,128)S(1)}, f32[512,128]{1,0:T(8,128)S(1)}, u32[]{:S(2)}, u32[]{:S(2)}) collective-permute-start(f32[512,128]{1,0:T(8,128)S(1)} %copy-done.8), channel_id=1, source_target_pairs={{0,16},{8,24},{16,0},{24,8},{1,17},{9,25},{17,1},{25,9},{2,18},{10... | collective-permute-start | bytes 786440 | tf_op jit(solution)/shard_map/ppermute | solution.py:490
  17.9 2.1 %copy-start.7 = (f32[512,128]{1,0:T(8,128)S(1)}, f32[512,128]{1,0:T(8,128)}, u32[]{:S(2)}) copy-start(f32[512,128]{1,0:T(8,128)} %get-tuple-element.62) | copy-start | bytes 786436
  17.9 4.9 %copy-start.5 = (f32[336,128]{1,0:T(8,128)S(1)}, f32[336,128]{1,0:T(8,128)}, u32[]{:S(2)}) copy-start(f32[336,128]{1,0:T(8,128)} %get-tuple-element.53.refs_1_) | copy-start | bytes 516100
  20.0 24.4 %collective-permute-start.7 = (f32[512,128]{1,0:T(8,128)S(1)}, f32[512,128]{1,0:T(8,128)S(1)}, u32[]{:S(2)}, u32[]{:S(2)}) collective-permute-start(f32[512,128]{1,0:T(8,128)S(1)} %copy-done.7), channel_id=1, source_target_pairs={{0,24},{8,0},{16,8},{24,16},{1,25},{9,1},{17,9},{25,17},{2,26},{10... | collective-permute-start | bytes 786440 | tf_op jit(solution)/shard_map/ppermute | solution.py:490
  23.3 21.1 %copy-start.4 = (f32[512,128]{1,0:T(8,128)S(1)}, f32[512,128]{1,0:T(8,128)}, u32[]{:S(2)}) copy-start(f32[512,128]{1,0:T(8,128)} %get-tuple-element.59.refs_0_) | copy-start | bytes 786436
  23.3 23.1 %collective-permute-start.8 = (f32[160,128]{1,0:T(8,128)S(1)}, f32[160,128]{1,0:T(8,128)S(1)}, u32[]{:S(2)}, u32[]{:S(2)}) collective-permute-start(f32[160,128]{1,0:T(8,128)S(1)} %bitcast.47), channel_id=1, source_target_pairs={{0,8},{8,16},{16,24},{24,25},{25,17},{17,9},{9,1},{1,2},{2,10},{10... | collective-permute-start | bytes 245768 | tf_op jit(solution)/shard_map/ppermute | solution.py:509
  37.1 9.4 %collective-permute-start.3 = (f32[176,128]{1,0:T(8,128)S(1)}, f32[176,128]{1,0:T(8,128)S(1)}, u32[]{:S(2)}, u32[]{:S(2)}) collective-permute-start(f32[176,128]{1,0:T(8,128)S(1)} %pad_maximum_fusion.3), channel_id=1, source_target_pairs={{8,0},{16,8},{24,16},{25,24},{17,25},{9,17},{1,9},{2,1},{10,2},{18... | collective-permute-start | bytes 270344 | tf_op jit(solution)/shard_map/ppermute | solution.py:509
  37.1 15.7 %collective-permute-start.11 = (f32[256,128]{1,0:T(8,128)S(1)}, f32[256,128]{1,0:T(8,128)S(1)}, u32[]{:S(2)}, u32[]{:S(2)}) collective-permute-start(f32[256,128]{1,0:T(8,128)S(1)} %get-tuple-element.75), channel_id=1, source_target_pairs={{0,8},{8,16},{16,24},{24,0},{1,9},{9,17},{17,25},{25,1},{2,10},{10... | collective-permute-start | bytes 393224 | tf_op jit(solution)/shard_map/ppermute | solution.py:490
  46.5 9.2 %collective-permute-start.9 = (f32[256,128]{1,0:T(8,128)S(1)}, f32[256,128]{1,0:T(8,128)S(1)}, u32[]{:S(2)}, u32[]{:S(2)}) collective-permute-start(f32[256,128]{1,0:T(8,128)S(1)} %bitcast.42), channel_id=1, source_target_pairs={{0,8},{8,16},{16,24},{24,25},{25,17},{17,9},{9,1},{1,2},{2,10},{10... | collective-permute-start | bytes 393224 | tf_op jit(solution)/shard_map/ppermute | solution.py:509
  52.7 5.0 %collective-permute-start.10 = (f32[256,128]{1,0:T(8,128)S(1)}, f32[256,128]{1,0:T(8,128)S(1)}, u32[]{:S(2)}, u32[]{:S(2)}) collective-permute-start(f32[256,128]{1,0:T(8,128)S(1)} %bitcast.41), channel_id=1, source_target_pairs={{8,0},{16,8},{24,16},{25,24},{17,25},{9,17},{1,9},{2,1},{10,2},{18... | collective-permute-start | bytes 393224 | tf_op jit(solution)/shard_map/ppermute | solution.py:509
  57.7 10.2 %collective-permute-start.12 = (f32[264,128]{1,0:T(8,128)S(1)}, f32[264,128]{1,0:T(8,128)S(1)}, u32[]{:S(2)}, u32[]{:S(2)}) collective-permute-start(f32[264,128]{1,0:T(8,128)S(1)} %pad_maximum_fusion), channel_id=1, source_target_pairs={{4,0},{0,4},{5,1},{1,5},{6,2},{2,6},{7,3},{3,7},{12,8},{8,12},{13,... | collective-permute-start | bytes 405512 | tf_op jit(solution)/shard_map/ppermute | solution.py:504
  59.3 8.7 %collective-permute-start.13 = (f32[256,128]{1,0:T(8,128)S(1)}, f32[256,128]{1,0:T(8,128)S(1)}, u32[]{:S(2)}, u32[]{:S(2)}) collective-permute-start(f32[256,128]{1,0:T(8,128)S(1)} %get-tuple-element.88), channel_id=1, source_target_pairs={{0,16},{8,24},{16,0},{24,8},{1,17},{9,25},{17,1},{25,9},{2,18},{10... | collective-permute-start | bytes 393224 | tf_op jit(solution)/shard_map/ppermute | solution.py:490
  59.5 8.5 %collective-permute-start.14 = (f32[256,128]{1,0:T(8,128)S(1)}, f32[256,128]{1,0:T(8,128)S(1)}, u32[]{:S(2)}, u32[]{:S(2)}) collective-permute-start(f32[256,128]{1,0:T(8,128)S(1)} %get-tuple-element.89), channel_id=1, source_target_pairs={{0,24},{8,0},{16,8},{24,16},{1,25},{9,1},{17,9},{25,17},{2,26},{10... | collective-permute-start | bytes 393224 | tf_op jit(solution)/shard_map/ppermute | solution.py:490
  65.4 22.7 %collective-permute-start.20 = (f32[256,128]{1,0:T(8,128)S(1)}, f32[256,128]{1,0:T(8,128)S(1)}, u32[]{:S(2)}, u32[]{:S(2)}) collective-permute-start(f32[256,128]{1,0:T(8,128)S(1)} %get-tuple-element.98), channel_id=1, source_target_pairs={{0,8},{8,16},{16,24},{24,0},{1,9},{9,17},{17,25},{25,1},{2,10},{10... | collective-permute-start | bytes 393224 | tf_op jit(solution)/shard_map/ppermute | solution.py:490
  68.5 9.8 %collective-permute-start.15 = (f32[168,128]{1,0:T(8,128)S(1)}, f32[168,128]{1,0:T(8,128)S(1)}, u32[]{:S(2)}, u32[]{:S(2)}) collective-permute-start(f32[168,128]{1,0:T(8,128)S(1)} %pad_maximum_fusion.6), channel_id=1, source_target_pairs={{8,0},{16,8},{24,16},{25,24},{17,25},{9,17},{1,9},{2,1},{10,2},{18... | collective-permute-start | bytes 258056 | tf_op jit(solution)/shard_map/ppermute | solution.py:509
  68.6 9.7 %collective-permute-start.16 = (f32[160,128]{1,0:T(8,128)S(1)}, f32[160,128]{1,0:T(8,128)S(1)}, u32[]{:S(2)}, u32[]{:S(2)}) collective-permute-start(f32[160,128]{1,0:T(8,128)S(1)} %pad_maximum_fusion.7), channel_id=1, source_target_pairs={{0,8},{8,16},{16,24},{24,25},{25,17},{17,9},{9,1},{1,2},{2,10},{10... | collective-permute-start | bytes 245768 | tf_op jit(solution)/shard_map/ppermute | solution.py:509
  74.0 17.0 %collective-permute-start.21 = (f32[256,128]{1,0:T(8,128)S(1)}, f32[256,128]{1,0:T(8,128)S(1)}, u32[]{:S(2)}, u32[]{:S(2)}) collective-permute-start(f32[256,128]{1,0:T(8,128)S(1)} %get-tuple-element.99), channel_id=1, source_target_pairs={{0,16},{8,24},{16,0},{24,8},{1,17},{9,25},{17,1},{25,9},{2,18},{10... | collective-permute-start | bytes 393224 | tf_op jit(solution)/shard_map/ppermute | solution.py:490
  75.4 15.5 %collective-permute-start.22 = (f32[256,128]{1,0:T(8,128)S(1)}, f32[256,128]{1,0:T(8,128)S(1)}, u32[]{:S(2)}, u32[]{:S(2)}) collective-permute-start(f32[256,128]{1,0:T(8,128)S(1)} %get-tuple-element.100), channel_id=1, source_target_pairs={{0,24},{8,0},{16,8},{24,16},{1,25},{9,1},{17,9},{25,17},{2,26},{10... | collective-permute-start | bytes 393224 | tf_op jit(solution)/shard_map/ppermute | solution.py:490
  78.3 12.6 %copy-start = (f32[2,16,64,128]{3,2,1,0:T(8,128)S(1)}, f32[2,16,64,128]{3,2,1,0:T(8,128)}, u32[]{:S(2)}) copy-start(f32[2,16,64,128]{3,2,1,0:T(8,128)} %gain.2) | copy-start | bytes 3145732
  78.4 12.6 %copy-start.1 = (s32[16,64,128]{2,1,0:T(8,128)S(1)}, s32[16,64,128]{2,1,0:T(8,128)}, u32[]{:S(2)}) copy-start(s32[16,64,128]{2,1,0:T(8,128)} %mask.5) | copy-start | bytes 1572868
  81.9 11.2 %collective-permute-start.17 = (f32[256,128]{1,0:T(8,128)S(1)}, f32[256,128]{1,0:T(8,128)S(1)}, u32[]{:S(2)}, u32[]{:S(2)}) collective-permute-start(f32[256,128]{1,0:T(8,128)S(1)} %get-tuple-element.95), channel_id=1, source_target_pairs={{0,8},{8,16},{16,24},{24,0},{1,9},{9,17},{17,25},{25,1},{2,10},{10... | collective-permute-start | bytes 393224 | tf_op jit(solution)/shard_map/ppermute | solution.py:490
  85.6 8.6 %collective-permute-start.18 = (f32[256,128]{1,0:T(8,128)S(1)}, f32[256,128]{1,0:T(8,128)S(1)}, u32[]{:S(2)}, u32[]{:S(2)}) collective-permute-start(f32[256,128]{1,0:T(8,128)S(1)} %get-tuple-element.96), channel_id=1, source_target_pairs={{0,16},{8,24},{16,0},{24,8},{1,17},{9,25},{17,1},{25,9},{2,18},{10... | collective-permute-start | bytes 393224 | tf_op jit(solution)/shard_map/ppermute | solution.py:490
  88.1 6.1 %collective-permute-start.19 = (f32[256,128]{1,0:T(8,128)S(1)}, f32[256,128]{1,0:T(8,128)S(1)}, u32[]{:S(2)}, u32[]{:S(2)}) collective-permute-start(f32[256,128]{1,0:T(8,128)S(1)} %get-tuple-element.97), channel_id=1, source_target_pairs={{0,24},{8,0},{16,8},{24,16},{1,25},{9,1},{17,9},{25,17},{2,26},{10... | collective-permute-start | bytes 393224 | tf_op jit(solution)/shard_map/ppermute | solution.py:490

commit v6 on v5

--- a/solution.py
+++ b/solution.py
@@ -137,46 +137,49 @@
     groups = len(starts)
     halos, outs = refs[masked:-4 - groups - 3 * masked], refs[-4 - groups - 3 * masked:-4 - 3 * masked]
     held, slots_held, sems, fetch_sems = refs[-4:]
-    if masked:
-        pairs = list(zip((along_i, along_j, refs[0]), refs[-7:-4]))
-        fetched = copies(pairs, fetch_sems)
-        along_i, along_j, sea = refs[-7:-4]
-        for copy in fetched[:2]:
-            copy.wait()
     group = lane_groups(rows, cols, groups)
     unroll = held.shape[0]
+    pieces = levels // unroll
+    if masked:
+        sources, (along_i, along_j, sea) = (along_i, along_j, refs[0]), refs[-7:-4]
+        fetched = []
+        for side, (source, target) in enumerate(zip(sources, (along_i, along_j, sea))):
+            pairs = [(source.at[pl.ds(k * unroll, unroll)], target.at[pl.ds(k * unroll, unroll)]) for k in range(pieces)]
+            fetched.append(copies(pairs, fetch_sems.at[side]))
+
+    def put(at, blocks):
+        for slot, block in enumerate(blocks):
+            slots_held[slot, pl.ds(at, block.shape[0]), :] = block
 
     for side, weight in enumerate((along_i, along_j)):
-
-        def some(outer, carry, side=side, weight=weight):
-            for halo, at in zip(halos, (0, STEPS + length)):
-                size = unroll * STEPS
-                block = halo[pl.ds(pl.multiple_of(side * levels * STEPS + outer * size, 8), size), :]
-                for k in range(unroll):
-                    held[k, pl.ds(at, STEPS), :] = block[k * STEPS:(k + 1) * STEPS]
+        for outer in range(pieces):
+            if masked:
+                fetched[side][outer].wait()
+            packed = []
             for k in range(unroll):
-                held[k, pl.ds(STEPS, length), :] = weight[outer * unroll + k]
-            packed = [
-                swap([held[k, pl.ds(start, rows), :] for start in starts], group, cols // groups)
-                for k in range(unroll)
-            ]
-            at = pl.multiple_of((side * levels + outer * unroll) * rows, 8)
-            for slot in range(groups):
-                block = jnp.concatenate([packed[k][slot] for k in range(unroll)], axis=0)
-                slots_held[slot, pl.ds(at, unroll * rows), :] = block
-            return carry
-
-        lax.fori_loop(0, levels // unroll, some, 0)
+                level = outer * unroll + k
+                if halos:
+                    for halo, at in zip(halos, (0, STEPS + length)):
+                        held[k, pl.ds(at, STEPS), :] = halo[pl.ds((side * levels + level) * STEPS, STEPS), :]
+                    held[k, pl.ds(STEPS, length), :] = weight[level]
+                    blocks = [held[k, pl.ds(start, rows), :] for start in starts]
+                else:
+                    blocks = [weight[level, pl.ds(start - STEPS, rows), :] for start in starts]
+                packed.append(swap(blocks, group, cols // groups))
+            put(
+                (side * levels + outer * unroll) * rows,
+                [jnp.concatenate([packed[k][slot] for k in range(unroll)], axis=0) for slot in range(groups)],
+            )
     if masked:
-        fetched[2].wait()
-        depth = sea[0]
-        for level in range(1, levels):
-            depth = depth + sea[level]
+        depth = jnp.zeros((length, cols), sea.dtype)
+        for outer in range(pieces):
+            fetched[2][outer].wait()
+            for level in range(outer * unroll, (outer + 1) * unroll):
+                depth = depth + sea[level]
         depth = depth.astype(jnp.float32)
         size = length // groups
         blocks = [depth[a * size:(a + 1) * size] for a in range(groups)]
-        for slot, block in enumerate(swap(blocks, lane_groups(size, cols, groups), cols // groups)):
-            slots_held[slot, pl.ds(2 * levels * rows, size), :] = block
+        put(2 * levels * rows, swap(blocks, lane_groups(size, cols, groups), cols // groups))
     slots = position()[0]
     for copy in copies([(slots_held.at[slots[d]], out) for d, out in enumerate(outs)], sems):
         copy.wait()
@@ -198,7 +201,7 @@
                 pltpu.VMEM((unroll, length + 2 * STEPS, cols), jnp.float32),
                 pltpu.VMEM((groups, *shape), jnp.float32),
                 pltpu.SemaphoreType.DMA((groups,)),
-                pltpu.SemaphoreType.DMA((3,)),
+                pltpu.SemaphoreType.DMA((3, levels // unroll)),
             ],
             compiler_params=params(VMEM_WHOLE if mask else VMEM_LIMIT),
             name="weight_messages",
@@ -415,29 +418,29 @@
 
 
 def result_kernel(runs, gain, mask, *refs):
-    parts, (out, held, done, sems, out_sems) = refs[:-5], refs[-5:]
+    parts, (out, done, out_sems) = refs[:-3], refs[-3:]
     fields, levels, _, cols = gain.shape
-    groups = held.shape[0]
+    groups = len(parts)
     rows = done.shape[2] // groups
     some = levels // RESULT_STEPS
     slots = position()[1]
-    fetched = copies([(parts[d], held.at[slots[d]]) for d in range(groups)], sems)
     group = lane_groups(rows, cols, groups)
-    for copy in fetched:
-        copy.wait()
+
+    def of_slot(slot, at):
+        x = parts[0][pl.ds(at, rows), :]
+        for d in range(1, groups):
+            x = jnp.where(slots[d] == slot, parts[d][pl.ds(at, rows), :], x)
+        return x
+
     stored = []
     for step in range(RESULT_STEPS):
-
-        def one(level, carry):
+        for level in range(step * some, (step + 1) * some):
             ocean = jnp.concatenate([mask[level, pl.ds(*run), :] for run in runs], axis=0).astype(jnp.float32)
             for field in range(fields):
-                at = pl.multiple_of((field * levels + level) * rows, rows)
-                blocks = swap([held[slot, pl.ds(at, rows), :] for slot in range(groups)], group, cols // groups)
+                at = (field * levels + level) * rows
+                blocks = swap([of_slot(slot, at) for slot in range(groups)], group, cols // groups)
                 gains = jnp.concatenate([gain[field, level, pl.ds(*run), :] for run in runs], axis=0)
                 done[field, level] = ocean * gains * jnp.concatenate(blocks, axis=0)
-            return carry
-
-        lax.fori_loop(step * some, (step + 1) * some, one, 0, unroll=True)
         these = pl.ds(step * some, some)
         pairs, at = [], 0
         for first, number in runs:
@@ -460,13 +463,11 @@
 
     return pl.pallas_call(
         kernel,
-        in_specs=[vmem()] * 2 + [anywhere] * (groups + len(more)),
+        in_specs=[vmem()] * (2 + groups) + [anywhere] * len(more),
         out_specs=anywhere,
         out_shape=jax.ShapeDtypeStruct(gain.shape, jnp.float32),
         scratch_shapes=[
-            pltpu.VMEM((groups, *parts[0].shape), jnp.float32),
             pltpu.VMEM((fields, levels, rows, cols), jnp.float32),
-            pltpu.SemaphoreType.DMA((groups,)),
             pltpu.SemaphoreType.DMA((RESULT_STEPS, len(runs))),
         ],
         input_output_aliases={2 + groups: 0} if more else {},
@@ -556,13 +557,16 @@
     forward = jnp.concatenate([by_device[:, t].reshape(2 * levels, order) for t in to], axis=0)
 
     scaled[1], outer_messages = lax.optimization_barrier((scaled[1], outer_messages))
-    early = shift(outer_messages[1], 1)
+    middle = devices // 2
+    early = shift(outer_messages[middle], middle)
     mixed = adjoint_mix(adjoint, depth, scaled, length, width)
     edges = flat(mixed[:, :STEPS]), flat(mixed[:, -STEPS:])
     edges, inner_weights = lax.optimization_barrier((edges, (here, left, right)))
     left, right = halo_j(*edges)
     left, right, outer_messages, early = lax.optimization_barrier((left, right, outer_messages, early))
-    outer_parts = [outer_messages[0], early] + [shift(outer_messages[d], d) for d in range(2, devices)]
+    outer_parts = [
+        early if d == middle else shift(outer_messages[d], d) if d else outer_messages[0] for d in range(devices)
+    ]
     field = [(list(range(length)), mixed, left, right)]
     weights = [(inner_rows, *inner_weights)]
     depths = [depth, right_depth]

time: 96.6 us -> 93.4 us (0.967)
  Pallas kernels: 23.1 us -> 21.6 us
  waiting for transfers between devices: 11.4 us -> 9.9 us
    ppermute x3, starting transfers between devices: 25.4 us -> 22.9 us  [halo_j(): lax.ppermute(last, ('lev', 'gy'), ahead)]
    ppermute x15, starting transfers between devices: 31.5 us -> 33.9 us  [shift(): lax.ppermute(x, 'lev', [(k, (k + d) % devices) for k in range(devices)])]
    ppermute x3, waiting for transfers between devices: 2.9 us -> 0.97 us  [halo_j(): lax.ppermute(last, ('lev', 'gy'), ahead)]
    pallas_call x2, Pallas kernels: 4.23 us -> 2.86 us  [result(): pl.pallas_call(kernel, in_specs=[vmem()] * (2 + groups) + [anywhere] * le...]
    ppermute x3, waiting for transfers between devices: 2.05 us -> 3.35 us  [halo_j(): lax.ppermute(first, ('lev', 'gy'), back)]
  transfers between devices with their start and end apart: 23 -> 23, of which waited for: 5 -> 6; matrix products, arithmetic and copies ran while one was open for 0% -> 0% of each run, Pallas kernels for 18% -> 18%
where the time goes in v6:
time: 93.4 us; the launch traced here: 93.2 us
  starting transfers between devices  59.9 us (64%)
  Pallas kernels  21.6 us (23%)
  waiting for transfers between devices  9.9 us (11%)
  local copies, waits for them, and re-layouts  1.24 us (1%)
    ppermute x15, starting transfers between devices, shift(): lax.ppermute(x, 'lev', [(k, (k + d) % devices) for k in range(devices)])  33.9 us
    ppermute x3, starting transfers between devices, halo_j(): lax.ppermute(last, ('lev', 'gy'), ahead)  22.9 us
    pallas_call x2, Pallas kernels, spread_mix(): pl.pallas_call(kernel, in_specs=[vmem()] * (1 + len(arrays)), out_specs=[...  6.91 us
    pallas_call x2, Pallas kernels, weight_messages(): pl.pallas_call(functools.partial(pack_kernel, starts, rows, len(mask)), i...  5.75 us
    ppermute x15, waiting for transfers between devices, shift(): lax.ppermute(x, 'lev', [(k, (k + d) % devices) for k in range(devices)])  5.57 us
    ppermute x3, waiting for transfers between devices, halo_j(): lax.ppermute(first, ('lev', 'gy'), back)  3.35 us
    pallas_call x1, Pallas kernels, scaled_messages(): pl.pallas_call(scaled_kernel, in_specs=[pl.BlockSpec(memory_space=pl.ANY)...  3.25 us
    ppermute x2, starting transfers between devices, halo_i(): both = lax.ppermute(jnp.concatenate([first, last], axis=0), 'gx', up)  3.11 us
  transfers between devices with their start and end apart: 23, of which 6 were waited for; matrix products, arithmetic and copies ran while one was open for 0% of the time, Pallas kernels for 18%

profile of v6, /device:TPU:0, one launch (start us, length us, event | category | flops | bytes accessed | tf_op | source)
XLA Modules:
  0.0 93.2 jit_solution(16874722421053624083)
XLA Ops:
  0.0 3.6 %weight_messages.2 = (f32[336,128]{1,0:T(8,128)}, f32[336,128]{1,0:T(8,128)}, f32[336,128]{1,0:T(8,128)}, f32[336,128]{1,0:T(8,128)}) custom-call(f32[16,64,128]{2,1,0:T(8,128)} %along_i.3, f32[16,64,128]{2,1,0:T(8,128)} %along_j.3, s32[16,64,128]{2,1,0:T(8,128)} %mask.5), custom_call_target="tpu_custom_call" | custom-call | tf_op jit(solution)/shard_map/weight_messages/pallas_call | solution.py:194
  3.6 3.1 %collective-permute-start = (f32[336,128]{1,0:T(8,128)}, f32[336,128]{1,0:T(8,128)S(1)}, u32[]{:S(2)}, u32[]{:S(2)}) collective-permute-start(f32[336,128]{1,0:T(8,128)} %get-tuple-element.54), channel_id=1, source_target_pairs={{0,8},{8,16},{16,24},{24,0},{1,9},{9,17},{17,25},{25,1},{2,10},{10... | collective-permute-start | bytes 516104 | tf_op jit(solution)/shard_map/ppermute | solution.py:491
  6.7 2.6 %collective-permute-start.1 = (f32[336,128]{1,0:T(8,128)}, f32[336,128]{1,0:T(8,128)S(1)}, u32[]{:S(2)}, u32[]{:S(2)}) collective-permute-start(f32[336,128]{1,0:T(8,128)} %get-tuple-element.55), channel_id=1, source_target_pairs={{0,16},{8,24},{16,0},{24,8},{1,17},{9,25},{17,1},{25,9},{2,18},{10... | collective-permute-start | bytes 516104 | tf_op jit(solution)/shard_map/ppermute | solution.py:491
  9.2 1.3 %collective-permute-start.2 = (f32[336,128]{1,0:T(8,128)}, f32[336,128]{1,0:T(8,128)S(1)}, u32[]{:S(2)}, u32[]{:S(2)}) collective-permute-start(f32[336,128]{1,0:T(8,128)} %get-tuple-element.56), channel_id=1, source_target_pairs={{0,24},{8,0},{16,8},{24,16},{1,25},{9,1},{17,9},{25,17},{2,26},{10... | collective-permute-start | bytes 516104 | tf_op jit(solution)/shard_map/ppermute | solution.py:491
  10.7 1.6 %collective-permute-start.5 = (f32[256,128]{1,0:T(8,128)S(1)}, f32[256,128]{1,0:T(8,128)S(1)}, u32[]{:S(2)}, u32[]{:S(2)}) collective-permute-start(f32[256,128]{1,0:T(8,128)S(1)} %pad_maximum_fusion.1), channel_id=1, source_target_pairs={{4,0},{0,4},{5,1},{1,5},{6,2},{2,6},{7,3},{3,7},{12,8},{8,12},{13,... | collective-permute-start | bytes 393224 | tf_op jit(solution)/shard_map/ppermute | solution.py:505
  12.2 3.3 %scaled_messages.1 = (f32[512,128]{1,0:T(8,128)}, f32[512,128]{1,0:T(8,128)}, f32[512,128]{1,0:T(8,128)}, f32[512,128]{1,0:T(8,128)}) custom-call(f32[2,16,64,128]{3,2,1,0:T(8,128)} %increment, f32[2,16,64,128]{3,2,1,0:T(8,128)} %gain.2, s32[16,64,128]{2,1,0:T(8,128)} %mask.5), custom_call_target="tpu_custom_call" | custom-call | tf_op jit(solution)/shard_map/scaled_messages/pallas_call | solution.py:117
  15.5 0.0 copy-start.6
  15.5 0.7 collective-permute-start.4
  16.2 0.1 copy-done.6
  16.4 0.0 copy-start.8
  16.4 0.1 copy.13.matrix
  16.5 0.0 collective-permute-done.5
  16.5 0.8 copy-done.8
  17.3 0.3 collective-permute-start.6
  17.7 2.2 %weight_messages.3 = (f32[256,128]{1,0:T(8,128)S(1)}, f32[256,128]{1,0:T(8,128)S(1)}, f32[256,128]{1,0:T(8,128)S(1)}, f32[256,128]{1,0:T(8,128)S(1)}) custom-call(f32[16,64,128]{2,1,0:T(8,128)S(1)} %copy-done.2, f32[16,64,128]{2,1,0:T(8,128)S(1)} %copy-done.3, f32[128,128]{1,0:T(8,128)S(1)} %get-tuple-element.65.refs_0_, ...), custom_call_target="tpu_custom_call" | custom-call | tf_op jit(solution)/shard_map/weight_messages/pallas_call | solution.py:194
  19.9 0.0 collective-permute-done.refs_2_
  19.9 2.8 %collective-permute-start.7 = (f32[512,128]{1,0:T(8,128)S(1)}, f32[512,128]{1,0:T(8,128)S(1)}, u32[]{:S(2)}, u32[]{:S(2)}) collective-permute-start(f32[512,128]{1,0:T(8,128)S(1)} %copy-done.7), channel_id=1, source_target_pairs={{0,24},{8,0},{16,8},{24,16},{1,25},{9,1},{17,9},{25,17},{2,26},{10... | collective-permute-start | bytes 786440 | tf_op jit(solution)/shard_map/ppermute | solution.py:491
  22.7 0.0 collective-permute-done.1.refs_3_
  22.7 0.0 collective-permute-done.2.refs_4_
  22.7 0.4 turn_weights.2.refs_5_.refs_10_
  23.1 0.0 copy-start.4
  23.2 13.6 %collective-permute-start.8 = (f32[160,128]{1,0:T(8,128)S(1)}, f32[160,128]{1,0:T(8,128)S(1)}, u32[]{:S(2)}, u32[]{:S(2)}) collective-permute-start(f32[160,128]{1,0:T(8,128)S(1)} %bitcast.47), channel_id=1, source_target_pairs={{0,8},{8,16},{16,24},{24,25},{25,17},{17,9},{9,1},{1,2},{2,10},{10... | collective-permute-start | bytes 245768 | tf_op jit(solution)/shard_map/ppermute | solution.py:510
  36.8 0.0 collective-permute-start.3
  36.8 0.0 collective-permute-done.4.refs_1_
  36.8 6.3 %collective-permute-start.11 = (f32[256,128]{1,0:T(8,128)S(1)}, f32[256,128]{1,0:T(8,128)S(1)}, u32[]{:S(2)}, u32[]{:S(2)}) collective-permute-start(f32[256,128]{1,0:T(8,128)S(1)} %get-tuple-element.76), channel_id=1, source_target_pairs={{0,16},{8,24},{16,0},{24,8},{1,17},{9,25},{17,1},{25,9},{2,18},{10... | collective-permute-start | bytes 393224 | tf_op jit(solution)/shard_map/ppermute | solution.py:491
  43.1 0.0 collective-permute-done.6.refs_2_
  43.1 0.0 collective-permute-done.7.refs_3_
  43.1 2.0 %adjoint_mix.1.refs_2_.refs_4_ = f32[64,32,128]{2,1,0:T(8,128)S(1)} custom-call(f32[128,128]{1,0:T(8,128)S(1)} %copy.13.matrix, f32[16,128]{1,0:T(8,128)S(1)} %slice_add_fusion.refs_0_.depths, f32[512,128]{1,0:T(8,128)S(1)} %copy-done.4, f32[512,128]{1,0:T(8,128)S(1)} %collective-permute-done.4.refs_1_, f32[512,128]{1,0:T(8,128)S(1)} %collective-permute-done.6.refs_2_, ...), custom_call_target="tpu_custom_call" | custom-call | tf_op jit(solution)/shard_map/adjoint_mix/pallas_call | solution.py:234
  45.2 0.0 collective-permute-done.3
  45.2 0.0 collective-permute-done.8.refs_6_.refs_11_
  45.2 7.3 %collective-permute-start.9 = (f32[256,128]{1,0:T(8,128)S(1)}, f32[256,128]{1,0:T(8,128)S(1)}, u32[]{:S(2)}, u32[]{:S(2)}) collective-permute-start(f32[256,128]{1,0:T(8,128)S(1)} %bitcast.42), channel_id=1, source_target_pairs={{0,8},{8,16},{16,24},{24,25},{25,17},{17,9},{9,1},{1,2},{2,10},{10... | collective-permute-start | bytes 393224 | tf_op jit(solution)/shard_map/ppermute | solution.py:510
  52.5 0.0 collective-permute-start.10
  52.5 1.9 %collective-permute-done.11.refs_4_ = f32[256,128]{1,0:T(8,128)S(1)} collective-permute-done((f32[256,128]{1,0:T(8,128)S(1)}, f32[256,128]{1,0:T(8,128)S(1)}, u32[]{:S(2)}, u32[]{:S(2)}) %collective-permute-start.11) | collective-permute-done | bytes 131104 | tf_op jit(solution)/shard_map/ppermute | solution.py:491
  54.4 1.0 %collective-permute-done.9.refs_3_.refs_5_ = f32[256,128]{1,0:T(8,128)S(1)} collective-permute-done((f32[256,128]{1,0:T(8,128)S(1)}, f32[256,128]{1,0:T(8,128)S(1)}, u32[]{:S(2)}, u32[]{:S(2)}) %collective-permute-start.9) | collective-permute-done | bytes 131104 | tf_op jit(solution)/shard_map/ppermute | solution.py:510
  55.4 2.1 %collective-permute-done.10.refs_4_.refs_6_ = f32[256,128]{1,0:T(8,128)S(1)} collective-permute-done((f32[256,128]{1,0:T(8,128)S(1)}, f32[256,128]{1,0:T(8,128)S(1)}, u32[]{:S(2)}, u32[]{:S(2)}) %collective-permute-start.10) | collective-permute-done | bytes 131104 | tf_op jit(solution)/shard_map/ppermute | solution.py:510
  57.4 1.6 %collective-permute-start.12 = (f32[264,128]{1,0:T(8,128)S(1)}, f32[264,128]{1,0:T(8,128)S(1)}, u32[]{:S(2)}, u32[]{:S(2)}) collective-permute-start(f32[264,128]{1,0:T(8,128)S(1)} %pad_maximum_fusion), channel_id=1, source_target_pairs={{4,0},{0,4},{5,1},{1,5},{6,2},{2,6},{7,3},{3,7},{12,8},{8,12},{13,... | collective-permute-start | bytes 405512 | tf_op jit(solution)/shard_map/ppermute | solution.py:505
  59.0 1.4 %collective-permute-start.13 = (f32[256,128]{1,0:T(8,128)S(1)}, f32[256,128]{1,0:T(8,128)S(1)}, u32[]{:S(2)}, u32[]{:S(2)}) collective-permute-start(f32[256,128]{1,0:T(8,128)S(1)} %get-tuple-element.87), channel_id=1, source_target_pairs={{0,8},{8,16},{16,24},{24,0},{1,9},{9,17},{17,25},{25,1},{2,10},{10... | collective-permute-start | bytes 393224 | tf_op jit(solution)/shard_map/ppermute | solution.py:491
  60.4 2.4 %collective-permute-start.14 = (f32[256,128]{1,0:T(8,128)S(1)}, f32[256,128]{1,0:T(8,128)S(1)}, u32[]{:S(2)}, u32[]{:S(2)}) collective-permute-start(f32[256,128]{1,0:T(8,128)S(1)} %get-tuple-element.89), channel_id=1, source_target_pairs={{0,24},{8,0},{16,8},{24,16},{1,25},{9,1},{17,9},{25,17},{2,26},{10... | collective-permute-start | bytes 393224 | tf_op jit(solution)/shard_map/ppermute | solution.py:491
  62.8 3.4 %spread_mix.2 = (f32[256,128]{1,0:T(8,128)S(1)}, f32[256,128]{1,0:T(8,128)S(1)}, f32[256,128]{1,0:T(8,128)S(1)}, f32[256,128]{1,0:T(8,128)S(1)}) custom-call(f32[128,128]{1,0:T(8,128)S(1)} %get-tuple-element.127.matrix, f32[16,128]{1,0:T(8,128)S(1)} %slice_add_fusion.refs_0_.depths, f32[16,128]{1,0:T(8,128)S(1)} %split.44.refs_1_, ...), custom_call_target="tpu_custom_call" | custom-call | tf_op jit(solution)/shard_map/spread_mix/pallas_call | solution.py:405
  66.2 0.1 collective-permute-start.20
  66.3 0.7 collective-permute-done.13.refs_3_
  67.0 0.0 collective-permute-done.14.refs_5_
  67.0 0.0 collective-permute-done.12
  67.1 0.4 turn_weights.3.refs_13_
  67.6 0.1 collective-permute-start.15
  67.7 2.0 %collective-permute-start.16 = (f32[160,128]{1,0:T(8,128)S(1)}, f32[160,128]{1,0:T(8,128)S(1)}, u32[]{:S(2)}, u32[]{:S(2)}) collective-permute-start(f32[160,128]{1,0:T(8,128)S(1)} %pad_maximum_fusion.7), channel_id=1, source_target_pairs={{0,8},{8,16},{16,24},{24,25},{25,17},{17,9},{9,1},{1,2},{2,10},{10... | collective-permute-start | bytes 245768 | tf_op jit(solution)/shard_map/ppermute | solution.py:510
  69.7 2.8 %collective-permute-start.21 = (f32[256,128]{1,0:T(8,128)S(1)}, f32[256,128]{1,0:T(8,128)S(1)}, u32[]{:S(2)}, u32[]{:S(2)}) collective-permute-start(f32[256,128]{1,0:T(8,128)S(1)} %get-tuple-element.99), channel_id=1, source_target_pairs={{0,16},{8,24},{16,0},{24,8},{1,17},{9,25},{17,1},{25,9},{2,18},{10... | collective-permute-start | bytes 393224 | tf_op jit(solution)/shard_map/ppermute | solution.py:491
  72.4 1.0 %collective-permute-start.22 = (f32[256,128]{1,0:T(8,128)S(1)}, f32[256,128]{1,0:T(8,128)S(1)}, u32[]{:S(2)}, u32[]{:S(2)}) collective-permute-start(f32[256,128]{1,0:T(8,128)S(1)} %get-tuple-element.100), channel_id=1, source_target_pairs={{0,24},{8,0},{16,8},{24,16},{1,25},{9,1},{17,9},{25,17},{2,26},{10... | collective-permute-start | bytes 393224 | tf_op jit(solution)/shard_map/ppermute | solution.py:491
  73.4 0.0 collective-permute-done.16
  73.4 1.3 %collective-permute-done.15 = f32[168,128]{1,0:T(8,128)S(1)} collective-permute-done((f32[168,128]{1,0:T(8,128)S(1)}, f32[168,128]{1,0:T(8,128)S(1)}, u32[]{:S(2)}, u32[]{:S(2)}) %collective-permute-start.15) | collective-permute-done | bytes 86048 | tf_op jit(solution)/shard_map/ppermute | solution.py:510
  74.7 0.0 copy-start
  74.7 0.0 copy-start.1
  74.7 3.5 %spread_mix.3 = (f32[256,128]{1,0:T(8,128)S(1)}, f32[256,128]{1,0:T(8,128)S(1)}, f32[256,128]{1,0:T(8,128)S(1)}, f32[256,128]{1,0:T(8,128)S(1)}) custom-call(f32[128,128]{1,0:T(8,128)S(1)} %get-tuple-element.127.matrix, f32[16,128]{1,0:T(8,128)S(1)} %slice_add_fusion.refs_0_.depths, f32[16,128]{1,0:T(8,128)S(1)} %split.44.refs_1_, ...), custom_call_target="tpu_custom_call" | custom-call | tf_op jit(solution)/shard_map/spread_mix/pallas_call | solution.py:405
  78.3 4.3 %collective-permute-start.17 = (f32[256,128]{1,0:T(8,128)S(1)}, f32[256,128]{1,0:T(8,128)S(1)}, u32[]{:S(2)}, u32[]{:S(2)}) collective-permute-start(f32[256,128]{1,0:T(8,128)S(1)} %get-tuple-element.95), channel_id=1, source_target_pairs={{0,8},{8,16},{16,24},{24,0},{1,9},{9,17},{17,25},{25,1},{2,10},{10... | collective-permute-start | bytes 393224 | tf_op jit(solution)/shard_map/ppermute | solution.py:491
  82.6 2.0 %collective-permute-start.18 = (f32[256,128]{1,0:T(8,128)S(1)}, f32[256,128]{1,0:T(8,128)S(1)}, u32[]{:S(2)}, u32[]{:S(2)}) collective-permute-start(f32[256,128]{1,0:T(8,128)S(1)} %get-tuple-element.96), channel_id=1, source_target_pairs={{0,16},{8,24},{16,0},{24,8},{1,17},{9,25},{17,1},{25,9},{2,18},{10... | collective-permute-start | bytes 393224 | tf_op jit(solution)/shard_map/ppermute | solution.py:491
  84.6 0.0 collective-permute-done.20.refs_1_
  84.6 2.8 %collective-permute-start.19 = (f32[256,128]{1,0:T(8,128)S(1)}, f32[256,128]{1,0:T(8,128)S(1)}, u32[]{:S(2)}, u32[]{:S(2)}) collective-permute-start(f32[256,128]{1,0:T(8,128)S(1)} %get-tuple-element.97), channel_id=1, source_target_pairs={{0,24},{8,0},{16,8},{24,16},{1,25},{9,1},{17,9},{25,17},{2,26},{10... | collective-permute-start | bytes 393224 | tf_op jit(solution)/shard_map/ppermute | solution.py:491
  87.4 0.0 collective-permute-done.21.refs_2_
  87.4 0.0 collective-permute-done.22.refs_3_
  87.4 1.4 %result.2.refs_4_ = f32[2,16,64,128]{3,2,1,0:T(8,128)} custom-call(f32[2,16,64,128]{3,2,1,0:T(8,128)S(1)} %copy-done, s32[16,64,128]{2,1,0:T(8,128)S(1)} %copy-done.1, f32[256,128]{1,0:T(8,128)S(1)} %get-tuple-element.85.refs_0_, f32[256,128]{1,0:T(8,128)S(1)} %collective-permute-done.20.refs_1_, f32[256,128]{1,0:T(8,128)S(1)} %collective-permute-done.21.refs_2_, ...), custom_call_target="tpu_custom_call" | custom-call | tf_op jit(solution)/shard_map/result/pallas_call | solution.py:464
  88.9 0.0 collective-permute-done.17.refs_1_
  88.9 2.8 %collective-permute-done.18.refs_2_ = f32[256,128]{1,0:T(8,128)S(1)} collective-permute-done((f32[256,128]{1,0:T(8,128)S(1)}, f32[256,128]{1,0:T(8,128)S(1)}, u32[]{:S(2)}, u32[]{:S(2)}) %collective-permute-start.18) | collective-permute-done | bytes 131104 | tf_op jit(solution)/shard_map/ppermute | solution.py:491
  91.7 0.0 collective-permute-done.19.refs_3_
  91.7 1.4 %result.3 = f32[2,16,64,128]{3,2,1,0:T(8,128)} custom-call(f32[2,16,64,128]{3,2,1,0:T(8,128)S(1)} %copy-done, s32[16,64,128]{2,1,0:T(8,128)S(1)} %copy-done.1, f32[256,128]{1,0:T(8,128)S(1)} %get-tuple-element.94.refs_0_, f32[256,128]{1,0:T(8,128)S(1)} %collective-permute-done.17.refs_1_, ...), custom_call_target="tpu_custom_call", output_to_operand_aliasing={{}: (6, {})} | custom-call | tf_op jit(solution)/shard_map/result/pallas_call | solution.py:464
  (39 shorter events, 0.3 us)
Async XLA Ops:
  0.0 10.6 %copy-start.3 = (f32[16,64,128]{2,1,0:T(8,128)S(1)}, f32[16,64,128]{2,1,0:T(8,128)}, u32[]{:S(2)}) copy-start(f32[16,64,128]{2,1,0:T(8,128)} %along_j.3) | copy-start | bytes 1572868
  0.0 10.6 %copy-start.2 = (f32[16,64,128]{2,1,0:T(8,128)S(1)}, f32[16,64,128]{2,1,0:T(8,128)}, u32[]{:S(2)}) copy-start(f32[16,64,128]{2,1,0:T(8,128)} %along_i.3) | copy-start | bytes 1572868
  3.6 16.3 %collective-permute-start = (f32[336,128]{1,0:T(8,128)}, f32[336,128]{1,0:T(8,128)S(1)}, u32[]{:S(2)}, u32[]{:S(2)}) collective-permute-start(f32[336,128]{1,0:T(8,128)} %get-tuple-element.54), channel_id=1, source_target_pairs={{0,8},{8,16},{16,24},{24,0},{1,9},{9,17},{17,25},{25,1},{2,10},{10... | collective-permute-start | bytes 516104 | tf_op jit(solution)/shard_map/ppermute | solution.py:491
  6.7 16.0 %collective-permute-start.1 = (f32[336,128]{1,0:T(8,128)}, f32[336,128]{1,0:T(8,128)S(1)}, u32[]{:S(2)}, u32[]{:S(2)}) collective-permute-start(f32[336,128]{1,0:T(8,128)} %get-tuple-element.55), channel_id=1, source_target_pairs={{0,16},{8,24},{16,0},{24,8},{1,17},{9,25},{17,1},{25,9},{2,18},{10... | collective-permute-start | bytes 516104 | tf_op jit(solution)/shard_map/ppermute | solution.py:491
  9.2 13.4 %collective-permute-start.2 = (f32[336,128]{1,0:T(8,128)}, f32[336,128]{1,0:T(8,128)S(1)}, u32[]{:S(2)}, u32[]{:S(2)}) collective-permute-start(f32[336,128]{1,0:T(8,128)} %get-tuple-element.56), channel_id=1, source_target_pairs={{0,24},{8,0},{16,8},{24,16},{1,25},{9,1},{17,9},{25,17},{2,26},{10... | collective-permute-start | bytes 516104 | tf_op jit(solution)/shard_map/ppermute | solution.py:491
  10.7 5.9 %collective-permute-start.5 = (f32[256,128]{1,0:T(8,128)S(1)}, f32[256,128]{1,0:T(8,128)S(1)}, u32[]{:S(2)}, u32[]{:S(2)}) collective-permute-start(f32[256,128]{1,0:T(8,128)S(1)} %pad_maximum_fusion.1), channel_id=1, source_target_pairs={{4,0},{0,4},{5,1},{1,5},{6,2},{2,6},{7,3},{3,7},{12,8},{8,12},{13,... | collective-permute-start | bytes 393224 | tf_op jit(solution)/shard_map/ppermute | solution.py:505
  15.5 0.8 copy-start.6
  15.5 21.3 %collective-permute-start.4 = (f32[512,128]{1,0:T(8,128)}, f32[512,128]{1,0:T(8,128)S(1)}, u32[]{:S(2)}, u32[]{:S(2)}) collective-permute-start(f32[512,128]{1,0:T(8,128)} %get-tuple-element.60), channel_id=1, source_target_pairs={{0,8},{8,16},{16,24},{24,0},{1,9},{9,17},{17,25},{25,1},{2,10},{10... | collective-permute-start | bytes 786440 | tf_op jit(solution)/shard_map/ppermute | solution.py:491
  16.4 1.0 %copy-start.8 = (f32[512,128]{1,0:T(8,128)S(1)}, f32[512,128]{1,0:T(8,128)}, u32[]{:S(2)}) copy-start(f32[512,128]{1,0:T(8,128)} %get-tuple-element.61) | copy-start | bytes 786436
  17.3 25.8 %collective-permute-start.6 = (f32[512,128]{1,0:T(8,128)S(1)}, f32[512,128]{1,0:T(8,128)S(1)}, u32[]{:S(2)}, u32[]{:S(2)}) collective-permute-start(f32[512,128]{1,0:T(8,128)S(1)} %copy-done.8), channel_id=1, source_target_pairs={{0,16},{8,24},{16,0},{24,8},{1,17},{9,25},{17,1},{25,9},{2,18},{10... | collective-permute-start | bytes 786440 | tf_op jit(solution)/shard_map/ppermute | solution.py:491
  17.7 2.2 %copy-start.7 = (f32[512,128]{1,0:T(8,128)S(1)}, f32[512,128]{1,0:T(8,128)}, u32[]{:S(2)}) copy-start(f32[512,128]{1,0:T(8,128)} %get-tuple-element.62) | copy-start | bytes 786436
  17.7 5.0 %copy-start.5 = (f32[336,128]{1,0:T(8,128)S(1)}, f32[336,128]{1,0:T(8,128)}, u32[]{:S(2)}) copy-start(f32[336,128]{1,0:T(8,128)} %get-tuple-element.53.refs_1_) | copy-start | bytes 516100
  19.9 23.2 %collective-permute-start.7 = (f32[512,128]{1,0:T(8,128)S(1)}, f32[512,128]{1,0:T(8,128)S(1)}, u32[]{:S(2)}, u32[]{:S(2)}) collective-permute-start(f32[512,128]{1,0:T(8,128)S(1)} %copy-done.7), channel_id=1, source_target_pairs={{0,24},{8,0},{16,8},{24,16},{1,25},{9,1},{17,9},{25,17},{2,26},{10... | collective-permute-start | bytes 786440 | tf_op jit(solution)/shard_map/ppermute | solution.py:491
  23.1 20.0 %copy-start.4 = (f32[512,128]{1,0:T(8,128)S(1)}, f32[512,128]{1,0:T(8,128)}, u32[]{:S(2)}) copy-start(f32[512,128]{1,0:T(8,128)} %get-tuple-element.59.refs_0_) | copy-start | bytes 786436
  23.2 22.0 %collective-permute-start.8 = (f32[160,128]{1,0:T(8,128)S(1)}, f32[160,128]{1,0:T(8,128)S(1)}, u32[]{:S(2)}, u32[]{:S(2)}) collective-permute-start(f32[160,128]{1,0:T(8,128)S(1)} %bitcast.47), channel_id=1, source_target_pairs={{0,8},{8,16},{16,24},{24,25},{25,17},{17,9},{9,1},{1,2},{2,10},{10... | collective-permute-start | bytes 245768 | tf_op jit(solution)/shard_map/ppermute | solution.py:510
  36.8 8.4 %collective-permute-start.3 = (f32[176,128]{1,0:T(8,128)S(1)}, f32[176,128]{1,0:T(8,128)S(1)}, u32[]{:S(2)}, u32[]{:S(2)}) collective-permute-start(f32[176,128]{1,0:T(8,128)S(1)} %pad_maximum_fusion.3), channel_id=1, source_target_pairs={{8,0},{16,8},{24,16},{25,24},{17,25},{9,17},{1,9},{2,1},{10,2},{18... | collective-permute-start | bytes 270344 | tf_op jit(solution)/shard_map/ppermute | solution.py:510
  36.8 17.6 %collective-permute-start.11 = (f32[256,128]{1,0:T(8,128)S(1)}, f32[256,128]{1,0:T(8,128)S(1)}, u32[]{:S(2)}, u32[]{:S(2)}) collective-permute-start(f32[256,128]{1,0:T(8,128)S(1)} %get-tuple-element.76), channel_id=1, source_target_pairs={{0,16},{8,24},{16,0},{24,8},{1,17},{9,25},{17,1},{25,9},{2,18},{10... | collective-permute-start | bytes 393224 | tf_op jit(solution)/shard_map/ppermute | solution.py:491
  45.2 10.2 %collective-permute-start.9 = (f32[256,128]{1,0:T(8,128)S(1)}, f32[256,128]{1,0:T(8,128)S(1)}, u32[]{:S(2)}, u32[]{:S(2)}) collective-permute-start(f32[256,128]{1,0:T(8,128)S(1)} %bitcast.42), channel_id=1, source_target_pairs={{0,8},{8,16},{16,24},{24,25},{25,17},{17,9},{9,1},{1,2},{2,10},{10... | collective-permute-start | bytes 393224 | tf_op jit(solution)/shard_map/ppermute | solution.py:510
  52.5 5.0 %collective-permute-start.10 = (f32[256,128]{1,0:T(8,128)S(1)}, f32[256,128]{1,0:T(8,128)S(1)}, u32[]{:S(2)}, u32[]{:S(2)}) collective-permute-start(f32[256,128]{1,0:T(8,128)S(1)} %bitcast.41), channel_id=1, source_target_pairs={{8,0},{16,8},{24,16},{25,24},{17,25},{9,17},{1,9},{2,1},{10,2},{18... | collective-permute-start | bytes 393224 | tf_op jit(solution)/shard_map/ppermute | solution.py:510
  57.4 9.6 %collective-permute-start.12 = (f32[264,128]{1,0:T(8,128)S(1)}, f32[264,128]{1,0:T(8,128)S(1)}, u32[]{:S(2)}, u32[]{:S(2)}) collective-permute-start(f32[264,128]{1,0:T(8,128)S(1)} %pad_maximum_fusion), channel_id=1, source_target_pairs={{4,0},{0,4},{5,1},{1,5},{6,2},{2,6},{7,3},{3,7},{12,8},{8,12},{13,... | collective-permute-start | bytes 405512 | tf_op jit(solution)/shard_map/ppermute | solution.py:505
  59.0 8.0 %collective-permute-start.13 = (f32[256,128]{1,0:T(8,128)S(1)}, f32[256,128]{1,0:T(8,128)S(1)}, u32[]{:S(2)}, u32[]{:S(2)}) collective-permute-start(f32[256,128]{1,0:T(8,128)S(1)} %get-tuple-element.87), channel_id=1, source_target_pairs={{0,8},{8,16},{16,24},{24,0},{1,9},{9,17},{17,25},{25,1},{2,10},{10... | collective-permute-start | bytes 393224 | tf_op jit(solution)/shard_map/ppermute | solution.py:491
  60.4 6.6 %collective-permute-start.14 = (f32[256,128]{1,0:T(8,128)S(1)}, f32[256,128]{1,0:T(8,128)S(1)}, u32[]{:S(2)}, u32[]{:S(2)}) collective-permute-start(f32[256,128]{1,0:T(8,128)S(1)} %get-tuple-element.89), channel_id=1, source_target_pairs={{0,24},{8,0},{16,8},{24,16},{1,25},{9,1},{17,9},{25,17},{2,26},{10... | collective-permute-start | bytes 393224 | tf_op jit(solution)/shard_map/ppermute | solution.py:491
  66.2 18.4 %collective-permute-start.20 = (f32[256,128]{1,0:T(8,128)S(1)}, f32[256,128]{1,0:T(8,128)S(1)}, u32[]{:S(2)}, u32[]{:S(2)}) collective-permute-start(f32[256,128]{1,0:T(8,128)S(1)} %get-tuple-element.98), channel_id=1, source_target_pairs={{0,8},{8,16},{16,24},{24,0},{1,9},{9,17},{17,25},{25,1},{2,10},{10... | collective-permute-start | bytes 393224 | tf_op jit(solution)/shard_map/ppermute | solution.py:491
  67.6 7.1 %collective-permute-start.15 = (f32[168,128]{1,0:T(8,128)S(1)}, f32[168,128]{1,0:T(8,128)S(1)}, u32[]{:S(2)}, u32[]{:S(2)}) collective-permute-start(f32[168,128]{1,0:T(8,128)S(1)} %pad_maximum_fusion.6), channel_id=1, source_target_pairs={{8,0},{16,8},{24,16},{25,24},{17,25},{9,17},{1,9},{2,1},{10,2},{18... | collective-permute-start | bytes 258056 | tf_op jit(solution)/shard_map/ppermute | solution.py:510
  67.7 5.7 %collective-permute-start.16 = (f32[160,128]{1,0:T(8,128)S(1)}, f32[160,128]{1,0:T(8,128)S(1)}, u32[]{:S(2)}, u32[]{:S(2)}) collective-permute-start(f32[160,128]{1,0:T(8,128)S(1)} %pad_maximum_fusion.7), channel_id=1, source_target_pairs={{0,8},{8,16},{16,24},{24,25},{25,17},{17,9},{9,1},{1,2},{2,10},{10... | collective-permute-start | bytes 245768 | tf_op jit(solution)/shard_map/ppermute | solution.py:510
  69.7 17.8 %collective-permute-start.21 = (f32[256,128]{1,0:T(8,128)S(1)}, f32[256,128]{1,0:T(8,128)S(1)}, u32[]{:S(2)}, u32[]{:S(2)}) collective-permute-start(f32[256,128]{1,0:T(8,128)S(1)} %get-tuple-element.99), channel_id=1, source_target_pairs={{0,16},{8,24},{16,0},{24,8},{1,17},{9,25},{17,1},{25,9},{2,18},{10... | collective-permute-start | bytes 393224 | tf_op jit(solution)/shard_map/ppermute | solution.py:491
  72.4 15.0 %collective-permute-start.22 = (f32[256,128]{1,0:T(8,128)S(1)}, f32[256,128]{1,0:T(8,128)S(1)}, u32[]{:S(2)}, u32[]{:S(2)}) collective-permute-start(f32[256,128]{1,0:T(8,128)S(1)} %get-tuple-element.100), channel_id=1, source_target_pairs={{0,24},{8,0},{16,8},{24,16},{1,25},{9,1},{17,9},{25,17},{2,26},{10... | collective-permute-start | bytes 393224 | tf_op jit(solution)/shard_map/ppermute | solution.py:491
  74.7 12.7 %copy-start = (f32[2,16,64,128]{3,2,1,0:T(8,128)S(1)}, f32[2,16,64,128]{3,2,1,0:T(8,128)}, u32[]{:S(2)}) copy-start(f32[2,16,64,128]{3,2,1,0:T(8,128)} %gain.2) | copy-start | bytes 3145732
  74.7 12.7 %copy-start.1 = (s32[16,64,128]{2,1,0:T(8,128)S(1)}, s32[16,64,128]{2,1,0:T(8,128)}, u32[]{:S(2)}) copy-start(s32[16,64,128]{2,1,0:T(8,128)} %mask.5) | copy-start | bytes 1572868
  78.3 10.6 %collective-permute-start.17 = (f32[256,128]{1,0:T(8,128)S(1)}, f32[256,128]{1,0:T(8,128)S(1)}, u32[]{:S(2)}, u32[]{:S(2)}) collective-permute-start(f32[256,128]{1,0:T(8,128)S(1)} %get-tuple-element.95), channel_id=1, source_target_pairs={{0,8},{8,16},{16,24},{24,0},{1,9},{9,17},{17,25},{25,1},{2,10},{10... | collective-permute-start | bytes 393224 | tf_op jit(solution)/shard_map/ppermute | solution.py:491
  82.6 9.1 %collective-permute-start.18 = (f32[256,128]{1,0:T(8,128)S(1)}, f32[256,128]{1,0:T(8,128)S(1)}, u32[]{:S(2)}, u32[]{:S(2)}) collective-permute-start(f32[256,128]{1,0:T(8,128)S(1)} %get-tuple-element.96), channel_id=1, source_target_pairs={{0,16},{8,24},{16,0},{24,8},{1,17},{9,25},{17,1},{25,9},{2,18},{10... | collective-permute-start | bytes 393224 | tf_op jit(solution)/shard_map/ppermute | solution.py:491
  84.6 7.1 %collective-permute-start.19 = (f32[256,128]{1,0:T(8,128)S(1)}, f32[256,128]{1,0:T(8,128)S(1)}, u32[]{:S(2)}, u32[]{:S(2)}) collective-permute-start(f32[256,128]{1,0:T(8,128)S(1)} %get-tuple-element.97), channel_id=1, source_target_pairs={{0,24},{8,0},{16,8},{24,16},{1,25},{9,1},{17,9},{25,17},{2,26},{10... | collective-permute-start | bytes 393224 | tf_op jit(solution)/shard_map/ppermute | solution.py:491

commit v7 on v6

--- a/solution.py
+++ b/solution.py
@@ -27,6 +27,10 @@
     return pl.BlockSpec(memory_space=pltpu.VMEM)
 
 
+def distances(devices):
+    return [0, devices // 2] + [d for d in range(1, devices) if d != devices // 2]
+
+
 def position():
     devices = lax.axis_size("lev")
     me = lax.axis_index("lev")
@@ -35,8 +39,8 @@
     def slot(lev):
         return jnp.where(flipped, devices - 1 - lev, lev)
 
-    to = [lax.rem(me + d, devices) for d in range(devices)]
-    source = [lax.rem(me + devices - d, devices) for d in range(devices)]
+    to = [lax.rem(me + d, devices) for d in distances(devices)]
+    source = [lax.rem(me + devices - d, devices) for d in distances(devices)]
     return [slot(lev) for lev in to], [slot(lev) for lev in source], source
 
 
@@ -91,21 +95,22 @@
             )
         )
 
+    depth = jnp.zeros((length, cols), jnp.float32)
+
+    def put(at, x):
+        blocks = swap([x[a * rows:(a + 1) * rows] for a in range(groups)], group, cols // groups)
+        for slot, block in enumerate(blocks):
+            held[slot, pl.ds(at, rows), :] = block
+
     for step in range(SCALED_STEPS):
         for copy in fetched[step]:
             copy.wait()
-
-        def one(level, carry):
+        for level in range(step * some, (step + 1) * some):
             ocean = sea[level].astype(jnp.float32)
+            depth = depth + ocean
             for field in range(fields):
-                at = pl.multiple_of((field * levels + level) * rows, rows)
-                x = ocean * gn[field, level] * inc[field, level]
-                blocks = swap([x[a * rows:(a + 1) * rows] for a in range(groups)], group, cols // groups)
-                for slot, block in enumerate(blocks):
-                    held[slot, pl.ds(at, rows), :] = block
-            return carry
-
-        lax.fori_loop(step * some, (step + 1) * some, one, 0, unroll=True)
+                put((field * levels + level) * rows, ocean * gn[field, level] * inc[field, level])
+    put(fields * levels * rows, depth)
     slots = position()[0]
     for copy in copies([(held.at[slots[d]], out) for d, out in enumerate(outs)], out_sems):
         copy.wait()
@@ -113,7 +118,7 @@
 
 def scaled_messages(increment, gain, mask, groups):
     fields, levels, length, cols = increment.shape
-    shape = (fields * levels * length // groups, cols)
+    shape = ((fields * levels + 1) * length // groups, cols)
     return pl.pallas_call(
         scaled_kernel,
         in_specs=[pl.BlockSpec(memory_space=pl.ANY)] * 3,
@@ -132,29 +137,15 @@
     )(increment, gain, mask)
 
 
-def pack_kernel(starts, rows, masked, along_i, along_j, *refs):
+def pack_kernel(starts, along_i, along_j, *refs):
     levels, length, cols = along_i.shape
     groups = len(starts)
-    halos, outs = refs[masked:-4 - groups - 3 * masked], refs[-4 - groups - 3 * masked:-4 - 3 * masked]
-    held, slots_held, sems, fetch_sems = refs[-4:]
+    halos, outs, (held, slots_held, sems) = refs[:-3 - groups], refs[-3 - groups:-3], refs[-3:]
+    rows = outs[0].shape[0] // (2 * levels)
     group = lane_groups(rows, cols, groups)
     unroll = held.shape[0]
-    pieces = levels // unroll
-    if masked:
-        sources, (along_i, along_j, sea) = (along_i, along_j, refs[0]), refs[-7:-4]
-        fetched = []
-        for side, (source, target) in enumerate(zip(sources, (along_i, along_j, sea))):
-            pairs = [(source.at[pl.ds(k * unroll, unroll)], target.at[pl.ds(k * unroll, unroll)]) for k in range(pieces)]
-            fetched.append(copies(pairs, fetch_sems.at[side]))
-
-    def put(at, blocks):
-        for slot, block in enumerate(blocks):
-            slots_held[slot, pl.ds(at, block.shape[0]), :] = block
-
     for side, weight in enumerate((along_i, along_j)):
-        for outer in range(pieces):
-            if masked:
-                fetched[side][outer].wait()
+        for outer in range(levels // unroll):
             packed = []
             for k in range(unroll):
                 level = outer * unroll + k
@@ -166,56 +157,45 @@
                 else:
                     blocks = [weight[level, pl.ds(start - STEPS, rows), :] for start in starts]
                 packed.append(swap(blocks, group, cols // groups))
-            put(
-                (side * levels + outer * unroll) * rows,
-                [jnp.concatenate([packed[k][slot] for k in range(unroll)], axis=0) for slot in range(groups)],
-            )
-    if masked:
-        depth = jnp.zeros((length, cols), sea.dtype)
-        for outer in range(pieces):
-            fetched[2][outer].wait()
-            for level in range(outer * unroll, (outer + 1) * unroll):
-                depth = depth + sea[level]
-        depth = depth.astype(jnp.float32)
-        size = length // groups
-        blocks = [depth[a * size:(a + 1) * size] for a in range(groups)]
-        put(2 * levels * rows, swap(blocks, lane_groups(size, cols, groups), cols // groups))
+            at = (side * levels + outer * unroll) * rows
+            for slot in range(groups):
+                block = jnp.concatenate([packed[k][slot] for k in range(unroll)], axis=0)
+                slots_held[slot, pl.ds(at, unroll * rows), :] = block
     slots = position()[0]
     for copy in copies([(slots_held.at[slots[d]], out) for d, out in enumerate(outs)], sems):
         copy.wait()
 
 
-def weight_messages(starts, rows, along_i, along_j, mask=(), halos=()):
+def weight_messages(starts, rows, along_i, along_j, halos=()):
     levels, length, cols = along_i.shape
     groups = len(starts)
-    shape = (2 * levels * rows + len(mask) * length // groups, cols)
+    shape = (2 * levels * rows, cols)
     unroll = 4
     return list(
         pl.pallas_call(
-            functools.partial(pack_kernel, starts, rows, len(mask)),
-            in_specs=[pl.BlockSpec(memory_space=pl.ANY) if mask else vmem()] * (2 + len(mask) + len(halos)),
+            functools.partial(pack_kernel, starts),
+            in_specs=[vmem()] * (2 + len(halos)),
             out_specs=[pl.BlockSpec(memory_space=pl.ANY)] * groups,
             out_shape=[jax.ShapeDtypeStruct(shape, jnp.float32)] * groups,
-            scratch_shapes=[pltpu.VMEM(x.shape, x.dtype) for x in ([along_i, along_j, *mask] if mask else [])]
-            + [
+            scratch_shapes=[
                 pltpu.VMEM((unroll, length + 2 * STEPS, cols), jnp.float32),
                 pltpu.VMEM((groups, *shape), jnp.float32),
                 pltpu.SemaphoreType.DMA((groups,)),
-                pltpu.SemaphoreType.DMA((3, levels // unroll)),
             ],
-            compiler_params=params(VMEM_WHOLE if mask else VMEM_LIMIT),
+            compiler_params=params(),
             name="weight_messages",
-        )(along_i, along_j, *mask, *halos)
-    )
-
-
-def adjoint_kernel(matrix, depths, *refs):
-    parts, out = refs[:-1], refs[-1]
+        )(along_i, along_j, *halos)
+    )
+
+
+def adjoint_kernel(matrix, *refs):
+    parts, out, depths = refs[:-2], refs[-2], refs[-1]
     length, width, order = out.shape
     groups = len(parts)
     rows = length // groups
     cols = groups * width
     count = order // groups
+    depths[...] = sum(part[pl.ds(count * rows, rows), :] for part in parts)
     level = lax.rem(lax.broadcasted_iota(jnp.int32, (order, cols), 0), order // 2).astype(jnp.float32)
 
     def one(i, carry):
@@ -230,15 +210,18 @@
     lax.fori_loop(0, rows, one, 0, unroll=4)
 
 
-def adjoint_mix(matrix, depths, parts, length, width):
+def adjoint_mix(matrix, parts, length, width):
     return pl.pallas_call(
         adjoint_kernel,
-        in_specs=[vmem()] * (2 + len(parts)),
-        out_specs=vmem(),
-        out_shape=jax.ShapeDtypeStruct((length, width, matrix.shape[0]), jnp.float32),
+        in_specs=[vmem()] * (1 + len(parts)),
+        out_specs=[vmem()] * 2,
+        out_shape=[
+            jax.ShapeDtypeStruct((length, width, matrix.shape[0]), jnp.float32),
+            jax.ShapeDtypeStruct((length // len(parts), width * len(parts)), jnp.float32),
+        ],
         compiler_params=params(),
         name="adjoint_mix",
-    )(matrix, depths, *parts)
+    )(matrix, *parts)
 
 
 def unfold(main, halo, groups):
@@ -484,14 +467,14 @@
     width = cols // devices
     rows = length // devices
     order = coupling.shape[0]
-    to = [lax.rem(lax.axis_index("lev") + d, devices) for d in range(devices)]
-    source = [lax.rem(lax.axis_index("lev") + devices - d, devices) for d in range(devices)]
+    to = [lax.rem(lax.axis_index("lev") + d, devices) for d in distances(devices)]
+    source = [lax.rem(lax.axis_index("lev") + devices - d, devices) for d in distances(devices)]
 
     def shift(x, d):
         return lax.ppermute(x, "lev", [(k, (k + d) % devices) for k in range(devices)])
 
     def exchange(parts):
-        return [parts[0]] + [shift(parts[d], d) for d in range(1, devices)]
+        return [parts[0]] + [shift(x, d) for x, d in zip(parts[1:], distances(devices)[1:])]
 
     up = [((k + 1) % gx_size, k) for k in range(gx_size)]
     down = [(b, a) for a, b in up]
@@ -526,52 +509,43 @@
     outer_starts = [a * some for a in range(half)] + [3 * quarter + 2 * STEPS + a * some for a in range(half)]
     windows = [list(range(-STEPS, quarter + STEPS)), list(range(3 * quarter - STEPS, length + STEPS))]
 
+    messages = scaled_messages(increment, norm_gain, sea_mask, devices)
+    scaled = exchange(messages)
+    _, diffusion_i, diffusion_j = lax.optimization_barrier((messages[0], diffusion_i, diffusion_j))
     inner_size = len(inner_rows) // devices
-    inner_messages = weight_messages(inner_starts, inner_size, diffusion_i, diffusion_j, [sea_mask])
+    inner_messages = weight_messages(inner_starts, inner_size, diffusion_i, diffusion_j)
     inner_parts = exchange(inner_messages)
-    inner_messages, edge_i, edge_j, increment, norm_gain = lax.optimization_barrier(
-        (inner_messages, diffusion_i, diffusion_j, increment, norm_gain)
-    )
+    _, edge_i, edge_j = lax.optimization_barrier((inner_messages[0], diffusion_i, diffusion_j))
     halos = halo_i(
         *[
             jnp.concatenate([flat(edge_i[:, at]), flat(edge_j[:, at])], axis=0)
             for at in (slice(0, STEPS), slice(-STEPS, None))
         ]
     )
-    messages = scaled_messages(increment, norm_gain, sea_mask, devices)
-    scaled = exchange(messages)
-    messages, halos = lax.optimization_barrier((messages, halos))
-    outer_messages = weight_messages(outer_starts, some, diffusion_i, diffusion_j, halos=halos)
-
-    depth = sum(part[2 * levels * inner_size:] for part in inner_parts)
-    here = turn_weights(inner_starts, inner_size, [depth], inner_parts, order)
-    left, right = halo_j(
-        jnp.concatenate([flat(here[:, :STEPS]), depth], axis=0),
-        flat(here[:, -STEPS:]),
-    )
-    right, right_depth = cut(right, len(inner_rows) * STEPS, rows)
+    outer_messages = weight_messages(outer_starts, some, diffusion_i, diffusion_j, halos)
 
     balance = jnp.eye(order, dtype=jnp.float32) + coupling
     by_device = balance.reshape(2, devices, levels, order)
     adjoint = jnp.concatenate([by_device[:, s].reshape(2 * levels, order) for s in source], axis=0).T
     forward = jnp.concatenate([by_device[:, t].reshape(2 * levels, order) for t in to], axis=0)
 
-    scaled[1], outer_messages = lax.optimization_barrier((scaled[1], outer_messages))
-    middle = devices // 2
-    early = shift(outer_messages[middle], middle)
-    mixed = adjoint_mix(adjoint, depth, scaled, length, width)
-    edges = flat(mixed[:, :STEPS]), flat(mixed[:, -STEPS:])
-    edges, inner_weights = lax.optimization_barrier((edges, (here, left, right)))
-    left, right = halo_j(*edges)
+    mixed, depth = adjoint_mix(adjoint, scaled, length, width)
+    left, right = halo_j(jnp.concatenate([flat(mixed[:, :STEPS]), depth], axis=0), flat(mixed[:, -STEPS:]))
+    right, right_depth = cut(right, length * STEPS, rows)
+    _, upper, lower = lax.optimization_barrier((left, mixed[:STEPS], mixed[-STEPS:]))
+    inner_parts, left, right = lax.optimization_barrier((inner_parts, left, right))
+    field = [(list(range(length)), mixed, left, right)]
+
+    inner_parts[1], outer_messages = lax.optimization_barrier((inner_parts[1], outer_messages))
+    early = shift(outer_messages[1], devices // 2)
+    here = turn_weights(inner_starts, inner_size, [depth], inner_parts, order)
+    left, right = halo_j(flat(here[:, :STEPS]), flat(here[:, -STEPS:]))
     left, right, outer_messages, early = lax.optimization_barrier((left, right, outer_messages, early))
-    outer_parts = [
-        early if d == middle else shift(outer_messages[d], d) if d else outer_messages[0] for d in range(devices)
-    ]
-    field = [(list(range(length)), mixed, left, right)]
-    weights = [(inner_rows, *inner_weights)]
+    weights = [(inner_rows, here, left, right)]
+    own, _, *others = outer_messages
+    outer_parts = [own, early] + [shift(x, d) for x, d in zip(others, distances(devices)[2:])]
     depths = [depth, right_depth]
     inner_mixed = spread_mix([inner_rows], forward, depths, field, weights, devices)
-    _, upper, lower = lax.optimization_barrier((left, mixed[:STEPS], mixed[-STEPS:]))
     _, outer_parts = lax.optimization_barrier((inner_mixed[0], outer_parts))
     inner_mixed = exchange(inner_mixed)
     out = result((inner,), norm_gain, sea_mask, inner_mixed, None)

time: 93.4 us -> 95.7 us (1.025)
  waiting for transfers between devices: 9.9 us -> 28.1 us
  starting transfers between devices: 59.9 us -> 45.4 us
    ppermute x3, starting transfers between devices: 22.9 us -> 10.2 us  [halo_j(): lax.ppermute(last, ('lev', 'gy'), ahead)]
    ppermute x15, waiting for transfers between devices: 5.57 us -> 13.6 us  [shift(): lax.ppermute(x, 'lev', [(k, (k + d) % devices) for k in range(devices)])]
    ppermute x15, starting transfers between devices: 33.9 us -> 29.9 us  [shift(): lax.ppermute(x, 'lev', [(k, (k + d) % devices) for k in range(devices)])]
    ppermute x3, waiting for transfers between devices: 0.97 us -> 4.52 us  [halo_j(): lax.ppermute(last, ('lev', 'gy'), ahead)]
    ppermute x3, waiting for transfers between devices: 3.35 us -> 6.69 us  [halo_j(): lax.ppermute(first, ('lev', 'gy'), back)]
    ppermute x2, waiting for transfers between devices: 0.01 us -> 3.29 us  [halo_i(): both = lax.ppermute(jnp.concatenate([first, last], axis=0), 'gx', up)]
    ppermute x3, starting transfers between devices: 0.07 us -> 1.86 us  [halo_j(): lax.ppermute(first, ('lev', 'gy'), back)]
  transfers between devices with their start and end apart: 23 -> 23, of which waited for: 6 -> 10; matrix products, arithmetic and copies ran while one was open for 0% -> 0% of each run, Pallas kernels for 18% -> 17%
where the time goes in v7:
time: 95.7 us; the launch traced here: 95.5 us
  starting transfers between devices  45.4 us (47%)
  waiting for transfers between devices  28.1 us (29%)
  Pallas kernels  21.1 us (22%)
    ppermute x15, starting transfers between devices, shift(): lax.ppermute(x, 'lev', [(k, (k + d) % devices) for k in range(devices)])  29.9 us
    ppermute x15, waiting for transfers between devices, shift(): lax.ppermute(x, 'lev', [(k, (k + d) % devices) for k in range(devices)])  13.6 us
    ppermute x3, starting transfers between devices, halo_j(): lax.ppermute(last, ('lev', 'gy'), ahead)  10.2 us
    pallas_call x2, Pallas kernels, spread_mix(): pl.pallas_call(kernel, in_specs=[vmem()] * (1 + len(arrays)), out_specs=[...  6.91 us
    ppermute x3, waiting for transfers between devices, halo_j(): lax.ppermute(first, ('lev', 'gy'), back)  6.69 us
    pallas_call x2, Pallas kernels, weight_messages(): pl.pallas_call(functools.partial(pack_kernel, starts), in_specs=[vmem()]...  5.16 us
    ppermute x3, waiting for transfers between devices, halo_j(): lax.ppermute(last, ('lev', 'gy'), ahead)  4.52 us
    ppermute x2, starting transfers between devices, halo_i(): both = lax.ppermute(jnp.concatenate([first, last], axis=0), 'gx', up)  3.43 us
  transfers between devices with their start and end apart: 23, of which 10 were waited for; matrix products, arithmetic and copies ran while one was open for 0% of the time, Pallas kernels for 17%

profile of v7, /device:TPU:0, one launch (start us, length us, event | category | flops | bytes accessed | tf_op | source)
XLA Modules:
  0.0 95.5 jit_solution(17470580904259901975)
XLA Ops:
  0.0 3.4 %scaled_messages.1 = (f32[528,128]{1,0:T(8,128)}, f32[528,128]{1,0:T(8,128)}, f32[528,128]{1,0:T(8,128)}, f32[528,128]{1,0:T(8,128)}) custom-call(f32[2,16,64,128]{3,2,1,0:T(8,128)} %increment.1, f32[2,16,64,128]{3,2,1,0:T(8,128)} %gain.5, s32[16,64,128]{2,1,0:T(8,128)} %mask.5), custom_call_target="tpu_custom_call" | custom-call | tf_op jit(solution)/shard_map/scaled_messages/pallas_call | solution.py:122
  3.4 4.1 %collective-permute-start = (f32[528,128]{1,0:T(8,128)}, f32[528,128]{1,0:T(8,128)S(1)}, u32[]{:S(2)}, u32[]{:S(2)}) collective-permute-start(f32[528,128]{1,0:T(8,128)} %get-tuple-element.55), channel_id=1, source_target_pairs={{0,16},{8,24},{16,0},{24,8},{1,17},{9,25},{17,1},{25,9},{2,18},{10... | collective-permute-start | bytes 811016 | tf_op jit(solution)/shard_map/ppermute | solution.py:474
  7.5 1.6 %collective-permute-start.1 = (f32[528,128]{1,0:T(8,128)}, f32[528,128]{1,0:T(8,128)S(1)}, u32[]{:S(2)}, u32[]{:S(2)}) collective-permute-start(f32[528,128]{1,0:T(8,128)} %get-tuple-element.56), channel_id=1, source_target_pairs={{0,8},{8,16},{16,24},{24,0},{1,9},{9,17},{17,25},{25,1},{2,10},{10... | collective-permute-start | bytes 811016 | tf_op jit(solution)/shard_map/ppermute | solution.py:474
  9.1 2.2 %collective-permute-start.2 = (f32[528,128]{1,0:T(8,128)}, f32[528,128]{1,0:T(8,128)S(1)}, u32[]{:S(2)}, u32[]{:S(2)}) collective-permute-start(f32[528,128]{1,0:T(8,128)} %get-tuple-element.57), channel_id=1, source_target_pairs={{0,24},{8,0},{16,8},{24,16},{1,25},{9,1},{17,9},{25,17},{2,26},{10... | collective-permute-start | bytes 811016 | tf_op jit(solution)/shard_map/ppermute | solution.py:474
  11.3 0.0 copy-done.3
  11.3 0.0 copy-done.2
  11.3 3.1 %weight_messages.2 = (f32[320,128]{1,0:T(8,128)S(1)}, f32[320,128]{1,0:T(8,128)S(1)}, f32[320,128]{1,0:T(8,128)S(1)}, f32[320,128]{1,0:T(8,128)S(1)}) custom-call(f32[16,64,128]{2,1,0:T(8,128)S(1)} %copy-done.2, f32[16,64,128]{2,1,0:T(8,128)S(1)} %copy-done.3), custom_call_target="tpu_custom_call" | custom-call | tf_op jit(solution)/shard_map/weight_messages/pallas_call | solution.py:175
  14.5 0.0 copy-start.5
  14.5 1.6 %collective-permute-start.9 = (f32[256,128]{1,0:T(8,128)S(1)}, f32[256,128]{1,0:T(8,128)S(1)}, u32[]{:S(2)}, u32[]{:S(2)}) collective-permute-start(f32[256,128]{1,0:T(8,128)S(1)} %pad_maximum_fusion.2), channel_id=1, source_target_pairs={{4,0},{0,4},{5,1},{1,5},{6,2},{2,6},{7,3},{3,7},{12,8},{8,12},{13,... | collective-permute-start | bytes 393224 | tf_op jit(solution)/shard_map/ppermute | solution.py:488
  16.1 0.0 collective-permute-start.6
  16.2 0.1 copy.13.matrix
  16.2 3.3 %collective-permute-done.9 = f32[256,128]{1,0:T(8,128)S(1)} collective-permute-done((f32[256,128]{1,0:T(8,128)S(1)}, f32[256,128]{1,0:T(8,128)S(1)}, u32[]{:S(2)}, u32[]{:S(2)}) %collective-permute-start.9) | collective-permute-done | bytes 131104 | tf_op jit(solution)/shard_map/ppermute | solution.py:488
  19.5 0.0 collective-permute-start.7
  19.6 0.0 copy-start.4
  19.6 2.1 %weight_messages.3 = (f32[256,128]{1,0:T(8,128)S(1)}, f32[256,128]{1,0:T(8,128)S(1)}, f32[256,128]{1,0:T(8,128)S(1)}, f32[256,128]{1,0:T(8,128)S(1)}) custom-call(f32[16,64,128]{2,1,0:T(8,128)S(1)} %copy-done.2, f32[16,64,128]{2,1,0:T(8,128)S(1)} %copy-done.3, f32[128,128]{1,0:T(8,128)S(1)} %get-tuple-element.122.refs_0_, ...), custom_call_target="tpu_custom_call" | custom-call | tf_op jit(solution)/shard_map/weight_messages/pallas_call | solution.py:175
  21.6 5.8 %collective-permute-done.refs_1_ = f32[528,128]{1,0:T(8,128)S(1)} collective-permute-done((f32[528,128]{1,0:T(8,128)}, f32[528,128]{1,0:T(8,128)S(1)}, u32[]{:S(2)}, u32[]{:S(2)}) %collective-permute-start) | collective-permute-done | bytes 270368 | tf_op jit(solution)/shard_map/ppermute | solution.py:474
  27.5 4.4 %collective-permute-start.8 = (f32[320,128]{1,0:T(8,128)S(1)}, f32[320,128]{1,0:T(8,128)S(1)}, u32[]{:S(2)}, u32[]{:S(2)}) collective-permute-start(f32[320,128]{1,0:T(8,128)S(1)} %get-tuple-element.67), channel_id=1, source_target_pairs={{0,24},{8,0},{16,8},{24,16},{1,25},{9,1},{17,9},{25,17},{2,26},{10... | collective-permute-start | bytes 491528 | tf_op jit(solution)/shard_map/ppermute | solution.py:474
  31.9 0.0 collective-permute-done.1.refs_2_
  31.9 0.0 collective-permute-done.2.refs_3_
  31.9 2.0 %adjoint_mix.1 = (f32[64,32,128]{2,1,0:T(8,128)S(1)}, f32[16,128]{1,0:T(8,128)S(1)}) custom-call(f32[128,128]{1,0:T(8,128)S(1)} %copy.13.matrix, f32[528,128]{1,0:T(8,128)S(1)} %copy-done.4, f32[528,128]{1,0:T(8,128)S(1)} %collective-permute-done.refs_1_, f32[528,128]{1,0:T(8,128)S(1)} %collective-permute-done.1.refs_2_, ...), custom_call_target="tpu_custom_call" | custom-call | tf_op jit(solution)/shard_map/adjoint_mix/pallas_call | solution.py:214
  34.0 8.2 %collective-permute-start.4 = (f32[256,128]{1,0:T(8,128)S(1)}, f32[256,128]{1,0:T(8,128)S(1)}, u32[]{:S(2)}, u32[]{:S(2)}) collective-permute-start(f32[256,128]{1,0:T(8,128)S(1)} %bitcast.41), channel_id=1, source_target_pairs={{0,8},{8,16},{16,24},{24,25},{25,17},{17,9},{9,1},{1,2},{2,10},{10... | collective-permute-start | bytes 393224 | tf_op jit(solution)/shard_map/ppermute | solution.py:493
  42.2 0.1 collective-permute-start.3
  42.3 2.5 %collective-permute-done.4.refs_3_.refs_5_ = f32[256,128]{1,0:T(8,128)S(1)} collective-permute-done((f32[256,128]{1,0:T(8,128)S(1)}, f32[256,128]{1,0:T(8,128)S(1)}, u32[]{:S(2)}, u32[]{:S(2)}) %collective-permute-start.4) | collective-permute-done | bytes 131104 | tf_op jit(solution)/shard_map/ppermute | solution.py:493
  44.7 1.9 %collective-permute-start.5 = (f32[264,128]{1,0:T(8,128)S(1)}, f32[264,128]{1,0:T(8,128)S(1)}, u32[]{:S(2)}, u32[]{:S(2)}) collective-permute-start(f32[264,128]{1,0:T(8,128)S(1)} %pad_maximum_fusion.1), channel_id=1, source_target_pairs={{4,0},{0,4},{5,1},{1,5},{6,2},{2,6},{7,3},{3,7},{12,8},{8,12},{13,... | collective-permute-start | bytes 405512 | tf_op jit(solution)/shard_map/ppermute | solution.py:488
  46.6 0.7 collective-permute-done.3
  47.3 0.0 collective-permute-done.6.refs_2_
  47.3 0.0 collective-permute-done.7.refs_3_
  47.3 0.0 collective-permute-done.8.refs_4_
  47.3 5.5 %collective-permute-start.12 = (f32[256,128]{1,0:T(8,128)S(1)}, f32[256,128]{1,0:T(8,128)S(1)}, u32[]{:S(2)}, u32[]{:S(2)}) collective-permute-start(f32[256,128]{1,0:T(8,128)S(1)} %get-tuple-element.82), channel_id=1, source_target_pairs={{0,16},{8,24},{16,0},{24,8},{1,17},{9,25},{17,1},{25,9},{2,18},{10... | collective-permute-start | bytes 393224 | tf_op jit(solution)/shard_map/ppermute | solution.py:474
  52.9 0.4 turn_weights.2.refs_5_.refs_10_
  53.4 0.1 collective-permute-start.10
  53.4 1.7 %collective-permute-start.11 = (f32[160,128]{1,0:T(8,128)S(1)}, f32[160,128]{1,0:T(8,128)S(1)}, u32[]{:S(2)}, u32[]{:S(2)}) collective-permute-start(f32[160,128]{1,0:T(8,128)S(1)} %bitcast.46), channel_id=1, source_target_pairs={{8,0},{16,8},{24,16},{25,24},{17,25},{9,17},{1,9},{2,1},{10,2},{18... | collective-permute-start | bytes 245768 | tf_op jit(solution)/shard_map/ppermute | solution.py:493
  55.2 0.0 collective-permute-done.5
  55.2 2.1 %collective-permute-done.10.refs_6_.refs_11_ = f32[160,128]{1,0:T(8,128)S(1)} collective-permute-done((f32[160,128]{1,0:T(8,128)S(1)}, f32[160,128]{1,0:T(8,128)S(1)}, u32[]{:S(2)}, u32[]{:S(2)}) %collective-permute-start.10) | collective-permute-done | bytes 81952 | tf_op jit(solution)/shard_map/ppermute | solution.py:493
  57.3 1.5 %collective-permute-done.11.refs_7_.refs_12_ = f32[160,128]{1,0:T(8,128)S(1)} collective-permute-done((f32[160,128]{1,0:T(8,128)S(1)}, f32[160,128]{1,0:T(8,128)S(1)}, u32[]{:S(2)}, u32[]{:S(2)}) %collective-permute-start.11) | collective-permute-done | bytes 81952 | tf_op jit(solution)/shard_map/ppermute | solution.py:493
  58.8 0.0 collective-permute-done.12.refs_3_
  58.8 1.4 %collective-permute-start.13 = (f32[256,128]{1,0:T(8,128)S(1)}, f32[256,128]{1,0:T(8,128)S(1)}, u32[]{:S(2)}, u32[]{:S(2)}) collective-permute-start(f32[256,128]{1,0:T(8,128)S(1)} %get-tuple-element.90), channel_id=1, source_target_pairs={{0,8},{8,16},{16,24},{24,0},{1,9},{9,17},{17,25},{25,1},{2,10},{10... | collective-permute-start | bytes 393224 | tf_op jit(solution)/shard_map/ppermute | solution.py:474
  60.2 2.4 %collective-permute-start.14 = (f32[256,128]{1,0:T(8,128)S(1)}, f32[256,128]{1,0:T(8,128)S(1)}, u32[]{:S(2)}, u32[]{:S(2)}) collective-permute-start(f32[256,128]{1,0:T(8,128)S(1)} %get-tuple-element.91), channel_id=1, source_target_pairs={{0,24},{8,0},{16,8},{24,16},{1,25},{9,1},{17,9},{25,17},{2,26},{10... | collective-permute-start | bytes 393224 | tf_op jit(solution)/shard_map/ppermute | solution.py:474
  62.6 3.4 %spread_mix.2 = (f32[256,128]{1,0:T(8,128)S(1)}, f32[256,128]{1,0:T(8,128)S(1)}, f32[256,128]{1,0:T(8,128)S(1)}, f32[256,128]{1,0:T(8,128)S(1)}) custom-call(f32[128,128]{1,0:T(8,128)S(1)} %get-tuple-element.129.matrix, f32[16,128]{1,0:T(8,128)S(1)} %get-tuple-element.58.refs_0_, f32[16,128]{1,0:T(8,128)S(1)} %split.44.refs_1_, ...), custom_call_target="tpu_custom_call" | custom-call | tf_op jit(solution)/shard_map/spread_mix/pallas_call | solution.py:388
  66.0 0.1 collective-permute-start.20
  66.1 0.9 collective-permute-done.13.refs_4_
  67.0 0.8 collective-permute-done.14.refs_5_
  67.7 0.4 turn_weights.3.refs_13_
  68.2 0.1 collective-permute-start.15
  68.2 2.0 %collective-permute-start.16 = (f32[160,128]{1,0:T(8,128)S(1)}, f32[160,128]{1,0:T(8,128)S(1)}, u32[]{:S(2)}, u32[]{:S(2)}) collective-permute-start(f32[160,128]{1,0:T(8,128)S(1)} %pad_maximum_fusion.7), channel_id=1, source_target_pairs={{0,8},{8,16},{16,24},{24,25},{25,17},{17,9},{9,1},{1,2},{2,10},{10... | collective-permute-start | bytes 245768 | tf_op jit(solution)/shard_map/ppermute | solution.py:493
  70.2 1.2 %collective-permute-start.21 = (f32[256,128]{1,0:T(8,128)S(1)}, f32[256,128]{1,0:T(8,128)S(1)}, u32[]{:S(2)}, u32[]{:S(2)}) collective-permute-start(f32[256,128]{1,0:T(8,128)S(1)} %get-tuple-element.101), channel_id=1, source_target_pairs={{0,8},{8,16},{16,24},{24,0},{1,9},{9,17},{17,25},{25,1},{2,10},{10... | collective-permute-start | bytes 393224 | tf_op jit(solution)/shard_map/ppermute | solution.py:474
  71.5 2.6 %collective-permute-start.22 = (f32[256,128]{1,0:T(8,128)S(1)}, f32[256,128]{1,0:T(8,128)S(1)}, u32[]{:S(2)}, u32[]{:S(2)}) collective-permute-start(f32[256,128]{1,0:T(8,128)S(1)} %get-tuple-element.102), channel_id=1, source_target_pairs={{0,24},{8,0},{16,8},{24,16},{1,25},{9,1},{17,9},{25,17},{2,26},{10... | collective-permute-start | bytes 393224 | tf_op jit(solution)/shard_map/ppermute | solution.py:474
  74.1 0.0 collective-permute-done.16
  74.1 4.5 %collective-permute-done.15 = f32[168,128]{1,0:T(8,128)S(1)} collective-permute-done((f32[168,128]{1,0:T(8,128)S(1)}, f32[168,128]{1,0:T(8,128)S(1)}, u32[]{:S(2)}, u32[]{:S(2)}) %collective-permute-start.15) | collective-permute-done | bytes 86048 | tf_op jit(solution)/shard_map/ppermute | solution.py:493
  78.6 0.0 copy-start
  78.6 0.0 copy-start.1
  78.6 3.6 %spread_mix.3 = (f32[256,128]{1,0:T(8,128)S(1)}, f32[256,128]{1,0:T(8,128)S(1)}, f32[256,128]{1,0:T(8,128)S(1)}, f32[256,128]{1,0:T(8,128)S(1)}) custom-call(f32[128,128]{1,0:T(8,128)S(1)} %get-tuple-element.129.matrix, f32[16,128]{1,0:T(8,128)S(1)} %get-tuple-element.58.refs_0_, f32[16,128]{1,0:T(8,128)S(1)} %split.44.refs_1_, ...), custom_call_target="tpu_custom_call" | custom-call | tf_op jit(solution)/shard_map/spread_mix/pallas_call | solution.py:388
  82.2 0.4 collective-permute-start.17
  82.7 1.1 %collective-permute-start.18 = (f32[256,128]{1,0:T(8,128)S(1)}, f32[256,128]{1,0:T(8,128)S(1)}, u32[]{:S(2)}, u32[]{:S(2)}) collective-permute-start(f32[256,128]{1,0:T(8,128)S(1)} %get-tuple-element.98), channel_id=1, source_target_pairs={{0,8},{8,16},{16,24},{24,0},{1,9},{9,17},{17,25},{25,1},{2,10},{10... | collective-permute-start | bytes 393224 | tf_op jit(solution)/shard_map/ppermute | solution.py:474
  83.7 0.0 collective-permute-done.20.refs_1_
  83.7 2.7 %collective-permute-start.19 = (f32[256,128]{1,0:T(8,128)S(1)}, f32[256,128]{1,0:T(8,128)S(1)}, u32[]{:S(2)}, u32[]{:S(2)}) collective-permute-start(f32[256,128]{1,0:T(8,128)S(1)} %get-tuple-element.99), channel_id=1, source_target_pairs={{0,24},{8,0},{16,8},{24,16},{1,25},{9,1},{17,9},{25,17},{2,26},{10... | collective-permute-start | bytes 393224 | tf_op jit(solution)/shard_map/ppermute | solution.py:474
  86.5 0.0 collective-permute-done.21.refs_2_
  86.5 0.0 collective-permute-done.22.refs_3_
  86.5 0.0 copy-done.1
  86.5 1.4 %result.2.refs_4_ = f32[2,16,64,128]{3,2,1,0:T(8,128)} custom-call(f32[2,16,64,128]{3,2,1,0:T(8,128)S(1)} %copy-done, s32[16,64,128]{2,1,0:T(8,128)S(1)} %copy-done.1, f32[256,128]{1,0:T(8,128)S(1)} %get-tuple-element.87.refs_0_, f32[256,128]{1,0:T(8,128)S(1)} %collective-permute-done.20.refs_1_, f32[256,128]{1,0:T(8,128)S(1)} %collective-permute-done.21.refs_2_, ...), custom_call_target="tpu_custom_call" | custom-call | tf_op jit(solution)/shard_map/result/pallas_call | solution.py:447
  87.9 6.1 %collective-permute-done.17.refs_1_ = f32[256,128]{1,0:T(8,128)S(1)} collective-permute-done((f32[256,128]{1,0:T(8,128)S(1)}, f32[256,128]{1,0:T(8,128)S(1)}, u32[]{:S(2)}, u32[]{:S(2)}) %collective-permute-start.17) | collective-permute-done | bytes 131104 | tf_op jit(solution)/shard_map/ppermute | solution.py:474
  94.1 0.0 collective-permute-done.18.refs_2_
  94.1 0.0 collective-permute-done.19.refs_3_
  94.1 1.4 %result.3 = f32[2,16,64,128]{3,2,1,0:T(8,128)} custom-call(f32[2,16,64,128]{3,2,1,0:T(8,128)S(1)} %copy-done, s32[16,64,128]{2,1,0:T(8,128)S(1)} %copy-done.1, f32[256,128]{1,0:T(8,128)S(1)} %get-tuple-element.96.refs_0_, f32[256,128]{1,0:T(8,128)S(1)} %collective-permute-done.17.refs_1_, ...), custom_call_target="tpu_custom_call", output_to_operand_aliasing={{}: (6, {})} | custom-call | tf_op jit(solution)/shard_map/result/pallas_call | solution.py:447
  (32 shorter events, 0.3 us)
Async XLA Ops:
  0.0 11.3 %copy-start.3 = (f32[16,64,128]{2,1,0:T(8,128)S(1)}, f32[16,64,128]{2,1,0:T(8,128)}, u32[]{:S(2)}) copy-start(f32[16,64,128]{2,1,0:T(8,128)} %along_j.1) | copy-start | bytes 1572868
  0.0 11.3 %copy-start.2 = (f32[16,64,128]{2,1,0:T(8,128)S(1)}, f32[16,64,128]{2,1,0:T(8,128)}, u32[]{:S(2)}) copy-start(f32[16,64,128]{2,1,0:T(8,128)} %along_i.1) | copy-start | bytes 1572868
  3.4 24.1 %collective-permute-start = (f32[528,128]{1,0:T(8,128)}, f32[528,128]{1,0:T(8,128)S(1)}, u32[]{:S(2)}, u32[]{:S(2)}) collective-permute-start(f32[528,128]{1,0:T(8,128)} %get-tuple-element.55), channel_id=1, source_target_pairs={{0,16},{8,24},{16,0},{24,8},{1,17},{9,25},{17,1},{25,9},{2,18},{10... | collective-permute-start | bytes 811016 | tf_op jit(solution)/shard_map/ppermute | solution.py:474
  7.5 24.4 %collective-permute-start.1 = (f32[528,128]{1,0:T(8,128)}, f32[528,128]{1,0:T(8,128)S(1)}, u32[]{:S(2)}, u32[]{:S(2)}) collective-permute-start(f32[528,128]{1,0:T(8,128)} %get-tuple-element.56), channel_id=1, source_target_pairs={{0,8},{8,16},{16,24},{24,0},{1,9},{9,17},{17,25},{25,1},{2,10},{10... | collective-permute-start | bytes 811016 | tf_op jit(solution)/shard_map/ppermute | solution.py:474
  9.1 22.8 %collective-permute-start.2 = (f32[528,128]{1,0:T(8,128)}, f32[528,128]{1,0:T(8,128)S(1)}, u32[]{:S(2)}, u32[]{:S(2)}) collective-permute-start(f32[528,128]{1,0:T(8,128)} %get-tuple-element.57), channel_id=1, source_target_pairs={{0,24},{8,0},{16,8},{24,16},{1,25},{9,1},{17,9},{25,17},{2,26},{10... | collective-permute-start | bytes 811016 | tf_op jit(solution)/shard_map/ppermute | solution.py:474
  14.5 1.6 %copy-start.5 = (f32[128,128]{1,0:T(8,128)S(1)}, f32[128,128]{1,0:T(8,128)}, u32[]{:S(2)}) copy-start(f32[128,128]{1,0:T(8,128)} %param.11) | copy-start | bytes 196612
  14.5 5.0 %collective-permute-start.9 = (f32[256,128]{1,0:T(8,128)S(1)}, f32[256,128]{1,0:T(8,128)S(1)}, u32[]{:S(2)}, u32[]{:S(2)}) collective-permute-start(f32[256,128]{1,0:T(8,128)S(1)} %pad_maximum_fusion.2), channel_id=1, source_target_pairs={{4,0},{0,4},{5,1},{1,5},{6,2},{2,6},{7,3},{3,7},{12,8},{8,12},{13,... | collective-permute-start | bytes 393224 | tf_op jit(solution)/shard_map/ppermute | solution.py:488
  16.1 31.3 %collective-permute-start.6 = (f32[320,128]{1,0:T(8,128)S(1)}, f32[320,128]{1,0:T(8,128)S(1)}, u32[]{:S(2)}, u32[]{:S(2)}) collective-permute-start(f32[320,128]{1,0:T(8,128)S(1)} %get-tuple-element.65), channel_id=1, source_target_pairs={{0,16},{8,24},{16,0},{24,8},{1,17},{9,25},{17,1},{25,9},{2,18},{10... | collective-permute-start | bytes 491528 | tf_op jit(solution)/shard_map/ppermute | solution.py:474
  19.5 27.8 %collective-permute-start.7 = (f32[320,128]{1,0:T(8,128)S(1)}, f32[320,128]{1,0:T(8,128)S(1)}, u32[]{:S(2)}, u32[]{:S(2)}) collective-permute-start(f32[320,128]{1,0:T(8,128)S(1)} %get-tuple-element.66), channel_id=1, source_target_pairs={{0,8},{8,16},{16,24},{24,0},{1,9},{9,17},{17,25},{25,1},{2,10},{10... | collective-permute-start | bytes 491528 | tf_op jit(solution)/shard_map/ppermute | solution.py:474
  19.6 12.4 %copy-start.4 = (f32[528,128]{1,0:T(8,128)S(1)}, f32[528,128]{1,0:T(8,128)}, u32[]{:S(2)}) copy-start(f32[528,128]{1,0:T(8,128)} %get-tuple-element.54.refs_0_) | copy-start | bytes 811012
  27.5 19.9 %collective-permute-start.8 = (f32[320,128]{1,0:T(8,128)S(1)}, f32[320,128]{1,0:T(8,128)S(1)}, u32[]{:S(2)}, u32[]{:S(2)}) collective-permute-start(f32[320,128]{1,0:T(8,128)S(1)} %get-tuple-element.67), channel_id=1, source_target_pairs={{0,24},{8,0},{16,8},{24,16},{1,25},{9,1},{17,9},{25,17},{2,26},{10... | collective-permute-start | bytes 491528 | tf_op jit(solution)/shard_map/ppermute | solution.py:474
  34.0 10.7 %collective-permute-start.4 = (f32[256,128]{1,0:T(8,128)S(1)}, f32[256,128]{1,0:T(8,128)S(1)}, u32[]{:S(2)}, u32[]{:S(2)}) collective-permute-start(f32[256,128]{1,0:T(8,128)S(1)} %bitcast.41), channel_id=1, source_target_pairs={{0,8},{8,16},{16,24},{24,25},{25,17},{17,9},{9,1},{1,2},{2,10},{10... | collective-permute-start | bytes 393224 | tf_op jit(solution)/shard_map/ppermute | solution.py:493
  42.2 5.1 %collective-permute-start.3 = (f32[272,128]{1,0:T(8,128)S(1)}, f32[272,128]{1,0:T(8,128)S(1)}, u32[]{:S(2)}, u32[]{:S(2)}) collective-permute-start(f32[272,128]{1,0:T(8,128)S(1)} %pad_maximum_fusion), channel_id=1, source_target_pairs={{8,0},{16,8},{24,16},{25,24},{17,25},{9,17},{1,9},{2,1},{10,2},{18... | collective-permute-start | bytes 417800 | tf_op jit(solution)/shard_map/ppermute | solution.py:493
  44.7 10.4 %collective-permute-start.5 = (f32[264,128]{1,0:T(8,128)S(1)}, f32[264,128]{1,0:T(8,128)S(1)}, u32[]{:S(2)}, u32[]{:S(2)}) collective-permute-start(f32[264,128]{1,0:T(8,128)S(1)} %pad_maximum_fusion.1), channel_id=1, source_target_pairs={{4,0},{0,4},{5,1},{1,5},{6,2},{2,6},{7,3},{3,7},{12,8},{8,12},{13,... | collective-permute-start | bytes 405512 | tf_op jit(solution)/shard_map/ppermute | solution.py:488
  47.3 11.4 %collective-permute-start.12 = (f32[256,128]{1,0:T(8,128)S(1)}, f32[256,128]{1,0:T(8,128)S(1)}, u32[]{:S(2)}, u32[]{:S(2)}) collective-permute-start(f32[256,128]{1,0:T(8,128)S(1)} %get-tuple-element.82), channel_id=1, source_target_pairs={{0,16},{8,24},{16,0},{24,8},{1,17},{9,25},{17,1},{25,9},{2,18},{10... | collective-permute-start | bytes 393224 | tf_op jit(solution)/shard_map/ppermute | solution.py:474
  53.4 3.9 %collective-permute-start.10 = (f32[160,128]{1,0:T(8,128)S(1)}, f32[160,128]{1,0:T(8,128)S(1)}, u32[]{:S(2)}, u32[]{:S(2)}) collective-permute-start(f32[160,128]{1,0:T(8,128)S(1)} %bitcast.47), channel_id=1, source_target_pairs={{0,8},{8,16},{16,24},{24,25},{25,17},{17,9},{9,1},{1,2},{2,10},{10... | collective-permute-start | bytes 245768 | tf_op jit(solution)/shard_map/ppermute | solution.py:493
  53.4 5.3 %collective-permute-start.11 = (f32[160,128]{1,0:T(8,128)S(1)}, f32[160,128]{1,0:T(8,128)S(1)}, u32[]{:S(2)}, u32[]{:S(2)}) collective-permute-start(f32[160,128]{1,0:T(8,128)S(1)} %bitcast.46), channel_id=1, source_target_pairs={{8,0},{16,8},{24,16},{25,24},{17,25},{9,17},{1,9},{2,1},{10,2},{18... | collective-permute-start | bytes 245768 | tf_op jit(solution)/shard_map/ppermute | solution.py:493
  58.8 8.2 %collective-permute-start.13 = (f32[256,128]{1,0:T(8,128)S(1)}, f32[256,128]{1,0:T(8,128)S(1)}, u32[]{:S(2)}, u32[]{:S(2)}) collective-permute-start(f32[256,128]{1,0:T(8,128)S(1)} %get-tuple-element.90), channel_id=1, source_target_pairs={{0,8},{8,16},{16,24},{24,0},{1,9},{9,17},{17,25},{25,1},{2,10},{10... | collective-permute-start | bytes 393224 | tf_op jit(solution)/shard_map/ppermute | solution.py:474
  60.2 7.5 %collective-permute-start.14 = (f32[256,128]{1,0:T(8,128)S(1)}, f32[256,128]{1,0:T(8,128)S(1)}, u32[]{:S(2)}, u32[]{:S(2)}) collective-permute-start(f32[256,128]{1,0:T(8,128)S(1)} %get-tuple-element.91), channel_id=1, source_target_pairs={{0,24},{8,0},{16,8},{24,16},{1,25},{9,1},{17,9},{25,17},{2,26},{10... | collective-permute-start | bytes 393224 | tf_op jit(solution)/shard_map/ppermute | solution.py:474
  66.0 17.8 %collective-permute-start.20 = (f32[256,128]{1,0:T(8,128)S(1)}, f32[256,128]{1,0:T(8,128)S(1)}, u32[]{:S(2)}, u32[]{:S(2)}) collective-permute-start(f32[256,128]{1,0:T(8,128)S(1)} %get-tuple-element.100), channel_id=1, source_target_pairs={{0,16},{8,24},{16,0},{24,8},{1,17},{9,25},{17,1},{25,9},{2,18},{10... | collective-permute-start | bytes 393224 | tf_op jit(solution)/shard_map/ppermute | solution.py:474
  68.2 10.5 %collective-permute-start.15 = (f32[168,128]{1,0:T(8,128)S(1)}, f32[168,128]{1,0:T(8,128)S(1)}, u32[]{:S(2)}, u32[]{:S(2)}) collective-permute-start(f32[168,128]{1,0:T(8,128)S(1)} %pad_maximum_fusion.6), channel_id=1, source_target_pairs={{8,0},{16,8},{24,16},{25,24},{17,25},{9,17},{1,9},{2,1},{10,2},{18... | collective-permute-start | bytes 258056 | tf_op jit(solution)/shard_map/ppermute | solution.py:493
  68.2 5.8 %collective-permute-start.16 = (f32[160,128]{1,0:T(8,128)S(1)}, f32[160,128]{1,0:T(8,128)S(1)}, u32[]{:S(2)}, u32[]{:S(2)}) collective-permute-start(f32[160,128]{1,0:T(8,128)S(1)} %pad_maximum_fusion.7), channel_id=1, source_target_pairs={{0,8},{8,16},{16,24},{24,25},{25,17},{17,9},{9,1},{1,2},{2,10},{10... | collective-permute-start | bytes 245768 | tf_op jit(solution)/shard_map/ppermute | solution.py:493
  70.2 16.2 %collective-permute-start.21 = (f32[256,128]{1,0:T(8,128)S(1)}, f32[256,128]{1,0:T(8,128)S(1)}, u32[]{:S(2)}, u32[]{:S(2)}) collective-permute-start(f32[256,128]{1,0:T(8,128)S(1)} %get-tuple-element.101), channel_id=1, source_target_pairs={{0,8},{8,16},{16,24},{24,0},{1,9},{9,17},{17,25},{25,1},{2,10},{10... | collective-permute-start | bytes 393224 | tf_op jit(solution)/shard_map/ppermute | solution.py:474
  71.5 15.0 %collective-permute-start.22 = (f32[256,128]{1,0:T(8,128)S(1)}, f32[256,128]{1,0:T(8,128)S(1)}, u32[]{:S(2)}, u32[]{:S(2)}) collective-permute-start(f32[256,128]{1,0:T(8,128)S(1)} %get-tuple-element.102), channel_id=1, source_target_pairs={{0,24},{8,0},{16,8},{24,16},{1,25},{9,1},{17,9},{25,17},{2,26},{10... | collective-permute-start | bytes 393224 | tf_op jit(solution)/shard_map/ppermute | solution.py:474
  78.6 7.9 %copy-start = (f32[2,16,64,128]{3,2,1,0:T(8,128)S(1)}, f32[2,16,64,128]{3,2,1,0:T(8,128)}, u32[]{:S(2)}) copy-start(f32[2,16,64,128]{3,2,1,0:T(8,128)} %gain.5) | copy-start | bytes 3145732
  78.6 7.9 %copy-start.1 = (s32[16,64,128]{2,1,0:T(8,128)S(1)}, s32[16,64,128]{2,1,0:T(8,128)}, u32[]{:S(2)}) copy-start(s32[16,64,128]{2,1,0:T(8,128)} %mask.5) | copy-start | bytes 1572868
  82.2 11.8 %collective-permute-start.17 = (f32[256,128]{1,0:T(8,128)S(1)}, f32[256,128]{1,0:T(8,128)S(1)}, u32[]{:S(2)}, u32[]{:S(2)}) collective-permute-start(f32[256,128]{1,0:T(8,128)S(1)} %get-tuple-element.97), channel_id=1, source_target_pairs={{0,16},{8,24},{16,0},{24,8},{1,17},{9,25},{17,1},{25,9},{2,18},{10... | collective-permute-start | bytes 393224 | tf_op jit(solution)/shard_map/ppermute | solution.py:474
  82.7 11.4 %collective-permute-start.18 = (f32[256,128]{1,0:T(8,128)S(1)}, f32[256,128]{1,0:T(8,128)S(1)}, u32[]{:S(2)}, u32[]{:S(2)}) collective-permute-start(f32[256,128]{1,0:T(8,128)S(1)} %get-tuple-element.98), channel_id=1, source_target_pairs={{0,8},{8,16},{16,24},{24,0},{1,9},{9,17},{17,25},{25,1},{2,10},{10... | collective-permute-start | bytes 393224 | tf_op jit(solution)/shard_map/ppermute | solution.py:474
  83.7 10.3 %collective-permute-start.19 = (f32[256,128]{1,0:T(8,128)S(1)}, f32[256,128]{1,0:T(8,128)S(1)}, u32[]{:S(2)}, u32[]{:S(2)}) collective-permute-start(f32[256,128]{1,0:T(8,128)S(1)} %get-tuple-element.99), channel_id=1, source_target_pairs={{0,24},{8,0},{16,8},{24,16},{1,25},{9,1},{17,9},{25,17},{2,26},{10... | collective-permute-start | bytes 393224 | tf_op jit(solution)/shard_map/ppermute | solution.py:474

commit v8 on v6

--- a/solution.py
+++ b/solution.py
@@ -27,6 +27,10 @@
     return pl.BlockSpec(memory_space=pltpu.VMEM)
 
 
+def distances(devices):
+    return [0, devices // 2] + [d for d in range(1, devices) if d != devices // 2]
+
+
 def position():
     devices = lax.axis_size("lev")
     me = lax.axis_index("lev")
@@ -35,8 +39,8 @@
     def slot(lev):
         return jnp.where(flipped, devices - 1 - lev, lev)
 
-    to = [lax.rem(me + d, devices) for d in range(devices)]
-    source = [lax.rem(me + devices - d, devices) for d in range(devices)]
+    to = [lax.rem(me + d, devices) for d in distances(devices)]
+    source = [lax.rem(me + devices - d, devices) for d in distances(devices)]
     return [slot(lev) for lev in to], [slot(lev) for lev in source], source
 
 
@@ -333,7 +337,7 @@
     half = order // 2
     _, ext, wide, _ = a.shape
     lane = lax.broadcasted_iota(jnp.int32, (wide, order), 1)
-    row = lax.broadcasted_iota(jnp.int32, (wide, order), 0)
+    last = lax.broadcasted_iota(jnp.int32, (PAD, order), 0) == PAD - 1
     nothing = jnp.zeros((PAD - STEPS, order), jnp.float32)
     masks[0], masks[1] = edge_masks(depths, order)
 
@@ -342,22 +346,24 @@
         main, left, right = some[piece]
         k = rows[piece].index(r)
         side = pl.ds(k * STEPS, STEPS)
-        return jnp.concatenate([nothing, left[side, :], main[k], right[side, :], nothing], axis=0)
+        return [jnp.concatenate([nothing, left[side, :]], axis=0), main[k], jnp.concatenate([right[side, :], nothing], axis=0)]
 
     for n, window in enumerate(windows):
         for e, r in enumerate(window):
-            a[n, e] = row_of(pieces[:len(field_rows)], field_rows, r)
-            w = row_of(pieces[len(field_rows):], weight_rows, r)
+            a[n, e] = jnp.concatenate(row_of(pieces[:len(field_rows)], field_rows, r), axis=0)
+            left, mid, right = row_of(pieces[len(field_rows):], weight_rows, r)
             at = pl.ds(STEPS + r, 1)
-            w = w * jnp.where(row == PAD - 1, masks[0, at, :], 1.0)
-            w = w * jnp.where(row == PAD + width - 1, masks[1, at, :], 1.0)
+            left = jnp.where(last, left * masks[0, at, :], left)
+            end = mid[width - PAD:]
+            end = jnp.where(last, end * masks[1, at, :], end)
+            w = jnp.concatenate([left, mid[:width - PAD], end, right], axis=0)
             other = pltpu.roll(w, half, 1)
             wi[n, e] = jnp.where(lane < half, w, other)
             wj[n, e] = jnp.where(lane < half, other, w)
 
     src, dst = a, b
     for step in range(STEPS):
-        begin, last = step + 1, ext - 2 - step
+        begin, stop = step + 1, ext - 1 - step
         for n in range(len(windows)):
 
             def one(r, carry, n=n, src=src, dst=dst):
@@ -369,7 +375,7 @@
                 return after, flux
 
             v = src[n, begin]
-            lax.fori_loop(begin, last + 1, one, (v, wi[n, begin - 1] * (v - src[n, begin - 1])), unroll=2)
+            lax.fori_loop(begin, stop, one, (v, wi[n, begin - 1] * (v - src[n, begin - 1])), unroll=2)
         src, dst = dst, src
 
     groups = len(outs)
@@ -484,14 +490,14 @@
     width = cols // devices
     rows = length // devices
     order = coupling.shape[0]
-    to = [lax.rem(lax.axis_index("lev") + d, devices) for d in range(devices)]
-    source = [lax.rem(lax.axis_index("lev") + devices - d, devices) for d in range(devices)]
+    to = [lax.rem(lax.axis_index("lev") + d, devices) for d in distances(devices)]
+    source = [lax.rem(lax.axis_index("lev") + devices - d, devices) for d in distances(devices)]
 
     def shift(x, d):
         return lax.ppermute(x, "lev", [(k, (k + d) % devices) for k in range(devices)])
 
     def exchange(parts):
-        return [parts[0]] + [shift(parts[d], d) for d in range(1, devices)]
+        return [parts[0]] + [shift(x, d) for x, d in zip(parts[1:], distances(devices)[1:])]
 
     up = [((k + 1) % gx_size, k) for k in range(gx_size)]
     down = [(b, a) for a, b in up]
@@ -557,16 +563,14 @@
     forward = jnp.concatenate([by_device[:, t].reshape(2 * levels, order) for t in to], axis=0)
 
     scaled[1], outer_messages = lax.optimization_barrier((scaled[1], outer_messages))
-    middle = devices // 2
-    early = shift(outer_messages[middle], middle)
+    early = shift(outer_messages[1], devices // 2)
     mixed = adjoint_mix(adjoint, depth, scaled, length, width)
     edges = flat(mixed[:, :STEPS]), flat(mixed[:, -STEPS:])
     edges, inner_weights = lax.optimization_barrier((edges, (here, left, right)))
     left, right = halo_j(*edges)
     left, right, outer_messages, early = lax.optimization_barrier((left, right, outer_messages, early))
-    outer_parts = [
-        early if d == middle else shift(outer_messages[d], d) if d else outer_messages[0] for d in range(devices)
-    ]
+    own, _, *others = outer_messages
+    outer_parts = [own, early] + [shift(x, d) for x, d in zip(others, distances(devices)[2:])]
     field = [(list(range(length)), mixed, left, right)]
     weights = [(inner_rows, *inner_weights)]
     depths = [depth, right_depth]

time: 93.4 us -> 93.1 us (level)
  starting transfers between devices: 59.9 us -> 49.8 us
  waiting for transfers between devices: 9.9 us -> 19.2 us
    ppermute x15, starting transfers between devices: 33.9 us -> 23.5 us  [shift(): lax.ppermute(x, 'lev', [(k, (k + d) % devices) for k in range(devices)])]
    ppermute x15, waiting for transfers between devices: 5.57 us -> 11.9 us  [shift(): lax.ppermute(x, 'lev', [(k, (k + d) % devices) for k in range(devices)])]
    ppermute x3, waiting for transfers between devices: 3.35 us -> 5.91 us  [halo_j(): lax.ppermute(first, ('lev', 'gy'), back)]
  transfers between devices with their start and end apart: 23 -> 23, of which waited for: 6 -> 8; matrix products, arithmetic and copies ran while one was open for 0% -> 0% of each run, Pallas kernels for 18% -> 18%
where the time goes in v8:
time: 93.1 us; the launch traced here: 92.9 us
  starting transfers between devices  49.8 us (53%)
  Pallas kernels  21.6 us (23%)
  waiting for transfers between devices  19.2 us (21%)
  local copies, waits for them, and re-layouts  1.87 us (2%)
    ppermute x15, starting transfers between devices, shift(): lax.ppermute(x, 'lev', [(k, (k + d) % devices) for k in range(devices)])  23.5 us
    ppermute x3, starting transfers between devices, halo_j(): lax.ppermute(last, ('lev', 'gy'), ahead)  22.7 us
    ppermute x15, waiting for transfers between devices, shift(): lax.ppermute(x, 'lev', [(k, (k + d) % devices) for k in range(devices)])  11.9 us
    pallas_call x2, Pallas kernels, spread_mix(): pl.pallas_call(kernel, in_specs=[vmem()] * (1 + len(arrays)), out_specs=[...  6.91 us
    ppermute x3, waiting for transfers between devices, halo_j(): lax.ppermute(first, ('lev', 'gy'), back)  5.91 us
    pallas_call x2, Pallas kernels, weight_messages(): pl.pallas_call(functools.partial(pack_kernel, starts, rows, len(mask)), i...  5.75 us
    ppermute x2, starting transfers between devices, halo_i(): both = lax.ppermute(jnp.concatenate([first, last], axis=0), 'gx', up)  3.46 us
    pallas_call x1, Pallas kernels, scaled_messages(): pl.pallas_call(scaled_kernel, in_specs=[pl.BlockSpec(memory_space=pl.ANY)...  3.25 us
  transfers between devices with their start and end apart: 23, of which 8 were waited for; matrix products, arithmetic and copies ran while one was open for 0% of the time, Pallas kernels for 18%

profile of v8, /device:TPU:0, one launch (start us, length us, event | category | flops | bytes accessed | tf_op | source)
XLA Modules:
  0.0 92.9 jit_solution(4304016107633838604)
XLA Ops:
  0.0 3.6 %weight_messages.2 = (f32[336,128]{1,0:T(8,128)}, f32[336,128]{1,0:T(8,128)}, f32[336,128]{1,0:T(8,128)}, f32[336,128]{1,0:T(8,128)}) custom-call(f32[16,64,128]{2,1,0:T(8,128)} %along_i.3, f32[16,64,128]{2,1,0:T(8,128)} %along_j.3, s32[16,64,128]{2,1,0:T(8,128)} %mask.5), custom_call_target="tpu_custom_call" | custom-call | tf_op jit(solution)/shard_map/weight_messages/pallas_call | solution.py:198
  3.6 4.1 %collective-permute-start = (f32[336,128]{1,0:T(8,128)}, f32[336,128]{1,0:T(8,128)S(1)}, u32[]{:S(2)}, u32[]{:S(2)}) collective-permute-start(f32[336,128]{1,0:T(8,128)} %get-tuple-element.54), channel_id=1, source_target_pairs={{0,16},{8,24},{16,0},{24,8},{1,17},{9,25},{17,1},{25,9},{2,18},{10... | collective-permute-start | bytes 516104 | tf_op jit(solution)/shard_map/ppermute | solution.py:497
  7.7 1.6 %collective-permute-start.1 = (f32[336,128]{1,0:T(8,128)}, f32[336,128]{1,0:T(8,128)S(1)}, u32[]{:S(2)}, u32[]{:S(2)}) collective-permute-start(f32[336,128]{1,0:T(8,128)} %get-tuple-element.55), channel_id=1, source_target_pairs={{0,8},{8,16},{16,24},{24,0},{1,9},{9,17},{17,25},{25,1},{2,10},{10... | collective-permute-start | bytes 516104 | tf_op jit(solution)/shard_map/ppermute | solution.py:497
  9.3 2.2 %collective-permute-start.2 = (f32[336,128]{1,0:T(8,128)}, f32[336,128]{1,0:T(8,128)S(1)}, u32[]{:S(2)}, u32[]{:S(2)}) collective-permute-start(f32[336,128]{1,0:T(8,128)} %get-tuple-element.56), channel_id=1, source_target_pairs={{0,24},{8,0},{16,8},{24,16},{1,25},{9,1},{17,9},{25,17},{2,26},{10... | collective-permute-start | bytes 516104 | tf_op jit(solution)/shard_map/ppermute | solution.py:497
  11.5 0.0 copy-done.2
  11.6 1.6 %collective-permute-start.5 = (f32[256,128]{1,0:T(8,128)S(1)}, f32[256,128]{1,0:T(8,128)S(1)}, u32[]{:S(2)}, u32[]{:S(2)}) collective-permute-start(f32[256,128]{1,0:T(8,128)S(1)} %pad_maximum_fusion.1), channel_id=1, source_target_pairs={{4,0},{0,4},{5,1},{1,5},{6,2},{2,6},{7,3},{3,7},{12,8},{8,12},{13,... | collective-permute-start | bytes 393224 | tf_op jit(solution)/shard_map/ppermute | solution.py:511
  13.1 3.3 %scaled_messages.1 = (f32[512,128]{1,0:T(8,128)}, f32[512,128]{1,0:T(8,128)}, f32[512,128]{1,0:T(8,128)}, f32[512,128]{1,0:T(8,128)}) custom-call(f32[2,16,64,128]{3,2,1,0:T(8,128)} %increment, f32[2,16,64,128]{3,2,1,0:T(8,128)} %gain.2, s32[16,64,128]{2,1,0:T(8,128)} %mask.5), custom_call_target="tpu_custom_call" | custom-call | tf_op jit(solution)/shard_map/scaled_messages/pallas_call | solution.py:121
  16.4 0.0 copy-start.6
  16.4 0.1 collective-permute-start.4
  16.5 0.7 copy-done.6
  17.3 0.1 copy.13.matrix
  17.4 0.0 collective-permute-done.5
  17.4 0.8 copy-done.8
  18.2 0.0 collective-permute-start.6
  18.3 2.2 %weight_messages.3 = (f32[256,128]{1,0:T(8,128)S(1)}, f32[256,128]{1,0:T(8,128)S(1)}, f32[256,128]{1,0:T(8,128)S(1)}, f32[256,128]{1,0:T(8,128)S(1)}) custom-call(f32[16,64,128]{2,1,0:T(8,128)S(1)} %copy-done.2, f32[16,64,128]{2,1,0:T(8,128)S(1)} %copy-done.3, f32[128,128]{1,0:T(8,128)S(1)} %get-tuple-element.65.refs_0_, ...), custom_call_target="tpu_custom_call" | custom-call | tf_op jit(solution)/shard_map/weight_messages/pallas_call | solution.py:198
  20.4 0.9 %collective-permute-done.refs_2_ = f32[336,128]{1,0:T(8,128)S(1)} collective-permute-done((f32[336,128]{1,0:T(8,128)}, f32[336,128]{1,0:T(8,128)S(1)}, u32[]{:S(2)}, u32[]{:S(2)}) %collective-permute-start) | collective-permute-done | bytes 172064 | tf_op jit(solution)/shard_map/ppermute | solution.py:497
  21.4 2.9 %collective-permute-start.7 = (f32[512,128]{1,0:T(8,128)S(1)}, f32[512,128]{1,0:T(8,128)S(1)}, u32[]{:S(2)}, u32[]{:S(2)}) collective-permute-start(f32[512,128]{1,0:T(8,128)S(1)} %copy-done.7), channel_id=1, source_target_pairs={{0,24},{8,0},{16,8},{24,16},{1,25},{9,1},{17,9},{25,17},{2,26},{10... | collective-permute-start | bytes 786440 | tf_op jit(solution)/shard_map/ppermute | solution.py:497
  24.3 0.0 collective-permute-done.1.refs_3_
  24.3 0.0 collective-permute-done.2.refs_4_
  24.4 0.4 turn_weights.2.refs_5_.refs_10_
  24.8 0.0 copy-start.4
  24.9 11.7 %collective-permute-start.8 = (f32[160,128]{1,0:T(8,128)S(1)}, f32[160,128]{1,0:T(8,128)S(1)}, u32[]{:S(2)}, u32[]{:S(2)}) collective-permute-start(f32[160,128]{1,0:T(8,128)S(1)} %bitcast.47), channel_id=1, source_target_pairs={{0,8},{8,16},{16,24},{24,25},{25,17},{17,9},{9,1},{1,2},{2,10},{10... | collective-permute-start | bytes 245768 | tf_op jit(solution)/shard_map/ppermute | solution.py:516
  36.6 0.0 collective-permute-start.3
  36.6 4.5 %collective-permute-done.4.refs_1_ = f32[512,128]{1,0:T(8,128)S(1)} collective-permute-done((f32[512,128]{1,0:T(8,128)}, f32[512,128]{1,0:T(8,128)S(1)}, u32[]{:S(2)}, u32[]{:S(2)}) %collective-permute-start.4) | collective-permute-done | bytes 262176 | tf_op jit(solution)/shard_map/ppermute | solution.py:497
  41.1 0.0 collective-permute-start.11
  41.1 0.0 collective-permute-done.6.refs_2_
  41.1 0.0 collective-permute-done.7.refs_3_
  41.1 2.0 %adjoint_mix.1.refs_2_.refs_4_ = f32[64,32,128]{2,1,0:T(8,128)S(1)} custom-call(f32[128,128]{1,0:T(8,128)S(1)} %copy.13.matrix, f32[16,128]{1,0:T(8,128)S(1)} %slice_add_fusion.refs_0_.depths, f32[512,128]{1,0:T(8,128)S(1)} %copy-done.4, f32[512,128]{1,0:T(8,128)S(1)} %collective-permute-done.4.refs_1_, f32[512,128]{1,0:T(8,128)S(1)} %collective-permute-done.6.refs_2_, ...), custom_call_target="tpu_custom_call" | custom-call | tf_op jit(solution)/shard_map/adjoint_mix/pallas_call | solution.py:238
  43.2 0.0 collective-permute-done.3
  43.2 0.0 collective-permute-done.8.refs_6_.refs_11_
  43.2 9.0 %collective-permute-start.9 = (f32[256,128]{1,0:T(8,128)S(1)}, f32[256,128]{1,0:T(8,128)S(1)}, u32[]{:S(2)}, u32[]{:S(2)}) collective-permute-start(f32[256,128]{1,0:T(8,128)S(1)} %bitcast.42), channel_id=1, source_target_pairs={{0,8},{8,16},{16,24},{24,25},{25,17},{17,9},{9,1},{1,2},{2,10},{10... | collective-permute-start | bytes 393224 | tf_op jit(solution)/shard_map/ppermute | solution.py:516
  52.2 0.0 collective-permute-start.10
  52.3 1.2 %collective-permute-done.11.refs_3_ = f32[256,128]{1,0:T(8,128)S(1)} collective-permute-done((f32[256,128]{1,0:T(8,128)S(1)}, f32[256,128]{1,0:T(8,128)S(1)}, u32[]{:S(2)}, u32[]{:S(2)}) %collective-permute-start.11) | collective-permute-done | bytes 131104 | tf_op jit(solution)/shard_map/ppermute | solution.py:497
  53.5 1.3 %collective-permute-done.9.refs_3_.refs_5_ = f32[256,128]{1,0:T(8,128)S(1)} collective-permute-done((f32[256,128]{1,0:T(8,128)S(1)}, f32[256,128]{1,0:T(8,128)S(1)}, u32[]{:S(2)}, u32[]{:S(2)}) %collective-permute-start.9) | collective-permute-done | bytes 131104 | tf_op jit(solution)/shard_map/ppermute | solution.py:516
  54.8 2.4 %collective-permute-done.10.refs_4_.refs_6_ = f32[256,128]{1,0:T(8,128)S(1)} collective-permute-done((f32[256,128]{1,0:T(8,128)S(1)}, f32[256,128]{1,0:T(8,128)S(1)}, u32[]{:S(2)}, u32[]{:S(2)}) %collective-permute-start.10) | collective-permute-done | bytes 131104 | tf_op jit(solution)/shard_map/ppermute | solution.py:516
  57.2 1.9 %collective-permute-start.12 = (f32[264,128]{1,0:T(8,128)S(1)}, f32[264,128]{1,0:T(8,128)S(1)}, u32[]{:S(2)}, u32[]{:S(2)}) collective-permute-start(f32[264,128]{1,0:T(8,128)S(1)} %pad_maximum_fusion), channel_id=1, source_target_pairs={{4,0},{0,4},{5,1},{1,5},{6,2},{2,6},{7,3},{3,7},{12,8},{8,12},{13,... | collective-permute-start | bytes 405512 | tf_op jit(solution)/shard_map/ppermute | solution.py:511
  59.1 1.5 %collective-permute-start.13 = (f32[256,128]{1,0:T(8,128)S(1)}, f32[256,128]{1,0:T(8,128)S(1)}, u32[]{:S(2)}, u32[]{:S(2)}) collective-permute-start(f32[256,128]{1,0:T(8,128)S(1)} %get-tuple-element.88), channel_id=1, source_target_pairs={{0,8},{8,16},{16,24},{24,0},{1,9},{9,17},{17,25},{25,1},{2,10},{10... | collective-permute-start | bytes 393224 | tf_op jit(solution)/shard_map/ppermute | solution.py:497
  60.6 2.3 %collective-permute-start.14 = (f32[256,128]{1,0:T(8,128)S(1)}, f32[256,128]{1,0:T(8,128)S(1)}, u32[]{:S(2)}, u32[]{:S(2)}) collective-permute-start(f32[256,128]{1,0:T(8,128)S(1)} %get-tuple-element.89), channel_id=1, source_target_pairs={{0,24},{8,0},{16,8},{24,16},{1,25},{9,1},{17,9},{25,17},{2,26},{10... | collective-permute-start | bytes 393224 | tf_op jit(solution)/shard_map/ppermute | solution.py:497
  63.0 3.4 %spread_mix.2 = (f32[256,128]{1,0:T(8,128)S(1)}, f32[256,128]{1,0:T(8,128)S(1)}, f32[256,128]{1,0:T(8,128)S(1)}, f32[256,128]{1,0:T(8,128)S(1)}) custom-call(f32[128,128]{1,0:T(8,128)S(1)} %get-tuple-element.127.matrix, f32[16,128]{1,0:T(8,128)S(1)} %slice_add_fusion.refs_0_.depths, f32[16,128]{1,0:T(8,128)S(1)} %split.44.refs_1_, ...), custom_call_target="tpu_custom_call" | custom-call | tf_op jit(solution)/shard_map/spread_mix/pallas_call | solution.py:411
  66.3 0.1 collective-permute-start.20
  66.4 1.0 %collective-permute-done.13.refs_4_ = f32[256,128]{1,0:T(8,128)S(1)} collective-permute-done((f32[256,128]{1,0:T(8,128)S(1)}, f32[256,128]{1,0:T(8,128)S(1)}, u32[]{:S(2)}, u32[]{:S(2)}) %collective-permute-start.13) | collective-permute-done | bytes 131104 | tf_op jit(solution)/shard_map/ppermute | solution.py:497
  67.4 0.0 collective-permute-done.14.refs_5_
  67.4 0.0 collective-permute-done.12
  67.5 0.4 turn_weights.3.refs_13_
  67.9 0.1 collective-permute-start.15
  68.0 2.0 %collective-permute-start.16 = (f32[160,128]{1,0:T(8,128)S(1)}, f32[160,128]{1,0:T(8,128)S(1)}, u32[]{:S(2)}, u32[]{:S(2)}) collective-permute-start(f32[160,128]{1,0:T(8,128)S(1)} %pad_maximum_fusion.7), channel_id=1, source_target_pairs={{0,8},{8,16},{16,24},{24,25},{25,17},{17,9},{9,1},{1,2},{2,10},{10... | collective-permute-start | bytes 245768 | tf_op jit(solution)/shard_map/ppermute | solution.py:516
  70.0 1.7 %collective-permute-start.21 = (f32[256,128]{1,0:T(8,128)S(1)}, f32[256,128]{1,0:T(8,128)S(1)}, u32[]{:S(2)}, u32[]{:S(2)}) collective-permute-start(f32[256,128]{1,0:T(8,128)S(1)} %get-tuple-element.99), channel_id=1, source_target_pairs={{0,8},{8,16},{16,24},{24,0},{1,9},{9,17},{17,25},{25,1},{2,10},{10... | collective-permute-start | bytes 393224 | tf_op jit(solution)/shard_map/ppermute | solution.py:497
  71.7 2.1 %collective-permute-start.22 = (f32[256,128]{1,0:T(8,128)S(1)}, f32[256,128]{1,0:T(8,128)S(1)}, u32[]{:S(2)}, u32[]{:S(2)}) collective-permute-start(f32[256,128]{1,0:T(8,128)S(1)} %get-tuple-element.100), channel_id=1, source_target_pairs={{0,24},{8,0},{16,8},{24,16},{1,25},{9,1},{17,9},{25,17},{2,26},{10... | collective-permute-start | bytes 393224 | tf_op jit(solution)/shard_map/ppermute | solution.py:497
  73.9 0.0 collective-permute-done.16
  73.9 3.5 %collective-permute-done.15 = f32[168,128]{1,0:T(8,128)S(1)} collective-permute-done((f32[168,128]{1,0:T(8,128)S(1)}, f32[168,128]{1,0:T(8,128)S(1)}, u32[]{:S(2)}, u32[]{:S(2)}) %collective-permute-start.15) | collective-permute-done | bytes 86048 | tf_op jit(solution)/shard_map/ppermute | solution.py:516
  77.4 0.0 copy-start
  77.4 0.0 copy-start.1
  77.4 3.5 %spread_mix.3 = (f32[256,128]{1,0:T(8,128)S(1)}, f32[256,128]{1,0:T(8,128)S(1)}, f32[256,128]{1,0:T(8,128)S(1)}, f32[256,128]{1,0:T(8,128)S(1)}) custom-call(f32[128,128]{1,0:T(8,128)S(1)} %get-tuple-element.127.matrix, f32[16,128]{1,0:T(8,128)S(1)} %slice_add_fusion.refs_0_.depths, f32[16,128]{1,0:T(8,128)S(1)} %split.44.refs_1_, ...), custom_call_target="tpu_custom_call" | custom-call | tf_op jit(solution)/shard_map/spread_mix/pallas_call | solution.py:411
  80.9 1.0 %collective-permute-start.17 = (f32[256,128]{1,0:T(8,128)S(1)}, f32[256,128]{1,0:T(8,128)S(1)}, u32[]{:S(2)}, u32[]{:S(2)}) collective-permute-start(f32[256,128]{1,0:T(8,128)S(1)} %get-tuple-element.95), channel_id=1, source_target_pairs={{0,16},{8,24},{16,0},{24,8},{1,17},{9,25},{17,1},{25,9},{2,18},{10... | collective-permute-start | bytes 393224 | tf_op jit(solution)/shard_map/ppermute | solution.py:497
  81.9 1.3 %collective-permute-start.18 = (f32[256,128]{1,0:T(8,128)S(1)}, f32[256,128]{1,0:T(8,128)S(1)}, u32[]{:S(2)}, u32[]{:S(2)}) collective-permute-start(f32[256,128]{1,0:T(8,128)S(1)} %get-tuple-element.96), channel_id=1, source_target_pairs={{0,8},{8,16},{16,24},{24,0},{1,9},{9,17},{17,25},{25,1},{2,10},{10... | collective-permute-start | bytes 393224 | tf_op jit(solution)/shard_map/ppermute | solution.py:497
  83.2 0.0 collective-permute-done.20.refs_1_
  83.2 2.5 %collective-permute-start.19 = (f32[256,128]{1,0:T(8,128)S(1)}, f32[256,128]{1,0:T(8,128)S(1)}, u32[]{:S(2)}, u32[]{:S(2)}) collective-permute-start(f32[256,128]{1,0:T(8,128)S(1)} %get-tuple-element.97), channel_id=1, source_target_pairs={{0,24},{8,0},{16,8},{24,16},{1,25},{9,1},{17,9},{25,17},{2,26},{10... | collective-permute-start | bytes 393224 | tf_op jit(solution)/shard_map/ppermute | solution.py:497
  85.8 0.0 collective-permute-done.21.refs_2_
  85.8 0.0 collective-permute-done.22.refs_3_
  85.8 1.4 %result.2.refs_4_ = f32[2,16,64,128]{3,2,1,0:T(8,128)} custom-call(f32[2,16,64,128]{3,2,1,0:T(8,128)S(1)} %copy-done, s32[16,64,128]{2,1,0:T(8,128)S(1)} %copy-done.1, f32[256,128]{1,0:T(8,128)S(1)} %get-tuple-element.85.refs_0_, f32[256,128]{1,0:T(8,128)S(1)} %collective-permute-done.20.refs_1_, f32[256,128]{1,0:T(8,128)S(1)} %collective-permute-done.21.refs_2_, ...), custom_call_target="tpu_custom_call" | custom-call | tf_op jit(solution)/shard_map/result/pallas_call | solution.py:470
  87.2 4.2 %collective-permute-done.17.refs_1_ = f32[256,128]{1,0:T(8,128)S(1)} collective-permute-done((f32[256,128]{1,0:T(8,128)S(1)}, f32[256,128]{1,0:T(8,128)S(1)}, u32[]{:S(2)}, u32[]{:S(2)}) %collective-permute-start.17) | collective-permute-done | bytes 131104 | tf_op jit(solution)/shard_map/ppermute | solution.py:497
  91.5 0.0 collective-permute-done.18.refs_2_
  91.5 0.0 collective-permute-done.19.refs_3_
  91.5 1.4 %result.3 = f32[2,16,64,128]{3,2,1,0:T(8,128)} custom-call(f32[2,16,64,128]{3,2,1,0:T(8,128)S(1)} %copy-done, s32[16,64,128]{2,1,0:T(8,128)S(1)} %copy-done.1, f32[256,128]{1,0:T(8,128)S(1)} %get-tuple-element.94.refs_0_, f32[256,128]{1,0:T(8,128)S(1)} %collective-permute-done.17.refs_1_, ...), custom_call_target="tpu_custom_call", output_to_operand_aliasing={{}: (6, {})} | custom-call | tf_op jit(solution)/shard_map/result/pallas_call | solution.py:470
  (39 shorter events, 0.3 us)
Async XLA Ops:
  0.0 11.5 %copy-start.3 = (f32[16,64,128]{2,1,0:T(8,128)S(1)}, f32[16,64,128]{2,1,0:T(8,128)}, u32[]{:S(2)}) copy-start(f32[16,64,128]{2,1,0:T(8,128)} %along_j.3) | copy-start | bytes 1572868
  0.0 11.5 %copy-start.2 = (f32[16,64,128]{2,1,0:T(8,128)S(1)}, f32[16,64,128]{2,1,0:T(8,128)}, u32[]{:S(2)}) copy-start(f32[16,64,128]{2,1,0:T(8,128)} %along_i.3) | copy-start | bytes 1572868
  3.6 17.8 %collective-permute-start = (f32[336,128]{1,0:T(8,128)}, f32[336,128]{1,0:T(8,128)S(1)}, u32[]{:S(2)}, u32[]{:S(2)}) collective-permute-start(f32[336,128]{1,0:T(8,128)} %get-tuple-element.54), channel_id=1, source_target_pairs={{0,16},{8,24},{16,0},{24,8},{1,17},{9,25},{17,1},{25,9},{2,18},{10... | collective-permute-start | bytes 516104 | tf_op jit(solution)/shard_map/ppermute | solution.py:497
  7.7 16.7 %collective-permute-start.1 = (f32[336,128]{1,0:T(8,128)}, f32[336,128]{1,0:T(8,128)S(1)}, u32[]{:S(2)}, u32[]{:S(2)}) collective-permute-start(f32[336,128]{1,0:T(8,128)} %get-tuple-element.55), channel_id=1, source_target_pairs={{0,8},{8,16},{16,24},{24,0},{1,9},{9,17},{17,25},{25,1},{2,10},{10... | collective-permute-start | bytes 516104 | tf_op jit(solution)/shard_map/ppermute | solution.py:497
  9.3 15.1 %collective-permute-start.2 = (f32[336,128]{1,0:T(8,128)}, f32[336,128]{1,0:T(8,128)S(1)}, u32[]{:S(2)}, u32[]{:S(2)}) collective-permute-start(f32[336,128]{1,0:T(8,128)} %get-tuple-element.56), channel_id=1, source_target_pairs={{0,24},{8,0},{16,8},{24,16},{1,25},{9,1},{17,9},{25,17},{2,26},{10... | collective-permute-start | bytes 516104 | tf_op jit(solution)/shard_map/ppermute | solution.py:497
  11.6 5.9 %collective-permute-start.5 = (f32[256,128]{1,0:T(8,128)S(1)}, f32[256,128]{1,0:T(8,128)S(1)}, u32[]{:S(2)}, u32[]{:S(2)}) collective-permute-start(f32[256,128]{1,0:T(8,128)S(1)} %pad_maximum_fusion.1), channel_id=1, source_target_pairs={{4,0},{0,4},{5,1},{1,5},{6,2},{2,6},{7,3},{3,7},{12,8},{8,12},{13,... | collective-permute-start | bytes 393224 | tf_op jit(solution)/shard_map/ppermute | solution.py:511
  16.4 0.8 copy-start.6
  16.4 24.7 %collective-permute-start.4 = (f32[512,128]{1,0:T(8,128)}, f32[512,128]{1,0:T(8,128)S(1)}, u32[]{:S(2)}, u32[]{:S(2)}) collective-permute-start(f32[512,128]{1,0:T(8,128)} %get-tuple-element.60), channel_id=1, source_target_pairs={{0,16},{8,24},{16,0},{24,8},{1,17},{9,25},{17,1},{25,9},{2,18},{10... | collective-permute-start | bytes 786440 | tf_op jit(solution)/shard_map/ppermute | solution.py:497
  17.3 1.0 %copy-start.8 = (f32[512,128]{1,0:T(8,128)S(1)}, f32[512,128]{1,0:T(8,128)}, u32[]{:S(2)}) copy-start(f32[512,128]{1,0:T(8,128)} %get-tuple-element.61) | copy-start | bytes 786436
  18.2 22.9 %collective-permute-start.6 = (f32[512,128]{1,0:T(8,128)S(1)}, f32[512,128]{1,0:T(8,128)S(1)}, u32[]{:S(2)}, u32[]{:S(2)}) collective-permute-start(f32[512,128]{1,0:T(8,128)S(1)} %copy-done.8), channel_id=1, source_target_pairs={{0,8},{8,16},{16,24},{24,0},{1,9},{9,17},{17,25},{25,1},{2,10},{10... | collective-permute-start | bytes 786440 | tf_op jit(solution)/shard_map/ppermute | solution.py:497
  18.2 3.2 %copy-start.7 = (f32[512,128]{1,0:T(8,128)S(1)}, f32[512,128]{1,0:T(8,128)}, u32[]{:S(2)}) copy-start(f32[512,128]{1,0:T(8,128)} %get-tuple-element.62) | copy-start | bytes 786436
  18.2 6.1 %copy-start.5 = (f32[336,128]{1,0:T(8,128)S(1)}, f32[336,128]{1,0:T(8,128)}, u32[]{:S(2)}) copy-start(f32[336,128]{1,0:T(8,128)} %get-tuple-element.53.refs_1_) | copy-start | bytes 516100
  21.4 19.7 %collective-permute-start.7 = (f32[512,128]{1,0:T(8,128)S(1)}, f32[512,128]{1,0:T(8,128)S(1)}, u32[]{:S(2)}, u32[]{:S(2)}) collective-permute-start(f32[512,128]{1,0:T(8,128)S(1)} %copy-done.7), channel_id=1, source_target_pairs={{0,24},{8,0},{16,8},{24,16},{1,25},{9,1},{17,9},{25,17},{2,26},{10... | collective-permute-start | bytes 786440 | tf_op jit(solution)/shard_map/ppermute | solution.py:497
  24.8 16.3 %copy-start.4 = (f32[512,128]{1,0:T(8,128)S(1)}, f32[512,128]{1,0:T(8,128)}, u32[]{:S(2)}) copy-start(f32[512,128]{1,0:T(8,128)} %get-tuple-element.59.refs_0_) | copy-start | bytes 786436
  24.9 18.3 %collective-permute-start.8 = (f32[160,128]{1,0:T(8,128)S(1)}, f32[160,128]{1,0:T(8,128)S(1)}, u32[]{:S(2)}, u32[]{:S(2)}) collective-permute-start(f32[160,128]{1,0:T(8,128)S(1)} %bitcast.47), channel_id=1, source_target_pairs={{0,8},{8,16},{16,24},{24,25},{25,17},{17,9},{9,1},{1,2},{2,10},{10... | collective-permute-start | bytes 245768 | tf_op jit(solution)/shard_map/ppermute | solution.py:516
  36.6 6.6 %collective-permute-start.3 = (f32[176,128]{1,0:T(8,128)S(1)}, f32[176,128]{1,0:T(8,128)S(1)}, u32[]{:S(2)}, u32[]{:S(2)}) collective-permute-start(f32[176,128]{1,0:T(8,128)S(1)} %pad_maximum_fusion.3), channel_id=1, source_target_pairs={{8,0},{16,8},{24,16},{25,24},{17,25},{9,17},{1,9},{2,1},{10,2},{18... | collective-permute-start | bytes 270344 | tf_op jit(solution)/shard_map/ppermute | solution.py:516
  41.1 12.3 %collective-permute-start.11 = (f32[256,128]{1,0:T(8,128)S(1)}, f32[256,128]{1,0:T(8,128)S(1)}, u32[]{:S(2)}, u32[]{:S(2)}) collective-permute-start(f32[256,128]{1,0:T(8,128)S(1)} %get-tuple-element.75), channel_id=1, source_target_pairs={{0,16},{8,24},{16,0},{24,8},{1,17},{9,25},{17,1},{25,9},{2,18},{10... | collective-permute-start | bytes 393224 | tf_op jit(solution)/shard_map/ppermute | solution.py:497
  43.2 11.5 %collective-permute-start.9 = (f32[256,128]{1,0:T(8,128)S(1)}, f32[256,128]{1,0:T(8,128)S(1)}, u32[]{:S(2)}, u32[]{:S(2)}) collective-permute-start(f32[256,128]{1,0:T(8,128)S(1)} %bitcast.42), channel_id=1, source_target_pairs={{0,8},{8,16},{16,24},{24,25},{25,17},{17,9},{9,1},{1,2},{2,10},{10... | collective-permute-start | bytes 393224 | tf_op jit(solution)/shard_map/ppermute | solution.py:516
  52.2 5.0 %collective-permute-start.10 = (f32[256,128]{1,0:T(8,128)S(1)}, f32[256,128]{1,0:T(8,128)S(1)}, u32[]{:S(2)}, u32[]{:S(2)}) collective-permute-start(f32[256,128]{1,0:T(8,128)S(1)} %bitcast.41), channel_id=1, source_target_pairs={{8,0},{16,8},{24,16},{25,24},{17,25},{9,17},{1,9},{2,1},{10,2},{18... | collective-permute-start | bytes 393224 | tf_op jit(solution)/shard_map/ppermute | solution.py:516
  57.2 10.2 %collective-permute-start.12 = (f32[264,128]{1,0:T(8,128)S(1)}, f32[264,128]{1,0:T(8,128)S(1)}, u32[]{:S(2)}, u32[]{:S(2)}) collective-permute-start(f32[264,128]{1,0:T(8,128)S(1)} %pad_maximum_fusion), channel_id=1, source_target_pairs={{4,0},{0,4},{5,1},{1,5},{6,2},{2,6},{7,3},{3,7},{12,8},{8,12},{13,... | collective-permute-start | bytes 405512 | tf_op jit(solution)/shard_map/ppermute | solution.py:511
  59.1 8.3 %collective-permute-start.13 = (f32[256,128]{1,0:T(8,128)S(1)}, f32[256,128]{1,0:T(8,128)S(1)}, u32[]{:S(2)}, u32[]{:S(2)}) collective-permute-start(f32[256,128]{1,0:T(8,128)S(1)} %get-tuple-element.88), channel_id=1, source_target_pairs={{0,8},{8,16},{16,24},{24,0},{1,9},{9,17},{17,25},{25,1},{2,10},{10... | collective-permute-start | bytes 393224 | tf_op jit(solution)/shard_map/ppermute | solution.py:497
  60.6 6.8 %collective-permute-start.14 = (f32[256,128]{1,0:T(8,128)S(1)}, f32[256,128]{1,0:T(8,128)S(1)}, u32[]{:S(2)}, u32[]{:S(2)}) collective-permute-start(f32[256,128]{1,0:T(8,128)S(1)} %get-tuple-element.89), channel_id=1, source_target_pairs={{0,24},{8,0},{16,8},{24,16},{1,25},{9,1},{17,9},{25,17},{2,26},{10... | collective-permute-start | bytes 393224 | tf_op jit(solution)/shard_map/ppermute | solution.py:497
  66.3 16.9 %collective-permute-start.20 = (f32[256,128]{1,0:T(8,128)S(1)}, f32[256,128]{1,0:T(8,128)S(1)}, u32[]{:S(2)}, u32[]{:S(2)}) collective-permute-start(f32[256,128]{1,0:T(8,128)S(1)} %get-tuple-element.98), channel_id=1, source_target_pairs={{0,16},{8,24},{16,0},{24,8},{1,17},{9,25},{17,1},{25,9},{2,18},{10... | collective-permute-start | bytes 393224 | tf_op jit(solution)/shard_map/ppermute | solution.py:497
  67.9 9.4 %collective-permute-start.15 = (f32[168,128]{1,0:T(8,128)S(1)}, f32[168,128]{1,0:T(8,128)S(1)}, u32[]{:S(2)}, u32[]{:S(2)}) collective-permute-start(f32[168,128]{1,0:T(8,128)S(1)} %pad_maximum_fusion.6), channel_id=1, source_target_pairs={{8,0},{16,8},{24,16},{25,24},{17,25},{9,17},{1,9},{2,1},{10,2},{18... | collective-permute-start | bytes 258056 | tf_op jit(solution)/shard_map/ppermute | solution.py:516
  68.0 5.8 %collective-permute-start.16 = (f32[160,128]{1,0:T(8,128)S(1)}, f32[160,128]{1,0:T(8,128)S(1)}, u32[]{:S(2)}, u32[]{:S(2)}) collective-permute-start(f32[160,128]{1,0:T(8,128)S(1)} %pad_maximum_fusion.7), channel_id=1, source_target_pairs={{0,8},{8,16},{16,24},{24,25},{25,17},{17,9},{9,1},{1,2},{2,10},{10... | collective-permute-start | bytes 245768 | tf_op jit(solution)/shard_map/ppermute | solution.py:516
  70.0 15.7 %collective-permute-start.21 = (f32[256,128]{1,0:T(8,128)S(1)}, f32[256,128]{1,0:T(8,128)S(1)}, u32[]{:S(2)}, u32[]{:S(2)}) collective-permute-start(f32[256,128]{1,0:T(8,128)S(1)} %get-tuple-element.99), channel_id=1, source_target_pairs={{0,8},{8,16},{16,24},{24,0},{1,9},{9,17},{17,25},{25,1},{2,10},{10... | collective-permute-start | bytes 393224 | tf_op jit(solution)/shard_map/ppermute | solution.py:497
  71.7 14.1 %collective-permute-start.22 = (f32[256,128]{1,0:T(8,128)S(1)}, f32[256,128]{1,0:T(8,128)S(1)}, u32[]{:S(2)}, u32[]{:S(2)}) collective-permute-start(f32[256,128]{1,0:T(8,128)S(1)} %get-tuple-element.100), channel_id=1, source_target_pairs={{0,24},{8,0},{16,8},{24,16},{1,25},{9,1},{17,9},{25,17},{2,26},{10... | collective-permute-start | bytes 393224 | tf_op jit(solution)/shard_map/ppermute | solution.py:497
  77.4 8.4 %copy-start = (f32[2,16,64,128]{3,2,1,0:T(8,128)S(1)}, f32[2,16,64,128]{3,2,1,0:T(8,128)}, u32[]{:S(2)}) copy-start(f32[2,16,64,128]{3,2,1,0:T(8,128)} %gain.2) | copy-start | bytes 3145732
  77.4 8.4 %copy-start.1 = (s32[16,64,128]{2,1,0:T(8,128)S(1)}, s32[16,64,128]{2,1,0:T(8,128)}, u32[]{:S(2)}) copy-start(s32[16,64,128]{2,1,0:T(8,128)} %mask.5) | copy-start | bytes 1572868
  80.9 10.5 %collective-permute-start.17 = (f32[256,128]{1,0:T(8,128)S(1)}, f32[256,128]{1,0:T(8,128)S(1)}, u32[]{:S(2)}, u32[]{:S(2)}) collective-permute-start(f32[256,128]{1,0:T(8,128)S(1)} %get-tuple-element.95), channel_id=1, source_target_pairs={{0,16},{8,24},{16,0},{24,8},{1,17},{9,25},{17,1},{25,9},{2,18},{10... | collective-permute-start | bytes 393224 | tf_op jit(solution)/shard_map/ppermute | solution.py:497
  81.9 9.5 %collective-permute-start.18 = (f32[256,128]{1,0:T(8,128)S(1)}, f32[256,128]{1,0:T(8,128)S(1)}, u32[]{:S(2)}, u32[]{:S(2)}) collective-permute-start(f32[256,128]{1,0:T(8,128)S(1)} %get-tuple-element.96), channel_id=1, source_target_pairs={{0,8},{8,16},{16,24},{24,0},{1,9},{9,17},{17,25},{25,1},{2,10},{10... | collective-permute-start | bytes 393224 | tf_op jit(solution)/shard_map/ppermute | solution.py:497
  83.2 8.2 %collective-permute-start.19 = (f32[256,128]{1,0:T(8,128)S(1)}, f32[256,128]{1,0:T(8,128)S(1)}, u32[]{:S(2)}, u32[]{:S(2)}) collective-permute-start(f32[256,128]{1,0:T(8,128)S(1)} %get-tuple-element.97), channel_id=1, source_target_pairs={{0,24},{8,0},{16,8},{24,16},{1,25},{9,1},{17,9},{25,17},{2,26},{10... | collective-permute-start | bytes 393224 | tf_op jit(solution)/shard_map/ppermute | solution.py:497

commit v9 on v8

--- a/solution.py
+++ b/solution.py
@@ -563,14 +563,12 @@
     forward = jnp.concatenate([by_device[:, t].reshape(2 * levels, order) for t in to], axis=0)
 
     scaled[1], outer_messages = lax.optimization_barrier((scaled[1], outer_messages))
-    early = shift(outer_messages[1], devices // 2)
+    outer_parts = exchange(outer_messages)
     mixed = adjoint_mix(adjoint, depth, scaled, length, width)
     edges = flat(mixed[:, :STEPS]), flat(mixed[:, -STEPS:])
     edges, inner_weights = lax.optimization_barrier((edges, (here, left, right)))
     left, right = halo_j(*edges)
-    left, right, outer_messages, early = lax.optimization_barrier((left, right, outer_messages, early))
-    own, _, *others = outer_messages
-    outer_parts = [own, early] + [shift(x, d) for x, d in zip(others, distances(devices)[2:])]
+    left, right, outer_parts = lax.optimization_barrier((left, right, outer_parts))
     field = [(list(range(length)), mixed, left, right)]
     weights = [(inner_rows, *inner_weights)]
     depths = [depth, right_depth]

time: 93.1 us -> 97.3 us (1.045)
  starting transfers between devices: 49.8 us -> 52.3 us
  waiting for transfers between devices: 19.2 us -> 20.8 us
    ppermute x15, starting transfers between devices: 23.5 us -> 32 us  [shift(): lax.ppermute(x, 'lev', [(k, (k + d) % devices) for k in range(devices)])]
    ppermute x3, starting transfers between devices: 22.7 us -> 16.6 us  [halo_j(): lax.ppermute(last, ('lev', 'gy'), ahead)]
    ppermute x15, waiting for transfers between devices: 11.9 us -> 14.8 us  [shift(): lax.ppermute(x, 'lev', [(k, (k + d) % devices) for k in range(devices)])]
    ppermute x3, waiting for transfers between devices: 1.32 us -> 0.01 us  [halo_j(): lax.ppermute(last, ('lev', 'gy'), ahead)]
  transfers between devices with their start and end apart: 23 -> 23, of which waited for: 8 -> 7; matrix products, arithmetic and copies ran while one was open for 0% -> 0% of each run, Pallas kernels for 18% -> 17%
where the time goes in v9:
time: 97.3 us; the launch traced here: 97.1 us
  starting transfers between devices  52.3 us (54%)
  Pallas kernels  21.6 us (22%)
  waiting for transfers between devices  20.8 us (21%)
  local copies, waits for them, and re-layouts  1.87 us (2%)
    ppermute x15, starting transfers between devices, shift(): lax.ppermute(x, 'lev', [(k, (k + d) % devices) for k in range(devices)])  32 us
    ppermute x3, starting transfers between devices, halo_j(): lax.ppermute(last, ('lev', 'gy'), ahead)  16.6 us
    ppermute x15, waiting for transfers between devices, shift(): lax.ppermute(x, 'lev', [(k, (k + d) % devices) for k in range(devices)])  14.8 us
    pallas_call x2, Pallas kernels, spread_mix(): pl.pallas_call(kernel, in_specs=[vmem()] * (1 + len(arrays)), out_specs=[...  6.91 us
    ppermute x3, waiting for transfers between devices, halo_j(): lax.ppermute(first, ('lev', 'gy'), back)  6.01 us
    pallas_call x2, Pallas kernels, weight_messages(): pl.pallas_call(functools.partial(pack_kernel, starts, rows, len(mask)), i...  5.75 us
    pallas_call x1, Pallas kernels, scaled_messages(): pl.pallas_call(scaled_kernel, in_specs=[pl.BlockSpec(memory_space=pl.ANY)...  3.25 us
    ppermute x2, starting transfers between devices, halo_i(): both = lax.ppermute(jnp.concatenate([first, last], axis=0), 'gx', up)  2.99 us
  transfers between devices with their start and end apart: 23, of which 7 were waited for; matrix products, arithmetic and copies ran while one was open for 0% of the time, Pallas kernels for 17%

profile of v9, /device:TPU:0, one launch (start us, length us, event | category | flops | bytes accessed | tf_op | source)
XLA Modules:
  0.0 97.1 jit_solution(4111823841125008145)
XLA Ops:
  0.0 3.6 %weight_messages.2 = (f32[336,128]{1,0:T(8,128)}, f32[336,128]{1,0:T(8,128)}, f32[336,128]{1,0:T(8,128)}, f32[336,128]{1,0:T(8,128)}) custom-call(f32[16,64,128]{2,1,0:T(8,128)} %along_i.3, f32[16,64,128]{2,1,0:T(8,128)} %along_j.3, s32[16,64,128]{2,1,0:T(8,128)} %mask.5), custom_call_target="tpu_custom_call" | custom-call | tf_op jit(solution)/shard_map/weight_messages/pallas_call | solution.py:198
  3.6 4.1 %collective-permute-start = (f32[336,128]{1,0:T(8,128)}, f32[336,128]{1,0:T(8,128)S(1)}, u32[]{:S(2)}, u32[]{:S(2)}) collective-permute-start(f32[336,128]{1,0:T(8,128)} %get-tuple-element.54), channel_id=1, source_target_pairs={{0,16},{8,24},{16,0},{24,8},{1,17},{9,25},{17,1},{25,9},{2,18},{10... | collective-permute-start | bytes 516104 | tf_op jit(solution)/shard_map/ppermute | solution.py:497
  7.7 1.6 %collective-permute-start.1 = (f32[336,128]{1,0:T(8,128)}, f32[336,128]{1,0:T(8,128)S(1)}, u32[]{:S(2)}, u32[]{:S(2)}) collective-permute-start(f32[336,128]{1,0:T(8,128)} %get-tuple-element.55), channel_id=1, source_target_pairs={{0,8},{8,16},{16,24},{24,0},{1,9},{9,17},{17,25},{25,1},{2,10},{10... | collective-permute-start | bytes 516104 | tf_op jit(solution)/shard_map/ppermute | solution.py:497
  9.3 2.2 %collective-permute-start.2 = (f32[336,128]{1,0:T(8,128)}, f32[336,128]{1,0:T(8,128)S(1)}, u32[]{:S(2)}, u32[]{:S(2)}) collective-permute-start(f32[336,128]{1,0:T(8,128)} %get-tuple-element.56), channel_id=1, source_target_pairs={{0,24},{8,0},{16,8},{24,16},{1,25},{9,1},{17,9},{25,17},{2,26},{10... | collective-permute-start | bytes 516104 | tf_op jit(solution)/shard_map/ppermute | solution.py:497
  11.6 1.6 %collective-permute-start.5 = (f32[256,128]{1,0:T(8,128)S(1)}, f32[256,128]{1,0:T(8,128)S(1)}, u32[]{:S(2)}, u32[]{:S(2)}) collective-permute-start(f32[256,128]{1,0:T(8,128)S(1)} %pad_maximum_fusion.1), channel_id=1, source_target_pairs={{4,0},{0,4},{5,1},{1,5},{6,2},{2,6},{7,3},{3,7},{12,8},{8,12},{13,... | collective-permute-start | bytes 393224 | tf_op jit(solution)/shard_map/ppermute | solution.py:511
  13.1 3.3 %scaled_messages.1 = (f32[512,128]{1,0:T(8,128)}, f32[512,128]{1,0:T(8,128)}, f32[512,128]{1,0:T(8,128)}, f32[512,128]{1,0:T(8,128)}) custom-call(f32[2,16,64,128]{3,2,1,0:T(8,128)} %increment, f32[2,16,64,128]{3,2,1,0:T(8,128)} %gain.2, s32[16,64,128]{2,1,0:T(8,128)} %mask.5), custom_call_target="tpu_custom_call" | custom-call | tf_op jit(solution)/shard_map/scaled_messages/pallas_call | solution.py:121
  16.4 0.0 copy-start.6
  16.4 0.1 collective-permute-start.4
  16.5 0.7 copy-done.6
  17.3 0.0 copy-start.8
  17.3 0.1 copy.13.matrix
  17.4 0.0 collective-permute-done.5
  17.4 0.8 copy-done.8
  18.2 0.0 collective-permute-start.6
  18.3 2.2 %weight_messages.3 = (f32[256,128]{1,0:T(8,128)S(1)}, f32[256,128]{1,0:T(8,128)S(1)}, f32[256,128]{1,0:T(8,128)S(1)}, f32[256,128]{1,0:T(8,128)S(1)}) custom-call(f32[16,64,128]{2,1,0:T(8,128)S(1)} %copy-done.2, f32[16,64,128]{2,1,0:T(8,128)S(1)} %copy-done.3, f32[128,128]{1,0:T(8,128)S(1)} %get-tuple-element.65.refs_0_, ...), custom_call_target="tpu_custom_call" | custom-call | tf_op jit(solution)/shard_map/weight_messages/pallas_call | solution.py:198
  20.4 0.9 collective-permute-done.refs_2_
  21.4 2.9 %collective-permute-start.7 = (f32[512,128]{1,0:T(8,128)S(1)}, f32[512,128]{1,0:T(8,128)S(1)}, u32[]{:S(2)}, u32[]{:S(2)}) collective-permute-start(f32[512,128]{1,0:T(8,128)S(1)} %copy-done.7), channel_id=1, source_target_pairs={{0,24},{8,0},{16,8},{24,16},{1,25},{9,1},{17,9},{25,17},{2,26},{10... | collective-permute-start | bytes 786440 | tf_op jit(solution)/shard_map/ppermute | solution.py:497
  24.3 0.0 collective-permute-done.1.refs_3_
  24.3 0.0 collective-permute-done.2.refs_4_
  24.4 0.4 turn_weights.2.refs_5_.refs_10_
  24.8 0.0 copy-start.4
  24.9 11.7 %collective-permute-start.8 = (f32[160,128]{1,0:T(8,128)S(1)}, f32[160,128]{1,0:T(8,128)S(1)}, u32[]{:S(2)}, u32[]{:S(2)}) collective-permute-start(f32[160,128]{1,0:T(8,128)S(1)} %bitcast.47), channel_id=1, source_target_pairs={{0,8},{8,16},{16,24},{24,25},{25,17},{17,9},{9,1},{1,2},{2,10},{10... | collective-permute-start | bytes 245768 | tf_op jit(solution)/shard_map/ppermute | solution.py:516
  36.6 0.0 collective-permute-start.3
  36.6 4.5 %collective-permute-done.4.refs_1_ = f32[512,128]{1,0:T(8,128)S(1)} collective-permute-done((f32[512,128]{1,0:T(8,128)}, f32[512,128]{1,0:T(8,128)S(1)}, u32[]{:S(2)}, u32[]{:S(2)}) %collective-permute-start.4) | collective-permute-done | bytes 262176 | tf_op jit(solution)/shard_map/ppermute | solution.py:497
  41.1 0.0 collective-permute-start.11
  41.1 0.0 collective-permute-done.6.refs_2_
  41.1 8.4 %collective-permute-start.12 = (f32[256,128]{1,0:T(8,128)S(1)}, f32[256,128]{1,0:T(8,128)S(1)}, u32[]{:S(2)}, u32[]{:S(2)}) collective-permute-start(f32[256,128]{1,0:T(8,128)S(1)} %get-tuple-element.76), channel_id=1, source_target_pairs={{0,8},{8,16},{16,24},{24,0},{1,9},{9,17},{17,25},{25,1},{2,10},{10... | collective-permute-start | bytes 393224 | tf_op jit(solution)/shard_map/ppermute | solution.py:497
  49.5 0.0 collective-permute-done.7.refs_3_
  49.5 0.0 collective-permute-start.13
  49.5 2.0 %adjoint_mix.1.refs_2_.refs_4_ = f32[64,32,128]{2,1,0:T(8,128)S(1)} custom-call(f32[128,128]{1,0:T(8,128)S(1)} %copy.13.matrix, f32[16,128]{1,0:T(8,128)S(1)} %slice_add_fusion.refs_0_.depths, f32[512,128]{1,0:T(8,128)S(1)} %copy-done.4, f32[512,128]{1,0:T(8,128)S(1)} %collective-permute-done.4.refs_1_, f32[512,128]{1,0:T(8,128)S(1)} %collective-permute-done.6.refs_2_, ...), custom_call_target="tpu_custom_call" | custom-call | tf_op jit(solution)/shard_map/adjoint_mix/pallas_call | solution.py:238
  51.5 0.0 collective-permute-done.3
  51.6 0.0 collective-permute-done.8.refs_6_.refs_11_
  51.6 3.5 %collective-permute-start.9 = (f32[256,128]{1,0:T(8,128)S(1)}, f32[256,128]{1,0:T(8,128)S(1)}, u32[]{:S(2)}, u32[]{:S(2)}) collective-permute-start(f32[256,128]{1,0:T(8,128)S(1)} %bitcast.42), channel_id=1, source_target_pairs={{0,8},{8,16},{16,24},{24,25},{25,17},{17,9},{9,1},{1,2},{2,10},{10... | collective-permute-start | bytes 393224 | tf_op jit(solution)/shard_map/ppermute | solution.py:516
  55.1 0.0 collective-permute-start.10
  55.1 2.0 %collective-permute-done.11.refs_3_ = f32[256,128]{1,0:T(8,128)S(1)} collective-permute-done((f32[256,128]{1,0:T(8,128)S(1)}, f32[256,128]{1,0:T(8,128)S(1)}, u32[]{:S(2)}, u32[]{:S(2)}) %collective-permute-start.11) | collective-permute-done | bytes 131104 | tf_op jit(solution)/shard_map/ppermute | solution.py:497
  57.1 0.0 collective-permute-done.12.refs_4_
  57.1 2.0 %collective-permute-done.13.refs_5_ = f32[256,128]{1,0:T(8,128)S(1)} collective-permute-done((f32[256,128]{1,0:T(8,128)S(1)}, f32[256,128]{1,0:T(8,128)S(1)}, u32[]{:S(2)}, u32[]{:S(2)}) %collective-permute-start.13) | collective-permute-done | bytes 131104 | tf_op jit(solution)/shard_map/ppermute | solution.py:497
  59.1 0.0 collective-permute-done.9.refs_3_.refs_5_
  59.1 1.7 %collective-permute-done.10.refs_4_.refs_6_ = f32[256,128]{1,0:T(8,128)S(1)} collective-permute-done((f32[256,128]{1,0:T(8,128)S(1)}, f32[256,128]{1,0:T(8,128)S(1)}, u32[]{:S(2)}, u32[]{:S(2)}) %collective-permute-start.10) | collective-permute-done | bytes 131104 | tf_op jit(solution)/shard_map/ppermute | solution.py:516
  60.9 1.4 %collective-permute-start.14 = (f32[264,128]{1,0:T(8,128)S(1)}, f32[264,128]{1,0:T(8,128)S(1)}, u32[]{:S(2)}, u32[]{:S(2)}) collective-permute-start(f32[264,128]{1,0:T(8,128)S(1)} %pad_maximum_fusion), channel_id=1, source_target_pairs={{4,0},{0,4},{5,1},{1,5},{6,2},{2,6},{7,3},{3,7},{12,8},{8,12},{13,... | collective-permute-start | bytes 405512 | tf_op jit(solution)/shard_map/ppermute | solution.py:511
  62.3 3.4 %spread_mix.2 = (f32[256,128]{1,0:T(8,128)S(1)}, f32[256,128]{1,0:T(8,128)S(1)}, f32[256,128]{1,0:T(8,128)S(1)}, f32[256,128]{1,0:T(8,128)S(1)}) custom-call(f32[128,128]{1,0:T(8,128)S(1)} %get-tuple-element.127.matrix, f32[16,128]{1,0:T(8,128)S(1)} %slice_add_fusion.refs_0_.depths, f32[16,128]{1,0:T(8,128)S(1)} %split.44.refs_1_, ...), custom_call_target="tpu_custom_call" | custom-call | tf_op jit(solution)/shard_map/spread_mix/pallas_call | solution.py:411
  65.7 3.7 %collective-permute-start.20 = (f32[256,128]{1,0:T(8,128)S(1)}, f32[256,128]{1,0:T(8,128)S(1)}, u32[]{:S(2)}, u32[]{:S(2)}) collective-permute-start(f32[256,128]{1,0:T(8,128)S(1)} %get-tuple-element.98), channel_id=1, source_target_pairs={{0,16},{8,24},{16,0},{24,8},{1,17},{9,25},{17,1},{25,9},{2,18},{10... | collective-permute-start | bytes 393224 | tf_op jit(solution)/shard_map/ppermute | solution.py:497
  69.4 0.0 collective-permute-done.14
  69.5 0.4 turn_weights.3.refs_13_
  70.0 0.7 collective-permute-start.15
  70.7 1.4 %collective-permute-start.16 = (f32[160,128]{1,0:T(8,128)S(1)}, f32[160,128]{1,0:T(8,128)S(1)}, u32[]{:S(2)}, u32[]{:S(2)}) collective-permute-start(f32[160,128]{1,0:T(8,128)S(1)} %pad_maximum_fusion.7), channel_id=1, source_target_pairs={{0,8},{8,16},{16,24},{24,25},{25,17},{17,9},{9,1},{1,2},{2,10},{10... | collective-permute-start | bytes 245768 | tf_op jit(solution)/shard_map/ppermute | solution.py:516
  72.1 1.0 %collective-permute-start.21 = (f32[256,128]{1,0:T(8,128)S(1)}, f32[256,128]{1,0:T(8,128)S(1)}, u32[]{:S(2)}, u32[]{:S(2)}) collective-permute-start(f32[256,128]{1,0:T(8,128)S(1)} %get-tuple-element.99), channel_id=1, source_target_pairs={{0,8},{8,16},{16,24},{24,0},{1,9},{9,17},{17,25},{25,1},{2,10},{10... | collective-permute-start | bytes 393224 | tf_op jit(solution)/shard_map/ppermute | solution.py:497
  73.1 2.8 %collective-permute-start.22 = (f32[256,128]{1,0:T(8,128)S(1)}, f32[256,128]{1,0:T(8,128)S(1)}, u32[]{:S(2)}, u32[]{:S(2)}) collective-permute-start(f32[256,128]{1,0:T(8,128)S(1)} %get-tuple-element.100), channel_id=1, source_target_pairs={{0,24},{8,0},{16,8},{24,16},{1,25},{9,1},{17,9},{25,17},{2,26},{10... | collective-permute-start | bytes 393224 | tf_op jit(solution)/shard_map/ppermute | solution.py:497
  75.9 0.0 collective-permute-done.16
  75.9 4.3 %collective-permute-done.15 = f32[168,128]{1,0:T(8,128)S(1)} collective-permute-done((f32[168,128]{1,0:T(8,128)S(1)}, f32[168,128]{1,0:T(8,128)S(1)}, u32[]{:S(2)}, u32[]{:S(2)}) %collective-permute-start.15) | collective-permute-done | bytes 86048 | tf_op jit(solution)/shard_map/ppermute | solution.py:516
  80.2 0.0 copy-start
  80.2 0.0 copy-start.1
  80.2 3.5 %spread_mix.3 = (f32[256,128]{1,0:T(8,128)S(1)}, f32[256,128]{1,0:T(8,128)S(1)}, f32[256,128]{1,0:T(8,128)S(1)}, f32[256,128]{1,0:T(8,128)S(1)}) custom-call(f32[128,128]{1,0:T(8,128)S(1)} %get-tuple-element.127.matrix, f32[16,128]{1,0:T(8,128)S(1)} %slice_add_fusion.refs_0_.depths, f32[16,128]{1,0:T(8,128)S(1)} %split.44.refs_1_, ...), custom_call_target="tpu_custom_call" | custom-call | tf_op jit(solution)/shard_map/spread_mix/pallas_call | solution.py:411
  83.8 1.3 %collective-permute-start.17 = (f32[256,128]{1,0:T(8,128)S(1)}, f32[256,128]{1,0:T(8,128)S(1)}, u32[]{:S(2)}, u32[]{:S(2)}) collective-permute-start(f32[256,128]{1,0:T(8,128)S(1)} %get-tuple-element.95), channel_id=1, source_target_pairs={{0,16},{8,24},{16,0},{24,8},{1,17},{9,25},{17,1},{25,9},{2,18},{10... | collective-permute-start | bytes 393224 | tf_op jit(solution)/shard_map/ppermute | solution.py:497
  85.1 0.0 collective-permute-start.18
  85.1 0.0 collective-permute-done.20.refs_1_
  85.1 3.8 %collective-permute-start.19 = (f32[256,128]{1,0:T(8,128)S(1)}, f32[256,128]{1,0:T(8,128)S(1)}, u32[]{:S(2)}, u32[]{:S(2)}) collective-permute-start(f32[256,128]{1,0:T(8,128)S(1)} %get-tuple-element.97), channel_id=1, source_target_pairs={{0,24},{8,0},{16,8},{24,16},{1,25},{9,1},{17,9},{25,17},{2,26},{10... | collective-permute-start | bytes 393224 | tf_op jit(solution)/shard_map/ppermute | solution.py:497
  88.9 0.0 collective-permute-done.21.refs_2_
  88.9 0.0 collective-permute-done.22.refs_3_
  88.9 1.4 %result.2.refs_4_ = f32[2,16,64,128]{3,2,1,0:T(8,128)} custom-call(f32[2,16,64,128]{3,2,1,0:T(8,128)S(1)} %copy-done, s32[16,64,128]{2,1,0:T(8,128)S(1)} %copy-done.1, f32[256,128]{1,0:T(8,128)S(1)} %get-tuple-element.85.refs_0_, f32[256,128]{1,0:T(8,128)S(1)} %collective-permute-done.20.refs_1_, f32[256,128]{1,0:T(8,128)S(1)} %collective-permute-done.21.refs_2_, ...), custom_call_target="tpu_custom_call" | custom-call | tf_op jit(solution)/shard_map/result/pallas_call | solution.py:470
  90.3 5.3 %collective-permute-done.17.refs_1_ = f32[256,128]{1,0:T(8,128)S(1)} collective-permute-done((f32[256,128]{1,0:T(8,128)S(1)}, f32[256,128]{1,0:T(8,128)S(1)}, u32[]{:S(2)}, u32[]{:S(2)}) %collective-permute-start.17) | collective-permute-done | bytes 131104 | tf_op jit(solution)/shard_map/ppermute | solution.py:497
  95.6 0.0 collective-permute-done.18.refs_2_
  95.6 0.0 collective-permute-done.19.refs_3_
  95.6 1.4 %result.3 = f32[2,16,64,128]{3,2,1,0:T(8,128)} custom-call(f32[2,16,64,128]{3,2,1,0:T(8,128)S(1)} %copy-done, s32[16,64,128]{2,1,0:T(8,128)S(1)} %copy-done.1, f32[256,128]{1,0:T(8,128)S(1)} %get-tuple-element.94.refs_0_, f32[256,128]{1,0:T(8,128)S(1)} %collective-permute-done.17.refs_1_, ...), custom_call_target="tpu_custom_call", output_to_operand_aliasing={{}: (6, {})} | custom-call | tf_op jit(solution)/shard_map/result/pallas_call | solution.py:470
  (39 shorter events, 0.3 us)
Async XLA Ops:
  0.0 11.5 %copy-start.3 = (f32[16,64,128]{2,1,0:T(8,128)S(1)}, f32[16,64,128]{2,1,0:T(8,128)}, u32[]{:S(2)}) copy-start(f32[16,64,128]{2,1,0:T(8,128)} %along_j.3) | copy-start | bytes 1572868
  0.0 11.5 %copy-start.2 = (f32[16,64,128]{2,1,0:T(8,128)S(1)}, f32[16,64,128]{2,1,0:T(8,128)}, u32[]{:S(2)}) copy-start(f32[16,64,128]{2,1,0:T(8,128)} %along_i.3) | copy-start | bytes 1572868
  3.6 17.8 %collective-permute-start = (f32[336,128]{1,0:T(8,128)}, f32[336,128]{1,0:T(8,128)S(1)}, u32[]{:S(2)}, u32[]{:S(2)}) collective-permute-start(f32[336,128]{1,0:T(8,128)} %get-tuple-element.54), channel_id=1, source_target_pairs={{0,16},{8,24},{16,0},{24,8},{1,17},{9,25},{17,1},{25,9},{2,18},{10... | collective-permute-start | bytes 516104 | tf_op jit(solution)/shard_map/ppermute | solution.py:497
  7.7 16.7 %collective-permute-start.1 = (f32[336,128]{1,0:T(8,128)}, f32[336,128]{1,0:T(8,128)S(1)}, u32[]{:S(2)}, u32[]{:S(2)}) collective-permute-start(f32[336,128]{1,0:T(8,128)} %get-tuple-element.55), channel_id=1, source_target_pairs={{0,8},{8,16},{16,24},{24,0},{1,9},{9,17},{17,25},{25,1},{2,10},{10... | collective-permute-start | bytes 516104 | tf_op jit(solution)/shard_map/ppermute | solution.py:497
  9.3 15.1 %collective-permute-start.2 = (f32[336,128]{1,0:T(8,128)}, f32[336,128]{1,0:T(8,128)S(1)}, u32[]{:S(2)}, u32[]{:S(2)}) collective-permute-start(f32[336,128]{1,0:T(8,128)} %get-tuple-element.56), channel_id=1, source_target_pairs={{0,24},{8,0},{16,8},{24,16},{1,25},{9,1},{17,9},{25,17},{2,26},{10... | collective-permute-start | bytes 516104 | tf_op jit(solution)/shard_map/ppermute | solution.py:497
  11.6 5.9 %collective-permute-start.5 = (f32[256,128]{1,0:T(8,128)S(1)}, f32[256,128]{1,0:T(8,128)S(1)}, u32[]{:S(2)}, u32[]{:S(2)}) collective-permute-start(f32[256,128]{1,0:T(8,128)S(1)} %pad_maximum_fusion.1), channel_id=1, source_target_pairs={{4,0},{0,4},{5,1},{1,5},{6,2},{2,6},{7,3},{3,7},{12,8},{8,12},{13,... | collective-permute-start | bytes 393224 | tf_op jit(solution)/shard_map/ppermute | solution.py:511
  16.4 0.8 copy-start.6
  16.4 24.7 %collective-permute-start.4 = (f32[512,128]{1,0:T(8,128)}, f32[512,128]{1,0:T(8,128)S(1)}, u32[]{:S(2)}, u32[]{:S(2)}) collective-permute-start(f32[512,128]{1,0:T(8,128)} %get-tuple-element.60), channel_id=1, source_target_pairs={{0,16},{8,24},{16,0},{24,8},{1,17},{9,25},{17,1},{25,9},{2,18},{10... | collective-permute-start | bytes 786440 | tf_op jit(solution)/shard_map/ppermute | solution.py:497
  17.3 1.0 copy-start.8
  18.2 22.9 %collective-permute-start.6 = (f32[512,128]{1,0:T(8,128)S(1)}, f32[512,128]{1,0:T(8,128)S(1)}, u32[]{:S(2)}, u32[]{:S(2)}) collective-permute-start(f32[512,128]{1,0:T(8,128)S(1)} %copy-done.8), channel_id=1, source_target_pairs={{0,8},{8,16},{16,24},{24,0},{1,9},{9,17},{17,25},{25,1},{2,10},{10... | collective-permute-start | bytes 786440 | tf_op jit(solution)/shard_map/ppermute | solution.py:497
  18.2 3.2 %copy-start.7 = (f32[512,128]{1,0:T(8,128)S(1)}, f32[512,128]{1,0:T(8,128)}, u32[]{:S(2)}) copy-start(f32[512,128]{1,0:T(8,128)} %get-tuple-element.62) | copy-start | bytes 786436
  18.2 6.1 %copy-start.5 = (f32[336,128]{1,0:T(8,128)S(1)}, f32[336,128]{1,0:T(8,128)}, u32[]{:S(2)}) copy-start(f32[336,128]{1,0:T(8,128)} %get-tuple-element.53.refs_1_) | copy-start | bytes 516100
  21.4 28.1 %collective-permute-start.7 = (f32[512,128]{1,0:T(8,128)S(1)}, f32[512,128]{1,0:T(8,128)S(1)}, u32[]{:S(2)}, u32[]{:S(2)}) collective-permute-start(f32[512,128]{1,0:T(8,128)S(1)} %copy-done.7), channel_id=1, source_target_pairs={{0,24},{8,0},{16,8},{24,16},{1,25},{9,1},{17,9},{25,17},{2,26},{10... | collective-permute-start | bytes 786440 | tf_op jit(solution)/shard_map/ppermute | solution.py:497
  24.8 24.7 %copy-start.4 = (f32[512,128]{1,0:T(8,128)S(1)}, f32[512,128]{1,0:T(8,128)}, u32[]{:S(2)}) copy-start(f32[512,128]{1,0:T(8,128)} %get-tuple-element.59.refs_0_) | copy-start | bytes 786436
  24.9 26.7 %collective-permute-start.8 = (f32[160,128]{1,0:T(8,128)S(1)}, f32[160,128]{1,0:T(8,128)S(1)}, u32[]{:S(2)}, u32[]{:S(2)}) collective-permute-start(f32[160,128]{1,0:T(8,128)S(1)} %bitcast.47), channel_id=1, source_target_pairs={{0,8},{8,16},{16,24},{24,25},{25,17},{17,9},{9,1},{1,2},{2,10},{10... | collective-permute-start | bytes 245768 | tf_op jit(solution)/shard_map/ppermute | solution.py:516
  36.6 15.0 %collective-permute-start.3 = (f32[176,128]{1,0:T(8,128)S(1)}, f32[176,128]{1,0:T(8,128)S(1)}, u32[]{:S(2)}, u32[]{:S(2)}) collective-permute-start(f32[176,128]{1,0:T(8,128)S(1)} %pad_maximum_fusion.3), channel_id=1, source_target_pairs={{8,0},{16,8},{24,16},{25,24},{17,25},{9,17},{1,9},{2,1},{10,2},{18... | collective-permute-start | bytes 270344 | tf_op jit(solution)/shard_map/ppermute | solution.py:516
  41.1 16.0 %collective-permute-start.11 = (f32[256,128]{1,0:T(8,128)S(1)}, f32[256,128]{1,0:T(8,128)S(1)}, u32[]{:S(2)}, u32[]{:S(2)}) collective-permute-start(f32[256,128]{1,0:T(8,128)S(1)} %get-tuple-element.75), channel_id=1, source_target_pairs={{0,16},{8,24},{16,0},{24,8},{1,17},{9,25},{17,1},{25,9},{2,18},{10... | collective-permute-start | bytes 393224 | tf_op jit(solution)/shard_map/ppermute | solution.py:497
  41.1 16.0 %collective-permute-start.12 = (f32[256,128]{1,0:T(8,128)S(1)}, f32[256,128]{1,0:T(8,128)S(1)}, u32[]{:S(2)}, u32[]{:S(2)}) collective-permute-start(f32[256,128]{1,0:T(8,128)S(1)} %get-tuple-element.76), channel_id=1, source_target_pairs={{0,8},{8,16},{16,24},{24,0},{1,9},{9,17},{17,25},{25,1},{2,10},{10... | collective-permute-start | bytes 393224 | tf_op jit(solution)/shard_map/ppermute | solution.py:497
  49.5 9.7 %collective-permute-start.13 = (f32[256,128]{1,0:T(8,128)S(1)}, f32[256,128]{1,0:T(8,128)S(1)}, u32[]{:S(2)}, u32[]{:S(2)}) collective-permute-start(f32[256,128]{1,0:T(8,128)S(1)} %get-tuple-element.77), channel_id=1, source_target_pairs={{0,24},{8,0},{16,8},{24,16},{1,25},{9,1},{17,9},{25,17},{2,26},{10... | collective-permute-start | bytes 393224 | tf_op jit(solution)/shard_map/ppermute | solution.py:497
  51.6 7.6 %collective-permute-start.9 = (f32[256,128]{1,0:T(8,128)S(1)}, f32[256,128]{1,0:T(8,128)S(1)}, u32[]{:S(2)}, u32[]{:S(2)}) collective-permute-start(f32[256,128]{1,0:T(8,128)S(1)} %bitcast.42), channel_id=1, source_target_pairs={{0,8},{8,16},{16,24},{24,25},{25,17},{17,9},{9,1},{1,2},{2,10},{10... | collective-permute-start | bytes 393224 | tf_op jit(solution)/shard_map/ppermute | solution.py:516
  55.1 5.8 %collective-permute-start.10 = (f32[256,128]{1,0:T(8,128)S(1)}, f32[256,128]{1,0:T(8,128)S(1)}, u32[]{:S(2)}, u32[]{:S(2)}) collective-permute-start(f32[256,128]{1,0:T(8,128)S(1)} %bitcast.41), channel_id=1, source_target_pairs={{8,0},{16,8},{24,16},{25,24},{17,25},{9,17},{1,9},{2,1},{10,2},{18... | collective-permute-start | bytes 393224 | tf_op jit(solution)/shard_map/ppermute | solution.py:516
  60.9 8.5 %collective-permute-start.14 = (f32[264,128]{1,0:T(8,128)S(1)}, f32[264,128]{1,0:T(8,128)S(1)}, u32[]{:S(2)}, u32[]{:S(2)}) collective-permute-start(f32[264,128]{1,0:T(8,128)S(1)} %pad_maximum_fusion), channel_id=1, source_target_pairs={{4,0},{0,4},{5,1},{1,5},{6,2},{2,6},{7,3},{3,7},{12,8},{8,12},{13,... | collective-permute-start | bytes 405512 | tf_op jit(solution)/shard_map/ppermute | solution.py:511
  65.7 19.4 %collective-permute-start.20 = (f32[256,128]{1,0:T(8,128)S(1)}, f32[256,128]{1,0:T(8,128)S(1)}, u32[]{:S(2)}, u32[]{:S(2)}) collective-permute-start(f32[256,128]{1,0:T(8,128)S(1)} %get-tuple-element.98), channel_id=1, source_target_pairs={{0,16},{8,24},{16,0},{24,8},{1,17},{9,25},{17,1},{25,9},{2,18},{10... | collective-permute-start | bytes 393224 | tf_op jit(solution)/shard_map/ppermute | solution.py:497
  70.0 10.2 %collective-permute-start.15 = (f32[168,128]{1,0:T(8,128)S(1)}, f32[168,128]{1,0:T(8,128)S(1)}, u32[]{:S(2)}, u32[]{:S(2)}) collective-permute-start(f32[168,128]{1,0:T(8,128)S(1)} %pad_maximum_fusion.6), channel_id=1, source_target_pairs={{8,0},{16,8},{24,16},{25,24},{17,25},{9,17},{1,9},{2,1},{10,2},{18... | collective-permute-start | bytes 258056 | tf_op jit(solution)/shard_map/ppermute | solution.py:516
  70.7 5.2 %collective-permute-start.16 = (f32[160,128]{1,0:T(8,128)S(1)}, f32[160,128]{1,0:T(8,128)S(1)}, u32[]{:S(2)}, u32[]{:S(2)}) collective-permute-start(f32[160,128]{1,0:T(8,128)S(1)} %pad_maximum_fusion.7), channel_id=1, source_target_pairs={{0,8},{8,16},{16,24},{24,25},{25,17},{17,9},{9,1},{1,2},{2,10},{10... | collective-permute-start | bytes 245768 | tf_op jit(solution)/shard_map/ppermute | solution.py:516
  72.1 16.8 %collective-permute-start.21 = (f32[256,128]{1,0:T(8,128)S(1)}, f32[256,128]{1,0:T(8,128)S(1)}, u32[]{:S(2)}, u32[]{:S(2)}) collective-permute-start(f32[256,128]{1,0:T(8,128)S(1)} %get-tuple-element.99), channel_id=1, source_target_pairs={{0,8},{8,16},{16,24},{24,0},{1,9},{9,17},{17,25},{25,1},{2,10},{10... | collective-permute-start | bytes 393224 | tf_op jit(solution)/shard_map/ppermute | solution.py:497
  73.1 15.8 %collective-permute-start.22 = (f32[256,128]{1,0:T(8,128)S(1)}, f32[256,128]{1,0:T(8,128)S(1)}, u32[]{:S(2)}, u32[]{:S(2)}) collective-permute-start(f32[256,128]{1,0:T(8,128)S(1)} %get-tuple-element.100), channel_id=1, source_target_pairs={{0,24},{8,0},{16,8},{24,16},{1,25},{9,1},{17,9},{25,17},{2,26},{10... | collective-permute-start | bytes 393224 | tf_op jit(solution)/shard_map/ppermute | solution.py:497
  80.2 8.7 %copy-start = (f32[2,16,64,128]{3,2,1,0:T(8,128)S(1)}, f32[2,16,64,128]{3,2,1,0:T(8,128)}, u32[]{:S(2)}) copy-start(f32[2,16,64,128]{3,2,1,0:T(8,128)} %gain.2) | copy-start | bytes 3145732
  80.2 8.7 %copy-start.1 = (s32[16,64,128]{2,1,0:T(8,128)S(1)}, s32[16,64,128]{2,1,0:T(8,128)}, u32[]{:S(2)}) copy-start(s32[16,64,128]{2,1,0:T(8,128)} %mask.5) | copy-start | bytes 1572868
  83.8 11.8 %collective-permute-start.17 = (f32[256,128]{1,0:T(8,128)S(1)}, f32[256,128]{1,0:T(8,128)S(1)}, u32[]{:S(2)}, u32[]{:S(2)}) collective-permute-start(f32[256,128]{1,0:T(8,128)S(1)} %get-tuple-element.95), channel_id=1, source_target_pairs={{0,16},{8,24},{16,0},{24,8},{1,17},{9,25},{17,1},{25,9},{2,18},{10... | collective-permute-start | bytes 393224 | tf_op jit(solution)/shard_map/ppermute | solution.py:497
  85.1 10.5 %collective-permute-start.18 = (f32[256,128]{1,0:T(8,128)S(1)}, f32[256,128]{1,0:T(8,128)S(1)}, u32[]{:S(2)}, u32[]{:S(2)}) collective-permute-start(f32[256,128]{1,0:T(8,128)S(1)} %get-tuple-element.96), channel_id=1, source_target_pairs={{0,8},{8,16},{16,24},{24,0},{1,9},{9,17},{17,25},{25,1},{2,10},{10... | collective-permute-start | bytes 393224 | tf_op jit(solution)/shard_map/ppermute | solution.py:497
  85.1 10.5 %collective-permute-start.19 = (f32[256,128]{1,0:T(8,128)S(1)}, f32[256,128]{1,0:T(8,128)S(1)}, u32[]{:S(2)}, u32[]{:S(2)}) collective-permute-start(f32[256,128]{1,0:T(8,128)S(1)} %get-tuple-element.97), channel_id=1, source_target_pairs={{0,24},{8,0},{16,8},{24,16},{1,25},{9,1},{17,9},{25,17},{2,26},{10... | collective-permute-start | bytes 393224 | tf_op jit(solution)/shard_map/ppermute | solution.py:497

commit v10 on v9

--- a/solution.py
+++ b/solution.py
@@ -28,7 +28,7 @@
 
 
 def distances(devices):
-    return [0, devices // 2] + [d for d in range(1, devices) if d != devices // 2]
+    return list(range(devices))
 
 
 def position():
@@ -562,22 +562,23 @@
     adjoint = jnp.concatenate([by_device[:, s].reshape(2 * levels, order) for s in source], axis=0).T
     forward = jnp.concatenate([by_device[:, t].reshape(2 * levels, order) for t in to], axis=0)
 
-    scaled[1], outer_messages = lax.optimization_barrier((scaled[1], outer_messages))
-    outer_parts = exchange(outer_messages)
+    middle = devices // 2
+    scaled, outer_messages = lax.optimization_barrier((scaled, outer_messages))
+    early = shift(outer_messages[middle], middle)
     mixed = adjoint_mix(adjoint, depth, scaled, length, width)
     edges = flat(mixed[:, :STEPS]), flat(mixed[:, -STEPS:])
     edges, inner_weights = lax.optimization_barrier((edges, (here, left, right)))
     left, right = halo_j(*edges)
-    left, right, outer_parts = lax.optimization_barrier((left, right, outer_parts))
+    left, right, outer_messages, early = lax.optimization_barrier((left, right, outer_messages, early))
+    outer_parts = [
+        early if d == middle else shift(outer_messages[d], d) if d else outer_messages[0] for d in range(devices)
+    ]
     field = [(list(range(length)), mixed, left, right)]
     weights = [(inner_rows, *inner_weights)]
     depths = [depth, right_depth]
     inner_mixed = spread_mix([inner_rows], forward, depths, field, weights, devices)
     _, upper, lower = lax.optimization_barrier((left, mixed[:STEPS], mixed[-STEPS:]))
     _, outer_parts = lax.optimization_barrier((inner_mixed[0], outer_parts))
-    inner_mixed = exchange(inner_mixed)
-    out = result((inner,), norm_gain, sea_mask, inner_mixed, None)
-
     above, below = halo_i(
         jnp.concatenate([flat(upper), depth[:STEPS]], axis=0),
         jnp.concatenate([flat(lower), depth[-STEPS:]], axis=0),
@@ -597,7 +598,11 @@
     weights.append((outer_rows, here, left, right))
     field.append((list(range(-STEPS, 0)) + list(range(length, length + STEPS)), halo, halo_left, halo_right))
     depths += [halo_depth, right_halo_depth]
-    outer_mixed = exchange(spread_mix(windows, forward, depths, field, weights, devices))
+    outer_mixed = spread_mix(windows, forward, depths, field, weights, devices)
+    _, last = lax.optimization_barrier((outer_mixed[0], inner_mixed[-1]))
+    inner_mixed = exchange(list(inner_mixed[:-1]) + [last])
+    out = result((inner,), norm_gain, sea_mask, inner_mixed, None)
+    outer_mixed = exchange(outer_mixed)
     return result(outer, norm_gain, sea_mask, outer_mixed, out)
 
 

time: 97.3 us -> 94.7 us (0.973)
  waiting for transfers between devices: 20.8 us -> 18.8 us
    ppermute x3, starting transfers between devices: 16.6 us -> 19.2 us  [halo_j(): lax.ppermute(last, ('lev', 'gy'), ahead)]
    ppermute x15, starting transfers between devices: 32 us -> 30 us  [shift(): lax.ppermute(x, 'lev', [(k, (k + d) % devices) for k in range(devices)])]
    ppermute x15, waiting for transfers between devices: 14.8 us -> 13.2 us  [shift(): lax.ppermute(x, 'lev', [(k, (k + d) % devices) for k in range(devices)])]
    ppermute x3, waiting for transfers between devices: 6.01 us -> 4.92 us  [halo_j(): lax.ppermute(first, ('lev', 'gy'), back)]
  transfers between devices with their start and end apart: 23 -> 23, of which waited for: 7 -> 9; matrix products, arithmetic and copies ran while one was open for 0% -> 0% of each run, Pallas kernels for 17% -> 18%
where the time goes in v10:
time: 94.7 us; the launch traced here: 94.4 us
  starting transfers between devices  52.4 us (55%)
  Pallas kernels  21.6 us (23%)
  waiting for transfers between devices  18.8 us (20%)
  local copies, waits for them, and re-layouts  1.24 us (1%)
    ppermute x15, starting transfers between devices, shift(): lax.ppermute(x, 'lev', [(k, (k + d) % devices) for k in range(devices)])  30 us
    ppermute x3, starting transfers between devices, halo_j(): lax.ppermute(last, ('lev', 'gy'), ahead)  19.2 us
    ppermute x15, waiting for transfers between devices, shift(): lax.ppermute(x, 'lev', [(k, (k + d) % devices) for k in range(devices)])  13.2 us
    pallas_call x2, Pallas kernels, spread_mix(): pl.pallas_call(kernel, in_specs=[vmem()] * (1 + len(arrays)), out_specs=[...  6.91 us
    pallas_call x2, Pallas kernels, weight_messages(): pl.pallas_call(functools.partial(pack_kernel, starts, rows, len(mask)), i...  5.75 us
    ppermute x3, waiting for transfers between devices, halo_j(): lax.ppermute(first, ('lev', 'gy'), back)  4.92 us
    pallas_call x1, Pallas kernels, scaled_messages(): pl.pallas_call(scaled_kernel, in_specs=[pl.BlockSpec(memory_space=pl.ANY)...  3.25 us
    ppermute x2, starting transfers between devices, halo_i(): both = lax.ppermute(jnp.concatenate([first, last], axis=0), 'gx', up)  3.12 us
  transfers between devices with their start and end apart: 23, of which 9 were waited for; matrix products, arithmetic and copies ran while one was open for 0% of the time, Pallas kernels for 18%

profile of v10, /device:TPU:0, one launch (start us, length us, event | category | flops | bytes accessed | tf_op | source)
XLA Modules:
  0.0 94.4 jit_solution(13641639755402657816)
XLA Ops:
  0.0 3.6 %weight_messages.2 = (f32[336,128]{1,0:T(8,128)}, f32[336,128]{1,0:T(8,128)}, f32[336,128]{1,0:T(8,128)}, f32[336,128]{1,0:T(8,128)}) custom-call(f32[16,64,128]{2,1,0:T(8,128)} %along_i.3, f32[16,64,128]{2,1,0:T(8,128)} %along_j.3, s32[16,64,128]{2,1,0:T(8,128)} %mask.5), custom_call_target="tpu_custom_call" | custom-call | tf_op jit(solution)/shard_map/weight_messages/pallas_call | solution.py:198
  3.6 3.1 %collective-permute-start = (f32[336,128]{1,0:T(8,128)}, f32[336,128]{1,0:T(8,128)S(1)}, u32[]{:S(2)}, u32[]{:S(2)}) collective-permute-start(f32[336,128]{1,0:T(8,128)} %get-tuple-element.58), channel_id=1, source_target_pairs={{0,8},{8,16},{16,24},{24,0},{1,9},{9,17},{17,25},{25,1},{2,10},{10... | collective-permute-start | bytes 516104 | tf_op jit(solution)/shard_map/ppermute | solution.py:497
  6.7 2.6 %collective-permute-start.1 = (f32[336,128]{1,0:T(8,128)}, f32[336,128]{1,0:T(8,128)S(1)}, u32[]{:S(2)}, u32[]{:S(2)}) collective-permute-start(f32[336,128]{1,0:T(8,128)} %get-tuple-element.59), channel_id=1, source_target_pairs={{0,16},{8,24},{16,0},{24,8},{1,17},{9,25},{17,1},{25,9},{2,18},{10... | collective-permute-start | bytes 516104 | tf_op jit(solution)/shard_map/ppermute | solution.py:497
  9.2 1.3 %collective-permute-start.2 = (f32[336,128]{1,0:T(8,128)}, f32[336,128]{1,0:T(8,128)S(1)}, u32[]{:S(2)}, u32[]{:S(2)}) collective-permute-start(f32[336,128]{1,0:T(8,128)} %get-tuple-element.60), channel_id=1, source_target_pairs={{0,24},{8,0},{16,8},{24,16},{1,25},{9,1},{17,9},{25,17},{2,26},{10... | collective-permute-start | bytes 516104 | tf_op jit(solution)/shard_map/ppermute | solution.py:497
  10.6 0.0 copy-done.2
  10.7 1.6 %collective-permute-start.7 = (f32[256,128]{1,0:T(8,128)S(1)}, f32[256,128]{1,0:T(8,128)S(1)}, u32[]{:S(2)}, u32[]{:S(2)}) collective-permute-start(f32[256,128]{1,0:T(8,128)S(1)} %pad_maximum_fusion.1), channel_id=1, source_target_pairs={{4,0},{0,4},{5,1},{1,5},{6,2},{2,6},{7,3},{3,7},{12,8},{8,12},{13,... | collective-permute-start | bytes 393224 | tf_op jit(solution)/shard_map/ppermute | solution.py:511
  12.2 3.3 %scaled_messages.1 = (f32[512,128]{1,0:T(8,128)}, f32[512,128]{1,0:T(8,128)}, f32[512,128]{1,0:T(8,128)}, f32[512,128]{1,0:T(8,128)}) custom-call(f32[2,16,64,128]{3,2,1,0:T(8,128)} %increment, f32[2,16,64,128]{3,2,1,0:T(8,128)} %gain.2, s32[16,64,128]{2,1,0:T(8,128)} %mask.5), custom_call_target="tpu_custom_call" | custom-call | tf_op jit(solution)/shard_map/scaled_messages/pallas_call | solution.py:121
  15.5 0.0 copy-start.6
  15.5 0.7 collective-permute-start.4
  16.2 0.1 copy-done.6
  16.4 0.1 copy.13.matrix
  16.5 0.0 collective-permute-done.7
  16.5 0.8 copy-done.8
  17.3 0.3 collective-permute-start.5
  17.7 2.2 %weight_messages.3 = (f32[256,128]{1,0:T(8,128)S(1)}, f32[256,128]{1,0:T(8,128)S(1)}, f32[256,128]{1,0:T(8,128)S(1)}, f32[256,128]{1,0:T(8,128)S(1)}) custom-call(f32[16,64,128]{2,1,0:T(8,128)S(1)} %copy-done.2, f32[16,64,128]{2,1,0:T(8,128)S(1)} %copy-done.3, f32[128,128]{1,0:T(8,128)S(1)} %get-tuple-element.69.refs_0_, ...), custom_call_target="tpu_custom_call" | custom-call | tf_op jit(solution)/shard_map/weight_messages/pallas_call | solution.py:198
  19.9 0.0 collective-permute-done.refs_2_
  19.9 2.8 %collective-permute-start.6 = (f32[512,128]{1,0:T(8,128)S(1)}, f32[512,128]{1,0:T(8,128)S(1)}, u32[]{:S(2)}, u32[]{:S(2)}) collective-permute-start(f32[512,128]{1,0:T(8,128)S(1)} %copy-done.7), channel_id=1, source_target_pairs={{0,24},{8,0},{16,8},{24,16},{1,25},{9,1},{17,9},{25,17},{2,26},{10... | collective-permute-start | bytes 786440 | tf_op jit(solution)/shard_map/ppermute | solution.py:497
  22.7 0.0 collective-permute-done.1.refs_3_
  22.7 0.0 collective-permute-done.2.refs_4_
  22.7 0.4 turn_weights.2.refs_5_.refs_10_
  23.1 0.0 copy-start.4
  23.2 13.6 %collective-permute-start.8 = (f32[160,128]{1,0:T(8,128)S(1)}, f32[160,128]{1,0:T(8,128)S(1)}, u32[]{:S(2)}, u32[]{:S(2)}) collective-permute-start(f32[160,128]{1,0:T(8,128)S(1)} %bitcast.47), channel_id=1, source_target_pairs={{0,8},{8,16},{16,24},{24,25},{25,17},{17,9},{9,1},{1,2},{2,10},{10... | collective-permute-start | bytes 245768 | tf_op jit(solution)/shard_map/ppermute | solution.py:516
  36.8 0.0 collective-permute-start.3
  36.8 0.0 collective-permute-done.4.refs_1_
  36.8 4.5 %collective-permute-done.5.refs_2_ = f32[512,128]{1,0:T(8,128)S(1)} collective-permute-done((f32[512,128]{1,0:T(8,128)S(1)}, f32[512,128]{1,0:T(8,128)S(1)}, u32[]{:S(2)}, u32[]{:S(2)}) %collective-permute-start.5) | collective-permute-done | bytes 262176 | tf_op jit(solution)/shard_map/ppermute | solution.py:497
  41.3 0.0 collective-permute-done.6.refs_3_
  41.3 5.2 %collective-permute-start.11 = (f32[256,128]{1,0:T(8,128)S(1)}, f32[256,128]{1,0:T(8,128)S(1)}, u32[]{:S(2)}, u32[]{:S(2)}) collective-permute-start(f32[256,128]{1,0:T(8,128)S(1)} %get-tuple-element.83), channel_id=1, source_target_pairs={{0,16},{8,24},{16,0},{24,8},{1,17},{9,25},{17,1},{25,9},{2,18},{10... | collective-permute-start | bytes 393224 | tf_op jit(solution)/shard_map/ppermute | solution.py:497
  46.5 2.0 %adjoint_mix.1.refs_2_.refs_4_ = f32[64,32,128]{2,1,0:T(8,128)S(1)} custom-call(f32[128,128]{1,0:T(8,128)S(1)} %copy.13.matrix, f32[16,128]{1,0:T(8,128)S(1)} %slice_add_fusion.refs_0_.depths, f32[512,128]{1,0:T(8,128)S(1)} %copy-done.4, f32[512,128]{1,0:T(8,128)S(1)} %collective-permute-done.4.refs_1_, f32[512,128]{1,0:T(8,128)S(1)} %collective-permute-done.5.refs_2_, ...), custom_call_target="tpu_custom_call" | custom-call | tf_op jit(solution)/shard_map/adjoint_mix/pallas_call | solution.py:238
  48.5 0.0 collective-permute-done.3
  48.6 0.0 collective-permute-done.8.refs_6_.refs_11_
  48.6 3.6 %collective-permute-start.9 = (f32[256,128]{1,0:T(8,128)S(1)}, f32[256,128]{1,0:T(8,128)S(1)}, u32[]{:S(2)}, u32[]{:S(2)}) collective-permute-start(f32[256,128]{1,0:T(8,128)S(1)} %bitcast.42), channel_id=1, source_target_pairs={{0,8},{8,16},{16,24},{24,25},{25,17},{17,9},{9,1},{1,2},{2,10},{10... | collective-permute-start | bytes 393224 | tf_op jit(solution)/shard_map/ppermute | solution.py:516
  52.1 0.0 collective-permute-start.10
  52.2 2.3 %collective-permute-done.11.refs_4_ = f32[256,128]{1,0:T(8,128)S(1)} collective-permute-done((f32[256,128]{1,0:T(8,128)S(1)}, f32[256,128]{1,0:T(8,128)S(1)}, u32[]{:S(2)}, u32[]{:S(2)}) %collective-permute-start.11) | collective-permute-done | bytes 131104 | tf_op jit(solution)/shard_map/ppermute | solution.py:497
  54.5 0.2 collective-permute-done.9.refs_3_.refs_5_
  54.7 2.4 %collective-permute-done.10.refs_4_.refs_6_ = f32[256,128]{1,0:T(8,128)S(1)} collective-permute-done((f32[256,128]{1,0:T(8,128)S(1)}, f32[256,128]{1,0:T(8,128)S(1)}, u32[]{:S(2)}, u32[]{:S(2)}) %collective-permute-start.10) | collective-permute-done | bytes 131104 | tf_op jit(solution)/shard_map/ppermute | solution.py:516
  57.1 1.6 %collective-permute-start.12 = (f32[264,128]{1,0:T(8,128)S(1)}, f32[264,128]{1,0:T(8,128)S(1)}, u32[]{:S(2)}, u32[]{:S(2)}) collective-permute-start(f32[264,128]{1,0:T(8,128)S(1)} %pad_maximum_fusion), channel_id=1, source_target_pairs={{4,0},{0,4},{5,1},{1,5},{6,2},{2,6},{7,3},{3,7},{12,8},{8,12},{13,... | collective-permute-start | bytes 405512 | tf_op jit(solution)/shard_map/ppermute | solution.py:511
  58.7 0.6 collective-permute-start.13
  59.3 3.3 %collective-permute-start.14 = (f32[256,128]{1,0:T(8,128)S(1)}, f32[256,128]{1,0:T(8,128)S(1)}, u32[]{:S(2)}, u32[]{:S(2)}) collective-permute-start(f32[256,128]{1,0:T(8,128)S(1)} %get-tuple-element.96), channel_id=1, source_target_pairs={{0,24},{8,0},{16,8},{24,16},{1,25},{9,1},{17,9},{25,17},{2,26},{10... | collective-permute-start | bytes 393224 | tf_op jit(solution)/shard_map/ppermute | solution.py:497
  62.5 3.4 %spread_mix.2 = (f32[256,128]{1,0:T(8,128)S(1)}, f32[256,128]{1,0:T(8,128)S(1)}, f32[256,128]{1,0:T(8,128)S(1)}, f32[256,128]{1,0:T(8,128)S(1)}) custom-call(f32[128,128]{1,0:T(8,128)S(1)} %get-tuple-element.135.matrix, f32[16,128]{1,0:T(8,128)S(1)} %slice_add_fusion.refs_0_.depths, f32[16,128]{1,0:T(8,128)S(1)} %split.44.refs_1_, ...), custom_call_target="tpu_custom_call" | custom-call | tf_op jit(solution)/shard_map/spread_mix/pallas_call | solution.py:411
  65.9 0.1 collective-permute-start.20
  66.0 0.7 collective-permute-done.13.refs_3_
  66.7 0.0 collective-permute-done.14.refs_5_
  66.7 0.0 collective-permute-done.12
  66.8 0.4 turn_weights.3.refs_13_
  67.3 0.1 collective-permute-start.15
  67.4 2.0 %collective-permute-start.16 = (f32[160,128]{1,0:T(8,128)S(1)}, f32[160,128]{1,0:T(8,128)S(1)}, u32[]{:S(2)}, u32[]{:S(2)}) collective-permute-start(f32[160,128]{1,0:T(8,128)S(1)} %pad_maximum_fusion.7), channel_id=1, source_target_pairs={{0,8},{8,16},{16,24},{24,25},{25,17},{17,9},{9,1},{1,2},{2,10},{10... | collective-permute-start | bytes 245768 | tf_op jit(solution)/shard_map/ppermute | solution.py:516
  69.4 1.9 %collective-permute-start.21 = (f32[256,128]{1,0:T(8,128)S(1)}, f32[256,128]{1,0:T(8,128)S(1)}, u32[]{:S(2)}, u32[]{:S(2)}) collective-permute-start(f32[256,128]{1,0:T(8,128)S(1)} %get-tuple-element.106), channel_id=1, source_target_pairs={{0,16},{8,24},{16,0},{24,8},{1,17},{9,25},{17,1},{25,9},{2,18},{10... | collective-permute-start | bytes 393224 | tf_op jit(solution)/shard_map/ppermute | solution.py:497
  71.3 0.4 collective-permute-done.16
  71.7 2.5 %collective-permute-done.15 = f32[168,128]{1,0:T(8,128)S(1)} collective-permute-done((f32[168,128]{1,0:T(8,128)S(1)}, f32[168,128]{1,0:T(8,128)S(1)}, u32[]{:S(2)}, u32[]{:S(2)}) %collective-permute-start.15) | collective-permute-done | bytes 86048 | tf_op jit(solution)/shard_map/ppermute | solution.py:516
  74.2 0.0 copy-start
  74.2 0.0 copy-start.1
  74.2 3.5 %spread_mix.3 = (f32[256,128]{1,0:T(8,128)S(1)}, f32[256,128]{1,0:T(8,128)S(1)}, f32[256,128]{1,0:T(8,128)S(1)}, f32[256,128]{1,0:T(8,128)S(1)}) custom-call(f32[128,128]{1,0:T(8,128)S(1)} %get-tuple-element.135.matrix, f32[16,128]{1,0:T(8,128)S(1)} %slice_add_fusion.refs_0_.depths, f32[16,128]{1,0:T(8,128)S(1)} %split.44.refs_1_, ...), custom_call_target="tpu_custom_call" | custom-call | tf_op jit(solution)/shard_map/spread_mix/pallas_call | solution.py:411
  77.8 1.2 %collective-permute-start.22 = (f32[256,128]{1,0:T(8,128)S(1)}, f32[256,128]{1,0:T(8,128)S(1)}, u32[]{:S(2)}, u32[]{:S(2)}) collective-permute-start(f32[256,128]{1,0:T(8,128)S(1)} %get-tuple-element.108), channel_id=1, source_target_pairs={{0,24},{8,0},{16,8},{24,16},{1,25},{9,1},{17,9},{25,17},{2,26},{10... | collective-permute-start | bytes 393224 | tf_op jit(solution)/shard_map/ppermute | solution.py:497
  79.0 2.7 %collective-permute-start.17 = (f32[256,128]{1,0:T(8,128)S(1)}, f32[256,128]{1,0:T(8,128)S(1)}, u32[]{:S(2)}, u32[]{:S(2)}) collective-permute-start(f32[256,128]{1,0:T(8,128)S(1)} %get-tuple-element.102), channel_id=1, source_target_pairs={{0,8},{8,16},{16,24},{24,0},{1,9},{9,17},{17,25},{25,1},{2,10},{10... | collective-permute-start | bytes 393224 | tf_op jit(solution)/shard_map/ppermute | solution.py:497
  81.6 1.4 %collective-permute-start.18 = (f32[256,128]{1,0:T(8,128)S(1)}, f32[256,128]{1,0:T(8,128)S(1)}, u32[]{:S(2)}, u32[]{:S(2)}) collective-permute-start(f32[256,128]{1,0:T(8,128)S(1)} %get-tuple-element.103), channel_id=1, source_target_pairs={{0,16},{8,24},{16,0},{24,8},{1,17},{9,25},{17,1},{25,9},{2,18},{10... | collective-permute-start | bytes 393224 | tf_op jit(solution)/shard_map/ppermute | solution.py:497
  83.0 0.0 collective-permute-done.20.refs_1_
  83.0 2.9 %collective-permute-start.19 = (f32[256,128]{1,0:T(8,128)S(1)}, f32[256,128]{1,0:T(8,128)S(1)}, u32[]{:S(2)}, u32[]{:S(2)}) collective-permute-start(f32[256,128]{1,0:T(8,128)S(1)} %get-tuple-element.104), channel_id=1, source_target_pairs={{0,24},{8,0},{16,8},{24,16},{1,25},{9,1},{17,9},{25,17},{2,26},{10... | collective-permute-start | bytes 393224 | tf_op jit(solution)/shard_map/ppermute | solution.py:497
  85.9 0.0 collective-permute-done.21.refs_2_
  85.9 1.9 %collective-permute-done.22.refs_3_ = f32[256,128]{1,0:T(8,128)S(1)} collective-permute-done((f32[256,128]{1,0:T(8,128)S(1)}, f32[256,128]{1,0:T(8,128)S(1)}, u32[]{:S(2)}, u32[]{:S(2)}) %collective-permute-start.22) | collective-permute-done | bytes 131104 | tf_op jit(solution)/shard_map/ppermute | solution.py:497
  87.9 1.4 %result.2.refs_4_ = f32[2,16,64,128]{3,2,1,0:T(8,128)} custom-call(f32[2,16,64,128]{3,2,1,0:T(8,128)S(1)} %copy-done, s32[16,64,128]{2,1,0:T(8,128)S(1)} %copy-done.1, f32[256,128]{1,0:T(8,128)S(1)} %get-tuple-element.92.refs_0_, f32[256,128]{1,0:T(8,128)S(1)} %collective-permute-done.20.refs_1_, f32[256,128]{1,0:T(8,128)S(1)} %collective-permute-done.21.refs_2_, ...), custom_call_target="tpu_custom_call" | custom-call | tf_op jit(solution)/shard_map/result/pallas_call | solution.py:470
  89.3 0.0 collective-permute-done.17.refs_1_
  89.3 3.7 %collective-permute-done.18.refs_2_ = f32[256,128]{1,0:T(8,128)S(1)} collective-permute-done((f32[256,128]{1,0:T(8,128)S(1)}, f32[256,128]{1,0:T(8,128)S(1)}, u32[]{:S(2)}, u32[]{:S(2)}) %collective-permute-start.18) | collective-permute-done | bytes 131104 | tf_op jit(solution)/shard_map/ppermute | solution.py:497
  93.0 0.0 collective-permute-done.19.refs_3_
  93.0 1.4 %result.3 = f32[2,16,64,128]{3,2,1,0:T(8,128)} custom-call(f32[2,16,64,128]{3,2,1,0:T(8,128)S(1)} %copy-done, s32[16,64,128]{2,1,0:T(8,128)S(1)} %copy-done.1, f32[256,128]{1,0:T(8,128)S(1)} %get-tuple-element.101.refs_0_, f32[256,128]{1,0:T(8,128)S(1)} %collective-permute-done.17.refs_1_, ...), custom_call_target="tpu_custom_call", output_to_operand_aliasing={{}: (6, {})} | custom-call | tf_op jit(solution)/shard_map/result/pallas_call | solution.py:470
  (39 shorter events, 0.3 us)
Async XLA Ops:
  0.0 10.6 %copy-start.3 = (f32[16,64,128]{2,1,0:T(8,128)S(1)}, f32[16,64,128]{2,1,0:T(8,128)}, u32[]{:S(2)}) copy-start(f32[16,64,128]{2,1,0:T(8,128)} %along_j.3) | copy-start | bytes 1572868
  0.0 10.6 %copy-start.2 = (f32[16,64,128]{2,1,0:T(8,128)S(1)}, f32[16,64,128]{2,1,0:T(8,128)}, u32[]{:S(2)}) copy-start(f32[16,64,128]{2,1,0:T(8,128)} %along_i.3) | copy-start | bytes 1572868
  3.6 16.3 %collective-permute-start = (f32[336,128]{1,0:T(8,128)}, f32[336,128]{1,0:T(8,128)S(1)}, u32[]{:S(2)}, u32[]{:S(2)}) collective-permute-start(f32[336,128]{1,0:T(8,128)} %get-tuple-element.58), channel_id=1, source_target_pairs={{0,8},{8,16},{16,24},{24,0},{1,9},{9,17},{17,25},{25,1},{2,10},{10... | collective-permute-start | bytes 516104 | tf_op jit(solution)/shard_map/ppermute | solution.py:497
  6.7 16.0 %collective-permute-start.1 = (f32[336,128]{1,0:T(8,128)}, f32[336,128]{1,0:T(8,128)S(1)}, u32[]{:S(2)}, u32[]{:S(2)}) collective-permute-start(f32[336,128]{1,0:T(8,128)} %get-tuple-element.59), channel_id=1, source_target_pairs={{0,16},{8,24},{16,0},{24,8},{1,17},{9,25},{17,1},{25,9},{2,18},{10... | collective-permute-start | bytes 516104 | tf_op jit(solution)/shard_map/ppermute | solution.py:497
  9.2 13.4 %collective-permute-start.2 = (f32[336,128]{1,0:T(8,128)}, f32[336,128]{1,0:T(8,128)S(1)}, u32[]{:S(2)}, u32[]{:S(2)}) collective-permute-start(f32[336,128]{1,0:T(8,128)} %get-tuple-element.60), channel_id=1, source_target_pairs={{0,24},{8,0},{16,8},{24,16},{1,25},{9,1},{17,9},{25,17},{2,26},{10... | collective-permute-start | bytes 516104 | tf_op jit(solution)/shard_map/ppermute | solution.py:497
  10.7 5.9 %collective-permute-start.7 = (f32[256,128]{1,0:T(8,128)S(1)}, f32[256,128]{1,0:T(8,128)S(1)}, u32[]{:S(2)}, u32[]{:S(2)}) collective-permute-start(f32[256,128]{1,0:T(8,128)S(1)} %pad_maximum_fusion.1), channel_id=1, source_target_pairs={{4,0},{0,4},{5,1},{1,5},{6,2},{2,6},{7,3},{3,7},{12,8},{8,12},{13,... | collective-permute-start | bytes 393224 | tf_op jit(solution)/shard_map/ppermute | solution.py:511
  15.5 0.8 copy-start.6
  15.5 21.3 %collective-permute-start.4 = (f32[512,128]{1,0:T(8,128)}, f32[512,128]{1,0:T(8,128)S(1)}, u32[]{:S(2)}, u32[]{:S(2)}) collective-permute-start(f32[512,128]{1,0:T(8,128)} %get-tuple-element.64), channel_id=1, source_target_pairs={{0,8},{8,16},{16,24},{24,0},{1,9},{9,17},{17,25},{25,1},{2,10},{10... | collective-permute-start | bytes 786440 | tf_op jit(solution)/shard_map/ppermute | solution.py:497
  16.4 1.0 %copy-start.8 = (f32[512,128]{1,0:T(8,128)S(1)}, f32[512,128]{1,0:T(8,128)}, u32[]{:S(2)}) copy-start(f32[512,128]{1,0:T(8,128)} %get-tuple-element.65) | copy-start | bytes 786436
  17.3 24.0 %collective-permute-start.5 = (f32[512,128]{1,0:T(8,128)S(1)}, f32[512,128]{1,0:T(8,128)S(1)}, u32[]{:S(2)}, u32[]{:S(2)}) collective-permute-start(f32[512,128]{1,0:T(8,128)S(1)} %copy-done.8), channel_id=1, source_target_pairs={{0,16},{8,24},{16,0},{24,8},{1,17},{9,25},{17,1},{25,9},{2,18},{10... | collective-permute-start | bytes 786440 | tf_op jit(solution)/shard_map/ppermute | solution.py:497
  17.7 2.2 %copy-start.7 = (f32[512,128]{1,0:T(8,128)S(1)}, f32[512,128]{1,0:T(8,128)}, u32[]{:S(2)}) copy-start(f32[512,128]{1,0:T(8,128)} %get-tuple-element.66) | copy-start | bytes 786436
  17.7 5.0 %copy-start.5 = (f32[336,128]{1,0:T(8,128)S(1)}, f32[336,128]{1,0:T(8,128)}, u32[]{:S(2)}) copy-start(f32[336,128]{1,0:T(8,128)} %get-tuple-element.57.refs_1_) | copy-start | bytes 516100
  19.9 21.4 %collective-permute-start.6 = (f32[512,128]{1,0:T(8,128)S(1)}, f32[512,128]{1,0:T(8,128)S(1)}, u32[]{:S(2)}, u32[]{:S(2)}) collective-permute-start(f32[512,128]{1,0:T(8,128)S(1)} %copy-done.7), channel_id=1, source_target_pairs={{0,24},{8,0},{16,8},{24,16},{1,25},{9,1},{17,9},{25,17},{2,26},{10... | collective-permute-start | bytes 786440 | tf_op jit(solution)/shard_map/ppermute | solution.py:497
  23.1 23.4 %copy-start.4 = (f32[512,128]{1,0:T(8,128)S(1)}, f32[512,128]{1,0:T(8,128)}, u32[]{:S(2)}) copy-start(f32[512,128]{1,0:T(8,128)} %get-tuple-element.75.refs_0_) | copy-start | bytes 786436
  23.2 25.4 %collective-permute-start.8 = (f32[160,128]{1,0:T(8,128)S(1)}, f32[160,128]{1,0:T(8,128)S(1)}, u32[]{:S(2)}, u32[]{:S(2)}) collective-permute-start(f32[160,128]{1,0:T(8,128)S(1)} %bitcast.47), channel_id=1, source_target_pairs={{0,8},{8,16},{16,24},{24,25},{25,17},{17,9},{9,1},{1,2},{2,10},{10... | collective-permute-start | bytes 245768 | tf_op jit(solution)/shard_map/ppermute | solution.py:516
  36.8 11.7 %collective-permute-start.3 = (f32[176,128]{1,0:T(8,128)S(1)}, f32[176,128]{1,0:T(8,128)S(1)}, u32[]{:S(2)}, u32[]{:S(2)}) collective-permute-start(f32[176,128]{1,0:T(8,128)S(1)} %pad_maximum_fusion.3), channel_id=1, source_target_pairs={{8,0},{16,8},{24,16},{25,24},{17,25},{9,17},{1,9},{2,1},{10,2},{18... | collective-permute-start | bytes 270344 | tf_op jit(solution)/shard_map/ppermute | solution.py:516
  41.3 13.2 %collective-permute-start.11 = (f32[256,128]{1,0:T(8,128)S(1)}, f32[256,128]{1,0:T(8,128)S(1)}, u32[]{:S(2)}, u32[]{:S(2)}) collective-permute-start(f32[256,128]{1,0:T(8,128)S(1)} %get-tuple-element.83), channel_id=1, source_target_pairs={{0,16},{8,24},{16,0},{24,8},{1,17},{9,25},{17,1},{25,9},{2,18},{10... | collective-permute-start | bytes 393224 | tf_op jit(solution)/shard_map/ppermute | solution.py:497
  48.6 6.1 %collective-permute-start.9 = (f32[256,128]{1,0:T(8,128)S(1)}, f32[256,128]{1,0:T(8,128)S(1)}, u32[]{:S(2)}, u32[]{:S(2)}) collective-permute-start(f32[256,128]{1,0:T(8,128)S(1)} %bitcast.42), channel_id=1, source_target_pairs={{0,8},{8,16},{16,24},{24,25},{25,17},{17,9},{9,1},{1,2},{2,10},{10... | collective-permute-start | bytes 393224 | tf_op jit(solution)/shard_map/ppermute | solution.py:516
  52.1 5.0 %collective-permute-start.10 = (f32[256,128]{1,0:T(8,128)S(1)}, f32[256,128]{1,0:T(8,128)S(1)}, u32[]{:S(2)}, u32[]{:S(2)}) collective-permute-start(f32[256,128]{1,0:T(8,128)S(1)} %bitcast.41), channel_id=1, source_target_pairs={{8,0},{16,8},{24,16},{25,24},{17,25},{9,17},{1,9},{2,1},{10,2},{18... | collective-permute-start | bytes 393224 | tf_op jit(solution)/shard_map/ppermute | solution.py:516
  57.1 9.6 %collective-permute-start.12 = (f32[264,128]{1,0:T(8,128)S(1)}, f32[264,128]{1,0:T(8,128)S(1)}, u32[]{:S(2)}, u32[]{:S(2)}) collective-permute-start(f32[264,128]{1,0:T(8,128)S(1)} %pad_maximum_fusion), channel_id=1, source_target_pairs={{4,0},{0,4},{5,1},{1,5},{6,2},{2,6},{7,3},{3,7},{12,8},{8,12},{13,... | collective-permute-start | bytes 405512 | tf_op jit(solution)/shard_map/ppermute | solution.py:511
  58.7 8.0 %collective-permute-start.13 = (f32[256,128]{1,0:T(8,128)S(1)}, f32[256,128]{1,0:T(8,128)S(1)}, u32[]{:S(2)}, u32[]{:S(2)}) collective-permute-start(f32[256,128]{1,0:T(8,128)S(1)} %get-tuple-element.94), channel_id=1, source_target_pairs={{0,8},{8,16},{16,24},{24,0},{1,9},{9,17},{17,25},{25,1},{2,10},{10... | collective-permute-start | bytes 393224 | tf_op jit(solution)/shard_map/ppermute | solution.py:497
  59.3 7.5 %collective-permute-start.14 = (f32[256,128]{1,0:T(8,128)S(1)}, f32[256,128]{1,0:T(8,128)S(1)}, u32[]{:S(2)}, u32[]{:S(2)}) collective-permute-start(f32[256,128]{1,0:T(8,128)S(1)} %get-tuple-element.96), channel_id=1, source_target_pairs={{0,24},{8,0},{16,8},{24,16},{1,25},{9,1},{17,9},{25,17},{2,26},{10... | collective-permute-start | bytes 393224 | tf_op jit(solution)/shard_map/ppermute | solution.py:497
  65.9 17.1 %collective-permute-start.20 = (f32[256,128]{1,0:T(8,128)S(1)}, f32[256,128]{1,0:T(8,128)S(1)}, u32[]{:S(2)}, u32[]{:S(2)}) collective-permute-start(f32[256,128]{1,0:T(8,128)S(1)} %get-tuple-element.105), channel_id=1, source_target_pairs={{0,8},{8,16},{16,24},{24,0},{1,9},{9,17},{17,25},{25,1},{2,10},{10... | collective-permute-start | bytes 393224 | tf_op jit(solution)/shard_map/ppermute | solution.py:497
  67.3 6.9 %collective-permute-start.15 = (f32[168,128]{1,0:T(8,128)S(1)}, f32[168,128]{1,0:T(8,128)S(1)}, u32[]{:S(2)}, u32[]{:S(2)}) collective-permute-start(f32[168,128]{1,0:T(8,128)S(1)} %pad_maximum_fusion.6), channel_id=1, source_target_pairs={{8,0},{16,8},{24,16},{25,24},{17,25},{9,17},{1,9},{2,1},{10,2},{18... | collective-permute-start | bytes 258056 | tf_op jit(solution)/shard_map/ppermute | solution.py:516
  67.4 4.3 %collective-permute-start.16 = (f32[160,128]{1,0:T(8,128)S(1)}, f32[160,128]{1,0:T(8,128)S(1)}, u32[]{:S(2)}, u32[]{:S(2)}) collective-permute-start(f32[160,128]{1,0:T(8,128)S(1)} %pad_maximum_fusion.7), channel_id=1, source_target_pairs={{0,8},{8,16},{16,24},{24,25},{25,17},{17,9},{9,1},{1,2},{2,10},{10... | collective-permute-start | bytes 245768 | tf_op jit(solution)/shard_map/ppermute | solution.py:516
  69.4 16.6 %collective-permute-start.21 = (f32[256,128]{1,0:T(8,128)S(1)}, f32[256,128]{1,0:T(8,128)S(1)}, u32[]{:S(2)}, u32[]{:S(2)}) collective-permute-start(f32[256,128]{1,0:T(8,128)S(1)} %get-tuple-element.106), channel_id=1, source_target_pairs={{0,16},{8,24},{16,0},{24,8},{1,17},{9,25},{17,1},{25,9},{2,18},{10... | collective-permute-start | bytes 393224 | tf_op jit(solution)/shard_map/ppermute | solution.py:497
  74.2 13.7 %copy-start = (f32[2,16,64,128]{3,2,1,0:T(8,128)S(1)}, f32[2,16,64,128]{3,2,1,0:T(8,128)}, u32[]{:S(2)}) copy-start(f32[2,16,64,128]{3,2,1,0:T(8,128)} %gain.2) | copy-start | bytes 3145732
  74.2 13.7 %copy-start.1 = (s32[16,64,128]{2,1,0:T(8,128)S(1)}, s32[16,64,128]{2,1,0:T(8,128)}, u32[]{:S(2)}) copy-start(s32[16,64,128]{2,1,0:T(8,128)} %mask.5) | copy-start | bytes 1572868
  77.8 10.1 %collective-permute-start.22 = (f32[256,128]{1,0:T(8,128)S(1)}, f32[256,128]{1,0:T(8,128)S(1)}, u32[]{:S(2)}, u32[]{:S(2)}) collective-permute-start(f32[256,128]{1,0:T(8,128)S(1)} %get-tuple-element.108), channel_id=1, source_target_pairs={{0,24},{8,0},{16,8},{24,16},{1,25},{9,1},{17,9},{25,17},{2,26},{10... | collective-permute-start | bytes 393224 | tf_op jit(solution)/shard_map/ppermute | solution.py:497
  79.0 10.4 %collective-permute-start.17 = (f32[256,128]{1,0:T(8,128)S(1)}, f32[256,128]{1,0:T(8,128)S(1)}, u32[]{:S(2)}, u32[]{:S(2)}) collective-permute-start(f32[256,128]{1,0:T(8,128)S(1)} %get-tuple-element.102), channel_id=1, source_target_pairs={{0,8},{8,16},{16,24},{24,0},{1,9},{9,17},{17,25},{25,1},{2,10},{10... | collective-permute-start | bytes 393224 | tf_op jit(solution)/shard_map/ppermute | solution.py:497
  81.6 11.4 %collective-permute-start.18 = (f32[256,128]{1,0:T(8,128)S(1)}, f32[256,128]{1,0:T(8,128)S(1)}, u32[]{:S(2)}, u32[]{:S(2)}) collective-permute-start(f32[256,128]{1,0:T(8,128)S(1)} %get-tuple-element.103), channel_id=1, source_target_pairs={{0,16},{8,24},{16,0},{24,8},{1,17},{9,25},{17,1},{25,9},{2,18},{10... | collective-permute-start | bytes 393224 | tf_op jit(solution)/shard_map/ppermute | solution.py:497
  83.0 10.0 %collective-permute-start.19 = (f32[256,128]{1,0:T(8,128)S(1)}, f32[256,128]{1,0:T(8,128)S(1)}, u32[]{:S(2)}, u32[]{:S(2)}) collective-permute-start(f32[256,128]{1,0:T(8,128)S(1)} %get-tuple-element.104), channel_id=1, source_target_pairs={{0,24},{8,0},{16,8},{24,16},{1,25},{9,1},{17,9},{25,17},{2,26},{10... | collective-permute-start | bytes 393224 | tf_op jit(solution)/shard_map/ppermute | solution.py:497

commit v11 on v8

--- a/solution.py
+++ b/solution.py
@@ -44,9 +44,9 @@
     return [slot(lev) for lev in to], [slot(lev) for lev in source], source
 
 
-def swap(blocks, group, width):
+def swap(blocks, group, width, axis=1):
     blocks = list(blocks)
-    cols = blocks[0].shape[1]
+    cols = blocks[0].shape[axis]
     bit = len(blocks) // 2
     while bit:
         shift = bit * width
@@ -54,8 +54,8 @@
         for a in range(len(blocks)):
             if not a & bit:
                 x, y = blocks[a], blocks[a + bit]
-                blocks[a] = jnp.where(low, x, pltpu.roll(y, shift, 1))
-                blocks[a + bit] = jnp.where(low, pltpu.roll(x, cols - shift, 1), y)
+                blocks[a] = jnp.where(low, x, pltpu.roll(y, shift, axis))
+                blocks[a + bit] = jnp.where(low, pltpu.roll(x, cols - shift, axis), y)
         bit //= 2
     return blocks
 
@@ -136,19 +136,21 @@
     )(increment, gain, mask)
 
 
-def pack_kernel(starts, rows, masked, along_i, along_j, *refs):
+def pack_kernel(pieces, masked, along_i, along_j, *refs):
     levels, length, cols = along_i.shape
-    groups = len(starts)
+    groups = len(pieces[0][0])
+    width = cols // groups
     halos, outs = refs[masked:-4 - groups - 3 * masked], refs[-4 - groups - 3 * masked:-4 - 3 * masked]
     held, slots_held, sems, fetch_sems = refs[-4:]
+    unroll = held.shape[0]
+    number = levels // unroll
+    starts, rows = pieces[0]
     group = lane_groups(rows, cols, groups)
-    unroll = held.shape[0]
-    pieces = levels // unroll
     if masked:
         sources, (along_i, along_j, sea) = (along_i, along_j, refs[0]), refs[-7:-4]
         fetched = []
         for side, (source, target) in enumerate(zip(sources, (along_i, along_j, sea))):
-            pairs = [(source.at[pl.ds(k * unroll, unroll)], target.at[pl.ds(k * unroll, unroll)]) for k in range(pieces)]
+            pairs = [(source.at[pl.ds(k * unroll, unroll)], target.at[pl.ds(k * unroll, unroll)]) for k in range(number)]
             fetched.append(copies(pairs, fetch_sems.at[side]))
 
     def put(at, blocks):
@@ -156,47 +158,57 @@
             slots_held[slot, pl.ds(at, block.shape[0]), :] = block
 
     for side, weight in enumerate((along_i, along_j)):
-        for outer in range(pieces):
+        for outer in range(number):
             if masked:
                 fetched[side][outer].wait()
-            packed = []
+            edges = []
             for k in range(unroll):
                 level = outer * unroll + k
+                index = side * levels + level
                 if halos:
                     for halo, at in zip(halos, (0, STEPS + length)):
-                        held[k, pl.ds(at, STEPS), :] = halo[pl.ds((side * levels + level) * STEPS, STEPS), :]
+                        held[k, pl.ds(at, STEPS), :] = halo[pl.ds(index * STEPS, STEPS), :]
                     held[k, pl.ds(STEPS, length), :] = weight[level]
                     blocks = [held[k, pl.ds(start, rows), :] for start in starts]
                 else:
                     blocks = [weight[level, pl.ds(start - STEPS, rows), :] for start in starts]
-                packed.append(swap(blocks, group, cols // groups))
-            put(
-                (side * levels + outer * unroll) * rows,
-                [jnp.concatenate([packed[k][slot] for k in range(unroll)], axis=0) for slot in range(groups)],
-            )
+                put(index * rows, swap(blocks, group, width))
+                if len(pieces) > 1:
+                    small = pieces[1][0]
+                    low, high = small[0] - 2 * STEPS, small[groups // 2] - STEPS
+                    row = lax.broadcasted_iota(jnp.int32, (2 * STEPS, cols), 0)
+                    upper = pltpu.roll(weight[level, pl.ds(low, 2 * STEPS), :], STEPS, 0)
+                    lower = pltpu.roll(weight[level, pl.ds(high, 2 * STEPS), :], STEPS, 0)
+                    edges.append(jnp.where(row < STEPS, upper, lower))
+            if edges:
+                each = pieces[1][1]
+                pairs = lax.broadcasted_iota(jnp.int32, edges[0].shape, 0) // each
+                edges = swap(edges, pairs, each, 0)
+                at = 2 * levels * rows + (side * levels + outer * unroll) * each
+                put(at, swap(edges, lane_groups(unroll * each, cols, groups), width))
     if masked:
         depth = jnp.zeros((length, cols), sea.dtype)
-        for outer in range(pieces):
+        for outer in range(number):
             fetched[2][outer].wait()
             for level in range(outer * unroll, (outer + 1) * unroll):
                 depth = depth + sea[level]
         depth = depth.astype(jnp.float32)
         size = length // groups
         blocks = [depth[a * size:(a + 1) * size] for a in range(groups)]
-        put(2 * levels * rows, swap(blocks, lane_groups(size, cols, groups), cols // groups))
+        put(2 * levels * sum(n for _, n in pieces), swap(blocks, lane_groups(size, cols, groups), width))
     slots = position()[0]
     for copy in copies([(slots_held.at[slots[d]], out) for d, out in enumerate(outs)], sems):
         copy.wait()
 
 
-def weight_messages(starts, rows, along_i, along_j, mask=(), halos=()):
+def weight_messages(pieces, along_i, along_j, mask=(), halos=()):
     levels, length, cols = along_i.shape
-    groups = len(starts)
-    shape = (2 * levels * rows + len(mask) * length // groups, cols)
+    groups = len(pieces[0][0])
+    shape = (2 * levels * sum(rows for _, rows in pieces) + len(mask) * length // groups, cols)
     unroll = 4
     return list(
         pl.pallas_call(
-            functools.partial(pack_kernel, starts, rows, len(mask)),
+            functools.partial(pack_kernel, pieces, len(mask)),
             in_specs=[pl.BlockSpec(memory_space=pl.ANY) if mask else vmem()] * (2 + len(mask) + len(halos)),
             out_specs=[pl.BlockSpec(memory_space=pl.ANY)] * groups,
             out_shape=[jax.ShapeDtypeStruct(shape, jnp.float32)] * groups,
@@ -213,8 +225,25 @@
     )
 
 
+def three(x):
+    high = x.astype(jnp.bfloat16)
+    rest = x - high.astype(jnp.float32)
+    middle = rest.astype(jnp.bfloat16)
+    return high, middle, (rest - middle.astype(jnp.float32)).astype(jnp.bfloat16)
+
+
+def left_terms(x):
+    high, middle, low = three(x)
+    return jnp.concatenate([high, middle, low, high, middle, high], axis=1)
+
+
+def right_terms(x, axis):
+    high, middle, low = three(x)
+    return jnp.concatenate([high, high, high, middle, middle, low], axis=axis)
+
+
 def adjoint_kernel(matrix, depths, *refs):
-    parts, out = refs[:-1], refs[-1]
+    parts, out, terms = refs[:-2], refs[-2], refs[-1]
     length, width, order = out.shape
     groups = len(parts)
     rows = length // groups
@@ -222,16 +251,21 @@
     count = order // groups
     level = lax.rem(lax.broadcasted_iota(jnp.int32, (order, cols), 0), order // 2).astype(jnp.float32)
 
-    def one(i, carry):
-        x = jnp.concatenate([part[pl.ds(i, count, rows), :] for part in parts], axis=0)
-        depth = depths[pl.ds(i, 1), :]
-        y = jnp.dot(matrix[...], x, precision=HIGHEST, preferred_element_type=jnp.float32)
-        y = jnp.where(level < depth, y, 0.0).T
-        for a in range(groups):
-            out[a * rows + i] = y[a * width:(a + 1) * width]
+    terms[...] = left_terms(matrix[...])
+
+    def two(pair, carry):
+        planes = [2 * pair, 2 * pair + 1]
+        x = jnp.concatenate(
+            [jnp.concatenate([part[pl.ds(i, count, rows), :] for part in parts], axis=0) for i in planes], axis=1
+        )
+        y = jnp.dot(terms[...], right_terms(x, 0), preferred_element_type=jnp.float32)
+        for k, i in enumerate(planes):
+            z = jnp.where(level < depths[pl.ds(i, 1), :], y[:, k * cols:(k + 1) * cols], 0.0).T
+            for a in range(groups):
+                out[a * rows + i] = z[a * width:(a + 1) * width]
         return carry
 
-    lax.fori_loop(0, rows, one, 0, unroll=4)
+    lax.fori_loop(0, rows // 2, two, 0, unroll=2)
 
 
 def adjoint_mix(matrix, depths, parts, length, width):
@@ -240,6 +274,7 @@
         in_specs=[vmem()] * (2 + len(parts)),
         out_specs=vmem(),
         out_shape=jax.ShapeDtypeStruct((length, width, matrix.shape[0]), jnp.float32),
+        scratch_shapes=[pltpu.VMEM((matrix.shape[0], 6 * matrix.shape[0]), jnp.bfloat16)],
         compiler_params=params(),
         name="adjoint_mix",
     )(matrix, depths, *parts)
@@ -255,20 +290,23 @@
     )
 
 
-def turn_kernel(starts, *refs):
-    depths, parts, (out, held, depth_i, depth_j) = refs[:-4 - len(starts)], refs[-4 - len(starts):-4], refs[-4:]
-    length, width, order = out.shape
-    groups = len(parts)
-    rows = length // groups
+def turn_kernel(pieces, *refs):
+    groups = len(pieces[0][0])
+    depths, parts, (out, held, depth_i, depth_j) = refs[:-4 - groups], refs[-4 - groups:-4], refs[-4:]
+    _, width, order = out.shape
     half = order // 2
     count = half // groups
     cols = width * groups
     source = position()[2]
-    for i in range(rows):
+    planes, base = [], 0
+    for starts, rows in pieces:
+        planes += [(base + i, rows, i, starts) for i in range(rows)]
+        base += 2 * count * rows
+    for k, (first, rows, _, _) in enumerate(planes):
         for d, part in enumerate(parts):
             for side in range(2):
                 at = pl.multiple_of(side * half + source[d] * count, 8)
-                held[i, pl.ds(at, count), :] = part[pl.ds(side * count * rows + i, count, rows), :]
+                held[k, pl.ds(at, count), :] = part[pl.ds(first + side * count * rows, count, rows), :]
 
     no_halo = jnp.zeros((2 * STEPS, cols), jnp.float32)
     depth = unfold(depths[0][...], depths[1][...] if len(depths) > 1 else no_halo, groups)
@@ -278,30 +316,35 @@
     depth_j[...] = jnp.minimum(depth, right)
     depth_i[pl.ds(0, tall - 1), :] = jnp.minimum(depth[:-1], depth[1:])
     depth_i[pl.ds(tall - 1, 1), :] = depth[tall - 1:]
-    group = lane_groups(rows, cols, groups)
-
-    def fold(ref):
+
+    def fold(ref, starts, rows):
+        group = lane_groups(rows, cols, groups)
         x = ref[pl.ds(starts[0], rows), :]
         for a in range(1, groups):
             x = jnp.where(group == a, pltpu.roll(ref[pl.ds(starts[a], rows), :], a * width, 1), x)
         return x
 
-    folded_i, folded_j = fold(depth_i), fold(depth_j)
+    folded = [(fold(depth_i, *piece), fold(depth_j, *piece)) for piece in pieces]
     level = lax.broadcasted_iota(jnp.int32, (half, cols), 0).astype(jnp.float32)
-    for i in range(rows):
-        along_i = jnp.where(level < folded_i[i:i + 1], held[i, pl.ds(0, half), :], 0.0)
-        along_j = jnp.where(level < folded_j[i:i + 1], held[i, pl.ds(half, half), :], 0.0)
-        turned = jnp.concatenate([along_i, along_j], axis=0).T
-        for a in range(groups):
-            out[a * rows + i] = turned[a * width:(a + 1) * width]
-
-
-def turn_weights(starts, rows, depths, parts, order):
+    at = 0
+    for n, (starts, rows) in enumerate(pieces):
+        for i in range(rows):
+            k = at // groups + i
+            along_i = jnp.where(level < folded[n][0][i:i + 1], held[k, pl.ds(0, half), :], 0.0)
+            along_j = jnp.where(level < folded[n][1][i:i + 1], held[k, pl.ds(half, half), :], 0.0)
+            turned = jnp.concatenate([along_i, along_j], axis=0).T
+            for a in range(groups):
+                out[at + a * rows + i] = turned[a * width:(a + 1) * width]
+        at += groups * rows
+
+
+def turn_weights(pieces, depths, parts, order):
     groups = len(parts)
     cols = parts[0].shape[1]
+    rows = sum(n for _, n in pieces)
     tall = depths[0].shape[0] * groups + 2 * STEPS
     return pl.pallas_call(
-        functools.partial(turn_kernel, starts),
+        functools.partial(turn_kernel, pieces),
         in_specs=[vmem()] * (len(depths) + groups),
         out_specs=vmem(),
         out_shape=jax.ShapeDtypeStruct((rows * groups, cols // groups, order), jnp.float32),
@@ -332,7 +375,7 @@
 def spread_kernel(windows, field_rows, weight_rows, count, matrix, *refs):
     depths, refs = refs[:count], refs[count:]
     pieces = [refs[3 * k:3 * k + 3] for k in range(len(field_rows) + len(weight_rows))]
-    outs, (a, b, wi, wj, masks) = refs[3 * len(pieces):-5], refs[-5:]
+    outs, (a, b, wi, wj, masks, terms) = refs[3 * len(pieces):-6], refs[-6:]
     width, order = pieces[0][0].shape[1:]
     half = order // 2
     _, ext, wide, _ = a.shape
@@ -383,18 +426,24 @@
     rows = len(windows) * (ext - 2 * STEPS) // groups
     each = groups // len(windows)
 
-    def mix(i, carry):
+    terms[...] = left_terms(matrix[...])
+
+    def mix(pair, carry):
+        planes = [2 * pair, 2 * pair + 1]
         x = jnp.concatenate(
-            [src[g // each, STEPS + g % each * rows + i, pl.ds(PAD, width), :] for g in range(groups)], axis=0
+            [src[g // each, STEPS + g % each * rows + i, pl.ds(PAD, width), :] for i in planes for g in range(groups)],
+            axis=0,
         )
         y = lax.dot_general(
-            matrix[...], x, (((1,), (1,)), ((), ())), precision=HIGHEST, preferred_element_type=jnp.float32
+            terms[...], right_terms(x, 1), (((1,), (1,)), ((), ())), preferred_element_type=jnp.float32
         )
-        for d, out in enumerate(outs):
-            out[pl.ds(i, count, rows), :] = y[d * count:(d + 1) * count]
+        cols = groups * width
+        for k, i in enumerate(planes):
+            for d, out in enumerate(outs):
+                out[pl.ds(i, count, rows), :] = y[d * count:(d + 1) * count, k * cols:(k + 1) * cols]
         return carry
 
-    lax.fori_loop(0, rows, mix, 0, unroll=4)
+    lax.fori_loop(0, rows // 2, mix, 0, unroll=2)
 
 
 def spread_mix(windows, matrix, depths, field, weights, groups):
@@ -414,7 +463,7 @@
         out_specs=[vmem()] * groups,
         out_shape=[shape] * groups,
         scratch_shapes=[pltpu.VMEM((len(windows), ext, width + 2 * PAD, order), jnp.float32)] * 4
-        + [pltpu.VMEM((2, tall, order), jnp.float32)],
+        + [pltpu.VMEM((2, tall, order), jnp.float32), pltpu.VMEM((order, 6 * order), jnp.bfloat16)],
         compiler_params=params(),
         name="spread_mix",
     )(matrix, *arrays)
@@ -526,14 +575,20 @@
     half = devices // 2
     inner = (quarter, 2 * quarter)
     outer = ((0, quarter), (3 * quarter, quarter))
-    inner_rows = list(range(quarter - STEPS, 3 * quarter + STEPS))
-    outer_rows = list(range(-STEPS, quarter - STEPS)) + list(range(3 * quarter + STEPS, length + STEPS))
-    inner_starts = [quarter + a * len(inner_rows) // devices for a in range(devices)]
-    outer_starts = [a * some for a in range(half)] + [3 * quarter + 2 * STEPS + a * some for a in range(half)]
+    inner_pieces = [
+        ([STEPS + quarter + a * some for a in range(devices)], some),
+        ([quarter + 2 * a for a in range(half)] + [STEPS + 3 * quarter + 2 * a for a in range(half)], 2),
+    ]
+    outer_pieces = [([a * some for a in range(half)] + [3 * quarter + 2 * STEPS + a * some for a in range(half)], some)]
+
+    def rows_of(pieces):
+        return [start - STEPS + i for starts, number in pieces for start in starts for i in range(number)]
+
+    inner_rows, outer_rows = rows_of(inner_pieces), rows_of(outer_pieces)
     windows = [list(range(-STEPS, quarter + STEPS)), list(range(3 * quarter - STEPS, length + STEPS))]
 
     inner_size = len(inner_rows) // devices
-    inner_messages = weight_messages(inner_starts, inner_size, diffusion_i, diffusion_j, [sea_mask])
+    inner_messages = weight_messages(inner_pieces, diffusion_i, diffusion_j, [sea_mask])
     inner_parts = exchange(inner_messages)
     inner_messages, edge_i, edge_j, increment, norm_gain = lax.optimization_barrier(
         (inner_messages, diffusion_i, diffusion_j, increment, norm_gain)
@@ -547,10 +602,10 @@
     messages = scaled_messages(increment, norm_gain, sea_mask, devices)
     scaled = exchange(messages)
     messages, halos = lax.optimization_barrier((messages, halos))
-    outer_messages = weight_messages(outer_starts, some, diffusion_i, diffusion_j, halos=halos)
+    outer_messages = weight_messages(outer_pieces, diffusion_i, diffusion_j, halos=halos)
 
     depth = sum(part[2 * levels * inner_size:] for part in inner_parts)
-    here = turn_weights(inner_starts, inner_size, [depth], inner_parts, order)
+    here = turn_weights(inner_pieces, [depth], inner_parts, order)
     left, right = halo_j(
         jnp.concatenate([flat(here[:, :STEPS]), depth], axis=0),
         flat(here[:, -STEPS:]),
@@ -574,7 +629,7 @@
     field = [(list(range(length)), mixed, left, right)]
     weights = [(inner_rows, *inner_weights)]
     depths = [depth, right_depth]
-    inner_mixed = spread_mix([inner_rows], forward, depths, field, weights, devices)
+    inner_mixed = spread_mix([sorted(inner_rows)], forward, depths, field, weights, devices)
     _, upper, lower = lax.optimization_barrier((left, mixed[:STEPS], mixed[-STEPS:]))
     _, outer_parts = lax.optimization_barrier((inner_mixed[0], outer_parts))
     inner_mixed = exchange(inner_mixed)
@@ -588,7 +643,7 @@
     below, below_depth = cut(below, STEPS * width, STEPS)
     halo_depth = jnp.concatenate([below_depth, above_depth], axis=0)
     halo = jnp.concatenate([above, below], axis=0).reshape(2 * STEPS, width, order)
-    here = turn_weights(outer_starts, some, [depth, halo_depth], outer_parts, order)
+    here = turn_weights(outer_pieces, [depth, halo_depth], outer_parts, order)
     left, right = halo_j(
         jnp.concatenate([flat(here[:, :STEPS]), flat(halo[:, :STEPS]), halo_depth], axis=0),
         jnp.concatenate([flat(here[:, -STEPS:]), flat(halo[:, -STEPS:])], axis=0),

time: 93.1 us -> 92.3 us (level)
  Pallas kernels: 21.6 us -> 20.3 us
    pallas_call x2, Pallas kernels: 6.91 us -> 5.89 us  [spread_mix(): pl.pallas_call(kernel, in_specs=[vmem()] * (1 + len(arrays)), out_specs=[...]
  transfers between devices with their start and end apart: 23 -> 23, of which waited for: 8 -> 8; matrix products, arithmetic and copies ran while one was open for 0% -> 0% of each run, Pallas kernels for 18% -> 17%
where the time goes in v11:
time: 92.3 us; the launch traced here: 92.1 us
  starting transfers between devices  49.8 us (54%)
  Pallas kernels  20.3 us (22%)
  waiting for transfers between devices  19.6 us (21%)
  local copies, waits for them, and re-layouts  1.87 us (2%)
    ppermute x15, starting transfers between devices, shift(): lax.ppermute(x, 'lev', [(k, (k + d) % devices) for k in range(devices)])  23.4 us
    ppermute x3, starting transfers between devices, halo_j(): lax.ppermute(last, ('lev', 'gy'), ahead)  22.9 us
    ppermute x15, waiting for transfers between devices, shift(): lax.ppermute(x, 'lev', [(k, (k + d) % devices) for k in range(devices)])  12.8 us
    pallas_call x2, Pallas kernels, spread_mix(): pl.pallas_call(kernel, in_specs=[vmem()] * (1 + len(arrays)), out_specs=[...  5.89 us
    ppermute x3, waiting for transfers between devices, halo_j(): lax.ppermute(first, ('lev', 'gy'), back)  5.68 us
    pallas_call x2, Pallas kernels, weight_messages(): pl.pallas_call(functools.partial(pack_kernel, pieces, len(mask)), in_spec...  5.63 us
    ppermute x2, starting transfers between devices, halo_i(): both = lax.ppermute(jnp.concatenate([first, last], axis=0), 'gx', up)  3.46 us
    pallas_call x1, Pallas kernels, scaled_messages(): pl.pallas_call(scaled_kernel, in_specs=[pl.BlockSpec(memory_space=pl.ANY)...  3.25 us
  transfers between devices with their start and end apart: 23, of which 8 were waited for; matrix products, arithmetic and copies ran while one was open for 0% of the time, Pallas kernels for 17%

profile of v11, /device:TPU:0, one launch (start us, length us, event | category | flops | bytes accessed | tf_op | source)
XLA Modules:
  0.0 92.1 jit_solution(10955197007350718447)
XLA Ops:
  0.0 3.5 %weight_messages.2 = (f32[336,128]{1,0:T(8,128)}, f32[336,128]{1,0:T(8,128)}, f32[336,128]{1,0:T(8,128)}, f32[336,128]{1,0:T(8,128)}) custom-call(f32[16,64,128]{2,1,0:T(8,128)} %along_i.3, f32[16,64,128]{2,1,0:T(8,128)} %along_j.3, s32[16,64,128]{2,1,0:T(8,128)} %mask.5), custom_call_target="tpu_custom_call" | custom-call | tf_op jit(solution)/shard_map/weight_messages/pallas_call | solution.py:210
  3.5 4.1 %collective-permute-start = (f32[336,128]{1,0:T(8,128)}, f32[336,128]{1,0:T(8,128)S(1)}, u32[]{:S(2)}, u32[]{:S(2)}) collective-permute-start(f32[336,128]{1,0:T(8,128)} %get-tuple-element.54), channel_id=1, source_target_pairs={{0,16},{8,24},{16,0},{24,8},{1,17},{9,25},{17,1},{25,9},{2,18},{10... | collective-permute-start | bytes 516104 | tf_op jit(solution)/shard_map/ppermute | solution.py:546
  7.6 1.6 %collective-permute-start.1 = (f32[336,128]{1,0:T(8,128)}, f32[336,128]{1,0:T(8,128)S(1)}, u32[]{:S(2)}, u32[]{:S(2)}) collective-permute-start(f32[336,128]{1,0:T(8,128)} %get-tuple-element.55), channel_id=1, source_target_pairs={{0,8},{8,16},{16,24},{24,0},{1,9},{9,17},{17,25},{25,1},{2,10},{10... | collective-permute-start | bytes 516104 | tf_op jit(solution)/shard_map/ppermute | solution.py:546
  9.1 2.2 %collective-permute-start.2 = (f32[336,128]{1,0:T(8,128)}, f32[336,128]{1,0:T(8,128)S(1)}, u32[]{:S(2)}, u32[]{:S(2)}) collective-permute-start(f32[336,128]{1,0:T(8,128)} %get-tuple-element.56), channel_id=1, source_target_pairs={{0,24},{8,0},{16,8},{24,16},{1,25},{9,1},{17,9},{25,17},{2,26},{10... | collective-permute-start | bytes 516104 | tf_op jit(solution)/shard_map/ppermute | solution.py:546
  11.4 0.0 copy-done.2
  11.4 1.6 %collective-permute-start.5 = (f32[256,128]{1,0:T(8,128)S(1)}, f32[256,128]{1,0:T(8,128)S(1)}, u32[]{:S(2)}, u32[]{:S(2)}) collective-permute-start(f32[256,128]{1,0:T(8,128)S(1)} %pad_maximum_fusion.1), channel_id=1, source_target_pairs={{4,0},{0,4},{5,1},{1,5},{6,2},{2,6},{7,3},{3,7},{12,8},{8,12},{13,... | collective-permute-start | bytes 393224 | tf_op jit(solution)/shard_map/ppermute | solution.py:560
  13.0 3.3 %scaled_messages.1 = (f32[512,128]{1,0:T(8,128)}, f32[512,128]{1,0:T(8,128)}, f32[512,128]{1,0:T(8,128)}, f32[512,128]{1,0:T(8,128)}) custom-call(f32[2,16,64,128]{3,2,1,0:T(8,128)} %increment, f32[2,16,64,128]{3,2,1,0:T(8,128)} %gain.2, s32[16,64,128]{2,1,0:T(8,128)} %mask.5), custom_call_target="tpu_custom_call" | custom-call | tf_op jit(solution)/shard_map/scaled_messages/pallas_call | solution.py:121
  16.3 0.0 copy-start.6
  16.3 0.1 collective-permute-start.4
  16.4 0.7 copy-done.6
  17.2 0.1 copy.13.matrix
  17.3 0.0 collective-permute-done.5
  17.3 0.8 copy-done.8
  18.1 0.0 collective-permute-start.6
  18.1 2.2 %weight_messages.3 = (f32[256,128]{1,0:T(8,128)S(1)}, f32[256,128]{1,0:T(8,128)S(1)}, f32[256,128]{1,0:T(8,128)S(1)}, f32[256,128]{1,0:T(8,128)S(1)}) custom-call(f32[16,64,128]{2,1,0:T(8,128)S(1)} %copy-done.2, f32[16,64,128]{2,1,0:T(8,128)S(1)} %copy-done.3, f32[128,128]{1,0:T(8,128)S(1)} %get-tuple-element.65.refs_0_, ...), custom_call_target="tpu_custom_call" | custom-call | tf_op jit(solution)/shard_map/weight_messages/pallas_call | solution.py:210
  20.3 0.9 %collective-permute-done.refs_2_ = f32[336,128]{1,0:T(8,128)S(1)} collective-permute-done((f32[336,128]{1,0:T(8,128)}, f32[336,128]{1,0:T(8,128)S(1)}, u32[]{:S(2)}, u32[]{:S(2)}) %collective-permute-start) | collective-permute-done | bytes 172064 | tf_op jit(solution)/shard_map/ppermute | solution.py:546
  21.3 2.9 %collective-permute-start.7 = (f32[512,128]{1,0:T(8,128)S(1)}, f32[512,128]{1,0:T(8,128)S(1)}, u32[]{:S(2)}, u32[]{:S(2)}) collective-permute-start(f32[512,128]{1,0:T(8,128)S(1)} %copy-done.7), channel_id=1, source_target_pairs={{0,24},{8,0},{16,8},{24,16},{1,25},{9,1},{17,9},{25,17},{2,26},{10... | collective-permute-start | bytes 786440 | tf_op jit(solution)/shard_map/ppermute | solution.py:546
  24.2 0.0 collective-permute-done.1.refs_3_
  24.2 0.0 collective-permute-done.2.refs_4_
  24.2 0.4 turn_weights.2.refs_5_.refs_10_
  24.7 0.0 copy-start.4
  24.8 11.7 %collective-permute-start.8 = (f32[160,128]{1,0:T(8,128)S(1)}, f32[160,128]{1,0:T(8,128)S(1)}, u32[]{:S(2)}, u32[]{:S(2)}) collective-permute-start(f32[160,128]{1,0:T(8,128)S(1)} %bitcast.47), channel_id=1, source_target_pairs={{0,8},{8,16},{16,24},{24,25},{25,17},{17,9},{9,1},{1,2},{2,10},{10... | collective-permute-start | bytes 245768 | tf_op jit(solution)/shard_map/ppermute | solution.py:565
  36.5 0.0 collective-permute-start.3
  36.5 4.5 %collective-permute-done.4.refs_1_ = f32[512,128]{1,0:T(8,128)S(1)} collective-permute-done((f32[512,128]{1,0:T(8,128)}, f32[512,128]{1,0:T(8,128)S(1)}, u32[]{:S(2)}, u32[]{:S(2)}) %collective-permute-start.4) | collective-permute-done | bytes 262176 | tf_op jit(solution)/shard_map/ppermute | solution.py:546
  41.0 0.0 collective-permute-start.11
  41.0 0.0 collective-permute-done.6.refs_2_
  41.0 0.0 collective-permute-done.7.refs_3_
  41.0 1.8 %adjoint_mix.1.refs_2_.refs_4_ = f32[64,32,128]{2,1,0:T(8,128)S(1)} custom-call(f32[128,128]{1,0:T(8,128)S(1)} %copy.13.matrix, f32[16,128]{1,0:T(8,128)S(1)} %slice_add_fusion.refs_0_.depths, f32[512,128]{1,0:T(8,128)S(1)} %copy-done.4, f32[512,128]{1,0:T(8,128)S(1)} %collective-permute-done.4.refs_1_, f32[512,128]{1,0:T(8,128)S(1)} %collective-permute-done.6.refs_2_, ...), custom_call_target="tpu_custom_call" | custom-call | tf_op jit(solution)/shard_map/adjoint_mix/pallas_call | solution.py:272
  42.9 0.0 collective-permute-done.3
  42.9 0.0 collective-permute-done.8.refs_6_.refs_11_
  42.9 9.1 %collective-permute-start.9 = (f32[256,128]{1,0:T(8,128)S(1)}, f32[256,128]{1,0:T(8,128)S(1)}, u32[]{:S(2)}, u32[]{:S(2)}) collective-permute-start(f32[256,128]{1,0:T(8,128)S(1)} %bitcast.42), channel_id=1, source_target_pairs={{0,8},{8,16},{16,24},{24,25},{25,17},{17,9},{9,1},{1,2},{2,10},{10... | collective-permute-start | bytes 393224 | tf_op jit(solution)/shard_map/ppermute | solution.py:565
  52.0 0.0 collective-permute-start.10
  52.0 1.3 %collective-permute-done.11.refs_3_ = f32[256,128]{1,0:T(8,128)S(1)} collective-permute-done((f32[256,128]{1,0:T(8,128)S(1)}, f32[256,128]{1,0:T(8,128)S(1)}, u32[]{:S(2)}, u32[]{:S(2)}) %collective-permute-start.11) | collective-permute-done | bytes 131104 | tf_op jit(solution)/shard_map/ppermute | solution.py:546
  53.3 1.2 %collective-permute-done.9.refs_3_.refs_5_ = f32[256,128]{1,0:T(8,128)S(1)} collective-permute-done((f32[256,128]{1,0:T(8,128)S(1)}, f32[256,128]{1,0:T(8,128)S(1)}, u32[]{:S(2)}, u32[]{:S(2)}) %collective-permute-start.9) | collective-permute-done | bytes 131104 | tf_op jit(solution)/shard_map/ppermute | solution.py:565
  54.5 2.4 %collective-permute-done.10.refs_4_.refs_6_ = f32[256,128]{1,0:T(8,128)S(1)} collective-permute-done((f32[256,128]{1,0:T(8,128)S(1)}, f32[256,128]{1,0:T(8,128)S(1)}, u32[]{:S(2)}, u32[]{:S(2)}) %collective-permute-start.10) | collective-permute-done | bytes 131104 | tf_op jit(solution)/shard_map/ppermute | solution.py:565
  57.0 1.9 %collective-permute-start.12 = (f32[264,128]{1,0:T(8,128)S(1)}, f32[264,128]{1,0:T(8,128)S(1)}, u32[]{:S(2)}, u32[]{:S(2)}) collective-permute-start(f32[264,128]{1,0:T(8,128)S(1)} %pad_maximum_fusion), channel_id=1, source_target_pairs={{4,0},{0,4},{5,1},{1,5},{6,2},{2,6},{7,3},{3,7},{12,8},{8,12},{13,... | collective-permute-start | bytes 405512 | tf_op jit(solution)/shard_map/ppermute | solution.py:560
  58.9 1.5 %collective-permute-start.13 = (f32[256,128]{1,0:T(8,128)S(1)}, f32[256,128]{1,0:T(8,128)S(1)}, u32[]{:S(2)}, u32[]{:S(2)}) collective-permute-start(f32[256,128]{1,0:T(8,128)S(1)} %get-tuple-element.88), channel_id=1, source_target_pairs={{0,8},{8,16},{16,24},{24,0},{1,9},{9,17},{17,25},{25,1},{2,10},{10... | collective-permute-start | bytes 393224 | tf_op jit(solution)/shard_map/ppermute | solution.py:546
  60.3 2.4 %collective-permute-start.14 = (f32[256,128]{1,0:T(8,128)S(1)}, f32[256,128]{1,0:T(8,128)S(1)}, u32[]{:S(2)}, u32[]{:S(2)}) collective-permute-start(f32[256,128]{1,0:T(8,128)S(1)} %get-tuple-element.89), channel_id=1, source_target_pairs={{0,24},{8,0},{16,8},{24,16},{1,25},{9,1},{17,9},{25,17},{2,26},{10... | collective-permute-start | bytes 393224 | tf_op jit(solution)/shard_map/ppermute | solution.py:546
  62.7 2.9 %spread_mix.2 = (f32[256,128]{1,0:T(8,128)S(1)}, f32[256,128]{1,0:T(8,128)S(1)}, f32[256,128]{1,0:T(8,128)S(1)}, f32[256,128]{1,0:T(8,128)S(1)}) custom-call(f32[128,128]{1,0:T(8,128)S(1)} %get-tuple-element.127.matrix, f32[16,128]{1,0:T(8,128)S(1)} %slice_add_fusion.refs_0_.depths, f32[16,128]{1,0:T(8,128)S(1)} %split.44.refs_1_, ...), custom_call_target="tpu_custom_call" | custom-call | tf_op jit(solution)/shard_map/spread_mix/pallas_call | solution.py:460
  65.5 0.1 collective-permute-start.20
  65.6 1.5 %collective-permute-done.13.refs_4_ = f32[256,128]{1,0:T(8,128)S(1)} collective-permute-done((f32[256,128]{1,0:T(8,128)S(1)}, f32[256,128]{1,0:T(8,128)S(1)}, u32[]{:S(2)}, u32[]{:S(2)}) %collective-permute-start.13) | collective-permute-done | bytes 131104 | tf_op jit(solution)/shard_map/ppermute | solution.py:546
  67.1 0.0 collective-permute-done.14.refs_5_
  67.2 0.0 collective-permute-done.12
  67.2 0.4 turn_weights.3.refs_13_
  67.7 0.1 collective-permute-start.15
  67.8 2.1 %collective-permute-start.16 = (f32[160,128]{1,0:T(8,128)S(1)}, f32[160,128]{1,0:T(8,128)S(1)}, u32[]{:S(2)}, u32[]{:S(2)}) collective-permute-start(f32[160,128]{1,0:T(8,128)S(1)} %pad_maximum_fusion.7), channel_id=1, source_target_pairs={{0,8},{8,16},{16,24},{24,25},{25,17},{17,9},{9,1},{1,2},{2,10},{10... | collective-permute-start | bytes 245768 | tf_op jit(solution)/shard_map/ppermute | solution.py:565
  69.8 1.9 %collective-permute-start.21 = (f32[256,128]{1,0:T(8,128)S(1)}, f32[256,128]{1,0:T(8,128)S(1)}, u32[]{:S(2)}, u32[]{:S(2)}) collective-permute-start(f32[256,128]{1,0:T(8,128)S(1)} %get-tuple-element.99), channel_id=1, source_target_pairs={{0,8},{8,16},{16,24},{24,0},{1,9},{9,17},{17,25},{25,1},{2,10},{10... | collective-permute-start | bytes 393224 | tf_op jit(solution)/shard_map/ppermute | solution.py:546
  71.8 1.9 %collective-permute-start.22 = (f32[256,128]{1,0:T(8,128)S(1)}, f32[256,128]{1,0:T(8,128)S(1)}, u32[]{:S(2)}, u32[]{:S(2)}) collective-permute-start(f32[256,128]{1,0:T(8,128)S(1)} %get-tuple-element.100), channel_id=1, source_target_pairs={{0,24},{8,0},{16,8},{24,16},{1,25},{9,1},{17,9},{25,17},{2,26},{10... | collective-permute-start | bytes 393224 | tf_op jit(solution)/shard_map/ppermute | solution.py:546
  73.7 0.0 collective-permute-done.16
  73.7 3.2 %collective-permute-done.15 = f32[168,128]{1,0:T(8,128)S(1)} collective-permute-done((f32[168,128]{1,0:T(8,128)S(1)}, f32[168,128]{1,0:T(8,128)S(1)}, u32[]{:S(2)}, u32[]{:S(2)}) %collective-permute-start.15) | collective-permute-done | bytes 86048 | tf_op jit(solution)/shard_map/ppermute | solution.py:565
  76.9 0.0 copy-start
  76.9 0.0 copy-start.1
  77.0 3.0 %spread_mix.3 = (f32[256,128]{1,0:T(8,128)S(1)}, f32[256,128]{1,0:T(8,128)S(1)}, f32[256,128]{1,0:T(8,128)S(1)}, f32[256,128]{1,0:T(8,128)S(1)}) custom-call(f32[128,128]{1,0:T(8,128)S(1)} %get-tuple-element.127.matrix, f32[16,128]{1,0:T(8,128)S(1)} %slice_add_fusion.refs_0_.depths, f32[16,128]{1,0:T(8,128)S(1)} %split.44.refs_1_, ...), custom_call_target="tpu_custom_call" | custom-call | tf_op jit(solution)/shard_map/spread_mix/pallas_call | solution.py:460
  80.0 0.9 collective-permute-start.17
  80.9 1.5 %collective-permute-start.18 = (f32[256,128]{1,0:T(8,128)S(1)}, f32[256,128]{1,0:T(8,128)S(1)}, u32[]{:S(2)}, u32[]{:S(2)}) collective-permute-start(f32[256,128]{1,0:T(8,128)S(1)} %get-tuple-element.96), channel_id=1, source_target_pairs={{0,8},{8,16},{16,24},{24,0},{1,9},{9,17},{17,25},{25,1},{2,10},{10... | collective-permute-start | bytes 393224 | tf_op jit(solution)/shard_map/ppermute | solution.py:546
  82.4 0.0 collective-permute-done.20.refs_1_
  82.4 2.4 %collective-permute-start.19 = (f32[256,128]{1,0:T(8,128)S(1)}, f32[256,128]{1,0:T(8,128)S(1)}, u32[]{:S(2)}, u32[]{:S(2)}) collective-permute-start(f32[256,128]{1,0:T(8,128)S(1)} %get-tuple-element.97), channel_id=1, source_target_pairs={{0,24},{8,0},{16,8},{24,16},{1,25},{9,1},{17,9},{25,17},{2,26},{10... | collective-permute-start | bytes 393224 | tf_op jit(solution)/shard_map/ppermute | solution.py:546
  84.7 0.0 collective-permute-done.21.refs_2_
  84.7 0.0 collective-permute-done.22.refs_3_
  84.7 1.4 %result.2.refs_4_ = f32[2,16,64,128]{3,2,1,0:T(8,128)} custom-call(f32[2,16,64,128]{3,2,1,0:T(8,128)S(1)} %copy-done, s32[16,64,128]{2,1,0:T(8,128)S(1)} %copy-done.1, f32[256,128]{1,0:T(8,128)S(1)} %get-tuple-element.85.refs_0_, f32[256,128]{1,0:T(8,128)S(1)} %collective-permute-done.20.refs_1_, f32[256,128]{1,0:T(8,128)S(1)} %collective-permute-done.21.refs_2_, ...), custom_call_target="tpu_custom_call" | custom-call | tf_op jit(solution)/shard_map/result/pallas_call | solution.py:519
  86.2 4.4 %collective-permute-done.17.refs_1_ = f32[256,128]{1,0:T(8,128)S(1)} collective-permute-done((f32[256,128]{1,0:T(8,128)S(1)}, f32[256,128]{1,0:T(8,128)S(1)}, u32[]{:S(2)}, u32[]{:S(2)}) %collective-permute-start.17) | collective-permute-done | bytes 131104 | tf_op jit(solution)/shard_map/ppermute | solution.py:546
  90.6 0.0 collective-permute-done.18.refs_2_
  90.6 0.0 collective-permute-done.19.refs_3_
  90.6 1.4 %result.3 = f32[2,16,64,128]{3,2,1,0:T(8,128)} custom-call(f32[2,16,64,128]{3,2,1,0:T(8,128)S(1)} %copy-done, s32[16,64,128]{2,1,0:T(8,128)S(1)} %copy-done.1, f32[256,128]{1,0:T(8,128)S(1)} %get-tuple-element.94.refs_0_, f32[256,128]{1,0:T(8,128)S(1)} %collective-permute-done.17.refs_1_, ...), custom_call_target="tpu_custom_call", output_to_operand_aliasing={{}: (6, {})} | custom-call | tf_op jit(solution)/shard_map/result/pallas_call | solution.py:519
  (39 shorter events, 0.3 us)
Async XLA Ops:
  0.0 11.4 %copy-start.3 = (f32[16,64,128]{2,1,0:T(8,128)S(1)}, f32[16,64,128]{2,1,0:T(8,128)}, u32[]{:S(2)}) copy-start(f32[16,64,128]{2,1,0:T(8,128)} %along_j.3) | copy-start | bytes 1572868
  0.0 11.4 %copy-start.2 = (f32[16,64,128]{2,1,0:T(8,128)S(1)}, f32[16,64,128]{2,1,0:T(8,128)}, u32[]{:S(2)}) copy-start(f32[16,64,128]{2,1,0:T(8,128)} %along_i.3) | copy-start | bytes 1572868
  3.5 17.8 %collective-permute-start = (f32[336,128]{1,0:T(8,128)}, f32[336,128]{1,0:T(8,128)S(1)}, u32[]{:S(2)}, u32[]{:S(2)}) collective-permute-start(f32[336,128]{1,0:T(8,128)} %get-tuple-element.54), channel_id=1, source_target_pairs={{0,16},{8,24},{16,0},{24,8},{1,17},{9,25},{17,1},{25,9},{2,18},{10... | collective-permute-start | bytes 516104 | tf_op jit(solution)/shard_map/ppermute | solution.py:546
  7.6 16.7 %collective-permute-start.1 = (f32[336,128]{1,0:T(8,128)}, f32[336,128]{1,0:T(8,128)S(1)}, u32[]{:S(2)}, u32[]{:S(2)}) collective-permute-start(f32[336,128]{1,0:T(8,128)} %get-tuple-element.55), channel_id=1, source_target_pairs={{0,8},{8,16},{16,24},{24,0},{1,9},{9,17},{17,25},{25,1},{2,10},{10... | collective-permute-start | bytes 516104 | tf_op jit(solution)/shard_map/ppermute | solution.py:546
  9.1 15.1 %collective-permute-start.2 = (f32[336,128]{1,0:T(8,128)}, f32[336,128]{1,0:T(8,128)S(1)}, u32[]{:S(2)}, u32[]{:S(2)}) collective-permute-start(f32[336,128]{1,0:T(8,128)} %get-tuple-element.56), channel_id=1, source_target_pairs={{0,24},{8,0},{16,8},{24,16},{1,25},{9,1},{17,9},{25,17},{2,26},{10... | collective-permute-start | bytes 516104 | tf_op jit(solution)/shard_map/ppermute | solution.py:546
  11.4 5.9 %collective-permute-start.5 = (f32[256,128]{1,0:T(8,128)S(1)}, f32[256,128]{1,0:T(8,128)S(1)}, u32[]{:S(2)}, u32[]{:S(2)}) collective-permute-start(f32[256,128]{1,0:T(8,128)S(1)} %pad_maximum_fusion.1), channel_id=1, source_target_pairs={{4,0},{0,4},{5,1},{1,5},{6,2},{2,6},{7,3},{3,7},{12,8},{8,12},{13,... | collective-permute-start | bytes 393224 | tf_op jit(solution)/shard_map/ppermute | solution.py:560
  16.3 0.8 copy-start.6
  16.3 24.7 %collective-permute-start.4 = (f32[512,128]{1,0:T(8,128)}, f32[512,128]{1,0:T(8,128)S(1)}, u32[]{:S(2)}, u32[]{:S(2)}) collective-permute-start(f32[512,128]{1,0:T(8,128)} %get-tuple-element.60), channel_id=1, source_target_pairs={{0,16},{8,24},{16,0},{24,8},{1,17},{9,25},{17,1},{25,9},{2,18},{10... | collective-permute-start | bytes 786440 | tf_op jit(solution)/shard_map/ppermute | solution.py:546
  17.1 1.0 %copy-start.8 = (f32[512,128]{1,0:T(8,128)S(1)}, f32[512,128]{1,0:T(8,128)}, u32[]{:S(2)}) copy-start(f32[512,128]{1,0:T(8,128)} %get-tuple-element.61) | copy-start | bytes 786436
  18.1 22.9 %collective-permute-start.6 = (f32[512,128]{1,0:T(8,128)S(1)}, f32[512,128]{1,0:T(8,128)S(1)}, u32[]{:S(2)}, u32[]{:S(2)}) collective-permute-start(f32[512,128]{1,0:T(8,128)S(1)} %copy-done.8), channel_id=1, source_target_pairs={{0,8},{8,16},{16,24},{24,0},{1,9},{9,17},{17,25},{25,1},{2,10},{10... | collective-permute-start | bytes 786440 | tf_op jit(solution)/shard_map/ppermute | solution.py:546
  18.1 3.2 %copy-start.7 = (f32[512,128]{1,0:T(8,128)S(1)}, f32[512,128]{1,0:T(8,128)}, u32[]{:S(2)}) copy-start(f32[512,128]{1,0:T(8,128)} %get-tuple-element.62) | copy-start | bytes 786436
  18.1 6.1 %copy-start.5 = (f32[336,128]{1,0:T(8,128)S(1)}, f32[336,128]{1,0:T(8,128)}, u32[]{:S(2)}) copy-start(f32[336,128]{1,0:T(8,128)} %get-tuple-element.53.refs_1_) | copy-start | bytes 516100
  21.3 19.7 %collective-permute-start.7 = (f32[512,128]{1,0:T(8,128)S(1)}, f32[512,128]{1,0:T(8,128)S(1)}, u32[]{:S(2)}, u32[]{:S(2)}) collective-permute-start(f32[512,128]{1,0:T(8,128)S(1)} %copy-done.7), channel_id=1, source_target_pairs={{0,24},{8,0},{16,8},{24,16},{1,25},{9,1},{17,9},{25,17},{2,26},{10... | collective-permute-start | bytes 786440 | tf_op jit(solution)/shard_map/ppermute | solution.py:546
  24.7 16.3 %copy-start.4 = (f32[512,128]{1,0:T(8,128)S(1)}, f32[512,128]{1,0:T(8,128)}, u32[]{:S(2)}) copy-start(f32[512,128]{1,0:T(8,128)} %get-tuple-element.59.refs_0_) | copy-start | bytes 786436
  24.8 18.1 %collective-permute-start.8 = (f32[160,128]{1,0:T(8,128)S(1)}, f32[160,128]{1,0:T(8,128)S(1)}, u32[]{:S(2)}, u32[]{:S(2)}) collective-permute-start(f32[160,128]{1,0:T(8,128)S(1)} %bitcast.47), channel_id=1, source_target_pairs={{0,8},{8,16},{16,24},{24,25},{25,17},{17,9},{9,1},{1,2},{2,10},{10... | collective-permute-start | bytes 245768 | tf_op jit(solution)/shard_map/ppermute | solution.py:565
  36.5 6.4 %collective-permute-start.3 = (f32[176,128]{1,0:T(8,128)S(1)}, f32[176,128]{1,0:T(8,128)S(1)}, u32[]{:S(2)}, u32[]{:S(2)}) collective-permute-start(f32[176,128]{1,0:T(8,128)S(1)} %pad_maximum_fusion.3), channel_id=1, source_target_pairs={{8,0},{16,8},{24,16},{25,24},{17,25},{9,17},{1,9},{2,1},{10,2},{18... | collective-permute-start | bytes 270344 | tf_op jit(solution)/shard_map/ppermute | solution.py:565
  41.0 12.4 %collective-permute-start.11 = (f32[256,128]{1,0:T(8,128)S(1)}, f32[256,128]{1,0:T(8,128)S(1)}, u32[]{:S(2)}, u32[]{:S(2)}) collective-permute-start(f32[256,128]{1,0:T(8,128)S(1)} %get-tuple-element.75), channel_id=1, source_target_pairs={{0,16},{8,24},{16,0},{24,8},{1,17},{9,25},{17,1},{25,9},{2,18},{10... | collective-permute-start | bytes 393224 | tf_op jit(solution)/shard_map/ppermute | solution.py:546
  42.9 11.6 %collective-permute-start.9 = (f32[256,128]{1,0:T(8,128)S(1)}, f32[256,128]{1,0:T(8,128)S(1)}, u32[]{:S(2)}, u32[]{:S(2)}) collective-permute-start(f32[256,128]{1,0:T(8,128)S(1)} %bitcast.42), channel_id=1, source_target_pairs={{0,8},{8,16},{16,24},{24,25},{25,17},{17,9},{9,1},{1,2},{2,10},{10... | collective-permute-start | bytes 393224 | tf_op jit(solution)/shard_map/ppermute | solution.py:565
  52.0 5.0 %collective-permute-start.10 = (f32[256,128]{1,0:T(8,128)S(1)}, f32[256,128]{1,0:T(8,128)S(1)}, u32[]{:S(2)}, u32[]{:S(2)}) collective-permute-start(f32[256,128]{1,0:T(8,128)S(1)} %bitcast.41), channel_id=1, source_target_pairs={{8,0},{16,8},{24,16},{25,24},{17,25},{9,17},{1,9},{2,1},{10,2},{18... | collective-permute-start | bytes 393224 | tf_op jit(solution)/shard_map/ppermute | solution.py:565
  57.0 10.2 %collective-permute-start.12 = (f32[264,128]{1,0:T(8,128)S(1)}, f32[264,128]{1,0:T(8,128)S(1)}, u32[]{:S(2)}, u32[]{:S(2)}) collective-permute-start(f32[264,128]{1,0:T(8,128)S(1)} %pad_maximum_fusion), channel_id=1, source_target_pairs={{4,0},{0,4},{5,1},{1,5},{6,2},{2,6},{7,3},{3,7},{12,8},{8,12},{13,... | collective-permute-start | bytes 405512 | tf_op jit(solution)/shard_map/ppermute | solution.py:560
  58.9 8.3 %collective-permute-start.13 = (f32[256,128]{1,0:T(8,128)S(1)}, f32[256,128]{1,0:T(8,128)S(1)}, u32[]{:S(2)}, u32[]{:S(2)}) collective-permute-start(f32[256,128]{1,0:T(8,128)S(1)} %get-tuple-element.88), channel_id=1, source_target_pairs={{0,8},{8,16},{16,24},{24,0},{1,9},{9,17},{17,25},{25,1},{2,10},{10... | collective-permute-start | bytes 393224 | tf_op jit(solution)/shard_map/ppermute | solution.py:546
  60.3 6.8 %collective-permute-start.14 = (f32[256,128]{1,0:T(8,128)S(1)}, f32[256,128]{1,0:T(8,128)S(1)}, u32[]{:S(2)}, u32[]{:S(2)}) collective-permute-start(f32[256,128]{1,0:T(8,128)S(1)} %get-tuple-element.89), channel_id=1, source_target_pairs={{0,24},{8,0},{16,8},{24,16},{1,25},{9,1},{17,9},{25,17},{2,26},{10... | collective-permute-start | bytes 393224 | tf_op jit(solution)/shard_map/ppermute | solution.py:546
  65.5 16.8 %collective-permute-start.20 = (f32[256,128]{1,0:T(8,128)S(1)}, f32[256,128]{1,0:T(8,128)S(1)}, u32[]{:S(2)}, u32[]{:S(2)}) collective-permute-start(f32[256,128]{1,0:T(8,128)S(1)} %get-tuple-element.98), channel_id=1, source_target_pairs={{0,16},{8,24},{16,0},{24,8},{1,17},{9,25},{17,1},{25,9},{2,18},{10... | collective-permute-start | bytes 393224 | tf_op jit(solution)/shard_map/ppermute | solution.py:546
  67.7 9.2 %collective-permute-start.15 = (f32[168,128]{1,0:T(8,128)S(1)}, f32[168,128]{1,0:T(8,128)S(1)}, u32[]{:S(2)}, u32[]{:S(2)}) collective-permute-start(f32[168,128]{1,0:T(8,128)S(1)} %pad_maximum_fusion.6), channel_id=1, source_target_pairs={{8,0},{16,8},{24,16},{25,24},{17,25},{9,17},{1,9},{2,1},{10,2},{18... | collective-permute-start | bytes 258056 | tf_op jit(solution)/shard_map/ppermute | solution.py:565
  67.8 5.9 %collective-permute-start.16 = (f32[160,128]{1,0:T(8,128)S(1)}, f32[160,128]{1,0:T(8,128)S(1)}, u32[]{:S(2)}, u32[]{:S(2)}) collective-permute-start(f32[160,128]{1,0:T(8,128)S(1)} %pad_maximum_fusion.7), channel_id=1, source_target_pairs={{0,8},{8,16},{16,24},{24,25},{25,17},{17,9},{9,1},{1,2},{2,10},{10... | collective-permute-start | bytes 245768 | tf_op jit(solution)/shard_map/ppermute | solution.py:565
  69.8 14.9 %collective-permute-start.21 = (f32[256,128]{1,0:T(8,128)S(1)}, f32[256,128]{1,0:T(8,128)S(1)}, u32[]{:S(2)}, u32[]{:S(2)}) collective-permute-start(f32[256,128]{1,0:T(8,128)S(1)} %get-tuple-element.99), channel_id=1, source_target_pairs={{0,8},{8,16},{16,24},{24,0},{1,9},{9,17},{17,25},{25,1},{2,10},{10... | collective-permute-start | bytes 393224 | tf_op jit(solution)/shard_map/ppermute | solution.py:546
  71.8 12.9 %collective-permute-start.22 = (f32[256,128]{1,0:T(8,128)S(1)}, f32[256,128]{1,0:T(8,128)S(1)}, u32[]{:S(2)}, u32[]{:S(2)}) collective-permute-start(f32[256,128]{1,0:T(8,128)S(1)} %get-tuple-element.100), channel_id=1, source_target_pairs={{0,24},{8,0},{16,8},{24,16},{1,25},{9,1},{17,9},{25,17},{2,26},{10... | collective-permute-start | bytes 393224 | tf_op jit(solution)/shard_map/ppermute | solution.py:546
  76.9 7.8 %copy-start = (f32[2,16,64,128]{3,2,1,0:T(8,128)S(1)}, f32[2,16,64,128]{3,2,1,0:T(8,128)}, u32[]{:S(2)}) copy-start(f32[2,16,64,128]{3,2,1,0:T(8,128)} %gain.2) | copy-start | bytes 3145732
  76.9 7.8 %copy-start.1 = (s32[16,64,128]{2,1,0:T(8,128)S(1)}, s32[16,64,128]{2,1,0:T(8,128)}, u32[]{:S(2)}) copy-start(s32[16,64,128]{2,1,0:T(8,128)} %mask.5) | copy-start | bytes 1572868
  80.0 10.6 %collective-permute-start.17 = (f32[256,128]{1,0:T(8,128)S(1)}, f32[256,128]{1,0:T(8,128)S(1)}, u32[]{:S(2)}, u32[]{:S(2)}) collective-permute-start(f32[256,128]{1,0:T(8,128)S(1)} %get-tuple-element.95), channel_id=1, source_target_pairs={{0,16},{8,24},{16,0},{24,8},{1,17},{9,25},{17,1},{25,9},{2,18},{10... | collective-permute-start | bytes 393224 | tf_op jit(solution)/shard_map/ppermute | solution.py:546
  80.9 9.7 %collective-permute-start.18 = (f32[256,128]{1,0:T(8,128)S(1)}, f32[256,128]{1,0:T(8,128)S(1)}, u32[]{:S(2)}, u32[]{:S(2)}) collective-permute-start(f32[256,128]{1,0:T(8,128)S(1)} %get-tuple-element.96), channel_id=1, source_target_pairs={{0,8},{8,16},{16,24},{24,0},{1,9},{9,17},{17,25},{25,1},{2,10},{10... | collective-permute-start | bytes 393224 | tf_op jit(solution)/shard_map/ppermute | solution.py:546
  82.4 8.2 %collective-permute-start.19 = (f32[256,128]{1,0:T(8,128)S(1)}, f32[256,128]{1,0:T(8,128)S(1)}, u32[]{:S(2)}, u32[]{:S(2)}) collective-permute-start(f32[256,128]{1,0:T(8,128)S(1)} %get-tuple-element.97), channel_id=1, source_target_pairs={{0,24},{8,0},{16,8},{24,16},{1,25},{9,1},{17,9},{25,17},{2,26},{10... | collective-permute-start | bytes 393224 | tf_op jit(solution)/shard_map/ppermute | solution.py:546

commit v12 on v11

--- a/solution.py
+++ b/solution.py
@@ -109,7 +109,7 @@
                     held[slot, pl.ds(at, rows), :] = block
             return carry
 
-        lax.fori_loop(step * some, (step + 1) * some, one, 0, unroll=True)
+        lax.fori_loop(step * some, (step + 1) * some, one, 0)
     slots = position()[0]
     for copy in copies([(held.at[slots[d]], out) for d, out in enumerate(outs)], out_sems):
         copy.wait()
@@ -140,39 +140,50 @@
     levels, length, cols = along_i.shape
     groups = len(pieces[0][0])
     width = cols // groups
-    halos, outs = refs[masked:-4 - groups - 3 * masked], refs[-4 - groups - 3 * masked:-4 - 3 * masked]
+    extra, refs = refs[:1 if masked else 2], refs[1 if masked else 2:]
+    outs, refs = refs[:groups], refs[groups:]
+    ends, refs = refs[:masked], refs[masked:]
     held, slots_held, sems, fetch_sems = refs[-4:]
     unroll = held.shape[0]
     number = levels // unroll
     starts, rows = pieces[0]
     group = lane_groups(rows, cols, groups)
-    if masked:
-        sources, (along_i, along_j, sea) = (along_i, along_j, refs[0]), refs[-7:-4]
-        fetched = []
-        for side, (source, target) in enumerate(zip(sources, (along_i, along_j, sea))):
-            pairs = [(source.at[pl.ds(k * unroll, unroll)], target.at[pl.ds(k * unroll, unroll)]) for k in range(number)]
-            fetched.append(copies(pairs, fetch_sems.at[side]))
+    sources = (along_i, along_j) + (extra if masked else ())
+    targets = refs[:-4]
+    fetched = []
+    for side, (source, target) in enumerate(zip(sources, targets)):
+        pairs = [(source.at[pl.ds(k * unroll, unroll)], target.at[pl.ds(k * unroll, unroll)]) for k in range(number)]
+        fetched.append(copies(pairs, fetch_sems.at[side]))
 
     def put(at, blocks):
         for slot, block in enumerate(blocks):
             slots_held[slot, pl.ds(at, block.shape[0]), :] = block
 
-    for side, weight in enumerate((along_i, along_j)):
-        for outer in range(number):
+    for side, weight in enumerate(targets[:2]):
+        for copy in fetched[side]:
+            copy.wait()
+
+        def some(outer, carry, side=side, weight=weight):
+            edges = []
+            first = side * levels + outer * unroll
             if masked:
-                fetched[side][outer].wait()
-            edges = []
+                for end, at in enumerate((0, length - STEPS)):
+                    block = [weight[outer * unroll + k, pl.ds(at, STEPS), :] for k in range(unroll)]
+                    to = pl.multiple_of((end * 2 * levels + first) * STEPS, 8)
+                    ends[0][pl.ds(to, unroll * STEPS), :] = jnp.concatenate(block, axis=0)
+            else:
+                to = pl.multiple_of(first * STEPS, 8)
+                blocks = [halo[pl.ds(to, unroll * STEPS), :] for halo in extra]
             for k in range(unroll):
                 level = outer * unroll + k
-                index = side * levels + level
-                if halos:
-                    for halo, at in zip(halos, (0, STEPS + length)):
-                        held[k, pl.ds(at, STEPS), :] = halo[pl.ds(index * STEPS, STEPS), :]
+                if masked:
+                    mine = [weight[level, pl.ds(start - STEPS, rows), :] for start in starts]
+                else:
+                    for block, at in zip(blocks, (0, STEPS + length)):
+                        held[k, pl.ds(at, STEPS), :] = block[k * STEPS:(k + 1) * STEPS]
                     held[k, pl.ds(STEPS, length), :] = weight[level]
-                    blocks = [held[k, pl.ds(start, rows), :] for start in starts]
-                else:
-                    blocks = [weight[level, pl.ds(start - STEPS, rows), :] for start in starts]
-                put(index * rows, swap(blocks, group, width))
+                    mine = [held[k, pl.ds(start, rows), :] for start in starts]
+                put(pl.multiple_of((first + k) * rows, 8), swap(mine, group, width))
                 if len(pieces) > 1:
                     small = pieces[1][0]
                     low, high = small[0] - 2 * STEPS, small[groups // 2] - STEPS
@@ -184,14 +195,16 @@
                 each = pieces[1][1]
                 pairs = lax.broadcasted_iota(jnp.int32, edges[0].shape, 0) // each
                 edges = swap(edges, pairs, each, 0)
-                at = 2 * levels * rows + (side * levels + outer * unroll) * each
-                put(at, swap(edges, lane_groups(unroll * each, cols, groups), width))
+                to = pl.multiple_of(2 * levels * rows + first * each, 8)
+                put(to, swap(edges, lane_groups(unroll * each, cols, groups), width))
+            return carry
+
+        lax.fori_loop(0, number, some, 0)
     if masked:
-        depth = jnp.zeros((length, cols), sea.dtype)
-        for outer in range(number):
-            fetched[2][outer].wait()
-            for level in range(outer * unroll, (outer + 1) * unroll):
-                depth = depth + sea[level]
+        for copy in fetched[2]:
+            copy.wait()
+        sea = targets[2]
+        depth = lax.fori_loop(0, levels, lambda level, x: x + sea[level], jnp.zeros((length, cols), sea.dtype), unroll=4)
         depth = depth.astype(jnp.float32)
         size = length // groups
         blocks = [depth[a * size:(a + 1) * size] for a in range(groups)]
@@ -205,14 +218,16 @@
     levels, length, cols = along_i.shape
     groups = len(pieces[0][0])
     shape = (2 * levels * sum(rows for _, rows in pieces) + len(mask) * length // groups, cols)
+    ends = [(4 * levels * STEPS, cols)] * len(mask)
     unroll = 4
+    anywhere = pl.BlockSpec(memory_space=pl.ANY)
     return list(
         pl.pallas_call(
             functools.partial(pack_kernel, pieces, len(mask)),
-            in_specs=[pl.BlockSpec(memory_space=pl.ANY) if mask else vmem()] * (2 + len(mask) + len(halos)),
-            out_specs=[pl.BlockSpec(memory_space=pl.ANY)] * groups,
-            out_shape=[jax.ShapeDtypeStruct(shape, jnp.float32)] * groups,
-            scratch_shapes=[pltpu.VMEM(x.shape, x.dtype) for x in ([along_i, along_j, *mask] if mask else [])]
+            in_specs=[anywhere] * (2 + len(mask)) + [vmem()] * len(halos),
+            out_specs=[anywhere] * groups + [vmem()] * len(ends),
+            out_shape=[jax.ShapeDtypeStruct(x, jnp.float32) for x in [shape] * groups + ends],
+            scratch_shapes=[pltpu.VMEM(x.shape, x.dtype) for x in (along_i, along_j, *mask)]
             + [
                 pltpu.VMEM((unroll, length + 2 * STEPS, cols), jnp.float32),
                 pltpu.VMEM((groups, *shape), jnp.float32),
@@ -589,19 +604,13 @@
 
     inner_size = len(inner_rows) // devices
     inner_messages = weight_messages(inner_pieces, diffusion_i, diffusion_j, [sea_mask])
+    *inner_messages, ends = inner_messages
     inner_parts = exchange(inner_messages)
-    inner_messages, edge_i, edge_j, increment, norm_gain = lax.optimization_barrier(
-        (inner_messages, diffusion_i, diffusion_j, increment, norm_gain)
-    )
-    halos = halo_i(
-        *[
-            jnp.concatenate([flat(edge_i[:, at]), flat(edge_j[:, at])], axis=0)
-            for at in (slice(0, STEPS), slice(-STEPS, None))
-        ]
-    )
+    _, increment, norm_gain = lax.optimization_barrier((inner_messages[0], increment, norm_gain))
     messages = scaled_messages(increment, norm_gain, sea_mask, devices)
     scaled = exchange(messages)
-    messages, halos = lax.optimization_barrier((messages, halos))
+    _, ends = lax.optimization_barrier((messages[0], ends))
+    halos = halo_i(*cut(ends, ends.shape[0] // 2, ends.shape[0] // 2))
     outer_messages = weight_messages(outer_pieces, diffusion_i, diffusion_j, halos=halos)
 
     depth = sum(part[2 * levels * inner_size:] for part in inner_parts)

time: 92.3 us -> 93 us (level)
  starting transfers between devices: 49.8 us -> 43.9 us
  waiting for transfers between devices: 19.6 us -> 24.2 us
  Pallas kernels: 20.3 us -> 23.9 us
  local copies, waits for them, and re-layouts: 1.87 us -> 0.33 us
    ppermute x3, starting transfers between devices: 22.9 us -> 16.2 us  [halo_j(): lax.ppermute(last, ('lev', 'gy'), ahead)]
    ppermute x2, waiting for transfers between devices: 0.01 us -> 3.29 us  [halo_i(): both = lax.ppermute(jnp.concatenate([first, last], axis=0), 'gx', up)]
    pallas_call x2, Pallas kernels: 5.63 us -> 7.72 us  [weight_messages(): pl.pallas_call(functools.partial(pack_kernel, pieces, len(mask)), in_spec...]
    pallas_call x1, Pallas kernels: 3.25 us -> 4.83 us  [scaled_messages(): pl.pallas_call(scaled_kernel, in_specs=[pl.BlockSpec(memory_space=pl.ANY)...]
    unnamed x18, local copies, waits for them, and re-layouts: 1.56 us -> 0.04 us
    ppermute x15, waiting for transfers between devices: 12.8 us -> 14 us  [shift(): lax.ppermute(x, 'lev', [(k, (k + d) % devices) for k in range(devices)])]
  transfers between devices with their start and end apart: 23 -> 23, of which waited for: 8 -> 9; matrix products, arithmetic and copies ran while one was open for 0% -> 0% of each run, Pallas kernels for 17% -> 20%
where the time goes in v12:
time: 93 us; the launch traced here: 92.8 us
  starting transfers between devices  43.9 us (47%)
  waiting for transfers between devices  24.2 us (26%)
  Pallas kernels  23.9 us (26%)
    ppermute x15, starting transfers between devices, shift(): lax.ppermute(x, 'lev', [(k, (k + d) % devices) for k in range(devices)])  24.2 us
    ppermute x3, starting transfers between devices, halo_j(): lax.ppermute(last, ('lev', 'gy'), ahead)  16.2 us
    ppermute x15, waiting for transfers between devices, shift(): lax.ppermute(x, 'lev', [(k, (k + d) % devices) for k in range(devices)])  14 us
    pallas_call x2, Pallas kernels, weight_messages(): pl.pallas_call(functools.partial(pack_kernel, pieces, len(mask)), in_spec...  7.72 us
    pallas_call x2, Pallas kernels, spread_mix(): pl.pallas_call(kernel, in_specs=[vmem()] * (1 + len(arrays)), out_specs=[...  5.9 us
    ppermute x3, waiting for transfers between devices, halo_j(): lax.ppermute(first, ('lev', 'gy'), back)  5.67 us
    pallas_call x1, Pallas kernels, scaled_messages(): pl.pallas_call(scaled_kernel, in_specs=[pl.BlockSpec(memory_space=pl.ANY)...  4.83 us
    ppermute x2, starting transfers between devices, halo_i(): both = lax.ppermute(jnp.concatenate([first, last], axis=0), 'gx', up)  3.45 us
  transfers between devices with their start and end apart: 23, of which 9 were waited for; matrix products, arithmetic and copies ran while one was open for 0% of the time, Pallas kernels for 20%

profile of v12, /device:TPU:0, one launch (start us, length us, event | category | flops | bytes accessed | tf_op | source)
XLA Modules:
  0.0 92.8 jit_solution(17316144092335453044)
XLA Ops:
  0.0 4.2 %weight_messages.2 = (f32[336,128]{1,0:T(8,128)}, f32[336,128]{1,0:T(8,128)}, f32[336,128]{1,0:T(8,128)}, f32[336,128]{1,0:T(8,128)}, f32[256,128]{1,0:T(8,128)}) custom-call(f32[16,64,128]{2,1,0:T(8,128)} %along_i.3, f32[16,64,128]{2,1,0:T(8,128)} %along_j.3, s32[16,64,128]{2,1,0:T(8,128)} %mask.5), custom_call_target="tpu_custom_call" | custom-call | tf_op jit(solution)/shard_map/weight_messages/pallas_call | solution.py:225
  4.2 4.1 %collective-permute-start = (f32[336,128]{1,0:T(8,128)}, f32[336,128]{1,0:T(8,128)S(1)}, u32[]{:S(2)}, u32[]{:S(2)}) collective-permute-start(f32[336,128]{1,0:T(8,128)} %get-tuple-element.53), channel_id=1, source_target_pairs={{0,16},{8,24},{16,0},{24,8},{1,17},{9,25},{17,1},{25,9},{2,18},{10... | collective-permute-start | bytes 516104 | tf_op jit(solution)/shard_map/ppermute | solution.py:561
  8.3 1.6 %collective-permute-start.1 = (f32[336,128]{1,0:T(8,128)}, f32[336,128]{1,0:T(8,128)S(1)}, u32[]{:S(2)}, u32[]{:S(2)}) collective-permute-start(f32[336,128]{1,0:T(8,128)} %get-tuple-element.54), channel_id=1, source_target_pairs={{0,8},{8,16},{16,24},{24,0},{1,9},{9,17},{17,25},{25,1},{2,10},{10... | collective-permute-start | bytes 516104 | tf_op jit(solution)/shard_map/ppermute | solution.py:561
  9.9 2.2 %collective-permute-start.2 = (f32[336,128]{1,0:T(8,128)}, f32[336,128]{1,0:T(8,128)S(1)}, u32[]{:S(2)}, u32[]{:S(2)}) collective-permute-start(f32[336,128]{1,0:T(8,128)} %get-tuple-element.55), channel_id=1, source_target_pairs={{0,24},{8,0},{16,8},{24,16},{1,25},{9,1},{17,9},{25,17},{2,26},{10... | collective-permute-start | bytes 516104 | tf_op jit(solution)/shard_map/ppermute | solution.py:561
  12.2 4.8 %scaled_messages.1 = (f32[512,128]{1,0:T(8,128)}, f32[512,128]{1,0:T(8,128)}, f32[512,128]{1,0:T(8,128)}, f32[512,128]{1,0:T(8,128)}) custom-call(f32[2,16,64,128]{3,2,1,0:T(8,128)} %increment, f32[2,16,64,128]{3,2,1,0:T(8,128)} %gain.2, s32[16,64,128]{2,1,0:T(8,128)} %mask.5), custom_call_target="tpu_custom_call" | custom-call | tf_op jit(solution)/shard_map/scaled_messages/pallas_call | solution.py:121
  17.0 0.0 copy-start.2
  17.0 0.0 copy-done.8
  17.0 1.6 %collective-permute-start.5 = (f32[256,128]{1,0:T(8,128)S(1)}, f32[256,128]{1,0:T(8,128)S(1)}, u32[]{:S(2)}, u32[]{:S(2)}) collective-permute-start(f32[256,128]{1,0:T(8,128)S(1)} %copy-done.8), channel_id=1, source_target_pairs={{4,0},{0,4},{5,1},{1,5},{6,2},{2,6},{7,3},{3,7},{12,8},{8,12},{13,... | collective-permute-start | bytes 393224 | tf_op jit(solution)/shard_map/ppermute | solution.py:575
  18.6 0.0 collective-permute-start.4
  18.6 0.0 copy-done.6
  18.7 0.1 copy.13.matrix
  18.8 3.3 %collective-permute-done.5 = f32[256,128]{1,0:T(8,128)S(1)} collective-permute-done((f32[256,128]{1,0:T(8,128)S(1)}, f32[256,128]{1,0:T(8,128)S(1)}, u32[]{:S(2)}, u32[]{:S(2)}) %collective-permute-start.5) | collective-permute-done | bytes 131104 | tf_op jit(solution)/shard_map/ppermute | solution.py:575
  22.0 0.0 collective-permute-start.6
  22.1 0.0 copy-done.3
  22.1 3.5 %weight_messages.3 = (f32[256,128]{1,0:T(8,128)S(1)}, f32[256,128]{1,0:T(8,128)S(1)}, f32[256,128]{1,0:T(8,128)S(1)}, f32[256,128]{1,0:T(8,128)S(1)}) custom-call(f32[16,64,128]{2,1,0:T(8,128)S(1)} %copy-done.2, f32[16,64,128]{2,1,0:T(8,128)S(1)} %copy-done.3, f32[128,128]{1,0:T(8,128)S(1)} %get-tuple-element.112.refs_0_, ...), custom_call_target="tpu_custom_call" | custom-call | tf_op jit(solution)/shard_map/weight_messages/pallas_call | solution.py:225
  25.6 0.0 collective-permute-done.refs_2_
  25.6 3.9 %collective-permute-start.7 = (f32[512,128]{1,0:T(8,128)S(1)}, f32[512,128]{1,0:T(8,128)S(1)}, u32[]{:S(2)}, u32[]{:S(2)}) collective-permute-start(f32[512,128]{1,0:T(8,128)S(1)} %copy-done.7), channel_id=1, source_target_pairs={{0,24},{8,0},{16,8},{24,16},{1,25},{9,1},{17,9},{25,17},{2,26},{10... | collective-permute-start | bytes 786440 | tf_op jit(solution)/shard_map/ppermute | solution.py:561
  29.5 0.0 collective-permute-done.1.refs_3_
  29.5 0.0 collective-permute-done.2.refs_4_
  29.5 0.4 turn_weights.2.refs_5_.refs_10_
  30.0 0.0 copy-start.4
  30.0 7.2 %collective-permute-start.8 = (f32[160,128]{1,0:T(8,128)S(1)}, f32[160,128]{1,0:T(8,128)S(1)}, u32[]{:S(2)}, u32[]{:S(2)}) collective-permute-start(f32[160,128]{1,0:T(8,128)S(1)} %bitcast.39), channel_id=1, source_target_pairs={{0,8},{8,16},{16,24},{24,25},{25,17},{17,9},{9,1},{1,2},{2,10},{10... | collective-permute-start | bytes 245768 | tf_op jit(solution)/shard_map/ppermute | solution.py:580
  37.2 0.0 collective-permute-start.3
  37.2 4.5 %collective-permute-done.4.refs_1_ = f32[512,128]{1,0:T(8,128)S(1)} collective-permute-done((f32[512,128]{1,0:T(8,128)}, f32[512,128]{1,0:T(8,128)S(1)}, u32[]{:S(2)}, u32[]{:S(2)}) %collective-permute-start.4) | collective-permute-done | bytes 262176 | tf_op jit(solution)/shard_map/ppermute | solution.py:561
  41.7 0.0 collective-permute-start.11
  41.7 0.0 collective-permute-done.6.refs_2_
  41.7 2.2 %collective-permute-done.7.refs_3_ = f32[512,128]{1,0:T(8,128)S(1)} collective-permute-done((f32[512,128]{1,0:T(8,128)S(1)}, f32[512,128]{1,0:T(8,128)S(1)}, u32[]{:S(2)}, u32[]{:S(2)}) %collective-permute-start.7) | collective-permute-done | bytes 262176 | tf_op jit(solution)/shard_map/ppermute | solution.py:561
  43.9 1.8 %adjoint_mix.1.refs_2_.refs_4_ = f32[64,32,128]{2,1,0:T(8,128)S(1)} custom-call(f32[128,128]{1,0:T(8,128)S(1)} %copy.13.matrix, f32[16,128]{1,0:T(8,128)S(1)} %slice_add_fusion.refs_0_.depths, f32[512,128]{1,0:T(8,128)S(1)} %copy-done.4, f32[512,128]{1,0:T(8,128)S(1)} %collective-permute-done.4.refs_1_, f32[512,128]{1,0:T(8,128)S(1)} %collective-permute-done.6.refs_2_, ...), custom_call_target="tpu_custom_call" | custom-call | tf_op jit(solution)/shard_map/adjoint_mix/pallas_call | solution.py:287
  45.8 0.0 collective-permute-done.3
  45.8 0.0 collective-permute-done.8.refs_6_.refs_11_
  45.8 6.9 %collective-permute-start.9 = (f32[256,128]{1,0:T(8,128)S(1)}, f32[256,128]{1,0:T(8,128)S(1)}, u32[]{:S(2)}, u32[]{:S(2)}) collective-permute-start(f32[256,128]{1,0:T(8,128)S(1)} %bitcast.38), channel_id=1, source_target_pairs={{0,8},{8,16},{16,24},{24,25},{25,17},{17,9},{9,1},{1,2},{2,10},{10... | collective-permute-start | bytes 393224 | tf_op jit(solution)/shard_map/ppermute | solution.py:580
  52.7 0.0 collective-permute-start.10
  52.7 1.3 %collective-permute-done.11.refs_3_ = f32[256,128]{1,0:T(8,128)S(1)} collective-permute-done((f32[256,128]{1,0:T(8,128)S(1)}, f32[256,128]{1,0:T(8,128)S(1)}, u32[]{:S(2)}, u32[]{:S(2)}) %collective-permute-start.11) | collective-permute-done | bytes 131104 | tf_op jit(solution)/shard_map/ppermute | solution.py:561
  54.1 1.2 %collective-permute-done.9.refs_3_.refs_5_ = f32[256,128]{1,0:T(8,128)S(1)} collective-permute-done((f32[256,128]{1,0:T(8,128)S(1)}, f32[256,128]{1,0:T(8,128)S(1)}, u32[]{:S(2)}, u32[]{:S(2)}) %collective-permute-start.9) | collective-permute-done | bytes 131104 | tf_op jit(solution)/shard_map/ppermute | solution.py:580
  55.3 2.4 %collective-permute-done.10.refs_4_.refs_6_ = f32[256,128]{1,0:T(8,128)S(1)} collective-permute-done((f32[256,128]{1,0:T(8,128)S(1)}, f32[256,128]{1,0:T(8,128)S(1)}, u32[]{:S(2)}, u32[]{:S(2)}) %collective-permute-start.10) | collective-permute-done | bytes 131104 | tf_op jit(solution)/shard_map/ppermute | solution.py:580
  57.7 1.9 %collective-permute-start.12 = (f32[264,128]{1,0:T(8,128)S(1)}, f32[264,128]{1,0:T(8,128)S(1)}, u32[]{:S(2)}, u32[]{:S(2)}) collective-permute-start(f32[264,128]{1,0:T(8,128)S(1)} %pad_maximum_fusion), channel_id=1, source_target_pairs={{4,0},{0,4},{5,1},{1,5},{6,2},{2,6},{7,3},{3,7},{12,8},{8,12},{13,... | collective-permute-start | bytes 405512 | tf_op jit(solution)/shard_map/ppermute | solution.py:575
  59.6 1.5 %collective-permute-start.13 = (f32[256,128]{1,0:T(8,128)S(1)}, f32[256,128]{1,0:T(8,128)S(1)}, u32[]{:S(2)}, u32[]{:S(2)}) collective-permute-start(f32[256,128]{1,0:T(8,128)S(1)} %get-tuple-element.84), channel_id=1, source_target_pairs={{0,8},{8,16},{16,24},{24,0},{1,9},{9,17},{17,25},{25,1},{2,10},{10... | collective-permute-start | bytes 393224 | tf_op jit(solution)/shard_map/ppermute | solution.py:561
  61.1 2.4 %collective-permute-start.14 = (f32[256,128]{1,0:T(8,128)S(1)}, f32[256,128]{1,0:T(8,128)S(1)}, u32[]{:S(2)}, u32[]{:S(2)}) collective-permute-start(f32[256,128]{1,0:T(8,128)S(1)} %get-tuple-element.85), channel_id=1, source_target_pairs={{0,24},{8,0},{16,8},{24,16},{1,25},{9,1},{17,9},{25,17},{2,26},{10... | collective-permute-start | bytes 393224 | tf_op jit(solution)/shard_map/ppermute | solution.py:561
  63.4 2.9 %spread_mix.2 = (f32[256,128]{1,0:T(8,128)S(1)}, f32[256,128]{1,0:T(8,128)S(1)}, f32[256,128]{1,0:T(8,128)S(1)}, f32[256,128]{1,0:T(8,128)S(1)}) custom-call(f32[128,128]{1,0:T(8,128)S(1)} %get-tuple-element.119.matrix, f32[16,128]{1,0:T(8,128)S(1)} %slice_add_fusion.refs_0_.depths, f32[16,128]{1,0:T(8,128)S(1)} %split.46.refs_1_, ...), custom_call_target="tpu_custom_call" | custom-call | tf_op jit(solution)/shard_map/spread_mix/pallas_call | solution.py:475
  66.3 0.1 collective-permute-start.20
  66.4 1.5 %collective-permute-done.13.refs_4_ = f32[256,128]{1,0:T(8,128)S(1)} collective-permute-done((f32[256,128]{1,0:T(8,128)S(1)}, f32[256,128]{1,0:T(8,128)S(1)}, u32[]{:S(2)}, u32[]{:S(2)}) %collective-permute-start.13) | collective-permute-done | bytes 131104 | tf_op jit(solution)/shard_map/ppermute | solution.py:561
  67.9 0.0 collective-permute-done.14.refs_5_
  67.9 0.0 collective-permute-done.12
  68.0 0.4 turn_weights.3.refs_13_
  68.4 0.1 collective-permute-start.15
  68.5 2.1 %collective-permute-start.16 = (f32[160,128]{1,0:T(8,128)S(1)}, f32[160,128]{1,0:T(8,128)S(1)}, u32[]{:S(2)}, u32[]{:S(2)}) collective-permute-start(f32[160,128]{1,0:T(8,128)S(1)} %pad_maximum_fusion.6), channel_id=1, source_target_pairs={{0,8},{8,16},{16,24},{24,25},{25,17},{17,9},{9,1},{1,2},{2,10},{10... | collective-permute-start | bytes 245768 | tf_op jit(solution)/shard_map/ppermute | solution.py:580
  70.6 1.9 %collective-permute-start.21 = (f32[256,128]{1,0:T(8,128)S(1)}, f32[256,128]{1,0:T(8,128)S(1)}, u32[]{:S(2)}, u32[]{:S(2)}) collective-permute-start(f32[256,128]{1,0:T(8,128)S(1)} %get-tuple-element.95), channel_id=1, source_target_pairs={{0,8},{8,16},{16,24},{24,0},{1,9},{9,17},{17,25},{25,1},{2,10},{10... | collective-permute-start | bytes 393224 | tf_op jit(solution)/shard_map/ppermute | solution.py:561
  72.6 1.9 %collective-permute-start.22 = (f32[256,128]{1,0:T(8,128)S(1)}, f32[256,128]{1,0:T(8,128)S(1)}, u32[]{:S(2)}, u32[]{:S(2)}) collective-permute-start(f32[256,128]{1,0:T(8,128)S(1)} %get-tuple-element.96), channel_id=1, source_target_pairs={{0,24},{8,0},{16,8},{24,16},{1,25},{9,1},{17,9},{25,17},{2,26},{10... | collective-permute-start | bytes 393224 | tf_op jit(solution)/shard_map/ppermute | solution.py:561
  74.4 0.0 collective-permute-done.16
  74.5 3.2 %collective-permute-done.15 = f32[168,128]{1,0:T(8,128)S(1)} collective-permute-done((f32[168,128]{1,0:T(8,128)S(1)}, f32[168,128]{1,0:T(8,128)S(1)}, u32[]{:S(2)}, u32[]{:S(2)}) %collective-permute-start.15) | collective-permute-done | bytes 86048 | tf_op jit(solution)/shard_map/ppermute | solution.py:580
  77.7 0.0 copy-start
  77.7 0.0 copy-start.1
  77.7 3.0 %spread_mix.3 = (f32[256,128]{1,0:T(8,128)S(1)}, f32[256,128]{1,0:T(8,128)S(1)}, f32[256,128]{1,0:T(8,128)S(1)}, f32[256,128]{1,0:T(8,128)S(1)}) custom-call(f32[128,128]{1,0:T(8,128)S(1)} %get-tuple-element.119.matrix, f32[16,128]{1,0:T(8,128)S(1)} %slice_add_fusion.refs_0_.depths, f32[16,128]{1,0:T(8,128)S(1)} %split.46.refs_1_, ...), custom_call_target="tpu_custom_call" | custom-call | tf_op jit(solution)/shard_map/spread_mix/pallas_call | solution.py:475
  80.8 0.9 collective-permute-start.17
  81.6 1.5 %collective-permute-start.18 = (f32[256,128]{1,0:T(8,128)S(1)}, f32[256,128]{1,0:T(8,128)S(1)}, u32[]{:S(2)}, u32[]{:S(2)}) collective-permute-start(f32[256,128]{1,0:T(8,128)S(1)} %get-tuple-element.92), channel_id=1, source_target_pairs={{0,8},{8,16},{16,24},{24,0},{1,9},{9,17},{17,25},{25,1},{2,10},{10... | collective-permute-start | bytes 393224 | tf_op jit(solution)/shard_map/ppermute | solution.py:561
  83.1 0.0 collective-permute-done.20.refs_1_
  83.1 2.4 %collective-permute-start.19 = (f32[256,128]{1,0:T(8,128)S(1)}, f32[256,128]{1,0:T(8,128)S(1)}, u32[]{:S(2)}, u32[]{:S(2)}) collective-permute-start(f32[256,128]{1,0:T(8,128)S(1)} %get-tuple-element.93), channel_id=1, source_target_pairs={{0,24},{8,0},{16,8},{24,16},{1,25},{9,1},{17,9},{25,17},{2,26},{10... | collective-permute-start | bytes 393224 | tf_op jit(solution)/shard_map/ppermute | solution.py:561
  85.5 0.0 collective-permute-done.21.refs_2_
  85.5 0.0 collective-permute-done.22.refs_3_
  85.5 1.4 %result.2.refs_4_ = f32[2,16,64,128]{3,2,1,0:T(8,128)} custom-call(f32[2,16,64,128]{3,2,1,0:T(8,128)S(1)} %copy-done, s32[16,64,128]{2,1,0:T(8,128)S(1)} %copy-done.1, f32[256,128]{1,0:T(8,128)S(1)} %get-tuple-element.81.refs_0_, f32[256,128]{1,0:T(8,128)S(1)} %collective-permute-done.20.refs_1_, f32[256,128]{1,0:T(8,128)S(1)} %collective-permute-done.21.refs_2_, ...), custom_call_target="tpu_custom_call" | custom-call | tf_op jit(solution)/shard_map/result/pallas_call | solution.py:534
  86.9 4.5 %collective-permute-done.17.refs_1_ = f32[256,128]{1,0:T(8,128)S(1)} collective-permute-done((f32[256,128]{1,0:T(8,128)S(1)}, f32[256,128]{1,0:T(8,128)S(1)}, u32[]{:S(2)}, u32[]{:S(2)}) %collective-permute-start.17) | collective-permute-done | bytes 131104 | tf_op jit(solution)/shard_map/ppermute | solution.py:561
  91.4 0.0 collective-permute-done.18.refs_2_
  91.4 0.0 collective-permute-done.19.refs_3_
  91.4 1.4 %result.3 = f32[2,16,64,128]{3,2,1,0:T(8,128)} custom-call(f32[2,16,64,128]{3,2,1,0:T(8,128)S(1)} %copy-done, s32[16,64,128]{2,1,0:T(8,128)S(1)} %copy-done.1, f32[256,128]{1,0:T(8,128)S(1)} %get-tuple-element.90.refs_0_, f32[256,128]{1,0:T(8,128)S(1)} %collective-permute-done.17.refs_1_, ...), custom_call_target="tpu_custom_call", output_to_operand_aliasing={{}: (6, {})} | custom-call | tf_op jit(solution)/shard_map/result/pallas_call | solution.py:534
  (37 shorter events, 0.3 us)
Async XLA Ops:
  4.2 21.4 %collective-permute-start = (f32[336,128]{1,0:T(8,128)}, f32[336,128]{1,0:T(8,128)S(1)}, u32[]{:S(2)}, u32[]{:S(2)}) collective-permute-start(f32[336,128]{1,0:T(8,128)} %get-tuple-element.53), channel_id=1, source_target_pairs={{0,16},{8,24},{16,0},{24,8},{1,17},{9,25},{17,1},{25,9},{2,18},{10... | collective-permute-start | bytes 516104 | tf_op jit(solution)/shard_map/ppermute | solution.py:561
  8.3 21.2 %collective-permute-start.1 = (f32[336,128]{1,0:T(8,128)}, f32[336,128]{1,0:T(8,128)S(1)}, u32[]{:S(2)}, u32[]{:S(2)}) collective-permute-start(f32[336,128]{1,0:T(8,128)} %get-tuple-element.54), channel_id=1, source_target_pairs={{0,8},{8,16},{16,24},{24,0},{1,9},{9,17},{17,25},{25,1},{2,10},{10... | collective-permute-start | bytes 516104 | tf_op jit(solution)/shard_map/ppermute | solution.py:561
  9.9 19.6 %collective-permute-start.2 = (f32[336,128]{1,0:T(8,128)}, f32[336,128]{1,0:T(8,128)S(1)}, u32[]{:S(2)}, u32[]{:S(2)}) collective-permute-start(f32[336,128]{1,0:T(8,128)} %get-tuple-element.55), channel_id=1, source_target_pairs={{0,24},{8,0},{16,8},{24,16},{1,25},{9,1},{17,9},{25,17},{2,26},{10... | collective-permute-start | bytes 516104 | tf_op jit(solution)/shard_map/ppermute | solution.py:561
  12.1 4.9 %copy-start.8 = (f32[256,128]{1,0:T(8,128)S(1)}, f32[256,128]{1,0:T(8,128)}, u32[]{:S(2)}) copy-start(f32[256,128]{1,0:T(8,128)} %get-tuple-element.60) | copy-start | bytes 393220
  12.2 6.4 %copy-start.6 = (f32[128,128]{1,0:T(8,128)S(1)}, f32[128,128]{1,0:T(8,128)}, u32[]{:S(2)}) copy-start(f32[128,128]{1,0:T(8,128)} %param.11) | copy-start | bytes 196612
  12.2 9.9 %copy-start.3 = (f32[16,64,128]{2,1,0:T(8,128)S(1)}, f32[16,64,128]{2,1,0:T(8,128)}, u32[]{:S(2)}) copy-start(f32[16,64,128]{2,1,0:T(8,128)} %along_j.3) | copy-start | bytes 1572868
  17.0 5.1 %copy-start.2 = (f32[16,64,128]{2,1,0:T(8,128)S(1)}, f32[16,64,128]{2,1,0:T(8,128)}, u32[]{:S(2)}) copy-start(f32[16,64,128]{2,1,0:T(8,128)} %along_i.3) | copy-start | bytes 1572868
  17.0 5.0 %collective-permute-start.5 = (f32[256,128]{1,0:T(8,128)S(1)}, f32[256,128]{1,0:T(8,128)S(1)}, u32[]{:S(2)}, u32[]{:S(2)}) collective-permute-start(f32[256,128]{1,0:T(8,128)S(1)} %copy-done.8), channel_id=1, source_target_pairs={{4,0},{0,4},{5,1},{1,5},{6,2},{2,6},{7,3},{3,7},{12,8},{8,12},{13,... | collective-permute-start | bytes 393224 | tf_op jit(solution)/shard_map/ppermute | solution.py:575
  18.6 23.2 %collective-permute-start.4 = (f32[512,128]{1,0:T(8,128)}, f32[512,128]{1,0:T(8,128)S(1)}, u32[]{:S(2)}, u32[]{:S(2)}) collective-permute-start(f32[512,128]{1,0:T(8,128)} %get-tuple-element.58), channel_id=1, source_target_pairs={{0,16},{8,24},{16,0},{24,8},{1,17},{9,25},{17,1},{25,9},{2,18},{10... | collective-permute-start | bytes 786440 | tf_op jit(solution)/shard_map/ppermute | solution.py:561
  22.0 19.7 %collective-permute-start.6 = (f32[512,128]{1,0:T(8,128)}, f32[512,128]{1,0:T(8,128)S(1)}, u32[]{:S(2)}, u32[]{:S(2)}) collective-permute-start(f32[512,128]{1,0:T(8,128)} %get-tuple-element.66), channel_id=1, source_target_pairs={{0,8},{8,16},{16,24},{24,0},{1,9},{9,17},{17,25},{25,1},{2,10},{10... | collective-permute-start | bytes 786440 | tf_op jit(solution)/shard_map/ppermute | solution.py:561
  22.1 3.5 %copy-start.7 = (f32[512,128]{1,0:T(8,128)S(1)}, f32[512,128]{1,0:T(8,128)}, u32[]{:S(2)}) copy-start(f32[512,128]{1,0:T(8,128)} %get-tuple-element.67) | copy-start | bytes 786436
  22.1 7.4 %copy-start.5 = (f32[336,128]{1,0:T(8,128)S(1)}, f32[336,128]{1,0:T(8,128)}, u32[]{:S(2)}) copy-start(f32[336,128]{1,0:T(8,128)} %get-tuple-element.51.refs_1_) | copy-start | bytes 516100
  25.6 18.3 %collective-permute-start.7 = (f32[512,128]{1,0:T(8,128)S(1)}, f32[512,128]{1,0:T(8,128)S(1)}, u32[]{:S(2)}, u32[]{:S(2)}) collective-permute-start(f32[512,128]{1,0:T(8,128)S(1)} %copy-done.7), channel_id=1, source_target_pairs={{0,24},{8,0},{16,8},{24,16},{1,25},{9,1},{17,9},{25,17},{2,26},{10... | collective-permute-start | bytes 786440 | tf_op jit(solution)/shard_map/ppermute | solution.py:561
  30.0 14.0 %copy-start.4 = (f32[512,128]{1,0:T(8,128)S(1)}, f32[512,128]{1,0:T(8,128)}, u32[]{:S(2)}) copy-start(f32[512,128]{1,0:T(8,128)} %get-tuple-element.57.refs_0_) | copy-start | bytes 786436
  30.0 15.8 %collective-permute-start.8 = (f32[160,128]{1,0:T(8,128)S(1)}, f32[160,128]{1,0:T(8,128)S(1)}, u32[]{:S(2)}, u32[]{:S(2)}) collective-permute-start(f32[160,128]{1,0:T(8,128)S(1)} %bitcast.39), channel_id=1, source_target_pairs={{0,8},{8,16},{16,24},{24,25},{25,17},{17,9},{9,1},{1,2},{2,10},{10... | collective-permute-start | bytes 245768 | tf_op jit(solution)/shard_map/ppermute | solution.py:580
  37.2 8.6 %collective-permute-start.3 = (f32[176,128]{1,0:T(8,128)S(1)}, f32[176,128]{1,0:T(8,128)S(1)}, u32[]{:S(2)}, u32[]{:S(2)}) collective-permute-start(f32[176,128]{1,0:T(8,128)S(1)} %pad_maximum_fusion.2), channel_id=1, source_target_pairs={{8,0},{16,8},{24,16},{25,24},{17,25},{9,17},{1,9},{2,1},{10,2},{18... | collective-permute-start | bytes 270344 | tf_op jit(solution)/shard_map/ppermute | solution.py:580
  41.7 12.4 %collective-permute-start.11 = (f32[256,128]{1,0:T(8,128)S(1)}, f32[256,128]{1,0:T(8,128)S(1)}, u32[]{:S(2)}, u32[]{:S(2)}) collective-permute-start(f32[256,128]{1,0:T(8,128)S(1)} %get-tuple-element.71), channel_id=1, source_target_pairs={{0,16},{8,24},{16,0},{24,8},{1,17},{9,25},{17,1},{25,9},{2,18},{10... | collective-permute-start | bytes 393224 | tf_op jit(solution)/shard_map/ppermute | solution.py:561
  45.8 9.4 %collective-permute-start.9 = (f32[256,128]{1,0:T(8,128)S(1)}, f32[256,128]{1,0:T(8,128)S(1)}, u32[]{:S(2)}, u32[]{:S(2)}) collective-permute-start(f32[256,128]{1,0:T(8,128)S(1)} %bitcast.38), channel_id=1, source_target_pairs={{0,8},{8,16},{16,24},{24,25},{25,17},{17,9},{9,1},{1,2},{2,10},{10... | collective-permute-start | bytes 393224 | tf_op jit(solution)/shard_map/ppermute | solution.py:580
  52.7 5.0 %collective-permute-start.10 = (f32[256,128]{1,0:T(8,128)S(1)}, f32[256,128]{1,0:T(8,128)S(1)}, u32[]{:S(2)}, u32[]{:S(2)}) collective-permute-start(f32[256,128]{1,0:T(8,128)S(1)} %bitcast.37), channel_id=1, source_target_pairs={{8,0},{16,8},{24,16},{25,24},{17,25},{9,17},{1,9},{2,1},{10,2},{18... | collective-permute-start | bytes 393224 | tf_op jit(solution)/shard_map/ppermute | solution.py:580
  57.7 10.2 %collective-permute-start.12 = (f32[264,128]{1,0:T(8,128)S(1)}, f32[264,128]{1,0:T(8,128)S(1)}, u32[]{:S(2)}, u32[]{:S(2)}) collective-permute-start(f32[264,128]{1,0:T(8,128)S(1)} %pad_maximum_fusion), channel_id=1, source_target_pairs={{4,0},{0,4},{5,1},{1,5},{6,2},{2,6},{7,3},{3,7},{12,8},{8,12},{13,... | collective-permute-start | bytes 405512 | tf_op jit(solution)/shard_map/ppermute | solution.py:575
  59.6 8.3 %collective-permute-start.13 = (f32[256,128]{1,0:T(8,128)S(1)}, f32[256,128]{1,0:T(8,128)S(1)}, u32[]{:S(2)}, u32[]{:S(2)}) collective-permute-start(f32[256,128]{1,0:T(8,128)S(1)} %get-tuple-element.84), channel_id=1, source_target_pairs={{0,8},{8,16},{16,24},{24,0},{1,9},{9,17},{17,25},{25,1},{2,10},{10... | collective-permute-start | bytes 393224 | tf_op jit(solution)/shard_map/ppermute | solution.py:561
  61.1 6.8 %collective-permute-start.14 = (f32[256,128]{1,0:T(8,128)S(1)}, f32[256,128]{1,0:T(8,128)S(1)}, u32[]{:S(2)}, u32[]{:S(2)}) collective-permute-start(f32[256,128]{1,0:T(8,128)S(1)} %get-tuple-element.85), channel_id=1, source_target_pairs={{0,24},{8,0},{16,8},{24,16},{1,25},{9,1},{17,9},{25,17},{2,26},{10... | collective-permute-start | bytes 393224 | tf_op jit(solution)/shard_map/ppermute | solution.py:561
  66.3 16.8 %collective-permute-start.20 = (f32[256,128]{1,0:T(8,128)S(1)}, f32[256,128]{1,0:T(8,128)S(1)}, u32[]{:S(2)}, u32[]{:S(2)}) collective-permute-start(f32[256,128]{1,0:T(8,128)S(1)} %get-tuple-element.94), channel_id=1, source_target_pairs={{0,16},{8,24},{16,0},{24,8},{1,17},{9,25},{17,1},{25,9},{2,18},{10... | collective-permute-start | bytes 393224 | tf_op jit(solution)/shard_map/ppermute | solution.py:561
  68.4 9.2 %collective-permute-start.15 = (f32[168,128]{1,0:T(8,128)S(1)}, f32[168,128]{1,0:T(8,128)S(1)}, u32[]{:S(2)}, u32[]{:S(2)}) collective-permute-start(f32[168,128]{1,0:T(8,128)S(1)} %pad_maximum_fusion.5), channel_id=1, source_target_pairs={{8,0},{16,8},{24,16},{25,24},{17,25},{9,17},{1,9},{2,1},{10,2},{18... | collective-permute-start | bytes 258056 | tf_op jit(solution)/shard_map/ppermute | solution.py:580
  68.5 5.9 %collective-permute-start.16 = (f32[160,128]{1,0:T(8,128)S(1)}, f32[160,128]{1,0:T(8,128)S(1)}, u32[]{:S(2)}, u32[]{:S(2)}) collective-permute-start(f32[160,128]{1,0:T(8,128)S(1)} %pad_maximum_fusion.6), channel_id=1, source_target_pairs={{0,8},{8,16},{16,24},{24,25},{25,17},{17,9},{9,1},{1,2},{2,10},{10... | collective-permute-start | bytes 245768 | tf_op jit(solution)/shard_map/ppermute | solution.py:580
  70.6 14.9 %collective-permute-start.21 = (f32[256,128]{1,0:T(8,128)S(1)}, f32[256,128]{1,0:T(8,128)S(1)}, u32[]{:S(2)}, u32[]{:S(2)}) collective-permute-start(f32[256,128]{1,0:T(8,128)S(1)} %get-tuple-element.95), channel_id=1, source_target_pairs={{0,8},{8,16},{16,24},{24,0},{1,9},{9,17},{17,25},{25,1},{2,10},{10... | collective-permute-start | bytes 393224 | tf_op jit(solution)/shard_map/ppermute | solution.py:561
  72.6 12.9 %collective-permute-start.22 = (f32[256,128]{1,0:T(8,128)S(1)}, f32[256,128]{1,0:T(8,128)S(1)}, u32[]{:S(2)}, u32[]{:S(2)}) collective-permute-start(f32[256,128]{1,0:T(8,128)S(1)} %get-tuple-element.96), channel_id=1, source_target_pairs={{0,24},{8,0},{16,8},{24,16},{1,25},{9,1},{17,9},{25,17},{2,26},{10... | collective-permute-start | bytes 393224 | tf_op jit(solution)/shard_map/ppermute | solution.py:561
  77.7 7.8 %copy-start = (f32[2,16,64,128]{3,2,1,0:T(8,128)S(1)}, f32[2,16,64,128]{3,2,1,0:T(8,128)}, u32[]{:S(2)}) copy-start(f32[2,16,64,128]{3,2,1,0:T(8,128)} %gain.2) | copy-start | bytes 3145732
  77.7 7.8 %copy-start.1 = (s32[16,64,128]{2,1,0:T(8,128)S(1)}, s32[16,64,128]{2,1,0:T(8,128)}, u32[]{:S(2)}) copy-start(s32[16,64,128]{2,1,0:T(8,128)} %mask.5) | copy-start | bytes 1572868
  80.8 10.6 %collective-permute-start.17 = (f32[256,128]{1,0:T(8,128)S(1)}, f32[256,128]{1,0:T(8,128)S(1)}, u32[]{:S(2)}, u32[]{:S(2)}) collective-permute-start(f32[256,128]{1,0:T(8,128)S(1)} %get-tuple-element.91), channel_id=1, source_target_pairs={{0,16},{8,24},{16,0},{24,8},{1,17},{9,25},{17,1},{25,9},{2,18},{10... | collective-permute-start | bytes 393224 | tf_op jit(solution)/shard_map/ppermute | solution.py:561
  81.6 9.7 %collective-permute-start.18 = (f32[256,128]{1,0:T(8,128)S(1)}, f32[256,128]{1,0:T(8,128)S(1)}, u32[]{:S(2)}, u32[]{:S(2)}) collective-permute-start(f32[256,128]{1,0:T(8,128)S(1)} %get-tuple-element.92), channel_id=1, source_target_pairs={{0,8},{8,16},{16,24},{24,0},{1,9},{9,17},{17,25},{25,1},{2,10},{10... | collective-permute-start | bytes 393224 | tf_op jit(solution)/shard_map/ppermute | solution.py:561
  83.1 8.3 %collective-permute-start.19 = (f32[256,128]{1,0:T(8,128)S(1)}, f32[256,128]{1,0:T(8,128)S(1)}, u32[]{:S(2)}, u32[]{:S(2)}) collective-permute-start(f32[256,128]{1,0:T(8,128)S(1)} %get-tuple-element.93), channel_id=1, source_target_pairs={{0,24},{8,0},{16,8},{24,16},{1,25},{9,1},{17,9},{25,17},{2,26},{10... | collective-permute-start | bytes 393224 | tf_op jit(solution)/shard_map/ppermute | solution.py:561

commit v13 on v11

--- a/solution.py
+++ b/solution.py
@@ -28,7 +28,7 @@
 
 
 def distances(devices):
-    return [0, devices // 2] + [d for d in range(1, devices) if d != devices // 2]
+    return list(range(devices))
 
 
 def position():
@@ -136,59 +136,52 @@
     )(increment, gain, mask)
 
 
-def pack_kernel(pieces, masked, along_i, along_j, *refs):
-    levels, length, cols = along_i.shape
+def pack_kernel(pieces, masked, *refs):
+    sources, refs = refs[:2 + masked], refs[2 + masked:]
     groups = len(pieces[0][0])
+    outs, refs = refs[:groups], refs[groups:]
+    targets, (slots_held, sems, fetch_sems) = refs[:2 + masked], refs[2 + masked:]
+    levels, length, cols = sources[0].shape
     width = cols // groups
-    halos, outs = refs[masked:-4 - groups - 3 * masked], refs[-4 - groups - 3 * masked:-4 - 3 * masked]
-    held, slots_held, sems, fetch_sems = refs[-4:]
-    unroll = held.shape[0]
-    number = levels // unroll
-    starts, rows = pieces[0]
-    group = lane_groups(rows, cols, groups)
-    if masked:
-        sources, (along_i, along_j, sea) = (along_i, along_j, refs[0]), refs[-7:-4]
-        fetched = []
-        for side, (source, target) in enumerate(zip(sources, (along_i, along_j, sea))):
-            pairs = [(source.at[pl.ds(k * unroll, unroll)], target.at[pl.ds(k * unroll, unroll)]) for k in range(number)]
-            fetched.append(copies(pairs, fetch_sems.at[side]))
+    unroll = groups
+    fetched = []
+    for side, (source, target) in enumerate(zip(sources, targets)):
+        pairs = [(source.at[pl.ds(k, unroll)], target.at[pl.ds(k, unroll)]) for k in range(0, levels, unroll)]
+        fetched.append(copies(pairs, fetch_sems.at[side]))
 
     def put(at, blocks):
         for slot, block in enumerate(blocks):
             slots_held[slot, pl.ds(at, block.shape[0]), :] = block
 
-    for side, weight in enumerate((along_i, along_j)):
-        for outer in range(number):
-            if masked:
-                fetched[side][outer].wait()
-            edges = []
-            for k in range(unroll):
-                level = outer * unroll + k
-                index = side * levels + level
-                if halos:
-                    for halo, at in zip(halos, (0, STEPS + length)):
-                        held[k, pl.ds(at, STEPS), :] = halo[pl.ds(index * STEPS, STEPS), :]
-                    held[k, pl.ds(STEPS, length), :] = weight[level]
-                    blocks = [held[k, pl.ds(start, rows), :] for start in starts]
+    for side, weight in enumerate(targets[:2]):
+        for outer in range(levels // unroll):
+            fetched[side][outer].wait()
+            some = range(outer * unroll, (outer + 1) * unroll)
+            base = 0
+            for starts, rows in pieces:
+                at = base + (side * levels + outer * unroll) * rows
+                base += 2 * levels * rows
+                if rows == 2:
+                    low, high = starts[0], starts[groups // 2]
+                    row = lax.broadcasted_iota(jnp.int32, (8, cols), 0)
+                    blocks = []
+                    for level in some:
+                        x, y = [weight[level, pl.ds(first // 8 * 8, 8), :] for first in (low, high)]
+                        x = pltpu.roll(x, 8 - low % 8, 0) if low % 8 else x
+                        y = pltpu.roll(y, 4, 0) if high % 8 == 0 else y
+                        blocks.append(jnp.where(row < 4, x, y))
+                    blocks = swap(blocks, row // 2, 2, 0)
+                    put(at, swap(blocks, lane_groups(8, cols, groups), width))
                 else:
-                    blocks = [weight[level, pl.ds(start - STEPS, rows), :] for start in starts]
-                put(index * rows, swap(blocks, group, width))
-                if len(pieces) > 1:
-                    small = pieces[1][0]
-                    low, high = small[0] - 2 * STEPS, small[groups // 2] - STEPS
-                    row = lax.broadcasted_iota(jnp.int32, (2 * STEPS, cols), 0)
-                    upper = pltpu.roll(weight[level, pl.ds(low, 2 * STEPS), :], STEPS, 0)
-                    lower = pltpu.roll(weight[level, pl.ds(high, 2 * STEPS), :], STEPS, 0)
-                    edges.append(jnp.where(row < STEPS, upper, lower))
-            if edges:
-                each = pieces[1][1]
-                pairs = lax.broadcasted_iota(jnp.int32, edges[0].shape, 0) // each
-                edges = swap(edges, pairs, each, 0)
-                at = 2 * levels * rows + (side * levels + outer * unroll) * each
-                put(at, swap(edges, lane_groups(unroll * each, cols, groups), width))
+                    group = lane_groups(rows, cols, groups)
+                    packed = [
+                        swap([weight[level, pl.ds(start, rows), :] for start in starts], group, width) for level in some
+                    ]
+                    put(at, [jnp.concatenate([x[slot] for x in packed], axis=0) for slot in range(groups)])
     if masked:
+        sea = targets[2]
         depth = jnp.zeros((length, cols), sea.dtype)
-        for outer in range(number):
+        for outer in range(levels // unroll):
             fetched[2][outer].wait()
             for level in range(outer * unroll, (outer + 1) * unroll):
                 depth = depth + sea[level]
@@ -201,27 +194,26 @@
         copy.wait()
 
 
-def weight_messages(pieces, along_i, along_j, mask=(), halos=()):
+def weight_messages(pieces, along_i, along_j, *mask):
     levels, length, cols = along_i.shape
     groups = len(pieces[0][0])
     shape = (2 * levels * sum(rows for _, rows in pieces) + len(mask) * length // groups, cols)
-    unroll = 4
+    anywhere = pl.BlockSpec(memory_space=pl.ANY)
     return list(
         pl.pallas_call(
             functools.partial(pack_kernel, pieces, len(mask)),
-            in_specs=[pl.BlockSpec(memory_space=pl.ANY) if mask else vmem()] * (2 + len(mask) + len(halos)),
-            out_specs=[pl.BlockSpec(memory_space=pl.ANY)] * groups,
+            in_specs=[anywhere] * (2 + len(mask)),
+            out_specs=[anywhere] * groups,
             out_shape=[jax.ShapeDtypeStruct(shape, jnp.float32)] * groups,
-            scratch_shapes=[pltpu.VMEM(x.shape, x.dtype) for x in ([along_i, along_j, *mask] if mask else [])]
+            scratch_shapes=[pltpu.VMEM(x.shape, x.dtype) for x in (along_i, along_j, *mask)]
             + [
-                pltpu.VMEM((unroll, length + 2 * STEPS, cols), jnp.float32),
                 pltpu.VMEM((groups, *shape), jnp.float32),
                 pltpu.SemaphoreType.DMA((groups,)),
-                pltpu.SemaphoreType.DMA((3, levels // unroll)),
+                pltpu.SemaphoreType.DMA((3, levels // groups)),
             ],
             compiler_params=params(VMEM_WHOLE if mask else VMEM_LIMIT),
             name="weight_messages",
-        )(along_i, along_j, *mask, *halos)
+        )(along_i, along_j, *mask)
     )
 
 
@@ -308,8 +300,7 @@
                 at = pl.multiple_of(side * half + source[d] * count, 8)
                 held[k, pl.ds(at, count), :] = part[pl.ds(first + side * count * rows, count, rows), :]
 
-    no_halo = jnp.zeros((2 * STEPS, cols), jnp.float32)
-    depth = unfold(depths[0][...], depths[1][...] if len(depths) > 1 else no_halo, groups)
+    depth = unfold(depths[0][...], depths[1][...], groups)
     tall = depth.shape[0]
     lane = lax.broadcasted_iota(jnp.int32, depth.shape, 1)
     right = jnp.where(lane == width - 1, depth, pltpu.roll(depth, cols - 1, 1))
@@ -319,9 +310,9 @@
 
     def fold(ref, starts, rows):
         group = lane_groups(rows, cols, groups)
-        x = ref[pl.ds(starts[0], rows), :]
+        x = ref[pl.ds(STEPS + starts[0], rows), :]
         for a in range(1, groups):
-            x = jnp.where(group == a, pltpu.roll(ref[pl.ds(starts[a], rows), :], a * width, 1), x)
+            x = jnp.where(group == a, pltpu.roll(ref[pl.ds(STEPS + starts[a], rows), :], a * width, 1), x)
         return x
 
     folded = [(fold(depth_i, *piece), fold(depth_j, *piece)) for piece in pieces]
@@ -575,85 +566,87 @@
     half = devices // 2
     inner = (quarter, 2 * quarter)
     outer = ((0, quarter), (3 * quarter, quarter))
+    rest = (quarter - 2 * STEPS) // half
     inner_pieces = [
-        ([STEPS + quarter + a * some for a in range(devices)], some),
-        ([quarter + 2 * a for a in range(half)] + [STEPS + 3 * quarter + 2 * a for a in range(half)], 2),
+        ([quarter + a * some for a in range(devices)], some),
+        ([quarter - STEPS + 2 * a for a in range(half)] + [3 * quarter + 2 * a for a in range(half)], 2),
+        ([2 * a for a in range(half)] + [length - STEPS + 2 * a for a in range(half)], 2),
     ]
-    outer_pieces = [([a * some for a in range(half)] + [3 * quarter + 2 * STEPS + a * some for a in range(half)], some)]
+    outer_pieces = [
+        ([STEPS + a * rest for a in range(half)] + [3 * quarter + STEPS + a * rest for a in range(half)], rest)
+    ]
 
     def rows_of(pieces):
-        return [start - STEPS + i for starts, number in pieces for start in starts for i in range(number)]
+        return [start + i for starts, number in pieces for start in starts for i in range(number)]
 
     inner_rows, outer_rows = rows_of(inner_pieces), rows_of(outer_pieces)
+    inner_window = list(range(quarter - STEPS, 3 * quarter + STEPS))
+    halo_rows = list(range(-STEPS, 0)) + list(range(length, length + STEPS))
     windows = [list(range(-STEPS, quarter + STEPS)), list(range(3 * quarter - STEPS, length + STEPS))]
 
-    inner_size = len(inner_rows) // devices
-    inner_messages = weight_messages(inner_pieces, diffusion_i, diffusion_j, [sea_mask])
+    inner_messages = weight_messages(inner_pieces, diffusion_i, diffusion_j, sea_mask)
     inner_parts = exchange(inner_messages)
-    inner_messages, edge_i, edge_j, increment, norm_gain = lax.optimization_barrier(
-        (inner_messages, diffusion_i, diffusion_j, increment, norm_gain)
-    )
-    halos = halo_i(
-        *[
-            jnp.concatenate([flat(edge_i[:, at]), flat(edge_j[:, at])], axis=0)
-            for at in (slice(0, STEPS), slice(-STEPS, None))
-        ]
-    )
+    _, increment, norm_gain = lax.optimization_barrier((inner_messages[0], increment, norm_gain))
     messages = scaled_messages(increment, norm_gain, sea_mask, devices)
     scaled = exchange(messages)
-    messages, halos = lax.optimization_barrier((messages, halos))
-    outer_messages = weight_messages(outer_pieces, diffusion_i, diffusion_j, halos=halos)
-
-    depth = sum(part[2 * levels * inner_size:] for part in inner_parts)
-    here = turn_weights(inner_pieces, [depth], inner_parts, order)
+    _, diffusion_i, diffusion_j = lax.optimization_barrier((messages[0], diffusion_i, diffusion_j))
+    outer_messages = weight_messages(outer_pieces, diffusion_i, diffusion_j)
+
+    size = 2 * levels * len(inner_rows) // devices
+    depth = sum(part[size:] for part in inner_parts)
+    above, below = halo_i(depth[:STEPS], depth[-STEPS:])
+    halo_depth = jnp.concatenate([below, above], axis=0)
+    here = turn_weights(inner_pieces, [depth, halo_depth], inner_parts, order)
+    ends = flat(here[-2 * STEPS:-STEPS]), flat(here[-STEPS:])
     left, right = halo_j(
-        jnp.concatenate([flat(here[:, :STEPS]), depth], axis=0),
-        flat(here[:, -STEPS:]),
+        jnp.concatenate([flat(here[:, :STEPS]), depth, halo_depth], axis=0), flat(here[:, -STEPS:])
     )
-    right, right_depth = cut(right, len(inner_rows) * STEPS, rows)
+    right, right_depth, right_halo_depth = cut(right, len(inner_rows) * STEPS, rows, 2 * STEPS)
+    depths = [depth, right_depth, halo_depth, right_halo_depth]
 
     balance = jnp.eye(order, dtype=jnp.float32) + coupling
     by_device = balance.reshape(2, devices, levels, order)
     adjoint = jnp.concatenate([by_device[:, s].reshape(2 * levels, order) for s in source], axis=0).T
     forward = jnp.concatenate([by_device[:, t].reshape(2 * levels, order) for t in to], axis=0)
 
+    middle = devices // 2
     scaled[1], outer_messages = lax.optimization_barrier((scaled[1], outer_messages))
-    early = shift(outer_messages[1], devices // 2)
+    early = shift(outer_messages[middle], middle)
     mixed = adjoint_mix(adjoint, depth, scaled, length, width)
     edges = flat(mixed[:, :STEPS]), flat(mixed[:, -STEPS:])
     edges, inner_weights = lax.optimization_barrier((edges, (here, left, right)))
     left, right = halo_j(*edges)
     left, right, outer_messages, early = lax.optimization_barrier((left, right, outer_messages, early))
-    own, _, *others = outer_messages
-    outer_parts = [own, early] + [shift(x, d) for x, d in zip(others, distances(devices)[2:])]
+    outer_parts = [
+        early if d == middle else shift(outer_messages[d], d) if d else outer_messages[0] for d in range(devices)
+    ]
     field = [(list(range(length)), mixed, left, right)]
     weights = [(inner_rows, *inner_weights)]
-    depths = [depth, right_depth]
-    inner_mixed = spread_mix([sorted(inner_rows)], forward, depths, field, weights, devices)
+    inner_mixed = spread_mix([inner_window], forward, depths[:2], field, weights, devices)
     _, upper, lower = lax.optimization_barrier((left, mixed[:STEPS], mixed[-STEPS:]))
     _, outer_parts = lax.optimization_barrier((inner_mixed[0], outer_parts))
+    above, below = halo_i(*[jnp.concatenate(pair, axis=0) for pair in zip((flat(upper), flat(lower)), ends)])
+    size = STEPS * width
+    halo, halo_weight = [
+        jnp.concatenate(pair, axis=0).reshape(2 * STEPS, width, order)
+        for pair in zip(cut(above, size, size), cut(below, size, size))
+    ]
+    here = turn_weights(outer_pieces, [depth, halo_depth], outer_parts, order)
+    inner_mixed = list(inner_mixed)
+    _, inner_mixed[2:] = lax.optimization_barrier(((here, halo), inner_mixed[2:]))
     inner_mixed = exchange(inner_mixed)
     out = result((inner,), norm_gain, sea_mask, inner_mixed, None)
-
-    above, below = halo_i(
-        jnp.concatenate([flat(upper), depth[:STEPS]], axis=0),
-        jnp.concatenate([flat(lower), depth[-STEPS:]], axis=0),
+    left, right = halo_j(
+        *[
+            jnp.concatenate([flat(x[:, at]) for x in (here, halo, halo_weight)], axis=0)
+            for at in (slice(0, STEPS), slice(-STEPS, None))
+        ]
     )
-    above, above_depth = cut(above, STEPS * width, STEPS)
-    below, below_depth = cut(below, STEPS * width, STEPS)
-    halo_depth = jnp.concatenate([below_depth, above_depth], axis=0)
-    halo = jnp.concatenate([above, below], axis=0).reshape(2 * STEPS, width, order)
-    here = turn_weights(outer_pieces, [depth, halo_depth], outer_parts, order)
-    left, right = halo_j(
-        jnp.concatenate([flat(here[:, :STEPS]), flat(halo[:, :STEPS]), halo_depth], axis=0),
-        jnp.concatenate([flat(here[:, -STEPS:]), flat(halo[:, -STEPS:])], axis=0),
-    )
-    sizes = len(outer_rows) * STEPS, 2 * STEPS * STEPS
-    left, halo_left = cut(left, *sizes)
-    right, halo_right, right_halo_depth = cut(right, *sizes, 2 * STEPS)
-    weights.append((outer_rows, here, left, right))
-    field.append((list(range(-STEPS, 0)) + list(range(length, length + STEPS)), halo, halo_left, halo_right))
-    depths += [halo_depth, right_halo_depth]
+    sizes = [rows * STEPS for rows in (len(outer_rows), 2 * STEPS, 2 * STEPS)]
+    left, halo_left, weight_left = cut(left, *sizes)
+    right, halo_right, weight_right = cut(right, *sizes)
+    weights += [(halo_rows, halo_weight, weight_left, weight_right), (outer_rows, here, left, right)]
+    field.append((halo_rows, halo, halo_left, halo_right))
     outer_mixed = exchange(spread_mix(windows, forward, depths, field, weights, devices))
     return result(outer, norm_gain, sea_mask, outer_mixed, out)
 

time: 92.3 us -> 93.9 us (1.017)
  waiting for transfers between devices: 19.6 us -> 23.6 us
  starting transfers between devices: 49.8 us -> 48.1 us
  local copies, waits for them, and re-layouts: 1.87 us -> 0.33 us
  Pallas kernels: 20.3 us -> 21.3 us
    ppermute x3, starting transfers between devices: 22.9 us -> 20.1 us  [halo_j(): lax.ppermute(last, ('lev', 'gy'), ahead)]
    ppermute x2, waiting for transfers between devices: 0.01 us -> 2.47 us  [halo_i(): both = lax.ppermute(jnp.concatenate([first, last], axis=0), 'gx', up)]
    ppermute x3, starting transfers between devices: 0.07 us -> 1.79 us  [halo_j(): lax.ppermute(first, ('lev', 'gy'), back)]
    unnamed x18 -> x14, local copies, waits for them, and re-layouts: 1.56 us -> 0.03 us
    ppermute x15, waiting for transfers between devices: 12.8 us -> 13.9 us  [shift(): lax.ppermute(x, 'lev', [(k, (k + d) % devices) for k in range(devices)])]
  transfers between devices with their start and end apart: 23 -> 23, of which waited for: 8 -> 9; matrix products, arithmetic and copies ran while one was open for 0% -> 0% of each run, Pallas kernels for 17% -> 17%
where the time goes in v13:
time: 93.9 us; the launch traced here: 93.8 us
  starting transfers between devices  48.1 us (51%)
  waiting for transfers between devices  23.6 us (25%)
  Pallas kernels  21.3 us (23%)
    ppermute x15, starting transfers between devices, shift(): lax.ppermute(x, 'lev', [(k, (k + d) % devices) for k in range(devices)])  23 us
    ppermute x3, starting transfers between devices, halo_j(): lax.ppermute(last, ('lev', 'gy'), ahead)  20.1 us
    ppermute x15, waiting for transfers between devices, shift(): lax.ppermute(x, 'lev', [(k, (k + d) % devices) for k in range(devices)])  13.9 us
    pallas_call x2, Pallas kernels, weight_messages(): pl.pallas_call(functools.partial(pack_kernel, pieces, len(mask)), in_spec...  6.55 us
    pallas_call x2, Pallas kernels, spread_mix(): pl.pallas_call(kernel, in_specs=[vmem()] * (1 + len(arrays)), out_specs=[...  5.91 us
    ppermute x3, waiting for transfers between devices, halo_j(): lax.ppermute(first, ('lev', 'gy'), back)  5.21 us
    pallas_call x1, Pallas kernels, scaled_messages(): pl.pallas_call(scaled_kernel, in_specs=[pl.BlockSpec(memory_space=pl.ANY)...  3.35 us
    ppermute x2, starting transfers between devices, halo_i(): both = lax.ppermute(jnp.concatenate([first, last], axis=0), 'gx', up)  3.32 us
  transfers between devices with their start and end apart: 23, of which 9 were waited for; matrix products, arithmetic and copies ran while one was open for 0% of the time, Pallas kernels for 17%

profile of v13, /device:TPU:0, one launch (start us, length us, event | category | flops | bytes accessed | tf_op | source)
XLA Modules:
  0.0 93.8 jit_solution(14480772899103021159)
XLA Ops:
  0.0 3.5 %weight_messages.2 = (f32[400,128]{1,0:T(8,128)}, f32[400,128]{1,0:T(8,128)}, f32[400,128]{1,0:T(8,128)}, f32[400,128]{1,0:T(8,128)}) custom-call(f32[16,64,128]{2,1,0:T(8,128)} %refs_0_.2, f32[16,64,128]{2,1,0:T(8,128)} %refs_1_.2, s32[16,64,128]{2,1,0:T(8,128)} %mask.5), custom_call_target="tpu_custom_call" | custom-call | tf_op jit(solution)/shard_map/weight_messages/pallas_call | solution.py:203
  3.5 3.1 %collective-permute-start = (f32[400,128]{1,0:T(8,128)}, f32[400,128]{1,0:T(8,128)S(1)}, u32[]{:S(2)}, u32[]{:S(2)}) collective-permute-start(f32[400,128]{1,0:T(8,128)} %get-tuple-element.55), channel_id=1, source_target_pairs={{0,8},{8,16},{16,24},{24,0},{1,9},{9,17},{17,25},{25,1},{2,10},{10... | collective-permute-start | bytes 614408 | tf_op jit(solution)/shard_map/ppermute | solution.py:537
  6.6 2.6 %collective-permute-start.1 = (f32[400,128]{1,0:T(8,128)}, f32[400,128]{1,0:T(8,128)S(1)}, u32[]{:S(2)}, u32[]{:S(2)}) collective-permute-start(f32[400,128]{1,0:T(8,128)} %get-tuple-element.56), channel_id=1, source_target_pairs={{0,16},{8,24},{16,0},{24,8},{1,17},{9,25},{17,1},{25,9},{2,18},{10... | collective-permute-start | bytes 614408 | tf_op jit(solution)/shard_map/ppermute | solution.py:537
  9.1 1.3 %collective-permute-start.2 = (f32[400,128]{1,0:T(8,128)}, f32[400,128]{1,0:T(8,128)S(1)}, u32[]{:S(2)}, u32[]{:S(2)}) collective-permute-start(f32[400,128]{1,0:T(8,128)} %get-tuple-element.57), channel_id=1, source_target_pairs={{0,24},{8,0},{16,8},{24,16},{1,25},{9,1},{17,9},{25,17},{2,26},{10... | collective-permute-start | bytes 614408 | tf_op jit(solution)/shard_map/ppermute | solution.py:537
  10.5 3.3 %scaled_messages.1 = (f32[512,128]{1,0:T(8,128)}, f32[512,128]{1,0:T(8,128)}, f32[512,128]{1,0:T(8,128)}, f32[512,128]{1,0:T(8,128)}) custom-call(f32[2,16,64,128]{3,2,1,0:T(8,128)} %increment, f32[2,16,64,128]{3,2,1,0:T(8,128)} %gain.2, s32[16,64,128]{2,1,0:T(8,128)} %mask.5), custom_call_target="tpu_custom_call" | custom-call | tf_op jit(solution)/shard_map/scaled_messages/pallas_call | solution.py:121
  13.9 0.0 copy-start.2
  13.9 0.7 collective-permute-start.5
  14.6 0.3 collective-permute-start.6
  14.9 0.0 copy-done.6
  15.0 0.0 collective-permute-done.refs_3_
  15.0 2.9 %collective-permute-start.7 = (f32[512,128]{1,0:T(8,128)}, f32[512,128]{1,0:T(8,128)S(1)}, u32[]{:S(2)}, u32[]{:S(2)}) collective-permute-start(f32[512,128]{1,0:T(8,128)} %get-tuple-element.69), channel_id=1, source_target_pairs={{0,24},{8,0},{16,8},{24,16},{1,25},{9,1},{17,9},{25,17},{2,26},{10... | collective-permute-start | bytes 786440 | tf_op jit(solution)/shard_map/ppermute | solution.py:537
  17.9 5.8 %collective-permute-done.1.refs_4_ = f32[400,128]{1,0:T(8,128)S(1)} collective-permute-done((f32[400,128]{1,0:T(8,128)}, f32[400,128]{1,0:T(8,128)S(1)}, u32[]{:S(2)}, u32[]{:S(2)}) %collective-permute-start.1) | collective-permute-done | bytes 204832 | tf_op jit(solution)/shard_map/ppermute | solution.py:537
  23.7 0.0 collective-permute-done.2.refs_5_
  23.7 0.0 copy-done.5
  23.7 1.8 %collective-permute-start.3 = (f32[8,128]{1,0:T(8,128)S(1)}, f32[8,128]{1,0:T(8,128)S(1)}, u32[]{:S(2)}, u32[]{:S(2)}) collective-permute-start(f32[8,128]{1,0:T(8,128)S(1)} %pad_maximum_fusion.8), channel_id=1, source_target_pairs={{4,0},{0,4},{5,1},{1,5},{6,2},{2,6},{7,3},{3,7},{12,8},{8,12},{13,... | collective-permute-start | bytes 12296 | tf_op jit(solution)/shard_map/ppermute | solution.py:551
  25.5 0.1 copy.13.matrix
  25.6 0.0 copy-done.3
  25.6 0.0 copy-done.2
  25.6 3.1 %weight_messages.3 = (f32[128,128]{1,0:T(8,128)S(1)}, f32[128,128]{1,0:T(8,128)S(1)}, f32[128,128]{1,0:T(8,128)S(1)}, f32[128,128]{1,0:T(8,128)S(1)}) custom-call(f32[16,64,128]{2,1,0:T(8,128)S(1)} %copy-done.2, f32[16,64,128]{2,1,0:T(8,128)S(1)} %copy-done.3), custom_call_target="tpu_custom_call" | custom-call | tf_op jit(solution)/shard_map/weight_messages/pallas_call | solution.py:203
  28.7 0.0 collective-permute-done.3.refs_1_.refs_2_
  28.7 0.5 turn_weights.2.refs_5_.refs_10_
  29.2 0.0 copy-start.4
  29.2 15.1 %collective-permute-start.8 = (f32[192,128]{1,0:T(8,128)S(1)}, f32[192,128]{1,0:T(8,128)S(1)}, u32[]{:S(2)}, u32[]{:S(2)}) collective-permute-start(f32[192,128]{1,0:T(8,128)S(1)} %bitcast.48), channel_id=1, source_target_pairs={{0,8},{8,16},{16,24},{24,25},{25,17},{17,9},{9,1},{1,2},{2,10},{10... | collective-permute-start | bytes 294920 | tf_op jit(solution)/shard_map/ppermute | solution.py:556
  44.4 0.1 collective-permute-start.4
  44.5 0.0 collective-permute-done.5.refs_1_
  44.5 1.5 %collective-permute-start.11 = (f32[128,128]{1,0:T(8,128)S(1)}, f32[128,128]{1,0:T(8,128)S(1)}, u32[]{:S(2)}, u32[]{:S(2)}) collective-permute-start(f32[128,128]{1,0:T(8,128)S(1)} %get-tuple-element.74), channel_id=1, source_target_pairs={{0,16},{8,24},{16,0},{24,8},{1,17},{9,25},{17,1},{25,9},{2,18},{10... | collective-permute-start | bytes 196616 | tf_op jit(solution)/shard_map/ppermute | solution.py:537
  46.0 0.0 collective-permute-done.6.refs_2_
  46.0 0.0 collective-permute-done.7.refs_3_
  46.1 1.8 %adjoint_mix.1.refs_2_.refs_4_ = f32[64,32,128]{2,1,0:T(8,128)S(1)} custom-call(f32[128,128]{1,0:T(8,128)S(1)} %copy.13.matrix, f32[16,128]{1,0:T(8,128)S(1)} %slice_add_fusion.refs_0_.depths, f32[512,128]{1,0:T(8,128)S(1)} %copy-done.4, f32[512,128]{1,0:T(8,128)S(1)} %collective-permute-done.5.refs_1_, f32[512,128]{1,0:T(8,128)S(1)} %collective-permute-done.6.refs_2_, ...), custom_call_target="tpu_custom_call" | custom-call | tf_op jit(solution)/shard_map/adjoint_mix/pallas_call | solution.py:264
  47.9 1.3 %collective-permute-done.4 = f32[216,128]{1,0:T(8,128)S(1)} collective-permute-done((f32[216,128]{1,0:T(8,128)S(1)}, f32[216,128]{1,0:T(8,128)S(1)}, u32[]{:S(2)}, u32[]{:S(2)}) %collective-permute-start.4) | collective-permute-done | bytes 110624 | tf_op jit(solution)/shard_map/ppermute | solution.py:556
  49.2 0.0 collective-permute-done.8.refs_6_.refs_11_
  49.2 4.9 %collective-permute-start.9 = (f32[256,128]{1,0:T(8,128)S(1)}, f32[256,128]{1,0:T(8,128)S(1)}, u32[]{:S(2)}, u32[]{:S(2)}) collective-permute-start(f32[256,128]{1,0:T(8,128)S(1)} %bitcast.45), channel_id=1, source_target_pairs={{0,8},{8,16},{16,24},{24,25},{25,17},{17,9},{9,1},{1,2},{2,10},{10... | collective-permute-start | bytes 393224 | tf_op jit(solution)/shard_map/ppermute | solution.py:556
  54.1 0.0 collective-permute-start.10
  54.1 0.5 collective-permute-done.11.refs_4_
  54.6 2.0 %collective-permute-done.9.refs_3_.refs_5_ = f32[256,128]{1,0:T(8,128)S(1)} collective-permute-done((f32[256,128]{1,0:T(8,128)S(1)}, f32[256,128]{1,0:T(8,128)S(1)}, u32[]{:S(2)}, u32[]{:S(2)}) %collective-permute-start.9) | collective-permute-done | bytes 131104 | tf_op jit(solution)/shard_map/ppermute | solution.py:556
  56.6 2.4 %collective-permute-done.10.refs_4_.refs_6_ = f32[256,128]{1,0:T(8,128)S(1)} collective-permute-done((f32[256,128]{1,0:T(8,128)S(1)}, f32[256,128]{1,0:T(8,128)S(1)}, u32[]{:S(2)}, u32[]{:S(2)}) %collective-permute-start.10) | collective-permute-done | bytes 131104 | tf_op jit(solution)/shard_map/ppermute | solution.py:556
  59.1 1.1 %collective-permute-start.13 = (f32[128,128]{1,0:T(8,128)S(1)}, f32[128,128]{1,0:T(8,128)S(1)}, u32[]{:S(2)}, u32[]{:S(2)}) collective-permute-start(f32[128,128]{1,0:T(8,128)S(1)} %get-tuple-element.85), channel_id=1, source_target_pairs={{0,8},{8,16},{16,24},{24,0},{1,9},{9,17},{17,25},{25,1},{2,10},{10... | collective-permute-start | bytes 196616 | tf_op jit(solution)/shard_map/ppermute | solution.py:537
  60.2 2.7 %collective-permute-start.14 = (f32[128,128]{1,0:T(8,128)S(1)}, f32[128,128]{1,0:T(8,128)S(1)}, u32[]{:S(2)}, u32[]{:S(2)}) collective-permute-start(f32[128,128]{1,0:T(8,128)S(1)} %get-tuple-element.87), channel_id=1, source_target_pairs={{0,24},{8,0},{16,8},{24,16},{1,25},{9,1},{17,9},{25,17},{2,26},{10... | collective-permute-start | bytes 196616 | tf_op jit(solution)/shard_map/ppermute | solution.py:537
  62.9 1.5 %collective-permute-start.12 = (f32[512,128]{1,0:T(8,128)S(1)}, f32[512,128]{1,0:T(8,128)S(1)}, u32[]{:S(2)}, u32[]{:S(2)}) collective-permute-start(f32[512,128]{1,0:T(8,128)S(1)} %pad_maximum_fusion), channel_id=1, source_target_pairs={{4,0},{0,4},{5,1},{1,5},{6,2},{2,6},{7,3},{3,7},{12,8},{8,12},{13,... | collective-permute-start | bytes 786440 | tf_op jit(solution)/shard_map/ppermute | solution.py:551
  64.5 2.9 %spread_mix.2 = (f32[256,128]{1,0:T(8,128)S(1)}, f32[256,128]{1,0:T(8,128)S(1)}, f32[256,128]{1,0:T(8,128)S(1)}, f32[256,128]{1,0:T(8,128)S(1)}) custom-call(f32[128,128]{1,0:T(8,128)S(1)} %get-tuple-element.129.matrix, f32[16,128]{1,0:T(8,128)S(1)} %slice_add_fusion.refs_0_.depths, f32[16,128]{1,0:T(8,128)S(1)} %split.52.refs_1_, ...), custom_call_target="tpu_custom_call" | custom-call | tf_op jit(solution)/shard_map/spread_mix/pallas_call | solution.py:451
  67.3 0.1 collective-permute-start.20
  67.4 0.0 collective-permute-done.13.refs_3_
  67.4 0.0 collective-permute-done.14.refs_5_
  67.4 0.3 turn_weights.3.refs_16_
  67.8 2.5 %collective-permute-done.12 = f32[512,128]{1,0:T(8,128)S(1)} collective-permute-done((f32[512,128]{1,0:T(8,128)S(1)}, f32[512,128]{1,0:T(8,128)S(1)}, u32[]{:S(2)}, u32[]{:S(2)}) %collective-permute-start.12) | collective-permute-done | bytes 262176 | tf_op jit(solution)/shard_map/ppermute | solution.py:551
  70.3 0.1 collective-permute-start.15
  70.4 1.7 %collective-permute-start.16 = (f32[128,128]{1,0:T(8,128)S(1)}, f32[128,128]{1,0:T(8,128)S(1)}, u32[]{:S(2)}, u32[]{:S(2)}) collective-permute-start(f32[128,128]{1,0:T(8,128)S(1)} %pad_maximum_fusion.7), channel_id=1, source_target_pairs={{8,0},{16,8},{24,16},{25,24},{17,25},{9,17},{1,9},{2,1},{10,2},{18... | collective-permute-start | bytes 196616 | tf_op jit(solution)/shard_map/ppermute | solution.py:556
  72.1 0.2 collective-permute-start.21
  72.4 2.5 %collective-permute-start.22 = (f32[256,128]{1,0:T(8,128)S(1)}, f32[256,128]{1,0:T(8,128)S(1)}, u32[]{:S(2)}, u32[]{:S(2)}) collective-permute-start(f32[256,128]{1,0:T(8,128)S(1)} %get-tuple-element.100), channel_id=1, source_target_pairs={{0,24},{8,0},{16,8},{24,16},{1,25},{9,1},{17,9},{25,17},{2,26},{10... | collective-permute-start | bytes 393224 | tf_op jit(solution)/shard_map/ppermute | solution.py:537
  74.9 0.0 collective-permute-done.15
  74.9 1.5 %collective-permute-done.16 = f32[128,128]{1,0:T(8,128)S(1)} collective-permute-done((f32[128,128]{1,0:T(8,128)S(1)}, f32[128,128]{1,0:T(8,128)S(1)}, u32[]{:S(2)}, u32[]{:S(2)}) %collective-permute-start.16) | collective-permute-done | bytes 65568 | tf_op jit(solution)/shard_map/ppermute | solution.py:556
  76.3 0.0 copy-start.1
  76.4 3.1 %spread_mix.3 = (f32[256,128]{1,0:T(8,128)S(1)}, f32[256,128]{1,0:T(8,128)S(1)}, f32[256,128]{1,0:T(8,128)S(1)}, f32[256,128]{1,0:T(8,128)S(1)}) custom-call(f32[128,128]{1,0:T(8,128)S(1)} %get-tuple-element.129.matrix, f32[16,128]{1,0:T(8,128)S(1)} %slice_add_fusion.refs_0_.depths, f32[16,128]{1,0:T(8,128)S(1)} %split.52.refs_1_, ...), custom_call_target="tpu_custom_call" | custom-call | tf_op jit(solution)/shard_map/spread_mix/pallas_call | solution.py:451
  79.4 1.4 %collective-permute-start.17 = (f32[256,128]{1,0:T(8,128)S(1)}, f32[256,128]{1,0:T(8,128)S(1)}, u32[]{:S(2)}, u32[]{:S(2)}) collective-permute-start(f32[256,128]{1,0:T(8,128)S(1)} %get-tuple-element.93), channel_id=1, source_target_pairs={{0,8},{8,16},{16,24},{24,0},{1,9},{9,17},{17,25},{25,1},{2,10},{10... | collective-permute-start | bytes 393224 | tf_op jit(solution)/shard_map/ppermute | solution.py:537
  80.8 0.3 collective-permute-start.18
  81.1 0.0 collective-permute-done.20.refs_1_
  81.1 2.2 %collective-permute-start.19 = (f32[256,128]{1,0:T(8,128)S(1)}, f32[256,128]{1,0:T(8,128)S(1)}, u32[]{:S(2)}, u32[]{:S(2)}) collective-permute-start(f32[256,128]{1,0:T(8,128)S(1)} %get-tuple-element.95), channel_id=1, source_target_pairs={{0,24},{8,0},{16,8},{24,16},{1,25},{9,1},{17,9},{25,17},{2,26},{10... | collective-permute-start | bytes 393224 | tf_op jit(solution)/shard_map/ppermute | solution.py:537
  83.3 0.0 collective-permute-done.21.refs_2_
  83.3 0.0 collective-permute-done.22.refs_3_
  83.3 1.4 %result.2.refs_4_ = f32[2,16,64,128]{3,2,1,0:T(8,128)} custom-call(f32[2,16,64,128]{3,2,1,0:T(8,128)S(1)} %copy-done, s32[16,64,128]{2,1,0:T(8,128)S(1)} %copy-done.1, f32[256,128]{1,0:T(8,128)S(1)} %get-tuple-element.83.refs_0_, f32[256,128]{1,0:T(8,128)S(1)} %collective-permute-done.20.refs_1_, f32[256,128]{1,0:T(8,128)S(1)} %collective-permute-done.21.refs_2_, ...), custom_call_target="tpu_custom_call" | custom-call | tf_op jit(solution)/shard_map/result/pallas_call | solution.py:510
  84.8 3.0 %collective-permute-done.17.refs_1_ = f32[256,128]{1,0:T(8,128)S(1)} collective-permute-done((f32[256,128]{1,0:T(8,128)S(1)}, f32[256,128]{1,0:T(8,128)S(1)}, u32[]{:S(2)}, u32[]{:S(2)}) %collective-permute-start.17) | collective-permute-done | bytes 131104 | tf_op jit(solution)/shard_map/ppermute | solution.py:537
  87.7 4.6 %collective-permute-done.18.refs_2_ = f32[256,128]{1,0:T(8,128)S(1)} collective-permute-done((f32[256,128]{1,0:T(8,128)S(1)}, f32[256,128]{1,0:T(8,128)S(1)}, u32[]{:S(2)}, u32[]{:S(2)}) %collective-permute-start.18) | collective-permute-done | bytes 131104 | tf_op jit(solution)/shard_map/ppermute | solution.py:537
  92.3 0.0 collective-permute-done.19.refs_3_
  92.3 1.5 %result.3 = f32[2,16,64,128]{3,2,1,0:T(8,128)} custom-call(f32[2,16,64,128]{3,2,1,0:T(8,128)S(1)} %copy-done, s32[16,64,128]{2,1,0:T(8,128)S(1)} %copy-done.1, f32[256,128]{1,0:T(8,128)S(1)} %get-tuple-element.92.refs_0_, f32[256,128]{1,0:T(8,128)S(1)} %collective-permute-done.17.refs_1_, ...), custom_call_target="tpu_custom_call", output_to_operand_aliasing={{}: (6, {})} | custom-call | tf_op jit(solution)/shard_map/result/pallas_call | solution.py:510
  (33 shorter events, 0.3 us)
Async XLA Ops:
  3.5 11.5 %collective-permute-start = (f32[400,128]{1,0:T(8,128)}, f32[400,128]{1,0:T(8,128)S(1)}, u32[]{:S(2)}, u32[]{:S(2)}) collective-permute-start(f32[400,128]{1,0:T(8,128)} %get-tuple-element.55), channel_id=1, source_target_pairs={{0,8},{8,16},{16,24},{24,0},{1,9},{9,17},{17,25},{25,1},{2,10},{10... | collective-permute-start | bytes 614408 | tf_op jit(solution)/shard_map/ppermute | solution.py:537
  6.6 17.1 %collective-permute-start.1 = (f32[400,128]{1,0:T(8,128)}, f32[400,128]{1,0:T(8,128)S(1)}, u32[]{:S(2)}, u32[]{:S(2)}) collective-permute-start(f32[400,128]{1,0:T(8,128)} %get-tuple-element.56), channel_id=1, source_target_pairs={{0,16},{8,24},{16,0},{24,8},{1,17},{9,25},{17,1},{25,9},{2,18},{10... | collective-permute-start | bytes 614408 | tf_op jit(solution)/shard_map/ppermute | solution.py:537
  9.1 14.5 %collective-permute-start.2 = (f32[400,128]{1,0:T(8,128)}, f32[400,128]{1,0:T(8,128)S(1)}, u32[]{:S(2)}, u32[]{:S(2)}) collective-permute-start(f32[400,128]{1,0:T(8,128)} %get-tuple-element.57), channel_id=1, source_target_pairs={{0,24},{8,0},{16,8},{24,16},{1,25},{9,1},{17,9},{25,17},{2,26},{10... | collective-permute-start | bytes 614408 | tf_op jit(solution)/shard_map/ppermute | solution.py:537
  10.5 4.4 %copy-start.6 = (f32[128,128]{1,0:T(8,128)S(1)}, f32[128,128]{1,0:T(8,128)}, u32[]{:S(2)}) copy-start(f32[128,128]{1,0:T(8,128)} %param.11) | copy-start | bytes 196612
  10.5 13.2 %copy-start.5 = (f32[400,128]{1,0:T(8,128)S(1)}, f32[400,128]{1,0:T(8,128)}, u32[]{:S(2)}) copy-start(f32[400,128]{1,0:T(8,128)} %get-tuple-element.53.refs_2_) | copy-start | bytes 614404
  10.5 15.1 %copy-start.3 = (f32[16,64,128]{2,1,0:T(8,128)S(1)}, f32[16,64,128]{2,1,0:T(8,128)}, u32[]{:S(2)}) copy-start(f32[16,64,128]{2,1,0:T(8,128)} %refs_1_.2) | copy-start | bytes 1572868
  13.9 11.8 %copy-start.2 = (f32[16,64,128]{2,1,0:T(8,128)S(1)}, f32[16,64,128]{2,1,0:T(8,128)}, u32[]{:S(2)}) copy-start(f32[16,64,128]{2,1,0:T(8,128)} %refs_0_.2) | copy-start | bytes 1572868
  13.9 30.6 %collective-permute-start.5 = (f32[512,128]{1,0:T(8,128)}, f32[512,128]{1,0:T(8,128)S(1)}, u32[]{:S(2)}, u32[]{:S(2)}) collective-permute-start(f32[512,128]{1,0:T(8,128)} %get-tuple-element.60), channel_id=1, source_target_pairs={{0,8},{8,16},{16,24},{24,0},{1,9},{9,17},{17,25},{25,1},{2,10},{10... | collective-permute-start | bytes 786440 | tf_op jit(solution)/shard_map/ppermute | solution.py:537
  14.6 31.4 %collective-permute-start.6 = (f32[512,128]{1,0:T(8,128)}, f32[512,128]{1,0:T(8,128)S(1)}, u32[]{:S(2)}, u32[]{:S(2)}) collective-permute-start(f32[512,128]{1,0:T(8,128)} %get-tuple-element.68), channel_id=1, source_target_pairs={{0,16},{8,24},{16,0},{24,8},{1,17},{9,25},{17,1},{25,9},{2,18},{10... | collective-permute-start | bytes 786440 | tf_op jit(solution)/shard_map/ppermute | solution.py:537
  15.0 31.0 %collective-permute-start.7 = (f32[512,128]{1,0:T(8,128)}, f32[512,128]{1,0:T(8,128)S(1)}, u32[]{:S(2)}, u32[]{:S(2)}) collective-permute-start(f32[512,128]{1,0:T(8,128)} %get-tuple-element.69), channel_id=1, source_target_pairs={{0,24},{8,0},{16,8},{24,16},{1,25},{9,1},{17,9},{25,17},{2,26},{10... | collective-permute-start | bytes 786440 | tf_op jit(solution)/shard_map/ppermute | solution.py:537
  23.7 5.0 %collective-permute-start.3 = (f32[8,128]{1,0:T(8,128)S(1)}, f32[8,128]{1,0:T(8,128)S(1)}, u32[]{:S(2)}, u32[]{:S(2)}) collective-permute-start(f32[8,128]{1,0:T(8,128)S(1)} %pad_maximum_fusion.8), channel_id=1, source_target_pairs={{4,0},{0,4},{5,1},{1,5},{6,2},{2,6},{7,3},{3,7},{12,8},{8,12},{13,... | collective-permute-start | bytes 12296 | tf_op jit(solution)/shard_map/ppermute | solution.py:551
  29.2 16.8 %copy-start.4 = (f32[512,128]{1,0:T(8,128)S(1)}, f32[512,128]{1,0:T(8,128)}, u32[]{:S(2)}) copy-start(f32[512,128]{1,0:T(8,128)} %get-tuple-element.59.refs_0_) | copy-start | bytes 786436
  29.2 20.0 %collective-permute-start.8 = (f32[192,128]{1,0:T(8,128)S(1)}, f32[192,128]{1,0:T(8,128)S(1)}, u32[]{:S(2)}, u32[]{:S(2)}) collective-permute-start(f32[192,128]{1,0:T(8,128)S(1)} %bitcast.48), channel_id=1, source_target_pairs={{0,8},{8,16},{16,24},{24,25},{25,17},{17,9},{9,1},{1,2},{2,10},{10... | collective-permute-start | bytes 294920 | tf_op jit(solution)/shard_map/ppermute | solution.py:556
  44.4 4.8 %collective-permute-start.4 = (f32[216,128]{1,0:T(8,128)S(1)}, f32[216,128]{1,0:T(8,128)S(1)}, u32[]{:S(2)}, u32[]{:S(2)}) collective-permute-start(f32[216,128]{1,0:T(8,128)S(1)} %pad_maximum_fusion.3), channel_id=1, source_target_pairs={{8,0},{16,8},{24,16},{25,24},{17,25},{9,17},{1,9},{2,1},{10,2},{18... | collective-permute-start | bytes 331784 | tf_op jit(solution)/shard_map/ppermute | solution.py:556
  44.5 10.1 %collective-permute-start.11 = (f32[128,128]{1,0:T(8,128)S(1)}, f32[128,128]{1,0:T(8,128)S(1)}, u32[]{:S(2)}, u32[]{:S(2)}) collective-permute-start(f32[128,128]{1,0:T(8,128)S(1)} %get-tuple-element.74), channel_id=1, source_target_pairs={{0,16},{8,24},{16,0},{24,8},{1,17},{9,25},{17,1},{25,9},{2,18},{10... | collective-permute-start | bytes 196616 | tf_op jit(solution)/shard_map/ppermute | solution.py:537
  49.2 7.4 %collective-permute-start.9 = (f32[256,128]{1,0:T(8,128)S(1)}, f32[256,128]{1,0:T(8,128)S(1)}, u32[]{:S(2)}, u32[]{:S(2)}) collective-permute-start(f32[256,128]{1,0:T(8,128)S(1)} %bitcast.45), channel_id=1, source_target_pairs={{0,8},{8,16},{16,24},{24,25},{25,17},{17,9},{9,1},{1,2},{2,10},{10... | collective-permute-start | bytes 393224 | tf_op jit(solution)/shard_map/ppermute | solution.py:556
  54.1 5.0 %collective-permute-start.10 = (f32[256,128]{1,0:T(8,128)S(1)}, f32[256,128]{1,0:T(8,128)S(1)}, u32[]{:S(2)}, u32[]{:S(2)}) collective-permute-start(f32[256,128]{1,0:T(8,128)S(1)} %bitcast.44), channel_id=1, source_target_pairs={{8,0},{16,8},{24,16},{25,24},{17,25},{9,17},{1,9},{2,1},{10,2},{18... | collective-permute-start | bytes 393224 | tf_op jit(solution)/shard_map/ppermute | solution.py:556
  59.1 8.3 %collective-permute-start.13 = (f32[128,128]{1,0:T(8,128)S(1)}, f32[128,128]{1,0:T(8,128)S(1)}, u32[]{:S(2)}, u32[]{:S(2)}) collective-permute-start(f32[128,128]{1,0:T(8,128)S(1)} %get-tuple-element.85), channel_id=1, source_target_pairs={{0,8},{8,16},{16,24},{24,0},{1,9},{9,17},{17,25},{25,1},{2,10},{10... | collective-permute-start | bytes 196616 | tf_op jit(solution)/shard_map/ppermute | solution.py:537
  60.2 7.2 %collective-permute-start.14 = (f32[128,128]{1,0:T(8,128)S(1)}, f32[128,128]{1,0:T(8,128)S(1)}, u32[]{:S(2)}, u32[]{:S(2)}) collective-permute-start(f32[128,128]{1,0:T(8,128)S(1)} %get-tuple-element.87), channel_id=1, source_target_pairs={{0,24},{8,0},{16,8},{24,16},{1,25},{9,1},{17,9},{25,17},{2,26},{10... | collective-permute-start | bytes 196616 | tf_op jit(solution)/shard_map/ppermute | solution.py:537
  62.9 7.3 %collective-permute-start.12 = (f32[512,128]{1,0:T(8,128)S(1)}, f32[512,128]{1,0:T(8,128)S(1)}, u32[]{:S(2)}, u32[]{:S(2)}) collective-permute-start(f32[512,128]{1,0:T(8,128)S(1)} %pad_maximum_fusion), channel_id=1, source_target_pairs={{4,0},{0,4},{5,1},{1,5},{6,2},{2,6},{7,3},{3,7},{12,8},{8,12},{13,... | collective-permute-start | bytes 786440 | tf_op jit(solution)/shard_map/ppermute | solution.py:551
  67.3 13.8 %collective-permute-start.20 = (f32[256,128]{1,0:T(8,128)S(1)}, f32[256,128]{1,0:T(8,128)S(1)}, u32[]{:S(2)}, u32[]{:S(2)}) collective-permute-start(f32[256,128]{1,0:T(8,128)S(1)} %get-tuple-element.96), channel_id=1, source_target_pairs={{0,8},{8,16},{16,24},{24,0},{1,9},{9,17},{17,25},{25,1},{2,10},{10... | collective-permute-start | bytes 393224 | tf_op jit(solution)/shard_map/ppermute | solution.py:537
  70.3 4.5 %collective-permute-start.15 = (f32[128,128]{1,0:T(8,128)S(1)}, f32[128,128]{1,0:T(8,128)S(1)}, u32[]{:S(2)}, u32[]{:S(2)}) collective-permute-start(f32[128,128]{1,0:T(8,128)S(1)} %pad_maximum_fusion.6), channel_id=1, source_target_pairs={{0,8},{8,16},{16,24},{24,25},{25,17},{17,9},{9,1},{1,2},{2,10},{10... | collective-permute-start | bytes 196616 | tf_op jit(solution)/shard_map/ppermute | solution.py:556
  70.4 5.9 %collective-permute-start.16 = (f32[128,128]{1,0:T(8,128)S(1)}, f32[128,128]{1,0:T(8,128)S(1)}, u32[]{:S(2)}, u32[]{:S(2)}) collective-permute-start(f32[128,128]{1,0:T(8,128)S(1)} %pad_maximum_fusion.7), channel_id=1, source_target_pairs={{8,0},{16,8},{24,16},{25,24},{17,25},{9,17},{1,9},{2,1},{10,2},{18... | collective-permute-start | bytes 196616 | tf_op jit(solution)/shard_map/ppermute | solution.py:556
  72.1 11.2 %collective-permute-start.21 = (f32[256,128]{1,0:T(8,128)S(1)}, f32[256,128]{1,0:T(8,128)S(1)}, u32[]{:S(2)}, u32[]{:S(2)}) collective-permute-start(f32[256,128]{1,0:T(8,128)S(1)} %get-tuple-element.99), channel_id=1, source_target_pairs={{0,16},{8,24},{16,0},{24,8},{1,17},{9,25},{17,1},{25,9},{2,18},{10... | collective-permute-start | bytes 393224 | tf_op jit(solution)/shard_map/ppermute | solution.py:537
  72.4 10.9 %collective-permute-start.22 = (f32[256,128]{1,0:T(8,128)S(1)}, f32[256,128]{1,0:T(8,128)S(1)}, u32[]{:S(2)}, u32[]{:S(2)}) collective-permute-start(f32[256,128]{1,0:T(8,128)S(1)} %get-tuple-element.100), channel_id=1, source_target_pairs={{0,24},{8,0},{16,8},{24,16},{1,25},{9,1},{17,9},{25,17},{2,26},{10... | collective-permute-start | bytes 393224 | tf_op jit(solution)/shard_map/ppermute | solution.py:537
  76.3 7.0 %copy-start = (f32[2,16,64,128]{3,2,1,0:T(8,128)S(1)}, f32[2,16,64,128]{3,2,1,0:T(8,128)}, u32[]{:S(2)}) copy-start(f32[2,16,64,128]{3,2,1,0:T(8,128)} %gain.2) | copy-start | bytes 3145732
  76.3 7.0 %copy-start.1 = (s32[16,64,128]{2,1,0:T(8,128)S(1)}, s32[16,64,128]{2,1,0:T(8,128)}, u32[]{:S(2)}) copy-start(s32[16,64,128]{2,1,0:T(8,128)} %mask.5) | copy-start | bytes 1572868
  79.4 8.3 %collective-permute-start.17 = (f32[256,128]{1,0:T(8,128)S(1)}, f32[256,128]{1,0:T(8,128)S(1)}, u32[]{:S(2)}, u32[]{:S(2)}) collective-permute-start(f32[256,128]{1,0:T(8,128)S(1)} %get-tuple-element.93), channel_id=1, source_target_pairs={{0,8},{8,16},{16,24},{24,0},{1,9},{9,17},{17,25},{25,1},{2,10},{10... | collective-permute-start | bytes 393224 | tf_op jit(solution)/shard_map/ppermute | solution.py:537
  80.8 11.5 %collective-permute-start.18 = (f32[256,128]{1,0:T(8,128)S(1)}, f32[256,128]{1,0:T(8,128)S(1)}, u32[]{:S(2)}, u32[]{:S(2)}) collective-permute-start(f32[256,128]{1,0:T(8,128)S(1)} %get-tuple-element.94), channel_id=1, source_target_pairs={{0,16},{8,24},{16,0},{24,8},{1,17},{9,25},{17,1},{25,9},{2,18},{10... | collective-permute-start | bytes 393224 | tf_op jit(solution)/shard_map/ppermute | solution.py:537
  81.1 11.2 %collective-permute-start.19 = (f32[256,128]{1,0:T(8,128)S(1)}, f32[256,128]{1,0:T(8,128)S(1)}, u32[]{:S(2)}, u32[]{:S(2)}) collective-permute-start(f32[256,128]{1,0:T(8,128)S(1)} %get-tuple-element.95), channel_id=1, source_target_pairs={{0,24},{8,0},{16,8},{24,16},{1,25},{9,1},{17,9},{25,17},{2,26},{10... | collective-permute-start | bytes 393224 | tf_op jit(solution)/shard_map/ppermute | solution.py:537

commit v14 on v11

--- a/solution.py
+++ b/solution.py
@@ -28,7 +28,7 @@
 
 
 def distances(devices):
-    return [0, devices // 2] + [d for d in range(1, devices) if d != devices // 2]
+    return list(range(devices))
 
 
 def position():
@@ -617,15 +617,17 @@
     adjoint = jnp.concatenate([by_device[:, s].reshape(2 * levels, order) for s in source], axis=0).T
     forward = jnp.concatenate([by_device[:, t].reshape(2 * levels, order) for t in to], axis=0)
 
-    scaled[1], outer_messages = lax.optimization_barrier((scaled[1], outer_messages))
-    early = shift(outer_messages[1], devices // 2)
+    middle = devices // 2
+    scaled, outer_messages = lax.optimization_barrier((scaled, outer_messages))
+    early = shift(outer_messages[middle], middle)
     mixed = adjoint_mix(adjoint, depth, scaled, length, width)
     edges = flat(mixed[:, :STEPS]), flat(mixed[:, -STEPS:])
     edges, inner_weights = lax.optimization_barrier((edges, (here, left, right)))
     left, right = halo_j(*edges)
     left, right, outer_messages, early = lax.optimization_barrier((left, right, outer_messages, early))
-    own, _, *others = outer_messages
-    outer_parts = [own, early] + [shift(x, d) for x, d in zip(others, distances(devices)[2:])]
+    outer_parts = [
+        early if d == middle else shift(outer_messages[d], d) if d else outer_messages[0] for d in range(devices)
+    ]
     field = [(list(range(length)), mixed, left, right)]
     weights = [(inner_rows, *inner_weights)]
     depths = [depth, right_depth]

time: 92.3 us -> 92.4 us (level)
  starting transfers between devices: 49.8 us -> 54.9 us
  waiting for transfers between devices: 19.6 us -> 15.3 us
    ppermute x15, starting transfers between devices: 23.4 us -> 32.5 us  [shift(): lax.ppermute(x, 'lev', [(k, (k + d) % devices) for k in range(devices)])]
    ppermute x3, starting transfers between devices: 22.9 us -> 19.2 us  [halo_j(): lax.ppermute(last, ('lev', 'gy'), ahead)]
    ppermute x3, waiting for transfers between devices: 5.68 us -> 3.89 us  [halo_j(): lax.ppermute(first, ('lev', 'gy'), back)]
    ppermute x15, waiting for transfers between devices: 12.8 us -> 11.4 us  [shift(): lax.ppermute(x, 'lev', [(k, (k + d) % devices) for k in range(devices)])]
    ppermute x3, waiting for transfers between devices: 1.17 us -> 0.01 us  [halo_j(): lax.ppermute(last, ('lev', 'gy'), ahead)]
  transfers between devices with their start and end apart: 23 -> 23, of which waited for: 8 -> 6; matrix products, arithmetic and copies ran while one was open for 0% -> 0% of each run, Pallas kernels for 17% -> 17%
where the time goes in v14:
time: 92.4 us; the launch traced here: 92.2 us
  starting transfers between devices  54.9 us (59%)
  Pallas kernels  20.2 us (22%)
  waiting for transfers between devices  15.3 us (17%)
  local copies, waits for them, and re-layouts  1.24 us (1%)
    ppermute x15, starting transfers between devices, shift(): lax.ppermute(x, 'lev', [(k, (k + d) % devices) for k in range(devices)])  32.5 us
    ppermute x3, starting transfers between devices, halo_j(): lax.ppermute(last, ('lev', 'gy'), ahead)  19.2 us
    ppermute x15, waiting for transfers between devices, shift(): lax.ppermute(x, 'lev', [(k, (k + d) % devices) for k in range(devices)])  11.4 us
    pallas_call x2, Pallas kernels, spread_mix(): pl.pallas_call(kernel, in_specs=[vmem()] * (1 + len(arrays)), out_specs=[...  5.89 us
    pallas_call x2, Pallas kernels, weight_messages(): pl.pallas_call(functools.partial(pack_kernel, pieces, len(mask)), in_spec...  5.63 us
    ppermute x3, waiting for transfers between devices, halo_j(): lax.ppermute(first, ('lev', 'gy'), back)  3.89 us
    pallas_call x1, Pallas kernels, scaled_messages(): pl.pallas_call(scaled_kernel, in_specs=[pl.BlockSpec(memory_space=pl.ANY)...  3.25 us
    ppermute x2, starting transfers between devices, halo_i(): both = lax.ppermute(jnp.concatenate([first, last], axis=0), 'gx', up)  3.12 us
  transfers between devices with their start and end apart: 23, of which 6 were waited for; matrix products, arithmetic and copies ran while one was open for 0% of the time, Pallas kernels for 17%

profile of v14, /device:TPU:0, one launch (start us, length us, event | category | flops | bytes accessed | tf_op | source)
XLA Modules:
  0.0 92.2 jit_solution(13096822418552767675)
XLA Ops:
  0.0 3.5 %weight_messages.2 = (f32[336,128]{1,0:T(8,128)}, f32[336,128]{1,0:T(8,128)}, f32[336,128]{1,0:T(8,128)}, f32[336,128]{1,0:T(8,128)}) custom-call(f32[16,64,128]{2,1,0:T(8,128)} %along_i.3, f32[16,64,128]{2,1,0:T(8,128)} %along_j.3, s32[16,64,128]{2,1,0:T(8,128)} %mask.5), custom_call_target="tpu_custom_call" | custom-call | tf_op jit(solution)/shard_map/weight_messages/pallas_call | solution.py:210
  3.5 3.1 %collective-permute-start = (f32[336,128]{1,0:T(8,128)}, f32[336,128]{1,0:T(8,128)S(1)}, u32[]{:S(2)}, u32[]{:S(2)}) collective-permute-start(f32[336,128]{1,0:T(8,128)} %get-tuple-element.57), channel_id=1, source_target_pairs={{0,8},{8,16},{16,24},{24,0},{1,9},{9,17},{17,25},{25,1},{2,10},{10... | collective-permute-start | bytes 516104 | tf_op jit(solution)/shard_map/ppermute | solution.py:546
  6.5 2.6 %collective-permute-start.1 = (f32[336,128]{1,0:T(8,128)}, f32[336,128]{1,0:T(8,128)S(1)}, u32[]{:S(2)}, u32[]{:S(2)}) collective-permute-start(f32[336,128]{1,0:T(8,128)} %get-tuple-element.58), channel_id=1, source_target_pairs={{0,16},{8,24},{16,0},{24,8},{1,17},{9,25},{17,1},{25,9},{2,18},{10... | collective-permute-start | bytes 516104 | tf_op jit(solution)/shard_map/ppermute | solution.py:546
  9.1 1.3 %collective-permute-start.2 = (f32[336,128]{1,0:T(8,128)}, f32[336,128]{1,0:T(8,128)S(1)}, u32[]{:S(2)}, u32[]{:S(2)}) collective-permute-start(f32[336,128]{1,0:T(8,128)} %get-tuple-element.59), channel_id=1, source_target_pairs={{0,24},{8,0},{16,8},{24,16},{1,25},{9,1},{17,9},{25,17},{2,26},{10... | collective-permute-start | bytes 516104 | tf_op jit(solution)/shard_map/ppermute | solution.py:546
  10.5 0.0 copy-done.3
  10.5 1.6 %collective-permute-start.7 = (f32[256,128]{1,0:T(8,128)S(1)}, f32[256,128]{1,0:T(8,128)S(1)}, u32[]{:S(2)}, u32[]{:S(2)}) collective-permute-start(f32[256,128]{1,0:T(8,128)S(1)} %pad_maximum_fusion.1), channel_id=1, source_target_pairs={{4,0},{0,4},{5,1},{1,5},{6,2},{2,6},{7,3},{3,7},{12,8},{8,12},{13,... | collective-permute-start | bytes 393224 | tf_op jit(solution)/shard_map/ppermute | solution.py:560
  12.1 3.3 %scaled_messages.1 = (f32[512,128]{1,0:T(8,128)}, f32[512,128]{1,0:T(8,128)}, f32[512,128]{1,0:T(8,128)}, f32[512,128]{1,0:T(8,128)}) custom-call(f32[2,16,64,128]{3,2,1,0:T(8,128)} %increment, f32[2,16,64,128]{3,2,1,0:T(8,128)} %gain.2, s32[16,64,128]{2,1,0:T(8,128)} %mask.5), custom_call_target="tpu_custom_call" | custom-call | tf_op jit(solution)/shard_map/scaled_messages/pallas_call | solution.py:121
  15.4 0.0 copy-start.6
  15.4 0.7 collective-permute-start.4
  16.1 0.1 copy-done.6
  16.3 0.1 copy.13.matrix
  16.4 0.0 collective-permute-done.7
  16.4 0.8 copy-done.8
  17.2 0.3 collective-permute-start.5
  17.6 2.2 %weight_messages.3 = (f32[256,128]{1,0:T(8,128)S(1)}, f32[256,128]{1,0:T(8,128)S(1)}, f32[256,128]{1,0:T(8,128)S(1)}, f32[256,128]{1,0:T(8,128)S(1)}) custom-call(f32[16,64,128]{2,1,0:T(8,128)S(1)} %copy-done.2, f32[16,64,128]{2,1,0:T(8,128)S(1)} %copy-done.3, f32[128,128]{1,0:T(8,128)S(1)} %get-tuple-element.68.refs_0_, ...), custom_call_target="tpu_custom_call" | custom-call | tf_op jit(solution)/shard_map/weight_messages/pallas_call | solution.py:210
  19.7 0.0 collective-permute-done.refs_2_
  19.8 2.8 %collective-permute-start.6 = (f32[512,128]{1,0:T(8,128)S(1)}, f32[512,128]{1,0:T(8,128)S(1)}, u32[]{:S(2)}, u32[]{:S(2)}) collective-permute-start(f32[512,128]{1,0:T(8,128)S(1)} %copy-done.7), channel_id=1, source_target_pairs={{0,24},{8,0},{16,8},{24,16},{1,25},{9,1},{17,9},{25,17},{2,26},{10... | collective-permute-start | bytes 786440 | tf_op jit(solution)/shard_map/ppermute | solution.py:546
  22.5 0.0 collective-permute-done.1.refs_3_
  22.5 0.0 collective-permute-done.2.refs_4_
  22.6 0.4 turn_weights.2.refs_5_.refs_10_
  23.0 0.0 copy-start.4
  23.1 13.6 %collective-permute-start.8 = (f32[160,128]{1,0:T(8,128)S(1)}, f32[160,128]{1,0:T(8,128)S(1)}, u32[]{:S(2)}, u32[]{:S(2)}) collective-permute-start(f32[160,128]{1,0:T(8,128)S(1)} %bitcast.47), channel_id=1, source_target_pairs={{0,8},{8,16},{16,24},{24,25},{25,17},{17,9},{9,1},{1,2},{2,10},{10... | collective-permute-start | bytes 245768 | tf_op jit(solution)/shard_map/ppermute | solution.py:565
  36.7 0.0 collective-permute-start.3
  36.7 0.0 collective-permute-done.4.refs_1_
  36.7 4.5 %collective-permute-done.5.refs_2_ = f32[512,128]{1,0:T(8,128)S(1)} collective-permute-done((f32[512,128]{1,0:T(8,128)S(1)}, f32[512,128]{1,0:T(8,128)S(1)}, u32[]{:S(2)}, u32[]{:S(2)}) %collective-permute-start.5) | collective-permute-done | bytes 262176 | tf_op jit(solution)/shard_map/ppermute | solution.py:546
  41.2 0.0 collective-permute-done.6.refs_3_
  41.2 5.2 %collective-permute-start.11 = (f32[256,128]{1,0:T(8,128)S(1)}, f32[256,128]{1,0:T(8,128)S(1)}, u32[]{:S(2)}, u32[]{:S(2)}) collective-permute-start(f32[256,128]{1,0:T(8,128)S(1)} %get-tuple-element.82), channel_id=1, source_target_pairs={{0,16},{8,24},{16,0},{24,8},{1,17},{9,25},{17,1},{25,9},{2,18},{10... | collective-permute-start | bytes 393224 | tf_op jit(solution)/shard_map/ppermute | solution.py:546
  46.4 1.8 %adjoint_mix.1.refs_2_.refs_4_ = f32[64,32,128]{2,1,0:T(8,128)S(1)} custom-call(f32[128,128]{1,0:T(8,128)S(1)} %copy.13.matrix, f32[16,128]{1,0:T(8,128)S(1)} %slice_add_fusion.refs_0_.depths, f32[512,128]{1,0:T(8,128)S(1)} %copy-done.4, f32[512,128]{1,0:T(8,128)S(1)} %collective-permute-done.4.refs_1_, f32[512,128]{1,0:T(8,128)S(1)} %collective-permute-done.5.refs_2_, ...), custom_call_target="tpu_custom_call" | custom-call | tf_op jit(solution)/shard_map/adjoint_mix/pallas_call | solution.py:272
  48.2 0.0 collective-permute-done.3
  48.2 0.0 collective-permute-done.8.refs_6_.refs_11_
  48.3 3.6 %collective-permute-start.9 = (f32[256,128]{1,0:T(8,128)S(1)}, f32[256,128]{1,0:T(8,128)S(1)}, u32[]{:S(2)}, u32[]{:S(2)}) collective-permute-start(f32[256,128]{1,0:T(8,128)S(1)} %bitcast.42), channel_id=1, source_target_pairs={{0,8},{8,16},{16,24},{24,25},{25,17},{17,9},{9,1},{1,2},{2,10},{10... | collective-permute-start | bytes 393224 | tf_op jit(solution)/shard_map/ppermute | solution.py:565
  51.8 0.0 collective-permute-start.10
  51.9 2.5 %collective-permute-done.11.refs_4_ = f32[256,128]{1,0:T(8,128)S(1)} collective-permute-done((f32[256,128]{1,0:T(8,128)S(1)}, f32[256,128]{1,0:T(8,128)S(1)}, u32[]{:S(2)}, u32[]{:S(2)}) %collective-permute-start.11) | collective-permute-done | bytes 131104 | tf_op jit(solution)/shard_map/ppermute | solution.py:546
  54.4 0.0 collective-permute-done.9.refs_3_.refs_5_
  54.4 2.4 %collective-permute-done.10.refs_4_.refs_6_ = f32[256,128]{1,0:T(8,128)S(1)} collective-permute-done((f32[256,128]{1,0:T(8,128)S(1)}, f32[256,128]{1,0:T(8,128)S(1)}, u32[]{:S(2)}, u32[]{:S(2)}) %collective-permute-start.10) | collective-permute-done | bytes 131104 | tf_op jit(solution)/shard_map/ppermute | solution.py:565
  56.8 1.6 %collective-permute-start.12 = (f32[264,128]{1,0:T(8,128)S(1)}, f32[264,128]{1,0:T(8,128)S(1)}, u32[]{:S(2)}, u32[]{:S(2)}) collective-permute-start(f32[264,128]{1,0:T(8,128)S(1)} %pad_maximum_fusion), channel_id=1, source_target_pairs={{4,0},{0,4},{5,1},{1,5},{6,2},{2,6},{7,3},{3,7},{12,8},{8,12},{13,... | collective-permute-start | bytes 405512 | tf_op jit(solution)/shard_map/ppermute | solution.py:560
  58.4 0.8 collective-permute-start.13
  59.1 3.1 %collective-permute-start.14 = (f32[256,128]{1,0:T(8,128)S(1)}, f32[256,128]{1,0:T(8,128)S(1)}, u32[]{:S(2)}, u32[]{:S(2)}) collective-permute-start(f32[256,128]{1,0:T(8,128)S(1)} %get-tuple-element.95), channel_id=1, source_target_pairs={{0,24},{8,0},{16,8},{24,16},{1,25},{9,1},{17,9},{25,17},{2,26},{10... | collective-permute-start | bytes 393224 | tf_op jit(solution)/shard_map/ppermute | solution.py:546
  62.2 2.9 %spread_mix.2 = (f32[256,128]{1,0:T(8,128)S(1)}, f32[256,128]{1,0:T(8,128)S(1)}, f32[256,128]{1,0:T(8,128)S(1)}, f32[256,128]{1,0:T(8,128)S(1)}) custom-call(f32[128,128]{1,0:T(8,128)S(1)} %get-tuple-element.133.matrix, f32[16,128]{1,0:T(8,128)S(1)} %slice_add_fusion.refs_0_.depths, f32[16,128]{1,0:T(8,128)S(1)} %split.44.refs_1_, ...), custom_call_target="tpu_custom_call" | custom-call | tf_op jit(solution)/shard_map/spread_mix/pallas_call | solution.py:460
  65.1 0.1 collective-permute-start.20
  65.1 1.3 %collective-permute-done.13.refs_3_ = f32[256,128]{1,0:T(8,128)S(1)} collective-permute-done((f32[256,128]{1,0:T(8,128)S(1)}, f32[256,128]{1,0:T(8,128)S(1)}, u32[]{:S(2)}, u32[]{:S(2)}) %collective-permute-start.13) | collective-permute-done | bytes 131104 | tf_op jit(solution)/shard_map/ppermute | solution.py:546
  66.4 0.0 collective-permute-done.14.refs_5_
  66.4 0.0 collective-permute-done.12
  66.5 0.4 turn_weights.3.refs_13_
  67.0 0.1 collective-permute-start.15
  67.0 2.0 %collective-permute-start.16 = (f32[160,128]{1,0:T(8,128)S(1)}, f32[160,128]{1,0:T(8,128)S(1)}, u32[]{:S(2)}, u32[]{:S(2)}) collective-permute-start(f32[160,128]{1,0:T(8,128)S(1)} %pad_maximum_fusion.7), channel_id=1, source_target_pairs={{0,8},{8,16},{16,24},{24,25},{25,17},{17,9},{9,1},{1,2},{2,10},{10... | collective-permute-start | bytes 245768 | tf_op jit(solution)/shard_map/ppermute | solution.py:565
  69.0 1.9 %collective-permute-start.21 = (f32[256,128]{1,0:T(8,128)S(1)}, f32[256,128]{1,0:T(8,128)S(1)}, u32[]{:S(2)}, u32[]{:S(2)}) collective-permute-start(f32[256,128]{1,0:T(8,128)S(1)} %get-tuple-element.105), channel_id=1, source_target_pairs={{0,16},{8,24},{16,0},{24,8},{1,17},{9,25},{17,1},{25,9},{2,18},{10... | collective-permute-start | bytes 393224 | tf_op jit(solution)/shard_map/ppermute | solution.py:546
  71.0 1.9 %collective-permute-start.22 = (f32[256,128]{1,0:T(8,128)S(1)}, f32[256,128]{1,0:T(8,128)S(1)}, u32[]{:S(2)}, u32[]{:S(2)}) collective-permute-start(f32[256,128]{1,0:T(8,128)S(1)} %get-tuple-element.106), channel_id=1, source_target_pairs={{0,24},{8,0},{16,8},{24,16},{1,25},{9,1},{17,9},{25,17},{2,26},{10... | collective-permute-start | bytes 393224 | tf_op jit(solution)/shard_map/ppermute | solution.py:546
  72.8 0.0 collective-permute-done.16
  72.9 1.4 %collective-permute-done.15 = f32[168,128]{1,0:T(8,128)S(1)} collective-permute-done((f32[168,128]{1,0:T(8,128)S(1)}, f32[168,128]{1,0:T(8,128)S(1)}, u32[]{:S(2)}, u32[]{:S(2)}) %collective-permute-start.15) | collective-permute-done | bytes 86048 | tf_op jit(solution)/shard_map/ppermute | solution.py:565
  74.3 0.0 copy-start
  74.3 0.0 copy-start.1
  74.3 3.0 %spread_mix.3 = (f32[256,128]{1,0:T(8,128)S(1)}, f32[256,128]{1,0:T(8,128)S(1)}, f32[256,128]{1,0:T(8,128)S(1)}, f32[256,128]{1,0:T(8,128)S(1)}) custom-call(f32[128,128]{1,0:T(8,128)S(1)} %get-tuple-element.133.matrix, f32[16,128]{1,0:T(8,128)S(1)} %slice_add_fusion.refs_0_.depths, f32[16,128]{1,0:T(8,128)S(1)} %split.44.refs_1_, ...), custom_call_target="tpu_custom_call" | custom-call | tf_op jit(solution)/shard_map/spread_mix/pallas_call | solution.py:460
  77.4 4.0 %collective-permute-start.17 = (f32[256,128]{1,0:T(8,128)S(1)}, f32[256,128]{1,0:T(8,128)S(1)}, u32[]{:S(2)}, u32[]{:S(2)}) collective-permute-start(f32[256,128]{1,0:T(8,128)S(1)} %get-tuple-element.101), channel_id=1, source_target_pairs={{0,8},{8,16},{16,24},{24,0},{1,9},{9,17},{17,25},{25,1},{2,10},{10... | collective-permute-start | bytes 393224 | tf_op jit(solution)/shard_map/ppermute | solution.py:546
  81.4 2.0 %collective-permute-start.18 = (f32[256,128]{1,0:T(8,128)S(1)}, f32[256,128]{1,0:T(8,128)S(1)}, u32[]{:S(2)}, u32[]{:S(2)}) collective-permute-start(f32[256,128]{1,0:T(8,128)S(1)} %get-tuple-element.102), channel_id=1, source_target_pairs={{0,16},{8,24},{16,0},{24,8},{1,17},{9,25},{17,1},{25,9},{2,18},{10... | collective-permute-start | bytes 393224 | tf_op jit(solution)/shard_map/ppermute | solution.py:546
  83.4 0.0 collective-permute-done.20.refs_1_
  83.4 2.8 %collective-permute-start.19 = (f32[256,128]{1,0:T(8,128)S(1)}, f32[256,128]{1,0:T(8,128)S(1)}, u32[]{:S(2)}, u32[]{:S(2)}) collective-permute-start(f32[256,128]{1,0:T(8,128)S(1)} %get-tuple-element.103), channel_id=1, source_target_pairs={{0,24},{8,0},{16,8},{24,16},{1,25},{9,1},{17,9},{25,17},{2,26},{10... | collective-permute-start | bytes 393224 | tf_op jit(solution)/shard_map/ppermute | solution.py:546
  86.2 0.0 collective-permute-done.21.refs_2_
  86.2 0.0 collective-permute-done.22.refs_3_
  86.3 1.4 %result.2.refs_4_ = f32[2,16,64,128]{3,2,1,0:T(8,128)} custom-call(f32[2,16,64,128]{3,2,1,0:T(8,128)S(1)} %copy-done, s32[16,64,128]{2,1,0:T(8,128)S(1)} %copy-done.1, f32[256,128]{1,0:T(8,128)S(1)} %get-tuple-element.91.refs_0_, f32[256,128]{1,0:T(8,128)S(1)} %collective-permute-done.20.refs_1_, f32[256,128]{1,0:T(8,128)S(1)} %collective-permute-done.21.refs_2_, ...), custom_call_target="tpu_custom_call" | custom-call | tf_op jit(solution)/shard_map/result/pallas_call | solution.py:519
  87.7 0.0 collective-permute-done.17.refs_1_
  87.7 3.1 %collective-permute-done.18.refs_2_ = f32[256,128]{1,0:T(8,128)S(1)} collective-permute-done((f32[256,128]{1,0:T(8,128)S(1)}, f32[256,128]{1,0:T(8,128)S(1)}, u32[]{:S(2)}, u32[]{:S(2)}) %collective-permute-start.18) | collective-permute-done | bytes 131104 | tf_op jit(solution)/shard_map/ppermute | solution.py:546
  90.8 0.0 collective-permute-done.19.refs_3_
  90.8 1.4 %result.3 = f32[2,16,64,128]{3,2,1,0:T(8,128)} custom-call(f32[2,16,64,128]{3,2,1,0:T(8,128)S(1)} %copy-done, s32[16,64,128]{2,1,0:T(8,128)S(1)} %copy-done.1, f32[256,128]{1,0:T(8,128)S(1)} %get-tuple-element.100.refs_0_, f32[256,128]{1,0:T(8,128)S(1)} %collective-permute-done.17.refs_1_, ...), custom_call_target="tpu_custom_call", output_to_operand_aliasing={{}: (6, {})} | custom-call | tf_op jit(solution)/shard_map/result/pallas_call | solution.py:519
  (39 shorter events, 0.3 us)
Async XLA Ops:
  0.0 10.5 %copy-start.3 = (f32[16,64,128]{2,1,0:T(8,128)S(1)}, f32[16,64,128]{2,1,0:T(8,128)}, u32[]{:S(2)}) copy-start(f32[16,64,128]{2,1,0:T(8,128)} %along_j.3) | copy-start | bytes 1572868
  0.0 10.5 %copy-start.2 = (f32[16,64,128]{2,1,0:T(8,128)S(1)}, f32[16,64,128]{2,1,0:T(8,128)}, u32[]{:S(2)}) copy-start(f32[16,64,128]{2,1,0:T(8,128)} %along_i.3) | copy-start | bytes 1572868
  3.5 16.3 %collective-permute-start = (f32[336,128]{1,0:T(8,128)}, f32[336,128]{1,0:T(8,128)S(1)}, u32[]{:S(2)}, u32[]{:S(2)}) collective-permute-start(f32[336,128]{1,0:T(8,128)} %get-tuple-element.57), channel_id=1, source_target_pairs={{0,8},{8,16},{16,24},{24,0},{1,9},{9,17},{17,25},{25,1},{2,10},{10... | collective-permute-start | bytes 516104 | tf_op jit(solution)/shard_map/ppermute | solution.py:546
  6.5 16.0 %collective-permute-start.1 = (f32[336,128]{1,0:T(8,128)}, f32[336,128]{1,0:T(8,128)S(1)}, u32[]{:S(2)}, u32[]{:S(2)}) collective-permute-start(f32[336,128]{1,0:T(8,128)} %get-tuple-element.58), channel_id=1, source_target_pairs={{0,16},{8,24},{16,0},{24,8},{1,17},{9,25},{17,1},{25,9},{2,18},{10... | collective-permute-start | bytes 516104 | tf_op jit(solution)/shard_map/ppermute | solution.py:546
  9.1 13.4 %collective-permute-start.2 = (f32[336,128]{1,0:T(8,128)}, f32[336,128]{1,0:T(8,128)S(1)}, u32[]{:S(2)}, u32[]{:S(2)}) collective-permute-start(f32[336,128]{1,0:T(8,128)} %get-tuple-element.59), channel_id=1, source_target_pairs={{0,24},{8,0},{16,8},{24,16},{1,25},{9,1},{17,9},{25,17},{2,26},{10... | collective-permute-start | bytes 516104 | tf_op jit(solution)/shard_map/ppermute | solution.py:546
  10.5 5.9 %collective-permute-start.7 = (f32[256,128]{1,0:T(8,128)S(1)}, f32[256,128]{1,0:T(8,128)S(1)}, u32[]{:S(2)}, u32[]{:S(2)}) collective-permute-start(f32[256,128]{1,0:T(8,128)S(1)} %pad_maximum_fusion.1), channel_id=1, source_target_pairs={{4,0},{0,4},{5,1},{1,5},{6,2},{2,6},{7,3},{3,7},{12,8},{8,12},{13,... | collective-permute-start | bytes 393224 | tf_op jit(solution)/shard_map/ppermute | solution.py:560
  15.4 0.8 copy-start.6
  15.4 21.3 %collective-permute-start.4 = (f32[512,128]{1,0:T(8,128)}, f32[512,128]{1,0:T(8,128)S(1)}, u32[]{:S(2)}, u32[]{:S(2)}) collective-permute-start(f32[512,128]{1,0:T(8,128)} %get-tuple-element.63), channel_id=1, source_target_pairs={{0,8},{8,16},{16,24},{24,0},{1,9},{9,17},{17,25},{25,1},{2,10},{10... | collective-permute-start | bytes 786440 | tf_op jit(solution)/shard_map/ppermute | solution.py:546
  16.2 1.0 %copy-start.8 = (f32[512,128]{1,0:T(8,128)S(1)}, f32[512,128]{1,0:T(8,128)}, u32[]{:S(2)}) copy-start(f32[512,128]{1,0:T(8,128)} %get-tuple-element.64) | copy-start | bytes 786436
  17.2 24.0 %collective-permute-start.5 = (f32[512,128]{1,0:T(8,128)S(1)}, f32[512,128]{1,0:T(8,128)S(1)}, u32[]{:S(2)}, u32[]{:S(2)}) collective-permute-start(f32[512,128]{1,0:T(8,128)S(1)} %copy-done.8), channel_id=1, source_target_pairs={{0,16},{8,24},{16,0},{24,8},{1,17},{9,25},{17,1},{25,9},{2,18},{10... | collective-permute-start | bytes 786440 | tf_op jit(solution)/shard_map/ppermute | solution.py:546
  17.5 2.2 %copy-start.7 = (f32[512,128]{1,0:T(8,128)S(1)}, f32[512,128]{1,0:T(8,128)}, u32[]{:S(2)}) copy-start(f32[512,128]{1,0:T(8,128)} %get-tuple-element.65) | copy-start | bytes 786436
  17.5 5.0 %copy-start.5 = (f32[336,128]{1,0:T(8,128)S(1)}, f32[336,128]{1,0:T(8,128)}, u32[]{:S(2)}) copy-start(f32[336,128]{1,0:T(8,128)} %get-tuple-element.56.refs_1_) | copy-start | bytes 516100
  19.8 21.4 %collective-permute-start.6 = (f32[512,128]{1,0:T(8,128)S(1)}, f32[512,128]{1,0:T(8,128)S(1)}, u32[]{:S(2)}, u32[]{:S(2)}) collective-permute-start(f32[512,128]{1,0:T(8,128)S(1)} %copy-done.7), channel_id=1, source_target_pairs={{0,24},{8,0},{16,8},{24,16},{1,25},{9,1},{17,9},{25,17},{2,26},{10... | collective-permute-start | bytes 786440 | tf_op jit(solution)/shard_map/ppermute | solution.py:546
  23.0 23.4 %copy-start.4 = (f32[512,128]{1,0:T(8,128)S(1)}, f32[512,128]{1,0:T(8,128)}, u32[]{:S(2)}) copy-start(f32[512,128]{1,0:T(8,128)} %get-tuple-element.74.refs_0_) | copy-start | bytes 786436
  23.1 25.2 %collective-permute-start.8 = (f32[160,128]{1,0:T(8,128)S(1)}, f32[160,128]{1,0:T(8,128)S(1)}, u32[]{:S(2)}, u32[]{:S(2)}) collective-permute-start(f32[160,128]{1,0:T(8,128)S(1)} %bitcast.47), channel_id=1, source_target_pairs={{0,8},{8,16},{16,24},{24,25},{25,17},{17,9},{9,1},{1,2},{2,10},{10... | collective-permute-start | bytes 245768 | tf_op jit(solution)/shard_map/ppermute | solution.py:565
  36.7 11.5 %collective-permute-start.3 = (f32[176,128]{1,0:T(8,128)S(1)}, f32[176,128]{1,0:T(8,128)S(1)}, u32[]{:S(2)}, u32[]{:S(2)}) collective-permute-start(f32[176,128]{1,0:T(8,128)S(1)} %pad_maximum_fusion.3), channel_id=1, source_target_pairs={{8,0},{16,8},{24,16},{25,24},{17,25},{9,17},{1,9},{2,1},{10,2},{18... | collective-permute-start | bytes 270344 | tf_op jit(solution)/shard_map/ppermute | solution.py:565
  41.2 13.2 %collective-permute-start.11 = (f32[256,128]{1,0:T(8,128)S(1)}, f32[256,128]{1,0:T(8,128)S(1)}, u32[]{:S(2)}, u32[]{:S(2)}) collective-permute-start(f32[256,128]{1,0:T(8,128)S(1)} %get-tuple-element.82), channel_id=1, source_target_pairs={{0,16},{8,24},{16,0},{24,8},{1,17},{9,25},{17,1},{25,9},{2,18},{10... | collective-permute-start | bytes 393224 | tf_op jit(solution)/shard_map/ppermute | solution.py:546
  48.3 6.1 %collective-permute-start.9 = (f32[256,128]{1,0:T(8,128)S(1)}, f32[256,128]{1,0:T(8,128)S(1)}, u32[]{:S(2)}, u32[]{:S(2)}) collective-permute-start(f32[256,128]{1,0:T(8,128)S(1)} %bitcast.42), channel_id=1, source_target_pairs={{0,8},{8,16},{16,24},{24,25},{25,17},{17,9},{9,1},{1,2},{2,10},{10... | collective-permute-start | bytes 393224 | tf_op jit(solution)/shard_map/ppermute | solution.py:565
  51.8 5.0 %collective-permute-start.10 = (f32[256,128]{1,0:T(8,128)S(1)}, f32[256,128]{1,0:T(8,128)S(1)}, u32[]{:S(2)}, u32[]{:S(2)}) collective-permute-start(f32[256,128]{1,0:T(8,128)S(1)} %bitcast.41), channel_id=1, source_target_pairs={{8,0},{16,8},{24,16},{25,24},{17,25},{9,17},{1,9},{2,1},{10,2},{18... | collective-permute-start | bytes 393224 | tf_op jit(solution)/shard_map/ppermute | solution.py:565
  56.8 9.6 %collective-permute-start.12 = (f32[264,128]{1,0:T(8,128)S(1)}, f32[264,128]{1,0:T(8,128)S(1)}, u32[]{:S(2)}, u32[]{:S(2)}) collective-permute-start(f32[264,128]{1,0:T(8,128)S(1)} %pad_maximum_fusion), channel_id=1, source_target_pairs={{4,0},{0,4},{5,1},{1,5},{6,2},{2,6},{7,3},{3,7},{12,8},{8,12},{13,... | collective-permute-start | bytes 405512 | tf_op jit(solution)/shard_map/ppermute | solution.py:560
  58.4 8.0 %collective-permute-start.13 = (f32[256,128]{1,0:T(8,128)S(1)}, f32[256,128]{1,0:T(8,128)S(1)}, u32[]{:S(2)}, u32[]{:S(2)}) collective-permute-start(f32[256,128]{1,0:T(8,128)S(1)} %get-tuple-element.93), channel_id=1, source_target_pairs={{0,8},{8,16},{16,24},{24,0},{1,9},{9,17},{17,25},{25,1},{2,10},{10... | collective-permute-start | bytes 393224 | tf_op jit(solution)/shard_map/ppermute | solution.py:546
  59.1 7.3 %collective-permute-start.14 = (f32[256,128]{1,0:T(8,128)S(1)}, f32[256,128]{1,0:T(8,128)S(1)}, u32[]{:S(2)}, u32[]{:S(2)}) collective-permute-start(f32[256,128]{1,0:T(8,128)S(1)} %get-tuple-element.95), channel_id=1, source_target_pairs={{0,24},{8,0},{16,8},{24,16},{1,25},{9,1},{17,9},{25,17},{2,26},{10... | collective-permute-start | bytes 393224 | tf_op jit(solution)/shard_map/ppermute | solution.py:546
  65.1 18.3 %collective-permute-start.20 = (f32[256,128]{1,0:T(8,128)S(1)}, f32[256,128]{1,0:T(8,128)S(1)}, u32[]{:S(2)}, u32[]{:S(2)}) collective-permute-start(f32[256,128]{1,0:T(8,128)S(1)} %get-tuple-element.104), channel_id=1, source_target_pairs={{0,8},{8,16},{16,24},{24,0},{1,9},{9,17},{17,25},{25,1},{2,10},{10... | collective-permute-start | bytes 393224 | tf_op jit(solution)/shard_map/ppermute | solution.py:546
  67.0 7.4 %collective-permute-start.15 = (f32[168,128]{1,0:T(8,128)S(1)}, f32[168,128]{1,0:T(8,128)S(1)}, u32[]{:S(2)}, u32[]{:S(2)}) collective-permute-start(f32[168,128]{1,0:T(8,128)S(1)} %pad_maximum_fusion.6), channel_id=1, source_target_pairs={{8,0},{16,8},{24,16},{25,24},{17,25},{9,17},{1,9},{2,1},{10,2},{18... | collective-permute-start | bytes 258056 | tf_op jit(solution)/shard_map/ppermute | solution.py:565
  67.0 5.8 %collective-permute-start.16 = (f32[160,128]{1,0:T(8,128)S(1)}, f32[160,128]{1,0:T(8,128)S(1)}, u32[]{:S(2)}, u32[]{:S(2)}) collective-permute-start(f32[160,128]{1,0:T(8,128)S(1)} %pad_maximum_fusion.7), channel_id=1, source_target_pairs={{0,8},{8,16},{16,24},{24,25},{25,17},{17,9},{9,1},{1,2},{2,10},{10... | collective-permute-start | bytes 245768 | tf_op jit(solution)/shard_map/ppermute | solution.py:565
  69.0 17.2 %collective-permute-start.21 = (f32[256,128]{1,0:T(8,128)S(1)}, f32[256,128]{1,0:T(8,128)S(1)}, u32[]{:S(2)}, u32[]{:S(2)}) collective-permute-start(f32[256,128]{1,0:T(8,128)S(1)} %get-tuple-element.105), channel_id=1, source_target_pairs={{0,16},{8,24},{16,0},{24,8},{1,17},{9,25},{17,1},{25,9},{2,18},{10... | collective-permute-start | bytes 393224 | tf_op jit(solution)/shard_map/ppermute | solution.py:546
  71.0 15.3 %collective-permute-start.22 = (f32[256,128]{1,0:T(8,128)S(1)}, f32[256,128]{1,0:T(8,128)S(1)}, u32[]{:S(2)}, u32[]{:S(2)}) collective-permute-start(f32[256,128]{1,0:T(8,128)S(1)} %get-tuple-element.106), channel_id=1, source_target_pairs={{0,24},{8,0},{16,8},{24,16},{1,25},{9,1},{17,9},{25,17},{2,26},{10... | collective-permute-start | bytes 393224 | tf_op jit(solution)/shard_map/ppermute | solution.py:546
  74.3 11.9 %copy-start = (f32[2,16,64,128]{3,2,1,0:T(8,128)S(1)}, f32[2,16,64,128]{3,2,1,0:T(8,128)}, u32[]{:S(2)}) copy-start(f32[2,16,64,128]{3,2,1,0:T(8,128)} %gain.2) | copy-start | bytes 3145732
  74.3 11.9 %copy-start.1 = (s32[16,64,128]{2,1,0:T(8,128)S(1)}, s32[16,64,128]{2,1,0:T(8,128)}, u32[]{:S(2)}) copy-start(s32[16,64,128]{2,1,0:T(8,128)} %mask.5) | copy-start | bytes 1572868
  77.4 10.3 %collective-permute-start.17 = (f32[256,128]{1,0:T(8,128)S(1)}, f32[256,128]{1,0:T(8,128)S(1)}, u32[]{:S(2)}, u32[]{:S(2)}) collective-permute-start(f32[256,128]{1,0:T(8,128)S(1)} %get-tuple-element.101), channel_id=1, source_target_pairs={{0,8},{8,16},{16,24},{24,0},{1,9},{9,17},{17,25},{25,1},{2,10},{10... | collective-permute-start | bytes 393224 | tf_op jit(solution)/shard_map/ppermute | solution.py:546
  81.4 9.4 %collective-permute-start.18 = (f32[256,128]{1,0:T(8,128)S(1)}, f32[256,128]{1,0:T(8,128)S(1)}, u32[]{:S(2)}, u32[]{:S(2)}) collective-permute-start(f32[256,128]{1,0:T(8,128)S(1)} %get-tuple-element.102), channel_id=1, source_target_pairs={{0,16},{8,24},{16,0},{24,8},{1,17},{9,25},{17,1},{25,9},{2,18},{10... | collective-permute-start | bytes 393224 | tf_op jit(solution)/shard_map/ppermute | solution.py:546
  83.4 7.4 %collective-permute-start.19 = (f32[256,128]{1,0:T(8,128)S(1)}, f32[256,128]{1,0:T(8,128)S(1)}, u32[]{:S(2)}, u32[]{:S(2)}) collective-permute-start(f32[256,128]{1,0:T(8,128)S(1)} %get-tuple-element.103), channel_id=1, source_target_pairs={{0,24},{8,0},{16,8},{24,16},{1,25},{9,1},{17,9},{25,17},{2,26},{10... | collective-permute-start | bytes 393224 | tf_op jit(solution)/shard_map/ppermute | solution.py:546

commit v15 on v14

--- a/solution.py
+++ b/solution.py
@@ -635,7 +635,6 @@
     _, upper, lower = lax.optimization_barrier((left, mixed[:STEPS], mixed[-STEPS:]))
     _, outer_parts = lax.optimization_barrier((inner_mixed[0], outer_parts))
     inner_mixed = exchange(inner_mixed)
-    out = result((inner,), norm_gain, sea_mask, inner_mixed, None)
 
     above, below = halo_i(
         jnp.concatenate([flat(upper), depth[:STEPS]], axis=0),
@@ -650,6 +649,11 @@
         jnp.concatenate([flat(here[:, :STEPS]), flat(halo[:, :STEPS]), halo_depth], axis=0),
         jnp.concatenate([flat(here[:, -STEPS:]), flat(halo[:, -STEPS:])], axis=0),
     )
+    light = [d for d in range(1, devices) if d != middle]
+    left, right, moved = lax.optimization_barrier((left, right, [inner_mixed[d] for d in light]))
+    for d, x in zip(light, moved):
+        inner_mixed[d] = x
+    out = result((inner,), norm_gain, sea_mask, inner_mixed, None)
     sizes = len(outer_rows) * STEPS, 2 * STEPS * STEPS
     left, halo_left = cut(left, *sizes)
     right, halo_right, right_halo_depth = cut(right, *sizes, 2 * STEPS)

time: 92.4 us -> 92.4 us (level)
    ppermute x3, waiting for transfers between devices: 3.89 us -> 2.46 us  [halo_j(): lax.ppermute(first, ('lev', 'gy'), back)]
    ppermute x3, waiting for transfers between devices: 0.01 us -> 1.02 us  [halo_j(): lax.ppermute(last, ('lev', 'gy'), ahead)]
    ppermute x15, waiting for transfers between devices: 11.4 us -> 12.4 us  [shift(): lax.ppermute(x, 'lev', [(k, (k + d) % devices) for k in range(devices)])]
where the time goes in v15:
time: 92.4 us; the launch traced here: 92.1 us
  starting transfers between devices  54.2 us (59%)
  Pallas kernels  20.2 us (22%)
  waiting for transfers between devices  15.9 us (17%)
  local copies, waits for them, and re-layouts  1.24 us (1%)
    ppermute x15, starting transfers between devices, shift(): lax.ppermute(x, 'lev', [(k, (k + d) % devices) for k in range(devices)])  31.9 us
    ppermute x3, starting transfers between devices, halo_j(): lax.ppermute(last, ('lev', 'gy'), ahead)  19.2 us
    ppermute x15, waiting for transfers between devices, shift(): lax.ppermute(x, 'lev', [(k, (k + d) % devices) for k in range(devices)])  12.4 us
    pallas_call x2, Pallas kernels, spread_mix(): pl.pallas_call(kernel, in_specs=[vmem()] * (1 + len(arrays)), out_specs=[...  5.89 us
    pallas_call x2, Pallas kernels, weight_messages(): pl.pallas_call(functools.partial(pack_kernel, pieces, len(mask)), in_spec...  5.63 us
    pallas_call x1, Pallas kernels, scaled_messages(): pl.pallas_call(scaled_kernel, in_specs=[pl.BlockSpec(memory_space=pl.ANY)...  3.25 us
    ppermute x2, starting transfers between devices, halo_i(): both = lax.ppermute(jnp.concatenate([first, last], axis=0), 'gx', up)  3.12 us
    pallas_call x2, Pallas kernels, result(): pl.pallas_call(kernel, in_specs=[vmem()] * (2 + groups) + [anywhere] * le...  2.86 us
  transfers between devices with their start and end apart: 23, of which 6 were waited for; matrix products, arithmetic and copies ran while one was open for 0% of the time, Pallas kernels for 17%

profile of v15, /device:TPU:0, one launch (start us, length us, event | category | flops | bytes accessed | tf_op | source)
XLA Modules:
  0.0 92.1 jit_solution(15336063392969143601)
XLA Ops:
  0.0 3.5 %weight_messages.2 = (f32[336,128]{1,0:T(8,128)}, f32[336,128]{1,0:T(8,128)}, f32[336,128]{1,0:T(8,128)}, f32[336,128]{1,0:T(8,128)}) custom-call(f32[16,64,128]{2,1,0:T(8,128)} %along_i.3, f32[16,64,128]{2,1,0:T(8,128)} %along_j.3, s32[16,64,128]{2,1,0:T(8,128)} %mask.5), custom_call_target="tpu_custom_call" | custom-call | tf_op jit(solution)/shard_map/weight_messages/pallas_call | solution.py:210
  3.5 3.1 %collective-permute-start = (f32[336,128]{1,0:T(8,128)}, f32[336,128]{1,0:T(8,128)S(1)}, u32[]{:S(2)}, u32[]{:S(2)}) collective-permute-start(f32[336,128]{1,0:T(8,128)} %get-tuple-element.61), channel_id=1, source_target_pairs={{0,8},{8,16},{16,24},{24,0},{1,9},{9,17},{17,25},{25,1},{2,10},{10... | collective-permute-start | bytes 516104 | tf_op jit(solution)/shard_map/ppermute | solution.py:546
  6.5 2.6 %collective-permute-start.1 = (f32[336,128]{1,0:T(8,128)}, f32[336,128]{1,0:T(8,128)S(1)}, u32[]{:S(2)}, u32[]{:S(2)}) collective-permute-start(f32[336,128]{1,0:T(8,128)} %get-tuple-element.62), channel_id=1, source_target_pairs={{0,16},{8,24},{16,0},{24,8},{1,17},{9,25},{17,1},{25,9},{2,18},{10... | collective-permute-start | bytes 516104 | tf_op jit(solution)/shard_map/ppermute | solution.py:546
  9.1 1.3 %collective-permute-start.2 = (f32[336,128]{1,0:T(8,128)}, f32[336,128]{1,0:T(8,128)S(1)}, u32[]{:S(2)}, u32[]{:S(2)}) collective-permute-start(f32[336,128]{1,0:T(8,128)} %get-tuple-element.63), channel_id=1, source_target_pairs={{0,24},{8,0},{16,8},{24,16},{1,25},{9,1},{17,9},{25,17},{2,26},{10... | collective-permute-start | bytes 516104 | tf_op jit(solution)/shard_map/ppermute | solution.py:546
  10.5 1.6 %collective-permute-start.7 = (f32[256,128]{1,0:T(8,128)S(1)}, f32[256,128]{1,0:T(8,128)S(1)}, u32[]{:S(2)}, u32[]{:S(2)}) collective-permute-start(f32[256,128]{1,0:T(8,128)S(1)} %pad_maximum_fusion.1), channel_id=1, source_target_pairs={{4,0},{0,4},{5,1},{1,5},{6,2},{2,6},{7,3},{3,7},{12,8},{8,12},{13,... | collective-permute-start | bytes 393224 | tf_op jit(solution)/shard_map/ppermute | solution.py:560
  12.1 3.3 %scaled_messages.1 = (f32[512,128]{1,0:T(8,128)}, f32[512,128]{1,0:T(8,128)}, f32[512,128]{1,0:T(8,128)}, f32[512,128]{1,0:T(8,128)}) custom-call(f32[2,16,64,128]{3,2,1,0:T(8,128)} %increment, f32[2,16,64,128]{3,2,1,0:T(8,128)} %gain.2, s32[16,64,128]{2,1,0:T(8,128)} %mask.5), custom_call_target="tpu_custom_call" | custom-call | tf_op jit(solution)/shard_map/scaled_messages/pallas_call | solution.py:121
  15.4 0.0 copy-start.6
  15.4 0.7 collective-permute-start.4
  16.1 0.1 copy-done.6
  16.3 0.1 copy.13.matrix
  16.4 0.0 collective-permute-done.7
  16.4 0.8 copy-done.8
  17.2 0.3 collective-permute-start.5
  17.6 2.2 %weight_messages.3 = (f32[256,128]{1,0:T(8,128)S(1)}, f32[256,128]{1,0:T(8,128)S(1)}, f32[256,128]{1,0:T(8,128)S(1)}, f32[256,128]{1,0:T(8,128)S(1)}) custom-call(f32[16,64,128]{2,1,0:T(8,128)S(1)} %copy-done.2, f32[16,64,128]{2,1,0:T(8,128)S(1)} %copy-done.3, f32[128,128]{1,0:T(8,128)S(1)} %get-tuple-element.72.refs_0_, ...), custom_call_target="tpu_custom_call" | custom-call | tf_op jit(solution)/shard_map/weight_messages/pallas_call | solution.py:210
  19.7 0.0 collective-permute-done.refs_2_
  19.8 2.8 %collective-permute-start.6 = (f32[512,128]{1,0:T(8,128)S(1)}, f32[512,128]{1,0:T(8,128)S(1)}, u32[]{:S(2)}, u32[]{:S(2)}) collective-permute-start(f32[512,128]{1,0:T(8,128)S(1)} %copy-done.7), channel_id=1, source_target_pairs={{0,24},{8,0},{16,8},{24,16},{1,25},{9,1},{17,9},{25,17},{2,26},{10... | collective-permute-start | bytes 786440 | tf_op jit(solution)/shard_map/ppermute | solution.py:546
  22.5 0.0 collective-permute-done.1.refs_3_
  22.5 0.0 collective-permute-done.2.refs_4_
  22.5 0.0 copy-done.5
  22.6 0.4 turn_weights.2.refs_5_.refs_10_
  23.0 0.0 copy-start.4
  23.1 13.6 %collective-permute-start.8 = (f32[160,128]{1,0:T(8,128)S(1)}, f32[160,128]{1,0:T(8,128)S(1)}, u32[]{:S(2)}, u32[]{:S(2)}) collective-permute-start(f32[160,128]{1,0:T(8,128)S(1)} %bitcast.47), channel_id=1, source_target_pairs={{0,8},{8,16},{16,24},{24,25},{25,17},{17,9},{9,1},{1,2},{2,10},{10... | collective-permute-start | bytes 245768 | tf_op jit(solution)/shard_map/ppermute | solution.py:565
  36.7 0.0 collective-permute-start.3
  36.7 0.0 collective-permute-done.4.refs_1_
  36.7 4.5 %collective-permute-done.5.refs_2_ = f32[512,128]{1,0:T(8,128)S(1)} collective-permute-done((f32[512,128]{1,0:T(8,128)S(1)}, f32[512,128]{1,0:T(8,128)S(1)}, u32[]{:S(2)}, u32[]{:S(2)}) %collective-permute-start.5) | collective-permute-done | bytes 262176 | tf_op jit(solution)/shard_map/ppermute | solution.py:546
  41.2 0.0 collective-permute-done.6.refs_3_
  41.2 5.2 %collective-permute-start.11 = (f32[256,128]{1,0:T(8,128)S(1)}, f32[256,128]{1,0:T(8,128)S(1)}, u32[]{:S(2)}, u32[]{:S(2)}) collective-permute-start(f32[256,128]{1,0:T(8,128)S(1)} %get-tuple-element.86), channel_id=1, source_target_pairs={{0,16},{8,24},{16,0},{24,8},{1,17},{9,25},{17,1},{25,9},{2,18},{10... | collective-permute-start | bytes 393224 | tf_op jit(solution)/shard_map/ppermute | solution.py:546
  46.4 1.8 %adjoint_mix.1.refs_2_.refs_4_ = f32[64,32,128]{2,1,0:T(8,128)S(1)} custom-call(f32[128,128]{1,0:T(8,128)S(1)} %copy.13.matrix, f32[16,128]{1,0:T(8,128)S(1)} %slice_add_fusion.refs_0_.depths, f32[512,128]{1,0:T(8,128)S(1)} %copy-done.4, f32[512,128]{1,0:T(8,128)S(1)} %collective-permute-done.4.refs_1_, f32[512,128]{1,0:T(8,128)S(1)} %collective-permute-done.5.refs_2_, ...), custom_call_target="tpu_custom_call" | custom-call | tf_op jit(solution)/shard_map/adjoint_mix/pallas_call | solution.py:272
  48.2 0.0 collective-permute-done.3
  48.2 0.0 collective-permute-done.8.refs_6_.refs_11_
  48.3 3.6 %collective-permute-start.9 = (f32[256,128]{1,0:T(8,128)S(1)}, f32[256,128]{1,0:T(8,128)S(1)}, u32[]{:S(2)}, u32[]{:S(2)}) collective-permute-start(f32[256,128]{1,0:T(8,128)S(1)} %bitcast.42), channel_id=1, source_target_pairs={{0,8},{8,16},{16,24},{24,25},{25,17},{17,9},{9,1},{1,2},{2,10},{10... | collective-permute-start | bytes 393224 | tf_op jit(solution)/shard_map/ppermute | solution.py:565
  51.8 0.0 collective-permute-start.10
  51.9 2.5 %collective-permute-done.11.refs_4_ = f32[256,128]{1,0:T(8,128)S(1)} collective-permute-done((f32[256,128]{1,0:T(8,128)S(1)}, f32[256,128]{1,0:T(8,128)S(1)}, u32[]{:S(2)}, u32[]{:S(2)}) %collective-permute-start.11) | collective-permute-done | bytes 131104 | tf_op jit(solution)/shard_map/ppermute | solution.py:546
  54.4 0.0 collective-permute-done.9.refs_3_.refs_5_
  54.4 2.4 %collective-permute-done.10.refs_4_.refs_6_ = f32[256,128]{1,0:T(8,128)S(1)} collective-permute-done((f32[256,128]{1,0:T(8,128)S(1)}, f32[256,128]{1,0:T(8,128)S(1)}, u32[]{:S(2)}, u32[]{:S(2)}) %collective-permute-start.10) | collective-permute-done | bytes 131104 | tf_op jit(solution)/shard_map/ppermute | solution.py:565
  56.8 1.6 %collective-permute-start.12 = (f32[264,128]{1,0:T(8,128)S(1)}, f32[264,128]{1,0:T(8,128)S(1)}, u32[]{:S(2)}, u32[]{:S(2)}) collective-permute-start(f32[264,128]{1,0:T(8,128)S(1)} %pad_maximum_fusion), channel_id=1, source_target_pairs={{4,0},{0,4},{5,1},{1,5},{6,2},{2,6},{7,3},{3,7},{12,8},{8,12},{13,... | collective-permute-start | bytes 405512 | tf_op jit(solution)/shard_map/ppermute | solution.py:560
  58.4 0.8 collective-permute-start.13
  59.1 3.1 %collective-permute-start.14 = (f32[256,128]{1,0:T(8,128)S(1)}, f32[256,128]{1,0:T(8,128)S(1)}, u32[]{:S(2)}, u32[]{:S(2)}) collective-permute-start(f32[256,128]{1,0:T(8,128)S(1)} %get-tuple-element.99), channel_id=1, source_target_pairs={{0,24},{8,0},{16,8},{24,16},{1,25},{9,1},{17,9},{25,17},{2,26},{10... | collective-permute-start | bytes 393224 | tf_op jit(solution)/shard_map/ppermute | solution.py:546
  62.2 2.9 %spread_mix.2 = (f32[256,128]{1,0:T(8,128)S(1)}, f32[256,128]{1,0:T(8,128)S(1)}, f32[256,128]{1,0:T(8,128)S(1)}, f32[256,128]{1,0:T(8,128)S(1)}) custom-call(f32[128,128]{1,0:T(8,128)S(1)} %get-tuple-element.141.matrix, f32[16,128]{1,0:T(8,128)S(1)} %slice_add_fusion.refs_0_.depths, f32[16,128]{1,0:T(8,128)S(1)} %split.44.refs_1_, ...), custom_call_target="tpu_custom_call" | custom-call | tf_op jit(solution)/shard_map/spread_mix/pallas_call | solution.py:460
  65.1 0.1 collective-permute-start.17
  65.1 3.8 %collective-permute-start.18 = (f32[256,128]{1,0:T(8,128)S(1)}, f32[256,128]{1,0:T(8,128)S(1)}, u32[]{:S(2)}, u32[]{:S(2)}) collective-permute-start(f32[256,128]{1,0:T(8,128)S(1)} %get-tuple-element.105), channel_id=1, source_target_pairs={{0,24},{8,0},{16,8},{24,16},{1,25},{9,1},{17,9},{25,17},{2,26},{10... | collective-permute-start | bytes 393224 | tf_op jit(solution)/shard_map/ppermute | solution.py:546
  68.9 0.0 collective-permute-done.13.refs_3_
  69.0 0.0 collective-permute-done.14.refs_5_
  69.0 0.0 collective-permute-done.12
  69.0 0.4 turn_weights.3.refs_13_
  69.5 0.1 collective-permute-start.16
  69.6 2.0 %collective-permute-start.15 = (f32[160,128]{1,0:T(8,128)S(1)}, f32[160,128]{1,0:T(8,128)S(1)}, u32[]{:S(2)}, u32[]{:S(2)}) collective-permute-start(f32[160,128]{1,0:T(8,128)S(1)} %pad_maximum_fusion.7), channel_id=1, source_target_pairs={{0,8},{8,16},{16,24},{24,25},{25,17},{17,9},{9,1},{1,2},{2,10},{10... | collective-permute-start | bytes 245768 | tf_op jit(solution)/shard_map/ppermute | solution.py:565
  71.6 0.0 collective-permute-start.22
  71.6 1.8 %collective-permute-done.17.refs_1_ = f32[256,128]{1,0:T(8,128)S(1)} collective-permute-done((f32[256,128]{1,0:T(8,128)S(1)}, f32[256,128]{1,0:T(8,128)S(1)}, u32[]{:S(2)}, u32[]{:S(2)}) %collective-permute-start.17) | collective-permute-done | bytes 131104 | tf_op jit(solution)/shard_map/ppermute | solution.py:546
  73.4 0.0 collective-permute-done.18.refs_3_
  73.4 1.0 %collective-permute-done.15 = f32[160,128]{1,0:T(8,128)S(1)} collective-permute-done((f32[160,128]{1,0:T(8,128)S(1)}, f32[160,128]{1,0:T(8,128)S(1)}, u32[]{:S(2)}, u32[]{:S(2)}) %collective-permute-start.15) | collective-permute-done | bytes 81952 | tf_op jit(solution)/shard_map/ppermute | solution.py:565
  74.4 0.0 collective-permute-done.16
  74.4 0.0 copy-start
  74.5 0.0 copy-start.1
  74.5 3.0 %spread_mix.3 = (f32[256,128]{1,0:T(8,128)S(1)}, f32[256,128]{1,0:T(8,128)S(1)}, f32[256,128]{1,0:T(8,128)S(1)}, f32[256,128]{1,0:T(8,128)S(1)}) custom-call(f32[128,128]{1,0:T(8,128)S(1)} %get-tuple-element.141.matrix, f32[16,128]{1,0:T(8,128)S(1)} %slice_add_fusion.refs_0_.depths, f32[16,128]{1,0:T(8,128)S(1)} %split.44.refs_1_, ...), custom_call_target="tpu_custom_call" | custom-call | tf_op jit(solution)/shard_map/spread_mix/pallas_call | solution.py:460
  77.5 3.2 %collective-permute-start.19 = (f32[256,128]{1,0:T(8,128)S(1)}, f32[256,128]{1,0:T(8,128)S(1)}, u32[]{:S(2)}, u32[]{:S(2)}) collective-permute-start(f32[256,128]{1,0:T(8,128)S(1)} %get-tuple-element.109), channel_id=1, source_target_pairs={{0,8},{8,16},{16,24},{24,0},{1,9},{9,17},{17,25},{25,1},{2,10},{10... | collective-permute-start | bytes 393224 | tf_op jit(solution)/shard_map/ppermute | solution.py:546
  80.7 2.1 %collective-permute-start.20 = (f32[256,128]{1,0:T(8,128)S(1)}, f32[256,128]{1,0:T(8,128)S(1)}, u32[]{:S(2)}, u32[]{:S(2)}) collective-permute-start(f32[256,128]{1,0:T(8,128)S(1)} %get-tuple-element.110), channel_id=1, source_target_pairs={{0,16},{8,24},{16,0},{24,8},{1,17},{9,25},{17,1},{25,9},{2,18},{10... | collective-permute-start | bytes 393224 | tf_op jit(solution)/shard_map/ppermute | solution.py:546
  82.8 2.8 %collective-permute-start.21 = (f32[256,128]{1,0:T(8,128)S(1)}, f32[256,128]{1,0:T(8,128)S(1)}, u32[]{:S(2)}, u32[]{:S(2)}) collective-permute-start(f32[256,128]{1,0:T(8,128)S(1)} %get-tuple-element.111), channel_id=1, source_target_pairs={{0,24},{8,0},{16,8},{24,16},{1,25},{9,1},{17,9},{25,17},{2,26},{10... | collective-permute-start | bytes 393224 | tf_op jit(solution)/shard_map/ppermute | solution.py:546
  85.7 0.0 collective-permute-done.22.refs_2_
  85.7 1.4 %result.2.refs_4_ = f32[2,16,64,128]{3,2,1,0:T(8,128)} custom-call(f32[2,16,64,128]{3,2,1,0:T(8,128)S(1)} %copy-done, s32[16,64,128]{2,1,0:T(8,128)S(1)} %copy-done.1, f32[256,128]{1,0:T(8,128)S(1)} %get-tuple-element.95.refs_0_, f32[256,128]{1,0:T(8,128)S(1)} %collective-permute-done.17.refs_1_, f32[256,128]{1,0:T(8,128)S(1)} %collective-permute-done.22.refs_2_, ...), custom_call_target="tpu_custom_call" | custom-call | tf_op jit(solution)/shard_map/result/pallas_call | solution.py:519
  87.1 0.0 collective-permute-done.19.refs_1_
  87.1 3.6 %collective-permute-done.20.refs_2_ = f32[256,128]{1,0:T(8,128)S(1)} collective-permute-done((f32[256,128]{1,0:T(8,128)S(1)}, f32[256,128]{1,0:T(8,128)S(1)}, u32[]{:S(2)}, u32[]{:S(2)}) %collective-permute-start.20) | collective-permute-done | bytes 131104 | tf_op jit(solution)/shard_map/ppermute | solution.py:546
  90.7 0.0 collective-permute-done.21.refs_3_
  90.7 1.4 %result.3 = f32[2,16,64,128]{3,2,1,0:T(8,128)} custom-call(f32[2,16,64,128]{3,2,1,0:T(8,128)S(1)} %copy-done, s32[16,64,128]{2,1,0:T(8,128)S(1)} %copy-done.1, f32[256,128]{1,0:T(8,128)S(1)} %get-tuple-element.108.refs_0_, f32[256,128]{1,0:T(8,128)S(1)} %collective-permute-done.19.refs_1_, ...), custom_call_target="tpu_custom_call", output_to_operand_aliasing={{}: (6, {})} | custom-call | tf_op jit(solution)/shard_map/result/pallas_call | solution.py:519
  (39 shorter events, 0.4 us)
Async XLA Ops:
  0.0 10.5 %copy-start.3 = (f32[16,64,128]{2,1,0:T(8,128)S(1)}, f32[16,64,128]{2,1,0:T(8,128)}, u32[]{:S(2)}) copy-start(f32[16,64,128]{2,1,0:T(8,128)} %along_j.3) | copy-start | bytes 1572868
  0.0 10.5 %copy-start.2 = (f32[16,64,128]{2,1,0:T(8,128)S(1)}, f32[16,64,128]{2,1,0:T(8,128)}, u32[]{:S(2)}) copy-start(f32[16,64,128]{2,1,0:T(8,128)} %along_i.3) | copy-start | bytes 1572868
  3.5 16.3 %collective-permute-start = (f32[336,128]{1,0:T(8,128)}, f32[336,128]{1,0:T(8,128)S(1)}, u32[]{:S(2)}, u32[]{:S(2)}) collective-permute-start(f32[336,128]{1,0:T(8,128)} %get-tuple-element.61), channel_id=1, source_target_pairs={{0,8},{8,16},{16,24},{24,0},{1,9},{9,17},{17,25},{25,1},{2,10},{10... | collective-permute-start | bytes 516104 | tf_op jit(solution)/shard_map/ppermute | solution.py:546
  6.5 16.0 %collective-permute-start.1 = (f32[336,128]{1,0:T(8,128)}, f32[336,128]{1,0:T(8,128)S(1)}, u32[]{:S(2)}, u32[]{:S(2)}) collective-permute-start(f32[336,128]{1,0:T(8,128)} %get-tuple-element.62), channel_id=1, source_target_pairs={{0,16},{8,24},{16,0},{24,8},{1,17},{9,25},{17,1},{25,9},{2,18},{10... | collective-permute-start | bytes 516104 | tf_op jit(solution)/shard_map/ppermute | solution.py:546
  9.1 13.4 %collective-permute-start.2 = (f32[336,128]{1,0:T(8,128)}, f32[336,128]{1,0:T(8,128)S(1)}, u32[]{:S(2)}, u32[]{:S(2)}) collective-permute-start(f32[336,128]{1,0:T(8,128)} %get-tuple-element.63), channel_id=1, source_target_pairs={{0,24},{8,0},{16,8},{24,16},{1,25},{9,1},{17,9},{25,17},{2,26},{10... | collective-permute-start | bytes 516104 | tf_op jit(solution)/shard_map/ppermute | solution.py:546
  10.5 5.9 %collective-permute-start.7 = (f32[256,128]{1,0:T(8,128)S(1)}, f32[256,128]{1,0:T(8,128)S(1)}, u32[]{:S(2)}, u32[]{:S(2)}) collective-permute-start(f32[256,128]{1,0:T(8,128)S(1)} %pad_maximum_fusion.1), channel_id=1, source_target_pairs={{4,0},{0,4},{5,1},{1,5},{6,2},{2,6},{7,3},{3,7},{12,8},{8,12},{13,... | collective-permute-start | bytes 393224 | tf_op jit(solution)/shard_map/ppermute | solution.py:560
  15.4 0.8 copy-start.6
  15.4 21.3 %collective-permute-start.4 = (f32[512,128]{1,0:T(8,128)}, f32[512,128]{1,0:T(8,128)S(1)}, u32[]{:S(2)}, u32[]{:S(2)}) collective-permute-start(f32[512,128]{1,0:T(8,128)} %get-tuple-element.67), channel_id=1, source_target_pairs={{0,8},{8,16},{16,24},{24,0},{1,9},{9,17},{17,25},{25,1},{2,10},{10... | collective-permute-start | bytes 786440 | tf_op jit(solution)/shard_map/ppermute | solution.py:546
  16.2 1.0 %copy-start.8 = (f32[512,128]{1,0:T(8,128)S(1)}, f32[512,128]{1,0:T(8,128)}, u32[]{:S(2)}) copy-start(f32[512,128]{1,0:T(8,128)} %get-tuple-element.68) | copy-start | bytes 786436
  17.2 24.0 %collective-permute-start.5 = (f32[512,128]{1,0:T(8,128)S(1)}, f32[512,128]{1,0:T(8,128)S(1)}, u32[]{:S(2)}, u32[]{:S(2)}) collective-permute-start(f32[512,128]{1,0:T(8,128)S(1)} %copy-done.8), channel_id=1, source_target_pairs={{0,16},{8,24},{16,0},{24,8},{1,17},{9,25},{17,1},{25,9},{2,18},{10... | collective-permute-start | bytes 786440 | tf_op jit(solution)/shard_map/ppermute | solution.py:546
  17.5 2.2 %copy-start.7 = (f32[512,128]{1,0:T(8,128)S(1)}, f32[512,128]{1,0:T(8,128)}, u32[]{:S(2)}) copy-start(f32[512,128]{1,0:T(8,128)} %get-tuple-element.69) | copy-start | bytes 786436
  17.5 5.0 %copy-start.5 = (f32[336,128]{1,0:T(8,128)S(1)}, f32[336,128]{1,0:T(8,128)}, u32[]{:S(2)}) copy-start(f32[336,128]{1,0:T(8,128)} %get-tuple-element.60.refs_1_) | copy-start | bytes 516100
  19.8 21.4 %collective-permute-start.6 = (f32[512,128]{1,0:T(8,128)S(1)}, f32[512,128]{1,0:T(8,128)S(1)}, u32[]{:S(2)}, u32[]{:S(2)}) collective-permute-start(f32[512,128]{1,0:T(8,128)S(1)} %copy-done.7), channel_id=1, source_target_pairs={{0,24},{8,0},{16,8},{24,16},{1,25},{9,1},{17,9},{25,17},{2,26},{10... | collective-permute-start | bytes 786440 | tf_op jit(solution)/shard_map/ppermute | solution.py:546
  23.0 23.4 %copy-start.4 = (f32[512,128]{1,0:T(8,128)S(1)}, f32[512,128]{1,0:T(8,128)}, u32[]{:S(2)}) copy-start(f32[512,128]{1,0:T(8,128)} %get-tuple-element.78.refs_0_) | copy-start | bytes 786436
  23.1 25.2 %collective-permute-start.8 = (f32[160,128]{1,0:T(8,128)S(1)}, f32[160,128]{1,0:T(8,128)S(1)}, u32[]{:S(2)}, u32[]{:S(2)}) collective-permute-start(f32[160,128]{1,0:T(8,128)S(1)} %bitcast.47), channel_id=1, source_target_pairs={{0,8},{8,16},{16,24},{24,25},{25,17},{17,9},{9,1},{1,2},{2,10},{10... | collective-permute-start | bytes 245768 | tf_op jit(solution)/shard_map/ppermute | solution.py:565
  36.7 11.5 %collective-permute-start.3 = (f32[176,128]{1,0:T(8,128)S(1)}, f32[176,128]{1,0:T(8,128)S(1)}, u32[]{:S(2)}, u32[]{:S(2)}) collective-permute-start(f32[176,128]{1,0:T(8,128)S(1)} %pad_maximum_fusion.3), channel_id=1, source_target_pairs={{8,0},{16,8},{24,16},{25,24},{17,25},{9,17},{1,9},{2,1},{10,2},{18... | collective-permute-start | bytes 270344 | tf_op jit(solution)/shard_map/ppermute | solution.py:565
  41.2 13.2 %collective-permute-start.11 = (f32[256,128]{1,0:T(8,128)S(1)}, f32[256,128]{1,0:T(8,128)S(1)}, u32[]{:S(2)}, u32[]{:S(2)}) collective-permute-start(f32[256,128]{1,0:T(8,128)S(1)} %get-tuple-element.86), channel_id=1, source_target_pairs={{0,16},{8,24},{16,0},{24,8},{1,17},{9,25},{17,1},{25,9},{2,18},{10... | collective-permute-start | bytes 393224 | tf_op jit(solution)/shard_map/ppermute | solution.py:546
  48.3 6.1 %collective-permute-start.9 = (f32[256,128]{1,0:T(8,128)S(1)}, f32[256,128]{1,0:T(8,128)S(1)}, u32[]{:S(2)}, u32[]{:S(2)}) collective-permute-start(f32[256,128]{1,0:T(8,128)S(1)} %bitcast.42), channel_id=1, source_target_pairs={{0,8},{8,16},{16,24},{24,25},{25,17},{17,9},{9,1},{1,2},{2,10},{10... | collective-permute-start | bytes 393224 | tf_op jit(solution)/shard_map/ppermute | solution.py:565
  51.8 5.0 %collective-permute-start.10 = (f32[256,128]{1,0:T(8,128)S(1)}, f32[256,128]{1,0:T(8,128)S(1)}, u32[]{:S(2)}, u32[]{:S(2)}) collective-permute-start(f32[256,128]{1,0:T(8,128)S(1)} %bitcast.41), channel_id=1, source_target_pairs={{8,0},{16,8},{24,16},{25,24},{17,25},{9,17},{1,9},{2,1},{10,2},{18... | collective-permute-start | bytes 393224 | tf_op jit(solution)/shard_map/ppermute | solution.py:565
  56.8 12.1 %collective-permute-start.12 = (f32[264,128]{1,0:T(8,128)S(1)}, f32[264,128]{1,0:T(8,128)S(1)}, u32[]{:S(2)}, u32[]{:S(2)}) collective-permute-start(f32[264,128]{1,0:T(8,128)S(1)} %pad_maximum_fusion), channel_id=1, source_target_pairs={{4,0},{0,4},{5,1},{1,5},{6,2},{2,6},{7,3},{3,7},{12,8},{8,12},{13,... | collective-permute-start | bytes 405512 | tf_op jit(solution)/shard_map/ppermute | solution.py:560
  58.4 10.6 %collective-permute-start.13 = (f32[256,128]{1,0:T(8,128)S(1)}, f32[256,128]{1,0:T(8,128)S(1)}, u32[]{:S(2)}, u32[]{:S(2)}) collective-permute-start(f32[256,128]{1,0:T(8,128)S(1)} %get-tuple-element.97), channel_id=1, source_target_pairs={{0,8},{8,16},{16,24},{24,0},{1,9},{9,17},{17,25},{25,1},{2,10},{10... | collective-permute-start | bytes 393224 | tf_op jit(solution)/shard_map/ppermute | solution.py:546
  59.1 9.8 %collective-permute-start.14 = (f32[256,128]{1,0:T(8,128)S(1)}, f32[256,128]{1,0:T(8,128)S(1)}, u32[]{:S(2)}, u32[]{:S(2)}) collective-permute-start(f32[256,128]{1,0:T(8,128)S(1)} %get-tuple-element.99), channel_id=1, source_target_pairs={{0,24},{8,0},{16,8},{24,16},{1,25},{9,1},{17,9},{25,17},{2,26},{10... | collective-permute-start | bytes 393224 | tf_op jit(solution)/shard_map/ppermute | solution.py:546
  65.1 8.3 %collective-permute-start.17 = (f32[256,128]{1,0:T(8,128)S(1)}, f32[256,128]{1,0:T(8,128)S(1)}, u32[]{:S(2)}, u32[]{:S(2)}) collective-permute-start(f32[256,128]{1,0:T(8,128)S(1)} %get-tuple-element.104), channel_id=1, source_target_pairs={{0,8},{8,16},{16,24},{24,0},{1,9},{9,17},{17,25},{25,1},{2,10},{10... | collective-permute-start | bytes 393224 | tf_op jit(solution)/shard_map/ppermute | solution.py:546
  65.1 8.2 %collective-permute-start.18 = (f32[256,128]{1,0:T(8,128)S(1)}, f32[256,128]{1,0:T(8,128)S(1)}, u32[]{:S(2)}, u32[]{:S(2)}) collective-permute-start(f32[256,128]{1,0:T(8,128)S(1)} %get-tuple-element.105), channel_id=1, source_target_pairs={{0,24},{8,0},{16,8},{24,16},{1,25},{9,1},{17,9},{25,17},{2,26},{10... | collective-permute-start | bytes 393224 | tf_op jit(solution)/shard_map/ppermute | solution.py:546
  69.5 4.9 %collective-permute-start.16 = (f32[168,128]{1,0:T(8,128)S(1)}, f32[168,128]{1,0:T(8,128)S(1)}, u32[]{:S(2)}, u32[]{:S(2)}) collective-permute-start(f32[168,128]{1,0:T(8,128)S(1)} %pad_maximum_fusion.6), channel_id=1, source_target_pairs={{8,0},{16,8},{24,16},{25,24},{17,25},{9,17},{1,9},{2,1},{10,2},{18... | collective-permute-start | bytes 258056 | tf_op jit(solution)/shard_map/ppermute | solution.py:565
  69.6 4.8 %collective-permute-start.15 = (f32[160,128]{1,0:T(8,128)S(1)}, f32[160,128]{1,0:T(8,128)S(1)}, u32[]{:S(2)}, u32[]{:S(2)}) collective-permute-start(f32[160,128]{1,0:T(8,128)S(1)} %pad_maximum_fusion.7), channel_id=1, source_target_pairs={{0,8},{8,16},{16,24},{24,25},{25,17},{17,9},{9,1},{1,2},{2,10},{10... | collective-permute-start | bytes 245768 | tf_op jit(solution)/shard_map/ppermute | solution.py:565
  71.6 14.1 %collective-permute-start.22 = (f32[256,128]{1,0:T(8,128)S(1)}, f32[256,128]{1,0:T(8,128)S(1)}, u32[]{:S(2)}, u32[]{:S(2)}) collective-permute-start(f32[256,128]{1,0:T(8,128)S(1)} %get-tuple-element.113), channel_id=1, source_target_pairs={{0,16},{8,24},{16,0},{24,8},{1,17},{9,25},{17,1},{25,9},{2,18},{10... | collective-permute-start | bytes 393224 | tf_op jit(solution)/shard_map/ppermute | solution.py:546
  74.4 11.2 %copy-start = (f32[2,16,64,128]{3,2,1,0:T(8,128)S(1)}, f32[2,16,64,128]{3,2,1,0:T(8,128)}, u32[]{:S(2)}) copy-start(f32[2,16,64,128]{3,2,1,0:T(8,128)} %gain.2) | copy-start | bytes 3145732
  74.5 11.2 %copy-start.1 = (s32[16,64,128]{2,1,0:T(8,128)S(1)}, s32[16,64,128]{2,1,0:T(8,128)}, u32[]{:S(2)}) copy-start(s32[16,64,128]{2,1,0:T(8,128)} %mask.5) | copy-start | bytes 1572868
  77.5 9.6 %collective-permute-start.19 = (f32[256,128]{1,0:T(8,128)S(1)}, f32[256,128]{1,0:T(8,128)S(1)}, u32[]{:S(2)}, u32[]{:S(2)}) collective-permute-start(f32[256,128]{1,0:T(8,128)S(1)} %get-tuple-element.109), channel_id=1, source_target_pairs={{0,8},{8,16},{16,24},{24,0},{1,9},{9,17},{17,25},{25,1},{2,10},{10... | collective-permute-start | bytes 393224 | tf_op jit(solution)/shard_map/ppermute | solution.py:546
  80.7 10.0 %collective-permute-start.20 = (f32[256,128]{1,0:T(8,128)S(1)}, f32[256,128]{1,0:T(8,128)S(1)}, u32[]{:S(2)}, u32[]{:S(2)}) collective-permute-start(f32[256,128]{1,0:T(8,128)S(1)} %get-tuple-element.110), channel_id=1, source_target_pairs={{0,16},{8,24},{16,0},{24,8},{1,17},{9,25},{17,1},{25,9},{2,18},{10... | collective-permute-start | bytes 393224 | tf_op jit(solution)/shard_map/ppermute | solution.py:546
  82.8 7.9 %collective-permute-start.21 = (f32[256,128]{1,0:T(8,128)S(1)}, f32[256,128]{1,0:T(8,128)S(1)}, u32[]{:S(2)}, u32[]{:S(2)}) collective-permute-start(f32[256,128]{1,0:T(8,128)S(1)} %get-tuple-element.111), channel_id=1, source_target_pairs={{0,24},{8,0},{16,8},{24,16},{1,25},{9,1},{17,9},{25,17},{2,26},{10... | collective-permute-start | bytes 393224 | tf_op jit(solution)/shard_map/ppermute | solution.py:546

commit v16 on v15

--- a/solution.py
+++ b/solution.py
@@ -265,7 +265,7 @@
                 out[a * rows + i] = z[a * width:(a + 1) * width]
         return carry
 
-    lax.fori_loop(0, rows // 2, two, 0, unroll=2)
+    lax.fori_loop(0, rows // 2, two, 0, unroll=rows // 2)
 
 
 def adjoint_mix(matrix, depths, parts, length, width):
@@ -418,7 +418,11 @@
                 return after, flux
 
             v = src[n, begin]
-            lax.fori_loop(begin, stop, one, (v, wi[n, begin - 1] * (v - src[n, begin - 1])), unroll=2)
+            carry = v, wi[n, begin - 1] * (v - src[n, begin - 1])
+            whole = (stop - begin) // 4 * 4
+            carry = lax.fori_loop(begin, begin + whole, one, carry, unroll=4)
+            for r in range(begin + whole, stop):
+                carry = one(r, carry)
         src, dst = dst, src
 
     groups = len(outs)
@@ -443,7 +447,7 @@
                 out[pl.ds(i, count, rows), :] = y[d * count:(d + 1) * count, k * cols:(k + 1) * cols]
         return carry
 
-    lax.fori_loop(0, rows // 2, mix, 0, unroll=2)
+    lax.fori_loop(0, rows // 2, mix, 0, unroll=rows // 2)
 
 
 def spread_mix(windows, matrix, depths, field, weights, groups):

time: 92.4 us -> 91.1 us (0.986)
  Pallas kernels: 20.2 us -> 18.8 us
  transfers between devices with their start and end apart: 23 -> 23, of which waited for: 6 -> 7; matrix products, arithmetic and copies ran while one was open for 0% -> 0% of each run, Pallas kernels for 17% -> 15%
where the time goes in v16:
time: 91.1 us; the launch traced here: 90.9 us
  starting transfers between devices  55 us (60%)
  Pallas kernels  18.8 us (21%)
  waiting for transfers between devices  15.3 us (17%)
  local copies, waits for them, and re-layouts  1.24 us (1%)
    ppermute x15, starting transfers between devices, shift(): lax.ppermute(x, 'lev', [(k, (k + d) % devices) for k in range(devices)])  32.6 us
    ppermute x3, starting transfers between devices, halo_j(): lax.ppermute(last, ('lev', 'gy'), ahead)  19.2 us
    ppermute x15, waiting for transfers between devices, shift(): lax.ppermute(x, 'lev', [(k, (k + d) % devices) for k in range(devices)])  12.5 us
    pallas_call x2, Pallas kernels, weight_messages(): pl.pallas_call(functools.partial(pack_kernel, pieces, len(mask)), in_spec...  5.63 us
    pallas_call x2, Pallas kernels, spread_mix(): pl.pallas_call(kernel, in_specs=[vmem()] * (1 + len(arrays)), out_specs=[...  5.36 us
    pallas_call x1, Pallas kernels, scaled_messages(): pl.pallas_call(scaled_kernel, in_specs=[pl.BlockSpec(memory_space=pl.ANY)...  3.25 us
    ppermute x2, starting transfers between devices, halo_i(): both = lax.ppermute(jnp.concatenate([first, last], axis=0), 'gx', up)  3.12 us
    pallas_call x2, Pallas kernels, result(): pl.pallas_call(kernel, in_specs=[vmem()] * (2 + groups) + [anywhere] * le...  2.86 us
  transfers between devices with their start and end apart: 23, of which 7 were waited for; matrix products, arithmetic and copies ran while one was open for 0% of the time, Pallas kernels for 15%

profile of v16, /device:TPU:0, one launch (start us, length us, event | category | flops | bytes accessed | tf_op | source)
XLA Modules:
  0.0 90.9 jit_solution(6594369949818417522)
XLA Ops:
  0.0 3.5 %weight_messages.2 = (f32[336,128]{1,0:T(8,128)}, f32[336,128]{1,0:T(8,128)}, f32[336,128]{1,0:T(8,128)}, f32[336,128]{1,0:T(8,128)}) custom-call(f32[16,64,128]{2,1,0:T(8,128)} %along_i.3, f32[16,64,128]{2,1,0:T(8,128)} %along_j.3, s32[16,64,128]{2,1,0:T(8,128)} %mask.5), custom_call_target="tpu_custom_call" | custom-call | tf_op jit(solution)/shard_map/weight_messages/pallas_call | solution.py:210
  3.5 3.1 %collective-permute-start = (f32[336,128]{1,0:T(8,128)}, f32[336,128]{1,0:T(8,128)S(1)}, u32[]{:S(2)}, u32[]{:S(2)}) collective-permute-start(f32[336,128]{1,0:T(8,128)} %get-tuple-element.61), channel_id=1, source_target_pairs={{0,8},{8,16},{16,24},{24,0},{1,9},{9,17},{17,25},{25,1},{2,10},{10... | collective-permute-start | bytes 516104 | tf_op jit(solution)/shard_map/ppermute | solution.py:550
  6.5 2.6 %collective-permute-start.1 = (f32[336,128]{1,0:T(8,128)}, f32[336,128]{1,0:T(8,128)S(1)}, u32[]{:S(2)}, u32[]{:S(2)}) collective-permute-start(f32[336,128]{1,0:T(8,128)} %get-tuple-element.62), channel_id=1, source_target_pairs={{0,16},{8,24},{16,0},{24,8},{1,17},{9,25},{17,1},{25,9},{2,18},{10... | collective-permute-start | bytes 516104 | tf_op jit(solution)/shard_map/ppermute | solution.py:550
  9.1 1.3 %collective-permute-start.2 = (f32[336,128]{1,0:T(8,128)}, f32[336,128]{1,0:T(8,128)S(1)}, u32[]{:S(2)}, u32[]{:S(2)}) collective-permute-start(f32[336,128]{1,0:T(8,128)} %get-tuple-element.63), channel_id=1, source_target_pairs={{0,24},{8,0},{16,8},{24,16},{1,25},{9,1},{17,9},{25,17},{2,26},{10... | collective-permute-start | bytes 516104 | tf_op jit(solution)/shard_map/ppermute | solution.py:550
  10.5 0.0 copy-done.3
  10.5 1.6 %collective-permute-start.7 = (f32[256,128]{1,0:T(8,128)S(1)}, f32[256,128]{1,0:T(8,128)S(1)}, u32[]{:S(2)}, u32[]{:S(2)}) collective-permute-start(f32[256,128]{1,0:T(8,128)S(1)} %pad_maximum_fusion.1), channel_id=1, source_target_pairs={{4,0},{0,4},{5,1},{1,5},{6,2},{2,6},{7,3},{3,7},{12,8},{8,12},{13,... | collective-permute-start | bytes 393224 | tf_op jit(solution)/shard_map/ppermute | solution.py:564
  12.1 3.3 %scaled_messages.1 = (f32[512,128]{1,0:T(8,128)}, f32[512,128]{1,0:T(8,128)}, f32[512,128]{1,0:T(8,128)}, f32[512,128]{1,0:T(8,128)}) custom-call(f32[2,16,64,128]{3,2,1,0:T(8,128)} %increment, f32[2,16,64,128]{3,2,1,0:T(8,128)} %gain.2, s32[16,64,128]{2,1,0:T(8,128)} %mask.5), custom_call_target="tpu_custom_call" | custom-call | tf_op jit(solution)/shard_map/scaled_messages/pallas_call | solution.py:121
  15.4 0.0 copy-start.6
  15.4 0.7 collective-permute-start.4
  16.1 0.1 copy-done.6
  16.3 0.1 copy.13.matrix
  16.4 0.0 collective-permute-done.7
  16.4 0.8 copy-done.8
  17.2 0.3 collective-permute-start.5
  17.6 2.2 %weight_messages.3 = (f32[256,128]{1,0:T(8,128)S(1)}, f32[256,128]{1,0:T(8,128)S(1)}, f32[256,128]{1,0:T(8,128)S(1)}, f32[256,128]{1,0:T(8,128)S(1)}) custom-call(f32[16,64,128]{2,1,0:T(8,128)S(1)} %copy-done.2, f32[16,64,128]{2,1,0:T(8,128)S(1)} %copy-done.3, f32[128,128]{1,0:T(8,128)S(1)} %get-tuple-element.72.refs_0_, ...), custom_call_target="tpu_custom_call" | custom-call | tf_op jit(solution)/shard_map/weight_messages/pallas_call | solution.py:210
  19.7 0.0 collective-permute-done.refs_2_
  19.8 2.8 %collective-permute-start.6 = (f32[512,128]{1,0:T(8,128)S(1)}, f32[512,128]{1,0:T(8,128)S(1)}, u32[]{:S(2)}, u32[]{:S(2)}) collective-permute-start(f32[512,128]{1,0:T(8,128)S(1)} %copy-done.7), channel_id=1, source_target_pairs={{0,24},{8,0},{16,8},{24,16},{1,25},{9,1},{17,9},{25,17},{2,26},{10... | collective-permute-start | bytes 786440 | tf_op jit(solution)/shard_map/ppermute | solution.py:550
  22.5 0.0 collective-permute-done.1.refs_3_
  22.5 0.0 collective-permute-done.2.refs_4_
  22.6 0.4 turn_weights.2.refs_5_.refs_10_
  23.0 0.0 copy-start.4
  23.1 13.6 %collective-permute-start.8 = (f32[160,128]{1,0:T(8,128)S(1)}, f32[160,128]{1,0:T(8,128)S(1)}, u32[]{:S(2)}, u32[]{:S(2)}) collective-permute-start(f32[160,128]{1,0:T(8,128)S(1)} %bitcast.47), channel_id=1, source_target_pairs={{0,8},{8,16},{16,24},{24,25},{25,17},{17,9},{9,1},{1,2},{2,10},{10... | collective-permute-start | bytes 245768 | tf_op jit(solution)/shard_map/ppermute | solution.py:569
  36.7 0.0 collective-permute-start.3
  36.7 0.0 collective-permute-done.4.refs_1_
  36.7 4.5 %collective-permute-done.5.refs_2_ = f32[512,128]{1,0:T(8,128)S(1)} collective-permute-done((f32[512,128]{1,0:T(8,128)S(1)}, f32[512,128]{1,0:T(8,128)S(1)}, u32[]{:S(2)}, u32[]{:S(2)}) %collective-permute-start.5) | collective-permute-done | bytes 262176 | tf_op jit(solution)/shard_map/ppermute | solution.py:550
  41.2 0.0 collective-permute-done.6.refs_3_
  41.2 5.2 %collective-permute-start.11 = (f32[256,128]{1,0:T(8,128)S(1)}, f32[256,128]{1,0:T(8,128)S(1)}, u32[]{:S(2)}, u32[]{:S(2)}) collective-permute-start(f32[256,128]{1,0:T(8,128)S(1)} %get-tuple-element.86), channel_id=1, source_target_pairs={{0,16},{8,24},{16,0},{24,8},{1,17},{9,25},{17,1},{25,9},{2,18},{10... | collective-permute-start | bytes 393224 | tf_op jit(solution)/shard_map/ppermute | solution.py:550
  46.4 0.9 %adjoint_mix.1.refs_2_.refs_4_ = f32[64,32,128]{2,1,0:T(8,128)S(1)} custom-call(f32[128,128]{1,0:T(8,128)S(1)} %copy.13.matrix, f32[16,128]{1,0:T(8,128)S(1)} %slice_add_fusion.refs_0_.depths, f32[512,128]{1,0:T(8,128)S(1)} %copy-done.4, f32[512,128]{1,0:T(8,128)S(1)} %collective-permute-done.4.refs_1_, f32[512,128]{1,0:T(8,128)S(1)} %collective-permute-done.5.refs_2_, ...), custom_call_target="tpu_custom_call" | custom-call | tf_op jit(solution)/shard_map/adjoint_mix/pallas_call | solution.py:272
  47.3 0.0 collective-permute-done.3
  47.4 0.0 collective-permute-done.8.refs_6_.refs_11_
  47.4 3.6 %collective-permute-start.9 = (f32[256,128]{1,0:T(8,128)S(1)}, f32[256,128]{1,0:T(8,128)S(1)}, u32[]{:S(2)}, u32[]{:S(2)}) collective-permute-start(f32[256,128]{1,0:T(8,128)S(1)} %bitcast.42), channel_id=1, source_target_pairs={{0,8},{8,16},{16,24},{24,25},{25,17},{17,9},{9,1},{1,2},{2,10},{10... | collective-permute-start | bytes 393224 | tf_op jit(solution)/shard_map/ppermute | solution.py:569
  51.0 0.0 collective-permute-start.10
  51.0 3.4 %collective-permute-done.11.refs_4_ = f32[256,128]{1,0:T(8,128)S(1)} collective-permute-done((f32[256,128]{1,0:T(8,128)S(1)}, f32[256,128]{1,0:T(8,128)S(1)}, u32[]{:S(2)}, u32[]{:S(2)}) %collective-permute-start.11) | collective-permute-done | bytes 131104 | tf_op jit(solution)/shard_map/ppermute | solution.py:550
  54.4 0.0 collective-permute-done.9.refs_3_.refs_5_
  54.4 1.6 %collective-permute-done.10.refs_4_.refs_6_ = f32[256,128]{1,0:T(8,128)S(1)} collective-permute-done((f32[256,128]{1,0:T(8,128)S(1)}, f32[256,128]{1,0:T(8,128)S(1)}, u32[]{:S(2)}, u32[]{:S(2)}) %collective-permute-start.10) | collective-permute-done | bytes 131104 | tf_op jit(solution)/shard_map/ppermute | solution.py:569
  55.9 1.6 %collective-permute-start.12 = (f32[264,128]{1,0:T(8,128)S(1)}, f32[264,128]{1,0:T(8,128)S(1)}, u32[]{:S(2)}, u32[]{:S(2)}) collective-permute-start(f32[264,128]{1,0:T(8,128)S(1)} %pad_maximum_fusion), channel_id=1, source_target_pairs={{4,0},{0,4},{5,1},{1,5},{6,2},{2,6},{7,3},{3,7},{12,8},{8,12},{13,... | collective-permute-start | bytes 405512 | tf_op jit(solution)/shard_map/ppermute | solution.py:564
  57.5 1.6 %collective-permute-start.13 = (f32[256,128]{1,0:T(8,128)S(1)}, f32[256,128]{1,0:T(8,128)S(1)}, u32[]{:S(2)}, u32[]{:S(2)}) collective-permute-start(f32[256,128]{1,0:T(8,128)S(1)} %get-tuple-element.97), channel_id=1, source_target_pairs={{0,8},{8,16},{16,24},{24,0},{1,9},{9,17},{17,25},{25,1},{2,10},{10... | collective-permute-start | bytes 393224 | tf_op jit(solution)/shard_map/ppermute | solution.py:550
  59.1 2.2 %collective-permute-start.14 = (f32[256,128]{1,0:T(8,128)S(1)}, f32[256,128]{1,0:T(8,128)S(1)}, u32[]{:S(2)}, u32[]{:S(2)}) collective-permute-start(f32[256,128]{1,0:T(8,128)S(1)} %get-tuple-element.99), channel_id=1, source_target_pairs={{0,24},{8,0},{16,8},{24,16},{1,25},{9,1},{17,9},{25,17},{2,26},{10... | collective-permute-start | bytes 393224 | tf_op jit(solution)/shard_map/ppermute | solution.py:550
  61.3 2.6 %spread_mix.2 = (f32[256,128]{1,0:T(8,128)S(1)}, f32[256,128]{1,0:T(8,128)S(1)}, f32[256,128]{1,0:T(8,128)S(1)}, f32[256,128]{1,0:T(8,128)S(1)}) custom-call(f32[128,128]{1,0:T(8,128)S(1)} %get-tuple-element.141.matrix, f32[16,128]{1,0:T(8,128)S(1)} %slice_add_fusion.refs_0_.depths, f32[16,128]{1,0:T(8,128)S(1)} %split.44.refs_1_, ...), custom_call_target="tpu_custom_call" | custom-call | tf_op jit(solution)/shard_map/spread_mix/pallas_call | solution.py:464
  63.9 0.1 collective-permute-start.17
  64.0 3.8 %collective-permute-start.18 = (f32[256,128]{1,0:T(8,128)S(1)}, f32[256,128]{1,0:T(8,128)S(1)}, u32[]{:S(2)}, u32[]{:S(2)}) collective-permute-start(f32[256,128]{1,0:T(8,128)S(1)} %get-tuple-element.105), channel_id=1, source_target_pairs={{0,24},{8,0},{16,8},{24,16},{1,25},{9,1},{17,9},{25,17},{2,26},{10... | collective-permute-start | bytes 393224 | tf_op jit(solution)/shard_map/ppermute | solution.py:550
  67.8 0.0 collective-permute-done.13.refs_3_
  67.8 0.0 collective-permute-done.14.refs_5_
  67.8 0.0 collective-permute-done.12
  67.9 0.4 turn_weights.3.refs_13_
  68.4 0.1 collective-permute-start.16
  68.5 2.0 %collective-permute-start.15 = (f32[160,128]{1,0:T(8,128)S(1)}, f32[160,128]{1,0:T(8,128)S(1)}, u32[]{:S(2)}, u32[]{:S(2)}) collective-permute-start(f32[160,128]{1,0:T(8,128)S(1)} %pad_maximum_fusion.7), channel_id=1, source_target_pairs={{0,8},{8,16},{16,24},{24,25},{25,17},{17,9},{9,1},{1,2},{2,10},{10... | collective-permute-start | bytes 245768 | tf_op jit(solution)/shard_map/ppermute | solution.py:569
  70.5 1.1 %collective-permute-start.22 = (f32[256,128]{1,0:T(8,128)S(1)}, f32[256,128]{1,0:T(8,128)S(1)}, u32[]{:S(2)}, u32[]{:S(2)}) collective-permute-start(f32[256,128]{1,0:T(8,128)S(1)} %get-tuple-element.113), channel_id=1, source_target_pairs={{0,16},{8,24},{16,0},{24,8},{1,17},{9,25},{17,1},{25,9},{2,18},{10... | collective-permute-start | bytes 393224 | tf_op jit(solution)/shard_map/ppermute | solution.py:550
  71.5 0.0 collective-permute-done.17.refs_1_
  71.6 1.4 %collective-permute-done.18.refs_3_ = f32[256,128]{1,0:T(8,128)S(1)} collective-permute-done((f32[256,128]{1,0:T(8,128)S(1)}, f32[256,128]{1,0:T(8,128)S(1)}, u32[]{:S(2)}, u32[]{:S(2)}) %collective-permute-start.18) | collective-permute-done | bytes 131104 | tf_op jit(solution)/shard_map/ppermute | solution.py:550
  73.0 0.3 collective-permute-done.15
  73.3 0.9 %collective-permute-done.16 = f32[168,128]{1,0:T(8,128)S(1)} collective-permute-done((f32[168,128]{1,0:T(8,128)S(1)}, f32[168,128]{1,0:T(8,128)S(1)}, u32[]{:S(2)}, u32[]{:S(2)}) %collective-permute-start.16) | collective-permute-done | bytes 86048 | tf_op jit(solution)/shard_map/ppermute | solution.py:569
  74.3 0.0 copy-start
  74.3 0.0 copy-start.1
  74.3 2.8 %spread_mix.3 = (f32[256,128]{1,0:T(8,128)S(1)}, f32[256,128]{1,0:T(8,128)S(1)}, f32[256,128]{1,0:T(8,128)S(1)}, f32[256,128]{1,0:T(8,128)S(1)}) custom-call(f32[128,128]{1,0:T(8,128)S(1)} %get-tuple-element.141.matrix, f32[16,128]{1,0:T(8,128)S(1)} %slice_add_fusion.refs_0_.depths, f32[16,128]{1,0:T(8,128)S(1)} %split.44.refs_1_, ...), custom_call_target="tpu_custom_call" | custom-call | tf_op jit(solution)/shard_map/spread_mix/pallas_call | solution.py:464
  77.1 3.0 %collective-permute-start.19 = (f32[256,128]{1,0:T(8,128)S(1)}, f32[256,128]{1,0:T(8,128)S(1)}, u32[]{:S(2)}, u32[]{:S(2)}) collective-permute-start(f32[256,128]{1,0:T(8,128)S(1)} %get-tuple-element.109), channel_id=1, source_target_pairs={{0,8},{8,16},{16,24},{24,0},{1,9},{9,17},{17,25},{25,1},{2,10},{10... | collective-permute-start | bytes 393224 | tf_op jit(solution)/shard_map/ppermute | solution.py:550
  80.1 2.0 %collective-permute-start.20 = (f32[256,128]{1,0:T(8,128)S(1)}, f32[256,128]{1,0:T(8,128)S(1)}, u32[]{:S(2)}, u32[]{:S(2)}) collective-permute-start(f32[256,128]{1,0:T(8,128)S(1)} %get-tuple-element.110), channel_id=1, source_target_pairs={{0,16},{8,24},{16,0},{24,8},{1,17},{9,25},{17,1},{25,9},{2,18},{10... | collective-permute-start | bytes 393224 | tf_op jit(solution)/shard_map/ppermute | solution.py:550
  82.0 2.8 %collective-permute-start.21 = (f32[256,128]{1,0:T(8,128)S(1)}, f32[256,128]{1,0:T(8,128)S(1)}, u32[]{:S(2)}, u32[]{:S(2)}) collective-permute-start(f32[256,128]{1,0:T(8,128)S(1)} %get-tuple-element.111), channel_id=1, source_target_pairs={{0,24},{8,0},{16,8},{24,16},{1,25},{9,1},{17,9},{25,17},{2,26},{10... | collective-permute-start | bytes 393224 | tf_op jit(solution)/shard_map/ppermute | solution.py:550
  84.9 0.0 collective-permute-done.22.refs_2_
  84.9 1.4 %result.2.refs_4_ = f32[2,16,64,128]{3,2,1,0:T(8,128)} custom-call(f32[2,16,64,128]{3,2,1,0:T(8,128)S(1)} %copy-done, s32[16,64,128]{2,1,0:T(8,128)S(1)} %copy-done.1, f32[256,128]{1,0:T(8,128)S(1)} %get-tuple-element.95.refs_0_, f32[256,128]{1,0:T(8,128)S(1)} %collective-permute-done.17.refs_1_, f32[256,128]{1,0:T(8,128)S(1)} %collective-permute-done.22.refs_2_, ...), custom_call_target="tpu_custom_call" | custom-call | tf_op jit(solution)/shard_map/result/pallas_call | solution.py:523
  86.3 0.0 collective-permute-done.19.refs_1_
  86.3 3.1 %collective-permute-done.20.refs_2_ = f32[256,128]{1,0:T(8,128)S(1)} collective-permute-done((f32[256,128]{1,0:T(8,128)S(1)}, f32[256,128]{1,0:T(8,128)S(1)}, u32[]{:S(2)}, u32[]{:S(2)}) %collective-permute-start.20) | collective-permute-done | bytes 131104 | tf_op jit(solution)/shard_map/ppermute | solution.py:550
  89.4 0.0 collective-permute-done.21.refs_3_
  89.4 1.4 %result.3 = f32[2,16,64,128]{3,2,1,0:T(8,128)} custom-call(f32[2,16,64,128]{3,2,1,0:T(8,128)S(1)} %copy-done, s32[16,64,128]{2,1,0:T(8,128)S(1)} %copy-done.1, f32[256,128]{1,0:T(8,128)S(1)} %get-tuple-element.108.refs_0_, f32[256,128]{1,0:T(8,128)S(1)} %collective-permute-done.19.refs_1_, ...), custom_call_target="tpu_custom_call", output_to_operand_aliasing={{}: (6, {})} | custom-call | tf_op jit(solution)/shard_map/result/pallas_call | solution.py:523
  (39 shorter events, 0.4 us)
Async XLA Ops:
  0.0 10.5 %copy-start.3 = (f32[16,64,128]{2,1,0:T(8,128)S(1)}, f32[16,64,128]{2,1,0:T(8,128)}, u32[]{:S(2)}) copy-start(f32[16,64,128]{2,1,0:T(8,128)} %along_j.3) | copy-start | bytes 1572868
  0.0 10.5 %copy-start.2 = (f32[16,64,128]{2,1,0:T(8,128)S(1)}, f32[16,64,128]{2,1,0:T(8,128)}, u32[]{:S(2)}) copy-start(f32[16,64,128]{2,1,0:T(8,128)} %along_i.3) | copy-start | bytes 1572868
  3.5 16.3 %collective-permute-start = (f32[336,128]{1,0:T(8,128)}, f32[336,128]{1,0:T(8,128)S(1)}, u32[]{:S(2)}, u32[]{:S(2)}) collective-permute-start(f32[336,128]{1,0:T(8,128)} %get-tuple-element.61), channel_id=1, source_target_pairs={{0,8},{8,16},{16,24},{24,0},{1,9},{9,17},{17,25},{25,1},{2,10},{10... | collective-permute-start | bytes 516104 | tf_op jit(solution)/shard_map/ppermute | solution.py:550
  6.5 16.0 %collective-permute-start.1 = (f32[336,128]{1,0:T(8,128)}, f32[336,128]{1,0:T(8,128)S(1)}, u32[]{:S(2)}, u32[]{:S(2)}) collective-permute-start(f32[336,128]{1,0:T(8,128)} %get-tuple-element.62), channel_id=1, source_target_pairs={{0,16},{8,24},{16,0},{24,8},{1,17},{9,25},{17,1},{25,9},{2,18},{10... | collective-permute-start | bytes 516104 | tf_op jit(solution)/shard_map/ppermute | solution.py:550
  9.1 13.4 %collective-permute-start.2 = (f32[336,128]{1,0:T(8,128)}, f32[336,128]{1,0:T(8,128)S(1)}, u32[]{:S(2)}, u32[]{:S(2)}) collective-permute-start(f32[336,128]{1,0:T(8,128)} %get-tuple-element.63), channel_id=1, source_target_pairs={{0,24},{8,0},{16,8},{24,16},{1,25},{9,1},{17,9},{25,17},{2,26},{10... | collective-permute-start | bytes 516104 | tf_op jit(solution)/shard_map/ppermute | solution.py:550
  10.5 5.9 %collective-permute-start.7 = (f32[256,128]{1,0:T(8,128)S(1)}, f32[256,128]{1,0:T(8,128)S(1)}, u32[]{:S(2)}, u32[]{:S(2)}) collective-permute-start(f32[256,128]{1,0:T(8,128)S(1)} %pad_maximum_fusion.1), channel_id=1, source_target_pairs={{4,0},{0,4},{5,1},{1,5},{6,2},{2,6},{7,3},{3,7},{12,8},{8,12},{13,... | collective-permute-start | bytes 393224 | tf_op jit(solution)/shard_map/ppermute | solution.py:564
  15.4 0.8 copy-start.6
  15.4 21.3 %collective-permute-start.4 = (f32[512,128]{1,0:T(8,128)}, f32[512,128]{1,0:T(8,128)S(1)}, u32[]{:S(2)}, u32[]{:S(2)}) collective-permute-start(f32[512,128]{1,0:T(8,128)} %get-tuple-element.67), channel_id=1, source_target_pairs={{0,8},{8,16},{16,24},{24,0},{1,9},{9,17},{17,25},{25,1},{2,10},{10... | collective-permute-start | bytes 786440 | tf_op jit(solution)/shard_map/ppermute | solution.py:550
  16.2 1.0 %copy-start.8 = (f32[512,128]{1,0:T(8,128)S(1)}, f32[512,128]{1,0:T(8,128)}, u32[]{:S(2)}) copy-start(f32[512,128]{1,0:T(8,128)} %get-tuple-element.68) | copy-start | bytes 786436
  17.2 24.0 %collective-permute-start.5 = (f32[512,128]{1,0:T(8,128)S(1)}, f32[512,128]{1,0:T(8,128)S(1)}, u32[]{:S(2)}, u32[]{:S(2)}) collective-permute-start(f32[512,128]{1,0:T(8,128)S(1)} %copy-done.8), channel_id=1, source_target_pairs={{0,16},{8,24},{16,0},{24,8},{1,17},{9,25},{17,1},{25,9},{2,18},{10... | collective-permute-start | bytes 786440 | tf_op jit(solution)/shard_map/ppermute | solution.py:550
  17.5 2.2 %copy-start.7 = (f32[512,128]{1,0:T(8,128)S(1)}, f32[512,128]{1,0:T(8,128)}, u32[]{:S(2)}) copy-start(f32[512,128]{1,0:T(8,128)} %get-tuple-element.69) | copy-start | bytes 786436
  17.5 5.0 %copy-start.5 = (f32[336,128]{1,0:T(8,128)S(1)}, f32[336,128]{1,0:T(8,128)}, u32[]{:S(2)}) copy-start(f32[336,128]{1,0:T(8,128)} %get-tuple-element.60.refs_1_) | copy-start | bytes 516100
  19.8 21.4 %collective-permute-start.6 = (f32[512,128]{1,0:T(8,128)S(1)}, f32[512,128]{1,0:T(8,128)S(1)}, u32[]{:S(2)}, u32[]{:S(2)}) collective-permute-start(f32[512,128]{1,0:T(8,128)S(1)} %copy-done.7), channel_id=1, source_target_pairs={{0,24},{8,0},{16,8},{24,16},{1,25},{9,1},{17,9},{25,17},{2,26},{10... | collective-permute-start | bytes 786440 | tf_op jit(solution)/shard_map/ppermute | solution.py:550
  23.0 23.4 %copy-start.4 = (f32[512,128]{1,0:T(8,128)S(1)}, f32[512,128]{1,0:T(8,128)}, u32[]{:S(2)}) copy-start(f32[512,128]{1,0:T(8,128)} %get-tuple-element.78.refs_0_) | copy-start | bytes 786436
  23.1 24.3 %collective-permute-start.8 = (f32[160,128]{1,0:T(8,128)S(1)}, f32[160,128]{1,0:T(8,128)S(1)}, u32[]{:S(2)}, u32[]{:S(2)}) collective-permute-start(f32[160,128]{1,0:T(8,128)S(1)} %bitcast.47), channel_id=1, source_target_pairs={{0,8},{8,16},{16,24},{24,25},{25,17},{17,9},{9,1},{1,2},{2,10},{10... | collective-permute-start | bytes 245768 | tf_op jit(solution)/shard_map/ppermute | solution.py:569
  36.7 10.7 %collective-permute-start.3 = (f32[176,128]{1,0:T(8,128)S(1)}, f32[176,128]{1,0:T(8,128)S(1)}, u32[]{:S(2)}, u32[]{:S(2)}) collective-permute-start(f32[176,128]{1,0:T(8,128)S(1)} %pad_maximum_fusion.3), channel_id=1, source_target_pairs={{8,0},{16,8},{24,16},{25,24},{17,25},{9,17},{1,9},{2,1},{10,2},{18... | collective-permute-start | bytes 270344 | tf_op jit(solution)/shard_map/ppermute | solution.py:569
  41.2 13.2 %collective-permute-start.11 = (f32[256,128]{1,0:T(8,128)S(1)}, f32[256,128]{1,0:T(8,128)S(1)}, u32[]{:S(2)}, u32[]{:S(2)}) collective-permute-start(f32[256,128]{1,0:T(8,128)S(1)} %get-tuple-element.86), channel_id=1, source_target_pairs={{0,16},{8,24},{16,0},{24,8},{1,17},{9,25},{17,1},{25,9},{2,18},{10... | collective-permute-start | bytes 393224 | tf_op jit(solution)/shard_map/ppermute | solution.py:550
  47.4 7.0 %collective-permute-start.9 = (f32[256,128]{1,0:T(8,128)S(1)}, f32[256,128]{1,0:T(8,128)S(1)}, u32[]{:S(2)}, u32[]{:S(2)}) collective-permute-start(f32[256,128]{1,0:T(8,128)S(1)} %bitcast.42), channel_id=1, source_target_pairs={{0,8},{8,16},{16,24},{24,25},{25,17},{17,9},{9,1},{1,2},{2,10},{10... | collective-permute-start | bytes 393224 | tf_op jit(solution)/shard_map/ppermute | solution.py:569
  51.0 5.0 %collective-permute-start.10 = (f32[256,128]{1,0:T(8,128)S(1)}, f32[256,128]{1,0:T(8,128)S(1)}, u32[]{:S(2)}, u32[]{:S(2)}) collective-permute-start(f32[256,128]{1,0:T(8,128)S(1)} %bitcast.41), channel_id=1, source_target_pairs={{8,0},{16,8},{24,16},{25,24},{17,25},{9,17},{1,9},{2,1},{10,2},{18... | collective-permute-start | bytes 393224 | tf_op jit(solution)/shard_map/ppermute | solution.py:569
  55.9 11.9 %collective-permute-start.12 = (f32[264,128]{1,0:T(8,128)S(1)}, f32[264,128]{1,0:T(8,128)S(1)}, u32[]{:S(2)}, u32[]{:S(2)}) collective-permute-start(f32[264,128]{1,0:T(8,128)S(1)} %pad_maximum_fusion), channel_id=1, source_target_pairs={{4,0},{0,4},{5,1},{1,5},{6,2},{2,6},{7,3},{3,7},{12,8},{8,12},{13,... | collective-permute-start | bytes 405512 | tf_op jit(solution)/shard_map/ppermute | solution.py:564
  57.5 10.3 %collective-permute-start.13 = (f32[256,128]{1,0:T(8,128)S(1)}, f32[256,128]{1,0:T(8,128)S(1)}, u32[]{:S(2)}, u32[]{:S(2)}) collective-permute-start(f32[256,128]{1,0:T(8,128)S(1)} %get-tuple-element.97), channel_id=1, source_target_pairs={{0,8},{8,16},{16,24},{24,0},{1,9},{9,17},{17,25},{25,1},{2,10},{10... | collective-permute-start | bytes 393224 | tf_op jit(solution)/shard_map/ppermute | solution.py:550
  59.1 8.7 %collective-permute-start.14 = (f32[256,128]{1,0:T(8,128)S(1)}, f32[256,128]{1,0:T(8,128)S(1)}, u32[]{:S(2)}, u32[]{:S(2)}) collective-permute-start(f32[256,128]{1,0:T(8,128)S(1)} %get-tuple-element.99), channel_id=1, source_target_pairs={{0,24},{8,0},{16,8},{24,16},{1,25},{9,1},{17,9},{25,17},{2,26},{10... | collective-permute-start | bytes 393224 | tf_op jit(solution)/shard_map/ppermute | solution.py:550
  63.9 7.6 %collective-permute-start.17 = (f32[256,128]{1,0:T(8,128)S(1)}, f32[256,128]{1,0:T(8,128)S(1)}, u32[]{:S(2)}, u32[]{:S(2)}) collective-permute-start(f32[256,128]{1,0:T(8,128)S(1)} %get-tuple-element.104), channel_id=1, source_target_pairs={{0,8},{8,16},{16,24},{24,0},{1,9},{9,17},{17,25},{25,1},{2,10},{10... | collective-permute-start | bytes 393224 | tf_op jit(solution)/shard_map/ppermute | solution.py:550
  64.0 9.0 %collective-permute-start.18 = (f32[256,128]{1,0:T(8,128)S(1)}, f32[256,128]{1,0:T(8,128)S(1)}, u32[]{:S(2)}, u32[]{:S(2)}) collective-permute-start(f32[256,128]{1,0:T(8,128)S(1)} %get-tuple-element.105), channel_id=1, source_target_pairs={{0,24},{8,0},{16,8},{24,16},{1,25},{9,1},{17,9},{25,17},{2,26},{10... | collective-permute-start | bytes 393224 | tf_op jit(solution)/shard_map/ppermute | solution.py:550
  68.4 5.8 %collective-permute-start.16 = (f32[168,128]{1,0:T(8,128)S(1)}, f32[168,128]{1,0:T(8,128)S(1)}, u32[]{:S(2)}, u32[]{:S(2)}) collective-permute-start(f32[168,128]{1,0:T(8,128)S(1)} %pad_maximum_fusion.6), channel_id=1, source_target_pairs={{8,0},{16,8},{24,16},{25,24},{17,25},{9,17},{1,9},{2,1},{10,2},{18... | collective-permute-start | bytes 258056 | tf_op jit(solution)/shard_map/ppermute | solution.py:569
  68.5 4.8 %collective-permute-start.15 = (f32[160,128]{1,0:T(8,128)S(1)}, f32[160,128]{1,0:T(8,128)S(1)}, u32[]{:S(2)}, u32[]{:S(2)}) collective-permute-start(f32[160,128]{1,0:T(8,128)S(1)} %pad_maximum_fusion.7), channel_id=1, source_target_pairs={{0,8},{8,16},{16,24},{24,25},{25,17},{17,9},{9,1},{1,2},{2,10},{10... | collective-permute-start | bytes 245768 | tf_op jit(solution)/shard_map/ppermute | solution.py:569
  70.5 14.4 %collective-permute-start.22 = (f32[256,128]{1,0:T(8,128)S(1)}, f32[256,128]{1,0:T(8,128)S(1)}, u32[]{:S(2)}, u32[]{:S(2)}) collective-permute-start(f32[256,128]{1,0:T(8,128)S(1)} %get-tuple-element.113), channel_id=1, source_target_pairs={{0,16},{8,24},{16,0},{24,8},{1,17},{9,25},{17,1},{25,9},{2,18},{10... | collective-permute-start | bytes 393224 | tf_op jit(solution)/shard_map/ppermute | solution.py:550
  74.3 10.6 %copy-start = (f32[2,16,64,128]{3,2,1,0:T(8,128)S(1)}, f32[2,16,64,128]{3,2,1,0:T(8,128)}, u32[]{:S(2)}) copy-start(f32[2,16,64,128]{3,2,1,0:T(8,128)} %gain.2) | copy-start | bytes 3145732
  74.3 10.6 %copy-start.1 = (s32[16,64,128]{2,1,0:T(8,128)S(1)}, s32[16,64,128]{2,1,0:T(8,128)}, u32[]{:S(2)}) copy-start(s32[16,64,128]{2,1,0:T(8,128)} %mask.5) | copy-start | bytes 1572868
  77.1 9.3 %collective-permute-start.19 = (f32[256,128]{1,0:T(8,128)S(1)}, f32[256,128]{1,0:T(8,128)S(1)}, u32[]{:S(2)}, u32[]{:S(2)}) collective-permute-start(f32[256,128]{1,0:T(8,128)S(1)} %get-tuple-element.109), channel_id=1, source_target_pairs={{0,8},{8,16},{16,24},{24,0},{1,9},{9,17},{17,25},{25,1},{2,10},{10... | collective-permute-start | bytes 393224 | tf_op jit(solution)/shard_map/ppermute | solution.py:550
  80.1 9.4 %collective-permute-start.20 = (f32[256,128]{1,0:T(8,128)S(1)}, f32[256,128]{1,0:T(8,128)S(1)}, u32[]{:S(2)}, u32[]{:S(2)}) collective-permute-start(f32[256,128]{1,0:T(8,128)S(1)} %get-tuple-element.110), channel_id=1, source_target_pairs={{0,16},{8,24},{16,0},{24,8},{1,17},{9,25},{17,1},{25,9},{2,18},{10... | collective-permute-start | bytes 393224 | tf_op jit(solution)/shard_map/ppermute | solution.py:550
  82.0 7.4 %collective-permute-start.21 = (f32[256,128]{1,0:T(8,128)S(1)}, f32[256,128]{1,0:T(8,128)S(1)}, u32[]{:S(2)}, u32[]{:S(2)}) collective-permute-start(f32[256,128]{1,0:T(8,128)S(1)} %get-tuple-element.111), channel_id=1, source_target_pairs={{0,24},{8,0},{16,8},{24,16},{1,25},{9,1},{17,9},{25,17},{2,26},{10... | collective-permute-start | bytes 393224 | tf_op jit(solution)/shard_map/ppermute | solution.py:550

commit v17 on v16

--- a/solution.py
+++ b/solution.py
@@ -419,8 +419,8 @@
 
             v = src[n, begin]
             carry = v, wi[n, begin - 1] * (v - src[n, begin - 1])
-            whole = (stop - begin) // 4 * 4
-            carry = lax.fori_loop(begin, begin + whole, one, carry, unroll=4)
+            whole = (stop - begin) // 8 * 8
+            carry = lax.fori_loop(begin, begin + whole, one, carry, unroll=8)
             for r in range(begin + whole, stop):
                 carry = one(r, carry)
         src, dst = dst, src

time: 91.1 us -> 91.1 us (level)
  no operation moved by 1% of the time
where the time goes in v17:
time: 91.1 us; the launch traced here: 90.9 us
  starting transfers between devices  55.2 us (61%)
  Pallas kernels  18.7 us (21%)
  waiting for transfers between devices  15.3 us (17%)
  local copies, waits for them, and re-layouts  1.24 us (1%)
    ppermute x15, starting transfers between devices, shift(): lax.ppermute(x, 'lev', [(k, (k + d) % devices) for k in range(devices)])  32.8 us
    ppermute x3, starting transfers between devices, halo_j(): lax.ppermute(last, ('lev', 'gy'), ahead)  19.2 us
    ppermute x15, waiting for transfers between devices, shift(): lax.ppermute(x, 'lev', [(k, (k + d) % devices) for k in range(devices)])  12.4 us
    pallas_call x2, Pallas kernels, weight_messages(): pl.pallas_call(functools.partial(pack_kernel, pieces, len(mask)), in_spec...  5.63 us
    pallas_call x2, Pallas kernels, spread_mix(): pl.pallas_call(kernel, in_specs=[vmem()] * (1 + len(arrays)), out_specs=[...  5.22 us
    pallas_call x1, Pallas kernels, scaled_messages(): pl.pallas_call(scaled_kernel, in_specs=[pl.BlockSpec(memory_space=pl.ANY)...  3.25 us
    ppermute x2, starting transfers between devices, halo_i(): both = lax.ppermute(jnp.concatenate([first, last], axis=0), 'gx', up)  3.12 us
    pallas_call x2, Pallas kernels, result(): pl.pallas_call(kernel, in_specs=[vmem()] * (2 + groups) + [anywhere] * le...  2.86 us
  transfers between devices with their start and end apart: 23, of which 7 were waited for; matrix products, arithmetic and copies ran while one was open for 0% of the time, Pallas kernels for 15%

profile of v17, /device:TPU:0, one launch (start us, length us, event | category | flops | bytes accessed | tf_op | source)
XLA Modules:
  0.0 90.9 jit_solution(6885574921857121802)
XLA Ops:
  0.0 3.5 %weight_messages.2 = (f32[336,128]{1,0:T(8,128)}, f32[336,128]{1,0:T(8,128)}, f32[336,128]{1,0:T(8,128)}, f32[336,128]{1,0:T(8,128)}) custom-call(f32[16,64,128]{2,1,0:T(8,128)} %along_i.3, f32[16,64,128]{2,1,0:T(8,128)} %along_j.3, s32[16,64,128]{2,1,0:T(8,128)} %mask.5), custom_call_target="tpu_custom_call" | custom-call | tf_op jit(solution)/shard_map/weight_messages/pallas_call | solution.py:210
  3.5 3.1 %collective-permute-start = (f32[336,128]{1,0:T(8,128)}, f32[336,128]{1,0:T(8,128)S(1)}, u32[]{:S(2)}, u32[]{:S(2)}) collective-permute-start(f32[336,128]{1,0:T(8,128)} %get-tuple-element.61), channel_id=1, source_target_pairs={{0,8},{8,16},{16,24},{24,0},{1,9},{9,17},{17,25},{25,1},{2,10},{10... | collective-permute-start | bytes 516104 | tf_op jit(solution)/shard_map/ppermute | solution.py:550
  6.5 2.6 %collective-permute-start.1 = (f32[336,128]{1,0:T(8,128)}, f32[336,128]{1,0:T(8,128)S(1)}, u32[]{:S(2)}, u32[]{:S(2)}) collective-permute-start(f32[336,128]{1,0:T(8,128)} %get-tuple-element.62), channel_id=1, source_target_pairs={{0,16},{8,24},{16,0},{24,8},{1,17},{9,25},{17,1},{25,9},{2,18},{10... | collective-permute-start | bytes 516104 | tf_op jit(solution)/shard_map/ppermute | solution.py:550
  9.1 1.3 %collective-permute-start.2 = (f32[336,128]{1,0:T(8,128)}, f32[336,128]{1,0:T(8,128)S(1)}, u32[]{:S(2)}, u32[]{:S(2)}) collective-permute-start(f32[336,128]{1,0:T(8,128)} %get-tuple-element.63), channel_id=1, source_target_pairs={{0,24},{8,0},{16,8},{24,16},{1,25},{9,1},{17,9},{25,17},{2,26},{10... | collective-permute-start | bytes 516104 | tf_op jit(solution)/shard_map/ppermute | solution.py:550
  10.5 0.0 copy-done.3
  10.5 1.6 %collective-permute-start.7 = (f32[256,128]{1,0:T(8,128)S(1)}, f32[256,128]{1,0:T(8,128)S(1)}, u32[]{:S(2)}, u32[]{:S(2)}) collective-permute-start(f32[256,128]{1,0:T(8,128)S(1)} %pad_maximum_fusion.1), channel_id=1, source_target_pairs={{4,0},{0,4},{5,1},{1,5},{6,2},{2,6},{7,3},{3,7},{12,8},{8,12},{13,... | collective-permute-start | bytes 393224 | tf_op jit(solution)/shard_map/ppermute | solution.py:564
  12.1 3.3 %scaled_messages.1 = (f32[512,128]{1,0:T(8,128)}, f32[512,128]{1,0:T(8,128)}, f32[512,128]{1,0:T(8,128)}, f32[512,128]{1,0:T(8,128)}) custom-call(f32[2,16,64,128]{3,2,1,0:T(8,128)} %increment, f32[2,16,64,128]{3,2,1,0:T(8,128)} %gain.2, s32[16,64,128]{2,1,0:T(8,128)} %mask.5), custom_call_target="tpu_custom_call" | custom-call | tf_op jit(solution)/shard_map/scaled_messages/pallas_call | solution.py:121
  15.4 0.0 copy-start.6
  15.4 0.7 collective-permute-start.4
  16.1 0.1 copy-done.6
  16.3 0.1 copy.13.matrix
  16.4 0.0 collective-permute-done.7
  16.4 0.8 copy-done.8
  17.2 0.3 collective-permute-start.5
  17.6 2.2 %weight_messages.3 = (f32[256,128]{1,0:T(8,128)S(1)}, f32[256,128]{1,0:T(8,128)S(1)}, f32[256,128]{1,0:T(8,128)S(1)}, f32[256,128]{1,0:T(8,128)S(1)}) custom-call(f32[16,64,128]{2,1,0:T(8,128)S(1)} %copy-done.2, f32[16,64,128]{2,1,0:T(8,128)S(1)} %copy-done.3, f32[128,128]{1,0:T(8,128)S(1)} %get-tuple-element.72.refs_0_, ...), custom_call_target="tpu_custom_call" | custom-call | tf_op jit(solution)/shard_map/weight_messages/pallas_call | solution.py:210
  19.7 0.0 collective-permute-done.refs_2_
  19.8 2.8 %collective-permute-start.6 = (f32[512,128]{1,0:T(8,128)S(1)}, f32[512,128]{1,0:T(8,128)S(1)}, u32[]{:S(2)}, u32[]{:S(2)}) collective-permute-start(f32[512,128]{1,0:T(8,128)S(1)} %copy-done.7), channel_id=1, source_target_pairs={{0,24},{8,0},{16,8},{24,16},{1,25},{9,1},{17,9},{25,17},{2,26},{10... | collective-permute-start | bytes 786440 | tf_op jit(solution)/shard_map/ppermute | solution.py:550
  22.5 0.0 collective-permute-done.1.refs_3_
  22.5 0.0 collective-permute-done.2.refs_4_
  22.6 0.4 turn_weights.2.refs_5_.refs_10_
  23.0 0.0 copy-start.4
  23.1 13.6 %collective-permute-start.8 = (f32[160,128]{1,0:T(8,128)S(1)}, f32[160,128]{1,0:T(8,128)S(1)}, u32[]{:S(2)}, u32[]{:S(2)}) collective-permute-start(f32[160,128]{1,0:T(8,128)S(1)} %bitcast.47), channel_id=1, source_target_pairs={{0,8},{8,16},{16,24},{24,25},{25,17},{17,9},{9,1},{1,2},{2,10},{10... | collective-permute-start | bytes 245768 | tf_op jit(solution)/shard_map/ppermute | solution.py:569
  36.7 0.0 collective-permute-start.3
  36.7 0.0 collective-permute-done.4.refs_1_
  36.7 4.5 %collective-permute-done.5.refs_2_ = f32[512,128]{1,0:T(8,128)S(1)} collective-permute-done((f32[512,128]{1,0:T(8,128)S(1)}, f32[512,128]{1,0:T(8,128)S(1)}, u32[]{:S(2)}, u32[]{:S(2)}) %collective-permute-start.5) | collective-permute-done | bytes 262176 | tf_op jit(solution)/shard_map/ppermute | solution.py:550
  41.2 0.0 collective-permute-done.6.refs_3_
  41.2 5.2 %collective-permute-start.11 = (f32[256,128]{1,0:T(8,128)S(1)}, f32[256,128]{1,0:T(8,128)S(1)}, u32[]{:S(2)}, u32[]{:S(2)}) collective-permute-start(f32[256,128]{1,0:T(8,128)S(1)} %get-tuple-element.86), channel_id=1, source_target_pairs={{0,16},{8,24},{16,0},{24,8},{1,17},{9,25},{17,1},{25,9},{2,18},{10... | collective-permute-start | bytes 393224 | tf_op jit(solution)/shard_map/ppermute | solution.py:550
  46.4 0.9 %adjoint_mix.1.refs_2_.refs_4_ = f32[64,32,128]{2,1,0:T(8,128)S(1)} custom-call(f32[128,128]{1,0:T(8,128)S(1)} %copy.13.matrix, f32[16,128]{1,0:T(8,128)S(1)} %slice_add_fusion.refs_0_.depths, f32[512,128]{1,0:T(8,128)S(1)} %copy-done.4, f32[512,128]{1,0:T(8,128)S(1)} %collective-permute-done.4.refs_1_, f32[512,128]{1,0:T(8,128)S(1)} %collective-permute-done.5.refs_2_, ...), custom_call_target="tpu_custom_call" | custom-call | tf_op jit(solution)/shard_map/adjoint_mix/pallas_call | solution.py:272
  47.3 0.0 collective-permute-done.3
  47.4 0.0 collective-permute-done.8.refs_6_.refs_11_
  47.4 3.6 %collective-permute-start.9 = (f32[256,128]{1,0:T(8,128)S(1)}, f32[256,128]{1,0:T(8,128)S(1)}, u32[]{:S(2)}, u32[]{:S(2)}) collective-permute-start(f32[256,128]{1,0:T(8,128)S(1)} %bitcast.42), channel_id=1, source_target_pairs={{0,8},{8,16},{16,24},{24,25},{25,17},{17,9},{9,1},{1,2},{2,10},{10... | collective-permute-start | bytes 393224 | tf_op jit(solution)/shard_map/ppermute | solution.py:569
  51.0 0.0 collective-permute-start.10
  51.0 3.4 %collective-permute-done.11.refs_4_ = f32[256,128]{1,0:T(8,128)S(1)} collective-permute-done((f32[256,128]{1,0:T(8,128)S(1)}, f32[256,128]{1,0:T(8,128)S(1)}, u32[]{:S(2)}, u32[]{:S(2)}) %collective-permute-start.11) | collective-permute-done | bytes 131104 | tf_op jit(solution)/shard_map/ppermute | solution.py:550
  54.4 0.0 collective-permute-done.9.refs_3_.refs_5_
  54.4 1.6 %collective-permute-done.10.refs_4_.refs_6_ = f32[256,128]{1,0:T(8,128)S(1)} collective-permute-done((f32[256,128]{1,0:T(8,128)S(1)}, f32[256,128]{1,0:T(8,128)S(1)}, u32[]{:S(2)}, u32[]{:S(2)}) %collective-permute-start.10) | collective-permute-done | bytes 131104 | tf_op jit(solution)/shard_map/ppermute | solution.py:569
  55.9 1.6 %collective-permute-start.12 = (f32[264,128]{1,0:T(8,128)S(1)}, f32[264,128]{1,0:T(8,128)S(1)}, u32[]{:S(2)}, u32[]{:S(2)}) collective-permute-start(f32[264,128]{1,0:T(8,128)S(1)} %pad_maximum_fusion), channel_id=1, source_target_pairs={{4,0},{0,4},{5,1},{1,5},{6,2},{2,6},{7,3},{3,7},{12,8},{8,12},{13,... | collective-permute-start | bytes 405512 | tf_op jit(solution)/shard_map/ppermute | solution.py:564
  57.5 1.6 %collective-permute-start.13 = (f32[256,128]{1,0:T(8,128)S(1)}, f32[256,128]{1,0:T(8,128)S(1)}, u32[]{:S(2)}, u32[]{:S(2)}) collective-permute-start(f32[256,128]{1,0:T(8,128)S(1)} %get-tuple-element.97), channel_id=1, source_target_pairs={{0,8},{8,16},{16,24},{24,0},{1,9},{9,17},{17,25},{25,1},{2,10},{10... | collective-permute-start | bytes 393224 | tf_op jit(solution)/shard_map/ppermute | solution.py:550
  59.1 2.2 %collective-permute-start.14 = (f32[256,128]{1,0:T(8,128)S(1)}, f32[256,128]{1,0:T(8,128)S(1)}, u32[]{:S(2)}, u32[]{:S(2)}) collective-permute-start(f32[256,128]{1,0:T(8,128)S(1)} %get-tuple-element.99), channel_id=1, source_target_pairs={{0,24},{8,0},{16,8},{24,16},{1,25},{9,1},{17,9},{25,17},{2,26},{10... | collective-permute-start | bytes 393224 | tf_op jit(solution)/shard_map/ppermute | solution.py:550
  61.3 2.5 %spread_mix.2 = (f32[256,128]{1,0:T(8,128)S(1)}, f32[256,128]{1,0:T(8,128)S(1)}, f32[256,128]{1,0:T(8,128)S(1)}, f32[256,128]{1,0:T(8,128)S(1)}) custom-call(f32[128,128]{1,0:T(8,128)S(1)} %get-tuple-element.141.matrix, f32[16,128]{1,0:T(8,128)S(1)} %slice_add_fusion.refs_0_.depths, f32[16,128]{1,0:T(8,128)S(1)} %split.44.refs_1_, ...), custom_call_target="tpu_custom_call" | custom-call | tf_op jit(solution)/shard_map/spread_mix/pallas_call | solution.py:464
  63.9 0.1 collective-permute-start.17
  63.9 3.8 %collective-permute-start.18 = (f32[256,128]{1,0:T(8,128)S(1)}, f32[256,128]{1,0:T(8,128)S(1)}, u32[]{:S(2)}, u32[]{:S(2)}) collective-permute-start(f32[256,128]{1,0:T(8,128)S(1)} %get-tuple-element.105), channel_id=1, source_target_pairs={{0,24},{8,0},{16,8},{24,16},{1,25},{9,1},{17,9},{25,17},{2,26},{10... | collective-permute-start | bytes 393224 | tf_op jit(solution)/shard_map/ppermute | solution.py:550
  67.7 0.0 collective-permute-done.13.refs_3_
  67.7 0.0 collective-permute-done.14.refs_5_
  67.7 0.0 collective-permute-done.12
  67.8 0.4 turn_weights.3.refs_13_
  68.3 0.1 collective-permute-start.16
  68.4 2.0 %collective-permute-start.15 = (f32[160,128]{1,0:T(8,128)S(1)}, f32[160,128]{1,0:T(8,128)S(1)}, u32[]{:S(2)}, u32[]{:S(2)}) collective-permute-start(f32[160,128]{1,0:T(8,128)S(1)} %pad_maximum_fusion.7), channel_id=1, source_target_pairs={{0,8},{8,16},{16,24},{24,25},{25,17},{17,9},{9,1},{1,2},{2,10},{10... | collective-permute-start | bytes 245768 | tf_op jit(solution)/shard_map/ppermute | solution.py:569
  70.4 1.2 %collective-permute-start.22 = (f32[256,128]{1,0:T(8,128)S(1)}, f32[256,128]{1,0:T(8,128)S(1)}, u32[]{:S(2)}, u32[]{:S(2)}) collective-permute-start(f32[256,128]{1,0:T(8,128)S(1)} %get-tuple-element.113), channel_id=1, source_target_pairs={{0,16},{8,24},{16,0},{24,8},{1,17},{9,25},{17,1},{25,9},{2,18},{10... | collective-permute-start | bytes 393224 | tf_op jit(solution)/shard_map/ppermute | solution.py:550
  71.5 0.0 collective-permute-done.17.refs_1_
  71.5 1.4 %collective-permute-done.18.refs_3_ = f32[256,128]{1,0:T(8,128)S(1)} collective-permute-done((f32[256,128]{1,0:T(8,128)S(1)}, f32[256,128]{1,0:T(8,128)S(1)}, u32[]{:S(2)}, u32[]{:S(2)}) %collective-permute-start.18) | collective-permute-done | bytes 131104 | tf_op jit(solution)/shard_map/ppermute | solution.py:550
  72.9 0.3 collective-permute-done.15
  73.2 1.0 %collective-permute-done.16 = f32[168,128]{1,0:T(8,128)S(1)} collective-permute-done((f32[168,128]{1,0:T(8,128)S(1)}, f32[168,128]{1,0:T(8,128)S(1)}, u32[]{:S(2)}, u32[]{:S(2)}) %collective-permute-start.16) | collective-permute-done | bytes 86048 | tf_op jit(solution)/shard_map/ppermute | solution.py:569
  74.2 0.0 copy-start
  74.2 0.0 copy-start.1
  74.3 2.7 %spread_mix.3 = (f32[256,128]{1,0:T(8,128)S(1)}, f32[256,128]{1,0:T(8,128)S(1)}, f32[256,128]{1,0:T(8,128)S(1)}, f32[256,128]{1,0:T(8,128)S(1)}) custom-call(f32[128,128]{1,0:T(8,128)S(1)} %get-tuple-element.141.matrix, f32[16,128]{1,0:T(8,128)S(1)} %slice_add_fusion.refs_0_.depths, f32[16,128]{1,0:T(8,128)S(1)} %split.44.refs_1_, ...), custom_call_target="tpu_custom_call" | custom-call | tf_op jit(solution)/shard_map/spread_mix/pallas_call | solution.py:464
  77.0 3.1 %collective-permute-start.19 = (f32[256,128]{1,0:T(8,128)S(1)}, f32[256,128]{1,0:T(8,128)S(1)}, u32[]{:S(2)}, u32[]{:S(2)}) collective-permute-start(f32[256,128]{1,0:T(8,128)S(1)} %get-tuple-element.109), channel_id=1, source_target_pairs={{0,8},{8,16},{16,24},{24,0},{1,9},{9,17},{17,25},{25,1},{2,10},{10... | collective-permute-start | bytes 393224 | tf_op jit(solution)/shard_map/ppermute | solution.py:550
  80.0 2.0 %collective-permute-start.20 = (f32[256,128]{1,0:T(8,128)S(1)}, f32[256,128]{1,0:T(8,128)S(1)}, u32[]{:S(2)}, u32[]{:S(2)}) collective-permute-start(f32[256,128]{1,0:T(8,128)S(1)} %get-tuple-element.110), channel_id=1, source_target_pairs={{0,16},{8,24},{16,0},{24,8},{1,17},{9,25},{17,1},{25,9},{2,18},{10... | collective-permute-start | bytes 393224 | tf_op jit(solution)/shard_map/ppermute | solution.py:550
  82.0 2.8 %collective-permute-start.21 = (f32[256,128]{1,0:T(8,128)S(1)}, f32[256,128]{1,0:T(8,128)S(1)}, u32[]{:S(2)}, u32[]{:S(2)}) collective-permute-start(f32[256,128]{1,0:T(8,128)S(1)} %get-tuple-element.111), channel_id=1, source_target_pairs={{0,24},{8,0},{16,8},{24,16},{1,25},{9,1},{17,9},{25,17},{2,26},{10... | collective-permute-start | bytes 393224 | tf_op jit(solution)/shard_map/ppermute | solution.py:550
  84.9 0.0 collective-permute-done.22.refs_2_
  84.9 1.4 %result.2.refs_4_ = f32[2,16,64,128]{3,2,1,0:T(8,128)} custom-call(f32[2,16,64,128]{3,2,1,0:T(8,128)S(1)} %copy-done, s32[16,64,128]{2,1,0:T(8,128)S(1)} %copy-done.1, f32[256,128]{1,0:T(8,128)S(1)} %get-tuple-element.95.refs_0_, f32[256,128]{1,0:T(8,128)S(1)} %collective-permute-done.17.refs_1_, f32[256,128]{1,0:T(8,128)S(1)} %collective-permute-done.22.refs_2_, ...), custom_call_target="tpu_custom_call" | custom-call | tf_op jit(solution)/shard_map/result/pallas_call | solution.py:523
  86.3 0.0 collective-permute-done.19.refs_1_
  86.3 3.1 %collective-permute-done.20.refs_2_ = f32[256,128]{1,0:T(8,128)S(1)} collective-permute-done((f32[256,128]{1,0:T(8,128)S(1)}, f32[256,128]{1,0:T(8,128)S(1)}, u32[]{:S(2)}, u32[]{:S(2)}) %collective-permute-start.20) | collective-permute-done | bytes 131104 | tf_op jit(solution)/shard_map/ppermute | solution.py:550
  89.4 0.0 collective-permute-done.21.refs_3_
  89.4 1.4 %result.3 = f32[2,16,64,128]{3,2,1,0:T(8,128)} custom-call(f32[2,16,64,128]{3,2,1,0:T(8,128)S(1)} %copy-done, s32[16,64,128]{2,1,0:T(8,128)S(1)} %copy-done.1, f32[256,128]{1,0:T(8,128)S(1)} %get-tuple-element.108.refs_0_, f32[256,128]{1,0:T(8,128)S(1)} %collective-permute-done.19.refs_1_, ...), custom_call_target="tpu_custom_call", output_to_operand_aliasing={{}: (6, {})} | custom-call | tf_op jit(solution)/shard_map/result/pallas_call | solution.py:523
  (39 shorter events, 0.4 us)
Async XLA Ops:
  0.0 10.5 %copy-start.3 = (f32[16,64,128]{2,1,0:T(8,128)S(1)}, f32[16,64,128]{2,1,0:T(8,128)}, u32[]{:S(2)}) copy-start(f32[16,64,128]{2,1,0:T(8,128)} %along_j.3) | copy-start | bytes 1572868
  0.0 10.5 %copy-start.2 = (f32[16,64,128]{2,1,0:T(8,128)S(1)}, f32[16,64,128]{2,1,0:T(8,128)}, u32[]{:S(2)}) copy-start(f32[16,64,128]{2,1,0:T(8,128)} %along_i.3) | copy-start | bytes 1572868
  3.5 16.3 %collective-permute-start = (f32[336,128]{1,0:T(8,128)}, f32[336,128]{1,0:T(8,128)S(1)}, u32[]{:S(2)}, u32[]{:S(2)}) collective-permute-start(f32[336,128]{1,0:T(8,128)} %get-tuple-element.61), channel_id=1, source_target_pairs={{0,8},{8,16},{16,24},{24,0},{1,9},{9,17},{17,25},{25,1},{2,10},{10... | collective-permute-start | bytes 516104 | tf_op jit(solution)/shard_map/ppermute | solution.py:550
  6.5 16.0 %collective-permute-start.1 = (f32[336,128]{1,0:T(8,128)}, f32[336,128]{1,0:T(8,128)S(1)}, u32[]{:S(2)}, u32[]{:S(2)}) collective-permute-start(f32[336,128]{1,0:T(8,128)} %get-tuple-element.62), channel_id=1, source_target_pairs={{0,16},{8,24},{16,0},{24,8},{1,17},{9,25},{17,1},{25,9},{2,18},{10... | collective-permute-start | bytes 516104 | tf_op jit(solution)/shard_map/ppermute | solution.py:550
  9.1 13.4 %collective-permute-start.2 = (f32[336,128]{1,0:T(8,128)}, f32[336,128]{1,0:T(8,128)S(1)}, u32[]{:S(2)}, u32[]{:S(2)}) collective-permute-start(f32[336,128]{1,0:T(8,128)} %get-tuple-element.63), channel_id=1, source_target_pairs={{0,24},{8,0},{16,8},{24,16},{1,25},{9,1},{17,9},{25,17},{2,26},{10... | collective-permute-start | bytes 516104 | tf_op jit(solution)/shard_map/ppermute | solution.py:550
  10.5 5.9 %collective-permute-start.7 = (f32[256,128]{1,0:T(8,128)S(1)}, f32[256,128]{1,0:T(8,128)S(1)}, u32[]{:S(2)}, u32[]{:S(2)}) collective-permute-start(f32[256,128]{1,0:T(8,128)S(1)} %pad_maximum_fusion.1), channel_id=1, source_target_pairs={{4,0},{0,4},{5,1},{1,5},{6,2},{2,6},{7,3},{3,7},{12,8},{8,12},{13,... | collective-permute-start | bytes 393224 | tf_op jit(solution)/shard_map/ppermute | solution.py:564
  15.4 0.8 copy-start.6
  15.4 21.3 %collective-permute-start.4 = (f32[512,128]{1,0:T(8,128)}, f32[512,128]{1,0:T(8,128)S(1)}, u32[]{:S(2)}, u32[]{:S(2)}) collective-permute-start(f32[512,128]{1,0:T(8,128)} %get-tuple-element.67), channel_id=1, source_target_pairs={{0,8},{8,16},{16,24},{24,0},{1,9},{9,17},{17,25},{25,1},{2,10},{10... | collective-permute-start | bytes 786440 | tf_op jit(solution)/shard_map/ppermute | solution.py:550
  16.2 1.0 %copy-start.8 = (f32[512,128]{1,0:T(8,128)S(1)}, f32[512,128]{1,0:T(8,128)}, u32[]{:S(2)}) copy-start(f32[512,128]{1,0:T(8,128)} %get-tuple-element.68) | copy-start | bytes 786436
  17.2 24.0 %collective-permute-start.5 = (f32[512,128]{1,0:T(8,128)S(1)}, f32[512,128]{1,0:T(8,128)S(1)}, u32[]{:S(2)}, u32[]{:S(2)}) collective-permute-start(f32[512,128]{1,0:T(8,128)S(1)} %copy-done.8), channel_id=1, source_target_pairs={{0,16},{8,24},{16,0},{24,8},{1,17},{9,25},{17,1},{25,9},{2,18},{10... | collective-permute-start | bytes 786440 | tf_op jit(solution)/shard_map/ppermute | solution.py:550
  17.5 2.2 %copy-start.7 = (f32[512,128]{1,0:T(8,128)S(1)}, f32[512,128]{1,0:T(8,128)}, u32[]{:S(2)}) copy-start(f32[512,128]{1,0:T(8,128)} %get-tuple-element.69) | copy-start | bytes 786436
  17.5 5.0 %copy-start.5 = (f32[336,128]{1,0:T(8,128)S(1)}, f32[336,128]{1,0:T(8,128)}, u32[]{:S(2)}) copy-start(f32[336,128]{1,0:T(8,128)} %get-tuple-element.60.refs_1_) | copy-start | bytes 516100
  19.8 21.4 %collective-permute-start.6 = (f32[512,128]{1,0:T(8,128)S(1)}, f32[512,128]{1,0:T(8,128)S(1)}, u32[]{:S(2)}, u32[]{:S(2)}) collective-permute-start(f32[512,128]{1,0:T(8,128)S(1)} %copy-done.7), channel_id=1, source_target_pairs={{0,24},{8,0},{16,8},{24,16},{1,25},{9,1},{17,9},{25,17},{2,26},{10... | collective-permute-start | bytes 786440 | tf_op jit(solution)/shard_map/ppermute | solution.py:550
  23.0 23.4 %copy-start.4 = (f32[512,128]{1,0:T(8,128)S(1)}, f32[512,128]{1,0:T(8,128)}, u32[]{:S(2)}) copy-start(f32[512,128]{1,0:T(8,128)} %get-tuple-element.78.refs_0_) | copy-start | bytes 786436
  23.1 24.3 %collective-permute-start.8 = (f32[160,128]{1,0:T(8,128)S(1)}, f32[160,128]{1,0:T(8,128)S(1)}, u32[]{:S(2)}, u32[]{:S(2)}) collective-permute-start(f32[160,128]{1,0:T(8,128)S(1)} %bitcast.47), channel_id=1, source_target_pairs={{0,8},{8,16},{16,24},{24,25},{25,17},{17,9},{9,1},{1,2},{2,10},{10... | collective-permute-start | bytes 245768 | tf_op jit(solution)/shard_map/ppermute | solution.py:569
  36.7 10.7 %collective-permute-start.3 = (f32[176,128]{1,0:T(8,128)S(1)}, f32[176,128]{1,0:T(8,128)S(1)}, u32[]{:S(2)}, u32[]{:S(2)}) collective-permute-start(f32[176,128]{1,0:T(8,128)S(1)} %pad_maximum_fusion.3), channel_id=1, source_target_pairs={{8,0},{16,8},{24,16},{25,24},{17,25},{9,17},{1,9},{2,1},{10,2},{18... | collective-permute-start | bytes 270344 | tf_op jit(solution)/shard_map/ppermute | solution.py:569
  41.2 13.2 %collective-permute-start.11 = (f32[256,128]{1,0:T(8,128)S(1)}, f32[256,128]{1,0:T(8,128)S(1)}, u32[]{:S(2)}, u32[]{:S(2)}) collective-permute-start(f32[256,128]{1,0:T(8,128)S(1)} %get-tuple-element.86), channel_id=1, source_target_pairs={{0,16},{8,24},{16,0},{24,8},{1,17},{9,25},{17,1},{25,9},{2,18},{10... | collective-permute-start | bytes 393224 | tf_op jit(solution)/shard_map/ppermute | solution.py:550
  47.4 7.0 %collective-permute-start.9 = (f32[256,128]{1,0:T(8,128)S(1)}, f32[256,128]{1,0:T(8,128)S(1)}, u32[]{:S(2)}, u32[]{:S(2)}) collective-permute-start(f32[256,128]{1,0:T(8,128)S(1)} %bitcast.42), channel_id=1, source_target_pairs={{0,8},{8,16},{16,24},{24,25},{25,17},{17,9},{9,1},{1,2},{2,10},{10... | collective-permute-start | bytes 393224 | tf_op jit(solution)/shard_map/ppermute | solution.py:569
  51.0 5.0 %collective-permute-start.10 = (f32[256,128]{1,0:T(8,128)S(1)}, f32[256,128]{1,0:T(8,128)S(1)}, u32[]{:S(2)}, u32[]{:S(2)}) collective-permute-start(f32[256,128]{1,0:T(8,128)S(1)} %bitcast.41), channel_id=1, source_target_pairs={{8,0},{16,8},{24,16},{25,24},{17,25},{9,17},{1,9},{2,1},{10,2},{18... | collective-permute-start | bytes 393224 | tf_op jit(solution)/shard_map/ppermute | solution.py:569
  55.9 11.8 %collective-permute-start.12 = (f32[264,128]{1,0:T(8,128)S(1)}, f32[264,128]{1,0:T(8,128)S(1)}, u32[]{:S(2)}, u32[]{:S(2)}) collective-permute-start(f32[264,128]{1,0:T(8,128)S(1)} %pad_maximum_fusion), channel_id=1, source_target_pairs={{4,0},{0,4},{5,1},{1,5},{6,2},{2,6},{7,3},{3,7},{12,8},{8,12},{13,... | collective-permute-start | bytes 405512 | tf_op jit(solution)/shard_map/ppermute | solution.py:564
  57.5 10.2 %collective-permute-start.13 = (f32[256,128]{1,0:T(8,128)S(1)}, f32[256,128]{1,0:T(8,128)S(1)}, u32[]{:S(2)}, u32[]{:S(2)}) collective-permute-start(f32[256,128]{1,0:T(8,128)S(1)} %get-tuple-element.97), channel_id=1, source_target_pairs={{0,8},{8,16},{16,24},{24,0},{1,9},{9,17},{17,25},{25,1},{2,10},{10... | collective-permute-start | bytes 393224 | tf_op jit(solution)/shard_map/ppermute | solution.py:550
  59.1 8.6 %collective-permute-start.14 = (f32[256,128]{1,0:T(8,128)S(1)}, f32[256,128]{1,0:T(8,128)S(1)}, u32[]{:S(2)}, u32[]{:S(2)}) collective-permute-start(f32[256,128]{1,0:T(8,128)S(1)} %get-tuple-element.99), channel_id=1, source_target_pairs={{0,24},{8,0},{16,8},{24,16},{1,25},{9,1},{17,9},{25,17},{2,26},{10... | collective-permute-start | bytes 393224 | tf_op jit(solution)/shard_map/ppermute | solution.py:550
  63.9 7.7 %collective-permute-start.17 = (f32[256,128]{1,0:T(8,128)S(1)}, f32[256,128]{1,0:T(8,128)S(1)}, u32[]{:S(2)}, u32[]{:S(2)}) collective-permute-start(f32[256,128]{1,0:T(8,128)S(1)} %get-tuple-element.104), channel_id=1, source_target_pairs={{0,8},{8,16},{16,24},{24,0},{1,9},{9,17},{17,25},{25,1},{2,10},{10... | collective-permute-start | bytes 393224 | tf_op jit(solution)/shard_map/ppermute | solution.py:550
  63.9 9.0 %collective-permute-start.18 = (f32[256,128]{1,0:T(8,128)S(1)}, f32[256,128]{1,0:T(8,128)S(1)}, u32[]{:S(2)}, u32[]{:S(2)}) collective-permute-start(f32[256,128]{1,0:T(8,128)S(1)} %get-tuple-element.105), channel_id=1, source_target_pairs={{0,24},{8,0},{16,8},{24,16},{1,25},{9,1},{17,9},{25,17},{2,26},{10... | collective-permute-start | bytes 393224 | tf_op jit(solution)/shard_map/ppermute | solution.py:550
  68.3 5.9 %collective-permute-start.16 = (f32[168,128]{1,0:T(8,128)S(1)}, f32[168,128]{1,0:T(8,128)S(1)}, u32[]{:S(2)}, u32[]{:S(2)}) collective-permute-start(f32[168,128]{1,0:T(8,128)S(1)} %pad_maximum_fusion.6), channel_id=1, source_target_pairs={{8,0},{16,8},{24,16},{25,24},{17,25},{9,17},{1,9},{2,1},{10,2},{18... | collective-permute-start | bytes 258056 | tf_op jit(solution)/shard_map/ppermute | solution.py:569
  68.4 4.8 %collective-permute-start.15 = (f32[160,128]{1,0:T(8,128)S(1)}, f32[160,128]{1,0:T(8,128)S(1)}, u32[]{:S(2)}, u32[]{:S(2)}) collective-permute-start(f32[160,128]{1,0:T(8,128)S(1)} %pad_maximum_fusion.7), channel_id=1, source_target_pairs={{0,8},{8,16},{16,24},{24,25},{25,17},{17,9},{9,1},{1,2},{2,10},{10... | collective-permute-start | bytes 245768 | tf_op jit(solution)/shard_map/ppermute | solution.py:569
  70.4 14.5 %collective-permute-start.22 = (f32[256,128]{1,0:T(8,128)S(1)}, f32[256,128]{1,0:T(8,128)S(1)}, u32[]{:S(2)}, u32[]{:S(2)}) collective-permute-start(f32[256,128]{1,0:T(8,128)S(1)} %get-tuple-element.113), channel_id=1, source_target_pairs={{0,16},{8,24},{16,0},{24,8},{1,17},{9,25},{17,1},{25,9},{2,18},{10... | collective-permute-start | bytes 393224 | tf_op jit(solution)/shard_map/ppermute | solution.py:550
  74.2 10.6 %copy-start = (f32[2,16,64,128]{3,2,1,0:T(8,128)S(1)}, f32[2,16,64,128]{3,2,1,0:T(8,128)}, u32[]{:S(2)}) copy-start(f32[2,16,64,128]{3,2,1,0:T(8,128)} %gain.2) | copy-start | bytes 3145732
  74.2 10.6 %copy-start.1 = (s32[16,64,128]{2,1,0:T(8,128)S(1)}, s32[16,64,128]{2,1,0:T(8,128)}, u32[]{:S(2)}) copy-start(s32[16,64,128]{2,1,0:T(8,128)} %mask.5) | copy-start | bytes 1572868
  77.0 9.3 %collective-permute-start.19 = (f32[256,128]{1,0:T(8,128)S(1)}, f32[256,128]{1,0:T(8,128)S(1)}, u32[]{:S(2)}, u32[]{:S(2)}) collective-permute-start(f32[256,128]{1,0:T(8,128)S(1)} %get-tuple-element.109), channel_id=1, source_target_pairs={{0,8},{8,16},{16,24},{24,0},{1,9},{9,17},{17,25},{25,1},{2,10},{10... | collective-permute-start | bytes 393224 | tf_op jit(solution)/shard_map/ppermute | solution.py:550
  80.0 9.4 %collective-permute-start.20 = (f32[256,128]{1,0:T(8,128)S(1)}, f32[256,128]{1,0:T(8,128)S(1)}, u32[]{:S(2)}, u32[]{:S(2)}) collective-permute-start(f32[256,128]{1,0:T(8,128)S(1)} %get-tuple-element.110), channel_id=1, source_target_pairs={{0,16},{8,24},{16,0},{24,8},{1,17},{9,25},{17,1},{25,9},{2,18},{10... | collective-permute-start | bytes 393224 | tf_op jit(solution)/shard_map/ppermute | solution.py:550
  82.0 7.4 %collective-permute-start.21 = (f32[256,128]{1,0:T(8,128)S(1)}, f32[256,128]{1,0:T(8,128)S(1)}, u32[]{:S(2)}, u32[]{:S(2)}) collective-permute-start(f32[256,128]{1,0:T(8,128)S(1)} %get-tuple-element.111), channel_id=1, source_target_pairs={{0,24},{8,0},{16,8},{24,16},{1,25},{9,1},{17,9},{25,17},{2,26},{10... | collective-permute-start | bytes 393224 | tf_op jit(solution)/shard_map/ppermute | solution.py:550

commit v18 on v17

--- a/solution.py
+++ b/solution.py
@@ -419,8 +419,8 @@
 
             v = src[n, begin]
             carry = v, wi[n, begin - 1] * (v - src[n, begin - 1])
-            whole = (stop - begin) // 8 * 8
-            carry = lax.fori_loop(begin, begin + whole, one, carry, unroll=8)
+            whole = (stop - begin) // 12 * 12
+            carry = lax.fori_loop(begin, begin + whole, one, carry, unroll=12)
             for r in range(begin + whole, stop):
                 carry = one(r, carry)
         src, dst = dst, src

time: 91.1 us -> 90.8 us (level)
  no operation moved by 1% of the time
where the time goes in v18:
time: 90.8 us; the launch traced here: 90.6 us
  starting transfers between devices  55.3 us (61%)
  Pallas kernels  18.2 us (20%)
  waiting for transfers between devices  15.3 us (17%)
  local copies, waits for them, and re-layouts  1.24 us (1%)
    ppermute x15, starting transfers between devices, shift(): lax.ppermute(x, 'lev', [(k, (k + d) % devices) for k in range(devices)])  32.9 us
    ppermute x3, starting transfers between devices, halo_j(): lax.ppermute(last, ('lev', 'gy'), ahead)  19.2 us
    ppermute x15, waiting for transfers between devices, shift(): lax.ppermute(x, 'lev', [(k, (k + d) % devices) for k in range(devices)])  12.4 us
    pallas_call x2, Pallas kernels, weight_messages(): pl.pallas_call(functools.partial(pack_kernel, pieces, len(mask)), in_spec...  5.63 us
    pallas_call x2, Pallas kernels, spread_mix(): pl.pallas_call(kernel, in_specs=[vmem()] * (1 + len(arrays)), out_specs=[...  4.72 us
    pallas_call x1, Pallas kernels, scaled_messages(): pl.pallas_call(scaled_kernel, in_specs=[pl.BlockSpec(memory_space=pl.ANY)...  3.25 us
    ppermute x2, starting transfers between devices, halo_i(): both = lax.ppermute(jnp.concatenate([first, last], axis=0), 'gx', up)  3.12 us
    pallas_call x2, Pallas kernels, result(): pl.pallas_call(kernel, in_specs=[vmem()] * (2 + groups) + [anywhere] * le...  2.86 us
  transfers between devices with their start and end apart: 23, of which 7 were waited for; matrix products, arithmetic and copies ran while one was open for 0% of the time, Pallas kernels for 15%

profile of v18, /device:TPU:0, one launch (start us, length us, event | category | flops | bytes accessed | tf_op | source)
XLA Modules:
  0.0 90.6 jit_solution(4007976954854633023)
XLA Ops:
  0.0 3.5 %weight_messages.2 = (f32[336,128]{1,0:T(8,128)}, f32[336,128]{1,0:T(8,128)}, f32[336,128]{1,0:T(8,128)}, f32[336,128]{1,0:T(8,128)}) custom-call(f32[16,64,128]{2,1,0:T(8,128)} %along_i.3, f32[16,64,128]{2,1,0:T(8,128)} %along_j.3, s32[16,64,128]{2,1,0:T(8,128)} %mask.5), custom_call_target="tpu_custom_call" | custom-call | tf_op jit(solution)/shard_map/weight_messages/pallas_call | solution.py:210
  3.5 3.1 %collective-permute-start = (f32[336,128]{1,0:T(8,128)}, f32[336,128]{1,0:T(8,128)S(1)}, u32[]{:S(2)}, u32[]{:S(2)}) collective-permute-start(f32[336,128]{1,0:T(8,128)} %get-tuple-element.61), channel_id=1, source_target_pairs={{0,8},{8,16},{16,24},{24,0},{1,9},{9,17},{17,25},{25,1},{2,10},{10... | collective-permute-start | bytes 516104 | tf_op jit(solution)/shard_map/ppermute | solution.py:550
  6.5 2.6 %collective-permute-start.1 = (f32[336,128]{1,0:T(8,128)}, f32[336,128]{1,0:T(8,128)S(1)}, u32[]{:S(2)}, u32[]{:S(2)}) collective-permute-start(f32[336,128]{1,0:T(8,128)} %get-tuple-element.62), channel_id=1, source_target_pairs={{0,16},{8,24},{16,0},{24,8},{1,17},{9,25},{17,1},{25,9},{2,18},{10... | collective-permute-start | bytes 516104 | tf_op jit(solution)/shard_map/ppermute | solution.py:550
  9.1 1.3 %collective-permute-start.2 = (f32[336,128]{1,0:T(8,128)}, f32[336,128]{1,0:T(8,128)S(1)}, u32[]{:S(2)}, u32[]{:S(2)}) collective-permute-start(f32[336,128]{1,0:T(8,128)} %get-tuple-element.63), channel_id=1, source_target_pairs={{0,24},{8,0},{16,8},{24,16},{1,25},{9,1},{17,9},{25,17},{2,26},{10... | collective-permute-start | bytes 516104 | tf_op jit(solution)/shard_map/ppermute | solution.py:550
  10.5 0.0 copy-done.2
  10.5 1.6 %collective-permute-start.7 = (f32[256,128]{1,0:T(8,128)S(1)}, f32[256,128]{1,0:T(8,128)S(1)}, u32[]{:S(2)}, u32[]{:S(2)}) collective-permute-start(f32[256,128]{1,0:T(8,128)S(1)} %pad_maximum_fusion.1), channel_id=1, source_target_pairs={{4,0},{0,4},{5,1},{1,5},{6,2},{2,6},{7,3},{3,7},{12,8},{8,12},{13,... | collective-permute-start | bytes 393224 | tf_op jit(solution)/shard_map/ppermute | solution.py:564
  12.1 3.3 %scaled_messages.1 = (f32[512,128]{1,0:T(8,128)}, f32[512,128]{1,0:T(8,128)}, f32[512,128]{1,0:T(8,128)}, f32[512,128]{1,0:T(8,128)}) custom-call(f32[2,16,64,128]{3,2,1,0:T(8,128)} %increment, f32[2,16,64,128]{3,2,1,0:T(8,128)} %gain.2, s32[16,64,128]{2,1,0:T(8,128)} %mask.5), custom_call_target="tpu_custom_call" | custom-call | tf_op jit(solution)/shard_map/scaled_messages/pallas_call | solution.py:121
  15.4 0.0 copy-start.6
  15.4 0.7 collective-permute-start.4
  16.1 0.1 copy-done.6
  16.3 0.1 copy.13.matrix
  16.4 0.0 collective-permute-done.7
  16.4 0.8 copy-done.8
  17.2 0.3 collective-permute-start.5
  17.6 2.2 %weight_messages.3 = (f32[256,128]{1,0:T(8,128)S(1)}, f32[256,128]{1,0:T(8,128)S(1)}, f32[256,128]{1,0:T(8,128)S(1)}, f32[256,128]{1,0:T(8,128)S(1)}) custom-call(f32[16,64,128]{2,1,0:T(8,128)S(1)} %copy-done.2, f32[16,64,128]{2,1,0:T(8,128)S(1)} %copy-done.3, f32[128,128]{1,0:T(8,128)S(1)} %get-tuple-element.72.refs_0_, ...), custom_call_target="tpu_custom_call" | custom-call | tf_op jit(solution)/shard_map/weight_messages/pallas_call | solution.py:210
  19.7 0.0 collective-permute-done.refs_2_
  19.8 2.8 %collective-permute-start.6 = (f32[512,128]{1,0:T(8,128)S(1)}, f32[512,128]{1,0:T(8,128)S(1)}, u32[]{:S(2)}, u32[]{:S(2)}) collective-permute-start(f32[512,128]{1,0:T(8,128)S(1)} %copy-done.7), channel_id=1, source_target_pairs={{0,24},{8,0},{16,8},{24,16},{1,25},{9,1},{17,9},{25,17},{2,26},{10... | collective-permute-start | bytes 786440 | tf_op jit(solution)/shard_map/ppermute | solution.py:550
  22.5 0.0 collective-permute-done.1.refs_3_
  22.5 0.0 collective-permute-done.2.refs_4_
  22.6 0.4 turn_weights.2.refs_5_.refs_10_
  23.0 0.0 copy-start.4
  23.1 13.6 %collective-permute-start.8 = (f32[160,128]{1,0:T(8,128)S(1)}, f32[160,128]{1,0:T(8,128)S(1)}, u32[]{:S(2)}, u32[]{:S(2)}) collective-permute-start(f32[160,128]{1,0:T(8,128)S(1)} %bitcast.47), channel_id=1, source_target_pairs={{0,8},{8,16},{16,24},{24,25},{25,17},{17,9},{9,1},{1,2},{2,10},{10... | collective-permute-start | bytes 245768 | tf_op jit(solution)/shard_map/ppermute | solution.py:569
  36.7 0.0 collective-permute-start.3
  36.7 0.0 collective-permute-done.4.refs_1_
  36.7 4.5 %collective-permute-done.5.refs_2_ = f32[512,128]{1,0:T(8,128)S(1)} collective-permute-done((f32[512,128]{1,0:T(8,128)S(1)}, f32[512,128]{1,0:T(8,128)S(1)}, u32[]{:S(2)}, u32[]{:S(2)}) %collective-permute-start.5) | collective-permute-done | bytes 262176 | tf_op jit(solution)/shard_map/ppermute | solution.py:550
  41.2 0.0 collective-permute-done.6.refs_3_
  41.2 5.2 %collective-permute-start.11 = (f32[256,128]{1,0:T(8,128)S(1)}, f32[256,128]{1,0:T(8,128)S(1)}, u32[]{:S(2)}, u32[]{:S(2)}) collective-permute-start(f32[256,128]{1,0:T(8,128)S(1)} %get-tuple-element.86), channel_id=1, source_target_pairs={{0,16},{8,24},{16,0},{24,8},{1,17},{9,25},{17,1},{25,9},{2,18},{10... | collective-permute-start | bytes 393224 | tf_op jit(solution)/shard_map/ppermute | solution.py:550
  46.4 0.9 %adjoint_mix.1.refs_2_.refs_4_ = f32[64,32,128]{2,1,0:T(8,128)S(1)} custom-call(f32[128,128]{1,0:T(8,128)S(1)} %copy.13.matrix, f32[16,128]{1,0:T(8,128)S(1)} %slice_add_fusion.refs_0_.depths, f32[512,128]{1,0:T(8,128)S(1)} %copy-done.4, f32[512,128]{1,0:T(8,128)S(1)} %collective-permute-done.4.refs_1_, f32[512,128]{1,0:T(8,128)S(1)} %collective-permute-done.5.refs_2_, ...), custom_call_target="tpu_custom_call" | custom-call | tf_op jit(solution)/shard_map/adjoint_mix/pallas_call | solution.py:272
  47.3 0.0 collective-permute-done.3
  47.4 0.0 collective-permute-done.8.refs_6_.refs_11_
  47.4 3.6 %collective-permute-start.9 = (f32[256,128]{1,0:T(8,128)S(1)}, f32[256,128]{1,0:T(8,128)S(1)}, u32[]{:S(2)}, u32[]{:S(2)}) collective-permute-start(f32[256,128]{1,0:T(8,128)S(1)} %bitcast.42), channel_id=1, source_target_pairs={{0,8},{8,16},{16,24},{24,25},{25,17},{17,9},{9,1},{1,2},{2,10},{10... | collective-permute-start | bytes 393224 | tf_op jit(solution)/shard_map/ppermute | solution.py:569
  51.0 0.0 collective-permute-start.10
  51.0 3.4 %collective-permute-done.11.refs_4_ = f32[256,128]{1,0:T(8,128)S(1)} collective-permute-done((f32[256,128]{1,0:T(8,128)S(1)}, f32[256,128]{1,0:T(8,128)S(1)}, u32[]{:S(2)}, u32[]{:S(2)}) %collective-permute-start.11) | collective-permute-done | bytes 131104 | tf_op jit(solution)/shard_map/ppermute | solution.py:550
  54.4 0.0 collective-permute-done.9.refs_3_.refs_5_
  54.4 1.6 %collective-permute-done.10.refs_4_.refs_6_ = f32[256,128]{1,0:T(8,128)S(1)} collective-permute-done((f32[256,128]{1,0:T(8,128)S(1)}, f32[256,128]{1,0:T(8,128)S(1)}, u32[]{:S(2)}, u32[]{:S(2)}) %collective-permute-start.10) | collective-permute-done | bytes 131104 | tf_op jit(solution)/shard_map/ppermute | solution.py:569
  55.9 1.6 %collective-permute-start.12 = (f32[264,128]{1,0:T(8,128)S(1)}, f32[264,128]{1,0:T(8,128)S(1)}, u32[]{:S(2)}, u32[]{:S(2)}) collective-permute-start(f32[264,128]{1,0:T(8,128)S(1)} %pad_maximum_fusion), channel_id=1, source_target_pairs={{4,0},{0,4},{5,1},{1,5},{6,2},{2,6},{7,3},{3,7},{12,8},{8,12},{13,... | collective-permute-start | bytes 405512 | tf_op jit(solution)/shard_map/ppermute | solution.py:564
  57.5 1.6 %collective-permute-start.13 = (f32[256,128]{1,0:T(8,128)S(1)}, f32[256,128]{1,0:T(8,128)S(1)}, u32[]{:S(2)}, u32[]{:S(2)}) collective-permute-start(f32[256,128]{1,0:T(8,128)S(1)} %get-tuple-element.97), channel_id=1, source_target_pairs={{0,8},{8,16},{16,24},{24,0},{1,9},{9,17},{17,25},{25,1},{2,10},{10... | collective-permute-start | bytes 393224 | tf_op jit(solution)/shard_map/ppermute | solution.py:550
  59.1 2.2 %collective-permute-start.14 = (f32[256,128]{1,0:T(8,128)S(1)}, f32[256,128]{1,0:T(8,128)S(1)}, u32[]{:S(2)}, u32[]{:S(2)}) collective-permute-start(f32[256,128]{1,0:T(8,128)S(1)} %get-tuple-element.99), channel_id=1, source_target_pairs={{0,24},{8,0},{16,8},{24,16},{1,25},{9,1},{17,9},{25,17},{2,26},{10... | collective-permute-start | bytes 393224 | tf_op jit(solution)/shard_map/ppermute | solution.py:550
  61.3 2.4 %spread_mix.2 = (f32[256,128]{1,0:T(8,128)S(1)}, f32[256,128]{1,0:T(8,128)S(1)}, f32[256,128]{1,0:T(8,128)S(1)}, f32[256,128]{1,0:T(8,128)S(1)}) custom-call(f32[128,128]{1,0:T(8,128)S(1)} %get-tuple-element.141.matrix, f32[16,128]{1,0:T(8,128)S(1)} %slice_add_fusion.refs_0_.depths, f32[16,128]{1,0:T(8,128)S(1)} %split.44.refs_1_, ...), custom_call_target="tpu_custom_call" | custom-call | tf_op jit(solution)/shard_map/spread_mix/pallas_call | solution.py:464
  63.8 0.1 collective-permute-start.17
  63.8 3.8 %collective-permute-start.18 = (f32[256,128]{1,0:T(8,128)S(1)}, f32[256,128]{1,0:T(8,128)S(1)}, u32[]{:S(2)}, u32[]{:S(2)}) collective-permute-start(f32[256,128]{1,0:T(8,128)S(1)} %get-tuple-element.105), channel_id=1, source_target_pairs={{0,24},{8,0},{16,8},{24,16},{1,25},{9,1},{17,9},{25,17},{2,26},{10... | collective-permute-start | bytes 393224 | tf_op jit(solution)/shard_map/ppermute | solution.py:550
  67.6 0.0 collective-permute-done.13.refs_3_
  67.6 0.0 collective-permute-done.14.refs_5_
  67.6 0.0 collective-permute-done.12
  67.7 0.4 turn_weights.3.refs_13_
  68.2 0.1 collective-permute-start.16
  68.3 2.0 %collective-permute-start.15 = (f32[160,128]{1,0:T(8,128)S(1)}, f32[160,128]{1,0:T(8,128)S(1)}, u32[]{:S(2)}, u32[]{:S(2)}) collective-permute-start(f32[160,128]{1,0:T(8,128)S(1)} %pad_maximum_fusion.7), channel_id=1, source_target_pairs={{0,8},{8,16},{16,24},{24,25},{25,17},{17,9},{9,1},{1,2},{2,10},{10... | collective-permute-start | bytes 245768 | tf_op jit(solution)/shard_map/ppermute | solution.py:569
  70.3 1.3 %collective-permute-start.22 = (f32[256,128]{1,0:T(8,128)S(1)}, f32[256,128]{1,0:T(8,128)S(1)}, u32[]{:S(2)}, u32[]{:S(2)}) collective-permute-start(f32[256,128]{1,0:T(8,128)S(1)} %get-tuple-element.113), channel_id=1, source_target_pairs={{0,16},{8,24},{16,0},{24,8},{1,17},{9,25},{17,1},{25,9},{2,18},{10... | collective-permute-start | bytes 393224 | tf_op jit(solution)/shard_map/ppermute | solution.py:550
  71.5 0.0 collective-permute-done.17.refs_1_
  71.5 1.3 %collective-permute-done.18.refs_3_ = f32[256,128]{1,0:T(8,128)S(1)} collective-permute-done((f32[256,128]{1,0:T(8,128)S(1)}, f32[256,128]{1,0:T(8,128)S(1)}, u32[]{:S(2)}, u32[]{:S(2)}) %collective-permute-start.18) | collective-permute-done | bytes 131104 | tf_op jit(solution)/shard_map/ppermute | solution.py:550
  72.8 0.3 collective-permute-done.15
  73.1 1.0 %collective-permute-done.16 = f32[168,128]{1,0:T(8,128)S(1)} collective-permute-done((f32[168,128]{1,0:T(8,128)S(1)}, f32[168,128]{1,0:T(8,128)S(1)}, u32[]{:S(2)}, u32[]{:S(2)}) %collective-permute-start.16) | collective-permute-done | bytes 86048 | tf_op jit(solution)/shard_map/ppermute | solution.py:569
  74.2 0.0 copy-start
  74.2 0.0 copy-start.1
  74.2 2.3 %spread_mix.3 = (f32[256,128]{1,0:T(8,128)S(1)}, f32[256,128]{1,0:T(8,128)S(1)}, f32[256,128]{1,0:T(8,128)S(1)}, f32[256,128]{1,0:T(8,128)S(1)}) custom-call(f32[128,128]{1,0:T(8,128)S(1)} %get-tuple-element.141.matrix, f32[16,128]{1,0:T(8,128)S(1)} %slice_add_fusion.refs_0_.depths, f32[16,128]{1,0:T(8,128)S(1)} %split.44.refs_1_, ...), custom_call_target="tpu_custom_call" | custom-call | tf_op jit(solution)/shard_map/spread_mix/pallas_call | solution.py:464
  76.5 3.9 %collective-permute-start.19 = (f32[256,128]{1,0:T(8,128)S(1)}, f32[256,128]{1,0:T(8,128)S(1)}, u32[]{:S(2)}, u32[]{:S(2)}) collective-permute-start(f32[256,128]{1,0:T(8,128)S(1)} %get-tuple-element.109), channel_id=1, source_target_pairs={{0,8},{8,16},{16,24},{24,0},{1,9},{9,17},{17,25},{25,1},{2,10},{10... | collective-permute-start | bytes 393224 | tf_op jit(solution)/shard_map/ppermute | solution.py:550
  80.4 1.3 %collective-permute-start.20 = (f32[256,128]{1,0:T(8,128)S(1)}, f32[256,128]{1,0:T(8,128)S(1)}, u32[]{:S(2)}, u32[]{:S(2)}) collective-permute-start(f32[256,128]{1,0:T(8,128)S(1)} %get-tuple-element.110), channel_id=1, source_target_pairs={{0,16},{8,24},{16,0},{24,8},{1,17},{9,25},{17,1},{25,9},{2,18},{10... | collective-permute-start | bytes 393224 | tf_op jit(solution)/shard_map/ppermute | solution.py:550
  81.7 2.8 %collective-permute-start.21 = (f32[256,128]{1,0:T(8,128)S(1)}, f32[256,128]{1,0:T(8,128)S(1)}, u32[]{:S(2)}, u32[]{:S(2)}) collective-permute-start(f32[256,128]{1,0:T(8,128)S(1)} %get-tuple-element.111), channel_id=1, source_target_pairs={{0,24},{8,0},{16,8},{24,16},{1,25},{9,1},{17,9},{25,17},{2,26},{10... | collective-permute-start | bytes 393224 | tf_op jit(solution)/shard_map/ppermute | solution.py:550
  84.5 0.0 collective-permute-done.22.refs_2_
  84.5 1.4 %result.2.refs_4_ = f32[2,16,64,128]{3,2,1,0:T(8,128)} custom-call(f32[2,16,64,128]{3,2,1,0:T(8,128)S(1)} %copy-done, s32[16,64,128]{2,1,0:T(8,128)S(1)} %copy-done.1, f32[256,128]{1,0:T(8,128)S(1)} %get-tuple-element.95.refs_0_, f32[256,128]{1,0:T(8,128)S(1)} %collective-permute-done.17.refs_1_, f32[256,128]{1,0:T(8,128)S(1)} %collective-permute-done.22.refs_2_, ...), custom_call_target="tpu_custom_call" | custom-call | tf_op jit(solution)/shard_map/result/pallas_call | solution.py:523
  85.9 0.0 collective-permute-done.19.refs_1_
  85.9 3.2 %collective-permute-done.20.refs_2_ = f32[256,128]{1,0:T(8,128)S(1)} collective-permute-done((f32[256,128]{1,0:T(8,128)S(1)}, f32[256,128]{1,0:T(8,128)S(1)}, u32[]{:S(2)}, u32[]{:S(2)}) %collective-permute-start.20) | collective-permute-done | bytes 131104 | tf_op jit(solution)/shard_map/ppermute | solution.py:550
  89.1 0.0 collective-permute-done.21.refs_3_
  89.2 1.4 %result.3 = f32[2,16,64,128]{3,2,1,0:T(8,128)} custom-call(f32[2,16,64,128]{3,2,1,0:T(8,128)S(1)} %copy-done, s32[16,64,128]{2,1,0:T(8,128)S(1)} %copy-done.1, f32[256,128]{1,0:T(8,128)S(1)} %get-tuple-element.108.refs_0_, f32[256,128]{1,0:T(8,128)S(1)} %collective-permute-done.19.refs_1_, ...), custom_call_target="tpu_custom_call", output_to_operand_aliasing={{}: (6, {})} | custom-call | tf_op jit(solution)/shard_map/result/pallas_call | solution.py:523
  (39 shorter events, 0.4 us)
Async XLA Ops:
  0.0 10.5 %copy-start.3 = (f32[16,64,128]{2,1,0:T(8,128)S(1)}, f32[16,64,128]{2,1,0:T(8,128)}, u32[]{:S(2)}) copy-start(f32[16,64,128]{2,1,0:T(8,128)} %along_j.3) | copy-start | bytes 1572868
  0.0 10.5 %copy-start.2 = (f32[16,64,128]{2,1,0:T(8,128)S(1)}, f32[16,64,128]{2,1,0:T(8,128)}, u32[]{:S(2)}) copy-start(f32[16,64,128]{2,1,0:T(8,128)} %along_i.3) | copy-start | bytes 1572868
  3.5 16.3 %collective-permute-start = (f32[336,128]{1,0:T(8,128)}, f32[336,128]{1,0:T(8,128)S(1)}, u32[]{:S(2)}, u32[]{:S(2)}) collective-permute-start(f32[336,128]{1,0:T(8,128)} %get-tuple-element.61), channel_id=1, source_target_pairs={{0,8},{8,16},{16,24},{24,0},{1,9},{9,17},{17,25},{25,1},{2,10},{10... | collective-permute-start | bytes 516104 | tf_op jit(solution)/shard_map/ppermute | solution.py:550
  6.5 16.0 %collective-permute-start.1 = (f32[336,128]{1,0:T(8,128)}, f32[336,128]{1,0:T(8,128)S(1)}, u32[]{:S(2)}, u32[]{:S(2)}) collective-permute-start(f32[336,128]{1,0:T(8,128)} %get-tuple-element.62), channel_id=1, source_target_pairs={{0,16},{8,24},{16,0},{24,8},{1,17},{9,25},{17,1},{25,9},{2,18},{10... | collective-permute-start | bytes 516104 | tf_op jit(solution)/shard_map/ppermute | solution.py:550
  9.1 13.4 %collective-permute-start.2 = (f32[336,128]{1,0:T(8,128)}, f32[336,128]{1,0:T(8,128)S(1)}, u32[]{:S(2)}, u32[]{:S(2)}) collective-permute-start(f32[336,128]{1,0:T(8,128)} %get-tuple-element.63), channel_id=1, source_target_pairs={{0,24},{8,0},{16,8},{24,16},{1,25},{9,1},{17,9},{25,17},{2,26},{10... | collective-permute-start | bytes 516104 | tf_op jit(solution)/shard_map/ppermute | solution.py:550
  10.5 5.9 %collective-permute-start.7 = (f32[256,128]{1,0:T(8,128)S(1)}, f32[256,128]{1,0:T(8,128)S(1)}, u32[]{:S(2)}, u32[]{:S(2)}) collective-permute-start(f32[256,128]{1,0:T(8,128)S(1)} %pad_maximum_fusion.1), channel_id=1, source_target_pairs={{4,0},{0,4},{5,1},{1,5},{6,2},{2,6},{7,3},{3,7},{12,8},{8,12},{13,... | collective-permute-start | bytes 393224 | tf_op jit(solution)/shard_map/ppermute | solution.py:564
  15.4 0.8 copy-start.6
  15.4 21.3 %collective-permute-start.4 = (f32[512,128]{1,0:T(8,128)}, f32[512,128]{1,0:T(8,128)S(1)}, u32[]{:S(2)}, u32[]{:S(2)}) collective-permute-start(f32[512,128]{1,0:T(8,128)} %get-tuple-element.67), channel_id=1, source_target_pairs={{0,8},{8,16},{16,24},{24,0},{1,9},{9,17},{17,25},{25,1},{2,10},{10... | collective-permute-start | bytes 786440 | tf_op jit(solution)/shard_map/ppermute | solution.py:550
  16.2 1.0 %copy-start.8 = (f32[512,128]{1,0:T(8,128)S(1)}, f32[512,128]{1,0:T(8,128)}, u32[]{:S(2)}) copy-start(f32[512,128]{1,0:T(8,128)} %get-tuple-element.68) | copy-start | bytes 786436
  17.2 24.0 %collective-permute-start.5 = (f32[512,128]{1,0:T(8,128)S(1)}, f32[512,128]{1,0:T(8,128)S(1)}, u32[]{:S(2)}, u32[]{:S(2)}) collective-permute-start(f32[512,128]{1,0:T(8,128)S(1)} %copy-done.8), channel_id=1, source_target_pairs={{0,16},{8,24},{16,0},{24,8},{1,17},{9,25},{17,1},{25,9},{2,18},{10... | collective-permute-start | bytes 786440 | tf_op jit(solution)/shard_map/ppermute | solution.py:550
  17.5 2.2 %copy-start.7 = (f32[512,128]{1,0:T(8,128)S(1)}, f32[512,128]{1,0:T(8,128)}, u32[]{:S(2)}) copy-start(f32[512,128]{1,0:T(8,128)} %get-tuple-element.69) | copy-start | bytes 786436
  17.5 5.0 %copy-start.5 = (f32[336,128]{1,0:T(8,128)S(1)}, f32[336,128]{1,0:T(8,128)}, u32[]{:S(2)}) copy-start(f32[336,128]{1,0:T(8,128)} %get-tuple-element.60.refs_1_) | copy-start | bytes 516100
  19.8 21.4 %collective-permute-start.6 = (f32[512,128]{1,0:T(8,128)S(1)}, f32[512,128]{1,0:T(8,128)S(1)}, u32[]{:S(2)}, u32[]{:S(2)}) collective-permute-start(f32[512,128]{1,0:T(8,128)S(1)} %copy-done.7), channel_id=1, source_target_pairs={{0,24},{8,0},{16,8},{24,16},{1,25},{9,1},{17,9},{25,17},{2,26},{10... | collective-permute-start | bytes 786440 | tf_op jit(solution)/shard_map/ppermute | solution.py:550
  23.0 23.4 %copy-start.4 = (f32[512,128]{1,0:T(8,128)S(1)}, f32[512,128]{1,0:T(8,128)}, u32[]{:S(2)}) copy-start(f32[512,128]{1,0:T(8,128)} %get-tuple-element.78.refs_0_) | copy-start | bytes 786436
  23.1 24.3 %collective-permute-start.8 = (f32[160,128]{1,0:T(8,128)S(1)}, f32[160,128]{1,0:T(8,128)S(1)}, u32[]{:S(2)}, u32[]{:S(2)}) collective-permute-start(f32[160,128]{1,0:T(8,128)S(1)} %bitcast.47), channel_id=1, source_target_pairs={{0,8},{8,16},{16,24},{24,25},{25,17},{17,9},{9,1},{1,2},{2,10},{10... | collective-permute-start | bytes 245768 | tf_op jit(solution)/shard_map/ppermute | solution.py:569
  36.7 10.7 %collective-permute-start.3 = (f32[176,128]{1,0:T(8,128)S(1)}, f32[176,128]{1,0:T(8,128)S(1)}, u32[]{:S(2)}, u32[]{:S(2)}) collective-permute-start(f32[176,128]{1,0:T(8,128)S(1)} %pad_maximum_fusion.3), channel_id=1, source_target_pairs={{8,0},{16,8},{24,16},{25,24},{17,25},{9,17},{1,9},{2,1},{10,2},{18... | collective-permute-start | bytes 270344 | tf_op jit(solution)/shard_map/ppermute | solution.py:569
  41.2 13.2 %collective-permute-start.11 = (f32[256,128]{1,0:T(8,128)S(1)}, f32[256,128]{1,0:T(8,128)S(1)}, u32[]{:S(2)}, u32[]{:S(2)}) collective-permute-start(f32[256,128]{1,0:T(8,128)S(1)} %get-tuple-element.86), channel_id=1, source_target_pairs={{0,16},{8,24},{16,0},{24,8},{1,17},{9,25},{17,1},{25,9},{2,18},{10... | collective-permute-start | bytes 393224 | tf_op jit(solution)/shard_map/ppermute | solution.py:550
  47.4 7.0 %collective-permute-start.9 = (f32[256,128]{1,0:T(8,128)S(1)}, f32[256,128]{1,0:T(8,128)S(1)}, u32[]{:S(2)}, u32[]{:S(2)}) collective-permute-start(f32[256,128]{1,0:T(8,128)S(1)} %bitcast.42), channel_id=1, source_target_pairs={{0,8},{8,16},{16,24},{24,25},{25,17},{17,9},{9,1},{1,2},{2,10},{10... | collective-permute-start | bytes 393224 | tf_op jit(solution)/shard_map/ppermute | solution.py:569
  51.0 5.0 %collective-permute-start.10 = (f32[256,128]{1,0:T(8,128)S(1)}, f32[256,128]{1,0:T(8,128)S(1)}, u32[]{:S(2)}, u32[]{:S(2)}) collective-permute-start(f32[256,128]{1,0:T(8,128)S(1)} %bitcast.41), channel_id=1, source_target_pairs={{8,0},{16,8},{24,16},{25,24},{17,25},{9,17},{1,9},{2,1},{10,2},{18... | collective-permute-start | bytes 393224 | tf_op jit(solution)/shard_map/ppermute | solution.py:569
  55.9 11.7 %collective-permute-start.12 = (f32[264,128]{1,0:T(8,128)S(1)}, f32[264,128]{1,0:T(8,128)S(1)}, u32[]{:S(2)}, u32[]{:S(2)}) collective-permute-start(f32[264,128]{1,0:T(8,128)S(1)} %pad_maximum_fusion), channel_id=1, source_target_pairs={{4,0},{0,4},{5,1},{1,5},{6,2},{2,6},{7,3},{3,7},{12,8},{8,12},{13,... | collective-permute-start | bytes 405512 | tf_op jit(solution)/shard_map/ppermute | solution.py:564
  57.5 10.1 %collective-permute-start.13 = (f32[256,128]{1,0:T(8,128)S(1)}, f32[256,128]{1,0:T(8,128)S(1)}, u32[]{:S(2)}, u32[]{:S(2)}) collective-permute-start(f32[256,128]{1,0:T(8,128)S(1)} %get-tuple-element.97), channel_id=1, source_target_pairs={{0,8},{8,16},{16,24},{24,0},{1,9},{9,17},{17,25},{25,1},{2,10},{10... | collective-permute-start | bytes 393224 | tf_op jit(solution)/shard_map/ppermute | solution.py:550
  59.1 8.5 %collective-permute-start.14 = (f32[256,128]{1,0:T(8,128)S(1)}, f32[256,128]{1,0:T(8,128)S(1)}, u32[]{:S(2)}, u32[]{:S(2)}) collective-permute-start(f32[256,128]{1,0:T(8,128)S(1)} %get-tuple-element.99), channel_id=1, source_target_pairs={{0,24},{8,0},{16,8},{24,16},{1,25},{9,1},{17,9},{25,17},{2,26},{10... | collective-permute-start | bytes 393224 | tf_op jit(solution)/shard_map/ppermute | solution.py:550
  63.8 7.8 %collective-permute-start.17 = (f32[256,128]{1,0:T(8,128)S(1)}, f32[256,128]{1,0:T(8,128)S(1)}, u32[]{:S(2)}, u32[]{:S(2)}) collective-permute-start(f32[256,128]{1,0:T(8,128)S(1)} %get-tuple-element.104), channel_id=1, source_target_pairs={{0,8},{8,16},{16,24},{24,0},{1,9},{9,17},{17,25},{25,1},{2,10},{10... | collective-permute-start | bytes 393224 | tf_op jit(solution)/shard_map/ppermute | solution.py:550
  63.8 9.0 %collective-permute-start.18 = (f32[256,128]{1,0:T(8,128)S(1)}, f32[256,128]{1,0:T(8,128)S(1)}, u32[]{:S(2)}, u32[]{:S(2)}) collective-permute-start(f32[256,128]{1,0:T(8,128)S(1)} %get-tuple-element.105), channel_id=1, source_target_pairs={{0,24},{8,0},{16,8},{24,16},{1,25},{9,1},{17,9},{25,17},{2,26},{10... | collective-permute-start | bytes 393224 | tf_op jit(solution)/shard_map/ppermute | solution.py:550
  68.2 6.0 %collective-permute-start.16 = (f32[168,128]{1,0:T(8,128)S(1)}, f32[168,128]{1,0:T(8,128)S(1)}, u32[]{:S(2)}, u32[]{:S(2)}) collective-permute-start(f32[168,128]{1,0:T(8,128)S(1)} %pad_maximum_fusion.6), channel_id=1, source_target_pairs={{8,0},{16,8},{24,16},{25,24},{17,25},{9,17},{1,9},{2,1},{10,2},{18... | collective-permute-start | bytes 258056 | tf_op jit(solution)/shard_map/ppermute | solution.py:569
  68.3 4.8 %collective-permute-start.15 = (f32[160,128]{1,0:T(8,128)S(1)}, f32[160,128]{1,0:T(8,128)S(1)}, u32[]{:S(2)}, u32[]{:S(2)}) collective-permute-start(f32[160,128]{1,0:T(8,128)S(1)} %pad_maximum_fusion.7), channel_id=1, source_target_pairs={{0,8},{8,16},{16,24},{24,25},{25,17},{17,9},{9,1},{1,2},{2,10},{10... | collective-permute-start | bytes 245768 | tf_op jit(solution)/shard_map/ppermute | solution.py:569
  70.3 14.2 %collective-permute-start.22 = (f32[256,128]{1,0:T(8,128)S(1)}, f32[256,128]{1,0:T(8,128)S(1)}, u32[]{:S(2)}, u32[]{:S(2)}) collective-permute-start(f32[256,128]{1,0:T(8,128)S(1)} %get-tuple-element.113), channel_id=1, source_target_pairs={{0,16},{8,24},{16,0},{24,8},{1,17},{9,25},{17,1},{25,9},{2,18},{10... | collective-permute-start | bytes 393224 | tf_op jit(solution)/shard_map/ppermute | solution.py:550
  74.2 10.3 %copy-start = (f32[2,16,64,128]{3,2,1,0:T(8,128)S(1)}, f32[2,16,64,128]{3,2,1,0:T(8,128)}, u32[]{:S(2)}) copy-start(f32[2,16,64,128]{3,2,1,0:T(8,128)} %gain.2) | copy-start | bytes 3145732
  74.2 10.3 %copy-start.1 = (s32[16,64,128]{2,1,0:T(8,128)S(1)}, s32[16,64,128]{2,1,0:T(8,128)}, u32[]{:S(2)}) copy-start(s32[16,64,128]{2,1,0:T(8,128)} %mask.5) | copy-start | bytes 1572868
  76.5 9.4 %collective-permute-start.19 = (f32[256,128]{1,0:T(8,128)S(1)}, f32[256,128]{1,0:T(8,128)S(1)}, u32[]{:S(2)}, u32[]{:S(2)}) collective-permute-start(f32[256,128]{1,0:T(8,128)S(1)} %get-tuple-element.109), channel_id=1, source_target_pairs={{0,8},{8,16},{16,24},{24,0},{1,9},{9,17},{17,25},{25,1},{2,10},{10... | collective-permute-start | bytes 393224 | tf_op jit(solution)/shard_map/ppermute | solution.py:550
  80.4 8.8 %collective-permute-start.20 = (f32[256,128]{1,0:T(8,128)S(1)}, f32[256,128]{1,0:T(8,128)S(1)}, u32[]{:S(2)}, u32[]{:S(2)}) collective-permute-start(f32[256,128]{1,0:T(8,128)S(1)} %get-tuple-element.110), channel_id=1, source_target_pairs={{0,16},{8,24},{16,0},{24,8},{1,17},{9,25},{17,1},{25,9},{2,18},{10... | collective-permute-start | bytes 393224 | tf_op jit(solution)/shard_map/ppermute | solution.py:550
  81.7 7.5 %collective-permute-start.21 = (f32[256,128]{1,0:T(8,128)S(1)}, f32[256,128]{1,0:T(8,128)S(1)}, u32[]{:S(2)}, u32[]{:S(2)}) collective-permute-start(f32[256,128]{1,0:T(8,128)S(1)} %get-tuple-element.111), channel_id=1, source_target_pairs={{0,24},{8,0},{16,8},{24,16},{1,25},{9,1},{17,9},{25,17},{2,26},{10... | collective-permute-start | bytes 393224 | tf_op jit(solution)/shard_map/ppermute | solution.py:550
